TPU v7x, 32 devices: a whole 2x2x4 slice. The times are simulated.
32 devices in a mesh: kv: 4 (over y, x), seq: 8 (over z, core).
Axes of the slice: x: 2, y: 2, z: 4, core: 2. Of those that a mesh axis runs over, the one named last changes fastest.
Arguments:
- queries: bfloat16 [8192, 4096], P('seq', 'kv'), may hold values from -40 to 40
- query_tangent: bfloat16 [8192, 4096], P('seq', 'kv'), may hold values from -6 to 6
- key_value: bfloat16 [8192, 2, 512], P('seq', None, 'kv'), may hold values from -40 to 40
- key_value_tangents: bfloat16 [8192, 2, 512], P('seq', None, 'kv'), may hold values from -6 to 6
- doc_lengths: int32 [64], replicated, may hold values from 1 to 1024, 8192 in all
- out_weight: bfloat16 [4096, 2048], P(('kv', 'seq')), may hold values from -0.5 to 0.5
- weight_tangent: bfloat16 [4096, 2048], P(('kv', 'seq')), may hold values from -0.25 to 0.25
Outputs:
- layer_out: bfloat16 [8192, 2048], P('seq', 'kv')
- out_tangent: bfloat16 [8192, 2048], P('seq', 'kv')
Inputs may be any that keep to these rules, and one draw needn't show every extreme that they name: `doc_lengths`: the 64 lengths sum to 8192; the longest is exactly 1024.
All inputs are finite; a program needn't handle non-finite values.
Results may differ from a plain program's by a relative error of at most 0.0057.
Values may be sent and summed in bfloat16 or wider, within the bound.
No kernel may reach another device: no remote copies, remote signals or barrier semaphores. Data moves between devices by JAX's collectives and lax.ppermute only.
A program may use at most 128 MiB of HBM per device.

v0:
```python
import math

import jax
import jax.numpy as jnp
from jax import lax
from jax.sharding import PartitionSpec as P

STRETCH = 32
WINDOW = 224


masked_score = -1e30


def passed_along(block, axis, distance):
    devices = range(lax.axis_size(axis))
    route = [(i - distance, i) for i in devices if i - distance in devices]
    return lax.ppermute(block, axis, route)


def attend(query_block, query_tan, key_rows, value_rows, key_tangent, value_tangent, lower_rel):
    head_dim = key_rows.shape[-1]
    score_scale = 1.0 / math.sqrt(head_dim)
    scores = (
        jnp.einsum("bcgh,brh->bgcr", query_block, key_rows, preferred_element_type=jnp.float32)
        * score_scale
    )
    tangent = (
        jnp.einsum("bcgh,brh->bgcr", query_tan, key_rows, preferred_element_type=jnp.float32)
        + jnp.einsum("bcgh,brh->bgcr", query_block, key_tangent, preferred_element_type=jnp.float32)
    ) * score_scale
    columns = jnp.arange(key_rows.shape[1]).astype(jnp.float32)[None, None, None, :]
    row_index = jnp.arange(query_block.shape[1]).astype(jnp.float32)[None, None, :, None]
    admitted = (columns >= lower_rel.astype(jnp.float32)[:, None, :, None]) & (
        columns <= row_index + WINDOW
    )
    scores = jnp.where(admitted, scores, masked_score)
    row_peak = jnp.max(scores, axis=-1, keepdims=True)
    exponent = jnp.where(admitted, jnp.exp(scores - row_peak), 0.0)
    row_total = jnp.sum(exponent, axis=-1, keepdims=True)
    probabilities = exponent / row_total
    tangent = jnp.where(admitted, tangent, 0.0)
    mean_tan = jnp.sum(probabilities * tangent, axis=-1, keepdims=True)
    prob_low = probabilities.astype(jnp.bfloat16)
    tangent_low = (probabilities * (tangent - mean_tan)).astype(jnp.bfloat16)
    outputs = jnp.einsum("bgcr,brh->bcgh", prob_low, value_rows, preferred_element_type=jnp.float32)
    out_tan = jnp.einsum(
        "bgcr,brh->bcgh", tangent_low, value_rows, preferred_element_type=jnp.float32
    ) + jnp.einsum("bgcr,brh->bcgh", prob_low, value_tangent, preferred_element_type=jnp.float32)
    return (outputs.astype(jnp.bfloat16), out_tan.astype(jnp.bfloat16))


def body(
    queries, query_tangent, key_value, key_value_tangents, doc_lengths, out_weight, weight_tangent
):
    local_tokens = queries.shape[0]
    head_dim = key_value.shape[2]
    group_width = queries.shape[1]
    heads_per_group = group_width // head_dim
    seq_index = lax.axis_index("seq")
    stretch_count = local_tokens // STRETCH
    span_count = (WINDOW + STRETCH) // STRETCH
    lead_blocks = WINDOW // STRETCH
    stacked = jnp.concatenate(
        [
            key_value.reshape(local_tokens, 2 * head_dim),
            key_value_tangents.reshape(local_tokens, 2 * head_dim),
        ],
        axis=1,
    )
    prior = passed_along(stacked[local_tokens - WINDOW :], "seq", 1)
    context = jnp.concatenate([prior, stacked], axis=0).reshape(
        lead_blocks + stretch_count, STRETCH, 4 * head_dim
    )
    windows = jnp.concatenate(
        [context[offset : offset + stretch_count] for offset in range(span_count)], axis=1
    )
    doc_ends = jnp.cumsum(doc_lengths)
    doc_starts = doc_ends - doc_lengths
    position = seq_index * local_tokens + jnp.arange(local_tokens, dtype=jnp.int32)
    inside = (doc_starts[None, :] <= position[:, None]) & (position[:, None] < doc_ends[None, :])
    doc_first = jnp.sum(jnp.where(inside, doc_starts[None, :], 0), axis=1)
    lower_bound = jnp.maximum(doc_first, position - WINDOW + 1)
    stretch_start = position.reshape(stretch_count, STRETCH)[:, :1]
    lower_rel = lower_bound.reshape(stretch_count, STRETCH) - (stretch_start - WINDOW)
    packed = jnp.concatenate([queries, query_tangent], axis=1).reshape(
        stretch_count, STRETCH, 2 * group_width
    )
    lead_shape = packed.shape[:-2]
    query_block = packed[..., :group_width].reshape(-1, STRETCH, heads_per_group, head_dim)
    query_tan = packed[..., group_width:].reshape(-1, STRETCH, heads_per_group, head_dim)
    outputs, out_tan = attend(
        query_block,
        query_tan,
        windows[..., :head_dim],
        windows[..., head_dim : 2 * head_dim],
        windows[..., 2 * head_dim : 3 * head_dim],
        windows[..., 3 * head_dim :],
        lower_rel,
    )
    attention_home = outputs.reshape(lead_shape + (STRETCH, group_width))
    tangent_home = out_tan.reshape(lead_shape + (STRETCH, group_width))
    attention = attention_home.reshape(local_tokens, group_width)
    attention_tan = tangent_home.reshape(local_tokens, group_width)
    full_weight, full_tangent = (
        lax.all_gather(out_weight, "seq", axis=0, tiled=True),
        lax.all_gather(weight_tangent, "seq", axis=0, tiled=True),
    )
    partial_value = jnp.dot(attention, full_weight, preferred_element_type=jnp.float32)
    partial_tan = jnp.dot(attention_tan, full_weight, preferred_element_type=jnp.float32) + jnp.dot(
        attention, full_tangent, preferred_element_type=jnp.float32
    )
    layer_out, out_tangent = (
        lax.psum_scatter(partial_value, "kv", scatter_dimension=1, tiled=True),
        lax.psum_scatter(partial_tan, "kv", scatter_dimension=1, tiled=True),
    )
    return (layer_out.astype(jnp.bfloat16), out_tangent.astype(jnp.bfloat16))


def solution(mesh):
    in_specs = (
        P("seq", "kv"),
        P("seq", "kv"),
        P("seq", None, "kv"),
        P("seq", None, "kv"),
        P(),
        P(("kv", "seq"), None),
        P(("kv", "seq"), None),
    )
    out_specs = (P("seq", "kv"), P("seq", "kv"))
    return jax.shard_map(body, mesh=mesh, in_specs=in_specs, out_specs=out_specs, check_vma=False)
```

profile of v0, /device:TPU:0, one launch (start us, length us, event | category | flops | bytes accessed | tf_op | source)
XLA Modules:
  0.0 301.2 jit_solution(13474129037057332198)
XLA Ops:
  7.2 0.7 all-gather.3.cloned.1.call-update
  8.0 1.1 bitcast_dynamic-update-slice_fusion.1
  9.1 1.1 bitcast_dynamic-update-slice_fusion
  10.2 3.1 %collective-permute-start = (bf16[224,512]{1,0:T(8,128)(2,1)S(1)}, bf16[224,512]{1,0:T(8,128)(2,1)}, u32[]{:S(2)}, u32[]{:S(2)}) collective-permute-start(bf16[224,512]{1,0:T(8,128)(2,1)S(1)} %slice.90), channel_id=1, source_target_pairs={{0,1},{1,2},{2,3},{3,4},{4,5},{5,6},{6,7},{8,9},{9,10},{10,11},{11... | collective-permute-start | bytes 688136 | tf_op jit(solution)/shard_map/ppermute | solution.py:18
  13.3 0.0 reduce-scatter.5.cloned.1.call-start
  13.4 2.2 concatenate.21
  15.5 1.1 concatenate.22
  16.7 2.8 pad_maximum_fusion
  19.5 2.3 slice_bitcast_fusion.4
  21.8 0.1 copy.23
  21.9 0.1 reduce-window.8
  22.0 0.1 reduce
  22.1 0.1 select_reduce_fusion
  22.2 0.1 reduce_sum.30
  22.3 0.1 fusion.37
  22.4 0.1 subtract_convert_fusion
  22.5 0.1 broadcast_compare_fusion
  22.6 0.3 compare_and_fusion
  22.8 2.2 pad_maximum_fusion.1
  25.0 0.1 constant_dynamic-update-slice_fusion.6
  25.2 0.1 constant_dynamic-update-slice_fusion.5
  25.3 0.1 constant_dynamic-update-slice_fusion.4
  25.4 0.1 constant_dynamic-update-slice_fusion.3
  25.5 0.1 constant_dynamic-update-slice_fusion.2
  25.6 0.1 constant_dynamic-update-slice_fusion.1
  25.7 0.1 constant_dynamic-update-slice_fusion
  25.9 0.6 copy-done.2
  26.4 0.2 copy-done.3
  26.6 0.1 maximum_dynamic-update-slice_fusion
  26.7 3.2 %copy-done = bf16[32,256,512]{2,1,0:T(8,128)(2,1)} copy-done((bf16[32,256,512]{2,1,0:T(8,128)(2,1)}, bf16[32,256,512]{2,1,0:T(8,128)(2,1)S(1)}, u32[]{:S(2)}) %copy-start) | copy-done | bytes 8388632
  29.9 1.2 fusion.17
  31.2 6.2 %fusion.40 = (f32[32,8,32]{2,1,0:T(8,128)S(1)}, f32[32,8,32,256]{3,2,1,0:T(8,128)}) fusion(f32[32,256,32,8]{1,2,3,0:T(8,128)S(1)} %fusion.17, pred[32,32,256]{2,1,0:T(8,128)(4,1)S(1)} %compare_and_fusion), kind=kOutput, calls=%fused_computation.84 | output fusion | flops 14680319 | bytes 17072128 | tf_op jit(solution)/shard_map/sub | solution.py:39
  37.4 3.5 %fusion.13 = f32[32,256,32,8]{1,2,3,0:T(8,128)S(1)} fusion(bf16[32,4,8,8,128]{4,3,2,1,0:T(8,128)(2,1)} %get-tuple-element.2, bf16[32,256,512]{2,1,0:T(8,128)(2,1)} %copy-done), kind=kOutput, calls=%fused_computation.28 | convolution fusion | flops 536870912 | bytes 12582912 | tf_op jit(solution)/shard_map/bcgh,brh->bgcr/dot_general | solution.py:29
  40.9 7.7 %multiply_reduce_fusion = (f32[32,8,32]{2,1,0:T(8,128)S(1)}, f32[32,8,32,256]{3,2,1,0:T(8,128)}) fusion(f32[32,8,32,256]{3,2,1,0:T(8,128)} %get-tuple-element.12, f32[32,8,32]{2,1,0:T(8,128)S(1)} %get-tuple-element.11, f32[32,256,32,8]{1,2,3,0:T(8,128)S(1)} %fusion.13, bf16[32,4,8,8,128]{4,3,2,1,0:T(8,128)(2,1)S(1)} %get-tuple-element.3, ...), kind=kOutput, calls=%fused_computation.4 | convolution fusion | flops 549445632 | bytes 29687808 | tf_op jit(solution)/shard_map/bcgh,brh->bgcr/dot_general | solution.py:30
  48.6 8.6 %fusion.2 = f32[32,128,8,32]{1,3,2,0:T(8,128)S(1)} fusion(f32[32,8,32,256]{3,2,1,0:T(8,128)} %get-tuple-element.14, f32[32,8,32]{2,1,0:T(8,128)S(1)} %get-tuple-element.13, bf16[32,256,512]{2,1,0:T(8,128)(2,1)} %copy-done, f32[32,8,32,256]{3,2,1,0:T(8,128)} %get-tuple-element.12, f32[32,8,32]{2,1,0:T(8,128)S(1)} %get-tuple-element.11), kind=kOutput, calls=%fused_computation.7 | convolution fusion | flops 545259520 | bytes 23134208 | tf_op jit(solution)/shard_map/bgcr,brh->bcgh/dot_general | solution.py:47
  57.2 0.4 copy-done.5
  57.6 2.8 fusion.28
  60.5 2.3 copy.28
  62.8 3.0 %convert_bitcast_fusion = bf16[32,32,8,128]{3,1,2,0:T(8,128)(2,1)S(1)} fusion(bf16[32,256,512]{2,1,0:T(8,128)(2,1)} %copy-done, f32[32,8,32,256]{3,2,1,0:T(8,128)S(1)} %copy-done.5, f32[32,8,32]{2,1,0:T(8,128)S(1)} %get-tuple-element.11), kind=kOutput, calls=%fused_computation.40 | convolution fusion | flops 542113792 | bytes 12615680 | tf_op jit(solution)/shard_map/bgcr,brh->bcgh/dot_general | solution.py:46
  65.8 1.0 copy.25
  66.8 11.0 %fusion.7 = f32[1024,2048]{1,0:T(8,128)} fusion(bf16[1024,2048]{1,0:T(8,128)(2,1)} %all-gather.3.cloned.1.call-done, bf16[128,8,8,128]{3,2,1,0:T(8,128)(2,1)} %bitcast.97), kind=kOutput, calls=%fused_computation.22 | convolution fusion | flops 4294967296 | bytes 14680064 | tf_op jit(solution)/shard_map/dot_general | solution.py:110
  77.8 29.2 %all-gather.5.cloned.1.call-done = bf16[1024,2048]{1,0:T(8,128)(2,1)} async-done(((bf16[128,2048]{1,0:T(8,128)(2,1)}), bf16[1024,2048]{1,0:T(8,128)(2,1)}) %all-gather.5.cloned.1.call-update) | async-done | bytes 4194320 | tf_op jit(solution)/shard_map/all_gather | solution.py:107
  107.0 10.1 %convolution_add_fusion = f32[1024,2048]{1,0:T(8,128)} fusion(f32[1024,2048]{1,0:T(8,128)} %fusion.7, bf16[1024,2048]{1,0:T(8,128)(2,1)} %all-gather.5.cloned.1.call-done, bf16[128,8,8,128]{3,2,1,0:T(8,128)(2,1)S(1)} %bitcast.95), kind=kOutput, calls=%fused_computation.15 | convolution fusion | flops 4297064448 | bytes 23068672 | tf_op jit(solution)/shard_map/dot_general | solution.py:110
  117.2 8.9 %fusion.11 = f32[1024,2048]{1,0:T(8,128)} fusion(bf16[1024,2048]{1,0:T(8,128)(2,1)} %all-gather.3.cloned.1.call-done, bf16[128,8,8,128]{3,2,1,0:T(8,128)(2,1)S(1)} %bitcast.96), kind=kOutput, calls=%fused_computation.26 | convolution fusion | flops 4294967296 | bytes 14680064 | tf_op jit(solution)/shard_map/dot_general | solution.py:109
  126.1 76.3 %reduce-scatter.5.cloned.1.call-done = f32[1024,512]{1,0:T(8,128)} async-done(((f32[1024,2048]{1,0:T(8,128)}), f32[1024,512]{1,0:T(8,128)}) %reduce-scatter.5.cloned.1.call-update) | async-done | bytes 2097168 | tf_op jit(solution)/shard_map/reduce_scatter | solution.py:115
  202.4 2.7 convert_element_type.56
  205.1 86.9 %reduce-scatter.3.cloned.1.call-done = f32[1024,512]{1,0:T(8,128)} async-done(((f32[1024,2048]{1,0:T(8,128)}), f32[1024,512]{1,0:T(8,128)}) %reduce-scatter.3.cloned.1.call-update) | async-done | bytes 2097168 | tf_op jit(solution)/shard_map/reduce_scatter | solution.py:114
  292.0 2.7 convert_element_type.52
  (22 shorter events, 0.3 us)
Async XLA Ops:
  7.2 8.4 %copy-start.1 = (bf16[1024,2,128]{2,1,0:T(2,128)(2,1)S(1)}, bf16[1024,2,128]{2,1,0:T(2,128)(2,1)}, u32[]{:S(2)}) copy-start(bf16[1024,2,128]{2,1,0:T(2,128)(2,1)} %param.10) | copy-start | bytes 1572868
  7.2 59.7 %all-gather.3.cloned.1.call-start = ((), (), s32[]{:S(2)}) async-start(), calls=%async_computation.2 | async-start | bytes 4718592 | tf_op jit(solution)/shard_map/all_gather | solution.py:106
  7.9 99.1 %all-gather.5.cloned.1.call-start = ((), (), s32[]{:S(2)}) async-start(), calls=%async_computation.4 | async-start | bytes 4718592 | tf_op jit(solution)/shard_map/all_gather | solution.py:107
  10.2 12.6 %collective-permute-start = (bf16[224,512]{1,0:T(8,128)(2,1)S(1)}, bf16[224,512]{1,0:T(8,128)(2,1)}, u32[]{:S(2)}, u32[]{:S(2)}) collective-permute-start(bf16[224,512]{1,0:T(8,128)(2,1)S(1)} %slice.90), channel_id=1, source_target_pairs={{0,1},{1,2},{2,3},{3,4},{4,5},{5,6},{6,7},{8,9},{9,10},{10,11},{11... | collective-permute-start | bytes 688136 | tf_op jit(solution)/shard_map/ppermute | solution.py:18
  13.3 189.1 %reduce-scatter.5.cloned.1.call-start = ((), (), s32[]{:S(2)}) async-start(), calls=%async_computation.5 | async-start | bytes 10485760 | tf_op jit(solution)/shard_map/reduce_scatter | solution.py:115
  19.5 2.3 copy-start.4
  25.4 1.1 copy-start.2
  25.4 1.2 copy-start.3
  26.7 3.2 %copy-start = (bf16[32,256,512]{2,1,0:T(8,128)(2,1)}, bf16[32,256,512]{2,1,0:T(8,128)(2,1)S(1)}, u32[]{:S(2)}) copy-start(bf16[32,256,512]{2,1,0:T(8,128)(2,1)S(1)} %maximum_dynamic-update-slice_fusion) | copy-start | bytes 25165828
  48.6 9.0 %copy-start.5 = (f32[32,8,32,256]{3,2,1,0:T(8,128)S(1)}, f32[32,8,32,256]{3,2,1,0:T(8,128)}, u32[]{:S(2)}) copy-start(f32[32,8,32,256]{3,2,1,0:T(8,128)} %get-tuple-element.12) | copy-start | bytes 25165828
  117.1 174.9 %reduce-scatter.3.cloned.1.call-start = ((), (), s32[]{:S(2)}) async-start(), calls=%async_computation.3 | async-start | bytes 10485760 | tf_op jit(solution)/shard_map/reduce_scatter | solution.py:114
Sparse Core Ops, SparseCore 0:
  9.6 49.8 all-gather.2
  61.1 45.8 all-gather.4
  117.3 85.0 reduce-scatter.4
  205.6 86.3 reduce-scatter.2
where the time goes:
time: 302 us; the launch traced here: 301 us
  waiting for transfers between devices  193 us (64%)
  matrix products  56.9 us (19%)
  other arithmetic  17.5 us (6%)
  local copies, waits for them, and re-layouts  16.5 us (5%)
  between operations  14 us (5%)
  starting transfers between devices  3.22 us (1%)
    reduce_scatter x1, waiting for transfers between devices, body(): lax.psum_scatter(partial_value, 'kv', scatter_dimension=1, tiled=True)  86.9 us
    reduce_scatter x1, waiting for transfers between devices, body(): lax.psum_scatter(partial_tan, 'kv', scatter_dimension=1, tiled=True)  76.3 us
    all_gather x1, waiting for transfers between devices, body(): lax.all_gather(weight_tangent, 'seq', axis=0, tiled=True)  29.2 us
    dot_general x1, matrix products, body(): jnp.dot(attention_tan, full_weight, preferred_element_type=jnp.float32)  11 us
    dot_general x1, matrix products, body(): jnp.dot(attention, full_tangent, preferred_element_type=jnp.float32)  10.1 us
    dot_general x1, matrix products, body(): jnp.dot(attention, full_weight, preferred_element_type=jnp.float32)  8.87 us
    dot_general x1, matrix products, attend(): jnp.einsum('bgcr,brh->bcgh', tangent_low, value_rows, preferred_element_t...  8.6 us
    unnamed x21, local copies, waits for them, and re-layouts  8.55 us
  transfers between devices with their start and end apart: 5, of which 3 were waited for; matrix products, arithmetic and copies ran while one was open for 24% of the time, Pallas kernels for 0%

commit v1 on v0

v1 whole, which is shorter than its diff:
```python
import functools
import math

import jax
import jax.numpy as jnp
from jax import lax
from jax.experimental import pallas as pl
from jax.experimental.pallas import tpu as pltpu
from jax.sharding import PartitionSpec as P

STRETCH = 32
WINDOW = 224
CHUNKS = 2
TILE = 128

masked_score = -1e30


def attention_kernel(heads, head_dim, q_ref, qt_ref, ctx_ref, low_ref, out_ref):
    rows = q_ref.shape[0]
    span = WINDOW + STRETCH
    width = heads * head_dim
    score_scale = 1.0 / math.sqrt(head_dim)
    to_log2 = score_scale * math.log2(math.e)
    step = pl.program_id(0)
    transposed = (((1,), (1,)), ((), ()))
    column = lax.broadcasted_iota(jnp.int32, (STRETCH, span), 1)
    row = lax.broadcasted_iota(jnp.int32, (STRETCH, span), 0)
    causal = column <= row + WINDOW
    for part in range(rows // STRETCH):
        here = slice(part * STRETCH, (part + 1) * STRETCH)
        base = pl.multiple_of(step * rows + part * STRETCH, STRETCH)
        keys = ctx_ref[pl.ds(base, span), : 2 * head_dim]
        values = ctx_ref[pl.ds(base, span), 2 * head_dim :]
        low = low_ref[here, :]
        low = jnp.concatenate([low] * (span // low.shape[1]), axis=1)
        admitted = causal & (column >= low)
        q = jnp.concatenate(
            [q_ref[here, h * head_dim : (h + 1) * head_dim] for h in range(heads)], axis=0
        )
        qt = jnp.concatenate(
            [qt_ref[here, h * head_dim : (h + 1) * head_dim] for h in range(heads)], axis=0
        )
        scores = lax.dot_general(
            q, keys[:, :head_dim], transposed, preferred_element_type=jnp.float32
        )
        tangent = lax.dot_general(
            jnp.concatenate([qt, q], axis=1), keys, transposed, preferred_element_type=jnp.float32
        )
        scores = scores.reshape(heads, STRETCH, span)
        tangent = tangent.reshape(heads, STRETCH, span)
        scores = jnp.where(admitted[None], scores, masked_score)
        peak = jnp.max(scores, axis=-1, keepdims=True)
        exponent = jnp.exp2((scores - peak) * to_log2)
        inverse = 1.0 / jnp.sum(exponent, axis=-1, keepdims=True)
        mean = jnp.sum(exponent * tangent, axis=-1, keepdims=True) * inverse
        prob = exponent * inverse
        prob_low = prob.astype(jnp.bfloat16).reshape(heads * STRETCH, span)
        tan_low = (prob * ((tangent - mean) * score_scale)).astype(jnp.bfloat16)
        tan_low = tan_low.reshape(heads * STRETCH, span)
        both = jnp.dot(prob_low, values, preferred_element_type=jnp.float32)
        more = jnp.dot(tan_low, values[:, :head_dim], preferred_element_type=jnp.float32)
        out = both[:, :head_dim].astype(jnp.bfloat16)
        out_tan = (both[:, head_dim:] + more).astype(jnp.bfloat16)
        for h in range(heads):
            of = slice(h * STRETCH, (h + 1) * STRETCH)
            out_ref[here, h * head_dim : (h + 1) * head_dim] = out[of]
            out_ref[here, width + h * head_dim : width + (h + 1) * head_dim] = out_tan[of]


def attention(queries, query_tangent, context, low):
    tokens, width = queries.shape
    head_dim = context.shape[1] // 4
    heads = width // head_dim
    elements = tokens * heads * (WINDOW + STRETCH)
    return pl.pallas_call(
        functools.partial(attention_kernel, heads, head_dim),
        grid=(tokens // TILE,),
        in_specs=[
            pl.BlockSpec((TILE, width), lambda i: (i, 0)),
            pl.BlockSpec((TILE, width), lambda i: (i, 0)),
            pl.BlockSpec(context.shape, lambda i: (0, 0)),
            pl.BlockSpec((TILE, low.shape[1]), lambda i: (i, 0)),
        ],
        out_specs=pl.BlockSpec((TILE, 2 * width), lambda i: (i, 0)),
        out_shape=jax.ShapeDtypeStruct((tokens, 2 * width), jnp.bfloat16),
        compiler_params=pltpu.CompilerParams(vmem_limit_bytes=48 * 1024 * 1024),
        cost_estimate=pl.CostEstimate(
            flops=12 * elements * head_dim, bytes_accessed=10 * tokens * width, transcendentals=elements
        ),
        name="attention",
    )(queries, query_tangent, context, low)


def across(block, flip):
    size = lax.axis_size("kv")
    return lax.ppermute(block, "kv", [(i, i ^ flip) for i in range(size)])


def relative_columns(weight, kv_index):
    size = lax.axis_size("kv")
    blocks = weight.reshape(weight.shape[0], size, -1)
    return [
        lax.dynamic_index_in_dim(blocks, kv_index ^ r, axis=1, keepdims=False) for r in range(size)
    ]


def body(
    queries, query_tangent, key_value, key_value_tangents, doc_lengths, out_weight, weight_tangent
):
    tokens, width = queries.shape
    head_dim = key_value.shape[2]
    seq_index = lax.axis_index("seq")
    kv_index = lax.axis_index("kv")
    seq_size = lax.axis_size("seq")

    value_blocks = relative_columns(out_weight, kv_index)
    tangent_blocks = relative_columns(weight_tangent, kv_index)
    part = value_blocks[0].shape[1] // CHUNKS
    gathered = []
    for chunk in range(CHUNKS):
        of = slice(chunk * part, (chunk + 1) * part)
        mine = jnp.stack(
            [
                jnp.concatenate([blocks[r][:, of] for r in (1, 3, 2, 0)], axis=1)
                for blocks in (tangent_blocks, value_blocks)
            ]
        )
        whole = lax.all_gather(mine, "seq", axis=1, tiled=True)
        gathered.append(whole.reshape(-1, whole.shape[-1]))

    stacked = jnp.concatenate(
        [key_value[:, 0], key_value_tangents[:, 0], key_value[:, 1], key_value_tangents[:, 1]],
        axis=1,
    )
    prior = lax.ppermute(
        stacked[tokens - WINDOW :], "seq", [(i, i + 1) for i in range(seq_size - 1)]
    )
    context = jnp.concatenate([prior, stacked], axis=0)

    doc_ends = jnp.cumsum(doc_lengths)
    doc_starts = doc_ends - doc_lengths
    position = seq_index * tokens + jnp.arange(tokens, dtype=jnp.int32)
    inside = (doc_starts[None, :] <= position[:, None]) & (position[:, None] < doc_ends[None, :])
    doc_first = jnp.sum(jnp.where(inside, doc_starts[None, :], 0), axis=1)
    lower = jnp.maximum(doc_first, position - WINDOW + 1)
    low = lower - (position // STRETCH * STRETCH - WINDOW)
    low = jnp.broadcast_to(low[:, None], (tokens, 128))

    pair = attention(queries, query_tangent, context, low)

    half = tokens // 2
    finished = []
    for weights in gathered:
        col = weights.shape[1] // 4
        rows = weights.shape[0] // 2

        def project(of, columns):
            value = jnp.dot(
                pair[of, :width], weights[rows:, columns], preferred_element_type=jnp.float32
            )
            tangent = jnp.dot(pair[of], weights[:, columns], preferred_element_type=jnp.float32)
            return jnp.stack([value, tangent])

        first, second = slice(0, half), slice(half, tokens)
        partial = project(slice(0, tokens), slice(0, 4 * col))
        send_x = partial[:, first, : 2 * col].astype(jnp.bfloat16)
        send_y = partial[:, second, col : 3 * col].astype(jnp.bfloat16)
        from_x = across(send_x, 1)
        from_y = across(send_y, 2)
        send_y2 = (partial[:, first, 2 * col : 3 * col] + from_x[:, :, col:]).astype(jnp.bfloat16)
        keep_first = partial[:, first, 3 * col :] + from_x[:, :, :col]
        send_x2 = (partial[:, second, :col] + from_y[:, :, :col]).astype(jnp.bfloat16)
        keep_second = partial[:, second, 3 * col :] + from_y[:, :, col:]
        from_y2 = across(send_y2, 2)
        from_x2 = across(send_x2, 1)
        finished.append(
            jnp.concatenate([keep_first + from_y2, keep_second + from_x2], axis=1).astype(
                jnp.bfloat16
            )
        )
    result = jnp.concatenate(finished, axis=2)
    return result[0], result[1]


def solution(mesh):
    in_specs = (
        P("seq", "kv"),
        P("seq", "kv"),
        P("seq", None, "kv"),
        P("seq", None, "kv"),
        P(),
        P(("kv", "seq"), None),
        P(("kv", "seq"), None),
    )
    out_specs = (P("seq", "kv"), P("seq", "kv"))
    return jax.shard_map(body, mesh=mesh, in_specs=in_specs, out_specs=out_specs, check_vma=False)
```

time: 302 us -> 180 us (0.60)
  waiting for transfers between devices: 193 us -> 99.6 us
  matrix products: 56.9 us -> 19.4 us
  Pallas kernels: 0 us -> 15.1 us
  other arithmetic: 17.5 us -> 6.57 us
  starting transfers between devices: 3.22 us -> 13.4 us
  local copies, waits for them, and re-layouts: 16.5 us -> 11.3 us
    reduce_scatter x2 -> x0, waiting for transfers between devices: 163 us -> none  [the longest x1 86.9 us: body(): lax.psum_scatter(partial_value, 'kv', scatter_dimension=1, tiled=True)]
    ppermute x1 -> x9, waiting for transfers between devices: 0.01 us -> 40.4 us  [the longest x8 39.8 us: across(): return lax.ppermute(block, 'kv', [(i, i ^ flip) for i in range(size)])]
    dot_general x9 -> x4, matrix products: 56.9 us -> 19.4 us  [the longest x2 12.4 us: project(): jnp.dot(pair[of], weights[:, columns], preferred_element_type=jnp.float32)]
    all_gather x2, waiting for transfers between devices: 29.2 us -> 59.2 us  [body(): whole = lax.all_gather(mine, 'seq', axis=1, tiled=True)]
    pallas_call x0 -> x1, Pallas kernels: none -> 15.1 us  [attention(): pl.pallas_call(functools.partial(attention_kernel, heads, head_dim), grid...]
    ppermute x1 -> x9, starting transfers between devices: 3.06 us -> 13.3 us  [the longest x8 10.8 us: across(): return lax.ppermute(block, 'kv', [(i, i ^ flip) for i in range(size)])]
    sub x2 -> x1, other arithmetic: 6.31 us -> 0.01 us  [body(): low = lower - (position // STRETCH * STRETCH - WINDOW)]
    convert_element_type x4 -> x2, other arithmetic: 5.47 us -> 0.88 us  [body(): (partial[:, first, 2 * col:3 * col] + from_x[:, :, col:]).astype(jnp.bflo...]
  transfers between devices with their start and end apart: 5 -> 11, of which waited for: 3 -> 7; matrix products, arithmetic and copies ran while one was open for 24% -> 15% of each run, Pallas kernels for 0% -> 8%
where the time goes in v1:
time: 180 us
  waiting for transfers between devices  99.6 us (55%)
  matrix products  19.4 us (11%)
  Pallas kernels  15.1 us (8%)
  between operations  14.5 us (8%)
  starting transfers between devices  13.4 us (7%)
  local copies, waits for them, and re-layouts  11.3 us (6%)
  other arithmetic  6.57 us (4%)
    all_gather x2, waiting for transfers between devices, body(): whole = lax.all_gather(mine, 'seq', axis=1, tiled=True)  59.2 us
    ppermute x8, waiting for transfers between devices, across(): return lax.ppermute(block, 'kv', [(i, i ^ flip) for i in range(size)])  39.8 us
    pallas_call x1, Pallas kernels, attention(): pl.pallas_call(functools.partial(attention_kernel, heads, head_dim), grid...  15.1 us
    dot_general x2, matrix products, project(): jnp.dot(pair[of], weights[:, columns], preferred_element_type=jnp.float32)  12.4 us
    ppermute x8, starting transfers between devices, across(): return lax.ppermute(block, 'kv', [(i, i ^ flip) for i in range(size)])  10.8 us
    dot_general x2, matrix products, project(): jnp.dot(pair[of, :width], weights[rows:, columns], preferred_element_type...  7.05 us
    unnamed x28, local copies, waits for them, and re-layouts  5.53 us
  transfers between devices with their start and end apart: 11, of which 7 were waited for; matrix products, arithmetic and copies ran while one was open for 15% of the time, Pallas kernels for 8%

profile of v1, /device:TPU:0, one launch (start us, length us, event | category | flops | bytes accessed | tf_op | source)
XLA Modules:
  0.0 179.9 jit_solution(4061392902720314476)
XLA Ops:
  7.2 1.3 copy.44
  8.5 1.3 copy.39
  10.0 0.1 copy.40
  10.1 0.1 copy.41
  10.3 0.1 copy.42
  10.4 0.1 copy.43
  11.2 0.8 pad_maximum_fusion.2
  12.2 0.8 pad_maximum_fusion.3
  13.0 0.7 fusion.41
  13.9 0.7 fusion.40
  14.7 0.7 pad_maximum_fusion.4
  15.4 2.5 %collective-permute-start = (bf16[224,512]{1,0:T(8,128)(2,1)}, bf16[224,512]{1,0:T(8,128)(2,1)S(1)}, u32[]{:S(2)}, u32[]{:S(2)}) collective-permute-start(bf16[224,512]{1,0:T(8,128)(2,1)} %pad_maximum_fusion.4), channel_id=1, source_target_pairs={{0,1},{1,2},{2,3},{3,4},{4,5},{5,6},{6,7},{8,9},{9,10},{10,11},{11... | collective-permute-start | bytes 688136 | tf_op jit(solution)/shard_map/ppermute | solution.py:136
  18.2 0.1 reduce
  18.3 0.1 select_reduce_fusion
  18.5 0.6 collective-permute-done
  19.1 0.1 maximum_maximum_fusion.1.ctx_ref
  19.2 0.2 broadcast_in_dim.13.low_ref
  19.4 1.6 copy-done.1
  21.0 15.1 %attention.1 = bf16[1024,2048]{1,0:T(8,128)(2,1)} custom-call(bf16[1024,1024]{1,0:T(8,128)(2,1)S(1)} %copy-done, bf16[1024,1024]{1,0:T(8,128)(2,1)S(1)} %copy-done.1, bf16[1248,512]{1,0:T(8,128)(2,1)S(1)} %maximum_maximum_fusion.1.ctx_ref, s32[1024,128]{1,0:T(8,128)S(1)} %broadcast_in_dim.13.low_ref), custom_call_target="tpu_custom_call" | custom-call | flops 3221225472 | bytes 10485760 | tf_op jit(solution)/shard_map/attention/pallas_call | solution.py:76
  36.1 25.9 %all-gather.3.cloned.1.call-done = bf16[2,1024,1024]{2,1,0:T(8,128)(2,1)} async-done(((bf16[2,128,1024]{2,1,0:T(8,128)(2,1)}), bf16[2,1024,1024]{2,1,0:T(8,128)(2,1)}) %all-gather.3.cloned.1.call-update) | async-done | bytes 4194320 | tf_op jit(solution)/shard_map/all_gather | solution.py:129
  62.1 4.7 %convolution_bitcast_fusion.3 = f32[1,1024,1024]{2,1,0:T(8,128)S(1)} fusion(bf16[2,1024,1024]{2,1,0:T(8,128)(2,1)} %all-gather.3.cloned.1.call-done, bf16[1024,2048]{1,0:T(8,128)(2,1)} %attention.1), kind=kOutput, calls=%fused_computation.23 | convolution fusion | flops 2147483648 | bytes 8388608 | tf_op jit(solution)/shard_map/dot_general | solution.py:159
  66.8 4.5 %convolution_bitcast_fusion.2 = f32[1,1024,1024]{2,1,0:T(8,128)S(1)} fusion(bf16[1024,2048]{1,0:T(8,128)(2,1)S(1)} %copy-done.11, bf16[2048,1024]{1,0:T(8,128)(2,1)S(1)} %bitcast.62), kind=kOutput, calls=%fused_computation.22 | convolution fusion | flops 4294967296 | bytes 12582912 | tf_op jit(solution)/shard_map/dot_general | solution.py:162
  71.3 0.7 fusion.1
  72.1 1.3 copy-done.4
  73.3 1.2 fusion.38
  74.5 1.5 collective-permute-start.1
  76.0 1.5 collective-permute-start.3
  77.4 33.2 %all-gather.5.cloned.1.call-done = bf16[2,1024,1024]{2,1,0:T(8,128)(2,1)} async-done(((bf16[2,128,1024]{2,1,0:T(8,128)(2,1)}), bf16[2,1024,1024]{2,1,0:T(8,128)(2,1)}) %all-gather.5.cloned.1.call-update) | async-done | bytes 4194320 | tf_op jit(solution)/shard_map/all_gather | solution.py:129
  110.7 7.9 %convolution_bitcast_fusion = f32[1,1024,1024]{2,1,0:T(8,128)S(1)} fusion(bf16[1024,2048]{1,0:T(8,128)(2,1)} %attention.1, bf16[2048,1024]{1,0:T(8,128)(2,1)} %bitcast.63), kind=kOutput, calls=%fused_computation.20 | convolution fusion | flops 4294967296 | bytes 12582912 | tf_op jit(solution)/shard_map/dot_general | solution.py:162
  118.6 2.3 %convolution_bitcast_fusion.1 = f32[1,1024,1024]{2,1,0:T(8,128)S(1)} fusion(bf16[2,1024,1024]{2,1,0:T(8,128)(2,1)S(1)} %copy-done.10, bf16[1024,2048]{1,0:T(8,128)(2,1)S(1)} %copy-done.12), kind=kOutput, calls=%fused_computation.21 | convolution fusion | flops 2147483648 | bytes 8388608 | tf_op jit(solution)/shard_map/dot_general | solution.py:159
  120.9 0.7 fusion
  121.7 0.1 fusion.39
  121.8 1.5 collective-permute-start.5
  123.4 1.5 collective-permute-start.7
  124.9 0.4 fusion.24
  125.3 1.2 collective-permute-start.2
  126.5 1.5 collective-permute-start.4
  128.0 19.9 %collective-permute-done.5 = bf16[2,512,512]{2,1,0:T(8,128)(2,1)S(1)} collective-permute-done((bf16[2,512,512]{2,1,0:T(8,128)(2,1)S(1)}, bf16[2,512,512]{2,1,0:T(8,128)(2,1)S(1)}, u32[]{:S(2)}, u32[]{:S(2)}) %collective-permute-start.5) | collective-permute-done | bytes 1048608 | tf_op jit(solution)/shard_map/ppermute | solution.py:97
  147.9 1.5 collective-permute-done.7
  149.4 0.4 fusion.10
  149.9 1.5 collective-permute-start.6
  151.4 0.6 collective-permute-start.8
  151.9 8.7 %collective-permute-done.2 = bf16[2,512,256]{2,1,0:T(8,128)(2,1)S(1)} collective-permute-done((bf16[2,512,256]{2,1,0:T(8,128)(2,1)S(1)}, bf16[2,512,256]{2,1,0:T(8,128)(2,1)S(1)}, u32[]{:S(2)}, u32[]{:S(2)}) %collective-permute-start.2) | collective-permute-done | bytes 524320 | tf_op jit(solution)/shard_map/ppermute | solution.py:97
  160.6 0.5 fusion.21
  161.2 9.7 %collective-permute-done.6 = bf16[2,512,256]{2,1,0:T(8,128)(2,1)S(1)} collective-permute-done((bf16[2,512,256]{2,1,0:T(8,128)(2,1)S(1)}, bf16[2,512,256]{2,1,0:T(8,128)(2,1)S(1)}, u32[]{:S(2)}, u32[]{:S(2)}) %collective-permute-start.6) | collective-permute-done | bytes 524320 | tf_op jit(solution)/shard_map/ppermute | solution.py:97
  170.9 0.5 fusion.7
  171.4 0.2 maximum_maximum_fusion
  171.6 1.5 slice_bitcast_fusion.4
  (56 shorter events, 1.3 us)
Async XLA Ops:
  7.2 54.9 %all-gather.3.cloned.1.call-start = ((), (), s32[]{:S(2)}) async-start(), calls=%async_computation | async-start | bytes 4718592 | tf_op jit(solution)/shard_map/all_gather | solution.py:129
  10.3 2.8 %copy-start.6 = (bf16[1024,2,128]{2,1,0:T(2,128)(2,1)S(1)}, bf16[1024,2,128]{2,1,0:T(2,128)(2,1)}, u32[]{:S(2)}) copy-start(bf16[1024,2,128]{2,1,0:T(2,128)(2,1)} %param.10) | copy-start | bytes 1572868
  11.1 2.7 %copy-start.7 = (bf16[1024,2,128]{2,1,0:T(2,128)(2,1)S(1)}, bf16[1024,2,128]{2,1,0:T(2,128)(2,1)}, u32[]{:S(2)}) copy-start(bf16[1024,2,128]{2,1,0:T(2,128)(2,1)} %param.9) | copy-start | bytes 1572868
  12.0 98.6 %all-gather.5.cloned.1.call-start = ((), (), s32[]{:S(2)}) async-start(), calls=%async_computation.1 | async-start | bytes 4718592 | tf_op jit(solution)/shard_map/all_gather | solution.py:129
  13.0 4.9 %copy-start.8 = (s32[64]{0:T(128)S(1)}, s32[64]{0:T(128)}, u32[]{:S(2)}) copy-start(s32[64]{0:T(128)} %param.11) | copy-start | bytes 772
  13.9 5.6 %copy-start = (bf16[1024,1024]{1,0:T(8,128)(2,1)S(1)}, bf16[1024,1024]{1,0:T(8,128)(2,1)}, u32[]{:S(2)}) copy-start(bf16[1024,1024]{1,0:T(8,128)(2,1)} %q_ref.1) | copy-start | bytes 6291460
  15.4 3.7 %collective-permute-start = (bf16[224,512]{1,0:T(8,128)(2,1)}, bf16[224,512]{1,0:T(8,128)(2,1)S(1)}, u32[]{:S(2)}, u32[]{:S(2)}) collective-permute-start(bf16[224,512]{1,0:T(8,128)(2,1)} %pad_maximum_fusion.4), channel_id=1, source_target_pairs={{0,1},{1,2},{2,3},{3,4},{4,5},{5,6},{6,7},{8,9},{9,10},{10,11},{11... | collective-permute-start | bytes 688136 | tf_op jit(solution)/shard_map/ppermute | solution.py:136
  19.4 1.6 copy-start.1
  62.1 4.7 %copy-start.9 = (bf16[2,1024,1024]{2,1,0:T(8,128)(2,1)S(1)}, bf16[2,1024,1024]{2,1,0:T(8,128)(2,1)}, u32[]{:S(2)}) copy-start(bf16[2,1024,1024]{2,1,0:T(8,128)(2,1)} %all-gather.3.cloned.1.call-done) | copy-start | bytes 12582916
  62.1 4.7 %copy-start.11 = (bf16[1024,2048]{1,0:T(8,128)(2,1)S(1)}, bf16[1024,2048]{1,0:T(8,128)(2,1)}, u32[]{:S(2)}) copy-start(bf16[1024,2048]{1,0:T(8,128)(2,1)} %attention.1) | copy-start | bytes 12582916
  66.8 4.5 %copy-start.2 = (f32[1,1024,1024]{2,1,0:T(8,128)}, f32[1,1024,1024]{2,1,0:T(8,128)S(1)}, u32[]{:S(2)}) copy-start(f32[1,1024,1024]{2,1,0:T(8,128)S(1)} %convolution_bitcast_fusion.3) | copy-start | bytes 12582916
  71.3 2.0 %copy-start.4 = (f32[1,1024,1024]{2,1,0:T(8,128)}, f32[1,1024,1024]{2,1,0:T(8,128)S(1)}, u32[]{:S(2)}) copy-start(f32[1,1024,1024]{2,1,0:T(8,128)S(1)} %convolution_bitcast_fusion.2) | copy-start | bytes 12582916
  74.5 50.3 %collective-permute-start.1 = (bf16[2,512,512]{2,1,0:T(8,128)(2,1)}, bf16[2,512,512]{2,1,0:T(8,128)(2,1)S(1)}, u32[]{:S(2)}, u32[]{:S(2)}) collective-permute-start(bf16[2,512,512]{2,1,0:T(8,128)(2,1)} %get-tuple-element.10), channel_id=1, source_target_pairs={{0,8},{8,0},{16,24},{24,16},{1,9},{9,1},{17,25},{25,17},{2,10},{10... | collective-permute-start | bytes 3145736 | tf_op jit(solution)/shard_map/ppermute | solution.py:97
  76.0 48.9 %collective-permute-start.3 = (bf16[2,512,512]{2,1,0:T(8,128)(2,1)S(1)}, bf16[2,512,512]{2,1,0:T(8,128)(2,1)S(1)}, u32[]{:S(2)}, u32[]{:S(2)}) collective-permute-start(bf16[2,512,512]{2,1,0:T(8,128)(2,1)S(1)} %get-tuple-element.11), channel_id=1, source_target_pairs={{0,16},{8,24},{16,0},{24,8},{1,17},{9,25},{17,1},{25,9},{2,18},{10... | collective-permute-start | bytes 3145736 | tf_op jit(solution)/shard_map/ppermute | solution.py:97
  110.7 7.9 %copy-start.10 = (bf16[2,1024,1024]{2,1,0:T(8,128)(2,1)S(1)}, bf16[2,1024,1024]{2,1,0:T(8,128)(2,1)}, u32[]{:S(2)}) copy-start(bf16[2,1024,1024]{2,1,0:T(8,128)(2,1)} %all-gather.5.cloned.1.call-done) | copy-start | bytes 12582916
  110.7 7.9 %copy-start.12 = (bf16[1024,2048]{1,0:T(8,128)(2,1)S(1)}, bf16[1024,2048]{1,0:T(8,128)(2,1)}, u32[]{:S(2)}) copy-start(bf16[1024,2048]{1,0:T(8,128)(2,1)} %attention.1) | copy-start | bytes 12582916
  120.9 3.9 %copy-start.5 = (f32[1,1024,1024]{2,1,0:T(8,128)S(1)}, f32[1,1024,1024]{2,1,0:T(8,128)}, u32[]{:S(2)}) copy-start(f32[1,1024,1024]{2,1,0:T(8,128)} %copy-done.4) | copy-start | bytes 12582916
  121.7 3.2 %copy-start.3 = (f32[1,1024,1024]{2,1,0:T(8,128)S(1)}, f32[1,1024,1024]{2,1,0:T(8,128)}, u32[]{:S(2)}) copy-start(f32[1,1024,1024]{2,1,0:T(8,128)} %copy-done.2) | copy-start | bytes 12582916
  121.8 26.1 %collective-permute-start.5 = (bf16[2,512,512]{2,1,0:T(8,128)(2,1)S(1)}, bf16[2,512,512]{2,1,0:T(8,128)(2,1)S(1)}, u32[]{:S(2)}, u32[]{:S(2)}) collective-permute-start(bf16[2,512,512]{2,1,0:T(8,128)(2,1)S(1)} %get-tuple-element.12), channel_id=1, source_target_pairs={{0,8},{8,0},{16,24},{24,16},{1,9},{9,1},{17,25},{25,17},{2,10},{10... | collective-permute-start | bytes 3145736 | tf_op jit(solution)/shard_map/ppermute | solution.py:97
  123.4 26.0 %collective-permute-start.7 = (bf16[2,512,512]{2,1,0:T(8,128)(2,1)S(1)}, bf16[2,512,512]{2,1,0:T(8,128)(2,1)S(1)}, u32[]{:S(2)}, u32[]{:S(2)}) collective-permute-start(bf16[2,512,512]{2,1,0:T(8,128)(2,1)S(1)} %get-tuple-element.13), channel_id=1, source_target_pairs={{0,16},{8,24},{16,0},{24,8},{1,17},{9,25},{17,1},{25,9},{2,18},{10... | collective-permute-start | bytes 3145736 | tf_op jit(solution)/shard_map/ppermute | solution.py:97
  125.3 35.3 %collective-permute-start.2 = (bf16[2,512,256]{2,1,0:T(8,128)(2,1)S(1)}, bf16[2,512,256]{2,1,0:T(8,128)(2,1)S(1)}, u32[]{:S(2)}, u32[]{:S(2)}) collective-permute-start(bf16[2,512,256]{2,1,0:T(8,128)(2,1)S(1)} %get-tuple-element.4), channel_id=1, source_target_pairs={{0,16},{8,24},{16,0},{24,8},{1,17},{9,25},{17,1},{25,9},{2,18},{10... | collective-permute-start | bytes 1572872 | tf_op jit(solution)/shard_map/ppermute | solution.py:97
  126.5 34.1 %collective-permute-start.4 = (bf16[2,512,256]{2,1,0:T(8,128)(2,1)S(1)}, bf16[2,512,256]{2,1,0:T(8,128)(2,1)S(1)}, u32[]{:S(2)}, u32[]{:S(2)}) collective-permute-start(bf16[2,512,256]{2,1,0:T(8,128)(2,1)S(1)} %get-tuple-element.5), channel_id=1, source_target_pairs={{0,8},{8,0},{16,24},{24,16},{1,9},{9,1},{17,25},{25,17},{2,10},{10... | collective-permute-start | bytes 1572872 | tf_op jit(solution)/shard_map/ppermute | solution.py:97
  149.9 21.0 %collective-permute-start.6 = (bf16[2,512,256]{2,1,0:T(8,128)(2,1)S(1)}, bf16[2,512,256]{2,1,0:T(8,128)(2,1)S(1)}, u32[]{:S(2)}, u32[]{:S(2)}) collective-permute-start(bf16[2,512,256]{2,1,0:T(8,128)(2,1)S(1)} %get-tuple-element.8), channel_id=1, source_target_pairs={{0,16},{8,24},{16,0},{24,8},{1,17},{9,25},{17,1},{25,9},{2,18},{10... | collective-permute-start | bytes 1572872 | tf_op jit(solution)/shard_map/ppermute | solution.py:97
  151.4 19.5 %collective-permute-start.8 = (bf16[2,512,256]{2,1,0:T(8,128)(2,1)S(1)}, bf16[2,512,256]{2,1,0:T(8,128)(2,1)S(1)}, u32[]{:S(2)}, u32[]{:S(2)}) collective-permute-start(bf16[2,512,256]{2,1,0:T(8,128)(2,1)S(1)} %get-tuple-element.9), channel_id=1, source_target_pairs={{0,8},{8,0},{16,24},{24,16},{1,9},{9,1},{17,25},{25,17},{2,10},{10... | collective-permute-start | bytes 1572872 | tf_op jit(solution)/shard_map/ppermute | solution.py:97
Sparse Core Ops, SparseCore 0:
  12.2 49.8 all-gather.2
  64.2 46.3 all-gather.4

commit v2 on v1

v2 whole, which is shorter than its diff:
```python
import functools
import math

import jax
import jax.numpy as jnp
from jax import lax
from jax.experimental import pallas as pl
from jax.experimental.pallas import tpu as pltpu
from jax.sharding import PartitionSpec as P

STRETCH = 32
WINDOW = 224
CHUNKS = 4
TILE = 128
CORES = 2
RELATIVE = (1, 3, 2, 0)

masked_score = -1e30
vmem_bytes = 48 * 1024 * 1024


def arrange_kernel(kv_ref, tangent_ref, value_ref, *chunk_refs):
    columns = tangent_ref.shape[1] // len(RELATIVE)
    part = columns // len(chunk_refs)
    for chunk, chunk_ref in enumerate(chunk_refs):
        for place, flip in enumerate(RELATIVE):
            start = pl.multiple_of((kv_ref[0] ^ flip) * columns + chunk * part, part)
            to = slice(place * part, (place + 1) * part)
            chunk_ref[0, :, to] = tangent_ref[:, pl.ds(start, part)]
            chunk_ref[1, :, to] = value_ref[:, pl.ds(start, part)]


def arrange(kv_index, tangent, value):
    rows, columns = value.shape
    shape = jax.ShapeDtypeStruct((2, rows, columns // CHUNKS), value.dtype)
    return pl.pallas_call(
        arrange_kernel,
        in_specs=[
            pl.BlockSpec(memory_space=pltpu.SMEM),
            pl.BlockSpec(memory_space=pltpu.VMEM),
            pl.BlockSpec(memory_space=pltpu.VMEM),
        ],
        out_specs=[pl.BlockSpec(memory_space=pltpu.VMEM)] * CHUNKS,
        out_shape=[shape] * CHUNKS,
        name="arrange",
    )(kv_index.reshape(1), tangent, value)


def attention_kernel(heads, head_dim, offset, order_ref, q_ref, qt_ref, ctx_ref, low_ref, out_ref):
    rows = q_ref.shape[0]
    span = WINDOW + STRETCH
    width = heads * head_dim
    score_scale = 1.0 / math.sqrt(head_dim)
    to_log2 = score_scale * math.log2(math.e)
    step = pl.program_id(0)
    transposed = (((1,), (1,)), ((), ()))
    column = lax.broadcasted_iota(jnp.int32, (STRETCH, span), 1)
    row = lax.broadcasted_iota(jnp.int32, (STRETCH, span), 0)
    causal = column <= row + WINDOW
    starts = [pl.multiple_of(order_ref[h] * head_dim, head_dim) for h in range(heads)]
    for part in range(rows // STRETCH):
        here = slice(part * STRETCH, (part + 1) * STRETCH)
        base = pl.multiple_of(offset + step * rows + part * STRETCH, STRETCH)
        keys = ctx_ref[pl.ds(base, span), : 2 * head_dim]
        values = ctx_ref[pl.ds(base, span), 2 * head_dim :]
        low = low_ref[here, :]
        low = jnp.concatenate([low] * (span // low.shape[1]), axis=1)
        admitted = causal & (column >= low)
        q = jnp.concatenate([q_ref[here, pl.ds(start, head_dim)] for start in starts], axis=0)
        qt = jnp.concatenate([qt_ref[here, pl.ds(start, head_dim)] for start in starts], axis=0)
        scores = lax.dot_general(
            q, keys[:, :head_dim], transposed, preferred_element_type=jnp.float32
        )
        tangent = lax.dot_general(
            jnp.concatenate([qt, q], axis=1), keys, transposed, preferred_element_type=jnp.float32
        )
        scores = scores.reshape(heads, STRETCH, span)
        tangent = tangent.reshape(heads, STRETCH, span)
        scores = jnp.where(admitted[None], scores, masked_score)
        peak = jnp.max(scores, axis=-1, keepdims=True)
        exponent = jnp.exp2((scores - peak) * to_log2)
        inverse = 1.0 / jnp.sum(exponent, axis=-1, keepdims=True)
        mean = jnp.sum(exponent * tangent, axis=-1, keepdims=True) * inverse
        prob = exponent * inverse
        prob_low = prob.astype(jnp.bfloat16).reshape(heads * STRETCH, span)
        tan_low = (prob * ((tangent - mean) * score_scale)).astype(jnp.bfloat16)
        tan_low = tan_low.reshape(heads * STRETCH, span)
        both = jnp.dot(prob_low, values, preferred_element_type=jnp.float32)
        more = jnp.dot(tan_low, values[:, :head_dim], preferred_element_type=jnp.float32)
        out = both[:, :head_dim].astype(jnp.bfloat16)
        out_tan = (both[:, head_dim:] + more).astype(jnp.bfloat16)
        for h in range(heads):
            of = slice(h * STRETCH, (h + 1) * STRETCH)
            out_ref[here, h * head_dim : (h + 1) * head_dim] = out[of]
            out_ref[here, width + h * head_dim : width + (h + 1) * head_dim] = out_tan[of]


def attention(half, order, queries, query_tangent, context, low):
    tokens, width = queries.shape[0] // 2, queries.shape[1]
    head_dim = context.shape[1] // 4
    heads = width // head_dim
    elements = tokens * heads * (WINDOW + STRETCH)
    steps = tokens // TILE
    offset = context.shape[0] - tokens - WINDOW
    return pl.pallas_call(
        functools.partial(attention_kernel, heads, head_dim, offset),
        grid=(steps,),
        in_specs=[
            pl.BlockSpec(memory_space=pltpu.SMEM),
            pl.BlockSpec((TILE, width), lambda i: (half * steps + i, 0)),
            pl.BlockSpec((TILE, width), lambda i: (half * steps + i, 0)),
            pl.BlockSpec(context.shape, lambda i: (0, 0)),
            pl.BlockSpec((TILE, low.shape[1]), lambda i: (half * steps + i, 0)),
        ],
        out_specs=pl.BlockSpec((TILE, 2 * width), lambda i: (i, 0)),
        out_shape=jax.ShapeDtypeStruct((tokens, 2 * width), jnp.bfloat16),
        compiler_params=pltpu.CompilerParams(vmem_limit_bytes=vmem_bytes),
        cost_estimate=pl.CostEstimate(
            flops=elements, bytes_accessed=tokens, transcendentals=0
        ),
        name="attention",
    )(order, queries, query_tangent, context, low)


def project_kernel(sent, kept, pair_ref, near_ref, far_ref, send_ref, keep_ref):
    depth = near_ref.shape[1]
    part = near_ref.shape[2] // len(RELATIVE)
    dot = functools.partial(jnp.dot, preferred_element_type=jnp.float32)
    near, near_tan = pair_ref[:, :depth], pair_ref[:, 2 * depth : 3 * depth]
    far, far_tan = pair_ref[:, depth : 2 * depth], pair_ref[:, 3 * depth :]
    value = dot(near, near_ref[1]) + dot(far, far_ref[1])
    tangent = dot(near, near_ref[0]) + dot(far, far_ref[0])
    tangent = tangent + dot(near_tan, near_ref[1]) + dot(far_tan, far_ref[1])
    for ref, flips in ((send_ref, sent), (keep_ref, kept)):
        for place, flip in enumerate(flips):
            at = RELATIVE.index(flip) * part
            to = slice(place * part, (place + 1) * part)
            ref[0, :, to] = value[:, at : at + part].astype(ref.dtype)
            ref[1, :, to] = tangent[:, at : at + part].astype(ref.dtype)


def project(sent, kept, pair, near, far):
    tokens, width = pair.shape
    tile = min(2 * TILE, tokens)
    steps = tokens // tile
    columns = near.shape[2]
    out = (2, tokens, columns // 2)
    block = pl.BlockSpec((2, tile, columns // 2), lambda i: (0, i, 0))
    return pl.pallas_call(
        functools.partial(project_kernel, sent, kept),
        grid=(steps,),
        in_specs=[
            pl.BlockSpec((tile, width), lambda i: (i, 0)),
            pl.BlockSpec(near.shape, lambda i: (0, 0, 0)),
            pl.BlockSpec(far.shape, lambda i: (0, 0, 0)),
        ],
        out_specs=[block, block],
        out_shape=[
            jax.ShapeDtypeStruct(out, jnp.bfloat16),
            jax.ShapeDtypeStruct(out, jnp.float32),
        ],
        compiler_params=pltpu.CompilerParams(vmem_limit_bytes=vmem_bytes),
        cost_estimate=pl.CostEstimate(
            flops=tokens * columns, bytes_accessed=tokens, transcendentals=0
        ),
        name="project",
    )(pair, near, far)


def across(block, flip):
    size = lax.axis_size("kv")
    return lax.ppermute(block, "kv", [(i, i ^ flip) for i in range(size)])


def along(block, chips):
    size = lax.axis_size("seq")
    return lax.ppermute(block, "seq", [(i, (i + CORES * chips) % size) for i in range(size)])


def other_core(block):
    return lax.ppermute(block, "seq", [(i, i ^ 1) for i in range(lax.axis_size("seq"))])


def hold(block, *until):
    return lax.optimization_barrier((block, *until))[0]


class Gather:
    def __init__(self, mine, chips):
        self.ahead, self.behind = [mine], [mine]
        self.forward, self.backward = chips // 2, (chips - 1) // 2

    def neighbours(self, *until):
        mine = hold(self.ahead[0], *until) if until else self.ahead[0]
        if self.forward:
            self.ahead.append(along(mine, 1))
        if self.backward:
            self.behind.append(along(mine, -1))

    def farther(self, *until):
        for _ in range(self.forward - 1):
            self.ahead.append(along(hold(self.ahead[-1], *until), 1))
        for _ in range(self.backward - 1):
            self.behind.append(along(hold(self.behind[-1], *until), -1))

    def finish(self):
        near = jnp.concatenate(self.ahead + self.behind[:0:-1], axis=1)
        return near, other_core(near)


def body(
    queries, query_tangent, key_value, key_value_tangents, doc_lengths, out_weight, weight_tangent
):
    tokens, width = queries.shape
    head_dim = key_value.shape[2]
    heads = width // head_dim
    half = tokens // 2
    seq_index = lax.axis_index("seq")
    kv_index = lax.axis_index("kv")
    seq_size = lax.axis_size("seq")
    chips = seq_size // CORES

    stacked = jnp.concatenate(
        [key_value[:, 0], key_value_tangents[:, 0], key_value[:, 1], key_value_tangents[:, 1]],
        axis=1,
    )
    prior = lax.ppermute(
        stacked[tokens - WINDOW :], "seq", [(i, i + 1) for i in range(seq_size - 1)]
    )
    context = jnp.concatenate([prior, stacked[:half]], axis=0)

    mine = arrange(kv_index, weight_tangent, out_weight)
    gathers = [Gather(block, chips) for block in mine]
    gathers[0].neighbours()
    gathers[1].neighbours()

    doc_ends = jnp.cumsum(doc_lengths)
    doc_starts = doc_ends - doc_lengths
    position = seq_index * tokens + jnp.arange(tokens, dtype=jnp.int32)
    inside = (doc_starts[None, :] <= position[:, None]) & (position[:, None] < doc_ends[None, :])
    doc_first = jnp.sum(jnp.where(inside, doc_starts[None, :], 0), axis=1)
    lower = jnp.maximum(doc_first, position - WINDOW + 1)
    low = lower - (position // STRETCH * STRETCH - WINDOW)
    low = jnp.broadcast_to(low[:, None], (tokens, 128))

    step = jnp.arange(chips, dtype=jnp.int32)
    chip, core = seq_index // CORES, seq_index % CORES
    owner = (chip - step + chips) % chips * CORES
    order = jnp.concatenate([owner + core, owner + 1 - core])
    whole_heads = order.shape[0] == heads

    def attend(part, context):
        heads_order = order if whole_heads else jnp.arange(heads, dtype=jnp.int32)
        pair = attention(part, heads_order, queries, query_tangent, context, low)
        if not whole_heads:
            pair = jnp.take(pair.reshape(half, 2, seq_size, -1), order, axis=2)
            pair = pair.reshape(half, 2 * width)
        return pair

    pair_second = attend(1, stacked)
    gathers[0].farther(pair_second)
    pair_first = attend(0, hold(context, pair_second))
    gathers[2].neighbours(pair_first)
    gathers[1].farther(pair_first)

    def first_stage(near, far, *until):
        pair = hold(pair_first, *until) if until else pair_first
        send_x, keep_x = project((1, 3), (2, 0), pair, near, far)
        from_x = across(send_x, 1)
        pair = hold(pair_second, send_x)
        send_y, keep_y = project((2, 3), (1, 0), pair, near, far)
        from_y = across(send_y, 2)
        return keep_x, from_x, keep_y, from_y

    def second_stage(keep_x, from_x, keep_y, from_y):
        part = keep_x.shape[2] // 2
        send_y2 = (keep_x[:, :, :part] + from_x[:, :, part:]).astype(jnp.bfloat16)
        from_y2 = across(send_y2, 2)
        send_x2 = (keep_y[:, :, :part] + from_y[:, :, part:]).astype(jnp.bfloat16)
        from_x2 = across(send_x2, 1)
        first = keep_x[:, :, part:] + from_x[:, :, :part] + from_y2
        second = keep_y[:, :, part:] + from_y[:, :, :part] + from_x2
        return jnp.concatenate([first, second], axis=1).astype(jnp.bfloat16)

    staged = []
    for chunk, gathering in enumerate(gathers):
        near, far = gathering.finish()
        now = first_stage(near, far)
        staged.append(now)
        if chunk + 1 < CHUNKS and chunk:
            gathers[chunk + 1].farther(now[0])
        if chunk + 3 < CHUNKS:
            gathers[chunk + 3].neighbours(now[0])
        if chunk:
            last = staged[chunk - 1]
            staged[chunk - 1] = (last[0], hold(last[1], now[0]), last[2], hold(last[3], now[2]))

    finished = [second_stage(*now) for now in staged]
    result = jnp.concatenate(finished, axis=2)
    return result[0], result[1]


def solution(mesh):
    in_specs = (
        P("seq", "kv"),
        P("seq", "kv"),
        P("seq", None, "kv"),
        P("seq", None, "kv"),
        P(),
        P(("kv", "seq"), None),
        P(("kv", "seq"), None),
    )
    out_specs = (P("seq", "kv"), P("seq", "kv"))
    return jax.shard_map(body, mesh=mesh, in_specs=in_specs, out_specs=out_specs, check_vma=False)
```

time: 180 us -> 178 us (0.989)
  starting transfers between devices: 13.4 us -> 36.3 us
  Pallas kernels: 15.1 us -> 36.7 us
  matrix products: 19.4 us -> 0 us
  waiting for transfers between devices: 99.6 us -> 85.9 us
  between operations: 14.5 us -> 1.17 us
  local copies, waits for them, and re-layouts: 11.3 us -> 6.83 us
  other arithmetic: 6.57 us -> 10.6 us
    all_gather x2 -> x0, waiting for transfers between devices: 59.2 us -> none  [body(): whole = lax.all_gather(mine, 'seq', axis=1, tiled=True)]
    ppermute x0 -> x16, waiting for transfers between devices: none -> 53.9 us  [the longest x12 53.9 us: along(): lax.ppermute(block, 'seq', [(i, (i + CORES * chips) % size) for i in rang...]
    pallas_call x1 -> x11, Pallas kernels: 15.1 us -> 36.7 us  [the longest x8 17.9 us: project(): pl.pallas_call(functools.partial(project_kernel, sent, kept), grid=(steps...]
    dot_general x4 -> x0, matrix products: 19.4 us -> none  [the longest x2 12.4 us: project(): jnp.dot(pair[of], weights[:, columns], preferred_element_type=jnp.float32)]
    ppermute x0 -> x16, starting transfers between devices: none -> 17.2 us  [the longest x12 16.8 us: along(): lax.ppermute(block, 'seq', [(i, (i + CORES * chips) % size) for i in rang...]
    ppermute x8 -> x16, waiting for transfers between devices: 39.8 us -> 32 us  [across(): return lax.ppermute(block, 'kv', [(i, i ^ flip) for i in range(size)])]
    ppermute x8 -> x16, starting transfers between devices: 10.8 us -> 16 us  [across(): return lax.ppermute(block, 'kv', [(i, i ^ flip) for i in range(size)])]
    unnamed x28 -> x30, local copies, waits for them, and re-layouts: 5.53 us -> 1.22 us
  transfers between devices with their start and end apart: 11 -> 33, of which waited for: 7 -> 18; matrix products, arithmetic and copies ran while one was open for 15% -> 7% of each run, Pallas kernels for 8% -> 21%
where the time goes in v2:
time: 178 us
  waiting for transfers between devices  85.9 us (48%)
  Pallas kernels  36.7 us (21%)
  starting transfers between devices  36.3 us (20%)
  other arithmetic  10.6 us (6%)
  local copies, waits for them, and re-layouts  6.83 us (4%)
    ppermute x12, waiting for transfers between devices, along(): lax.ppermute(block, 'seq', [(i, (i + CORES * chips) % size) for i in rang...  53.9 us
    ppermute x16, waiting for transfers between devices, across(): return lax.ppermute(block, 'kv', [(i, i ^ flip) for i in range(size)])  32 us
    pallas_call x8, Pallas kernels, project(): pl.pallas_call(functools.partial(project_kernel, sent, kept), grid=(steps...  17.9 us
    ppermute x12, starting transfers between devices, along(): lax.ppermute(block, 'seq', [(i, (i + CORES * chips) % size) for i in rang...  16.8 us
    pallas_call x2, Pallas kernels, attention(): pl.pallas_call(functools.partial(attention_kernel, heads, head_dim, offse...  16.4 us
    ppermute x16, starting transfers between devices, across(): return lax.ppermute(block, 'kv', [(i, i ^ flip) for i in range(size)])  16 us
    another operation x10, other arithmetic  4.71 us
  transfers between devices with their start and end apart: 33, of which 18 were waited for; matrix products, arithmetic and copies ran while one was open for 7% of the time, Pallas kernels for 21%

profile of v2, /device:TPU:0, one launch (start us, length us, event | category | flops | bytes accessed | tf_op | source)
XLA Modules:
  0.0 177.5 jit_solution(11927400011299831381)
XLA Ops:
  0.6 2.2 %fusion.8 = (bf16[1024,1,128]{2,1,0:T(2,128)(2,1)S(1)}, bf16[1024,1,128]{2,1,0:T(2,128)(2,1)S(1)}) fusion(bf16[1024,2,128]{2,1,0:T(2,128)(2,1)} %param.9), kind=kLoop, calls=%fused_computation.62 | loop fusion | bytes 1048576 | tf_op jit(solution)/shard_map/slice | solution.py:224
  4.6 3.1 %collective-permute-start = (bf16[224,512]{1,0:T(8,128)(2,1)}, bf16[224,512]{1,0:T(8,128)(2,1)}, u32[]{:S(2)}, u32[]{:S(2)}) collective-permute-start(bf16[224,512]{1,0:T(8,128)(2,1)} %slice.160), channel_id=1, source_target_pairs={{0,1},{1,2},{2,3},{3,4},{4,5},{5,6},{6,7},{8,9},{9,10},{10,11},{11... | collective-permute-start | bytes 688136 | tf_op jit(solution)/shard_map/ppermute | solution.py:227
  7.6 2.5 %arrange.1 = (bf16[2,128,512]{2,1,0:T(8,128)(2,1)}, bf16[2,128,512]{2,1,0:T(8,128)(2,1)}, bf16[2,128,512]{2,1,0:T(8,128)(2,1)}, bf16[2,128,512]{2,1,0:T(8,128)(2,1)}) custom-call(s32[1]{0:T(128)} %bitcast.5.kv_ref, bf16[128,2048]{1,0:T(8,128)(2,1)} %tangent_ref.1, bf16[128,2048]{1,0:T(8,128)(2,1)} %value_ref.1), custom_call_target="tpu_custom_call" | custom-call | tf_op jit(solution)/shard_map/arrange/pallas_call | solution.py:36
  10.1 1.9 %collective-permute-start.6 = (bf16[2,128,512]{2,1,0:T(8,128)(2,1)}, bf16[2,128,512]{2,1,0:T(8,128)(2,1)S(1)}, u32[]{:S(2)}, u32[]{:S(2)}) collective-permute-start(bf16[2,128,512]{2,1,0:T(8,128)(2,1)} %get-tuple-element.44), channel_id=1, source_target_pairs={{0,2},{1,3},{2,4},{3,5},{4,6},{5,7},{6,0},{7,1},{8,10},{9,11},{10,... | collective-permute-start | bytes 786440 | tf_op jit(solution)/shard_map/ppermute | solution.py:177
  12.8 8.2 %attention.2.pair_ref = bf16[512,2048]{1,0:T(8,128)(2,1)S(1)} custom-call(s32[8]{0:T(128)S(1)} %pad_add_fusion.order_ref, bf16[1024,1024]{1,0:T(8,128)(2,1)S(1)} %copy-done, bf16[1024,1024]{1,0:T(8,128)(2,1)} %qt_ref.3, bf16[1024,512]{1,0:T(8,128)(2,1)S(1)} %pad_maximum_fusion.ctx_ref, s32[1024,128]{1,0:T(8,128)S(1)} %broadcast_in_dim.13.low_ref), custom_call_target="tpu_custom_call" | custom-call | flops 1048576 | bytes 512 | tf_op jit(solution)/shard_map/attention/pallas_call | solution.py:105
  22.0 8.2 %attention.3.pair_ref = bf16[512,2048]{1,0:T(8,128)(2,1)S(1)} custom-call(s32[8]{0:T(128)S(1)} %pad_add_fusion.order_ref, bf16[1024,1024]{1,0:T(8,128)(2,1)S(1)} %copy-done, bf16[1024,1024]{1,0:T(8,128)(2,1)} %qt_ref.3, bf16[736,512]{1,0:T(8,128)(2,1)S(1)} %pad_maximum_fusion.1.ctx_ref, s32[1024,128]{1,0:T(8,128)S(1)} %broadcast_in_dim.13.low_ref), custom_call_target="tpu_custom_call" | custom-call | flops 1048576 | bytes 512 | tf_op jit(solution)/shard_map/attention/pallas_call | solution.py:105
  30.3 1.7 collective-permute-start.7
  31.9 2.2 %collective-permute-start.8 = (bf16[2,128,512]{2,1,0:T(8,128)(2,1)S(1)}, bf16[2,128,512]{2,1,0:T(8,128)(2,1)S(1)}, u32[]{:S(2)}, u32[]{:S(2)}) collective-permute-start(bf16[2,128,512]{2,1,0:T(8,128)(2,1)S(1)} %copy-done.7), channel_id=1, source_target_pairs={{0,6},{1,7},{2,0},{3,1},{4,2},{5,3},{6,4},{7,5},{8,14},{9,15},{10,... | collective-permute-start | bytes 786440 | tf_op jit(solution)/shard_map/ppermute | solution.py:177
  34.2 6.9 %collective-permute-done.7 = bf16[2,128,512]{2,1,0:T(8,128)(2,1)S(1)} collective-permute-done((bf16[2,128,512]{2,1,0:T(8,128)(2,1)S(1)}, bf16[2,128,512]{2,1,0:T(8,128)(2,1)S(1)}, u32[]{:S(2)}, u32[]{:S(2)}) %collective-permute-start.7) | collective-permute-done | bytes 262176 | tf_op jit(solution)/shard_map/ppermute | solution.py:177
  41.1 5.5 %collective-permute-done.8 = bf16[2,128,512]{2,1,0:T(8,128)(2,1)S(1)} collective-permute-done((bf16[2,128,512]{2,1,0:T(8,128)(2,1)S(1)}, bf16[2,128,512]{2,1,0:T(8,128)(2,1)S(1)}, u32[]{:S(2)}, u32[]{:S(2)}) %collective-permute-start.8) | collective-permute-done | bytes 262176 | tf_op jit(solution)/shard_map/ppermute | solution.py:177
  47.4 9.8 %collective-permute-done.1 = bf16[2,128,512]{2,1,0:T(8,128)(2,1)S(1)} collective-permute-done((bf16[2,128,512]{2,1,0:T(8,128)(2,1)S(1)}, bf16[2,128,512]{2,1,0:T(8,128)(2,1)S(1)}, u32[]{:S(2)}, u32[]{:S(2)}) %collective-permute-start.1) | collective-permute-done | bytes 262176 | tf_op jit(solution)/shard_map/ppermute | solution.py:177
  57.2 3.8 %collective-permute-start.3 = (bf16[2,128,512]{2,1,0:T(8,128)(2,1)S(1)}, bf16[2,128,512]{2,1,0:T(8,128)(2,1)S(1)}, u32[]{:S(2)}, u32[]{:S(2)}) collective-permute-start(bf16[2,128,512]{2,1,0:T(8,128)(2,1)S(1)} %copy-done.6), channel_id=1, source_target_pairs={{0,6},{1,7},{2,0},{3,1},{4,2},{5,3},{6,4},{7,5},{8,14},{9,15},{10,... | collective-permute-start | bytes 786440 | tf_op jit(solution)/shard_map/ppermute | solution.py:177
  61.2 7.1 %collective-permute-done.2 = bf16[2,128,512]{2,1,0:T(8,128)(2,1)S(1)} collective-permute-done((bf16[2,128,512]{2,1,0:T(8,128)(2,1)S(1)}, bf16[2,128,512]{2,1,0:T(8,128)(2,1)S(1)}, u32[]{:S(2)}, u32[]{:S(2)}) %collective-permute-start.2) | collective-permute-done | bytes 262176 | tf_op jit(solution)/shard_map/ppermute | solution.py:177
  68.3 2.3 %collective-permute-done.3 = bf16[2,128,512]{2,1,0:T(8,128)(2,1)S(1)} collective-permute-done((bf16[2,128,512]{2,1,0:T(8,128)(2,1)S(1)}, bf16[2,128,512]{2,1,0:T(8,128)(2,1)S(1)}, u32[]{:S(2)}, u32[]{:S(2)}) %collective-permute-start.3) | collective-permute-done | bytes 262176 | tf_op jit(solution)/shard_map/ppermute | solution.py:177
  70.7 2.1 %project.9 = (bf16[2,512,256]{2,1,0:T(8,128)(2,1)S(1)}, f32[2,512,256]{2,1,0:T(8,128)S(1)}) custom-call(bf16[512,2048]{1,0:T(8,128)(2,1)S(1)} %attention.3.pair_ref, bf16[2,512,512]{2,1,0:T(8,128)(2,1)S(1)} %constant_dynamic-update-slice_fusion.4.near_ref, bf16[2,512,512]{2,1,0:T(8,128)(2,1)S(1)} %collective-permute-done.9.far_ref), custom_call_target="tpu_custom_call" | custom-call | flops 262144 | bytes 512 | tf_op jit(solution)/shard_map/project/pallas_call | solution.py:149
  72.8 5.3 %collective-permute-done.14 = bf16[2,128,512]{2,1,0:T(8,128)(2,1)S(1)} collective-permute-done((bf16[2,128,512]{2,1,0:T(8,128)(2,1)S(1)}, bf16[2,128,512]{2,1,0:T(8,128)(2,1)S(1)}, u32[]{:S(2)}, u32[]{:S(2)}) %collective-permute-start.14) | collective-permute-done | bytes 262176 | tf_op jit(solution)/shard_map/ppermute | solution.py:177
  78.1 3.8 %collective-permute-start.16 = (bf16[2,128,512]{2,1,0:T(8,128)(2,1)S(1)}, bf16[2,128,512]{2,1,0:T(8,128)(2,1)S(1)}, u32[]{:S(2)}, u32[]{:S(2)}) collective-permute-start(bf16[2,128,512]{2,1,0:T(8,128)(2,1)S(1)} %copy-done.5), channel_id=1, source_target_pairs={{0,6},{1,7},{2,0},{3,1},{4,2},{5,3},{6,4},{7,5},{8,14},{9,15},{10,... | collective-permute-start | bytes 786440 | tf_op jit(solution)/shard_map/ppermute | solution.py:177
  81.9 7.2 %collective-permute-done.15 = bf16[2,128,512]{2,1,0:T(8,128)(2,1)S(1)} collective-permute-done((bf16[2,128,512]{2,1,0:T(8,128)(2,1)S(1)}, bf16[2,128,512]{2,1,0:T(8,128)(2,1)S(1)}, u32[]{:S(2)}, u32[]{:S(2)}) %collective-permute-start.15) | collective-permute-done | bytes 262176 | tf_op jit(solution)/shard_map/ppermute | solution.py:177
  89.1 1.5 collective-permute-done.16
  90.7 2.1 %project.8 = (bf16[2,512,256]{2,1,0:T(8,128)(2,1)S(1)}, f32[2,512,256]{2,1,0:T(8,128)S(1)}) custom-call(bf16[512,2048]{1,0:T(8,128)(2,1)S(1)} %attention.3.pair_ref, bf16[2,512,512]{2,1,0:T(8,128)(2,1)S(1)} %constant_dynamic-update-slice_fusion.near_ref, bf16[2,512,512]{2,1,0:T(8,128)(2,1)S(1)} %collective-permute-done.4.far_ref), custom_call_target="tpu_custom_call" | custom-call | flops 262144 | bytes 512 | tf_op jit(solution)/shard_map/project/pallas_call | solution.py:149
  92.8 1.5 collective-permute-start.5
  95.0 2.7 %project.10 = (bf16[2,512,256]{2,1,0:T(8,128)(2,1)}, f32[2,512,256]{2,1,0:T(8,128)S(1)}) custom-call(bf16[512,2048]{1,0:T(8,128)(2,1)S(1)} %attention.2.pair_ref, bf16[2,512,512]{2,1,0:T(8,128)(2,1)S(1)} %constant_dynamic-update-slice_fusion.near_ref, bf16[2,512,512]{2,1,0:T(8,128)(2,1)S(1)} %collective-permute-done.4.far_ref), custom_call_target="tpu_custom_call" | custom-call | flops 262144 | bytes 512 | tf_op jit(solution)/shard_map/project/pallas_call | solution.py:149
  97.7 1.5 collective-permute-start.11
  99.9 2.7 %project.11 = (bf16[2,512,256]{2,1,0:T(8,128)(2,1)}, f32[2,512,256]{2,1,0:T(8,128)S(1)}) custom-call(bf16[512,2048]{1,0:T(8,128)(2,1)S(1)} %attention.2.pair_ref, bf16[2,512,512]{2,1,0:T(8,128)(2,1)S(1)} %constant_dynamic-update-slice_fusion.4.near_ref, bf16[2,512,512]{2,1,0:T(8,128)(2,1)S(1)} %collective-permute-done.9.far_ref), custom_call_target="tpu_custom_call" | custom-call | flops 262144 | bytes 512 | tf_op jit(solution)/shard_map/project/pallas_call | solution.py:149
  102.6 2.0 %collective-permute-done.22 = bf16[2,128,512]{2,1,0:T(8,128)(2,1)} collective-permute-done((bf16[2,128,512]{2,1,0:T(8,128)(2,1)S(1)}, bf16[2,128,512]{2,1,0:T(8,128)(2,1)}, u32[]{:S(2)}, u32[]{:S(2)}) %collective-permute-start.22) | collective-permute-done | bytes 262176 | tf_op jit(solution)/shard_map/ppermute | solution.py:177
  104.6 1.1 collective-permute-start.24
  107.7 1.5 collective-permute-start.19
  109.2 2.1 %project.12 = (bf16[2,512,256]{2,1,0:T(8,128)(2,1)S(1)}, f32[2,512,256]{2,1,0:T(8,128)S(1)}) custom-call(bf16[512,2048]{1,0:T(8,128)(2,1)S(1)} %attention.3.pair_ref, bf16[2,512,512]{2,1,0:T(8,128)(2,1)S(1)} %constant_dynamic-update-slice_fusion.8.near_ref, bf16[2,512,512]{2,1,0:T(8,128)(2,1)S(1)} %collective-permute-done.17.far_ref), custom_call_target="tpu_custom_call" | custom-call | flops 262144 | bytes 512 | tf_op jit(solution)/shard_map/project/pallas_call | solution.py:149
  114.3 6.4 %collective-permute-done.23 = bf16[2,128,512]{2,1,0:T(8,128)(2,1)S(1)} collective-permute-done((bf16[2,128,512]{2,1,0:T(8,128)(2,1)}, bf16[2,128,512]{2,1,0:T(8,128)(2,1)S(1)}, u32[]{:S(2)}, u32[]{:S(2)}) %collective-permute-start.23) | collective-permute-done | bytes 262176 | tf_op jit(solution)/shard_map/ppermute | solution.py:177
  120.7 1.5 collective-permute-start.12
  122.4 6.2 %collective-permute-done.10 = bf16[2,512,128]{2,1,0:T(8,128)(2,1)S(1)} collective-permute-done((bf16[2,512,128]{2,1,0:T(8,128)(2,1)S(1)}, bf16[2,512,128]{2,1,0:T(8,128)(2,1)S(1)}, u32[]{:S(2)}, u32[]{:S(2)}) %collective-permute-start.10) | collective-permute-done | bytes 262176 | tf_op jit(solution)/shard_map/ppermute | solution.py:172
  128.5 1.0 add_convert_fusion.14
  130.6 1.6 collective-permute-start.18
  132.8 2.1 %project.13 = (bf16[2,512,256]{2,1,0:T(8,128)(2,1)S(1)}, f32[2,512,256]{2,1,0:T(8,128)S(1)}) custom-call(bf16[512,2048]{1,0:T(8,128)(2,1)S(1)} %attention.2.pair_ref, bf16[2,512,512]{2,1,0:T(8,128)(2,1)S(1)} %constant_dynamic-update-slice_fusion.8.near_ref, bf16[2,512,512]{2,1,0:T(8,128)(2,1)S(1)} %collective-permute-done.17.far_ref), custom_call_target="tpu_custom_call" | custom-call | flops 262144 | bytes 512 | tf_op jit(solution)/shard_map/project/pallas_call | solution.py:149
  136.0 1.5 collective-permute-start.20
  138.0 1.0 add_convert_fusion.10
  139.1 2.1 %project.14 = (bf16[2,512,256]{2,1,0:T(8,128)(2,1)S(1)}, f32[2,512,256]{2,1,0:T(8,128)S(1)}) custom-call(bf16[512,2048]{1,0:T(8,128)(2,1)S(1)} %attention.3.pair_ref, bf16[2,512,512]{2,1,0:T(8,128)(2,1)S(1)} %constant_dynamic-update-slice_fusion.12.near_ref, bf16[2,512,512]{2,1,0:T(8,128)(2,1)S(1)} %collective-permute-done.25.far_ref), custom_call_target="tpu_custom_call" | custom-call | flops 262144 | bytes 512 | tf_op jit(solution)/shard_map/project/pallas_call | solution.py:149
  141.1 6.0 %collective-permute-done.21 = bf16[2,512,256]{2,1,0:T(8,128)(2,1)} collective-permute-done((bf16[2,512,256]{2,1,0:T(8,128)(2,1)S(1)}, bf16[2,512,256]{2,1,0:T(8,128)(2,1)}, u32[]{:S(2)}, u32[]{:S(2)}) %collective-permute-start.21) | collective-permute-done | bytes 524320 | tf_op jit(solution)/shard_map/ppermute | solution.py:172
  149.3 3.4 %collective-permute-done.20 = bf16[2,512,128]{2,1,0:T(8,128)(2,1)S(1)} collective-permute-done((bf16[2,512,128]{2,1,0:T(8,128)(2,1)S(1)}, bf16[2,512,128]{2,1,0:T(8,128)(2,1)S(1)}, u32[]{:S(2)}, u32[]{:S(2)}) %collective-permute-start.20) | collective-permute-done | bytes 262176 | tf_op jit(solution)/shard_map/ppermute | solution.py:172
  152.7 1.0 add_convert_fusion.8
  153.7 2.1 %project.15 = (bf16[2,512,256]{2,1,0:T(8,128)(2,1)S(1)}, f32[2,512,256]{2,1,0:T(8,128)S(1)}) custom-call(bf16[512,2048]{1,0:T(8,128)(2,1)S(1)} %attention.2.pair_ref, bf16[2,512,512]{2,1,0:T(8,128)(2,1)S(1)} %constant_dynamic-update-slice_fusion.12.near_ref, bf16[2,512,512]{2,1,0:T(8,128)(2,1)S(1)} %collective-permute-done.25.far_ref), custom_call_target="tpu_custom_call" | custom-call | flops 262144 | bytes 512 | tf_op jit(solution)/shard_map/project/pallas_call | solution.py:149
  157.1 1.0 add_convert_fusion.6
  158.1 5.8 %collective-permute-done.29 = bf16[2,512,256]{2,1,0:T(8,128)(2,1)S(1)} collective-permute-done((bf16[2,512,256]{2,1,0:T(8,128)(2,1)S(1)}, bf16[2,512,256]{2,1,0:T(8,128)(2,1)S(1)}, u32[]{:S(2)}, u32[]{:S(2)}) %collective-permute-start.29) | collective-permute-done | bytes 524320 | tf_op jit(solution)/shard_map/ppermute | solution.py:172
  164.0 1.1 collective-permute-start.30
  165.1 4.1 %collective-permute-done.31 = bf16[2,512,256]{2,1,0:T(8,128)(2,1)S(1)} collective-permute-done((bf16[2,512,256]{2,1,0:T(8,128)(2,1)S(1)}, bf16[2,512,256]{2,1,0:T(8,128)(2,1)S(1)}, u32[]{:S(2)}, u32[]{:S(2)}) %collective-permute-start.31) | collective-permute-done | bytes 524320 | tf_op jit(solution)/shard_map/ppermute | solution.py:172
  170.1 1.9 %collective-permute-done.30 = bf16[2,512,128]{2,1,0:T(8,128)(2,1)S(1)} collective-permute-done((bf16[2,512,128]{2,1,0:T(8,128)(2,1)S(1)}, bf16[2,512,128]{2,1,0:T(8,128)(2,1)S(1)}, u32[]{:S(2)}, u32[]{:S(2)}) %collective-permute-start.30) | collective-permute-done | bytes 262176 | tf_op jit(solution)/shard_map/ppermute | solution.py:172
  172.1 3.6 %collective-permute-done.32 = bf16[2,512,128]{2,1,0:T(8,128)(2,1)S(1)} collective-permute-done((bf16[2,512,128]{2,1,0:T(8,128)(2,1)S(1)}, bf16[2,512,128]{2,1,0:T(8,128)(2,1)S(1)}, u32[]{:S(2)}, u32[]{:S(2)}) %collective-permute-start.32) | collective-permute-done | bytes 262176 | tf_op jit(solution)/shard_map/ppermute | solution.py:172
  176.1 1.5 slice_bitcast_fusion
  (99 shorter events, 19.1 us)
Async XLA Ops:
  0.6 2.2 %copy-start.1 = (bf16[1024,2,128]{2,1,0:T(2,128)(2,1)S(1)}, bf16[1024,2,128]{2,1,0:T(2,128)(2,1)}, u32[]{:S(2)}) copy-start(bf16[1024,2,128]{2,1,0:T(2,128)(2,1)} %param.10) | copy-start | bytes 1572868
  3.7 8.3 %copy-start.8 = (s32[64]{0:T(128)S(1)}, s32[64]{0:T(128)}, u32[]{:S(2)}) copy-start(s32[64]{0:T(128)} %param.11) | copy-start | bytes 772
  3.9 9.0 %copy-start = (bf16[1024,1024]{1,0:T(8,128)(2,1)S(1)}, bf16[1024,1024]{1,0:T(8,128)(2,1)}, u32[]{:S(2)}) copy-start(bf16[1024,1024]{1,0:T(8,128)(2,1)} %q_ref.3) | copy-start | bytes 6291460
  4.6 16.4 %collective-permute-start = (bf16[224,512]{1,0:T(8,128)(2,1)}, bf16[224,512]{1,0:T(8,128)(2,1)}, u32[]{:S(2)}, u32[]{:S(2)}) collective-permute-start(bf16[224,512]{1,0:T(8,128)(2,1)} %slice.160), channel_id=1, source_target_pairs={{0,1},{1,2},{2,3},{3,4},{4,5},{5,6},{6,7},{8,9},{9,10},{10,11},{11... | collective-permute-start | bytes 688136 | tf_op jit(solution)/shard_map/ppermute | solution.py:227
  10.1 20.2 %collective-permute-start.6 = (bf16[2,128,512]{2,1,0:T(8,128)(2,1)}, bf16[2,128,512]{2,1,0:T(8,128)(2,1)S(1)}, u32[]{:S(2)}, u32[]{:S(2)}) collective-permute-start(bf16[2,128,512]{2,1,0:T(8,128)(2,1)} %get-tuple-element.44), channel_id=1, source_target_pairs={{0,2},{1,3},{2,4},{3,5},{4,6},{5,7},{6,0},{7,1},{8,10},{9,11},{10,... | collective-permute-start | bytes 786440 | tf_op jit(solution)/shard_map/ppermute | solution.py:177
  22.0 9.9 %copy-start.7 = (bf16[2,128,512]{2,1,0:T(8,128)(2,1)S(1)}, bf16[2,128,512]{2,1,0:T(8,128)(2,1)}, u32[]{:S(2)}) copy-start(bf16[2,128,512]{2,1,0:T(8,128)(2,1)} %get-tuple-element.44) | copy-start | bytes 786436
  30.2 16.6 %copy-start.6 = (bf16[2,128,512]{2,1,0:T(8,128)(2,1)S(1)}, bf16[2,128,512]{2,1,0:T(8,128)(2,1)}, u32[]{:S(2)}) copy-start(bf16[2,128,512]{2,1,0:T(8,128)(2,1)} %get-tuple-element.40) | copy-start | bytes 786436
  30.3 30.8 %copy-start.5 = (bf16[2,128,512]{2,1,0:T(8,128)(2,1)S(1)}, bf16[2,128,512]{2,1,0:T(8,128)(2,1)}, u32[]{:S(2)}) copy-start(bf16[2,128,512]{2,1,0:T(8,128)(2,1)} %get-tuple-element.56) | copy-start | bytes 786436
  30.3 10.8 %collective-permute-start.7 = (bf16[2,128,512]{2,1,0:T(8,128)(2,1)S(1)}, bf16[2,128,512]{2,1,0:T(8,128)(2,1)S(1)}, u32[]{:S(2)}, u32[]{:S(2)}) collective-permute-start(bf16[2,128,512]{2,1,0:T(8,128)(2,1)S(1)} %collective-permute-done.6), channel_id=1, source_target_pairs={{0,2},{1,3},{2,4},{3,5},{4,6},{5,7},{6,0},{7,1},{8,10},{9,11},{10,... | collective-permute-start | bytes 786440 | tf_op jit(solution)/shard_map/ppermute | solution.py:177
  31.9 14.7 %collective-permute-start.8 = (bf16[2,128,512]{2,1,0:T(8,128)(2,1)S(1)}, bf16[2,128,512]{2,1,0:T(8,128)(2,1)S(1)}, u32[]{:S(2)}, u32[]{:S(2)}) collective-permute-start(bf16[2,128,512]{2,1,0:T(8,128)(2,1)S(1)} %copy-done.7), channel_id=1, source_target_pairs={{0,6},{1,7},{2,0},{3,1},{4,2},{5,3},{6,4},{7,5},{8,14},{9,15},{10,... | collective-permute-start | bytes 786440 | tf_op jit(solution)/shard_map/ppermute | solution.py:177
  46.6 24.1 %collective-permute-start.9 = (bf16[2,512,512]{2,1,0:T(8,128)(2,1)S(1)}, bf16[2,512,512]{2,1,0:T(8,128)(2,1)S(1)}, u32[]{:S(2)}, u32[]{:S(2)}) collective-permute-start(bf16[2,512,512]{2,1,0:T(8,128)(2,1)S(1)} %constant_dynamic-update-slice_fusion.4.near_ref), channel_id=1, source_target_pairs={{0,1},{1,0},{2,3},{3,2},{4,5},{5,4},{6,7},{7,6},{8,9},{9,8},{10,11... | collective-permute-start | bytes 3145736 | tf_op jit(solution)/shard_map/ppermute | solution.py:181
  46.8 10.4 %collective-permute-start.1 = (bf16[2,128,512]{2,1,0:T(8,128)(2,1)S(1)}, bf16[2,128,512]{2,1,0:T(8,128)(2,1)S(1)}, u32[]{:S(2)}, u32[]{:S(2)}) collective-permute-start(bf16[2,128,512]{2,1,0:T(8,128)(2,1)S(1)} %copy-done.6), channel_id=1, source_target_pairs={{0,2},{1,3},{2,4},{3,5},{4,6},{5,7},{6,0},{7,1},{8,10},{9,11},{10,... | collective-permute-start | bytes 786440 | tf_op jit(solution)/shard_map/ppermute | solution.py:177
  57.2 11.0 %collective-permute-start.2 = (bf16[2,128,512]{2,1,0:T(8,128)(2,1)S(1)}, bf16[2,128,512]{2,1,0:T(8,128)(2,1)S(1)}, u32[]{:S(2)}, u32[]{:S(2)}) collective-permute-start(bf16[2,128,512]{2,1,0:T(8,128)(2,1)S(1)} %collective-permute-done.1), channel_id=1, source_target_pairs={{0,2},{1,3},{2,4},{3,5},{4,6},{5,7},{6,0},{7,1},{8,10},{9,11},{10,... | collective-permute-start | bytes 786440 | tf_op jit(solution)/shard_map/ppermute | solution.py:177
  57.2 13.4 %collective-permute-start.3 = (bf16[2,128,512]{2,1,0:T(8,128)(2,1)S(1)}, bf16[2,128,512]{2,1,0:T(8,128)(2,1)S(1)}, u32[]{:S(2)}, u32[]{:S(2)}) collective-permute-start(bf16[2,128,512]{2,1,0:T(8,128)(2,1)S(1)} %copy-done.6), channel_id=1, source_target_pairs={{0,6},{1,7},{2,0},{3,1},{4,2},{5,3},{6,4},{7,5},{8,14},{9,15},{10,... | collective-permute-start | bytes 786440 | tf_op jit(solution)/shard_map/ppermute | solution.py:177
  61.1 17.0 %collective-permute-start.14 = (bf16[2,128,512]{2,1,0:T(8,128)(2,1)S(1)}, bf16[2,128,512]{2,1,0:T(8,128)(2,1)S(1)}, u32[]{:S(2)}, u32[]{:S(2)}) collective-permute-start(bf16[2,128,512]{2,1,0:T(8,128)(2,1)S(1)} %copy-done.5), channel_id=1, source_target_pairs={{0,2},{1,3},{2,4},{3,5},{4,6},{5,7},{6,0},{7,1},{8,10},{9,11},{10,... | collective-permute-start | bytes 786440 | tf_op jit(solution)/shard_map/ppermute | solution.py:177
  70.6 20.1 %collective-permute-start.4 = (bf16[2,512,512]{2,1,0:T(8,128)(2,1)S(1)}, bf16[2,512,512]{2,1,0:T(8,128)(2,1)S(1)}, u32[]{:S(2)}, u32[]{:S(2)}) collective-permute-start(bf16[2,512,512]{2,1,0:T(8,128)(2,1)S(1)} %constant_dynamic-update-slice_fusion.near_ref), channel_id=1, source_target_pairs={{0,1},{1,0},{2,3},{3,2},{4,5},{5,4},{6,7},{7,6},{8,9},{9,8},{10,11... | collective-permute-start | bytes 3145736 | tf_op jit(solution)/shard_map/ppermute | solution.py:181
  78.1 11.0 %collective-permute-start.15 = (bf16[2,128,512]{2,1,0:T(8,128)(2,1)S(1)}, bf16[2,128,512]{2,1,0:T(8,128)(2,1)S(1)}, u32[]{:S(2)}, u32[]{:S(2)}) collective-permute-start(bf16[2,128,512]{2,1,0:T(8,128)(2,1)S(1)} %collective-permute-done.14), channel_id=1, source_target_pairs={{0,2},{1,3},{2,4},{3,5},{4,6},{5,7},{6,0},{7,1},{8,10},{9,11},{10,... | collective-permute-start | bytes 786440 | tf_op jit(solution)/shard_map/ppermute | solution.py:177
  78.1 12.5 %collective-permute-start.16 = (bf16[2,128,512]{2,1,0:T(8,128)(2,1)S(1)}, bf16[2,128,512]{2,1,0:T(8,128)(2,1)S(1)}, u32[]{:S(2)}, u32[]{:S(2)}) collective-permute-start(bf16[2,128,512]{2,1,0:T(8,128)(2,1)S(1)} %copy-done.5), channel_id=1, source_target_pairs={{0,6},{1,7},{2,0},{3,1},{4,2},{5,3},{6,4},{7,5},{8,14},{9,15},{10,... | collective-permute-start | bytes 786440 | tf_op jit(solution)/shard_map/ppermute | solution.py:177
  90.6 3.7 %copy-start.4 = (bf16[2,128,512]{2,1,0:T(8,128)(2,1)S(1)}, bf16[2,128,512]{2,1,0:T(8,128)(2,1)}, u32[]{:S(2)}) copy-start(bf16[2,128,512]{2,1,0:T(8,128)(2,1)} %get-tuple-element.66) | copy-start | bytes 786436
  90.6 18.6 %collective-permute-start.17 = (bf16[2,512,512]{2,1,0:T(8,128)(2,1)S(1)}, bf16[2,512,512]{2,1,0:T(8,128)(2,1)S(1)}, u32[]{:S(2)}, u32[]{:S(2)}) collective-permute-start(bf16[2,512,512]{2,1,0:T(8,128)(2,1)S(1)} %constant_dynamic-update-slice_fusion.8.near_ref), channel_id=1, source_target_pairs={{0,1},{1,0},{2,3},{3,2},{4,5},{5,4},{6,7},{7,6},{8,9},{9,8},{10,11... | collective-permute-start | bytes 3145736 | tf_op jit(solution)/shard_map/ppermute | solution.py:181
  92.8 14.9 %collective-permute-start.5 = (bf16[2,512,256]{2,1,0:T(8,128)(2,1)S(1)}, bf16[2,512,256]{2,1,0:T(8,128)(2,1)}, u32[]{:S(2)}, u32[]{:S(2)}) collective-permute-start(bf16[2,512,256]{2,1,0:T(8,128)(2,1)S(1)} %get-tuple-element.43), channel_id=1, source_target_pairs={{0,8},{8,0},{16,24},{24,16},{1,9},{9,1},{17,25},{25,17},{2,10},{10... | collective-permute-start | bytes 1572872 | tf_op jit(solution)/shard_map/ppermute | solution.py:172
  94.3 10.3 %collective-permute-start.22 = (bf16[2,128,512]{2,1,0:T(8,128)(2,1)S(1)}, bf16[2,128,512]{2,1,0:T(8,128)(2,1)}, u32[]{:S(2)}, u32[]{:S(2)}) collective-permute-start(bf16[2,128,512]{2,1,0:T(8,128)(2,1)S(1)} %copy-done.4), channel_id=1, source_target_pairs={{0,2},{1,3},{2,4},{3,5},{4,6},{5,7},{6,0},{7,1},{8,10},{9,11},{10,... | collective-permute-start | bytes 786440 | tf_op jit(solution)/shard_map/ppermute | solution.py:177
  97.7 15.5 %collective-permute-start.11 = (bf16[2,512,256]{2,1,0:T(8,128)(2,1)}, bf16[2,512,256]{2,1,0:T(8,128)(2,1)S(1)}, u32[]{:S(2)}, u32[]{:S(2)}) collective-permute-start(bf16[2,512,256]{2,1,0:T(8,128)(2,1)} %get-tuple-element.50), channel_id=1, source_target_pairs={{0,16},{8,24},{16,0},{24,8},{1,17},{9,25},{17,1},{25,9},{2,18},{10... | collective-permute-start | bytes 1572872 | tf_op jit(solution)/shard_map/ppermute | solution.py:172
  99.3 30.3 %collective-permute-start.13 = (bf16[2,512,256]{2,1,0:T(8,128)(2,1)S(1)}, bf16[2,512,256]{2,1,0:T(8,128)(2,1)}, u32[]{:S(2)}, u32[]{:S(2)}) collective-permute-start(bf16[2,512,256]{2,1,0:T(8,128)(2,1)S(1)} %get-tuple-element.51), channel_id=1, source_target_pairs={{0,8},{8,0},{16,24},{24,16},{1,9},{9,1},{17,25},{25,17},{2,10},{10... | collective-permute-start | bytes 1572872 | tf_op jit(solution)/shard_map/ppermute | solution.py:172
  104.6 17.6 %collective-permute-start.24 = (bf16[2,128,512]{2,1,0:T(8,128)(2,1)S(1)}, bf16[2,128,512]{2,1,0:T(8,128)(2,1)S(1)}, u32[]{:S(2)}, u32[]{:S(2)}) collective-permute-start(bf16[2,128,512]{2,1,0:T(8,128)(2,1)S(1)} %copy-done.4), channel_id=1, source_target_pairs={{0,6},{1,7},{2,0},{3,1},{4,2},{5,3},{6,4},{7,5},{8,14},{9,15},{10,... | collective-permute-start | bytes 786440 | tf_op jit(solution)/shard_map/ppermute | solution.py:177
  107.7 27.2 %collective-permute-start.19 = (bf16[2,512,256]{2,1,0:T(8,128)(2,1)}, bf16[2,512,256]{2,1,0:T(8,128)(2,1)}, u32[]{:S(2)}, u32[]{:S(2)}) collective-permute-start(bf16[2,512,256]{2,1,0:T(8,128)(2,1)} %get-tuple-element.60), channel_id=1, source_target_pairs={{0,16},{8,24},{16,0},{24,8},{1,17},{9,25},{17,1},{25,9},{2,18},{10... | collective-permute-start | bytes 1572872 | tf_op jit(solution)/shard_map/ppermute | solution.py:172
  111.3 9.4 %collective-permute-start.23 = (bf16[2,128,512]{2,1,0:T(8,128)(2,1)}, bf16[2,128,512]{2,1,0:T(8,128)(2,1)S(1)}, u32[]{:S(2)}, u32[]{:S(2)}) collective-permute-start(bf16[2,128,512]{2,1,0:T(8,128)(2,1)} %collective-permute-done.22), channel_id=1, source_target_pairs={{0,2},{1,3},{2,4},{3,5},{4,6},{5,7},{6,0},{7,1},{8,10},{9,11},{10,... | collective-permute-start | bytes 786440 | tf_op jit(solution)/shard_map/ppermute | solution.py:177
  113.2 9.0 %copy-start.2 = (bf16[2,512,256]{2,1,0:T(8,128)(2,1)}, bf16[2,512,256]{2,1,0:T(8,128)(2,1)S(1)}, u32[]{:S(2)}) copy-start(bf16[2,512,256]{2,1,0:T(8,128)(2,1)S(1)} %collective-permute-done.11) | copy-start | bytes 1572868
  113.2 15.3 %collective-permute-start.10 = (bf16[2,512,128]{2,1,0:T(8,128)(2,1)S(1)}, bf16[2,512,128]{2,1,0:T(8,128)(2,1)S(1)}, u32[]{:S(2)}, u32[]{:S(2)}) collective-permute-start(bf16[2,512,128]{2,1,0:T(8,128)(2,1)S(1)} %add_convert_fusion.15), channel_id=1, source_target_pairs={{0,16},{8,24},{16,0},{24,8},{1,17},{9,25},{17,1},{25,9},{2,18},{10... | collective-permute-start | bytes 786440 | tf_op jit(solution)/shard_map/ppermute | solution.py:172
  120.7 12.0 %collective-permute-start.12 = (bf16[2,512,128]{2,1,0:T(8,128)(2,1)S(1)}, bf16[2,512,128]{2,1,0:T(8,128)(2,1)S(1)}, u32[]{:S(2)}, u32[]{:S(2)}) collective-permute-start(bf16[2,512,128]{2,1,0:T(8,128)(2,1)S(1)} %add_convert_fusion.13), channel_id=1, source_target_pairs={{0,8},{8,0},{16,24},{24,16},{1,9},{9,1},{17,25},{25,17},{2,10},{10... | collective-permute-start | bytes 786440 | tf_op jit(solution)/shard_map/ppermute | solution.py:172
  122.3 10.5 %copy-start.3 = (bf16[2,512,256]{2,1,0:T(8,128)(2,1)S(1)}, bf16[2,512,256]{2,1,0:T(8,128)(2,1)}, u32[]{:S(2)}) copy-start(bf16[2,512,256]{2,1,0:T(8,128)(2,1)} %copy-done.2) | copy-start | bytes 1572868
  122.3 16.8 %collective-permute-start.25 = (bf16[2,512,512]{2,1,0:T(8,128)(2,1)S(1)}, bf16[2,512,512]{2,1,0:T(8,128)(2,1)S(1)}, u32[]{:S(2)}, u32[]{:S(2)}) collective-permute-start(bf16[2,512,512]{2,1,0:T(8,128)(2,1)S(1)} %constant_dynamic-update-slice_fusion.12.near_ref), channel_id=1, source_target_pairs={{0,1},{1,0},{2,3},{3,2},{4,5},{5,4},{6,7},{7,6},{8,9},{9,8},{10,11... | collective-permute-start | bytes 3145736 | tf_op jit(solution)/shard_map/ppermute | solution.py:181
  130.6 7.4 %collective-permute-start.18 = (bf16[2,512,128]{2,1,0:T(8,128)(2,1)S(1)}, bf16[2,512,128]{2,1,0:T(8,128)(2,1)S(1)}, u32[]{:S(2)}, u32[]{:S(2)}) collective-permute-start(bf16[2,512,128]{2,1,0:T(8,128)(2,1)S(1)} %add_convert_fusion.11), channel_id=1, source_target_pairs={{0,16},{8,24},{16,0},{24,8},{1,17},{9,25},{17,1},{25,9},{2,18},{10... | collective-permute-start | bytes 786440 | tf_op jit(solution)/shard_map/ppermute | solution.py:172
  132.2 15.0 %collective-permute-start.21 = (bf16[2,512,256]{2,1,0:T(8,128)(2,1)S(1)}, bf16[2,512,256]{2,1,0:T(8,128)(2,1)}, u32[]{:S(2)}, u32[]{:S(2)}) collective-permute-start(bf16[2,512,256]{2,1,0:T(8,128)(2,1)S(1)} %get-tuple-element.61), channel_id=1, source_target_pairs={{0,8},{8,0},{16,24},{24,16},{1,9},{9,1},{17,25},{25,17},{2,10},{10... | collective-permute-start | bytes 1572872 | tf_op jit(solution)/shard_map/ppermute | solution.py:172
  136.0 16.7 %collective-permute-start.20 = (bf16[2,512,128]{2,1,0:T(8,128)(2,1)S(1)}, bf16[2,512,128]{2,1,0:T(8,128)(2,1)S(1)}, u32[]{:S(2)}, u32[]{:S(2)}) collective-permute-start(bf16[2,512,128]{2,1,0:T(8,128)(2,1)S(1)} %add_convert_fusion.9), channel_id=1, source_target_pairs={{0,8},{8,0},{16,24},{24,16},{1,9},{9,1},{17,25},{25,17},{2,10},{10... | collective-permute-start | bytes 786440 | tf_op jit(solution)/shard_map/ppermute | solution.py:172
  137.5 18.3 %collective-permute-start.27 = (bf16[2,512,256]{2,1,0:T(8,128)(2,1)S(1)}, bf16[2,512,256]{2,1,0:T(8,128)(2,1)S(1)}, u32[]{:S(2)}, u32[]{:S(2)}) collective-permute-start(bf16[2,512,256]{2,1,0:T(8,128)(2,1)S(1)} %get-tuple-element.70), channel_id=1, source_target_pairs={{0,16},{8,24},{16,0},{24,8},{1,17},{9,25},{17,1},{25,9},{2,18},{10... | collective-permute-start | bytes 1572872 | tf_op jit(solution)/shard_map/ppermute | solution.py:172
  148.2 8.9 %collective-permute-start.26 = (bf16[2,512,128]{2,1,0:T(8,128)(2,1)S(1)}, bf16[2,512,128]{2,1,0:T(8,128)(2,1)S(1)}, u32[]{:S(2)}, u32[]{:S(2)}) collective-permute-start(bf16[2,512,128]{2,1,0:T(8,128)(2,1)S(1)} %add_convert_fusion.7), channel_id=1, source_target_pairs={{0,16},{8,24},{16,0},{24,8},{1,17},{9,25},{17,1},{25,9},{2,18},{10... | collective-permute-start | bytes 786440 | tf_op jit(solution)/shard_map/ppermute | solution.py:172
  148.7 15.2 %collective-permute-start.29 = (bf16[2,512,256]{2,1,0:T(8,128)(2,1)S(1)}, bf16[2,512,256]{2,1,0:T(8,128)(2,1)S(1)}, u32[]{:S(2)}, u32[]{:S(2)}) collective-permute-start(bf16[2,512,256]{2,1,0:T(8,128)(2,1)S(1)} %get-tuple-element.71), channel_id=1, source_target_pairs={{0,8},{8,0},{16,24},{24,16},{1,9},{9,1},{17,25},{25,17},{2,10},{10... | collective-permute-start | bytes 1572872 | tf_op jit(solution)/shard_map/ppermute | solution.py:172
  155.8 13.4 %collective-permute-start.31 = (bf16[2,512,256]{2,1,0:T(8,128)(2,1)S(1)}, bf16[2,512,256]{2,1,0:T(8,128)(2,1)S(1)}, u32[]{:S(2)}, u32[]{:S(2)}) collective-permute-start(bf16[2,512,256]{2,1,0:T(8,128)(2,1)S(1)} %get-tuple-element.75), channel_id=1, source_target_pairs={{0,16},{8,24},{16,0},{24,8},{1,17},{9,25},{17,1},{25,9},{2,18},{10... | collective-permute-start | bytes 1572872 | tf_op jit(solution)/shard_map/ppermute | solution.py:172
  156.4 13.6 %collective-permute-start.28 = (bf16[2,512,128]{2,1,0:T(8,128)(2,1)S(1)}, bf16[2,512,128]{2,1,0:T(8,128)(2,1)S(1)}, u32[]{:S(2)}, u32[]{:S(2)}) collective-permute-start(bf16[2,512,128]{2,1,0:T(8,128)(2,1)S(1)} %add_convert_fusion.5), channel_id=1, source_target_pairs={{0,8},{8,0},{16,24},{24,16},{1,9},{9,1},{17,25},{25,17},{2,10},{10... | collective-permute-start | bytes 786440 | tf_op jit(solution)/shard_map/ppermute | solution.py:172
  164.0 8.0 %collective-permute-start.30 = (bf16[2,512,128]{2,1,0:T(8,128)(2,1)S(1)}, bf16[2,512,128]{2,1,0:T(8,128)(2,1)S(1)}, u32[]{:S(2)}, u32[]{:S(2)}) collective-permute-start(bf16[2,512,128]{2,1,0:T(8,128)(2,1)S(1)} %add_convert_fusion.3), channel_id=1, source_target_pairs={{0,16},{8,24},{16,0},{24,8},{1,17},{9,25},{17,1},{25,9},{2,18},{10... | collective-permute-start | bytes 786440 | tf_op jit(solution)/shard_map/ppermute | solution.py:172
  169.2 6.4 %collective-permute-start.32 = (bf16[2,512,128]{2,1,0:T(8,128)(2,1)S(1)}, bf16[2,512,128]{2,1,0:T(8,128)(2,1)S(1)}, u32[]{:S(2)}, u32[]{:S(2)}) collective-permute-start(bf16[2,512,128]{2,1,0:T(8,128)(2,1)S(1)} %add_convert_fusion.1), channel_id=1, source_target_pairs={{0,8},{8,0},{16,24},{24,16},{1,9},{9,1},{17,25},{25,17},{2,10},{10... | collective-permute-start | bytes 786440 | tf_op jit(solution)/shard_map/ppermute | solution.py:172

commit v3 on v2

--- a/solution.py
+++ b/solution.py
@@ -122,15 +122,18 @@
     )(order, queries, query_tangent, context, low)
 
 
-def project_kernel(sent, kept, pair_ref, near_ref, far_ref, send_ref, keep_ref):
-    depth = near_ref.shape[1]
-    part = near_ref.shape[2] // len(RELATIVE)
+def project_kernel(sent, kept, pair_ref, *refs):
+    *weight_refs, send_ref, keep_ref = refs
+    width = pair_ref.shape[1] // 2
+    part = weight_refs[0].shape[2] // len(RELATIVE)
     dot = functools.partial(jnp.dot, preferred_element_type=jnp.float32)
-    near, near_tan = pair_ref[:, :depth], pair_ref[:, 2 * depth : 3 * depth]
-    far, far_tan = pair_ref[:, depth : 2 * depth], pair_ref[:, 3 * depth :]
-    value = dot(near, near_ref[1]) + dot(far, far_ref[1])
-    tangent = dot(near, near_ref[0]) + dot(far, far_ref[0])
-    tangent = tangent + dot(near_tan, near_ref[1]) + dot(far_tan, far_ref[1])
+    value, tangent, start = 0.0, 0.0, 0
+    for ref in weight_refs:
+        end = start + ref.shape[1]
+        attended, attended_tan = pair_ref[:, start:end], pair_ref[:, width + start : width + end]
+        value += dot(attended, ref[1])
+        tangent += dot(attended, ref[0]) + dot(attended_tan, ref[1])
+        start = end
     for ref, flips in ((send_ref, sent), (keep_ref, kept)):
         for place, flip in enumerate(flips):
             at = RELATIVE.index(flip) * part
@@ -139,20 +142,18 @@
             ref[1, :, to] = tangent[:, at : at + part].astype(ref.dtype)
 
 
-def project(sent, kept, pair, near, far):
+def project(sent, kept, pair, weights):
     tokens, width = pair.shape
     tile = min(2 * TILE, tokens)
-    steps = tokens // tile
-    columns = near.shape[2]
+    columns = weights[0].shape[2]
     out = (2, tokens, columns // 2)
     block = pl.BlockSpec((2, tile, columns // 2), lambda i: (0, i, 0))
     return pl.pallas_call(
         functools.partial(project_kernel, sent, kept),
-        grid=(steps,),
+        grid=(tokens // tile,),
         in_specs=[
             pl.BlockSpec((tile, width), lambda i: (i, 0)),
-            pl.BlockSpec(near.shape, lambda i: (0, 0, 0)),
-            pl.BlockSpec(far.shape, lambda i: (0, 0, 0)),
+            *[pl.BlockSpec(piece.shape, lambda i: (0, 0, 0)) for piece in weights],
         ],
         out_specs=[block, block],
         out_shape=[
@@ -164,7 +165,7 @@
             flops=tokens * columns, bytes_accessed=tokens, transcendentals=0
         ),
         name="project",
-    )(pair, near, far)
+    )(pair, *weights)
 
 
 def across(block, flip):
@@ -187,25 +188,35 @@
 
 class Gather:
     def __init__(self, mine, chips):
-        self.ahead, self.behind = [mine], [mine]
+        self.blocks = {0: mine}
+        self.chips = chips
         self.forward, self.backward = chips // 2, (chips - 1) // 2
 
-    def neighbours(self, *until):
-        mine = hold(self.ahead[0], *until) if until else self.ahead[0]
+    def ahead(self):
         if self.forward:
-            self.ahead.append(along(mine, 1))
+            self.blocks[1] = along(self.blocks[0], 1)
+
+    def behind(self):
         if self.backward:
-            self.behind.append(along(mine, -1))
-
-    def farther(self, *until):
-        for _ in range(self.forward - 1):
-            self.ahead.append(along(hold(self.ahead[-1], *until), 1))
-        for _ in range(self.backward - 1):
-            self.behind.append(along(hold(self.behind[-1], *until), -1))
-
-    def finish(self):
-        near = jnp.concatenate(self.ahead + self.behind[:0:-1], axis=1)
-        return near, other_core(near)
+            self.blocks[self.chips - 1] = along(self.blocks[0], -1)
+
+    def farther(self):
+        for step in range(2, self.forward + 1):
+            self.blocks[step] = along(self.blocks[step - 1], 1)
+        for step in range(2, self.backward + 1):
+            self.blocks[self.chips - step] = along(self.blocks[self.chips - step + 1], -1)
+
+    def early(self):
+        near = jnp.concatenate([self.blocks[0], self.blocks[1]], axis=1)
+        self.first = [near, other_core(near)]
+
+    def late(self):
+        near = jnp.concatenate([self.blocks[step] for step in range(2, self.chips)], axis=1)
+        return [near, other_core(near)]
+
+
+def together(*trees):
+    return lax.optimization_barrier(trees)
 
 
 def body(
@@ -220,6 +231,15 @@
     seq_size = lax.axis_size("seq")
     chips = seq_size // CORES
 
+    mine = arrange(kv_index, weight_tangent, out_weight)
+    gathers = [Gather(block, chips) for block in mine]
+    gathers[0].ahead()
+    gathers[0].behind()
+    gathers[1].ahead()
+
+    key_value, key_value_tangents, _ = lax.optimization_barrier(
+        (key_value, key_value_tangents, mine[0])
+    )
     stacked = jnp.concatenate(
         [key_value[:, 0], key_value_tangents[:, 0], key_value[:, 1], key_value_tangents[:, 1]],
         axis=1,
@@ -227,12 +247,6 @@
     prior = lax.ppermute(
         stacked[tokens - WINDOW :], "seq", [(i, i + 1) for i in range(seq_size - 1)]
     )
-    context = jnp.concatenate([prior, stacked[:half]], axis=0)
-
-    mine = arrange(kv_index, weight_tangent, out_weight)
-    gathers = [Gather(block, chips) for block in mine]
-    gathers[0].neighbours()
-    gathers[1].neighbours()
 
     doc_ends = jnp.cumsum(doc_lengths)
     doc_starts = doc_ends - doc_lengths
@@ -246,7 +260,8 @@
     step = jnp.arange(chips, dtype=jnp.int32)
     chip, core = seq_index // CORES, seq_index % CORES
     owner = (chip - step + chips) % chips * CORES
-    order = jnp.concatenate([owner + core, owner + 1 - core])
+    near, far = owner + core, owner + 1 - core
+    order = jnp.concatenate([near[:2], far[:2], near[2:], far[2:]])
     whole_heads = order.shape[0] == heads
 
     def attend(part, context):
@@ -258,44 +273,79 @@
         return pair
 
     pair_second = attend(1, stacked)
-    gathers[0].farther(pair_second)
-    pair_first = attend(0, hold(context, pair_second))
-    gathers[2].neighbours(pair_first)
-    gathers[1].farther(pair_first)
-
-    def first_stage(near, far, *until):
-        pair = hold(pair_first, *until) if until else pair_first
-        send_x, keep_x = project((1, 3), (2, 0), pair, near, far)
+    pair_second, prior, gathers[0].blocks = together(pair_second, prior, gathers[0].blocks)
+    gathers[0].farther()
+    pair_first = attend(0, jnp.concatenate([prior, stacked[:half]], axis=0))
+
+    def add_stage(keep, received, place):
+        part = keep.shape[2] // 2
+        of = slice(place * part, (place + 1) * part)
+        return (keep[:, :, :part] + received[:, :, of]).astype(jnp.bfloat16)
+
+    def total(keep, received, place, last):
+        part = keep.shape[2] // 2
+        of = slice(place * part, (place + 1) * part)
+        return (keep[:, :, part:] + received[:, :, of] + last).astype(jnp.bfloat16)
+
+    staged, sums, finished = [None] * CHUNKS, [None] * CHUNKS, []
+
+    def second_stage(chunk):
+        keep_x, from_x, keep_y, from_y = staged[chunk]
+        send_y = add_stage(keep_x, from_x, 1)
+        send_x = add_stage(keep_y, from_y, 1)
+        sums[chunk] = (send_y, send_x)
+
+    def finish(chunk, last_y, last_x):
+        keep_x, from_x, keep_y, from_y = staged[chunk]
+        first = total(keep_x, from_x, 0, last_y)
+        second = total(keep_y, from_y, 0, last_x)
+        finished.append(jnp.concatenate([first, second], axis=1))
+
+    def last_exchange(chunk):
+        send_y, send_x = sums[chunk]
+        return across(send_y, 2), across(send_x, 1)
+
+    def take(chunk):
+        keep_x, from_x, keep_y, from_y = staged[chunk]
+        return (from_x, from_y)
+
+    def put(chunk, from_x, from_y):
+        keep_x, _, keep_y, _ = staged[chunk]
+        staged[chunk] = (keep_x, from_x, keep_y, from_y)
+
+    gathers[0].early()
+    exchanged, send_y = (), ()
+    for chunk in range(CHUNKS):
+        here = gathers[chunk]
+        ahead = gathers[chunk + 1].blocks if chunk + 1 < CHUNKS else {}
+        here.blocks, here.first, ahead, pair_first, exchanged, _ = together(
+            here.blocks, here.first, ahead, pair_first, exchanged, send_y
+        )
+        weights = here.first + here.late()
+        if chunk + 1 < CHUNKS:
+            gathers[chunk + 1].blocks = ahead
+            gathers[chunk + 1].behind()
+            gathers[chunk + 1].farther()
+            gathers[chunk + 1].early()
+        if chunk + 2 < CHUNKS:
+            gathers[chunk + 2].ahead()
+        if chunk >= 2:
+            finish(chunk - 2, *exchanged)
+        if chunk >= 1:
+            received, weights[2] = together(take(chunk - 1), weights[2])
+            put(chunk - 1, *received)
+            second_stage(chunk - 1)
+            sums[chunk - 1], pair_first = together(sums[chunk - 1], pair_first)
+            exchanged = last_exchange(chunk - 1)
+        send_x, keep_x = project((1, 3), (2, 0), pair_first, weights)
         from_x = across(send_x, 1)
-        pair = hold(pair_second, send_x)
-        send_y, keep_y = project((2, 3), (1, 0), pair, near, far)
+        send_y, keep_y = project((2, 3), (1, 0), hold(pair_second, send_x), weights)
         from_y = across(send_y, 2)
-        return keep_x, from_x, keep_y, from_y
-
-    def second_stage(keep_x, from_x, keep_y, from_y):
-        part = keep_x.shape[2] // 2
-        send_y2 = (keep_x[:, :, :part] + from_x[:, :, part:]).astype(jnp.bfloat16)
-        from_y2 = across(send_y2, 2)
-        send_x2 = (keep_y[:, :, :part] + from_y[:, :, part:]).astype(jnp.bfloat16)
-        from_x2 = across(send_x2, 1)
-        first = keep_x[:, :, part:] + from_x[:, :, :part] + from_y2
-        second = keep_y[:, :, part:] + from_y[:, :, :part] + from_x2
-        return jnp.concatenate([first, second], axis=1).astype(jnp.bfloat16)
-
-    staged = []
-    for chunk, gathering in enumerate(gathers):
-        near, far = gathering.finish()
-        now = first_stage(near, far)
-        staged.append(now)
-        if chunk + 1 < CHUNKS and chunk:
-            gathers[chunk + 1].farther(now[0])
-        if chunk + 3 < CHUNKS:
-            gathers[chunk + 3].neighbours(now[0])
-        if chunk:
-            last = staged[chunk - 1]
-            staged[chunk - 1] = (last[0], hold(last[1], now[0]), last[2], hold(last[3], now[2]))
-
-    finished = [second_stage(*now) for now in staged]
+        staged[chunk] = (keep_x, from_x, keep_y, from_y)
+    second_stage(CHUNKS - 1)
+    last = last_exchange(CHUNKS - 1)
+    finish(CHUNKS - 2, *exchanged)
+    finish(CHUNKS - 1, *last)
     result = jnp.concatenate(finished, axis=2)
     return result[0], result[1]
 

time: 178 us -> 146 us (0.82)
  waiting for transfers between devices: 85.9 us -> 49.4 us
  starting transfers between devices: 36.3 us -> 42.1 us
  other arithmetic: 10.6 us -> 6.94 us
  local copies, waits for them, and re-layouts: 6.83 us -> 9.77 us
    ppermute x12, waiting for transfers between devices: 53.9 us -> 18.5 us  [along(): lax.ppermute(block, 'seq', [(i, (i + CORES * chips) % size) for i in rang...]
    another operation x10 -> x2, other arithmetic: 4.71 us -> 0.2 us
    ppermute x12, starting transfers between devices: 16.8 us -> 20.2 us  [along(): lax.ppermute(block, 'seq', [(i, (i + CORES * chips) % size) for i in rang...]
    concatenate x4 -> x8, local copies, waits for them, and re-layouts: 0.07 us -> 3 us  [the longest x4 1.98 us: early(): near = jnp.concatenate([self.blocks[0], self.blocks[1]], axis=1)]
    ppermute x16, starting transfers between devices: 16 us -> 18.9 us  [across(): return lax.ppermute(block, 'kv', [(i, i ^ flip) for i in range(size)])]
    slice x3, local copies, waits for them, and re-layouts: 2.95 us -> 0.18 us  [the longest x2 0.15 us: body(): order = jnp.concatenate([near[:2], far[:2], near[2:], far[2:]])]
    convert_element_type x8 -> x16, other arithmetic: 4.24 us -> 5.11 us  [the longest x8 3.45 us: add_stage(): return (keep[:, :, :part] + received[:, :, of]).astype(jnp.bfloat16)]
  transfers between devices with their start and end apart: 33 -> 37, of which waited for: 18 -> 15; matrix products, arithmetic and copies ran while one was open for 7% -> 9% of each run, Pallas kernels for 21% -> 23%
where the time goes in v3:
time: 146 us; the launch traced here: 145 us
  waiting for transfers between devices  49.4 us (34%)
  starting transfers between devices  42.1 us (29%)
  Pallas kernels  35.5 us (24%)
  local copies, waits for them, and re-layouts  9.77 us (7%)
  other arithmetic  6.94 us (5%)
    ppermute x16, waiting for transfers between devices, across(): return lax.ppermute(block, 'kv', [(i, i ^ flip) for i in range(size)])  30.9 us
    ppermute x12, starting transfers between devices, along(): lax.ppermute(block, 'seq', [(i, (i + CORES * chips) % size) for i in rang...  20.2 us
    ppermute x16, starting transfers between devices, across(): return lax.ppermute(block, 'kv', [(i, i ^ flip) for i in range(size)])  18.9 us
    ppermute x12, waiting for transfers between devices, along(): lax.ppermute(block, 'seq', [(i, (i + CORES * chips) % size) for i in rang...  18.5 us
    pallas_call x8, Pallas kernels, project(): pl.pallas_call(functools.partial(project_kernel, sent, kept), grid=(token...  16.6 us
    pallas_call x2, Pallas kernels, attention(): pl.pallas_call(functools.partial(attention_kernel, heads, head_dim, offse...  16.4 us
    convert_element_type x8, other arithmetic, add_stage(): return (keep[:, :, :part] + received[:, :, of]).astype(jnp.bfloat16)  3.45 us
  transfers between devices with their start and end apart: 37, of which 15 were waited for; matrix products, arithmetic and copies ran while one was open for 9% of the time, Pallas kernels for 23%

profile of v3, /device:TPU:0, one launch (start us, length us, event | category | flops | bytes accessed | tf_op | source)
XLA Modules:
  0.0 145.0 jit_solution(16270148105978389717)
XLA Ops:
  0.6 2.5 %arrange.1 = (bf16[2,128,512]{2,1,0:T(8,128)(2,1)}, bf16[2,128,512]{2,1,0:T(8,128)(2,1)}, bf16[2,128,512]{2,1,0:T(8,128)(2,1)}, bf16[2,128,512]{2,1,0:T(8,128)(2,1)}) custom-call(s32[1]{0:T(128)} %bitcast.kv_ref, bf16[128,2048]{1,0:T(8,128)(2,1)} %tangent_ref.1, bf16[128,2048]{1,0:T(8,128)(2,1)} %value_ref.1), custom_call_target="tpu_custom_call" | custom-call | tf_op jit(solution)/shard_map/arrange/pallas_call | solution.py:36
  3.2 3.0 %collective-permute-start.1 = (bf16[2,128,512]{2,1,0:T(8,128)(2,1)}, bf16[2,128,512]{2,1,0:T(8,128)(2,1)}, u32[]{:S(2)}, u32[]{:S(2)}) collective-permute-start(bf16[2,128,512]{2,1,0:T(8,128)(2,1)} %get-tuple-element.84), channel_id=1, source_target_pairs={{0,2},{1,3},{2,4},{3,5},{4,6},{5,7},{6,0},{7,1},{8,10},{9,11},{10,... | collective-permute-start | bytes 786440 | tf_op jit(solution)/shard_map/ppermute | solution.py:178
  6.2 2.0 %collective-permute-start.2 = (bf16[2,128,512]{2,1,0:T(8,128)(2,1)}, bf16[2,128,512]{2,1,0:T(8,128)(2,1)S(1)}, u32[]{:S(2)}, u32[]{:S(2)}) collective-permute-start(bf16[2,128,512]{2,1,0:T(8,128)(2,1)} %get-tuple-element.84), channel_id=1, source_target_pairs={{0,6},{1,7},{2,0},{3,1},{4,2},{5,3},{6,4},{7,5},{8,14},{9,15},{10,... | collective-permute-start | bytes 786440 | tf_op jit(solution)/shard_map/ppermute | solution.py:178
  8.2 1.1 copy.19
  10.3 2.1 %collective-permute-start = (bf16[224,512]{1,0:T(8,128)(2,1)}, bf16[224,512]{1,0:T(8,128)(2,1)}, u32[]{:S(2)}, u32[]{:S(2)}) collective-permute-start(bf16[224,512]{1,0:T(8,128)(2,1)} %slice.180), channel_id=1, source_target_pairs={{0,1},{1,2},{2,3},{3,4},{4,5},{5,6},{6,7},{8,9},{9,10},{10,11},{11... | collective-permute-start | bytes 688136 | tf_op jit(solution)/shard_map/ppermute | solution.py:247
  13.4 8.2 %attention.2.pair_ref = bf16[512,2048]{1,0:T(8,128)(2,1)S(1)} custom-call(s32[8]{0:T(128)S(1)} %pad_add_fusion.order_ref, bf16[1024,1024]{1,0:T(8,128)(2,1)S(1)} %copy-done, bf16[1024,1024]{1,0:T(8,128)(2,1)} %qt_ref.3, bf16[1024,512]{1,0:T(8,128)(2,1)S(1)} %pad_maximum_fusion.ctx_ref, s32[1024,128]{1,0:T(8,128)S(1)} %broadcast_in_dim.13.low_ref), custom_call_target="tpu_custom_call" | custom-call | flops 1048576 | bytes 512 | tf_op jit(solution)/shard_map/attention/pallas_call | solution.py:105
  21.7 1.0 constant_dynamic-update-slice_fusion.refs_0_
  22.8 1.5 %collective-permute-start.5 = (bf16[2,128,512]{2,1,0:T(8,128)(2,1)S(1)}, bf16[2,128,512]{2,1,0:T(8,128)(2,1)S(1)}, u32[]{:S(2)}, u32[]{:S(2)}) collective-permute-start(bf16[2,128,512]{2,1,0:T(8,128)(2,1)S(1)} %copy-done.17), channel_id=1, source_target_pairs={{0,2},{1,3},{2,4},{3,5},{4,6},{5,7},{6,0},{7,1},{8,10},{9,11},{10,... | collective-permute-start | bytes 786440 | tf_op jit(solution)/shard_map/ppermute | solution.py:178
  24.3 1.6 %collective-permute-start.3 = (bf16[2,128,512]{2,1,0:T(8,128)(2,1)}, bf16[2,128,512]{2,1,0:T(8,128)(2,1)S(1)}, u32[]{:S(2)}, u32[]{:S(2)}) collective-permute-start(bf16[2,128,512]{2,1,0:T(8,128)(2,1)} %collective-permute-done.1), channel_id=1, source_target_pairs={{0,2},{1,3},{2,4},{3,5},{4,6},{5,7},{6,0},{7,1},{8,10},{9,11},{10,... | collective-permute-start | bytes 786440 | tf_op jit(solution)/shard_map/ppermute | solution.py:178
  25.9 1.0 pad_maximum_fusion.1.ctx_ref
  26.9 8.2 %attention.3.pair_ref = bf16[512,2048]{1,0:T(8,128)(2,1)S(1)} custom-call(s32[8]{0:T(128)S(1)} %pad_add_fusion.order_ref, bf16[1024,1024]{1,0:T(8,128)(2,1)S(1)} %copy-done, bf16[1024,1024]{1,0:T(8,128)(2,1)} %qt_ref.3, bf16[736,512]{1,0:T(8,128)(2,1)S(1)} %pad_maximum_fusion.1.ctx_ref, s32[1024,128]{1,0:T(8,128)S(1)} %broadcast_in_dim.13.low_ref), custom_call_target="tpu_custom_call" | custom-call | flops 1048576 | bytes 512 | tf_op jit(solution)/shard_map/attention/pallas_call | solution.py:105
  35.1 3.9 %collective-permute-done.3 = bf16[2,128,512]{2,1,0:T(8,128)(2,1)S(1)} collective-permute-done((bf16[2,128,512]{2,1,0:T(8,128)(2,1)}, bf16[2,128,512]{2,1,0:T(8,128)(2,1)S(1)}, u32[]{:S(2)}, u32[]{:S(2)}) %collective-permute-start.3) | collective-permute-done | bytes 262176 | tf_op jit(solution)/shard_map/ppermute | solution.py:178
  39.7 3.8 %collective-permute-start.10 = (bf16[2,128,512]{2,1,0:T(8,128)(2,1)S(1)}, bf16[2,128,512]{2,1,0:T(8,128)(2,1)S(1)}, u32[]{:S(2)}, u32[]{:S(2)}) collective-permute-start(bf16[2,128,512]{2,1,0:T(8,128)(2,1)S(1)} %copy-done.17), channel_id=1, source_target_pairs={{0,6},{1,7},{2,0},{3,1},{4,2},{5,3},{6,4},{7,5},{8,14},{9,15},{10,... | collective-permute-start | bytes 786440 | tf_op jit(solution)/shard_map/ppermute | solution.py:178
  43.5 2.1 %project.8 = (bf16[2,512,256]{2,1,0:T(8,128)(2,1)S(1)}, f32[2,512,256]{2,1,0:T(8,128)S(1)}) custom-call(bf16[512,2048]{1,0:T(8,128)(2,1)S(1)} %attention.3.pair_ref, bf16[2,256,512]{2,1,0:T(8,128)(2,1)S(1)} %constant_dynamic-update-slice_fusion.refs_0_, bf16[2,256,512]{2,1,0:T(8,128)(2,1)S(1)} %collective-permute-done.4.refs_1_, ...), custom_call_target="tpu_custom_call" | custom-call | flops 262144 | bytes 512 | tf_op jit(solution)/shard_map/project/pallas_call | solution.py:151
  45.6 2.1 %project.9 = (bf16[2,512,256]{2,1,0:T(8,128)(2,1)S(1)}, f32[2,512,256]{2,1,0:T(8,128)S(1)}) custom-call(bf16[512,2048]{1,0:T(8,128)(2,1)S(1)} %attention.2.pair_ref, bf16[2,256,512]{2,1,0:T(8,128)(2,1)S(1)} %constant_dynamic-update-slice_fusion.refs_0_, bf16[2,256,512]{2,1,0:T(8,128)(2,1)S(1)} %collective-permute-done.4.refs_1_, ...), custom_call_target="tpu_custom_call" | custom-call | flops 262144 | bytes 512 | tf_op jit(solution)/shard_map/project/pallas_call | solution.py:151
  47.7 1.6 %collective-permute-start.8 = (bf16[2,512,256]{2,1,0:T(8,128)(2,1)S(1)}, bf16[2,512,256]{2,1,0:T(8,128)(2,1)S(1)}, u32[]{:S(2)}, u32[]{:S(2)}) collective-permute-start(bf16[2,512,256]{2,1,0:T(8,128)(2,1)S(1)} %get-tuple-element.98), channel_id=1, source_target_pairs={{0,16},{8,24},{16,0},{24,8},{1,17},{9,25},{17,1},{25,9},{2,18},{10... | collective-permute-start | bytes 1572872 | tf_op jit(solution)/shard_map/ppermute | solution.py:173
  49.3 1.4 collective-permute-done.12
  50.7 1.5 %collective-permute-start.7 = (bf16[2,512,256]{2,1,0:T(8,128)(2,1)S(1)}, bf16[2,512,256]{2,1,0:T(8,128)(2,1)S(1)}, u32[]{:S(2)}, u32[]{:S(2)}) collective-permute-start(bf16[2,512,256]{2,1,0:T(8,128)(2,1)S(1)} %get-tuple-element.95), channel_id=1, source_target_pairs={{0,8},{8,0},{16,24},{24,16},{1,9},{9,1},{17,25},{25,17},{2,10},{10... | collective-permute-start | bytes 1572872 | tf_op jit(solution)/shard_map/ppermute | solution.py:173
  52.2 1.4 collective-permute-done.10
  54.1 7.8 %collective-permute-done.9 = bf16[2,128,512]{2,1,0:T(8,128)(2,1)S(1)} collective-permute-done((bf16[2,128,512]{2,1,0:T(8,128)(2,1)S(1)}, bf16[2,128,512]{2,1,0:T(8,128)(2,1)S(1)}, u32[]{:S(2)}, u32[]{:S(2)}) %collective-permute-start.9) | collective-permute-done | bytes 262176 | tf_op jit(solution)/shard_map/ppermute | solution.py:178
  62.2 3.9 %collective-permute-start.14 = (bf16[2,128,512]{2,1,0:T(8,128)(2,1)S(1)}, bf16[2,128,512]{2,1,0:T(8,128)(2,1)S(1)}, u32[]{:S(2)}, u32[]{:S(2)}) collective-permute-start(bf16[2,128,512]{2,1,0:T(8,128)(2,1)S(1)} %copy-done.16), channel_id=1, source_target_pairs={{0,6},{1,7},{2,0},{3,1},{4,2},{5,3},{6,4},{7,5},{8,14},{9,15},{10,... | collective-permute-start | bytes 786440 | tf_op jit(solution)/shard_map/ppermute | solution.py:178
  66.9 1.6 %collective-permute-start.17 = (bf16[2,512,128]{2,1,0:T(8,128)(2,1)S(1)}, bf16[2,512,128]{2,1,0:T(8,128)(2,1)S(1)}, u32[]{:S(2)}, u32[]{:S(2)}) collective-permute-start(bf16[2,512,128]{2,1,0:T(8,128)(2,1)S(1)} %add_convert_fusion.15), channel_id=1, source_target_pairs={{0,16},{8,24},{16,0},{24,8},{1,17},{9,25},{17,1},{25,9},{2,18},{10... | collective-permute-start | bytes 786440 | tf_op jit(solution)/shard_map/ppermute | solution.py:173
  68.5 1.5 %collective-permute-start.18 = (bf16[2,512,128]{2,1,0:T(8,128)(2,1)S(1)}, bf16[2,512,128]{2,1,0:T(8,128)(2,1)S(1)}, u32[]{:S(2)}, u32[]{:S(2)}) collective-permute-start(bf16[2,512,128]{2,1,0:T(8,128)(2,1)S(1)} %add_convert_fusion.14), channel_id=1, source_target_pairs={{0,8},{8,0},{16,24},{24,16},{1,9},{9,1},{17,25},{25,17},{2,10},{10... | collective-permute-start | bytes 786440 | tf_op jit(solution)/shard_map/ppermute | solution.py:173
  70.0 2.1 %project.10 = (bf16[2,512,256]{2,1,0:T(8,128)(2,1)S(1)}, f32[2,512,256]{2,1,0:T(8,128)S(1)}) custom-call(bf16[512,2048]{1,0:T(8,128)(2,1)S(1)} %attention.3.pair_ref, bf16[2,256,512]{2,1,0:T(8,128)(2,1)S(1)} %constant_dynamic-update-slice_fusion.4.refs_0_, bf16[2,256,512]{2,1,0:T(8,128)(2,1)S(1)} %collective-permute-done.11.refs_1_, ...), custom_call_target="tpu_custom_call" | custom-call | flops 262144 | bytes 512 | tf_op jit(solution)/shard_map/project/pallas_call | solution.py:151
  72.1 2.1 %project.11 = (bf16[2,512,256]{2,1,0:T(8,128)(2,1)S(1)}, f32[2,512,256]{2,1,0:T(8,128)S(1)}) custom-call(bf16[512,2048]{1,0:T(8,128)(2,1)S(1)} %attention.2.pair_ref, bf16[2,256,512]{2,1,0:T(8,128)(2,1)S(1)} %constant_dynamic-update-slice_fusion.4.refs_0_, bf16[2,256,512]{2,1,0:T(8,128)(2,1)S(1)} %collective-permute-done.11.refs_1_, ...), custom_call_target="tpu_custom_call" | custom-call | flops 262144 | bytes 512 | tf_op jit(solution)/shard_map/project/pallas_call | solution.py:151
  74.8 3.2 %collective-permute-done.14 = bf16[2,128,512]{2,1,0:T(8,128)(2,1)S(1)} collective-permute-done((bf16[2,128,512]{2,1,0:T(8,128)(2,1)S(1)}, bf16[2,128,512]{2,1,0:T(8,128)(2,1)S(1)}, u32[]{:S(2)}, u32[]{:S(2)}) %collective-permute-start.14) | collective-permute-done | bytes 262176 | tf_op jit(solution)/shard_map/ppermute | solution.py:178
  78.0 1.5 %collective-permute-start.20 = (bf16[2,512,256]{2,1,0:T(8,128)(2,1)S(1)}, bf16[2,512,256]{2,1,0:T(8,128)(2,1)S(1)}, u32[]{:S(2)}, u32[]{:S(2)}) collective-permute-start(bf16[2,512,256]{2,1,0:T(8,128)(2,1)S(1)} %get-tuple-element.117), channel_id=1, source_target_pairs={{0,8},{8,0},{16,24},{24,16},{1,9},{9,1},{17,25},{25,17},{2,10},{10... | collective-permute-start | bytes 1572872 | tf_op jit(solution)/shard_map/ppermute | solution.py:173
  80.2 3.4 %collective-permute-start.23 = (bf16[2,128,512]{2,1,0:T(8,128)(2,1)}, bf16[2,128,512]{2,1,0:T(8,128)(2,1)}, u32[]{:S(2)}, u32[]{:S(2)}) collective-permute-start(bf16[2,128,512]{2,1,0:T(8,128)(2,1)} %get-tuple-element.126), channel_id=1, source_target_pairs={{0,6},{1,7},{2,0},{3,1},{4,2},{5,3},{6,4},{7,5},{8,14},{9,15},{10,... | collective-permute-start | bytes 786440 | tf_op jit(solution)/shard_map/ppermute | solution.py:178
  83.5 1.0 constant_dynamic-update-slice_fusion.13
  84.6 1.0 constant_dynamic-update-slice_fusion.12.refs_0_
  85.5 1.8 %collective-permute-done.21 = bf16[2,512,256]{2,1,0:T(8,128)(2,1)S(1)} collective-permute-done((bf16[2,512,256]{2,1,0:T(8,128)(2,1)S(1)}, bf16[2,512,256]{2,1,0:T(8,128)(2,1)S(1)}, u32[]{:S(2)}, u32[]{:S(2)}) %collective-permute-start.21) | collective-permute-done | bytes 524320 | tf_op jit(solution)/shard_map/ppermute | solution.py:173
  87.3 4.5 %collective-permute-done.20 = bf16[2,512,256]{2,1,0:T(8,128)(2,1)S(1)} collective-permute-done((bf16[2,512,256]{2,1,0:T(8,128)(2,1)S(1)}, bf16[2,512,256]{2,1,0:T(8,128)(2,1)S(1)}, u32[]{:S(2)}, u32[]{:S(2)}) %collective-permute-start.20) | collective-permute-done | bytes 524320 | tf_op jit(solution)/shard_map/ppermute | solution.py:173
  93.5 1.6 %collective-permute-start.25 = (bf16[2,512,128]{2,1,0:T(8,128)(2,1)}, bf16[2,512,128]{2,1,0:T(8,128)(2,1)S(1)}, u32[]{:S(2)}, u32[]{:S(2)}) collective-permute-start(bf16[2,512,128]{2,1,0:T(8,128)(2,1)} %add_convert_fusion.11), channel_id=1, source_target_pairs={{0,16},{8,24},{16,0},{24,8},{1,17},{9,25},{17,1},{25,9},{2,18},{10... | collective-permute-start | bytes 786440 | tf_op jit(solution)/shard_map/ppermute | solution.py:173
  95.1 1.5 %collective-permute-start.26 = (bf16[2,512,128]{2,1,0:T(8,128)(2,1)}, bf16[2,512,128]{2,1,0:T(8,128)(2,1)}, u32[]{:S(2)}, u32[]{:S(2)}) collective-permute-start(bf16[2,512,128]{2,1,0:T(8,128)(2,1)} %add_convert_fusion.10), channel_id=1, source_target_pairs={{0,8},{8,0},{16,24},{24,16},{1,9},{9,1},{17,25},{25,17},{2,10},{10... | collective-permute-start | bytes 786440 | tf_op jit(solution)/shard_map/ppermute | solution.py:173
  96.5 2.1 %project.12 = (bf16[2,512,256]{2,1,0:T(8,128)(2,1)S(1)}, f32[2,512,256]{2,1,0:T(8,128)S(1)}) custom-call(bf16[512,2048]{1,0:T(8,128)(2,1)S(1)} %attention.3.pair_ref, bf16[2,256,512]{2,1,0:T(8,128)(2,1)S(1)} %constant_dynamic-update-slice_fusion.8.refs_0_, bf16[2,256,512]{2,1,0:T(8,128)(2,1)S(1)} %collective-permute-done.15.refs_1_, ...), custom_call_target="tpu_custom_call" | custom-call | flops 262144 | bytes 512 | tf_op jit(solution)/shard_map/project/pallas_call | solution.py:151
  98.7 2.1 %project.13 = (bf16[2,512,256]{2,1,0:T(8,128)(2,1)S(1)}, f32[2,512,256]{2,1,0:T(8,128)S(1)}) custom-call(bf16[512,2048]{1,0:T(8,128)(2,1)S(1)} %attention.2.pair_ref, bf16[2,256,512]{2,1,0:T(8,128)(2,1)S(1)} %constant_dynamic-update-slice_fusion.8.refs_0_, bf16[2,256,512]{2,1,0:T(8,128)(2,1)S(1)} %collective-permute-done.15.refs_1_, ...), custom_call_target="tpu_custom_call" | custom-call | flops 262144 | bytes 512 | tf_op jit(solution)/shard_map/project/pallas_call | solution.py:151
  105.0 8.7 %collective-permute-done.29 = bf16[2,512,256]{2,1,0:T(8,128)(2,1)S(1)} collective-permute-done((bf16[2,512,256]{2,1,0:T(8,128)(2,1)S(1)}, bf16[2,512,256]{2,1,0:T(8,128)(2,1)S(1)}, u32[]{:S(2)}, u32[]{:S(2)}) %collective-permute-start.29) | collective-permute-done | bytes 524320 | tf_op jit(solution)/shard_map/ppermute | solution.py:173
  115.9 2.1 %project.14 = (bf16[2,512,256]{2,1,0:T(8,128)(2,1)S(1)}, f32[2,512,256]{2,1,0:T(8,128)S(1)}) custom-call(bf16[512,2048]{1,0:T(8,128)(2,1)S(1)} %attention.3.pair_ref, bf16[2,256,512]{2,1,0:T(8,128)(2,1)S(1)} %constant_dynamic-update-slice_fusion.12.refs_0_, bf16[2,256,512]{2,1,0:T(8,128)(2,1)S(1)} %collective-permute-done.24.refs_1_, ...), custom_call_target="tpu_custom_call" | custom-call | flops 262144 | bytes 512 | tf_op jit(solution)/shard_map/project/pallas_call | solution.py:151
  117.9 1.6 %collective-permute-start.33 = (bf16[2,512,256]{2,1,0:T(8,128)(2,1)S(1)}, bf16[2,512,256]{2,1,0:T(8,128)(2,1)S(1)}, u32[]{:S(2)}, u32[]{:S(2)}) collective-permute-start(bf16[2,512,256]{2,1,0:T(8,128)(2,1)S(1)} %get-tuple-element.156), channel_id=1, source_target_pairs={{0,8},{8,0},{16,24},{24,16},{1,9},{9,1},{17,25},{25,17},{2,10},{10... | collective-permute-start | bytes 1572872 | tf_op jit(solution)/shard_map/ppermute | solution.py:173
  119.7 2.1 %project.15 = (bf16[2,512,256]{2,1,0:T(8,128)(2,1)S(1)}, f32[2,512,256]{2,1,0:T(8,128)S(1)}) custom-call(bf16[512,2048]{1,0:T(8,128)(2,1)S(1)} %attention.2.pair_ref, bf16[2,256,512]{2,1,0:T(8,128)(2,1)S(1)} %constant_dynamic-update-slice_fusion.12.refs_0_, bf16[2,256,512]{2,1,0:T(8,128)(2,1)S(1)} %collective-permute-done.24.refs_1_, ...), custom_call_target="tpu_custom_call" | custom-call | flops 262144 | bytes 512 | tf_op jit(solution)/shard_map/project/pallas_call | solution.py:151
  121.8 1.6 %collective-permute-start.35 = (bf16[2,512,256]{2,1,0:T(8,128)(2,1)S(1)}, bf16[2,512,256]{2,1,0:T(8,128)(2,1)S(1)}, u32[]{:S(2)}, u32[]{:S(2)}) collective-permute-start(bf16[2,512,256]{2,1,0:T(8,128)(2,1)S(1)} %get-tuple-element.159), channel_id=1, source_target_pairs={{0,16},{8,24},{16,0},{24,8},{1,17},{9,25},{17,1},{25,9},{2,18},{10... | collective-permute-start | bytes 1572872 | tf_op jit(solution)/shard_map/ppermute | solution.py:173
  123.4 1.0 add_convert_fusion.8
  125.1 7.7 %collective-permute-done.33 = bf16[2,512,256]{2,1,0:T(8,128)(2,1)S(1)} collective-permute-done((bf16[2,512,256]{2,1,0:T(8,128)(2,1)S(1)}, bf16[2,512,256]{2,1,0:T(8,128)(2,1)S(1)}, u32[]{:S(2)}, u32[]{:S(2)}) %collective-permute-start.33) | collective-permute-done | bytes 524320 | tf_op jit(solution)/shard_map/ppermute | solution.py:173
  132.9 1.6 %collective-permute-start.34 = (bf16[2,512,128]{2,1,0:T(8,128)(2,1)S(1)}, bf16[2,512,128]{2,1,0:T(8,128)(2,1)S(1)}, u32[]{:S(2)}, u32[]{:S(2)}) collective-permute-start(bf16[2,512,128]{2,1,0:T(8,128)(2,1)S(1)} %add_convert_fusion.3), channel_id=1, source_target_pairs={{0,16},{8,24},{16,0},{24,8},{1,17},{9,25},{17,1},{25,9},{2,18},{10... | collective-permute-start | bytes 786440 | tf_op jit(solution)/shard_map/ppermute | solution.py:173
  134.6 2.1 %collective-permute-done.35 = bf16[2,512,256]{2,1,0:T(8,128)(2,1)S(1)} collective-permute-done((bf16[2,512,256]{2,1,0:T(8,128)(2,1)S(1)}, bf16[2,512,256]{2,1,0:T(8,128)(2,1)S(1)}, u32[]{:S(2)}, u32[]{:S(2)}) %collective-permute-start.35) | collective-permute-done | bytes 524320 | tf_op jit(solution)/shard_map/ppermute | solution.py:173
  137.4 2.2 %collective-permute-done.34 = bf16[2,512,128]{2,1,0:T(8,128)(2,1)S(1)} collective-permute-done((bf16[2,512,128]{2,1,0:T(8,128)(2,1)S(1)}, bf16[2,512,128]{2,1,0:T(8,128)(2,1)S(1)}, u32[]{:S(2)}, u32[]{:S(2)}) %collective-permute-start.34) | collective-permute-done | bytes 262176 | tf_op jit(solution)/shard_map/ppermute | solution.py:173
  139.7 3.5 %collective-permute-done.36 = bf16[2,512,128]{2,1,0:T(8,128)(2,1)S(1)} collective-permute-done((bf16[2,512,128]{2,1,0:T(8,128)(2,1)S(1)}, bf16[2,512,128]{2,1,0:T(8,128)(2,1)S(1)}, u32[]{:S(2)}, u32[]{:S(2)}) %collective-permute-start.36) | collective-permute-done | bytes 262176 | tf_op jit(solution)/shard_map/ppermute | solution.py:173
  143.6 1.5 %slice_bitcast_fusion = (bf16[1024,512]{1,0:T(8,128)(2,1)}, bf16[1024,512]{1,0:T(8,128)(2,1)}) fusion(bf16[2,1024,512]{2,1,0:T(8,128)(2,1)S(1)} %maximum_maximum_fusion), kind=kLoop, calls=%fused_computation.1 | loop fusion | bytes 4194304 | tf_op jit(solution)/shard_map/squeeze | solution.py:350
  (132 shorter events, 15.5 us)
Async XLA Ops:
  0.6 8.7 %copy-start.3 = (bf16[1024,2,128]{2,1,0:T(2,128)(2,1)S(1)}, bf16[1024,2,128]{2,1,0:T(2,128)(2,1)}, u32[]{:S(2)}) copy-start(bf16[1024,2,128]{2,1,0:T(2,128)(2,1)} %param.10) | copy-start | bytes 1572868
  3.2 18.5 %collective-permute-start.1 = (bf16[2,128,512]{2,1,0:T(8,128)(2,1)}, bf16[2,128,512]{2,1,0:T(8,128)(2,1)}, u32[]{:S(2)}, u32[]{:S(2)}) collective-permute-start(bf16[2,128,512]{2,1,0:T(8,128)(2,1)} %get-tuple-element.84), channel_id=1, source_target_pairs={{0,2},{1,3},{2,4},{3,5},{4,6},{5,7},{6,0},{7,1},{8,10},{9,11},{10,... | collective-permute-start | bytes 786440 | tf_op jit(solution)/shard_map/ppermute | solution.py:178
  6.2 15.5 %collective-permute-start.2 = (bf16[2,128,512]{2,1,0:T(8,128)(2,1)}, bf16[2,128,512]{2,1,0:T(8,128)(2,1)S(1)}, u32[]{:S(2)}, u32[]{:S(2)}) collective-permute-start(bf16[2,128,512]{2,1,0:T(8,128)(2,1)} %get-tuple-element.84), channel_id=1, source_target_pairs={{0,6},{1,7},{2,0},{3,1},{4,2},{5,3},{6,4},{7,5},{8,14},{9,15},{10,... | collective-permute-start | bytes 786440 | tf_op jit(solution)/shard_map/ppermute | solution.py:178
  10.3 11.3 %collective-permute-start = (bf16[224,512]{1,0:T(8,128)(2,1)}, bf16[224,512]{1,0:T(8,128)(2,1)}, u32[]{:S(2)}, u32[]{:S(2)}) collective-permute-start(bf16[224,512]{1,0:T(8,128)(2,1)} %slice.180), channel_id=1, source_target_pairs={{0,1},{1,2},{2,3},{3,4},{4,5},{5,6},{6,7},{8,9},{9,10},{10,11},{11... | collective-permute-start | bytes 688136 | tf_op jit(solution)/shard_map/ppermute | solution.py:247
  13.4 8.3 %copy-start.18 = (bf16[2,128,512]{2,1,0:T(8,128)(2,1)S(1)}, bf16[2,128,512]{2,1,0:T(8,128)(2,1)}, u32[]{:S(2)}) copy-start(bf16[2,128,512]{2,1,0:T(8,128)(2,1)} %get-tuple-element.84) | copy-start | bytes 786436
  13.4 9.4 %copy-start.17 = (bf16[2,128,512]{2,1,0:T(8,128)(2,1)S(1)}, bf16[2,128,512]{2,1,0:T(8,128)(2,1)}, u32[]{:S(2)}) copy-start(bf16[2,128,512]{2,1,0:T(8,128)(2,1)} %get-tuple-element.99) | copy-start | bytes 786436
  22.7 16.2 %collective-permute-start.4 = (bf16[2,256,512]{2,1,0:T(8,128)(2,1)S(1)}, bf16[2,256,512]{2,1,0:T(8,128)(2,1)S(1)}, u32[]{:S(2)}, u32[]{:S(2)}) collective-permute-start(bf16[2,256,512]{2,1,0:T(8,128)(2,1)S(1)} %constant_dynamic-update-slice_fusion.refs_0_), channel_id=1, source_target_pairs={{0,1},{1,0},{2,3},{3,2},{4,5},{5,4},{6,7},{7,6},{8,9},{9,8},{10,11... | collective-permute-start | bytes 1572872 | tf_op jit(solution)/shard_map/ppermute | solution.py:182
  22.8 12.2 %collective-permute-start.5 = (bf16[2,128,512]{2,1,0:T(8,128)(2,1)S(1)}, bf16[2,128,512]{2,1,0:T(8,128)(2,1)S(1)}, u32[]{:S(2)}, u32[]{:S(2)}) collective-permute-start(bf16[2,128,512]{2,1,0:T(8,128)(2,1)S(1)} %copy-done.17), channel_id=1, source_target_pairs={{0,2},{1,3},{2,4},{3,5},{4,6},{5,7},{6,0},{7,1},{8,10},{9,11},{10,... | collective-permute-start | bytes 786440 | tf_op jit(solution)/shard_map/ppermute | solution.py:178
  24.3 14.6 %collective-permute-start.3 = (bf16[2,128,512]{2,1,0:T(8,128)(2,1)}, bf16[2,128,512]{2,1,0:T(8,128)(2,1)S(1)}, u32[]{:S(2)}, u32[]{:S(2)}) collective-permute-start(bf16[2,128,512]{2,1,0:T(8,128)(2,1)} %collective-permute-done.1), channel_id=1, source_target_pairs={{0,2},{1,3},{2,4},{3,5},{4,6},{5,7},{6,0},{7,1},{8,10},{9,11},{10,... | collective-permute-start | bytes 786440 | tf_op jit(solution)/shard_map/ppermute | solution.py:178
  35.0 4.6 %copy-start.16 = (bf16[2,128,512]{2,1,0:T(8,128)(2,1)S(1)}, bf16[2,128,512]{2,1,0:T(8,128)(2,1)}, u32[]{:S(2)}) copy-start(bf16[2,128,512]{2,1,0:T(8,128)(2,1)} %get-tuple-element.105) | copy-start | bytes 786436
  39.0 4.5 %collective-permute-start.6 = (bf16[2,256,512]{2,1,0:T(8,128)(2,1)S(1)}, bf16[2,256,512]{2,1,0:T(8,128)(2,1)S(1)}, u32[]{:S(2)}, u32[]{:S(2)}) collective-permute-start(bf16[2,256,512]{2,1,0:T(8,128)(2,1)S(1)} %constant_dynamic-update-slice_fusion.2.refs_2_), channel_id=1, source_target_pairs={{0,1},{1,0},{2,3},{3,2},{4,5},{5,4},{6,7},{7,6},{8,9},{9,8},{10,11... | collective-permute-start | bytes 1572872 | tf_op jit(solution)/shard_map/ppermute | solution.py:182
  39.1 22.8 %collective-permute-start.11 = (bf16[2,256,512]{2,1,0:T(8,128)(2,1)S(1)}, bf16[2,256,512]{2,1,0:T(8,128)(2,1)S(1)}, u32[]{:S(2)}, u32[]{:S(2)}) collective-permute-start(bf16[2,256,512]{2,1,0:T(8,128)(2,1)S(1)} %constant_dynamic-update-slice_fusion.4.refs_0_), channel_id=1, source_target_pairs={{0,1},{1,0},{2,3},{3,2},{4,5},{5,4},{6,7},{7,6},{8,9},{9,8},{10,11... | collective-permute-start | bytes 1572872 | tf_op jit(solution)/shard_map/ppermute | solution.py:182
  39.7 11.0 %collective-permute-start.12 = (bf16[2,128,512]{2,1,0:T(8,128)(2,1)S(1)}, bf16[2,128,512]{2,1,0:T(8,128)(2,1)S(1)}, u32[]{:S(2)}, u32[]{:S(2)}) collective-permute-start(bf16[2,128,512]{2,1,0:T(8,128)(2,1)S(1)} %copy-done.16), channel_id=1, source_target_pairs={{0,2},{1,3},{2,4},{3,5},{4,6},{5,7},{6,0},{7,1},{8,10},{9,11},{10,... | collective-permute-start | bytes 786440 | tf_op jit(solution)/shard_map/ppermute | solution.py:178
  39.7 14.0 %collective-permute-start.10 = (bf16[2,128,512]{2,1,0:T(8,128)(2,1)S(1)}, bf16[2,128,512]{2,1,0:T(8,128)(2,1)S(1)}, u32[]{:S(2)}, u32[]{:S(2)}) collective-permute-start(bf16[2,128,512]{2,1,0:T(8,128)(2,1)S(1)} %copy-done.17), channel_id=1, source_target_pairs={{0,6},{1,7},{2,0},{3,1},{4,2},{5,3},{6,4},{7,5},{8,14},{9,15},{10,... | collective-permute-start | bytes 786440 | tf_op jit(solution)/shard_map/ppermute | solution.py:178
  43.5 18.4 %collective-permute-start.9 = (bf16[2,128,512]{2,1,0:T(8,128)(2,1)S(1)}, bf16[2,128,512]{2,1,0:T(8,128)(2,1)S(1)}, u32[]{:S(2)}, u32[]{:S(2)}) collective-permute-start(bf16[2,128,512]{2,1,0:T(8,128)(2,1)S(1)} %collective-permute-done.5), channel_id=1, source_target_pairs={{0,2},{1,3},{2,4},{3,5},{4,6},{5,7},{6,0},{7,1},{8,10},{9,11},{10,... | collective-permute-start | bytes 786440 | tf_op jit(solution)/shard_map/ppermute | solution.py:178
  47.7 14.5 %collective-permute-start.8 = (bf16[2,512,256]{2,1,0:T(8,128)(2,1)S(1)}, bf16[2,512,256]{2,1,0:T(8,128)(2,1)S(1)}, u32[]{:S(2)}, u32[]{:S(2)}) collective-permute-start(bf16[2,512,256]{2,1,0:T(8,128)(2,1)S(1)} %get-tuple-element.98), channel_id=1, source_target_pairs={{0,16},{8,24},{16,0},{24,8},{1,17},{9,25},{17,1},{25,9},{2,18},{10... | collective-permute-start | bytes 1572872 | tf_op jit(solution)/shard_map/ppermute | solution.py:173
  50.7 15.4 %collective-permute-start.7 = (bf16[2,512,256]{2,1,0:T(8,128)(2,1)S(1)}, bf16[2,512,256]{2,1,0:T(8,128)(2,1)S(1)}, u32[]{:S(2)}, u32[]{:S(2)}) collective-permute-start(bf16[2,512,256]{2,1,0:T(8,128)(2,1)S(1)} %get-tuple-element.95), channel_id=1, source_target_pairs={{0,8},{8,0},{16,24},{24,16},{1,9},{9,1},{17,25},{25,17},{2,10},{10... | collective-permute-start | bytes 1572872 | tf_op jit(solution)/shard_map/ppermute | solution.py:173
  53.6 13.3 %collective-permute-start.16 = (bf16[2,128,512]{2,1,0:T(8,128)(2,1)}, bf16[2,128,512]{2,1,0:T(8,128)(2,1)}, u32[]{:S(2)}, u32[]{:S(2)}) collective-permute-start(bf16[2,128,512]{2,1,0:T(8,128)(2,1)} %get-tuple-element.126), channel_id=1, source_target_pairs={{0,2},{1,3},{2,4},{3,5},{4,6},{5,7},{6,0},{7,1},{8,10},{9,11},{10,... | collective-permute-start | bytes 786440 | tf_op jit(solution)/shard_map/ppermute | solution.py:178
  62.0 6.6 %collective-permute-start.19 = (bf16[2,256,512]{2,1,0:T(8,128)(2,1)S(1)}, bf16[2,256,512]{2,1,0:T(8,128)(2,1)S(1)}, u32[]{:S(2)}, u32[]{:S(2)}) collective-permute-start(bf16[2,256,512]{2,1,0:T(8,128)(2,1)S(1)} %constant_dynamic-update-slice_fusion.6.refs_2_), channel_id=1, source_target_pairs={{0,1},{1,0},{2,3},{3,2},{4,5},{5,4},{6,7},{7,6},{8,9},{9,8},{10,11... | collective-permute-start | bytes 1572872 | tf_op jit(solution)/shard_map/ppermute | solution.py:182
  62.0 12.2 %collective-permute-start.13 = (bf16[2,128,512]{2,1,0:T(8,128)(2,1)S(1)}, bf16[2,128,512]{2,1,0:T(8,128)(2,1)S(1)}, u32[]{:S(2)}, u32[]{:S(2)}) collective-permute-start(bf16[2,128,512]{2,1,0:T(8,128)(2,1)S(1)} %collective-permute-done.12), channel_id=1, source_target_pairs={{0,2},{1,3},{2,4},{3,5},{4,6},{5,7},{6,0},{7,1},{8,10},{9,11},{10,... | collective-permute-start | bytes 786440 | tf_op jit(solution)/shard_map/ppermute | solution.py:178
  62.2 15.8 %collective-permute-start.14 = (bf16[2,128,512]{2,1,0:T(8,128)(2,1)S(1)}, bf16[2,128,512]{2,1,0:T(8,128)(2,1)S(1)}, u32[]{:S(2)}, u32[]{:S(2)}) collective-permute-start(bf16[2,128,512]{2,1,0:T(8,128)(2,1)S(1)} %copy-done.16), channel_id=1, source_target_pairs={{0,6},{1,7},{2,0},{3,1},{4,2},{5,3},{6,4},{7,5},{8,14},{9,15},{10,... | collective-permute-start | bytes 786440 | tf_op jit(solution)/shard_map/ppermute | solution.py:178
  66.0 13.5 %collective-permute-start.15 = (bf16[2,256,512]{2,1,0:T(8,128)(2,1)S(1)}, bf16[2,256,512]{2,1,0:T(8,128)(2,1)S(1)}, u32[]{:S(2)}, u32[]{:S(2)}) collective-permute-start(bf16[2,256,512]{2,1,0:T(8,128)(2,1)S(1)} %constant_dynamic-update-slice_fusion.8.refs_0_), channel_id=1, source_target_pairs={{0,1},{1,0},{2,3},{3,2},{4,5},{5,4},{6,7},{7,6},{8,9},{9,8},{10,11... | collective-permute-start | bytes 1572872 | tf_op jit(solution)/shard_map/ppermute | solution.py:182
  66.9 12.6 %collective-permute-start.17 = (bf16[2,512,128]{2,1,0:T(8,128)(2,1)S(1)}, bf16[2,512,128]{2,1,0:T(8,128)(2,1)S(1)}, u32[]{:S(2)}, u32[]{:S(2)}) collective-permute-start(bf16[2,512,128]{2,1,0:T(8,128)(2,1)S(1)} %add_convert_fusion.15), channel_id=1, source_target_pairs={{0,16},{8,24},{16,0},{24,8},{1,17},{9,25},{17,1},{25,9},{2,18},{10... | collective-permute-start | bytes 786440 | tf_op jit(solution)/shard_map/ppermute | solution.py:173
  68.5 11.0 %collective-permute-start.18 = (bf16[2,512,128]{2,1,0:T(8,128)(2,1)S(1)}, bf16[2,512,128]{2,1,0:T(8,128)(2,1)S(1)}, u32[]{:S(2)}, u32[]{:S(2)}) collective-permute-start(bf16[2,512,128]{2,1,0:T(8,128)(2,1)S(1)} %add_convert_fusion.14), channel_id=1, source_target_pairs={{0,8},{8,0},{16,24},{24,16},{1,9},{9,1},{17,25},{25,17},{2,10},{10... | collective-permute-start | bytes 786440 | tf_op jit(solution)/shard_map/ppermute | solution.py:173
  74.2 13.1 %collective-permute-start.21 = (bf16[2,512,256]{2,1,0:T(8,128)(2,1)S(1)}, bf16[2,512,256]{2,1,0:T(8,128)(2,1)S(1)}, u32[]{:S(2)}, u32[]{:S(2)}) collective-permute-start(bf16[2,512,256]{2,1,0:T(8,128)(2,1)S(1)} %get-tuple-element.119), channel_id=1, source_target_pairs={{0,16},{8,24},{16,0},{24,8},{1,17},{9,25},{17,1},{25,9},{2,18},{10... | collective-permute-start | bytes 1572872 | tf_op jit(solution)/shard_map/ppermute | solution.py:173
  78.0 13.9 %collective-permute-start.20 = (bf16[2,512,256]{2,1,0:T(8,128)(2,1)S(1)}, bf16[2,512,256]{2,1,0:T(8,128)(2,1)S(1)}, u32[]{:S(2)}, u32[]{:S(2)}) collective-permute-start(bf16[2,512,256]{2,1,0:T(8,128)(2,1)S(1)} %get-tuple-element.117), channel_id=1, source_target_pairs={{0,8},{8,0},{16,24},{24,16},{1,9},{9,1},{17,25},{25,17},{2,10},{10... | collective-permute-start | bytes 1572872 | tf_op jit(solution)/shard_map/ppermute | solution.py:173
  79.5 6.0 %copy-start.12 = (bf16[2,512,128]{2,1,0:T(8,128)(2,1)}, bf16[2,512,128]{2,1,0:T(8,128)(2,1)S(1)}, u32[]{:S(2)}) copy-start(bf16[2,512,128]{2,1,0:T(8,128)(2,1)S(1)} %collective-permute-done.17) | copy-start | bytes 786436
  79.6 15.5 %collective-permute-start.27 = (bf16[2,256,512]{2,1,0:T(8,128)(2,1)S(1)}, bf16[2,256,512]{2,1,0:T(8,128)(2,1)S(1)}, u32[]{:S(2)}, u32[]{:S(2)}) collective-permute-start(bf16[2,256,512]{2,1,0:T(8,128)(2,1)S(1)} %constant_dynamic-update-slice_fusion.10.refs_2_), channel_id=1, source_target_pairs={{0,1},{1,0},{2,3},{3,2},{4,5},{5,4},{6,7},{7,6},{8,9},{9,8},{10,11... | collective-permute-start | bytes 1572872 | tf_op jit(solution)/shard_map/ppermute | solution.py:182
  79.7 21.1 %collective-permute-start.22 = (bf16[2,128,512]{2,1,0:T(8,128)(2,1)}, bf16[2,128,512]{2,1,0:T(8,128)(2,1)}, u32[]{:S(2)}, u32[]{:S(2)}) collective-permute-start(bf16[2,128,512]{2,1,0:T(8,128)(2,1)} %collective-permute-done.16), channel_id=1, source_target_pairs={{0,2},{1,3},{2,4},{3,5},{4,6},{5,7},{6,0},{7,1},{8,10},{9,11},{10,... | collective-permute-start | bytes 786440 | tf_op jit(solution)/shard_map/ppermute | solution.py:178
  80.2 21.2 %collective-permute-start.23 = (bf16[2,128,512]{2,1,0:T(8,128)(2,1)}, bf16[2,128,512]{2,1,0:T(8,128)(2,1)}, u32[]{:S(2)}, u32[]{:S(2)}) collective-permute-start(bf16[2,128,512]{2,1,0:T(8,128)(2,1)} %get-tuple-element.126), channel_id=1, source_target_pairs={{0,6},{1,7},{2,0},{3,1},{4,2},{5,3},{6,4},{7,5},{8,14},{9,15},{10,... | collective-permute-start | bytes 786440 | tf_op jit(solution)/shard_map/ppermute | solution.py:178
  87.3 7.7 %copy-start.6 = (bf16[2,512,256]{2,1,0:T(8,128)(2,1)}, bf16[2,512,256]{2,1,0:T(8,128)(2,1)S(1)}, u32[]{:S(2)}) copy-start(bf16[2,512,256]{2,1,0:T(8,128)(2,1)S(1)} %collective-permute-done.21) | copy-start | bytes 1572868
  87.3 14.6 %collective-permute-start.24 = (bf16[2,256,512]{2,1,0:T(8,128)(2,1)S(1)}, bf16[2,256,512]{2,1,0:T(8,128)(2,1)S(1)}, u32[]{:S(2)}, u32[]{:S(2)}) collective-permute-start(bf16[2,256,512]{2,1,0:T(8,128)(2,1)S(1)} %constant_dynamic-update-slice_fusion.12.refs_0_), channel_id=1, source_target_pairs={{0,1},{1,0},{2,3},{3,2},{4,5},{5,4},{6,7},{7,6},{8,9},{9,8},{10,11... | collective-permute-start | bytes 1572872 | tf_op jit(solution)/shard_map/ppermute | solution.py:182
  91.9 6.7 %copy-start.8 = (bf16[2,512,256]{2,1,0:T(8,128)(2,1)}, bf16[2,512,256]{2,1,0:T(8,128)(2,1)S(1)}, u32[]{:S(2)}) copy-start(bf16[2,512,256]{2,1,0:T(8,128)(2,1)S(1)} %collective-permute-done.20) | copy-start | bytes 1572868
  93.5 8.5 %collective-permute-start.25 = (bf16[2,512,128]{2,1,0:T(8,128)(2,1)}, bf16[2,512,128]{2,1,0:T(8,128)(2,1)S(1)}, u32[]{:S(2)}, u32[]{:S(2)}) collective-permute-start(bf16[2,512,128]{2,1,0:T(8,128)(2,1)} %add_convert_fusion.11), channel_id=1, source_target_pairs={{0,16},{8,24},{16,0},{24,8},{1,17},{9,25},{17,1},{25,9},{2,18},{10... | collective-permute-start | bytes 786440 | tf_op jit(solution)/shard_map/ppermute | solution.py:173
  95.1 7.8 %collective-permute-start.26 = (bf16[2,512,128]{2,1,0:T(8,128)(2,1)}, bf16[2,512,128]{2,1,0:T(8,128)(2,1)}, u32[]{:S(2)}, u32[]{:S(2)}) collective-permute-start(bf16[2,512,128]{2,1,0:T(8,128)(2,1)} %add_convert_fusion.10), channel_id=1, source_target_pairs={{0,8},{8,0},{16,24},{24,16},{1,9},{9,1},{17,25},{25,17},{2,10},{10... | collective-permute-start | bytes 786440 | tf_op jit(solution)/shard_map/ppermute | solution.py:173
  98.6 16.0 %copy-start.1 = (f32[2,512,256]{2,1,0:T(8,128)}, f32[2,512,256]{2,1,0:T(8,128)S(1)}, u32[]{:S(2)}) copy-start(f32[2,512,256]{2,1,0:T(8,128)S(1)} %get-tuple-element.142) | copy-start | bytes 3145732
  100.8 13.0 %collective-permute-start.28 = (bf16[2,512,256]{2,1,0:T(8,128)(2,1)S(1)}, bf16[2,512,256]{2,1,0:T(8,128)(2,1)S(1)}, u32[]{:S(2)}, u32[]{:S(2)}) collective-permute-start(bf16[2,512,256]{2,1,0:T(8,128)(2,1)S(1)} %get-tuple-element.137), channel_id=1, source_target_pairs={{0,8},{8,0},{16,24},{24,16},{1,9},{9,1},{17,25},{25,17},{2,10},{10... | collective-permute-start | bytes 1572872 | tf_op jit(solution)/shard_map/ppermute | solution.py:173
  101.4 12.3 %collective-permute-start.29 = (bf16[2,512,256]{2,1,0:T(8,128)(2,1)S(1)}, bf16[2,512,256]{2,1,0:T(8,128)(2,1)S(1)}, u32[]{:S(2)}, u32[]{:S(2)}) collective-permute-start(bf16[2,512,256]{2,1,0:T(8,128)(2,1)S(1)} %get-tuple-element.139), channel_id=1, source_target_pairs={{0,16},{8,24},{16,0},{24,8},{1,17},{9,25},{17,1},{25,9},{2,18},{10... | collective-permute-start | bytes 1572872 | tf_op jit(solution)/shard_map/ppermute | solution.py:173
  104.8 11.0 %collective-permute-start.32 = (bf16[2,256,512]{2,1,0:T(8,128)(2,1)S(1)}, bf16[2,256,512]{2,1,0:T(8,128)(2,1)S(1)}, u32[]{:S(2)}, u32[]{:S(2)}) collective-permute-start(bf16[2,256,512]{2,1,0:T(8,128)(2,1)S(1)} %constant_dynamic-update-slice_fusion.14.refs_2_), channel_id=1, source_target_pairs={{0,1},{1,0},{2,3},{3,2},{4,5},{5,4},{6,7},{7,6},{8,9},{9,8},{10,11... | collective-permute-start | bytes 1572872 | tf_op jit(solution)/shard_map/ppermute | solution.py:182
  115.4 9.6 %collective-permute-start.30 = (bf16[2,512,128]{2,1,0:T(8,128)(2,1)}, bf16[2,512,128]{2,1,0:T(8,128)(2,1)S(1)}, u32[]{:S(2)}, u32[]{:S(2)}) collective-permute-start(bf16[2,512,128]{2,1,0:T(8,128)(2,1)} %add_convert_fusion.7), channel_id=1, source_target_pairs={{0,16},{8,24},{16,0},{24,8},{1,17},{9,25},{17,1},{25,9},{2,18},{10... | collective-permute-start | bytes 786440 | tf_op jit(solution)/shard_map/ppermute | solution.py:173
  117.9 14.9 %collective-permute-start.33 = (bf16[2,512,256]{2,1,0:T(8,128)(2,1)S(1)}, bf16[2,512,256]{2,1,0:T(8,128)(2,1)S(1)}, u32[]{:S(2)}, u32[]{:S(2)}) collective-permute-start(bf16[2,512,256]{2,1,0:T(8,128)(2,1)S(1)} %get-tuple-element.156), channel_id=1, source_target_pairs={{0,8},{8,0},{16,24},{24,16},{1,9},{9,1},{17,25},{25,17},{2,10},{10... | collective-permute-start | bytes 1572872 | tf_op jit(solution)/shard_map/ppermute | solution.py:173
  119.6 4.8 %copy-start.19 = (bf16[2,512,128]{2,1,0:T(8,128)(2,1)S(1)}, bf16[2,512,128]{2,1,0:T(8,128)(2,1)}, u32[]{:S(2)}) copy-start(bf16[2,512,128]{2,1,0:T(8,128)(2,1)} %add_convert_fusion.6) | copy-start | bytes 786436
  119.7 5.4 %copy-start.2 = (f32[2,512,256]{2,1,0:T(8,128)S(1)}, f32[2,512,256]{2,1,0:T(8,128)}, u32[]{:S(2)}) copy-start(f32[2,512,256]{2,1,0:T(8,128)} %copy-done.1) | copy-start | bytes 3145732
  119.7 5.4 %copy-start.11 = (bf16[2,512,256]{2,1,0:T(8,128)(2,1)S(1)}, bf16[2,512,256]{2,1,0:T(8,128)(2,1)}, u32[]{:S(2)}) copy-start(bf16[2,512,256]{2,1,0:T(8,128)(2,1)} %copy-done.10) | copy-start | bytes 1572868
  121.8 14.9 %collective-permute-start.35 = (bf16[2,512,256]{2,1,0:T(8,128)(2,1)S(1)}, bf16[2,512,256]{2,1,0:T(8,128)(2,1)S(1)}, u32[]{:S(2)}, u32[]{:S(2)}) collective-permute-start(bf16[2,512,256]{2,1,0:T(8,128)(2,1)S(1)} %get-tuple-element.159), channel_id=1, source_target_pairs={{0,16},{8,24},{16,0},{24,8},{1,17},{9,25},{17,1},{25,9},{2,18},{10... | collective-permute-start | bytes 1572872 | tf_op jit(solution)/shard_map/ppermute | solution.py:173
  124.4 12.9 %collective-permute-start.31 = (bf16[2,512,128]{2,1,0:T(8,128)(2,1)S(1)}, bf16[2,512,128]{2,1,0:T(8,128)(2,1)S(1)}, u32[]{:S(2)}, u32[]{:S(2)}) collective-permute-start(bf16[2,512,128]{2,1,0:T(8,128)(2,1)S(1)} %copy-done.19), channel_id=1, source_target_pairs={{0,8},{8,0},{16,24},{24,16},{1,9},{9,1},{17,25},{25,17},{2,10},{10... | collective-permute-start | bytes 786440 | tf_op jit(solution)/shard_map/ppermute | solution.py:173
  132.9 6.7 %collective-permute-start.34 = (bf16[2,512,128]{2,1,0:T(8,128)(2,1)S(1)}, bf16[2,512,128]{2,1,0:T(8,128)(2,1)S(1)}, u32[]{:S(2)}, u32[]{:S(2)}) collective-permute-start(bf16[2,512,128]{2,1,0:T(8,128)(2,1)S(1)} %add_convert_fusion.3), channel_id=1, source_target_pairs={{0,16},{8,24},{16,0},{24,8},{1,17},{9,25},{17,1},{25,9},{2,18},{10... | collective-permute-start | bytes 786440 | tf_op jit(solution)/shard_map/ppermute | solution.py:173
  136.8 6.4 %collective-permute-start.36 = (bf16[2,512,128]{2,1,0:T(8,128)(2,1)S(1)}, bf16[2,512,128]{2,1,0:T(8,128)(2,1)S(1)}, u32[]{:S(2)}, u32[]{:S(2)}) collective-permute-start(bf16[2,512,128]{2,1,0:T(8,128)(2,1)S(1)} %add_convert_fusion.1), channel_id=1, source_target_pairs={{0,8},{8,0},{16,24},{24,16},{1,9},{9,1},{17,25},{25,17},{2,10},{10... | collective-permute-start | bytes 786440 | tf_op jit(solution)/shard_map/ppermute | solution.py:173
  (10 other events, 30.8 us)

commit v4 on v3

v4 whole, which is shorter than its diff:
```python
import functools
import math

import jax
import jax.numpy as jnp
from jax import lax
from jax.experimental import pallas as pl
from jax.experimental.pallas import tpu as pltpu
from jax.sharding import PartitionSpec as P

STRETCH = 32
WINDOW = 224
GROUPS = (2, 2)
TILE = 128
CORES = 2
RELATIVE = (1, 3, 2, 0)

masked_score = -1e30
vmem_bytes = 48 * 1024 * 1024


def arrange_kernel(kv_ref, tangent_ref, value_ref, *group_refs):
    columns = tangent_ref.shape[1] // len(RELATIVE)
    chunk = 0
    for group_ref in group_refs:
        part = group_ref.shape[3] // len(RELATIVE)
        for index in range(group_ref.shape[0]):
            for place, flip in enumerate(RELATIVE):
                start = pl.multiple_of((kv_ref[0] ^ flip) * columns + chunk * part, part)
                to = slice(place * part, (place + 1) * part)
                group_ref[index, 0, :, to] = tangent_ref[:, pl.ds(start, part)]
                group_ref[index, 1, :, to] = value_ref[:, pl.ds(start, part)]
            chunk += 1


def arrange(kv_index, tangent, value):
    rows, columns = value.shape
    shapes = [
        jax.ShapeDtypeStruct((count, 2, rows, columns // sum(GROUPS)), value.dtype)
        for count in GROUPS
    ]
    return pl.pallas_call(
        arrange_kernel,
        in_specs=[
            pl.BlockSpec(memory_space=pltpu.SMEM),
            pl.BlockSpec(memory_space=pltpu.VMEM),
            pl.BlockSpec(memory_space=pltpu.VMEM),
        ],
        out_specs=[pl.BlockSpec(memory_space=pltpu.VMEM)] * len(GROUPS),
        out_shape=shapes,
        name="arrange",
    )(kv_index.reshape(1), tangent, value)


def attention_kernel(heads, head_dim, offset, order_ref, q_ref, qt_ref, ctx_ref, low_ref, out_ref):
    rows = q_ref.shape[0]
    span = WINDOW + STRETCH
    width = heads * head_dim
    score_scale = 1.0 / math.sqrt(head_dim)
    to_log2 = score_scale * math.log2(math.e)
    step = pl.program_id(0)
    transposed = (((1,), (1,)), ((), ()))
    column = lax.broadcasted_iota(jnp.int32, (STRETCH, span), 1)
    row = lax.broadcasted_iota(jnp.int32, (STRETCH, span), 0)
    causal = column <= row + WINDOW
    starts = [pl.multiple_of(order_ref[h] * head_dim, head_dim) for h in range(heads)]

    def window(part):
        return pl.ds(pl.multiple_of(offset + step * rows + part * STRETCH, STRETCH), span)

    def score(part):
        here = slice(part * STRETCH, (part + 1) * STRETCH)
        keys = ctx_ref[window(part), : 2 * head_dim]
        q = jnp.concatenate([q_ref[here, pl.ds(start, head_dim)] for start in starts], axis=0)
        qt = jnp.concatenate([qt_ref[here, pl.ds(start, head_dim)] for start in starts], axis=0)
        scores = lax.dot_general(
            q, keys[:, :head_dim], transposed, preferred_element_type=jnp.float32
        )
        tangent = lax.dot_general(
            jnp.concatenate([qt, q], axis=1), keys, transposed, preferred_element_type=jnp.float32
        )
        return scores.reshape(heads, STRETCH, span), tangent.reshape(heads, STRETCH, span)

    def weigh(part, scores, tangent):
        low = low_ref[part * STRETCH : (part + 1) * STRETCH, :]
        low = jnp.concatenate([low] * (span // low.shape[1]), axis=1)
        admitted = causal & (column >= low)
        scores = jnp.where(admitted[None], scores, masked_score)
        peak = jnp.max(scores, axis=-1, keepdims=True)
        exponent = jnp.exp2((scores - peak) * to_log2)
        inverse = 1.0 / jnp.sum(exponent, axis=-1, keepdims=True)
        mean = jnp.sum(exponent * tangent, axis=-1, keepdims=True) * inverse
        prob = exponent * inverse
        prob_low = prob.astype(jnp.bfloat16).reshape(heads * STRETCH, span)
        tan_low = (prob * ((tangent - mean) * score_scale)).astype(jnp.bfloat16)
        return prob_low, tan_low.reshape(heads * STRETCH, span)

    def gather_values(part, prob_low, tan_low):
        here = slice(part * STRETCH, (part + 1) * STRETCH)
        values = ctx_ref[window(part), 2 * head_dim :]
        both = jnp.dot(prob_low, values, preferred_element_type=jnp.float32)
        more = jnp.dot(tan_low, values[:, :head_dim], preferred_element_type=jnp.float32)
        out = both[:, :head_dim].astype(jnp.bfloat16)
        out_tan = (both[:, head_dim:] + more).astype(jnp.bfloat16)
        for h in range(heads):
            of = slice(h * STRETCH, (h + 1) * STRETCH)
            out_ref[here, h * head_dim : (h + 1) * head_dim] = out[of]
            out_ref[here, width + h * head_dim : width + (h + 1) * head_dim] = out_tan[of]

    parts = rows // STRETCH
    scored, weighed = score(0), None
    for part in range(parts):
        following = score(part + 1) if part + 1 < parts else None
        if weighed is not None:
            gather_values(part - 1, *weighed)
        weighed = weigh(part, *scored)
        scored = following
    gather_values(parts - 1, *weighed)


def attention(half, order, queries, query_tangent, context, low):
    tokens, width = queries.shape[0] // 2, queries.shape[1]
    head_dim = context.shape[1] // 4
    heads = width // head_dim
    elements = tokens * heads * (WINDOW + STRETCH)
    steps = tokens // TILE
    offset = context.shape[0] - tokens - WINDOW
    return pl.pallas_call(
        functools.partial(attention_kernel, heads, head_dim, offset),
        grid=(steps,),
        in_specs=[
            pl.BlockSpec(memory_space=pltpu.SMEM),
            pl.BlockSpec((TILE, width), lambda i: (half * steps + i, 0)),
            pl.BlockSpec((TILE, width), lambda i: (half * steps + i, 0)),
            pl.BlockSpec(context.shape, lambda i: (0, 0)),
            pl.BlockSpec((TILE, low.shape[1]), lambda i: (half * steps + i, 0)),
        ],
        out_specs=pl.BlockSpec((TILE, 2 * width), lambda i: (i, 0)),
        out_shape=jax.ShapeDtypeStruct((tokens, 2 * width), jnp.bfloat16),
        compiler_params=pltpu.CompilerParams(vmem_limit_bytes=vmem_bytes),
        cost_estimate=pl.CostEstimate(
            flops=elements, bytes_accessed=tokens, transcendentals=0
        ),
        name="attention",
    )(order, queries, query_tangent, context, low)


def project_kernel(sent, kept, pair_ref, *refs):
    *weight_refs, send_ref, keep_ref = refs
    width = pair_ref.shape[1] // 2
    rows = weight_refs[0].shape[1]
    part = weight_refs[0].shape[2] // len(RELATIVE)
    dot = functools.partial(jnp.dot, preferred_element_type=jnp.float32)
    value, tangent, start = 0.0, 0.0, 0
    joined = max(1, 256 // rows)
    for first in range(0, len(weight_refs), joined):
        refs = weight_refs[first : first + joined]
        end = start + rows * len(refs)
        tan_weight = jnp.concatenate([ref[0] for ref in refs], axis=0)
        weight = jnp.concatenate([ref[1] for ref in refs], axis=0)
        attended, attended_tan = pair_ref[:, start:end], pair_ref[:, width + start : width + end]
        value += dot(attended, weight)
        tangent += dot(attended, tan_weight) + dot(attended_tan, weight)
        start = end
    for ref, flips in ((send_ref, sent), (keep_ref, kept)):
        for place, flip in enumerate(flips):
            at = RELATIVE.index(flip) * part
            to = slice(place * part, (place + 1) * part)
            ref[0, :, to] = value[:, at : at + part].astype(ref.dtype)
            ref[1, :, to] = tangent[:, at : at + part].astype(ref.dtype)


def project(sent, kept, pair, index, weights):
    tokens, width = pair.shape
    tile = min(2 * TILE, tokens)
    _, _, rows, columns = weights[0].shape
    out = (2, tokens, columns // 2)
    block = pl.BlockSpec((2, tile, columns // 2), lambda i: (0, i, 0))
    piece = pl.BlockSpec((None, 2, rows, columns), lambda i: (index, 0, 0, 0))
    return pl.pallas_call(
        functools.partial(project_kernel, sent, kept),
        grid=(tokens // tile,),
        in_specs=[pl.BlockSpec((tile, width), lambda i: (i, 0))] + [piece] * len(weights),
        out_specs=[block, block],
        out_shape=[
            jax.ShapeDtypeStruct(out, jnp.bfloat16),
            jax.ShapeDtypeStruct(out, jnp.float32),
        ],
        compiler_params=pltpu.CompilerParams(vmem_limit_bytes=vmem_bytes),
        cost_estimate=pl.CostEstimate(
            flops=tokens * columns, bytes_accessed=tokens, transcendentals=0
        ),
        name="project",
    )(pair, *weights)


def finish_kernel(keep_x, from_x, last_y, keep_y, from_y, last_x, *refs):
    value_ref, tangent_ref = refs[-2:]
    half = keep_x.shape[1]
    for mat, ref in enumerate((value_ref, tangent_ref)):
        first = keep_x[mat] + from_x[mat] + last_y[mat]
        second = keep_y[mat] + from_y[mat] + last_x[mat]
        ref[:half, :] = first.astype(ref.dtype)
        ref[half:, :] = second.astype(ref.dtype)


def finish(chunk, chunks, outputs, keep_x, from_x, last_y, keep_y, from_y, last_x):
    half, part = last_y.shape[1:]
    kept = pl.BlockSpec((2, half, part), lambda i: (0, 0, 1))
    received = pl.BlockSpec((2, half, part), lambda i: (0, 0, 0))
    shape = jax.ShapeDtypeStruct((2 * half, part * chunks), jnp.bfloat16)
    return pl.pallas_call(
        finish_kernel,
        grid=(1,),
        in_specs=[kept, received, received] * 2 + [pl.BlockSpec(memory_space=pl.ANY)] * len(outputs),
        out_specs=[pl.BlockSpec((2 * half, part), lambda i: (0, chunk))] * 2,
        out_shape=[shape, shape],
        input_output_aliases={6 + i: i for i in range(len(outputs))},
        compiler_params=pltpu.CompilerParams(vmem_limit_bytes=vmem_bytes),
        name="finish",
    )(keep_x, from_x, last_y, keep_y, from_y, last_x, *outputs)


def across(block, flip):
    size = lax.axis_size("kv")
    return lax.ppermute(block, "kv", [(i, i ^ flip) for i in range(size)])


def along(block, chips):
    size = lax.axis_size("seq")
    return lax.ppermute(block, "seq", [(i, (i + CORES * chips) % size) for i in range(size)])


def other_core(block):
    return lax.ppermute(block, "seq", [(i, i ^ 1) for i in range(lax.axis_size("seq"))])


def together(*trees):
    return lax.optimization_barrier(trees)


class Gather:
    def __init__(self, mine, chips):
        self.blocks = {0: mine}
        self.others = {}
        self.chips = chips
        self.forward, self.backward = chips // 2, (chips - 1) // 2

    def neighbours(self):
        if self.forward:
            self.blocks[1] = along(self.blocks[0], 1)
        if self.backward:
            self.blocks[self.chips - 1] = along(self.blocks[0], -1)

    def farther(self):
        for step in range(2, self.forward + 1):
            self.blocks[step] = along(self.blocks[step - 1], 1)
        for step in range(2, self.backward + 1):
            self.blocks[self.chips - step] = along(self.blocks[self.chips - step + 1], -1)

    def near(self):
        steps = (0, 1, self.chips - 1)
        return {step: self.blocks[step] for step in steps if step in self.blocks}

    def exchange(self, blocks):
        for step, block in blocks.items():
            if step not in self.others:
                self.others[step] = other_core(block)

    def all(self):
        weights = []
        for step in range(self.chips):
            weights += [self.blocks[step], self.others[step]]
        return weights

    def get(self):
        return self.blocks, self.others

    def put(self, state):
        self.blocks, self.others = (dict(part) for part in state)


def body(
    queries, query_tangent, key_value, key_value_tangents, doc_lengths, out_weight, weight_tangent
):
    tokens, width = queries.shape
    head_dim = key_value.shape[2]
    heads = width // head_dim
    half = tokens // 2
    seq_index = lax.axis_index("seq")
    kv_index = lax.axis_index("kv")
    seq_size = lax.axis_size("seq")
    chips = seq_size // CORES

    mine = arrange(kv_index, weight_tangent, out_weight)
    early, late = [Gather(block, chips) for block in mine]
    early.neighbours()

    key_value, key_value_tangents, _ = lax.optimization_barrier(
        (key_value, key_value_tangents, mine[0])
    )
    stacked = jnp.concatenate(
        [key_value[:, 0], key_value_tangents[:, 0], key_value[:, 1], key_value_tangents[:, 1]],
        axis=1,
    )
    prior = lax.ppermute(
        stacked[tokens - WINDOW :], "seq", [(i, i + 1) for i in range(seq_size - 1)]
    )

    doc_ends = jnp.cumsum(doc_lengths)
    doc_starts = doc_ends - doc_lengths
    position = seq_index * tokens + jnp.arange(tokens, dtype=jnp.int32)
    inside = (doc_starts[None, :] <= position[:, None]) & (position[:, None] < doc_ends[None, :])
    doc_first = jnp.sum(jnp.where(inside, doc_starts[None, :], 0), axis=1)
    lower = jnp.maximum(doc_first, position - WINDOW + 1)
    low = lower - (position // STRETCH * STRETCH - WINDOW)
    low = jnp.broadcast_to(low[:, None], (tokens, 128))

    step = jnp.arange(chips, dtype=jnp.int32)
    chip, core = seq_index // CORES, seq_index % CORES
    owner = (chip - step + chips) % chips * CORES
    order = jnp.stack([owner + core, owner + 1 - core], axis=1).reshape(-1)
    whole_heads = order.shape[0] == heads

    def attend(part, context):
        heads_order = order if whole_heads else jnp.arange(heads, dtype=jnp.int32)
        pair = attention(part, heads_order, queries, query_tangent, context, low)
        if not whole_heads:
            pair = jnp.take(pair.reshape(half, 2, seq_size, -1), order, axis=2)
            pair = pair.reshape(half, 2 * width)
        return pair

    def first_stage(gathering, index, pairs):
        weights = gathering.all()
        send_x, keep_x = project((1, 3), (2, 0), pairs[0], index, weights)
        from_x = across(send_x, 1)
        pair, send_x = together(pairs[1], send_x)
        send_y, keep_y = project((2, 3), (1, 0), pair, index, weights)
        from_y = across(send_y, 2)
        return (keep_x, keep_y), (from_x, from_y), send_y

    def second_sums(kept, received):
        part = kept[0].shape[2] // 2
        return [
            (keep[:, :, :part] + block[:, :, part:]).astype(jnp.bfloat16)
            for keep, block in zip(kept, received)
        ]

    def second_stage(sums):
        return across(sums[0], 2), across(sums[1], 1)

    chunks = sum(GROUPS)

    def write(chunk, outputs, kept, received, last):
        return finish(
            chunk, chunks, outputs, kept[0], received[0], last[0], kept[1], received[1], last[1]
        )

    pair_second = attend(1, stacked)
    pair_second, prior, state, held = together(pair_second, prior, early.get(), late.blocks)
    early.put(state)
    late.blocks = dict(held)
    early.farther()
    early.exchange(early.near())
    late.exchange(late.near())
    pair_first = attend(0, jnp.concatenate([prior, stacked[:half]], axis=0))

    pairs, state, held = together((pair_first, pair_second), early.get(), late.get())
    early.put(state)
    late.put(held)
    early.exchange(early.blocks)
    late.neighbours()
    kept0, from0, send = first_stage(early, 0, pairs)
    pairs, send = together(pairs, send)
    kept1, from1, send = first_stage(early, 1, pairs)

    from0, state, pairs, send = together(from0, late.get(), pairs, send)
    late.put(state)
    late.farther()
    sums = second_sums(kept0, from0)
    last0 = second_stage(sums)

    from1, last0, sums, pairs, held = together(from1, last0, sums, pairs, late.near())
    late.blocks.update(held)
    late.exchange(held)
    sums = second_sums(kept1, from1)
    last1 = second_stage(sums)
    outputs = write(0, (), kept0, from0, last0)

    state, sums, pairs = together(late.get(), sums, pairs)
    late.put(state)
    late.exchange(late.blocks)
    state, last1, pairs = together(late.get(), last1, pairs)
    late.put(state)
    kept2, from2, send = first_stage(late, 0, pairs)
    pairs, send = together(pairs, send)
    kept3, from3, send = first_stage(late, 1, pairs)

    from2, send = together(from2, send)
    sums = second_sums(kept2, from2)
    last2 = second_stage(sums)
    outputs = write(1, outputs, kept1, from1, last1)

    from3, sums = together(from3, sums)
    sums = second_sums(kept3, from3)
    last3 = second_stage(sums)
    outputs = write(2, outputs, kept2, from2, last2)
    outputs = write(3, outputs, kept3, from3, last3)
    return tuple(outputs)


def solution(mesh):
    in_specs = (
        P("seq", "kv"),
        P("seq", "kv"),
        P("seq", None, "kv"),
        P("seq", None, "kv"),
        P(),
        P(("kv", "seq"), None),
        P(("kv", "seq"), None),
    )
    out_specs = (P("seq", "kv"), P("seq", "kv"))
    return jax.shard_map(body, mesh=mesh, in_specs=in_specs, out_specs=out_specs, check_vma=False)
```

time: 146 us -> 148 us (1.014)
  Pallas kernels: 35.5 us -> 45.9 us
  starting transfers between devices: 42.1 us -> 33.7 us
  waiting for transfers between devices: 49.4 us -> 55.5 us
  other arithmetic: 6.94 us -> 2.94 us
  local copies, waits for them, and re-layouts: 9.77 us -> 8.11 us
    pallas_call x8, Pallas kernels: 16.6 us -> 27.9 us  [project(): pl.pallas_call(functools.partial(project_kernel, sent, kept), grid=(token...]
    ppermute x12 -> x6, starting transfers between devices: 20.2 us -> 12.4 us  [along(): lax.ppermute(block, 'seq', [(i, (i + CORES * chips) % size) for i in rang...]
    pallas_call x2, Pallas kernels: 16.4 us -> 10.6 us  [attention(): pl.pallas_call(functools.partial(attention_kernel, heads, head_dim, offse...]
    pallas_call x0 -> x4, Pallas kernels: none -> 4.9 us  [finish(): pl.pallas_call(finish_kernel, grid=(1,), in_specs=[kept, received, receiv...]
    ppermute x16, waiting for transfers between devices: 30.9 us -> 35.4 us  [across(): return lax.ppermute(block, 'kv', [(i, i ^ flip) for i in range(size)])]
    convert_element_type x16 -> x8, other arithmetic: 5.11 us -> 1.4 us  [second_sums(): (keep[:, :, :part] + block[:, :, part:]).astype(jnp.bfloat16)]
    unnamed x50 -> x30, local copies, waits for them, and re-layouts: 2.89 us -> 6.47 us
    concatenate x8 -> x0, local copies, waits for them, and re-layouts: 3 us -> none  [the longest x4 1.98 us: early(): near = jnp.concatenate([self.blocks[0], self.blocks[1]], axis=1)]
  transfers between devices with their start and end apart: 37 -> 31, of which waited for: 15 -> 17; matrix products, arithmetic and copies ran while one was open for 9% -> 3% of each run, Pallas kernels for 23% -> 23%
where the time goes in v4:
time: 148 us; the launch traced here: 147 us
  waiting for transfers between devices  55.5 us (38%)
  Pallas kernels  45.9 us (31%)
  starting transfers between devices  33.7 us (23%)
  local copies, waits for them, and re-layouts  8.11 us (5%)
  other arithmetic  2.94 us (2%)
    ppermute x16, waiting for transfers between devices, across(): return lax.ppermute(block, 'kv', [(i, i ^ flip) for i in range(size)])  35.4 us
    pallas_call x8, Pallas kernels, project(): pl.pallas_call(functools.partial(project_kernel, sent, kept), grid=(token...  27.9 us
    ppermute x6, waiting for transfers between devices, along(): lax.ppermute(block, 'seq', [(i, (i + CORES * chips) % size) for i in rang...  18.5 us
    ppermute x16, starting transfers between devices, across(): return lax.ppermute(block, 'kv', [(i, i ^ flip) for i in range(size)])  17.4 us
    ppermute x6, starting transfers between devices, along(): lax.ppermute(block, 'seq', [(i, (i + CORES * chips) % size) for i in rang...  12.4 us
    pallas_call x2, Pallas kernels, attention(): pl.pallas_call(functools.partial(attention_kernel, heads, head_dim, offse...  10.6 us
    unnamed x30, local copies, waits for them, and re-layouts  6.47 us
    pallas_call x4, Pallas kernels, finish(): pl.pallas_call(finish_kernel, grid=(1,), in_specs=[kept, received, receiv...  4.9 us
  transfers between devices with their start and end apart: 31, of which 17 were waited for; matrix products, arithmetic and copies ran while one was open for 3% of the time, Pallas kernels for 23%

profile of v4, /device:TPU:0, one launch (start us, length us, event | category | flops | bytes accessed | tf_op | source)
XLA Modules:
  0.0 147.2 jit_solution(10312997866936021276)
XLA Ops:
  0.6 2.5 %arrange.1 = (bf16[2,2,128,512]{3,2,1,0:T(8,128)(2,1)}, bf16[2,2,128,512]{3,2,1,0:T(8,128)(2,1)}) custom-call(s32[1]{0:T(128)} %bitcast.kv_ref, bf16[128,2048]{1,0:T(8,128)(2,1)} %tangent_ref.1, bf16[128,2048]{1,0:T(8,128)(2,1)} %value_ref.1), custom_call_target="tpu_custom_call" | custom-call | tf_op jit(solution)/shard_map/arrange/pallas_call | solution.py:42
  3.1 3.0 %collective-permute-start.1 = (bf16[2,2,128,512]{3,2,1,0:T(8,128)(2,1)}, bf16[2,2,128,512]{3,2,1,0:T(8,128)(2,1)S(1)}, u32[]{:S(2)}, u32[]{:S(2)}) collective-permute-start(bf16[2,2,128,512]{3,2,1,0:T(8,128)(2,1)} %get-tuple-element.107.refs_0_), channel_id=1, source_target_pairs={{0,2},{1,3},{2,4},{3,5},{4,6},{5,7},{6,0},{7,1},{8,10},{9,11},{10,... | collective-permute-start | bytes 1572872 | tf_op jit(solution)/shard_map/ppermute | solution.py:231
  6.2 2.0 %collective-permute-start.2 = (bf16[2,2,128,512]{3,2,1,0:T(8,128)(2,1)}, bf16[2,2,128,512]{3,2,1,0:T(8,128)(2,1)S(1)}, u32[]{:S(2)}, u32[]{:S(2)}) collective-permute-start(bf16[2,2,128,512]{3,2,1,0:T(8,128)(2,1)} %get-tuple-element.107.refs_0_), channel_id=1, source_target_pairs={{0,6},{1,7},{2,0},{3,1},{4,2},{5,3},{6,4},{7,5},{8,14},{9,15},{10,... | collective-permute-start | bytes 1572872 | tf_op jit(solution)/shard_map/ppermute | solution.py:231
  8.2 1.1 copy.25
  9.7 1.0 copy-done.5
  10.6 2.1 %collective-permute-start = (bf16[224,512]{1,0:T(8,128)(2,1)S(1)}, bf16[224,512]{1,0:T(8,128)(2,1)}, u32[]{:S(2)}, u32[]{:S(2)}) collective-permute-start(bf16[224,512]{1,0:T(8,128)(2,1)S(1)} %slice.92), channel_id=1, source_target_pairs={{0,1},{1,2},{2,3},{3,4},{4,5},{5,6},{6,7},{8,9},{9,10},{10,11},{11... | collective-permute-start | bytes 688136 | tf_op jit(solution)/shard_map/ppermute | solution.py:306
  13.6 1.2 copy-done.6
  14.9 5.3 %attention.2.pair_ref = bf16[512,2048]{1,0:T(8,128)(2,1)S(1)} custom-call(s32[8]{0:T(128)S(1)} %reshape.118.order_ref, bf16[1024,1024]{1,0:T(8,128)(2,1)S(1)} %copy-done.4, bf16[1024,1024]{1,0:T(8,128)(2,1)} %qt_ref.3, bf16[1024,512]{1,0:T(8,128)(2,1)S(1)} %copy-done.6, s32[1024,128]{1,0:T(8,128)S(1)} %broadcast_in_dim.13.low_ref), custom_call_target="tpu_custom_call" | custom-call | flops 1048576 | bytes 512 | tf_op jit(solution)/shard_map/attention/pallas_call | solution.py:128
  20.2 1.3 copy-done
  21.5 9.5 %collective-permute-done.2.refs_6_ = bf16[2,2,128,512]{3,2,1,0:T(8,128)(2,1)S(1)} collective-permute-done((bf16[2,2,128,512]{3,2,1,0:T(8,128)(2,1)}, bf16[2,2,128,512]{3,2,1,0:T(8,128)(2,1)S(1)}, u32[]{:S(2)}, u32[]{:S(2)}) %collective-permute-start.2) | collective-permute-done | bytes 524320 | tf_op jit(solution)/shard_map/ppermute | solution.py:231
  31.0 2.9 %collective-permute-start.3 = (bf16[2,2,128,512]{3,2,1,0:T(8,128)(2,1)S(1)}, bf16[2,2,128,512]{3,2,1,0:T(8,128)(2,1)S(1)}, u32[]{:S(2)}, u32[]{:S(2)}) collective-permute-start(bf16[2,2,128,512]{3,2,1,0:T(8,128)(2,1)S(1)} %collective-permute-done.1.refs_2_), channel_id=1, source_target_pairs={{0,2},{1,3},{2,4},{3,5},{4,6},{5,7},{6,0},{7,1},{8,10},{9,11},{10,... | collective-permute-start | bytes 1572872 | tf_op jit(solution)/shard_map/ppermute | solution.py:231
  34.9 1.0 pad_maximum_fusion.1.ctx_ref
  35.9 5.2 %attention.3.pair_ref = bf16[512,2048]{1,0:T(8,128)(2,1)S(1)} custom-call(s32[8]{0:T(128)S(1)} %reshape.118.order_ref, bf16[1024,1024]{1,0:T(8,128)(2,1)S(1)} %copy-done.4, bf16[1024,1024]{1,0:T(8,128)(2,1)} %qt_ref.3, bf16[736,512]{1,0:T(8,128)(2,1)S(1)} %pad_maximum_fusion.1.ctx_ref, s32[1024,128]{1,0:T(8,128)S(1)} %broadcast_in_dim.13.low_ref), custom_call_target="tpu_custom_call" | custom-call | flops 1048576 | bytes 512 | tf_op jit(solution)/shard_map/attention/pallas_call | solution.py:128
  41.2 1.3 copy-done.1
  42.5 4.6 %collective-permute-done.3.refs_4_ = bf16[2,2,128,512]{3,2,1,0:T(8,128)(2,1)S(1)} collective-permute-done((bf16[2,2,128,512]{3,2,1,0:T(8,128)(2,1)S(1)}, bf16[2,2,128,512]{3,2,1,0:T(8,128)(2,1)S(1)}, u32[]{:S(2)}, u32[]{:S(2)}) %collective-permute-start.3) | collective-permute-done | bytes 524320 | tf_op jit(solution)/shard_map/ppermute | solution.py:231
  47.2 3.8 %collective-permute-start.14 = (bf16[2,2,128,512]{3,2,1,0:T(8,128)(2,1)S(1)}, bf16[2,2,128,512]{3,2,1,0:T(8,128)(2,1)S(1)}, u32[]{:S(2)}, u32[]{:S(2)}) collective-permute-start(bf16[2,2,128,512]{3,2,1,0:T(8,128)(2,1)S(1)} %copy-done.2), channel_id=1, source_target_pairs={{0,6},{1,7},{2,0},{3,1},{4,2},{5,3},{6,4},{7,5},{8,14},{9,15},{10,... | collective-permute-start | bytes 1572872 | tf_op jit(solution)/shard_map/ppermute | solution.py:231
  51.1 3.3 %project.8 = (bf16[2,512,256]{2,1,0:T(8,128)(2,1)S(1)}, f32[2,512,256]{2,1,0:T(8,128)S(1)}) custom-call(bf16[512,2048]{1,0:T(8,128)(2,1)} %copy-done.1, bf16[2,2,128,512]{3,2,1,0:T(8,128)(2,1)S(1)} %copy-done.3, bf16[2,2,128,512]{3,2,1,0:T(8,128)(2,1)S(1)} %collective-permute-done.4.refs_1_, bf16[2,2,128,512]{3,2,1,0:T(8,128)(2,1)S(1)} %collective-permute-done.1.refs_2_, ...), custom_call_target="tpu_custom_call" | custom-call | flops 262144 | bytes 512 | tf_op jit(solution)/shard_map/project/pallas_call | solution.py:180
  54.4 3.3 %project.9 = (bf16[2,512,256]{2,1,0:T(8,128)(2,1)S(1)}, f32[2,512,256]{2,1,0:T(8,128)S(1)}) custom-call(bf16[512,2048]{1,0:T(8,128)(2,1)} %copy-done, bf16[2,2,128,512]{3,2,1,0:T(8,128)(2,1)S(1)} %copy-done.3, bf16[2,2,128,512]{3,2,1,0:T(8,128)(2,1)S(1)} %collective-permute-done.4.refs_1_, bf16[2,2,128,512]{3,2,1,0:T(8,128)(2,1)S(1)} %collective-permute-done.1.refs_2_, ...), custom_call_target="tpu_custom_call" | custom-call | flops 262144 | bytes 512 | tf_op jit(solution)/shard_map/project/pallas_call | solution.py:180
  57.7 1.6 %collective-permute-start.12 = (bf16[2,512,256]{2,1,0:T(8,128)(2,1)S(1)}, bf16[2,512,256]{2,1,0:T(8,128)(2,1)S(1)}, u32[]{:S(2)}, u32[]{:S(2)}) collective-permute-start(bf16[2,512,256]{2,1,0:T(8,128)(2,1)S(1)} %get-tuple-element.116), channel_id=1, source_target_pairs={{0,16},{8,24},{16,0},{24,8},{1,17},{9,25},{17,1},{25,9},{2,18},{10... | collective-permute-start | bytes 1572872 | tf_op jit(solution)/shard_map/ppermute | solution.py:226
  59.3 1.5 %collective-permute-start.11 = (bf16[2,512,256]{2,1,0:T(8,128)(2,1)S(1)}, bf16[2,512,256]{2,1,0:T(8,128)(2,1)S(1)}, u32[]{:S(2)}, u32[]{:S(2)}) collective-permute-start(bf16[2,512,256]{2,1,0:T(8,128)(2,1)S(1)} %get-tuple-element.114), channel_id=1, source_target_pairs={{0,8},{8,0},{16,24},{24,16},{1,9},{9,1},{17,25},{25,17},{2,10},{10... | collective-permute-start | bytes 1572872 | tf_op jit(solution)/shard_map/ppermute | solution.py:226
  60.8 3.3 %project.10 = (bf16[2,512,256]{2,1,0:T(8,128)(2,1)S(1)}, f32[2,512,256]{2,1,0:T(8,128)S(1)}) custom-call(bf16[512,2048]{1,0:T(8,128)(2,1)} %copy-done.1, bf16[2,2,128,512]{3,2,1,0:T(8,128)(2,1)S(1)} %copy-done.3, bf16[2,2,128,512]{3,2,1,0:T(8,128)(2,1)S(1)} %collective-permute-done.4.refs_1_, bf16[2,2,128,512]{3,2,1,0:T(8,128)(2,1)S(1)} %collective-permute-done.1.refs_2_, ...), custom_call_target="tpu_custom_call" | custom-call | flops 262144 | bytes 512 | tf_op jit(solution)/shard_map/project/pallas_call | solution.py:180
  64.7 3.3 %project.11 = (bf16[2,512,256]{2,1,0:T(8,128)(2,1)S(1)}, f32[2,512,256]{2,1,0:T(8,128)S(1)}) custom-call(bf16[512,2048]{1,0:T(8,128)(2,1)} %copy-done, bf16[2,2,128,512]{3,2,1,0:T(8,128)(2,1)S(1)} %copy-done.3, bf16[2,2,128,512]{3,2,1,0:T(8,128)(2,1)S(1)} %collective-permute-done.4.refs_1_, bf16[2,2,128,512]{3,2,1,0:T(8,128)(2,1)S(1)} %collective-permute-done.1.refs_2_, ...), custom_call_target="tpu_custom_call" | custom-call | flops 262144 | bytes 512 | tf_op jit(solution)/shard_map/project/pallas_call | solution.py:180
  68.6 4.1 %collective-permute-done.14.refs_6_ = bf16[2,2,128,512]{3,2,1,0:T(8,128)(2,1)S(1)} collective-permute-done((bf16[2,2,128,512]{3,2,1,0:T(8,128)(2,1)S(1)}, bf16[2,2,128,512]{3,2,1,0:T(8,128)(2,1)S(1)}, u32[]{:S(2)}, u32[]{:S(2)}) %collective-permute-start.14) | collective-permute-done | bytes 524320 | tf_op jit(solution)/shard_map/ppermute | solution.py:231
  72.7 1.4 collective-permute-done.11.from_x
  74.2 1.6 %collective-permute-start.16 = (bf16[2,512,128]{2,1,0:T(8,128)(2,1)S(1)}, bf16[2,512,128]{2,1,0:T(8,128)(2,1)S(1)}, u32[]{:S(2)}, u32[]{:S(2)}) collective-permute-start(bf16[2,512,128]{2,1,0:T(8,128)(2,1)S(1)} %add_convert_fusion.6), channel_id=1, source_target_pairs={{0,8},{8,0},{16,24},{24,16},{1,9},{9,1},{17,25},{25,17},{2,10},{10... | collective-permute-start | bytes 786440 | tf_op jit(solution)/shard_map/ppermute | solution.py:226
  77.0 6.8 %collective-permute-done.10.from_y = bf16[2,512,256]{2,1,0:T(8,128)(2,1)S(1)} collective-permute-done((bf16[2,512,256]{2,1,0:T(8,128)(2,1)S(1)}, bf16[2,512,256]{2,1,0:T(8,128)(2,1)S(1)}, u32[]{:S(2)}, u32[]{:S(2)}) %collective-permute-start.10) | collective-permute-done | bytes 524320 | tf_op jit(solution)/shard_map/ppermute | solution.py:226
  83.8 1.6 %collective-permute-done.9.from_x = bf16[2,512,256]{2,1,0:T(8,128)(2,1)S(1)} collective-permute-done((bf16[2,512,256]{2,1,0:T(8,128)(2,1)S(1)}, bf16[2,512,256]{2,1,0:T(8,128)(2,1)S(1)}, u32[]{:S(2)}, u32[]{:S(2)}) %collective-permute-start.9) | collective-permute-done | bytes 524320 | tf_op jit(solution)/shard_map/ppermute | solution.py:226
  85.4 4.2 %collective-permute-done.16.last_x = bf16[2,512,128]{2,1,0:T(8,128)(2,1)S(1)} collective-permute-done((bf16[2,512,128]{2,1,0:T(8,128)(2,1)S(1)}, bf16[2,512,128]{2,1,0:T(8,128)(2,1)S(1)}, u32[]{:S(2)}, u32[]{:S(2)}) %collective-permute-start.16) | collective-permute-done | bytes 262176 | tf_op jit(solution)/shard_map/ppermute | solution.py:226
  92.4 1.5 %collective-permute-start.22 = (bf16[2,512,128]{2,1,0:T(8,128)(2,1)S(1)}, bf16[2,512,128]{2,1,0:T(8,128)(2,1)S(1)}, u32[]{:S(2)}, u32[]{:S(2)}) collective-permute-start(bf16[2,512,128]{2,1,0:T(8,128)(2,1)S(1)} %add_convert_fusion.4), channel_id=1, source_target_pairs={{0,8},{8,0},{16,24},{24,16},{1,9},{9,1},{17,25},{25,17},{2,10},{10... | collective-permute-start | bytes 786440 | tf_op jit(solution)/shard_map/ppermute | solution.py:226
  94.4 6.6 %collective-permute-done.22.last_x = bf16[2,512,128]{2,1,0:T(8,128)(2,1)S(1)} collective-permute-done((bf16[2,512,128]{2,1,0:T(8,128)(2,1)S(1)}, bf16[2,512,128]{2,1,0:T(8,128)(2,1)S(1)}, u32[]{:S(2)}, u32[]{:S(2)}) %collective-permute-start.22) | collective-permute-done | bytes 262176 | tf_op jit(solution)/shard_map/ppermute | solution.py:226
  101.0 1.2 collective-permute-done.21.last_y
  102.2 4.1 %project.12 = (bf16[2,512,256]{2,1,0:T(8,128)(2,1)}, f32[2,512,256]{2,1,0:T(8,128)S(1)}) custom-call(bf16[512,2048]{1,0:T(8,128)(2,1)} %copy-done.1, bf16[2,2,128,512]{3,2,1,0:T(8,128)(2,1)S(1)} %copy-done.2, bf16[2,2,128,512]{3,2,1,0:T(8,128)(2,1)S(1)} %collective-permute-done.7.refs_1_, bf16[2,2,128,512]{3,2,1,0:T(8,128)(2,1)S(1)} %collective-permute-done.13.refs_2_, ...), custom_call_target="tpu_custom_call" | custom-call | flops 262144 | bytes 512 | tf_op jit(solution)/shard_map/project/pallas_call | solution.py:180
  106.3 4.0 %project.13 = (bf16[2,512,256]{2,1,0:T(8,128)(2,1)}, f32[2,512,256]{2,1,0:T(8,128)S(1)}) custom-call(bf16[512,2048]{1,0:T(8,128)(2,1)} %copy-done, bf16[2,2,128,512]{3,2,1,0:T(8,128)(2,1)S(1)} %copy-done.2, bf16[2,2,128,512]{3,2,1,0:T(8,128)(2,1)S(1)} %collective-permute-done.7.refs_1_, bf16[2,2,128,512]{3,2,1,0:T(8,128)(2,1)S(1)} %collective-permute-done.13.refs_2_, ...), custom_call_target="tpu_custom_call" | custom-call | flops 262144 | bytes 512 | tf_op jit(solution)/shard_map/project/pallas_call | solution.py:180
  111.3 3.3 %project.14 = (bf16[2,512,256]{2,1,0:T(8,128)(2,1)S(1)}, f32[2,512,256]{2,1,0:T(8,128)S(1)}) custom-call(bf16[512,2048]{1,0:T(8,128)(2,1)} %copy-done.1, bf16[2,2,128,512]{3,2,1,0:T(8,128)(2,1)S(1)} %copy-done.2, bf16[2,2,128,512]{3,2,1,0:T(8,128)(2,1)S(1)} %collective-permute-done.7.refs_1_, bf16[2,2,128,512]{3,2,1,0:T(8,128)(2,1)S(1)} %collective-permute-done.13.refs_2_, ...), custom_call_target="tpu_custom_call" | custom-call | flops 262144 | bytes 512 | tf_op jit(solution)/shard_map/project/pallas_call | solution.py:180
  115.4 3.3 %project.15 = (bf16[2,512,256]{2,1,0:T(8,128)(2,1)S(1)}, f32[2,512,256]{2,1,0:T(8,128)S(1)}) custom-call(bf16[512,2048]{1,0:T(8,128)(2,1)} %copy-done, bf16[2,2,128,512]{3,2,1,0:T(8,128)(2,1)S(1)} %copy-done.2, bf16[2,2,128,512]{3,2,1,0:T(8,128)(2,1)S(1)} %collective-permute-done.7.refs_1_, bf16[2,2,128,512]{3,2,1,0:T(8,128)(2,1)S(1)} %collective-permute-done.13.refs_2_, ...), custom_call_target="tpu_custom_call" | custom-call | flops 262144 | bytes 512 | tf_op jit(solution)/shard_map/project/pallas_call | solution.py:180
  119.5 1.5 %collective-permute-start.24 = (bf16[2,512,256]{2,1,0:T(8,128)(2,1)}, bf16[2,512,256]{2,1,0:T(8,128)(2,1)S(1)}, u32[]{:S(2)}, u32[]{:S(2)}) collective-permute-start(bf16[2,512,256]{2,1,0:T(8,128)(2,1)} %copy-done.12), channel_id=1, source_target_pairs={{0,16},{8,24},{16,0},{24,8},{1,17},{9,25},{17,1},{25,9},{2,18},{10... | collective-permute-start | bytes 1572872 | tf_op jit(solution)/shard_map/ppermute | solution.py:226
  121.0 1.5 %collective-permute-start.23 = (bf16[2,512,256]{2,1,0:T(8,128)(2,1)}, bf16[2,512,256]{2,1,0:T(8,128)(2,1)S(1)}, u32[]{:S(2)}, u32[]{:S(2)}) collective-permute-start(bf16[2,512,256]{2,1,0:T(8,128)(2,1)} %copy-done.11), channel_id=1, source_target_pairs={{0,8},{8,0},{16,24},{24,16},{1,9},{9,1},{17,25},{25,17},{2,10},{10... | collective-permute-start | bytes 1572872 | tf_op jit(solution)/shard_map/ppermute | solution.py:226
  122.5 2.8 %collective-permute-done.26.from_y = bf16[2,512,256]{2,1,0:T(8,128)(2,1)S(1)} collective-permute-done((bf16[2,512,256]{2,1,0:T(8,128)(2,1)}, bf16[2,512,256]{2,1,0:T(8,128)(2,1)S(1)}, u32[]{:S(2)}, u32[]{:S(2)}) %collective-permute-start.26) | collective-permute-done | bytes 524320 | tf_op jit(solution)/shard_map/ppermute | solution.py:226
  126.0 1.0 add_convert_fusion.3
  127.0 1.9 %collective-permute-start.29 = (bf16[2,512,128]{2,1,0:T(8,128)(2,1)S(1)}, bf16[2,512,128]{2,1,0:T(8,128)(2,1)S(1)}, u32[]{:S(2)}, u32[]{:S(2)}) collective-permute-start(bf16[2,512,128]{2,1,0:T(8,128)(2,1)S(1)} %add_convert_fusion.3), channel_id=1, source_target_pairs={{0,16},{8,24},{16,0},{24,8},{1,17},{9,25},{17,1},{25,9},{2,18},{10... | collective-permute-start | bytes 786440 | tf_op jit(solution)/shard_map/ppermute | solution.py:226
  128.9 7.6 %collective-permute-done.24.from_y = bf16[2,512,256]{2,1,0:T(8,128)(2,1)S(1)} collective-permute-done((bf16[2,512,256]{2,1,0:T(8,128)(2,1)}, bf16[2,512,256]{2,1,0:T(8,128)(2,1)S(1)}, u32[]{:S(2)}, u32[]{:S(2)}) %collective-permute-start.24) | collective-permute-done | bytes 524320 | tf_op jit(solution)/shard_map/ppermute | solution.py:226
  136.6 1.1 collective-permute-start.28
  137.8 1.3 collective-permute-start.27
  139.1 1.0 finish.4
  140.1 1.0 finish.5
  142.2 1.9 %finish.6 = (bf16[1024,512]{1,0:T(8,128)(2,1)}, bf16[1024,512]{1,0:T(8,128)(2,1)}) custom-call(f32[2,512,256]{2,1,0:T(8,128)S(1)} %get-tuple-element.171.keep_x, bf16[2,512,256]{2,1,0:T(8,128)(2,1)} %collective-permute-done.25.from_x, bf16[2,512,128]{2,1,0:T(8,128)(2,1)S(1)} %collective-permute-done.29.last_y, ...), custom_call_target="tpu_custom_call", output_to_operand_aliasing={{0}: (6, {}), {1}: (7, {})} | custom-call | tf_op jit(solution)/shard_map/finish/pallas_call | solution.py:212
  144.0 2.2 %collective-permute-done.28.last_x = bf16[2,512,128]{2,1,0:T(8,128)(2,1)S(1)} collective-permute-done((bf16[2,512,128]{2,1,0:T(8,128)(2,1)S(1)}, bf16[2,512,128]{2,1,0:T(8,128)(2,1)S(1)}, u32[]{:S(2)}, u32[]{:S(2)}) %collective-permute-start.28) | collective-permute-done | bytes 262176 | tf_op jit(solution)/shard_map/ppermute | solution.py:226
  146.2 1.0 finish.7
  (86 shorter events, 12.5 us)
Async XLA Ops:
  0.6 8.7 %copy-start.13 = (bf16[1024,2,128]{2,1,0:T(2,128)(2,1)S(1)}, bf16[1024,2,128]{2,1,0:T(2,128)(2,1)}, u32[]{:S(2)}) copy-start(bf16[1024,2,128]{2,1,0:T(2,128)(2,1)} %param.10) | copy-start | bytes 1572868
  3.1 18.4 %collective-permute-start.1 = (bf16[2,2,128,512]{3,2,1,0:T(8,128)(2,1)}, bf16[2,2,128,512]{3,2,1,0:T(8,128)(2,1)S(1)}, u32[]{:S(2)}, u32[]{:S(2)}) collective-permute-start(bf16[2,2,128,512]{3,2,1,0:T(8,128)(2,1)} %get-tuple-element.107.refs_0_), channel_id=1, source_target_pairs={{0,2},{1,3},{2,4},{3,5},{4,6},{5,7},{6,0},{7,1},{8,10},{9,11},{10,... | collective-permute-start | bytes 1572872 | tf_op jit(solution)/shard_map/ppermute | solution.py:231
  6.2 24.8 %collective-permute-start.2 = (bf16[2,2,128,512]{3,2,1,0:T(8,128)(2,1)}, bf16[2,2,128,512]{3,2,1,0:T(8,128)(2,1)S(1)}, u32[]{:S(2)}, u32[]{:S(2)}) collective-permute-start(bf16[2,2,128,512]{3,2,1,0:T(8,128)(2,1)} %get-tuple-element.107.refs_0_), channel_id=1, source_target_pairs={{0,6},{1,7},{2,0},{3,1},{4,2},{5,3},{6,4},{7,5},{8,14},{9,15},{10,... | collective-permute-start | bytes 1572872 | tf_op jit(solution)/shard_map/ppermute | solution.py:231
  9.4 3.4 %copy-start.14 = (s32[64]{0:T(128)S(1)}, s32[64]{0:T(128)}, u32[]{:S(2)}) copy-start(s32[64]{0:T(128)} %param.11) | copy-start | bytes 772
  9.5 4.1 %copy-start.4 = (bf16[1024,1024]{1,0:T(8,128)(2,1)S(1)}, bf16[1024,1024]{1,0:T(8,128)(2,1)}, u32[]{:S(2)}) copy-start(bf16[1024,1024]{1,0:T(8,128)(2,1)} %q_ref.3) | copy-start | bytes 6291460
  9.7 1.0 copy-start.5
  10.6 10.9 %collective-permute-start = (bf16[224,512]{1,0:T(8,128)(2,1)S(1)}, bf16[224,512]{1,0:T(8,128)(2,1)}, u32[]{:S(2)}, u32[]{:S(2)}) collective-permute-start(bf16[224,512]{1,0:T(8,128)(2,1)S(1)} %slice.92), channel_id=1, source_target_pairs={{0,1},{1,2},{2,3},{3,4},{4,5},{5,6},{6,7},{8,9},{9,10},{10,11},{11... | collective-permute-start | bytes 688136 | tf_op jit(solution)/shard_map/ppermute | solution.py:306
  13.6 1.2 copy-start.6
  14.9 19.0 %copy-start.3 = (bf16[2,2,128,512]{3,2,1,0:T(8,128)(2,1)S(1)}, bf16[2,2,128,512]{3,2,1,0:T(8,128)(2,1)}, u32[]{:S(2)}) copy-start(bf16[2,2,128,512]{3,2,1,0:T(8,128)(2,1)} %get-tuple-element.107.refs_0_) | copy-start | bytes 1572868
  14.9 19.6 %copy-start.2 = (bf16[2,2,128,512]{3,2,1,0:T(8,128)(2,1)S(1)}, bf16[2,2,128,512]{3,2,1,0:T(8,128)(2,1)}, u32[]{:S(2)}) copy-start(bf16[2,2,128,512]{3,2,1,0:T(8,128)(2,1)} %get-tuple-element.154.refs_0_) | copy-start | bytes 1572868
  14.9 20.1 %slice-start = ((bf16[1024,512]{1,0:T(8,128)(2,1)}), bf16[512,512]{1,0:T(8,128)(2,1)S(1)}, s32[]{:S(2)}) async-start(bf16[1024,512]{1,0:T(8,128)(2,1)} %copy-done.5), calls=%async_computation | async-start | bytes 1048576 | tf_op jit(solution)/shard_map/slice | solution.py:366
  20.2 1.3 copy-start
  31.0 16.1 %collective-permute-start.3 = (bf16[2,2,128,512]{3,2,1,0:T(8,128)(2,1)S(1)}, bf16[2,2,128,512]{3,2,1,0:T(8,128)(2,1)S(1)}, u32[]{:S(2)}, u32[]{:S(2)}) collective-permute-start(bf16[2,2,128,512]{3,2,1,0:T(8,128)(2,1)S(1)} %collective-permute-done.1.refs_2_), channel_id=1, source_target_pairs={{0,2},{1,3},{2,4},{3,5},{4,6},{5,7},{6,0},{7,1},{8,10},{9,11},{10,... | collective-permute-start | bytes 1572872 | tf_op jit(solution)/shard_map/ppermute | solution.py:231
  33.9 13.2 %collective-permute-start.5 = (bf16[2,2,128,512]{3,2,1,0:T(8,128)(2,1)S(1)}, bf16[2,2,128,512]{3,2,1,0:T(8,128)(2,1)S(1)}, u32[]{:S(2)}, u32[]{:S(2)}) collective-permute-start(bf16[2,2,128,512]{3,2,1,0:T(8,128)(2,1)S(1)} %collective-permute-done.1.refs_2_), channel_id=1, source_target_pairs={{0,1},{1,0},{2,3},{3,2},{4,5},{5,4},{6,7},{7,6},{8,9},{9,8},{10,11... | collective-permute-start | bytes 1572872 | tf_op jit(solution)/shard_map/ppermute | solution.py:235
  33.9 13.2 %collective-permute-start.4 = (bf16[2,2,128,512]{3,2,1,0:T(8,128)(2,1)S(1)}, bf16[2,2,128,512]{3,2,1,0:T(8,128)(2,1)S(1)}, u32[]{:S(2)}, u32[]{:S(2)}) collective-permute-start(bf16[2,2,128,512]{3,2,1,0:T(8,128)(2,1)S(1)} %copy-done.3), channel_id=1, source_target_pairs={{0,1},{1,0},{2,3},{3,2},{4,5},{5,4},{6,7},{7,6},{8,9},{9,8},{10,11... | collective-permute-start | bytes 1572872 | tf_op jit(solution)/shard_map/ppermute | solution.py:235
  34.4 12.7 %collective-permute-start.6 = (bf16[2,2,128,512]{3,2,1,0:T(8,128)(2,1)S(1)}, bf16[2,2,128,512]{3,2,1,0:T(8,128)(2,1)S(1)}, u32[]{:S(2)}, u32[]{:S(2)}) collective-permute-start(bf16[2,2,128,512]{3,2,1,0:T(8,128)(2,1)S(1)} %collective-permute-done.2.refs_6_), channel_id=1, source_target_pairs={{0,1},{1,0},{2,3},{3,2},{4,5},{5,4},{6,7},{7,6},{8,9},{9,8},{10,11... | collective-permute-start | bytes 1572872 | tf_op jit(solution)/shard_map/ppermute | solution.py:235
  34.4 12.7 %collective-permute-start.7 = (bf16[2,2,128,512]{3,2,1,0:T(8,128)(2,1)S(1)}, bf16[2,2,128,512]{3,2,1,0:T(8,128)(2,1)S(1)}, u32[]{:S(2)}, u32[]{:S(2)}) collective-permute-start(bf16[2,2,128,512]{3,2,1,0:T(8,128)(2,1)S(1)} %copy-done.2), channel_id=1, source_target_pairs={{0,1},{1,0},{2,3},{3,2},{4,5},{5,4},{6,7},{7,6},{8,9},{9,8},{10,11... | collective-permute-start | bytes 1572872 | tf_op jit(solution)/shard_map/ppermute | solution.py:235
  41.1 1.4 copy-start.1
  47.1 4.0 %collective-permute-start.8 = (bf16[2,2,128,512]{3,2,1,0:T(8,128)(2,1)S(1)}, bf16[2,2,128,512]{3,2,1,0:T(8,128)(2,1)S(1)}, u32[]{:S(2)}, u32[]{:S(2)}) collective-permute-start(bf16[2,2,128,512]{3,2,1,0:T(8,128)(2,1)S(1)} %collective-permute-done.3.refs_4_), channel_id=1, source_target_pairs={{0,1},{1,0},{2,3},{3,2},{4,5},{5,4},{6,7},{7,6},{8,9},{9,8},{10,11... | collective-permute-start | bytes 1572872 | tf_op jit(solution)/shard_map/ppermute | solution.py:235
  47.2 20.9 %collective-permute-start.13 = (bf16[2,2,128,512]{3,2,1,0:T(8,128)(2,1)S(1)}, bf16[2,2,128,512]{3,2,1,0:T(8,128)(2,1)S(1)}, u32[]{:S(2)}, u32[]{:S(2)}) collective-permute-start(bf16[2,2,128,512]{3,2,1,0:T(8,128)(2,1)S(1)} %copy-done.2), channel_id=1, source_target_pairs={{0,2},{1,3},{2,4},{3,5},{4,6},{5,7},{6,0},{7,1},{8,10},{9,11},{10,... | collective-permute-start | bytes 1572872 | tf_op jit(solution)/shard_map/ppermute | solution.py:231
  47.2 25.5 %collective-permute-start.14 = (bf16[2,2,128,512]{3,2,1,0:T(8,128)(2,1)S(1)}, bf16[2,2,128,512]{3,2,1,0:T(8,128)(2,1)S(1)}, u32[]{:S(2)}, u32[]{:S(2)}) collective-permute-start(bf16[2,2,128,512]{3,2,1,0:T(8,128)(2,1)S(1)} %copy-done.2), channel_id=1, source_target_pairs={{0,6},{1,7},{2,0},{3,1},{4,2},{5,3},{6,4},{7,5},{8,14},{9,15},{10,... | collective-permute-start | bytes 1572872 | tf_op jit(solution)/shard_map/ppermute | solution.py:231
  57.7 15.0 %collective-permute-start.12 = (bf16[2,512,256]{2,1,0:T(8,128)(2,1)S(1)}, bf16[2,512,256]{2,1,0:T(8,128)(2,1)S(1)}, u32[]{:S(2)}, u32[]{:S(2)}) collective-permute-start(bf16[2,512,256]{2,1,0:T(8,128)(2,1)S(1)} %get-tuple-element.116), channel_id=1, source_target_pairs={{0,16},{8,24},{16,0},{24,8},{1,17},{9,25},{17,1},{25,9},{2,18},{10... | collective-permute-start | bytes 1572872 | tf_op jit(solution)/shard_map/ppermute | solution.py:226
  59.3 14.8 %collective-permute-start.11 = (bf16[2,512,256]{2,1,0:T(8,128)(2,1)S(1)}, bf16[2,512,256]{2,1,0:T(8,128)(2,1)S(1)}, u32[]{:S(2)}, u32[]{:S(2)}) collective-permute-start(bf16[2,512,256]{2,1,0:T(8,128)(2,1)S(1)} %get-tuple-element.114), channel_id=1, source_target_pairs={{0,8},{8,0},{16,24},{24,16},{1,9},{9,1},{17,25},{25,17},{2,10},{10... | collective-permute-start | bytes 1572872 | tf_op jit(solution)/shard_map/ppermute | solution.py:226
  64.1 21.3 %collective-permute-start.9 = (bf16[2,512,256]{2,1,0:T(8,128)(2,1)S(1)}, bf16[2,512,256]{2,1,0:T(8,128)(2,1)S(1)}, u32[]{:S(2)}, u32[]{:S(2)}) collective-permute-start(bf16[2,512,256]{2,1,0:T(8,128)(2,1)S(1)} %get-tuple-element.118), channel_id=1, source_target_pairs={{0,8},{8,0},{16,24},{24,16},{1,9},{9,1},{17,25},{25,17},{2,10},{10... | collective-permute-start | bytes 1572872 | tf_op jit(solution)/shard_map/ppermute | solution.py:226
  68.1 15.8 %collective-permute-start.10 = (bf16[2,512,256]{2,1,0:T(8,128)(2,1)S(1)}, bf16[2,512,256]{2,1,0:T(8,128)(2,1)S(1)}, u32[]{:S(2)}, u32[]{:S(2)}) collective-permute-start(bf16[2,512,256]{2,1,0:T(8,128)(2,1)S(1)} %get-tuple-element.121), channel_id=1, source_target_pairs={{0,16},{8,24},{16,0},{24,8},{1,17},{9,25},{17,1},{25,9},{2,18},{10... | collective-permute-start | bytes 1572872 | tf_op jit(solution)/shard_map/ppermute | solution.py:226
  74.2 15.4 %collective-permute-start.16 = (bf16[2,512,128]{2,1,0:T(8,128)(2,1)S(1)}, bf16[2,512,128]{2,1,0:T(8,128)(2,1)S(1)}, u32[]{:S(2)}, u32[]{:S(2)}) collective-permute-start(bf16[2,512,128]{2,1,0:T(8,128)(2,1)S(1)} %add_convert_fusion.6), channel_id=1, source_target_pairs={{0,8},{8,0},{16,24},{24,16},{1,9},{9,1},{17,25},{25,17},{2,10},{10... | collective-permute-start | bytes 786440 | tf_op jit(solution)/shard_map/ppermute | solution.py:226
  75.8 13.8 %collective-permute-start.15 = (bf16[2,512,128]{2,1,0:T(8,128)(2,1)S(1)}, bf16[2,512,128]{2,1,0:T(8,128)(2,1)S(1)}, u32[]{:S(2)}, u32[]{:S(2)}) collective-permute-start(bf16[2,512,128]{2,1,0:T(8,128)(2,1)S(1)} %add_convert_fusion.7), channel_id=1, source_target_pairs={{0,16},{8,24},{16,0},{24,8},{1,17},{9,25},{17,1},{25,9},{2,18},{10... | collective-permute-start | bytes 786440 | tf_op jit(solution)/shard_map/ppermute | solution.py:226
  76.4 14.2 %collective-permute-start.17 = (bf16[2,2,128,512]{3,2,1,0:T(8,128)(2,1)S(1)}, bf16[2,2,128,512]{3,2,1,0:T(8,128)(2,1)S(1)}, u32[]{:S(2)}, u32[]{:S(2)}) collective-permute-start(bf16[2,2,128,512]{3,2,1,0:T(8,128)(2,1)S(1)} %collective-permute-done.13.refs_2_), channel_id=1, source_target_pairs={{0,2},{1,3},{2,4},{3,5},{4,6},{5,7},{6,0},{7,1},{8,10},{9,11},{10,... | collective-permute-start | bytes 1572872 | tf_op jit(solution)/shard_map/ppermute | solution.py:231
  89.6 1.9 %collective-permute-start.18 = (bf16[2,2,128,512]{3,2,1,0:T(8,128)(2,1)S(1)}, bf16[2,2,128,512]{3,2,1,0:T(8,128)(2,1)S(1)}, u32[]{:S(2)}, u32[]{:S(2)}) collective-permute-start(bf16[2,2,128,512]{3,2,1,0:T(8,128)(2,1)S(1)} %collective-permute-done.13.refs_2_), channel_id=1, source_target_pairs={{0,1},{1,0},{2,3},{3,2},{4,5},{5,4},{6,7},{7,6},{8,9},{9,8},{10,11... | collective-permute-start | bytes 1572872 | tf_op jit(solution)/shard_map/ppermute | solution.py:235
  89.6 2.7 %collective-permute-start.19 = (bf16[2,2,128,512]{3,2,1,0:T(8,128)(2,1)S(1)}, bf16[2,2,128,512]{3,2,1,0:T(8,128)(2,1)S(1)}, u32[]{:S(2)}, u32[]{:S(2)}) collective-permute-start(bf16[2,2,128,512]{3,2,1,0:T(8,128)(2,1)S(1)} %collective-permute-done.14.refs_6_), channel_id=1, source_target_pairs={{0,1},{1,0},{2,3},{3,2},{4,5},{5,4},{6,7},{7,6},{8,9},{9,8},{10,11... | collective-permute-start | bytes 1572872 | tf_op jit(solution)/shard_map/ppermute | solution.py:235
  92.3 9.9 %collective-permute-start.20 = (bf16[2,2,128,512]{3,2,1,0:T(8,128)(2,1)S(1)}, bf16[2,2,128,512]{3,2,1,0:T(8,128)(2,1)S(1)}, u32[]{:S(2)}, u32[]{:S(2)}) collective-permute-start(bf16[2,2,128,512]{3,2,1,0:T(8,128)(2,1)S(1)} %collective-permute-done.17.refs_4_), channel_id=1, source_target_pairs={{0,1},{1,0},{2,3},{3,2},{4,5},{5,4},{6,7},{7,6},{8,9},{9,8},{10,11... | collective-permute-start | bytes 1572872 | tf_op jit(solution)/shard_map/ppermute | solution.py:235
  92.4 8.6 %collective-permute-start.22 = (bf16[2,512,128]{2,1,0:T(8,128)(2,1)S(1)}, bf16[2,512,128]{2,1,0:T(8,128)(2,1)S(1)}, u32[]{:S(2)}, u32[]{:S(2)}) collective-permute-start(bf16[2,512,128]{2,1,0:T(8,128)(2,1)S(1)} %add_convert_fusion.4), channel_id=1, source_target_pairs={{0,8},{8,0},{16,24},{24,16},{1,9},{9,1},{17,25},{25,17},{2,10},{10... | collective-permute-start | bytes 786440 | tf_op jit(solution)/shard_map/ppermute | solution.py:226
  93.9 8.3 %collective-permute-start.21 = (bf16[2,512,128]{2,1,0:T(8,128)(2,1)S(1)}, bf16[2,512,128]{2,1,0:T(8,128)(2,1)S(1)}, u32[]{:S(2)}, u32[]{:S(2)}) collective-permute-start(bf16[2,512,128]{2,1,0:T(8,128)(2,1)S(1)} %add_convert_fusion.5), channel_id=1, source_target_pairs={{0,16},{8,24},{16,0},{24,8},{1,17},{9,25},{17,1},{25,9},{2,18},{10... | collective-permute-start | bytes 786440 | tf_op jit(solution)/shard_map/ppermute | solution.py:226
  101.0 5.3 %copy-start.7 = (bf16[2,512,128]{2,1,0:T(8,128)(2,1)}, bf16[2,512,128]{2,1,0:T(8,128)(2,1)S(1)}, u32[]{:S(2)}) copy-start(bf16[2,512,128]{2,1,0:T(8,128)(2,1)S(1)} %collective-permute-done.22.last_x) | copy-start | bytes 786436
  102.2 4.1 %copy-start.9 = (bf16[2,512,128]{2,1,0:T(8,128)(2,1)}, bf16[2,512,128]{2,1,0:T(8,128)(2,1)S(1)}, u32[]{:S(2)}) copy-start(bf16[2,512,128]{2,1,0:T(8,128)(2,1)S(1)} %collective-permute-done.21.last_y) | copy-start | bytes 786436
  110.2 15.1 %collective-permute-start.26 = (bf16[2,512,256]{2,1,0:T(8,128)(2,1)}, bf16[2,512,256]{2,1,0:T(8,128)(2,1)S(1)}, u32[]{:S(2)}, u32[]{:S(2)}) collective-permute-start(bf16[2,512,256]{2,1,0:T(8,128)(2,1)} %get-tuple-element.164), channel_id=1, source_target_pairs={{0,16},{8,24},{16,0},{24,8},{1,17},{9,25},{17,1},{25,9},{2,18},{10... | collective-permute-start | bytes 1572872 | tf_op jit(solution)/shard_map/ppermute | solution.py:226
  110.7 14.6 %collective-permute-start.25 = (bf16[2,512,256]{2,1,0:T(8,128)(2,1)}, bf16[2,512,256]{2,1,0:T(8,128)(2,1)}, u32[]{:S(2)}, u32[]{:S(2)}) collective-permute-start(bf16[2,512,256]{2,1,0:T(8,128)(2,1)} %get-tuple-element.162), channel_id=1, source_target_pairs={{0,8},{8,0},{16,24},{24,16},{1,9},{9,1},{17,25},{25,17},{2,10},{10... | collective-permute-start | bytes 1572872 | tf_op jit(solution)/shard_map/ppermute | solution.py:226
  114.6 0.8 copy-start.11
  118.7 0.8 copy-start.12
  119.5 17.0 %collective-permute-start.24 = (bf16[2,512,256]{2,1,0:T(8,128)(2,1)}, bf16[2,512,256]{2,1,0:T(8,128)(2,1)S(1)}, u32[]{:S(2)}, u32[]{:S(2)}) collective-permute-start(bf16[2,512,256]{2,1,0:T(8,128)(2,1)} %copy-done.12), channel_id=1, source_target_pairs={{0,16},{8,24},{16,0},{24,8},{1,17},{9,25},{17,1},{25,9},{2,18},{10... | collective-permute-start | bytes 1572872 | tf_op jit(solution)/shard_map/ppermute | solution.py:226
  121.0 15.5 %collective-permute-start.23 = (bf16[2,512,256]{2,1,0:T(8,128)(2,1)}, bf16[2,512,256]{2,1,0:T(8,128)(2,1)S(1)}, u32[]{:S(2)}, u32[]{:S(2)}) collective-permute-start(bf16[2,512,256]{2,1,0:T(8,128)(2,1)} %copy-done.11), channel_id=1, source_target_pairs={{0,8},{8,0},{16,24},{24,16},{1,9},{9,1},{17,25},{25,17},{2,10},{10... | collective-permute-start | bytes 1572872 | tf_op jit(solution)/shard_map/ppermute | solution.py:226
  125.4 16.5 %collective-permute-start.30 = (bf16[2,512,128]{2,1,0:T(8,128)(2,1)S(1)}, bf16[2,512,128]{2,1,0:T(8,128)(2,1)S(1)}, u32[]{:S(2)}, u32[]{:S(2)}) collective-permute-start(bf16[2,512,128]{2,1,0:T(8,128)(2,1)S(1)} %add_convert_fusion.2), channel_id=1, source_target_pairs={{0,8},{8,0},{16,24},{24,16},{1,9},{9,1},{17,25},{25,17},{2,10},{10... | collective-permute-start | bytes 786440 | tf_op jit(solution)/shard_map/ppermute | solution.py:226
  127.0 15.2 %collective-permute-start.29 = (bf16[2,512,128]{2,1,0:T(8,128)(2,1)S(1)}, bf16[2,512,128]{2,1,0:T(8,128)(2,1)S(1)}, u32[]{:S(2)}, u32[]{:S(2)}) collective-permute-start(bf16[2,512,128]{2,1,0:T(8,128)(2,1)S(1)} %add_convert_fusion.3), channel_id=1, source_target_pairs={{0,16},{8,24},{16,0},{24,8},{1,17},{9,25},{17,1},{25,9},{2,18},{10... | collective-permute-start | bytes 786440 | tf_op jit(solution)/shard_map/ppermute | solution.py:226
  136.6 9.6 %collective-permute-start.28 = (bf16[2,512,128]{2,1,0:T(8,128)(2,1)S(1)}, bf16[2,512,128]{2,1,0:T(8,128)(2,1)S(1)}, u32[]{:S(2)}, u32[]{:S(2)}) collective-permute-start(bf16[2,512,128]{2,1,0:T(8,128)(2,1)S(1)} %add_convert_fusion), channel_id=1, source_target_pairs={{0,8},{8,0},{16,24},{24,16},{1,9},{9,1},{17,25},{25,17},{2,10},{10... | collective-permute-start | bytes 786440 | tf_op jit(solution)/shard_map/ppermute | solution.py:226
  137.8 2.4 %copy-start.8 = (bf16[2,512,128]{2,1,0:T(8,128)(2,1)S(1)}, bf16[2,512,128]{2,1,0:T(8,128)(2,1)}, u32[]{:S(2)}) copy-start(bf16[2,512,128]{2,1,0:T(8,128)(2,1)} %copy-done.7) | copy-start | bytes 786436
  137.8 2.4 %copy-start.10 = (bf16[2,512,128]{2,1,0:T(8,128)(2,1)S(1)}, bf16[2,512,128]{2,1,0:T(8,128)(2,1)}, u32[]{:S(2)}) copy-start(bf16[2,512,128]{2,1,0:T(8,128)(2,1)} %copy-done.9) | copy-start | bytes 786436
  137.8 8.4 %collective-permute-start.27 = (bf16[2,512,128]{2,1,0:T(8,128)(2,1)S(1)}, bf16[2,512,128]{2,1,0:T(8,128)(2,1)S(1)}, u32[]{:S(2)}, u32[]{:S(2)}) collective-permute-start(bf16[2,512,128]{2,1,0:T(8,128)(2,1)S(1)} %add_convert_fusion.1), channel_id=1, source_target_pairs={{0,16},{8,24},{16,0},{24,8},{1,17},{9,25},{17,1},{25,9},{2,18},{10... | collective-permute-start | bytes 786440 | tf_op jit(solution)/shard_map/ppermute | solution.py:226

commit v5 on v4

--- a/solution.py
+++ b/solution.py
@@ -10,26 +10,28 @@
 
 STRETCH = 32
 WINDOW = 224
-GROUPS = (2, 2)
+GROUPS = (1, 1, 2)
 TILE = 128
 CORES = 2
 RELATIVE = (1, 3, 2, 0)
 
 masked_score = -1e30
-vmem_bytes = 48 * 1024 * 1024
-
-
-def arrange_kernel(kv_ref, tangent_ref, value_ref, *group_refs):
+vmem_bytes = 16 * 1024 * 1024
+
+
+def arrange_kernel(kv_ref, tangent_ref, value_ref, whole_ref, *group_refs):
     columns = tangent_ref.shape[1] // len(RELATIVE)
+    part = whole_ref.shape[3] // len(RELATIVE)
     chunk = 0
     for group_ref in group_refs:
-        part = group_ref.shape[3] // len(RELATIVE)
         for index in range(group_ref.shape[0]):
             for place, flip in enumerate(RELATIVE):
                 start = pl.multiple_of((kv_ref[0] ^ flip) * columns + chunk * part, part)
                 to = slice(place * part, (place + 1) * part)
-                group_ref[index, 0, :, to] = tangent_ref[:, pl.ds(start, part)]
-                group_ref[index, 1, :, to] = value_ref[:, pl.ds(start, part)]
+                for mat, ref in enumerate((tangent_ref, value_ref)):
+                    block = ref[:, pl.ds(start, part)]
+                    whole_ref[chunk, mat, :, to] = block
+                    group_ref[index, mat, :, to] = block
             chunk += 1
 
 
@@ -37,7 +39,7 @@
     rows, columns = value.shape
     shapes = [
         jax.ShapeDtypeStruct((count, 2, rows, columns // sum(GROUPS)), value.dtype)
-        for count in GROUPS
+        for count in (sum(GROUPS), *GROUPS)
     ]
     return pl.pallas_call(
         arrange_kernel,
@@ -46,8 +48,9 @@
             pl.BlockSpec(memory_space=pltpu.VMEM),
             pl.BlockSpec(memory_space=pltpu.VMEM),
         ],
-        out_specs=[pl.BlockSpec(memory_space=pltpu.VMEM)] * len(GROUPS),
+        out_specs=[pl.BlockSpec(memory_space=pltpu.VMEM)] * len(shapes),
         out_shape=shapes,
+        compiler_params=pltpu.CompilerParams(vmem_limit_bytes=vmem_bytes),
         name="arrange",
     )(kv_index.reshape(1), tangent, value)
 
@@ -145,53 +148,79 @@
     )(order, queries, query_tangent, context, low)
 
 
-def project_kernel(sent, kept, pair_ref, *refs):
-    *weight_refs, send_ref, keep_ref = refs
-    width = pair_ref.shape[1] // 2
-    rows = weight_refs[0].shape[1]
-    part = weight_refs[0].shape[2] // len(RELATIVE)
-    dot = functools.partial(jnp.dot, preferred_element_type=jnp.float32)
-    value, tangent, start = 0.0, 0.0, 0
-    joined = max(1, 256 // rows)
-    for first in range(0, len(weight_refs), joined):
-        refs = weight_refs[first : first + joined]
-        end = start + rows * len(refs)
-        tan_weight = jnp.concatenate([ref[0] for ref in refs], axis=0)
-        weight = jnp.concatenate([ref[1] for ref in refs], axis=0)
-        attended, attended_tan = pair_ref[:, start:end], pair_ref[:, width + start : width + end]
-        value += dot(attended, weight)
-        tangent += dot(attended, tan_weight) + dot(attended_tan, weight)
-        start = end
-    for ref, flips in ((send_ref, sent), (keep_ref, kept)):
-        for place, flip in enumerate(flips):
-            at = RELATIVE.index(flip) * part
-            to = slice(place * part, (place + 1) * part)
-            ref[0, :, to] = value[:, at : at + part].astype(ref.dtype)
-            ref[1, :, to] = tangent[:, at : at + part].astype(ref.dtype)
-
-
-def project(sent, kept, pair, index, weights):
-    tokens, width = pair.shape
+def project_kernel(places, first_ref, second_ref, *refs):
+    count = len(places)
+    piece_refs = refs[:count]
+    send_x, keep_x, send_y, keep_y, weight_ref, sems = refs[count:]
+    step, steps = pl.program_id(0), pl.num_programs(0)
+    rows = piece_refs[0].shape[2]
+    depth = count * rows
+    part = weight_ref.shape[2] // len(RELATIVE)
+
+    @pl.when(step == 0)
+    def _():
+        copies = []
+        for place, (index, ref) in enumerate(zip(places, piece_refs)):
+            to = weight_ref.at[:, pl.ds(place * rows, rows), :]
+            copies.append(pltpu.make_async_copy(ref.at[index], to, sems.at[place]))
+            copies[-1].start()
+        for copy in copies:
+            copy.wait()
+
+    def run(pair_ref, send_ref, keep_ref, sent, kept):
+        dot = functools.partial(jnp.dot, preferred_element_type=jnp.float32)
+        value = dot(pair_ref[:, :depth], weight_ref[1])
+        tangent = dot(pair_ref[:, :depth], weight_ref[0]) + dot(pair_ref[:, depth:], weight_ref[1])
+        for ref, flips in ((send_ref, sent), (keep_ref, kept)):
+            for place, flip in enumerate(flips):
+                at = RELATIVE.index(flip) * part
+                to = slice(place * part, (place + 1) * part)
+                ref[0, :, to] = value[:, at : at + part].astype(ref.dtype)
+                ref[1, :, to] = tangent[:, at : at + part].astype(ref.dtype)
+
+    @pl.when(step < steps // 2)
+    def _():
+        run(first_ref, send_x, keep_x, (1, 3), (2, 0))
+
+    @pl.when(step >= steps // 2)
+    def _():
+        run(second_ref, send_y, keep_y, (2, 3), (1, 0))
+
+
+def project(pairs, pieces):
+    tokens, width = pairs[0].shape
     tile = min(2 * TILE, tokens)
-    _, _, rows, columns = weights[0].shape
+    steps = tokens // tile
+    places = [index for index, _ in pieces]
+    blocks = [block for _, block in pieces]
+    _, _, rows, columns = blocks[0].shape
+    early = lambda i: jnp.minimum(i, steps - 1)
+    late = lambda i: jnp.maximum(i - steps, 0)
     out = (2, tokens, columns // 2)
-    block = pl.BlockSpec((2, tile, columns // 2), lambda i: (0, i, 0))
-    piece = pl.BlockSpec((None, 2, rows, columns), lambda i: (index, 0, 0, 0))
+    first = pl.BlockSpec((2, tile, columns // 2), lambda i: (0, early(i), 0))
+    second = pl.BlockSpec((2, tile, columns // 2), lambda i: (0, late(i), 0))
+    send = jax.ShapeDtypeStruct(out, jnp.bfloat16)
+    keep = jax.ShapeDtypeStruct(out, jnp.float32)
     return pl.pallas_call(
-        functools.partial(project_kernel, sent, kept),
-        grid=(tokens // tile,),
-        in_specs=[pl.BlockSpec((tile, width), lambda i: (i, 0))] + [piece] * len(weights),
-        out_specs=[block, block],
-        out_shape=[
-            jax.ShapeDtypeStruct(out, jnp.bfloat16),
-            jax.ShapeDtypeStruct(out, jnp.float32),
+        functools.partial(project_kernel, places),
+        grid=(2 * steps,),
+        in_specs=[
+            pl.BlockSpec((tile, width), lambda i: (early(i), 0)),
+            pl.BlockSpec((tile, width), lambda i: (late(i), 0)),
+            *[pl.BlockSpec(memory_space=pl.ANY)] * len(blocks),
+        ],
+        out_specs=[first, first, second, second],
+        out_shape=[send, keep, send, keep],
+        scratch_shapes=[
+            pltpu.VMEM((2, rows * len(blocks), columns), jnp.bfloat16),
+            pltpu.SemaphoreType.DMA((len(blocks),)),
         ],
         compiler_params=pltpu.CompilerParams(vmem_limit_bytes=vmem_bytes),
         cost_estimate=pl.CostEstimate(
             flops=tokens * columns, bytes_accessed=tokens, transcendentals=0
         ),
         name="project",
-    )(pair, *weights)
+    )(*pairs, *blocks)
 
 
 def finish_kernel(keep_x, from_x, last_y, keep_y, from_y, last_x, *refs):
@@ -246,38 +275,38 @@
         self.chips = chips
         self.forward, self.backward = chips // 2, (chips - 1) // 2
 
-    def neighbours(self):
+    def ahead(self):
         if self.forward:
             self.blocks[1] = along(self.blocks[0], 1)
+
+    def behind(self):
         if self.backward:
             self.blocks[self.chips - 1] = along(self.blocks[0], -1)
 
-    def farther(self):
+    def farther_ahead(self):
         for step in range(2, self.forward + 1):
             self.blocks[step] = along(self.blocks[step - 1], 1)
+
+    def farther_behind(self):
         for step in range(2, self.backward + 1):
             self.blocks[self.chips - step] = along(self.blocks[self.chips - step + 1], -1)
 
-    def near(self):
-        steps = (0, 1, self.chips - 1)
-        return {step: self.blocks[step] for step in steps if step in self.blocks}
-
-    def exchange(self, blocks):
-        for step, block in blocks.items():
-            if step not in self.others:
-                self.others[step] = other_core(block)
-
-    def all(self):
-        weights = []
-        for step in range(self.chips):
-            weights += [self.blocks[step], self.others[step]]
-        return weights
+    def exchange(self, *steps):
+        for step in steps or range(1, self.chips):
+            if step % self.chips in self.blocks and step % self.chips not in self.others:
+                self.others[step % self.chips] = other_core(self.blocks[step % self.chips])
 
     def get(self):
         return self.blocks, self.others
 
     def put(self, state):
         self.blocks, self.others = (dict(part) for part in state)
+
+    def pieces(self, index, whole, chunk):
+        pieces = [(index, self.blocks[0]), (chunk, whole)]
+        for step in range(1, self.chips):
+            pieces += [(index, self.blocks[step]), (index, self.others[step])]
+        return pieces
 
 
 def body(
@@ -292,9 +321,11 @@
     seq_size = lax.axis_size("seq")
     chips = seq_size // CORES
 
-    mine = arrange(kv_index, weight_tangent, out_weight)
-    early, late = [Gather(block, chips) for block in mine]
-    early.neighbours()
+    whole, *mine = arrange(kv_index, weight_tangent, out_weight)
+    one, two, rest = [Gather(block, chips) for block in mine]
+    one.ahead()
+    one.behind()
+    whole = other_core(whole)
 
     key_value, key_value_tangents, _ = lax.optimization_barrier(
         (key_value, key_value_tangents, mine[0])
@@ -330,14 +361,11 @@
             pair = pair.reshape(half, 2 * width)
         return pair
 
-    def first_stage(gathering, index, pairs):
-        weights = gathering.all()
-        send_x, keep_x = project((1, 3), (2, 0), pairs[0], index, weights)
-        from_x = across(send_x, 1)
-        pair, send_x = together(pairs[1], send_x)
-        send_y, keep_y = project((2, 3), (1, 0), pair, index, weights)
-        from_y = across(send_y, 2)
-        return (keep_x, keep_y), (from_x, from_y), send_y
+    def first_stage(gathering, index, chunk, pairs, last=()):
+        pieces = gathering.pieces(index, whole, chunk)
+        send_x, keep_x, send_y, keep_y = project(pairs, pieces)
+        send_x, send_y, last = together(send_x, send_y, last)
+        return (keep_x, keep_y), (across(send_x, 1), across(send_y, 2)), send_y, last
 
     def second_sums(kept, received):
         part = kept[0].shape[2] // 2
@@ -357,44 +385,57 @@
         )
 
     pair_second = attend(1, stacked)
-    pair_second, prior, state, held = together(pair_second, prior, early.get(), late.blocks)
-    early.put(state)
-    late.blocks = dict(held)
-    early.farther()
-    early.exchange(early.near())
-    late.exchange(late.near())
+    pair_second, prior, state, held = together(pair_second, prior, one.get(), two.blocks)
+    one.put(state)
+    two.blocks = dict(held)
+    one.farther_ahead()
+    one.farther_behind()
+    one.exchange(1, -1)
+    two.ahead()
     pair_first = attend(0, jnp.concatenate([prior, stacked[:half]], axis=0))
 
-    pairs, state, held = together((pair_first, pair_second), early.get(), late.get())
-    early.put(state)
-    late.put(held)
-    early.exchange(early.blocks)
-    late.neighbours()
-    kept0, from0, send = first_stage(early, 0, pairs)
-    pairs, send = together(pairs, send)
-    kept1, from1, send = first_stage(early, 1, pairs)
-
-    from0, state, pairs, send = together(from0, late.get(), pairs, send)
-    late.put(state)
-    late.farther()
+    pairs, whole, state, held, mine = together(
+        (pair_first, pair_second), whole, one.get(), two.get(), rest.blocks
+    )
+    one.put(state)
+    two.put(held)
+    rest.blocks = dict(mine)
+    one.exchange()
+    two.farther_ahead()
+    two.behind()
+    two.exchange(1)
+    kept0, from0, send, _ = first_stage(one, 0, 0, pairs)
+
+    held, pairs, send = together(two.get(), pairs, send)
+    two.put(held)
+    two.farther_behind()
+    two.exchange()
+    rest.ahead()
+    rest.behind()
+    held, from0 = together(two.get(), from0)
+    two.put(held)
     sums = second_sums(kept0, from0)
     last0 = second_stage(sums)
-
-    from1, last0, sums, pairs, held = together(from1, last0, sums, pairs, late.near())
-    late.blocks.update(held)
-    late.exchange(held)
+    pairs, sums = together(pairs, sums)
+    kept1, from1, send, last0 = first_stage(two, 0, 1, pairs, last0)
+
+    state, send = together(rest.get(), send)
+    rest.put(state)
+    rest.farther_ahead()
+    rest.exchange(1, -1)
+    rest.farther_behind()
+    outputs = write(0, (), kept0, from0, last0)
+
+    from1, pairs, send, outputs = together(from1, pairs, send, outputs)
     sums = second_sums(kept1, from1)
     last1 = second_stage(sums)
-    outputs = write(0, (), kept0, from0, last0)
-
-    state, sums, pairs = together(late.get(), sums, pairs)
-    late.put(state)
-    late.exchange(late.blocks)
-    state, last1, pairs = together(late.get(), last1, pairs)
-    late.put(state)
-    kept2, from2, send = first_stage(late, 0, pairs)
+
+    state, sums, pairs = together(rest.get(), sums, pairs)
+    rest.put(state)
+    rest.exchange()
+    kept2, from2, send, last1 = first_stage(rest, 0, 2, pairs, last1)
     pairs, send = together(pairs, send)
-    kept3, from3, send = first_stage(late, 1, pairs)
+    kept3, from3, send, _ = first_stage(rest, 1, 3, pairs)
 
     from2, send = together(from2, send)
     sums = second_sums(kept2, from2)

time: 148 us -> 153 us (1.034)
  waiting for transfers between devices: 55.5 us -> 69.7 us
  Pallas kernels: 45.9 us -> 34 us
  starting transfers between devices: 33.7 us -> 37.8 us
    ppermute x6 -> x9, waiting for transfers between devices: 18.5 us -> 35.4 us  [along(): lax.ppermute(block, 'seq', [(i, (i + CORES * chips) % size) for i in rang...]
    pallas_call x8 -> x4, Pallas kernels: 27.9 us -> 19.1 us  [project(): pl.pallas_call(functools.partial(project_kernel, places), grid=(2 * steps...]
    ppermute x16, waiting for transfers between devices: 35.4 us -> 32.4 us  [across(): return lax.ppermute(block, 'kv', [(i, i ^ flip) for i in range(size)])]
    ppermute x6 -> x9, starting transfers between devices: 12.4 us -> 15.3 us  [along(): lax.ppermute(block, 'seq', [(i, (i + CORES * chips) % size) for i in rang...]
    unnamed x30 -> x20, local copies, waits for them, and re-layouts: 6.47 us -> 5.88 us
  transfers between devices with their start and end apart: 31 -> 36, of which waited for: 17 -> 20; matrix products, arithmetic and copies ran while one was open for 3% -> 3% of each run, Pallas kernels for 23% -> 21%
where the time goes in v5:
time: 153 us
  waiting for transfers between devices  69.7 us (46%)
  starting transfers between devices  37.8 us (25%)
  Pallas kernels  34 us (22%)
  local copies, waits for them, and re-layouts  8.24 us (5%)
  other arithmetic  1.98 us (1%)
    ppermute x9, waiting for transfers between devices, along(): lax.ppermute(block, 'seq', [(i, (i + CORES * chips) % size) for i in rang...  35.4 us
    ppermute x16, waiting for transfers between devices, across(): return lax.ppermute(block, 'kv', [(i, i ^ flip) for i in range(size)])  32.4 us
    pallas_call x4, Pallas kernels, project(): pl.pallas_call(functools.partial(project_kernel, places), grid=(2 * steps...  19.1 us
    ppermute x16, starting transfers between devices, across(): return lax.ppermute(block, 'kv', [(i, i ^ flip) for i in range(size)])  17.6 us
    ppermute x9, starting transfers between devices, along(): lax.ppermute(block, 'seq', [(i, (i + CORES * chips) % size) for i in rang...  15.3 us
    pallas_call x2, Pallas kernels, attention(): pl.pallas_call(functools.partial(attention_kernel, heads, head_dim, offse...  9.52 us
    unnamed x20, local copies, waits for them, and re-layouts  5.88 us
    pallas_call x4, Pallas kernels, finish(): pl.pallas_call(finish_kernel, grid=(1,), in_specs=[kept, received, receiv...  4.05 us
  transfers between devices with their start and end apart: 36, of which 20 were waited for; matrix products, arithmetic and copies ran while one was open for 3% of the time, Pallas kernels for 21%

profile of v5, /device:TPU:0, one launch (start us, length us, event | category | flops | bytes accessed | tf_op | source)
XLA Modules:
  0.0 152.6 jit_solution(13277358828130925606)
XLA Ops:
  0.6 1.0 copy-done.6
  1.7 1.0 copy-done.7
  2.7 1.4 arrange.1
  4.1 5.0 %collective-permute-start.2 = (bf16[1,2,128,512]{3,2,1,0:T(8,128)(2,1)}, bf16[1,2,128,512]{3,2,1,0:T(8,128)(2,1)}, u32[]{:S(2)}, u32[]{:S(2)}) collective-permute-start(bf16[1,2,128,512]{3,2,1,0:T(8,128)(2,1)} %get-tuple-element.118.refs_0_), channel_id=1, source_target_pairs={{0,6},{1,7},{2,0},{3,1},{4,2},{5,3},{6,4},{7,5},{8,14},{9,15},{10,... | collective-permute-start | bytes 786440 | tf_op jit(solution)/shard_map/ppermute | solution.py:260
  9.1 1.1 copy.25
  10.6 0.7 slice.92
  11.3 1.0 copy-done.2
  12.3 3.1 %collective-permute-start = (bf16[224,512]{1,0:T(8,128)(2,1)}, bf16[224,512]{1,0:T(8,128)(2,1)}, u32[]{:S(2)}, u32[]{:S(2)}) collective-permute-start(bf16[224,512]{1,0:T(8,128)(2,1)} %slice.92), channel_id=1, source_target_pairs={{0,1},{1,2},{2,3},{3,4},{4,5},{5,6},{6,7},{8,9},{9,10},{10,11},{11... | collective-permute-start | bytes 688136 | tf_op jit(solution)/shard_map/ppermute | solution.py:337
  16.3 1.6 %copy-done.1 = bf16[1024,1024]{1,0:T(8,128)(2,1)S(1)} copy-done((bf16[1024,1024]{1,0:T(8,128)(2,1)S(1)}, bf16[1024,1024]{1,0:T(8,128)(2,1)}, u32[]{:S(2)}) %copy-start.1) | copy-done | bytes 2097176
  17.8 1.2 copy-done.3
  19.1 4.8 %attention.2.second_ref = bf16[512,2048]{1,0:T(8,128)(2,1)S(1)} custom-call(s32[8]{0:T(128)S(1)} %reshape.118.order_ref, bf16[1024,1024]{1,0:T(8,128)(2,1)S(1)} %copy-done, bf16[1024,1024]{1,0:T(8,128)(2,1)S(1)} %copy-done.1, bf16[1024,512]{1,0:T(8,128)(2,1)S(1)} %copy-done.3, s32[1024,128]{1,0:T(8,128)S(1)} %broadcast_in_dim.13.low_ref), custom_call_target="tpu_custom_call" | custom-call | flops 1048576 | bytes 512 | tf_op jit(solution)/shard_map/attention/pallas_call | solution.py:131
  23.9 1.7 %collective-permute-start.7 = (bf16[1,2,128,512]{3,2,1,0:T(8,128)(2,1)S(1)}, bf16[1,2,128,512]{3,2,1,0:T(8,128)(2,1)S(1)}, u32[]{:S(2)}, u32[]{:S(2)}) collective-permute-start(bf16[1,2,128,512]{3,2,1,0:T(8,128)(2,1)S(1)} %get-tuple-element.142.refs_0_), channel_id=1, source_target_pairs={{0,2},{1,3},{2,4},{3,5},{4,6},{5,7},{6,0},{7,1},{8,10},{9,11},{10,... | collective-permute-start | bytes 786440 | tf_op jit(solution)/shard_map/ppermute | solution.py:260
  25.9 2.0 %collective-permute-start.4 = (bf16[1,2,128,512]{3,2,1,0:T(8,128)(2,1)}, bf16[1,2,128,512]{3,2,1,0:T(8,128)(2,1)S(1)}, u32[]{:S(2)}, u32[]{:S(2)}) collective-permute-start(bf16[1,2,128,512]{3,2,1,0:T(8,128)(2,1)} %collective-permute-done.1.refs_2_), channel_id=1, source_target_pairs={{0,2},{1,3},{2,4},{3,5},{4,6},{5,7},{6,0},{7,1},{8,10},{9,11},{10,... | collective-permute-start | bytes 786440 | tf_op jit(solution)/shard_map/ppermute | solution.py:260
  27.8 1.0 pad_maximum_fusion.1.ctx_ref
  28.8 4.8 %attention.3.first_ref = bf16[512,2048]{1,0:T(8,128)(2,1)S(1)} custom-call(s32[8]{0:T(128)S(1)} %reshape.118.order_ref, bf16[1024,1024]{1,0:T(8,128)(2,1)S(1)} %copy-done, bf16[1024,1024]{1,0:T(8,128)(2,1)S(1)} %copy-done.1, bf16[736,512]{1,0:T(8,128)(2,1)S(1)} %pad_maximum_fusion.1.ctx_ref, s32[1024,128]{1,0:T(8,128)S(1)} %broadcast_in_dim.13.low_ref), custom_call_target="tpu_custom_call" | custom-call | flops 1048576 | bytes 512 | tf_op jit(solution)/shard_map/attention/pallas_call | solution.py:131
  33.6 1.3 collective-permute-done.7.refs_2_
  34.9 5.2 %collective-permute-done.4.refs_4_ = bf16[1,2,128,512]{3,2,1,0:T(8,128)(2,1)S(1)} collective-permute-done((bf16[1,2,128,512]{3,2,1,0:T(8,128)(2,1)}, bf16[1,2,128,512]{3,2,1,0:T(8,128)(2,1)S(1)}, u32[]{:S(2)}, u32[]{:S(2)}) %collective-permute-start.4) | collective-permute-done | bytes 262176 | tf_op jit(solution)/shard_map/ppermute | solution.py:260
  40.6 3.8 %collective-permute-start.11 = (bf16[1,2,128,512]{3,2,1,0:T(8,128)(2,1)S(1)}, bf16[1,2,128,512]{3,2,1,0:T(8,128)(2,1)S(1)}, u32[]{:S(2)}, u32[]{:S(2)}) collective-permute-start(bf16[1,2,128,512]{3,2,1,0:T(8,128)(2,1)S(1)} %get-tuple-element.142.refs_0_), channel_id=1, source_target_pairs={{0,6},{1,7},{2,0},{3,1},{4,2},{5,3},{6,4},{7,5},{8,14},{9,15},{10,... | collective-permute-start | bytes 786440 | tf_op jit(solution)/shard_map/ppermute | solution.py:260
  44.4 5.5 %project.4 = (bf16[2,512,256]{2,1,0:T(8,128)(2,1)S(1)}, f32[2,512,256]{2,1,0:T(8,128)S(1)}, bf16[2,512,256]{2,1,0:T(8,128)(2,1)S(1)}, f32[2,512,256]{2,1,0:T(8,128)S(1)}) custom-call(bf16[512,2048]{1,0:T(8,128)(2,1)S(1)} %attention.3.first_ref, bf16[512,2048]{1,0:T(8,128)(2,1)S(1)} %attention.2.second_ref, ...), custom_call_target="tpu_custom_call" | custom-call | flops 262144 | bytes 512 | tf_op jit(solution)/shard_map/project/pallas_call | solution.py:204
  49.9 1.6 %collective-permute-start.16 = (bf16[2,512,256]{2,1,0:T(8,128)(2,1)S(1)}, bf16[2,512,256]{2,1,0:T(8,128)(2,1)S(1)}, u32[]{:S(2)}, u32[]{:S(2)}) collective-permute-start(bf16[2,512,256]{2,1,0:T(8,128)(2,1)S(1)} %get-tuple-element.136), channel_id=1, source_target_pairs={{0,8},{8,0},{16,24},{24,16},{1,9},{9,1},{17,25},{25,17},{2,10},{10... | collective-permute-start | bytes 1572872 | tf_op jit(solution)/shard_map/ppermute | solution.py:255
  51.5 1.5 collective-permute-start.17
  53.0 1.4 collective-permute-done.11.refs_6_
  54.9 1.0 collective-permute-done.14.refs_5_
  56.3 6.9 %collective-permute-done.16.from_x = bf16[2,512,256]{2,1,0:T(8,128)(2,1)S(1)} collective-permute-done((bf16[2,512,256]{2,1,0:T(8,128)(2,1)S(1)}, bf16[2,512,256]{2,1,0:T(8,128)(2,1)S(1)}, u32[]{:S(2)}, u32[]{:S(2)}) %collective-permute-start.16) | collective-permute-done | bytes 524320 | tf_op jit(solution)/shard_map/ppermute | solution.py:255
  63.3 1.2 collective-permute-done.17.from_y
  65.2 1.6 %collective-permute-start.18 = (bf16[2,512,128]{2,1,0:T(8,128)(2,1)S(1)}, bf16[2,512,128]{2,1,0:T(8,128)(2,1)S(1)}, u32[]{:S(2)}, u32[]{:S(2)}) collective-permute-start(bf16[2,512,128]{2,1,0:T(8,128)(2,1)S(1)} %add_convert_fusion.7), channel_id=1, source_target_pairs={{0,16},{8,24},{16,0},{24,8},{1,17},{9,25},{17,1},{25,9},{2,18},{10... | collective-permute-start | bytes 786440 | tf_op jit(solution)/shard_map/ppermute | solution.py:255
  67.1 1.7 %collective-permute-start.8 = (bf16[2,2,128,512]{3,2,1,0:T(8,128)(2,1)S(1)}, bf16[2,2,128,512]{3,2,1,0:T(8,128)(2,1)S(1)}, u32[]{:S(2)}, u32[]{:S(2)}) collective-permute-start(bf16[2,2,128,512]{3,2,1,0:T(8,128)(2,1)S(1)} %copy-done.5), channel_id=1, source_target_pairs={{0,2},{1,3},{2,4},{3,5},{4,6},{5,7},{6,0},{7,1},{8,10},{9,11},{10,... | collective-permute-start | bytes 1572872 | tf_op jit(solution)/shard_map/ppermute | solution.py:260
  68.8 4.5 %project.5 = (bf16[2,512,256]{2,1,0:T(8,128)(2,1)S(1)}, f32[2,512,256]{2,1,0:T(8,128)S(1)}, bf16[2,512,256]{2,1,0:T(8,128)(2,1)S(1)}, f32[2,512,256]{2,1,0:T(8,128)S(1)}) custom-call(bf16[512,2048]{1,0:T(8,128)(2,1)S(1)} %attention.3.first_ref, bf16[512,2048]{1,0:T(8,128)(2,1)S(1)} %attention.2.second_ref, ...), custom_call_target="tpu_custom_call" | custom-call | flops 262144 | bytes 512 | tf_op jit(solution)/shard_map/project/pallas_call | solution.py:204
  73.4 1.6 %collective-permute-start.23 = (bf16[2,512,256]{2,1,0:T(8,128)(2,1)S(1)}, bf16[2,512,256]{2,1,0:T(8,128)(2,1)S(1)}, u32[]{:S(2)}, u32[]{:S(2)}) collective-permute-start(bf16[2,512,256]{2,1,0:T(8,128)(2,1)S(1)} %get-tuple-element.156), channel_id=1, source_target_pairs={{0,8},{8,0},{16,24},{24,16},{1,9},{9,1},{17,25},{25,17},{2,10},{10... | collective-permute-start | bytes 1572872 | tf_op jit(solution)/shard_map/ppermute | solution.py:255
  75.4 14.1 %collective-permute-done.9.refs_6_ = bf16[2,2,128,512]{3,2,1,0:T(8,128)(2,1)S(1)} collective-permute-done((bf16[2,2,128,512]{3,2,1,0:T(8,128)(2,1)S(1)}, bf16[2,2,128,512]{3,2,1,0:T(8,128)(2,1)S(1)}, u32[]{:S(2)}, u32[]{:S(2)}) %collective-permute-start.9) | collective-permute-done | bytes 524320 | tf_op jit(solution)/shard_map/ppermute | solution.py:260
  90.7 1.0 finish.4
  92.2 13.5 %collective-permute-done.20.refs_4_ = bf16[2,2,128,512]{3,2,1,0:T(8,128)(2,1)S(1)} collective-permute-done((bf16[2,2,128,512]{3,2,1,0:T(8,128)(2,1)S(1)}, bf16[2,2,128,512]{3,2,1,0:T(8,128)(2,1)S(1)}, u32[]{:S(2)}, u32[]{:S(2)}) %collective-permute-start.20) | collective-permute-done | bytes 524320 | tf_op jit(solution)/shard_map/ppermute | solution.py:260
  105.7 1.5 collective-permute-start.27
  107.7 4.5 %project.6 = (bf16[2,512,256]{2,1,0:T(8,128)(2,1)S(1)}, f32[2,512,256]{2,1,0:T(8,128)S(1)}, bf16[2,512,256]{2,1,0:T(8,128)(2,1)S(1)}, f32[2,512,256]{2,1,0:T(8,128)S(1)}) custom-call(bf16[512,2048]{1,0:T(8,128)(2,1)S(1)} %attention.3.first_ref, bf16[512,2048]{1,0:T(8,128)(2,1)S(1)} %attention.2.second_ref, bf16[2,2,128,512]{3,2,1,0:T(8,128)(2,1)S(1)} %copy-done.5, ...), custom_call_target="tpu_custom_call" | custom-call | flops 262144 | bytes 512 | tf_op jit(solution)/shard_map/project/pallas_call | solution.py:204
  112.2 2.2 %collective-permute-done.27.last_x = bf16[2,512,128]{2,1,0:T(8,128)(2,1)S(1)} collective-permute-done((bf16[2,512,128]{2,1,0:T(8,128)(2,1)S(1)}, bf16[2,512,128]{2,1,0:T(8,128)(2,1)S(1)}, u32[]{:S(2)}, u32[]{:S(2)}) %collective-permute-start.27) | collective-permute-done | bytes 262176 | tf_op jit(solution)/shard_map/ppermute | solution.py:255
  114.4 1.2 collective-permute-done.26.last_y
  116.7 4.5 %project.7 = (bf16[2,512,256]{2,1,0:T(8,128)(2,1)S(1)}, f32[2,512,256]{2,1,0:T(8,128)S(1)}, bf16[2,512,256]{2,1,0:T(8,128)(2,1)S(1)}, f32[2,512,256]{2,1,0:T(8,128)S(1)}) custom-call(bf16[512,2048]{1,0:T(8,128)(2,1)S(1)} %attention.3.first_ref, bf16[512,2048]{1,0:T(8,128)(2,1)S(1)} %attention.2.second_ref, bf16[2,2,128,512]{3,2,1,0:T(8,128)(2,1)S(1)} %copy-done.5, ...), custom_call_target="tpu_custom_call" | custom-call | flops 262144 | bytes 512 | tf_op jit(solution)/shard_map/project/pallas_call | solution.py:204
  121.2 1.5 %collective-permute-start.28 = (bf16[2,512,256]{2,1,0:T(8,128)(2,1)S(1)}, bf16[2,512,256]{2,1,0:T(8,128)(2,1)S(1)}, u32[]{:S(2)}, u32[]{:S(2)}) collective-permute-start(bf16[2,512,256]{2,1,0:T(8,128)(2,1)S(1)} %get-tuple-element.182), channel_id=1, source_target_pairs={{0,8},{8,0},{16,24},{24,16},{1,9},{9,1},{17,25},{25,17},{2,10},{10... | collective-permute-start | bytes 1572872 | tf_op jit(solution)/shard_map/ppermute | solution.py:255
  122.7 1.5 collective-permute-start.29
  124.3 6.2 %collective-permute-done.30.from_x = bf16[2,512,256]{2,1,0:T(8,128)(2,1)S(1)} collective-permute-done((bf16[2,512,256]{2,1,0:T(8,128)(2,1)S(1)}, bf16[2,512,256]{2,1,0:T(8,128)(2,1)S(1)}, u32[]{:S(2)}, u32[]{:S(2)}) %collective-permute-start.30) | collective-permute-done | bytes 524320 | tf_op jit(solution)/shard_map/ppermute | solution.py:255
  131.1 1.5 %collective-permute-start.35 = (bf16[2,512,128]{2,1,0:T(8,128)(2,1)S(1)}, bf16[2,512,128]{2,1,0:T(8,128)(2,1)S(1)}, u32[]{:S(2)}, u32[]{:S(2)}) collective-permute-start(bf16[2,512,128]{2,1,0:T(8,128)(2,1)S(1)} %add_convert_fusion.2), channel_id=1, source_target_pairs={{0,8},{8,0},{16,24},{24,16},{1,9},{9,1},{17,25},{25,17},{2,10},{10... | collective-permute-start | bytes 786440 | tf_op jit(solution)/shard_map/ppermute | solution.py:255
  133.2 8.5 %collective-permute-done.28.from_x = bf16[2,512,256]{2,1,0:T(8,128)(2,1)S(1)} collective-permute-done((bf16[2,512,256]{2,1,0:T(8,128)(2,1)S(1)}, bf16[2,512,256]{2,1,0:T(8,128)(2,1)S(1)}, u32[]{:S(2)}, u32[]{:S(2)}) %collective-permute-start.28) | collective-permute-done | bytes 524320 | tf_op jit(solution)/shard_map/ppermute | solution.py:255
  142.3 1.5 %collective-permute-start.33 = (bf16[2,512,128]{2,1,0:T(8,128)(2,1)S(1)}, bf16[2,512,128]{2,1,0:T(8,128)(2,1)S(1)}, u32[]{:S(2)}, u32[]{:S(2)}) collective-permute-start(bf16[2,512,128]{2,1,0:T(8,128)(2,1)S(1)} %add_convert_fusion), channel_id=1, source_target_pairs={{0,8},{8,0},{16,24},{24,16},{1,9},{9,1},{17,25},{25,17},{2,10},{10... | collective-permute-start | bytes 786440 | tf_op jit(solution)/shard_map/ppermute | solution.py:255
  144.5 1.0 finish.5
  145.5 1.8 %collective-permute-done.35.last_x = bf16[2,512,128]{2,1,0:T(8,128)(2,1)S(1)} collective-permute-done((bf16[2,512,128]{2,1,0:T(8,128)(2,1)S(1)}, bf16[2,512,128]{2,1,0:T(8,128)(2,1)S(1)}, u32[]{:S(2)}, u32[]{:S(2)}) %collective-permute-start.35) | collective-permute-done | bytes 262176 | tf_op jit(solution)/shard_map/ppermute | solution.py:255
  147.9 1.0 finish.6
  148.9 2.4 %collective-permute-done.33.last_x = bf16[2,512,128]{2,1,0:T(8,128)(2,1)S(1)} collective-permute-done((bf16[2,512,128]{2,1,0:T(8,128)(2,1)S(1)}, bf16[2,512,128]{2,1,0:T(8,128)(2,1)S(1)}, u32[]{:S(2)}, u32[]{:S(2)}) %collective-permute-start.33) | collective-permute-done | bytes 262176 | tf_op jit(solution)/shard_map/ppermute | solution.py:255
  151.6 1.0 finish.7
  (82 shorter events, 10.9 us)
Async XLA Ops:
  0.6 1.0 copy-start.6
  1.7 1.0 copy-start.7
  2.7 7.5 %copy-start.8 = (bf16[1024,2,128]{2,1,0:T(2,128)(2,1)S(1)}, bf16[1024,2,128]{2,1,0:T(2,128)(2,1)}, u32[]{:S(2)}) copy-start(bf16[1024,2,128]{2,1,0:T(2,128)(2,1)} %param.10) | copy-start | bytes 1572868
  4.1 6.4 %copy-start.4 = (bf16[2,2,128,512]{3,2,1,0:T(8,128)(2,1)}, bf16[2,2,128,512]{3,2,1,0:T(8,128)(2,1)S(1)}, u32[]{:S(2)}) copy-start(bf16[2,2,128,512]{3,2,1,0:T(8,128)(2,1)S(1)} %get-tuple-element.168.refs_0_) | copy-start | bytes 1572868
  4.1 19.8 %collective-permute-start.2 = (bf16[1,2,128,512]{3,2,1,0:T(8,128)(2,1)}, bf16[1,2,128,512]{3,2,1,0:T(8,128)(2,1)}, u32[]{:S(2)}, u32[]{:S(2)}) collective-permute-start(bf16[1,2,128,512]{3,2,1,0:T(8,128)(2,1)} %get-tuple-element.118.refs_0_), channel_id=1, source_target_pairs={{0,6},{1,7},{2,0},{3,1},{4,2},{5,3},{6,4},{7,5},{8,14},{9,15},{10,... | collective-permute-start | bytes 786440 | tf_op jit(solution)/shard_map/ppermute | solution.py:260
  9.1 14.7 %collective-permute-start.1 = (bf16[1,2,128,512]{3,2,1,0:T(8,128)(2,1)}, bf16[1,2,128,512]{3,2,1,0:T(8,128)(2,1)}, u32[]{:S(2)}, u32[]{:S(2)}) collective-permute-start(bf16[1,2,128,512]{3,2,1,0:T(8,128)(2,1)} %get-tuple-element.118.refs_0_), channel_id=1, source_target_pairs={{0,2},{1,3},{2,4},{3,5},{4,6},{5,7},{6,0},{7,1},{8,10},{9,11},{10,... | collective-permute-start | bytes 786440 | tf_op jit(solution)/shard_map/ppermute | solution.py:260
  9.1 30.9 %collective-permute-start.3 = (bf16[4,2,128,512]{3,2,1,0:T(8,128)(2,1)}, bf16[4,2,128,512]{3,2,1,0:T(8,128)(2,1)S(1)}, u32[]{:S(2)}, u32[]{:S(2)}) collective-permute-start(bf16[4,2,128,512]{3,2,1,0:T(8,128)(2,1)} %get-tuple-element.107), channel_id=1, source_target_pairs={{0,1},{1,0},{2,3},{3,2},{4,5},{5,4},{6,7},{7,6},{8,9},{9,8},{10,11... | collective-permute-start | bytes 3145736 | tf_op jit(solution)/shard_map/ppermute | solution.py:264
  10.3 5.0 %copy-start.9 = (s32[64]{0:T(128)S(1)}, s32[64]{0:T(128)}, u32[]{:S(2)}) copy-start(s32[64]{0:T(128)} %param.11) | copy-start | bytes 772
  10.4 5.8 %copy-start = (bf16[1024,1024]{1,0:T(8,128)(2,1)S(1)}, bf16[1024,1024]{1,0:T(8,128)(2,1)}, u32[]{:S(2)}) copy-start(bf16[1024,1024]{1,0:T(8,128)(2,1)} %q_ref.3) | copy-start | bytes 6291460
  11.3 1.0 copy-start.2
  12.3 11.5 %collective-permute-start = (bf16[224,512]{1,0:T(8,128)(2,1)}, bf16[224,512]{1,0:T(8,128)(2,1)}, u32[]{:S(2)}, u32[]{:S(2)}) collective-permute-start(bf16[224,512]{1,0:T(8,128)(2,1)} %slice.92), channel_id=1, source_target_pairs={{0,1},{1,2},{2,3},{3,4},{4,5},{5,6},{6,7},{8,9},{9,10},{10,11},{11... | collective-permute-start | bytes 688136 | tf_op jit(solution)/shard_map/ppermute | solution.py:337
  16.2 1.6 %copy-start.1 = (bf16[1024,1024]{1,0:T(8,128)(2,1)S(1)}, bf16[1024,1024]{1,0:T(8,128)(2,1)}, u32[]{:S(2)}) copy-start(bf16[1024,1024]{1,0:T(8,128)(2,1)} %qt_ref.3) | copy-start | bytes 6291460
  17.8 1.2 copy-start.3
  19.1 8.8 %slice-start = ((bf16[1024,512]{1,0:T(8,128)(2,1)}), bf16[512,512]{1,0:T(8,128)(2,1)S(1)}, s32[]{:S(2)}) async-start(bf16[1024,512]{1,0:T(8,128)(2,1)} %copy-done.2), calls=%async_computation | async-start | bytes 1048576 | tf_op jit(solution)/shard_map/slice | solution.py:395
  23.9 9.8 %collective-permute-start.6 = (bf16[1,2,128,512]{3,2,1,0:T(8,128)(2,1)}, bf16[1,2,128,512]{3,2,1,0:T(8,128)(2,1)S(1)}, u32[]{:S(2)}, u32[]{:S(2)}) collective-permute-start(bf16[1,2,128,512]{3,2,1,0:T(8,128)(2,1)} %collective-permute-done.2.refs_6_), channel_id=1, source_target_pairs={{0,1},{1,0},{2,3},{3,2},{4,5},{5,4},{6,7},{7,6},{8,9},{9,8},{10,11... | collective-permute-start | bytes 786440 | tf_op jit(solution)/shard_map/ppermute | solution.py:264
  23.9 11.0 %collective-permute-start.7 = (bf16[1,2,128,512]{3,2,1,0:T(8,128)(2,1)S(1)}, bf16[1,2,128,512]{3,2,1,0:T(8,128)(2,1)S(1)}, u32[]{:S(2)}, u32[]{:S(2)}) collective-permute-start(bf16[1,2,128,512]{3,2,1,0:T(8,128)(2,1)S(1)} %get-tuple-element.142.refs_0_), channel_id=1, source_target_pairs={{0,2},{1,3},{2,4},{3,5},{4,6},{5,7},{6,0},{7,1},{8,10},{9,11},{10,... | collective-permute-start | bytes 786440 | tf_op jit(solution)/shard_map/ppermute | solution.py:260
  25.7 9.2 %collective-permute-start.5 = (bf16[1,2,128,512]{3,2,1,0:T(8,128)(2,1)}, bf16[1,2,128,512]{3,2,1,0:T(8,128)(2,1)S(1)}, u32[]{:S(2)}, u32[]{:S(2)}) collective-permute-start(bf16[1,2,128,512]{3,2,1,0:T(8,128)(2,1)} %collective-permute-done.1.refs_2_), channel_id=1, source_target_pairs={{0,1},{1,0},{2,3},{3,2},{4,5},{5,4},{6,7},{7,6},{8,9},{9,8},{10,11... | collective-permute-start | bytes 786440 | tf_op jit(solution)/shard_map/ppermute | solution.py:264
  25.9 14.2 %collective-permute-start.4 = (bf16[1,2,128,512]{3,2,1,0:T(8,128)(2,1)}, bf16[1,2,128,512]{3,2,1,0:T(8,128)(2,1)S(1)}, u32[]{:S(2)}, u32[]{:S(2)}) collective-permute-start(bf16[1,2,128,512]{3,2,1,0:T(8,128)(2,1)} %collective-permute-done.1.refs_2_), channel_id=1, source_target_pairs={{0,2},{1,3},{2,4},{3,5},{4,6},{5,7},{6,0},{7,1},{8,10},{9,11},{10,... | collective-permute-start | bytes 786440 | tf_op jit(solution)/shard_map/ppermute | solution.py:260
  40.1 4.3 %collective-permute-start.13 = (bf16[1,2,128,512]{3,2,1,0:T(8,128)(2,1)S(1)}, bf16[1,2,128,512]{3,2,1,0:T(8,128)(2,1)S(1)}, u32[]{:S(2)}, u32[]{:S(2)}) collective-permute-start(bf16[1,2,128,512]{3,2,1,0:T(8,128)(2,1)S(1)} %collective-permute-done.4.refs_4_), channel_id=1, source_target_pairs={{0,1},{1,0},{2,3},{3,2},{4,5},{5,4},{6,7},{7,6},{8,9},{9,8},{10,11... | collective-permute-start | bytes 786440 | tf_op jit(solution)/shard_map/ppermute | solution.py:264
  40.1 14.3 %collective-permute-start.12 = (bf16[1,2,128,512]{3,2,1,0:T(8,128)(2,1)S(1)}, bf16[1,2,128,512]{3,2,1,0:T(8,128)(2,1)S(1)}, u32[]{:S(2)}, u32[]{:S(2)}) collective-permute-start(bf16[1,2,128,512]{3,2,1,0:T(8,128)(2,1)S(1)} %collective-permute-done.7.refs_2_), channel_id=1, source_target_pairs={{0,1},{1,0},{2,3},{3,2},{4,5},{5,4},{6,7},{7,6},{8,9},{9,8},{10,11... | collective-permute-start | bytes 786440 | tf_op jit(solution)/shard_map/ppermute | solution.py:264
  40.6 13.8 %collective-permute-start.10 = (bf16[1,2,128,512]{3,2,1,0:T(8,128)(2,1)S(1)}, bf16[1,2,128,512]{3,2,1,0:T(8,128)(2,1)S(1)}, u32[]{:S(2)}, u32[]{:S(2)}) collective-permute-start(bf16[1,2,128,512]{3,2,1,0:T(8,128)(2,1)S(1)} %collective-permute-done.7.refs_2_), channel_id=1, source_target_pairs={{0,2},{1,3},{2,4},{3,5},{4,6},{5,7},{6,0},{7,1},{8,10},{9,11},{10,... | collective-permute-start | bytes 786440 | tf_op jit(solution)/shard_map/ppermute | solution.py:260
  40.6 13.8 %collective-permute-start.11 = (bf16[1,2,128,512]{3,2,1,0:T(8,128)(2,1)S(1)}, bf16[1,2,128,512]{3,2,1,0:T(8,128)(2,1)S(1)}, u32[]{:S(2)}, u32[]{:S(2)}) collective-permute-start(bf16[1,2,128,512]{3,2,1,0:T(8,128)(2,1)S(1)} %get-tuple-element.142.refs_0_), channel_id=1, source_target_pairs={{0,6},{1,7},{2,0},{3,1},{4,2},{5,3},{6,4},{7,5},{8,14},{9,15},{10,... | collective-permute-start | bytes 786440 | tf_op jit(solution)/shard_map/ppermute | solution.py:260
  49.9 16.9 %copy-start.5 = (bf16[2,2,128,512]{3,2,1,0:T(8,128)(2,1)S(1)}, bf16[2,2,128,512]{3,2,1,0:T(8,128)(2,1)}, u32[]{:S(2)}) copy-start(bf16[2,2,128,512]{3,2,1,0:T(8,128)(2,1)} %copy-done.4) | copy-start | bytes 1572868
  49.9 13.3 %collective-permute-start.16 = (bf16[2,512,256]{2,1,0:T(8,128)(2,1)S(1)}, bf16[2,512,256]{2,1,0:T(8,128)(2,1)S(1)}, u32[]{:S(2)}, u32[]{:S(2)}) collective-permute-start(bf16[2,512,256]{2,1,0:T(8,128)(2,1)S(1)} %get-tuple-element.136), channel_id=1, source_target_pairs={{0,8},{8,0},{16,24},{24,16},{1,9},{9,1},{17,25},{25,17},{2,10},{10... | collective-permute-start | bytes 1572872 | tf_op jit(solution)/shard_map/ppermute | solution.py:255
  51.5 13.0 %collective-permute-start.17 = (bf16[2,512,256]{2,1,0:T(8,128)(2,1)S(1)}, bf16[2,512,256]{2,1,0:T(8,128)(2,1)S(1)}, u32[]{:S(2)}, u32[]{:S(2)}) collective-permute-start(bf16[2,512,256]{2,1,0:T(8,128)(2,1)S(1)} %get-tuple-element.127), channel_id=1, source_target_pairs={{0,16},{8,24},{16,0},{24,8},{1,17},{9,25},{17,1},{25,9},{2,18},{10... | collective-permute-start | bytes 1572872 | tf_op jit(solution)/shard_map/ppermute | solution.py:255
  54.4 1.5 %collective-permute-start.14 = (bf16[1,2,128,512]{3,2,1,0:T(8,128)(2,1)S(1)}, bf16[1,2,128,512]{3,2,1,0:T(8,128)(2,1)S(1)}, u32[]{:S(2)}, u32[]{:S(2)}) collective-permute-start(bf16[1,2,128,512]{3,2,1,0:T(8,128)(2,1)S(1)} %collective-permute-done.10.refs_4_), channel_id=1, source_target_pairs={{0,1},{1,0},{2,3},{3,2},{4,5},{5,4},{6,7},{7,6},{8,9},{9,8},{10,11... | collective-permute-start | bytes 786440 | tf_op jit(solution)/shard_map/ppermute | solution.py:264
  54.4 1.9 %collective-permute-start.15 = (bf16[1,2,128,512]{3,2,1,0:T(8,128)(2,1)S(1)}, bf16[1,2,128,512]{3,2,1,0:T(8,128)(2,1)S(1)}, u32[]{:S(2)}, u32[]{:S(2)}) collective-permute-start(bf16[1,2,128,512]{3,2,1,0:T(8,128)(2,1)S(1)} %collective-permute-done.11.refs_6_), channel_id=1, source_target_pairs={{0,1},{1,0},{2,3},{3,2},{4,5},{5,4},{6,7},{7,6},{8,9},{9,8},{10,11... | collective-permute-start | bytes 786440 | tf_op jit(solution)/shard_map/ppermute | solution.py:264
  64.5 8.8 %collective-permute-start.19 = (bf16[2,512,128]{2,1,0:T(8,128)(2,1)S(1)}, bf16[2,512,128]{2,1,0:T(8,128)(2,1)S(1)}, u32[]{:S(2)}, u32[]{:S(2)}) collective-permute-start(bf16[2,512,128]{2,1,0:T(8,128)(2,1)S(1)} %add_convert_fusion.6), channel_id=1, source_target_pairs={{0,8},{8,0},{16,24},{24,16},{1,9},{9,1},{17,25},{25,17},{2,10},{10... | collective-permute-start | bytes 786440 | tf_op jit(solution)/shard_map/ppermute | solution.py:255
  65.2 8.2 %collective-permute-start.18 = (bf16[2,512,128]{2,1,0:T(8,128)(2,1)S(1)}, bf16[2,512,128]{2,1,0:T(8,128)(2,1)S(1)}, u32[]{:S(2)}, u32[]{:S(2)}) collective-permute-start(bf16[2,512,128]{2,1,0:T(8,128)(2,1)S(1)} %add_convert_fusion.7), channel_id=1, source_target_pairs={{0,16},{8,24},{16,0},{24,8},{1,17},{9,25},{17,1},{25,9},{2,18},{10... | collective-permute-start | bytes 786440 | tf_op jit(solution)/shard_map/ppermute | solution.py:255
  66.8 22.8 %collective-permute-start.9 = (bf16[2,2,128,512]{3,2,1,0:T(8,128)(2,1)S(1)}, bf16[2,2,128,512]{3,2,1,0:T(8,128)(2,1)S(1)}, u32[]{:S(2)}, u32[]{:S(2)}) collective-permute-start(bf16[2,2,128,512]{3,2,1,0:T(8,128)(2,1)S(1)} %copy-done.5), channel_id=1, source_target_pairs={{0,6},{1,7},{2,0},{3,1},{4,2},{5,3},{6,4},{7,5},{8,14},{9,15},{10,... | collective-permute-start | bytes 1572872 | tf_op jit(solution)/shard_map/ppermute | solution.py:260
  67.1 22.5 %collective-permute-start.8 = (bf16[2,2,128,512]{3,2,1,0:T(8,128)(2,1)S(1)}, bf16[2,2,128,512]{3,2,1,0:T(8,128)(2,1)S(1)}, u32[]{:S(2)}, u32[]{:S(2)}) collective-permute-start(bf16[2,2,128,512]{3,2,1,0:T(8,128)(2,1)S(1)} %copy-done.5), channel_id=1, source_target_pairs={{0,2},{1,3},{2,4},{3,5},{4,6},{5,7},{6,0},{7,1},{8,10},{9,11},{10,... | collective-permute-start | bytes 1572872 | tf_op jit(solution)/shard_map/ppermute | solution.py:260
  73.4 18.4 %collective-permute-start.23 = (bf16[2,512,256]{2,1,0:T(8,128)(2,1)S(1)}, bf16[2,512,256]{2,1,0:T(8,128)(2,1)S(1)}, u32[]{:S(2)}, u32[]{:S(2)}) collective-permute-start(bf16[2,512,256]{2,1,0:T(8,128)(2,1)S(1)} %get-tuple-element.156), channel_id=1, source_target_pairs={{0,8},{8,0},{16,24},{24,16},{1,9},{9,1},{17,25},{25,17},{2,10},{10... | collective-permute-start | bytes 1572872 | tf_op jit(solution)/shard_map/ppermute | solution.py:255
  74.9 16.8 %collective-permute-start.24 = (bf16[2,512,256]{2,1,0:T(8,128)(2,1)S(1)}, bf16[2,512,256]{2,1,0:T(8,128)(2,1)S(1)}, u32[]{:S(2)}, u32[]{:S(2)}) collective-permute-start(bf16[2,512,256]{2,1,0:T(8,128)(2,1)S(1)} %get-tuple-element.151), channel_id=1, source_target_pairs={{0,16},{8,24},{16,0},{24,8},{1,17},{9,25},{17,1},{25,9},{2,18},{10... | collective-permute-start | bytes 1572872 | tf_op jit(solution)/shard_map/ppermute | solution.py:255
  89.5 2.3 %collective-permute-start.22 = (bf16[2,2,128,512]{3,2,1,0:T(8,128)(2,1)S(1)}, bf16[2,2,128,512]{3,2,1,0:T(8,128)(2,1)S(1)}, u32[]{:S(2)}, u32[]{:S(2)}) collective-permute-start(bf16[2,2,128,512]{3,2,1,0:T(8,128)(2,1)S(1)} %collective-permute-done.9.refs_6_), channel_id=1, source_target_pairs={{0,1},{1,0},{2,3},{3,2},{4,5},{5,4},{6,7},{7,6},{8,9},{9,8},{10,11... | collective-permute-start | bytes 1572872 | tf_op jit(solution)/shard_map/ppermute | solution.py:264
  89.6 2.7 %collective-permute-start.21 = (bf16[2,2,128,512]{3,2,1,0:T(8,128)(2,1)S(1)}, bf16[2,2,128,512]{3,2,1,0:T(8,128)(2,1)S(1)}, u32[]{:S(2)}, u32[]{:S(2)}) collective-permute-start(bf16[2,2,128,512]{3,2,1,0:T(8,128)(2,1)S(1)} %collective-permute-done.8.refs_2_), channel_id=1, source_target_pairs={{0,1},{1,0},{2,3},{3,2},{4,5},{5,4},{6,7},{7,6},{8,9},{9,8},{10,11... | collective-permute-start | bytes 1572872 | tf_op jit(solution)/shard_map/ppermute | solution.py:264
  90.1 15.6 %collective-permute-start.20 = (bf16[2,2,128,512]{3,2,1,0:T(8,128)(2,1)S(1)}, bf16[2,2,128,512]{3,2,1,0:T(8,128)(2,1)S(1)}, u32[]{:S(2)}, u32[]{:S(2)}) collective-permute-start(bf16[2,2,128,512]{3,2,1,0:T(8,128)(2,1)S(1)} %collective-permute-done.8.refs_2_), channel_id=1, source_target_pairs={{0,2},{1,3},{2,4},{3,5},{4,6},{5,7},{6,0},{7,1},{8,10},{9,11},{10,... | collective-permute-start | bytes 1572872 | tf_op jit(solution)/shard_map/ppermute | solution.py:260
  105.7 2.0 %collective-permute-start.25 = (bf16[2,2,128,512]{3,2,1,0:T(8,128)(2,1)S(1)}, bf16[2,2,128,512]{3,2,1,0:T(8,128)(2,1)S(1)}, u32[]{:S(2)}, u32[]{:S(2)}) collective-permute-start(bf16[2,2,128,512]{3,2,1,0:T(8,128)(2,1)S(1)} %collective-permute-done.20.refs_4_), channel_id=1, source_target_pairs={{0,1},{1,0},{2,3},{3,2},{4,5},{5,4},{6,7},{7,6},{8,9},{9,8},{10,11... | collective-permute-start | bytes 1572872 | tf_op jit(solution)/shard_map/ppermute | solution.py:264
  105.7 8.7 %collective-permute-start.27 = (bf16[2,512,128]{2,1,0:T(8,128)(2,1)S(1)}, bf16[2,512,128]{2,1,0:T(8,128)(2,1)S(1)}, u32[]{:S(2)}, u32[]{:S(2)}) collective-permute-start(bf16[2,512,128]{2,1,0:T(8,128)(2,1)S(1)} %add_convert_fusion.4), channel_id=1, source_target_pairs={{0,8},{8,0},{16,24},{24,16},{1,9},{9,1},{17,25},{25,17},{2,10},{10... | collective-permute-start | bytes 786440 | tf_op jit(solution)/shard_map/ppermute | solution.py:255
  107.2 8.4 %collective-permute-start.26 = (bf16[2,512,128]{2,1,0:T(8,128)(2,1)S(1)}, bf16[2,512,128]{2,1,0:T(8,128)(2,1)S(1)}, u32[]{:S(2)}, u32[]{:S(2)}) collective-permute-start(bf16[2,512,128]{2,1,0:T(8,128)(2,1)S(1)} %add_convert_fusion.5), channel_id=1, source_target_pairs={{0,16},{8,24},{16,0},{24,8},{1,17},{9,25},{17,1},{25,9},{2,18},{10... | collective-permute-start | bytes 786440 | tf_op jit(solution)/shard_map/ppermute | solution.py:255
  115.6 14.9 %collective-permute-start.30 = (bf16[2,512,256]{2,1,0:T(8,128)(2,1)S(1)}, bf16[2,512,256]{2,1,0:T(8,128)(2,1)S(1)}, u32[]{:S(2)}, u32[]{:S(2)}) collective-permute-start(bf16[2,512,256]{2,1,0:T(8,128)(2,1)S(1)} %get-tuple-element.185), channel_id=1, source_target_pairs={{0,8},{8,0},{16,24},{24,16},{1,9},{9,1},{17,25},{25,17},{2,10},{10... | collective-permute-start | bytes 1572872 | tf_op jit(solution)/shard_map/ppermute | solution.py:255
  116.2 14.9 %collective-permute-start.31 = (bf16[2,512,256]{2,1,0:T(8,128)(2,1)S(1)}, bf16[2,512,256]{2,1,0:T(8,128)(2,1)S(1)}, u32[]{:S(2)}, u32[]{:S(2)}) collective-permute-start(bf16[2,512,256]{2,1,0:T(8,128)(2,1)S(1)} %get-tuple-element.176), channel_id=1, source_target_pairs={{0,16},{8,24},{16,0},{24,8},{1,17},{9,25},{17,1},{25,9},{2,18},{10... | collective-permute-start | bytes 1572872 | tf_op jit(solution)/shard_map/ppermute | solution.py:255
  121.2 20.5 %collective-permute-start.28 = (bf16[2,512,256]{2,1,0:T(8,128)(2,1)S(1)}, bf16[2,512,256]{2,1,0:T(8,128)(2,1)S(1)}, u32[]{:S(2)}, u32[]{:S(2)}) collective-permute-start(bf16[2,512,256]{2,1,0:T(8,128)(2,1)S(1)} %get-tuple-element.182), channel_id=1, source_target_pairs={{0,8},{8,0},{16,24},{24,16},{1,9},{9,1},{17,25},{25,17},{2,10},{10... | collective-permute-start | bytes 1572872 | tf_op jit(solution)/shard_map/ppermute | solution.py:255
  122.7 19.5 %collective-permute-start.29 = (bf16[2,512,256]{2,1,0:T(8,128)(2,1)S(1)}, bf16[2,512,256]{2,1,0:T(8,128)(2,1)S(1)}, u32[]{:S(2)}, u32[]{:S(2)}) collective-permute-start(bf16[2,512,256]{2,1,0:T(8,128)(2,1)S(1)} %get-tuple-element.183), channel_id=1, source_target_pairs={{0,16},{8,24},{16,0},{24,8},{1,17},{9,25},{17,1},{25,9},{2,18},{10... | collective-permute-start | bytes 1572872 | tf_op jit(solution)/shard_map/ppermute | solution.py:255
  131.1 16.2 %collective-permute-start.35 = (bf16[2,512,128]{2,1,0:T(8,128)(2,1)S(1)}, bf16[2,512,128]{2,1,0:T(8,128)(2,1)S(1)}, u32[]{:S(2)}, u32[]{:S(2)}) collective-permute-start(bf16[2,512,128]{2,1,0:T(8,128)(2,1)S(1)} %add_convert_fusion.2), channel_id=1, source_target_pairs={{0,8},{8,0},{16,24},{24,16},{1,9},{9,1},{17,25},{25,17},{2,10},{10... | collective-permute-start | bytes 786440 | tf_op jit(solution)/shard_map/ppermute | solution.py:255
  132.7 15.2 %collective-permute-start.34 = (bf16[2,512,128]{2,1,0:T(8,128)(2,1)S(1)}, bf16[2,512,128]{2,1,0:T(8,128)(2,1)S(1)}, u32[]{:S(2)}, u32[]{:S(2)}) collective-permute-start(bf16[2,512,128]{2,1,0:T(8,128)(2,1)S(1)} %add_convert_fusion.3), channel_id=1, source_target_pairs={{0,16},{8,24},{16,0},{24,8},{1,17},{9,25},{17,1},{25,9},{2,18},{10... | collective-permute-start | bytes 786440 | tf_op jit(solution)/shard_map/ppermute | solution.py:255
  142.3 9.0 %collective-permute-start.33 = (bf16[2,512,128]{2,1,0:T(8,128)(2,1)S(1)}, bf16[2,512,128]{2,1,0:T(8,128)(2,1)S(1)}, u32[]{:S(2)}, u32[]{:S(2)}) collective-permute-start(bf16[2,512,128]{2,1,0:T(8,128)(2,1)S(1)} %add_convert_fusion), channel_id=1, source_target_pairs={{0,8},{8,0},{16,24},{24,16},{1,9},{9,1},{17,25},{25,17},{2,10},{10... | collective-permute-start | bytes 786440 | tf_op jit(solution)/shard_map/ppermute | solution.py:255
  143.9 7.7 %collective-permute-start.32 = (bf16[2,512,128]{2,1,0:T(8,128)(2,1)S(1)}, bf16[2,512,128]{2,1,0:T(8,128)(2,1)S(1)}, u32[]{:S(2)}, u32[]{:S(2)}) collective-permute-start(bf16[2,512,128]{2,1,0:T(8,128)(2,1)S(1)} %add_convert_fusion.1), channel_id=1, source_target_pairs={{0,16},{8,24},{16,0},{24,8},{1,17},{9,25},{17,1},{25,9},{2,18},{10... | collective-permute-start | bytes 786440 | tf_op jit(solution)/shard_map/ppermute | solution.py:255

commit v6 on v5

v6 whole, which is shorter than its diff:
```python
import functools
import math

import jax
import jax.numpy as jnp
from jax import lax
from jax.experimental import pallas as pl
from jax.experimental.pallas import tpu as pltpu
from jax.sharding import PartitionSpec as P

STRETCH = 32
WINDOW = 224
CHUNKS = 4
TILE = 128
CORES = 2

masked_score = -1e30
vmem_bytes = 16 * 1024 * 1024


def arrange_kernel(owners, tangent_ref, value_ref, whole_ref, *chunk_refs):
    columns = tangent_ref.shape[1] // owners
    part = columns // len(chunk_refs)
    for chunk, chunk_ref in enumerate(chunk_refs):
        for owner in range(owners):
            of = slice(owner * columns + chunk * part, owner * columns + (chunk + 1) * part)
            to = slice(owner * part, (owner + 1) * part)
            for mat, ref in enumerate((tangent_ref, value_ref)):
                whole_ref[chunk, mat, :, to] = ref[:, of]
                chunk_ref[mat, :, to] = ref[:, of]


def arrange(owners, tangent, value):
    rows, columns = value.shape
    chunk = (2, rows, columns // CHUNKS)
    shapes = [jax.ShapeDtypeStruct(shape, value.dtype) for shape in [(CHUNKS, *chunk)] + [chunk] * CHUNKS]
    return pl.pallas_call(
        functools.partial(arrange_kernel, owners),
        in_specs=[pl.BlockSpec(memory_space=pltpu.VMEM)] * 2,
        out_specs=[pl.BlockSpec(memory_space=pltpu.VMEM)] * len(shapes),
        out_shape=shapes,
        compiler_params=pltpu.CompilerParams(vmem_limit_bytes=vmem_bytes),
        name="arrange",
    )(tangent, value)


def attention_kernel(heads, head_dim, offset, order_ref, q_ref, qt_ref, ctx_ref, low_ref, out_ref):
    rows = q_ref.shape[0]
    span = WINDOW + STRETCH
    width = heads * head_dim
    score_scale = 1.0 / math.sqrt(head_dim)
    to_log2 = score_scale * math.log2(math.e)
    step = pl.program_id(0)
    transposed = (((1,), (1,)), ((), ()))
    column = lax.broadcasted_iota(jnp.int32, (STRETCH, span), 1)
    row = lax.broadcasted_iota(jnp.int32, (STRETCH, span), 0)
    causal = column <= row + WINDOW
    starts = [pl.multiple_of(order_ref[h] * head_dim, head_dim) for h in range(heads)]

    def window(part):
        return pl.ds(pl.multiple_of(offset + step * rows + part * STRETCH, STRETCH), span)

    def score(part):
        here = slice(part * STRETCH, (part + 1) * STRETCH)
        keys = ctx_ref[window(part), : 2 * head_dim]
        q = jnp.concatenate([q_ref[here, pl.ds(start, head_dim)] for start in starts], axis=0)
        qt = jnp.concatenate([qt_ref[here, pl.ds(start, head_dim)] for start in starts], axis=0)
        scores = lax.dot_general(
            q, keys[:, :head_dim], transposed, preferred_element_type=jnp.float32
        )
        tangent = lax.dot_general(
            jnp.concatenate([qt, q], axis=1), keys, transposed, preferred_element_type=jnp.float32
        )
        return scores.reshape(heads, STRETCH, span), tangent.reshape(heads, STRETCH, span)

    def weigh(part, scores, tangent):
        low = low_ref[part * STRETCH : (part + 1) * STRETCH, :]
        low = jnp.concatenate([low] * (span // low.shape[1]), axis=1)
        admitted = causal & (column >= low)
        scores = jnp.where(admitted[None], scores, masked_score)
        peak = jnp.max(scores, axis=-1, keepdims=True)
        exponent = jnp.exp2((scores - peak) * to_log2)
        inverse = 1.0 / jnp.sum(exponent, axis=-1, keepdims=True)
        mean = jnp.sum(exponent * tangent, axis=-1, keepdims=True) * inverse
        prob = exponent * inverse
        prob_low = prob.astype(jnp.bfloat16).reshape(heads * STRETCH, span)
        tan_low = (prob * ((tangent - mean) * score_scale)).astype(jnp.bfloat16)
        return prob_low, tan_low.reshape(heads * STRETCH, span)

    def gather_values(part, prob_low, tan_low):
        here = slice(part * STRETCH, (part + 1) * STRETCH)
        values = ctx_ref[window(part), 2 * head_dim :]
        both = jnp.dot(prob_low, values, preferred_element_type=jnp.float32)
        more = jnp.dot(tan_low, values[:, :head_dim], preferred_element_type=jnp.float32)
        out = both[:, :head_dim].astype(jnp.bfloat16)
        out_tan = (both[:, head_dim:] + more).astype(jnp.bfloat16)
        for h in range(heads):
            of = slice(h * STRETCH, (h + 1) * STRETCH)
            out_ref[here, h * head_dim : (h + 1) * head_dim] = out[of]
            out_ref[here, width + h * head_dim : width + (h + 1) * head_dim] = out_tan[of]

    parts = rows // STRETCH
    scored, weighed = score(0), None
    for part in range(parts):
        following = score(part + 1) if part + 1 < parts else None
        if weighed is not None:
            gather_values(part - 1, *weighed)
        weighed = weigh(part, *scored)
        scored = following
    gather_values(parts - 1, *weighed)


def attention(half, order, queries, query_tangent, context, low):
    tokens, width = queries.shape[0] // 2, queries.shape[1]
    head_dim = context.shape[1] // 4
    heads = width // head_dim
    elements = tokens * heads * (WINDOW + STRETCH)
    steps = tokens // TILE
    offset = context.shape[0] - tokens - WINDOW
    return pl.pallas_call(
        functools.partial(attention_kernel, heads, head_dim, offset),
        grid=(steps,),
        in_specs=[
            pl.BlockSpec(memory_space=pltpu.SMEM),
            pl.BlockSpec((TILE, width), lambda i: (half * steps + i, 0)),
            pl.BlockSpec((TILE, width), lambda i: (half * steps + i, 0)),
            pl.BlockSpec(context.shape, lambda i: (0, 0)),
            pl.BlockSpec((TILE, low.shape[1]), lambda i: (half * steps + i, 0)),
        ],
        out_specs=pl.BlockSpec((TILE, 2 * width), lambda i: (i, 0)),
        out_shape=jax.ShapeDtypeStruct((tokens, 2 * width), jnp.bfloat16),
        compiler_params=pltpu.CompilerParams(vmem_limit_bytes=vmem_bytes),
        cost_estimate=pl.CostEstimate(
            flops=elements, bytes_accessed=tokens, transcendentals=0
        ),
        name="attention",
    )(order, queries, query_tangent, context, low)


def project_kernel(chunk, first_ref, second_ref, whole_ref, *refs):
    *piece_refs, send_ref, weight_ref, sems = refs
    step, steps = pl.program_id(0), pl.num_programs(0)
    rows = whole_ref.shape[2]
    depth = weight_ref.shape[1]
    owners, _, _, part = send_ref.shape
    sources = [piece_refs[0], whole_ref.at[chunk], *piece_refs[1:]]

    @pl.when(step == 0)
    def _():
        copies = []
        for place, source in enumerate(sources):
            to = weight_ref.at[:, pl.ds(place * rows, rows), :]
            copies.append(pltpu.make_async_copy(source, to, sems.at[place]))
            copies[-1].start()
        for copy in copies:
            copy.wait()

    def run(pair_ref):
        dot = functools.partial(jnp.dot, preferred_element_type=jnp.float32)
        value = dot(pair_ref[:, :depth], weight_ref[1])
        tangent = dot(pair_ref[:, :depth], weight_ref[0]) + dot(pair_ref[:, depth:], weight_ref[1])
        for owner in range(owners):
            of = slice(owner * part, (owner + 1) * part)
            send_ref[owner, 0] = value[:, of].astype(send_ref.dtype)
            send_ref[owner, 1] = tangent[:, of].astype(send_ref.dtype)

    @pl.when(step < steps // 2)
    def _():
        run(first_ref)

    @pl.when(step >= steps // 2)
    def _():
        run(second_ref)


def project(owners, chunk, pairs, whole, pieces):
    tokens, width = pairs[0].shape
    tile = min(2 * TILE, tokens)
    steps = tokens // tile
    _, rows, columns = pieces[0].shape
    part = columns // owners
    count = len(pieces) + 1
    return pl.pallas_call(
        functools.partial(project_kernel, chunk),
        grid=(2 * steps,),
        in_specs=[
            pl.BlockSpec((tile, width), lambda i: (jnp.minimum(i, steps - 1), 0)),
            pl.BlockSpec((tile, width), lambda i: (jnp.maximum(i - steps, 0), 0)),
            *[pl.BlockSpec(memory_space=pl.ANY)] * count,
        ],
        out_specs=pl.BlockSpec((owners, 2, tile, part), lambda i: (0, 0, i, 0)),
        out_shape=jax.ShapeDtypeStruct((owners, 2, 2 * tokens, part), jnp.bfloat16),
        scratch_shapes=[
            pltpu.VMEM((2, rows * count, columns), jnp.bfloat16),
            pltpu.SemaphoreType.DMA((count,)),
        ],
        compiler_params=pltpu.CompilerParams(vmem_limit_bytes=vmem_bytes),
        cost_estimate=pl.CostEstimate(
            flops=tokens * columns, bytes_accessed=tokens, transcendentals=0
        ),
        name="project",
    )(*pairs, whole, *pieces)


def finish_kernel(parts_ref, *refs):
    for mat, ref in enumerate(refs[-2:]):
        total = parts_ref[0, mat].astype(jnp.float32)
        for owner in range(1, parts_ref.shape[0]):
            total = total + parts_ref[owner, mat]
        ref[...] = total.astype(ref.dtype)


def finish(chunk, outputs, parts):
    owners, _, tokens, part = parts.shape
    shape = jax.ShapeDtypeStruct((tokens, part * CHUNKS), jnp.bfloat16)
    tile = tokens // 2
    return pl.pallas_call(
        finish_kernel,
        grid=(tokens // tile,),
        in_specs=[
            pl.BlockSpec((owners, 2, tile, part), lambda i: (0, 0, i, 0)),
            *[pl.BlockSpec(memory_space=pl.ANY)] * len(outputs),
        ],
        out_specs=[pl.BlockSpec((tile, part), lambda i: (i, chunk))] * 2,
        out_shape=[shape, shape],
        input_output_aliases={1 + i: i for i in range(len(outputs))},
        compiler_params=pltpu.CompilerParams(vmem_limit_bytes=vmem_bytes),
        name="finish",
    )(parts, *outputs)


def along(block, chips):
    size = lax.axis_size("seq")
    return lax.ppermute(block, "seq", [(i, (i + CORES * chips) % size) for i in range(size)])


def other_core(block):
    return lax.ppermute(block, "seq", [(i, i ^ 1) for i in range(lax.axis_size("seq"))])


def together(*trees):
    return lax.optimization_barrier(trees)


class Gather:
    def __init__(self, mine, chips):
        self.blocks = {0: mine}
        self.others = {}
        self.chips = chips
        self.forward, self.backward = chips // 2, (chips - 1) // 2

    def ahead(self):
        if self.forward:
            self.blocks[1] = along(self.blocks[0], 1)

    def behind(self):
        if self.backward:
            self.blocks[self.chips - 1] = along(self.blocks[0], -1)

    def farther_ahead(self):
        for step in range(2, self.forward + 1):
            self.blocks[step] = along(self.blocks[step - 1], 1)

    def farther_behind(self):
        for step in range(2, self.backward + 1):
            self.blocks[self.chips - step] = along(self.blocks[self.chips - step + 1], -1)

    def exchange(self, *steps):
        for step in steps or range(1, self.chips):
            if step % self.chips in self.blocks and step % self.chips not in self.others:
                self.others[step % self.chips] = other_core(self.blocks[step % self.chips])

    def get(self):
        return self.blocks, self.others

    def put(self, state):
        self.blocks, self.others = (dict(part) for part in state)

    def pieces(self):
        pieces = [self.blocks[0]]
        for step in range(1, self.chips):
            pieces += [self.blocks[step], self.others[step]]
        return pieces


def body(
    queries, query_tangent, key_value, key_value_tangents, doc_lengths, out_weight, weight_tangent
):
    tokens, width = queries.shape
    head_dim = key_value.shape[2]
    heads = width // head_dim
    half = tokens // 2
    seq_index = lax.axis_index("seq")
    seq_size = lax.axis_size("seq")
    chips = seq_size // CORES

    owners = lax.axis_size("kv")
    whole, *mine = arrange(owners, weight_tangent, out_weight)
    gathers = [Gather(block, chips) for block in mine]
    gathers[0].behind()
    gathers[0].ahead()
    whole = other_core(whole)

    key_value, key_value_tangents, _ = lax.optimization_barrier(
        (key_value, key_value_tangents, mine[0])
    )
    stacked = jnp.concatenate(
        [key_value[:, 0], key_value_tangents[:, 0], key_value[:, 1], key_value_tangents[:, 1]],
        axis=1,
    )
    prior = lax.ppermute(
        stacked[tokens - WINDOW :], "seq", [(i, i + 1) for i in range(seq_size - 1)]
    )

    doc_ends = jnp.cumsum(doc_lengths)
    doc_starts = doc_ends - doc_lengths
    position = seq_index * tokens + jnp.arange(tokens, dtype=jnp.int32)
    inside = (doc_starts[None, :] <= position[:, None]) & (position[:, None] < doc_ends[None, :])
    doc_first = jnp.sum(jnp.where(inside, doc_starts[None, :], 0), axis=1)
    lower = jnp.maximum(doc_first, position - WINDOW + 1)
    low = lower - (position // STRETCH * STRETCH - WINDOW)
    low = jnp.broadcast_to(low[:, None], (tokens, 128))

    step = jnp.arange(chips, dtype=jnp.int32)
    chip, core = seq_index // CORES, seq_index % CORES
    owner = (chip - step + chips) % chips * CORES
    order = jnp.stack([owner + core, owner + 1 - core], axis=1).reshape(-1)
    whole_heads = order.shape[0] == heads

    def attend(part, context):
        heads_order = order if whole_heads else jnp.arange(heads, dtype=jnp.int32)
        pair = attention(part, heads_order, queries, query_tangent, context, low)
        if not whole_heads:
            pair = jnp.take(pair.reshape(half, 2, seq_size, -1), order, axis=2)
            pair = pair.reshape(half, 2 * width)
        return pair

    pair_second = attend(1, stacked)
    state, held, pair_second, prior = together(
        gathers[0].get(), gathers[1].blocks, pair_second, prior
    )
    gathers[0].put(state)
    gathers[1].blocks = dict(held)
    gathers[0].farther_ahead()
    gathers[0].farther_behind()
    gathers[0].exchange(1, -1)
    gathers[1].ahead()
    pair_first = attend(0, jnp.concatenate([prior, stacked[:half]], axis=0))

    pairs, sent = (pair_first, pair_second), ()
    received, outputs = [], ()
    for chunk in range(CHUNKS):
        states = [gathering.get() for gathering in gathers]
        arrived = received[chunk - 2] if chunk >= 2 else ()
        states, pairs, whole, arrived, sent = together(states, pairs, whole, arrived, sent)
        for gathering, state in zip(gathers, states):
            gathering.put(state)
        if chunk + 1 < CHUNKS:
            gathers[chunk + 1].behind()
            gathers[chunk + 1].farther_ahead()
            gathers[chunk + 1].farther_behind()
            gathers[chunk + 1].exchange(1)
        if chunk + 2 < CHUNKS:
            gathers[chunk + 2].ahead()
        gathers[chunk].exchange()
        sent = project(owners, chunk, pairs, whole, gathers[chunk].pieces())
        received.append(lax.all_to_all(sent, "kv", 0, 0, tiled=True))
        if chunk >= 2:
            outputs = finish(chunk - 2, outputs, arrived)
    for chunk in range(max(CHUNKS - 2, 0), CHUNKS):
        outputs = finish(chunk, outputs, received[chunk])
    return tuple(outputs)


def solution(mesh):
    in_specs = (
        P("seq", "kv"),
        P("seq", "kv"),
        P("seq", None, "kv"),
        P("seq", None, "kv"),
        P(),
        P(("kv", "seq"), None),
        P(("kv", "seq"), None),
    )
    out_specs = (P("seq", "kv"), P("seq", "kv"))
    return jax.shard_map(body, mesh=mesh, in_specs=in_specs, out_specs=out_specs, check_vma=False)
```

time: 153 us -> 184 us (1.20)
  local copies, waits for them, and re-layouts: 8.24 us -> 26.2 us
  waiting for transfers between devices: 69.7 us -> 79.1 us
  Pallas kernels: 34 us -> 37.1 us
    ppermute x16 -> x0, waiting for transfers between devices: 32.4 us -> none  [across(): return lax.ppermute(block, 'kv', [(i, i ^ flip) for i in range(size)])]
    ppermute x9 -> x12, waiting for transfers between devices: 35.4 us -> 54.9 us  [along(): lax.ppermute(block, 'seq', [(i, (i + CORES * chips) % size) for i in rang...]
    all_to_all x0 -> x4, waiting for transfers between devices: none -> 18.4 us  [body(): received.append(lax.all_to_all(sent, 'kv', 0, 0, tiled=True))]
    unnamed x20 -> x58, local copies, waits for them, and re-layouts: 5.88 us -> 23.8 us
    ppermute x16 -> x0, starting transfers between devices: 17.6 us -> none  [across(): return lax.ppermute(block, 'kv', [(i, i ^ flip) for i in range(size)])]
    all_to_all x0 -> x4, starting transfers between devices: none -> 17 us  [body(): received.append(lax.all_to_all(sent, 'kv', 0, 0, tiled=True))]
    ppermute x10 -> x13, waiting for transfers between devices: 1.78 us -> 5.74 us  [other_core(): lax.ppermute(block, 'seq', [(i, i ^ 1) for i in range(lax.axis_size('seq'...]
    pallas_call x9, Pallas kernels: 24.5 us -> 27.9 us  [the longest x4 18.4 us: project(): pl.pallas_call(functools.partial(project_kernel, chunk), grid=(2 * steps,...]
  transfers between devices with their start and end apart: 36 -> 30, of which waited for: 20 -> 19; matrix products, arithmetic and copies ran while one was open for 3% -> 2% of each run, Pallas kernels for 21% -> 16%
where the time goes in v6:
time: 184 us; the launch traced here: 183 us
  waiting for transfers between devices  79.1 us (43%)
  starting transfers between devices  37.8 us (21%)
  Pallas kernels  37.1 us (20%)
  local copies, waits for them, and re-layouts  26.2 us (14%)
    ppermute x12, waiting for transfers between devices, along(): lax.ppermute(block, 'seq', [(i, (i + CORES * chips) % size) for i in rang...  54.9 us
    unnamed x58, local copies, waits for them, and re-layouts  23.8 us
    all_to_all x4, waiting for transfers between devices, body(): received.append(lax.all_to_all(sent, 'kv', 0, 0, tiled=True))  18.4 us
    pallas_call x4, Pallas kernels, project(): pl.pallas_call(functools.partial(project_kernel, chunk), grid=(2 * steps,...  18.4 us
    all_to_all x4, starting transfers between devices, body(): received.append(lax.all_to_all(sent, 'kv', 0, 0, tiled=True))  17 us
    ppermute x12, starting transfers between devices, along(): lax.ppermute(block, 'seq', [(i, (i + CORES * chips) % size) for i in rang...  16 us
    pallas_call x2, Pallas kernels, attention(): pl.pallas_call(functools.partial(attention_kernel, heads, head_dim, offse...  9.26 us
    pallas_call x4, Pallas kernels, finish(): pl.pallas_call(finish_kernel, grid=(tokens // tile,), in_specs=[pl.BlockS...  8.1 us
  transfers between devices with their start and end apart: 30, of which 19 were waited for; matrix products, arithmetic and copies ran while one was open for 2% of the time, Pallas kernels for 16%

profile of v6, /device:TPU:0, one launch (start us, length us, event | category | flops | bytes accessed | tf_op | source)
XLA Modules:
  0.0 182.7 jit_solution(18040556803024521686)
XLA Ops:
  0.6 1.0 copy-done.14
  1.7 1.0 copy-done.15
  2.7 1.4 arrange.1
  4.1 5.0 %collective-permute-start.1 = (bf16[2,128,512]{2,1,0:T(8,128)(2,1)}, bf16[2,128,512]{2,1,0:T(8,128)(2,1)}, u32[]{:S(2)}, u32[]{:S(2)}) collective-permute-start(bf16[2,128,512]{2,1,0:T(8,128)(2,1)} %get-tuple-element.78.refs_0_), channel_id=1, source_target_pairs={{0,6},{1,7},{2,0},{3,1},{4,2},{5,3},{6,4},{7,5},{8,14},{9,15},{10,... | collective-permute-start | bytes 786440 | tf_op jit(solution)/shard_map/ppermute | solution.py:234
  9.2 1.1 copy.25
  12.3 3.1 %collective-permute-start.2 = (bf16[224,512]{1,0:T(8,128)(2,1)}, bf16[224,512]{1,0:T(8,128)(2,1)}, u32[]{:S(2)}, u32[]{:S(2)}) collective-permute-start(bf16[224,512]{1,0:T(8,128)(2,1)} %slice.28), channel_id=1, source_target_pairs={{0,1},{1,2},{2,3},{3,4},{4,5},{5,6},{6,7},{8,9},{9,10},{10,11},{11... | collective-permute-start | bytes 688136 | tf_op jit(solution)/shard_map/ppermute | solution.py:311
  16.3 1.6 copy-done.8
  17.9 1.6 copy-done.10
  19.5 1.2 copy-done.13
  20.7 4.6 %attention.2.second_ref = bf16[512,2048]{1,0:T(8,128)(2,1)S(1)} custom-call(s32[8]{0:T(128)S(1)} %reshape.115.order_ref, bf16[1024,1024]{1,0:T(8,128)(2,1)S(1)} %copy-done.8, bf16[1024,1024]{1,0:T(8,128)(2,1)S(1)} %copy-done.10, bf16[1024,512]{1,0:T(8,128)(2,1)S(1)} %copy-done.13, s32[1024,128]{1,0:T(8,128)S(1)} %broadcast_in_dim.13.low_ref), custom_call_target="tpu_custom_call" | custom-call | flops 1048576 | bytes 512 | tf_op jit(solution)/shard_map/attention/pallas_call | solution.py:120
  26.0 3.4 %collective-permute-start.3 = (bf16[2,128,512]{2,1,0:T(8,128)(2,1)}, bf16[2,128,512]{2,1,0:T(8,128)(2,1)S(1)}, u32[]{:S(2)}, u32[]{:S(2)}) collective-permute-start(bf16[2,128,512]{2,1,0:T(8,128)(2,1)} %collective-permute-done.refs_1_), channel_id=1, source_target_pairs={{0,2},{1,3},{2,4},{3,5},{4,6},{5,7},{6,0},{7,1},{8,10},{9,11},{10,... | collective-permute-start | bytes 786440 | tf_op jit(solution)/shard_map/ppermute | solution.py:234
  30.4 4.6 %attention.3.first_ref = bf16[512,2048]{1,0:T(8,128)(2,1)S(1)} custom-call(s32[8]{0:T(128)S(1)} %reshape.115.order_ref, bf16[1024,1024]{1,0:T(8,128)(2,1)S(1)} %copy-done.9, bf16[1024,1024]{1,0:T(8,128)(2,1)S(1)} %copy-done.11, bf16[736,512]{1,0:T(8,128)(2,1)S(1)} %pad_maximum_fusion.1.ctx_ref, s32[1024,128]{1,0:T(8,128)S(1)} %broadcast_in_dim.13.low_ref), custom_call_target="tpu_custom_call" | custom-call | flops 1048576 | bytes 512 | tf_op jit(solution)/shard_map/attention/pallas_call | solution.py:120
  35.0 1.4 collective-permute-done.6.refs_1_
  36.5 5.1 %collective-permute-done.3.refs_3_ = bf16[2,128,512]{2,1,0:T(8,128)(2,1)S(1)} collective-permute-done((bf16[2,128,512]{2,1,0:T(8,128)(2,1)}, bf16[2,128,512]{2,1,0:T(8,128)(2,1)S(1)}, u32[]{:S(2)}, u32[]{:S(2)}) %collective-permute-start.3) | collective-permute-done | bytes 262176 | tf_op jit(solution)/shard_map/ppermute | solution.py:234
  41.6 1.5 collective-permute-done.8.refs_4_
  43.1 5.3 %project.4 = bf16[4,2,1024,128]{3,2,1,0:T(8,128)(2,1)S(1)} custom-call(bf16[512,2048]{1,0:T(8,128)(2,1)S(1)} %attention.3.first_ref, bf16[512,2048]{1,0:T(8,128)(2,1)S(1)} %attention.2.second_ref, bf16[4,2,128,512]{3,2,1,0:T(8,128)(2,1)S(1)} %collective-permute-done.7.whole_ref, bf16[2,128,512]{2,1,0:T(8,128)(2,1)} %get-tuple-element.78.refs_0_, ...), custom_call_target="tpu_custom_call" | custom-call | flops 262144 | bytes 512 | tf_op jit(solution)/shard_map/project/pallas_call | solution.py:183
  48.5 1.4 copy-done
  49.9 1.4 copy-done.6
  51.2 4.5 %all-to-all-start = ((bf16[4,2,1024,128]{3,2,1,0:T(8,128)(2,1)}), bf16[4,2,1024,128]{3,2,1,0:T(8,128)(2,1)}, u32[]{:S(2)}, u32[]{:S(2)}) async-start(bf16[4,2,1024,128]{3,2,1,0:T(8,128)(2,1)} %copy-done.6), calls=%async_computation | async-start | bytes 4194304 | tf_op jit(solution)/shard_map/all_to_all | solution.py:367
  55.7 1.4 collective-permute-start.10
  57.8 6.8 %collective-permute-done.10.refs_5_ = bf16[2,128,512]{2,1,0:T(8,128)(2,1)S(1)} collective-permute-done((bf16[2,128,512]{2,1,0:T(8,128)(2,1)}, bf16[2,128,512]{2,1,0:T(8,128)(2,1)S(1)}, u32[]{:S(2)}, u32[]{:S(2)}) %collective-permute-start.10) | collective-permute-done | bytes 262176 | tf_op jit(solution)/shard_map/ppermute | solution.py:234
  64.6 6.6 %collective-permute-done.12.refs_1_ = bf16[2,128,512]{2,1,0:T(8,128)(2,1)S(1)} collective-permute-done((bf16[2,128,512]{2,1,0:T(8,128)(2,1)}, bf16[2,128,512]{2,1,0:T(8,128)(2,1)S(1)}, u32[]{:S(2)}, u32[]{:S(2)}) %collective-permute-start.12) | collective-permute-done | bytes 262176 | tf_op jit(solution)/shard_map/ppermute | solution.py:234
  71.2 4.8 %collective-permute-done.9.refs_3_ = bf16[2,128,512]{2,1,0:T(8,128)(2,1)S(1)} collective-permute-done((bf16[2,128,512]{2,1,0:T(8,128)(2,1)}, bf16[2,128,512]{2,1,0:T(8,128)(2,1)S(1)}, u32[]{:S(2)}, u32[]{:S(2)}) %collective-permute-start.9) | collective-permute-done | bytes 262176 | tf_op jit(solution)/shard_map/ppermute | solution.py:234
  76.5 1.0 collective-permute-done.13.refs_4_
  77.9 1.6 copy-done.1
  81.4 4.3 %project.5 = bf16[4,2,1024,128]{3,2,1,0:T(8,128)(2,1)S(1)} custom-call(bf16[512,2048]{1,0:T(8,128)(2,1)S(1)} %copy-done.1, bf16[512,2048]{1,0:T(8,128)(2,1)S(1)} %attention.2.second_ref, bf16[4,2,128,512]{3,2,1,0:T(8,128)(2,1)S(1)} %collective-permute-done.7.whole_ref, bf16[2,128,512]{2,1,0:T(8,128)(2,1)S(1)} %copy-done.20, ...), custom_call_target="tpu_custom_call" | custom-call | flops 262144 | bytes 512 | tf_op jit(solution)/shard_map/project/pallas_call | solution.py:183
  85.8 1.4 copy-done.4
  87.2 4.5 %all-to-all-start.1 = ((bf16[4,2,1024,128]{3,2,1,0:T(8,128)(2,1)}), bf16[4,2,1024,128]{3,2,1,0:T(8,128)(2,1)}, u32[]{:S(2)}, u32[]{:S(2)}) async-start(bf16[4,2,1024,128]{3,2,1,0:T(8,128)(2,1)} %copy-done.4), calls=%async_computation.1 | async-start | bytes 4194304 | tf_op jit(solution)/shard_map/all_to_all | solution.py:367
  91.7 1.8 collective-permute-start.16
  94.6 6.0 %collective-permute-done.16.refs_5_ = bf16[2,128,512]{2,1,0:T(8,128)(2,1)S(1)} collective-permute-done((bf16[2,128,512]{2,1,0:T(8,128)(2,1)}, bf16[2,128,512]{2,1,0:T(8,128)(2,1)S(1)}, u32[]{:S(2)}, u32[]{:S(2)}) %collective-permute-start.16) | collective-permute-done | bytes 262176 | tf_op jit(solution)/shard_map/ppermute | solution.py:234
  100.7 6.4 %collective-permute-done.18.refs_1_ = bf16[2,128,512]{2,1,0:T(8,128)(2,1)S(1)} collective-permute-done((bf16[2,128,512]{2,1,0:T(8,128)(2,1)S(1)}, bf16[2,128,512]{2,1,0:T(8,128)(2,1)S(1)}, u32[]{:S(2)}, u32[]{:S(2)}) %collective-permute-start.18) | collective-permute-done | bytes 262176 | tf_op jit(solution)/shard_map/ppermute | solution.py:234
  107.1 4.8 %collective-permute-done.15.refs_3_ = bf16[2,128,512]{2,1,0:T(8,128)(2,1)S(1)} collective-permute-done((bf16[2,128,512]{2,1,0:T(8,128)(2,1)}, bf16[2,128,512]{2,1,0:T(8,128)(2,1)S(1)}, u32[]{:S(2)}, u32[]{:S(2)}) %collective-permute-start.15) | collective-permute-done | bytes 262176 | tf_op jit(solution)/shard_map/ppermute | solution.py:234
  113.8 1.6 copy-done.2
  117.3 4.3 %project.6 = bf16[4,2,1024,128]{3,2,1,0:T(8,128)(2,1)S(1)} custom-call(bf16[512,2048]{1,0:T(8,128)(2,1)S(1)} %copy-done.2, bf16[512,2048]{1,0:T(8,128)(2,1)S(1)} %attention.2.second_ref, bf16[4,2,128,512]{3,2,1,0:T(8,128)(2,1)S(1)} %collective-permute-done.7.whole_ref, bf16[2,128,512]{2,1,0:T(8,128)(2,1)S(1)} %copy-done.17, ...), custom_call_target="tpu_custom_call" | custom-call | flops 262144 | bytes 512 | tf_op jit(solution)/shard_map/project/pallas_call | solution.py:183
  121.7 1.3 copy-done.5
  123.0 4.4 %all-to-all-start.3 = ((bf16[4,2,1024,128]{3,2,1,0:T(8,128)(2,1)}), bf16[4,2,1024,128]{3,2,1,0:T(8,128)(2,1)}, u32[]{:S(2)}, u32[]{:S(2)}) async-start(bf16[4,2,1024,128]{3,2,1,0:T(8,128)(2,1)} %copy-done.5), calls=%async_computation.3 | async-start | bytes 4194304 | tf_op jit(solution)/shard_map/all_to_all | solution.py:367
  127.5 1.6 collective-permute-start.22
  129.5 6.3 %collective-permute-done.22.refs_5_ = bf16[2,128,512]{2,1,0:T(8,128)(2,1)S(1)} collective-permute-done((bf16[2,128,512]{2,1,0:T(8,128)(2,1)S(1)}, bf16[2,128,512]{2,1,0:T(8,128)(2,1)S(1)}, u32[]{:S(2)}, u32[]{:S(2)}) %collective-permute-start.22) | collective-permute-done | bytes 262176 | tf_op jit(solution)/shard_map/ppermute | solution.py:234
  135.9 6.5 %collective-permute-done.21.refs_3_ = bf16[2,128,512]{2,1,0:T(8,128)(2,1)S(1)} collective-permute-done((bf16[2,128,512]{2,1,0:T(8,128)(2,1)}, bf16[2,128,512]{2,1,0:T(8,128)(2,1)S(1)}, u32[]{:S(2)}, u32[]{:S(2)}) %collective-permute-start.21) | collective-permute-done | bytes 262176 | tf_op jit(solution)/shard_map/ppermute | solution.py:234
  144.3 1.6 copy-done.3
  146.8 4.3 %project.7 = bf16[4,2,1024,128]{3,2,1,0:T(8,128)(2,1)S(1)} custom-call(bf16[512,2048]{1,0:T(8,128)(2,1)S(1)} %copy-done.3, bf16[512,2048]{1,0:T(8,128)(2,1)S(1)} %attention.2.second_ref, bf16[4,2,128,512]{3,2,1,0:T(8,128)(2,1)S(1)} %collective-permute-done.7.whole_ref, bf16[2,128,512]{2,1,0:T(8,128)(2,1)S(1)} %get-tuple-element.115.refs_0_, ...), custom_call_target="tpu_custom_call" | custom-call | flops 262144 | bytes 512 | tf_op jit(solution)/shard_map/project/pallas_call | solution.py:183
  151.2 1.4 copy-done.7
  153.0 3.6 %all-to-all-start.2 = ((bf16[4,2,1024,128]{3,2,1,0:T(8,128)(2,1)}), bf16[4,2,1024,128]{3,2,1,0:T(8,128)(2,1)S(1)}, u32[]{:S(2)}, u32[]{:S(2)}) async-start(bf16[4,2,1024,128]{3,2,1,0:T(8,128)(2,1)} %copy-done.7), calls=%async_computation.2 | async-start | bytes 4194304 | tf_op jit(solution)/shard_map/all_to_all | solution.py:367
  156.6 2.4 %finish.4 = (bf16[1024,512]{1,0:T(8,128)(2,1)}, bf16[1024,512]{1,0:T(8,128)(2,1)}) custom-call(bf16[4,2,1024,128]{3,2,1,0:T(8,128)(2,1)} %all-to-all-done.parts_ref), custom_call_target="tpu_custom_call" | custom-call | tf_op jit(solution)/shard_map/finish/pallas_call | solution.py:217
  158.9 2.3 %finish.5 = (bf16[1024,512]{1,0:T(8,128)(2,1)}, bf16[1024,512]{1,0:T(8,128)(2,1)}) custom-call(bf16[4,2,1024,128]{3,2,1,0:T(8,128)(2,1)} %all-to-all-done.1.parts_ref, bf16[1024,512]{1,0:T(8,128)(2,1)} %get-tuple-element.122.refs_0_, bf16[1024,512]{1,0:T(8,128)(2,1)} %get-tuple-element.123.refs_1_), custom_call_target="tpu_custom_call", output_to_operand_aliasing={{0}: (1, {}), {1}: (2, {})} | custom-call | tf_op jit(solution)/shard_map/finish/pallas_call | solution.py:217
  161.3 2.3 %finish.6 = (bf16[1024,512]{1,0:T(8,128)(2,1)}, bf16[1024,512]{1,0:T(8,128)(2,1)}) custom-call(bf16[4,2,1024,128]{3,2,1,0:T(8,128)(2,1)} %all-to-all-done.3.parts_ref, bf16[1024,512]{1,0:T(8,128)(2,1)} %get-tuple-element.124.refs_0_, bf16[1024,512]{1,0:T(8,128)(2,1)} %get-tuple-element.125.refs_1_), custom_call_target="tpu_custom_call", output_to_operand_aliasing={{0}: (1, {}), {1}: (2, {})} | custom-call | tf_op jit(solution)/shard_map/finish/pallas_call | solution.py:217
  163.6 18.0 %all-to-all-done.2.parts_ref = bf16[4,2,1024,128]{3,2,1,0:T(8,128)(2,1)S(1)} async-done(((bf16[4,2,1024,128]{3,2,1,0:T(8,128)(2,1)}), bf16[4,2,1024,128]{3,2,1,0:T(8,128)(2,1)S(1)}, u32[]{:S(2)}, u32[]{:S(2)}) %all-to-all-start.2) | async-done | bytes 2097184 | tf_op jit(solution)/shard_map/all_to_all | solution.py:367
  181.6 1.1 finish.7
  (100 shorter events, 16.7 us)
Async XLA Ops:
  2.7 7.6 %copy-start.27 = (bf16[1024,2,128]{2,1,0:T(2,128)(2,1)S(1)}, bf16[1024,2,128]{2,1,0:T(2,128)(2,1)}, u32[]{:S(2)}) copy-start(bf16[1024,2,128]{2,1,0:T(2,128)(2,1)} %param.10) | copy-start | bytes 1572868
  4.1 6.4 %copy-start.16 = (bf16[2,128,512]{2,1,0:T(8,128)(2,1)}, bf16[2,128,512]{2,1,0:T(8,128)(2,1)S(1)}, u32[]{:S(2)}) copy-start(bf16[2,128,512]{2,1,0:T(8,128)(2,1)S(1)} %get-tuple-element.102.refs_0_) | copy-start | bytes 786436
  4.1 6.4 %copy-start.18 = (bf16[2,128,512]{2,1,0:T(8,128)(2,1)}, bf16[2,128,512]{2,1,0:T(8,128)(2,1)S(1)}, u32[]{:S(2)}) copy-start(bf16[2,128,512]{2,1,0:T(8,128)(2,1)S(1)} %get-tuple-element.91.refs_0_) | copy-start | bytes 786436
  4.1 21.2 %collective-permute-start.1 = (bf16[2,128,512]{2,1,0:T(8,128)(2,1)}, bf16[2,128,512]{2,1,0:T(8,128)(2,1)}, u32[]{:S(2)}, u32[]{:S(2)}) collective-permute-start(bf16[2,128,512]{2,1,0:T(8,128)(2,1)} %get-tuple-element.78.refs_0_), channel_id=1, source_target_pairs={{0,6},{1,7},{2,0},{3,1},{4,2},{5,3},{6,4},{7,5},{8,14},{9,15},{10,... | collective-permute-start | bytes 786440 | tf_op jit(solution)/shard_map/ppermute | solution.py:234
  9.2 16.2 %collective-permute-start = (bf16[2,128,512]{2,1,0:T(8,128)(2,1)}, bf16[2,128,512]{2,1,0:T(8,128)(2,1)}, u32[]{:S(2)}, u32[]{:S(2)}) collective-permute-start(bf16[2,128,512]{2,1,0:T(8,128)(2,1)} %get-tuple-element.78.refs_0_), channel_id=1, source_target_pairs={{0,2},{1,3},{2,4},{3,5},{4,6},{5,7},{6,0},{7,1},{8,10},{9,11},{10,... | collective-permute-start | bytes 786440 | tf_op jit(solution)/shard_map/ppermute | solution.py:234
  9.2 32.4 %collective-permute-start.7 = (bf16[4,2,128,512]{3,2,1,0:T(8,128)(2,1)}, bf16[4,2,128,512]{3,2,1,0:T(8,128)(2,1)S(1)}, u32[]{:S(2)}, u32[]{:S(2)}) collective-permute-start(bf16[4,2,128,512]{3,2,1,0:T(8,128)(2,1)} %get-tuple-element.77), channel_id=1, source_target_pairs={{0,1},{1,0},{2,3},{3,2},{4,5},{5,4},{6,7},{7,6},{8,9},{9,8},{10,11... | collective-permute-start | bytes 3145736 | tf_op jit(solution)/shard_map/ppermute | solution.py:238
  10.4 5.1 %copy-start.28 = (s32[64]{0:T(128)S(1)}, s32[64]{0:T(128)}, u32[]{:S(2)}) copy-start(s32[64]{0:T(128)} %param.11) | copy-start | bytes 772
  12.3 13.0 %collective-permute-start.2 = (bf16[224,512]{1,0:T(8,128)(2,1)}, bf16[224,512]{1,0:T(8,128)(2,1)}, u32[]{:S(2)}, u32[]{:S(2)}) collective-permute-start(bf16[224,512]{1,0:T(8,128)(2,1)} %slice.28), channel_id=1, source_target_pairs={{0,1},{1,2},{2,3},{3,4},{4,5},{5,6},{6,7},{8,9},{9,10},{10,11},{11... | collective-permute-start | bytes 688136 | tf_op jit(solution)/shard_map/ppermute | solution.py:311
  16.3 1.6 copy-start.8
  17.9 1.6 copy-start.10
  20.7 4.8 %copy-start.19 = (bf16[2,128,512]{2,1,0:T(8,128)(2,1)S(1)}, bf16[2,128,512]{2,1,0:T(8,128)(2,1)}, u32[]{:S(2)}) copy-start(bf16[2,128,512]{2,1,0:T(8,128)(2,1)} %copy-done.18) | copy-start | bytes 786436
  20.7 8.6 %slice-start = ((bf16[1024,512]{1,0:T(8,128)(2,1)}), bf16[512,512]{1,0:T(8,128)(2,1)S(1)}, s32[]{:S(2)}) async-start(bf16[1024,512]{1,0:T(8,128)(2,1)} %copy-done.12), calls=%async_computation.4 | async-start | bytes 1048576 | tf_op jit(solution)/shard_map/slice | solution.py:348
  20.7 9.6 %copy-start.11 = (bf16[1024,1024]{1,0:T(8,128)(2,1)S(1)}, bf16[1024,1024]{1,0:T(8,128)(2,1)}, u32[]{:S(2)}) copy-start(bf16[1024,1024]{1,0:T(8,128)(2,1)} %qt_ref.3) | copy-start | bytes 6291460
  25.4 5.0 %copy-start.9 = (bf16[1024,1024]{1,0:T(8,128)(2,1)S(1)}, bf16[1024,1024]{1,0:T(8,128)(2,1)}, u32[]{:S(2)}) copy-start(bf16[1024,1024]{1,0:T(8,128)(2,1)} %q_ref.3) | copy-start | bytes 6291460
  25.4 9.6 %collective-permute-start.5 = (bf16[2,128,512]{2,1,0:T(8,128)(2,1)}, bf16[2,128,512]{2,1,0:T(8,128)(2,1)S(1)}, u32[]{:S(2)}, u32[]{:S(2)}) collective-permute-start(bf16[2,128,512]{2,1,0:T(8,128)(2,1)} %collective-permute-done.1.refs_5_), channel_id=1, source_target_pairs={{0,1},{1,0},{2,3},{3,2},{4,5},{5,4},{6,7},{7,6},{8,9},{9,8},{10,11... | collective-permute-start | bytes 786440 | tf_op jit(solution)/shard_map/ppermute | solution.py:238
  25.5 11.0 %collective-permute-start.6 = (bf16[2,128,512]{2,1,0:T(8,128)(2,1)S(1)}, bf16[2,128,512]{2,1,0:T(8,128)(2,1)S(1)}, u32[]{:S(2)}, u32[]{:S(2)}) collective-permute-start(bf16[2,128,512]{2,1,0:T(8,128)(2,1)S(1)} %copy-done.19), channel_id=1, source_target_pairs={{0,2},{1,3},{2,4},{3,5},{4,6},{5,7},{6,0},{7,1},{8,10},{9,11},{10,... | collective-permute-start | bytes 786440 | tf_op jit(solution)/shard_map/ppermute | solution.py:234
  26.0 10.5 %collective-permute-start.4 = (bf16[2,128,512]{2,1,0:T(8,128)(2,1)}, bf16[2,128,512]{2,1,0:T(8,128)(2,1)S(1)}, u32[]{:S(2)}, u32[]{:S(2)}) collective-permute-start(bf16[2,128,512]{2,1,0:T(8,128)(2,1)} %collective-permute-done.refs_1_), channel_id=1, source_target_pairs={{0,1},{1,0},{2,3},{3,2},{4,5},{5,4},{6,7},{7,6},{8,9},{9,8},{10,11... | collective-permute-start | bytes 786440 | tf_op jit(solution)/shard_map/ppermute | solution.py:238
  26.0 15.6 %collective-permute-start.3 = (bf16[2,128,512]{2,1,0:T(8,128)(2,1)}, bf16[2,128,512]{2,1,0:T(8,128)(2,1)S(1)}, u32[]{:S(2)}, u32[]{:S(2)}) collective-permute-start(bf16[2,128,512]{2,1,0:T(8,128)(2,1)} %collective-permute-done.refs_1_), channel_id=1, source_target_pairs={{0,2},{1,3},{2,4},{3,5},{4,6},{5,7},{6,0},{7,1},{8,10},{9,11},{10,... | collective-permute-start | bytes 786440 | tf_op jit(solution)/shard_map/ppermute | solution.py:234
  36.5 5.2 %copy-start.21 = (bf16[2,128,512]{2,1,0:T(8,128)(2,1)}, bf16[2,128,512]{2,1,0:T(8,128)(2,1)S(1)}, u32[]{:S(2)}) copy-start(bf16[2,128,512]{2,1,0:T(8,128)(2,1)S(1)} %collective-permute-done.6.refs_1_) | copy-start | bytes 786436
  41.6 1.5 collective-permute-start.8
  51.2 36.0 %all-to-all-start = ((bf16[4,2,1024,128]{3,2,1,0:T(8,128)(2,1)}), bf16[4,2,1024,128]{3,2,1,0:T(8,128)(2,1)}, u32[]{:S(2)}, u32[]{:S(2)}) async-start(bf16[4,2,1024,128]{3,2,1,0:T(8,128)(2,1)} %copy-done.6), calls=%async_computation | async-start | bytes 4194304 | tf_op jit(solution)/shard_map/all_to_all | solution.py:367
  55.7 8.9 %collective-permute-start.10 = (bf16[2,128,512]{2,1,0:T(8,128)(2,1)}, bf16[2,128,512]{2,1,0:T(8,128)(2,1)S(1)}, u32[]{:S(2)}, u32[]{:S(2)}) collective-permute-start(bf16[2,128,512]{2,1,0:T(8,128)(2,1)} %copy-done.18), channel_id=1, source_target_pairs={{0,6},{1,7},{2,0},{3,1},{4,2},{5,3},{6,4},{7,5},{8,14},{9,15},{10,... | collective-permute-start | bytes 786440 | tf_op jit(solution)/shard_map/ppermute | solution.py:234
  57.1 14.1 %collective-permute-start.12 = (bf16[2,128,512]{2,1,0:T(8,128)(2,1)}, bf16[2,128,512]{2,1,0:T(8,128)(2,1)S(1)}, u32[]{:S(2)}, u32[]{:S(2)}) collective-permute-start(bf16[2,128,512]{2,1,0:T(8,128)(2,1)} %copy-done.16), channel_id=1, source_target_pairs={{0,2},{1,3},{2,4},{3,5},{4,6},{5,7},{6,0},{7,1},{8,10},{9,11},{10,... | collective-permute-start | bytes 786440 | tf_op jit(solution)/shard_map/ppermute | solution.py:234
  57.8 13.5 %collective-permute-start.11 = (bf16[2,128,512]{2,1,0:T(8,128)(2,1)}, bf16[2,128,512]{2,1,0:T(8,128)(2,1)S(1)}, u32[]{:S(2)}, u32[]{:S(2)}) collective-permute-start(bf16[2,128,512]{2,1,0:T(8,128)(2,1)} %copy-done.21), channel_id=1, source_target_pairs={{0,1},{1,0},{2,3},{3,2},{4,5},{5,4},{6,7},{7,6},{8,9},{9,8},{10,11... | collective-permute-start | bytes 786440 | tf_op jit(solution)/shard_map/ppermute | solution.py:238
  57.8 18.3 %collective-permute-start.9 = (bf16[2,128,512]{2,1,0:T(8,128)(2,1)}, bf16[2,128,512]{2,1,0:T(8,128)(2,1)S(1)}, u32[]{:S(2)}, u32[]{:S(2)}) collective-permute-start(bf16[2,128,512]{2,1,0:T(8,128)(2,1)} %copy-done.21), channel_id=1, source_target_pairs={{0,2},{1,3},{2,4},{3,5},{4,6},{5,7},{6,0},{7,1},{8,10},{9,11},{10,... | collective-permute-start | bytes 786440 | tf_op jit(solution)/shard_map/ppermute | solution.py:234
  71.2 6.4 %copy-start.23 = (bf16[2,128,512]{2,1,0:T(8,128)(2,1)}, bf16[2,128,512]{2,1,0:T(8,128)(2,1)S(1)}, u32[]{:S(2)}) copy-start(bf16[2,128,512]{2,1,0:T(8,128)(2,1)S(1)} %collective-permute-done.12.refs_1_) | copy-start | bytes 786436
  76.0 1.5 collective-permute-start.13
  76.0 1.9 %collective-permute-start.14 = (bf16[2,128,512]{2,1,0:T(8,128)(2,1)S(1)}, bf16[2,128,512]{2,1,0:T(8,128)(2,1)S(1)}, u32[]{:S(2)}, u32[]{:S(2)}) collective-permute-start(bf16[2,128,512]{2,1,0:T(8,128)(2,1)S(1)} %collective-permute-done.10.refs_5_), channel_id=1, source_target_pairs={{0,1},{1,0},{2,3},{3,2},{4,5},{5,4},{6,7},{7,6},{8,9},{9,8},{10,11... | collective-permute-start | bytes 786440 | tf_op jit(solution)/shard_map/ppermute | solution.py:238
  77.9 1.6 copy-start.1
  85.8 1.4 copy-start.4
  87.2 35.8 %all-to-all-start.1 = ((bf16[4,2,1024,128]{3,2,1,0:T(8,128)(2,1)}), bf16[4,2,1024,128]{3,2,1,0:T(8,128)(2,1)}, u32[]{:S(2)}, u32[]{:S(2)}) async-start(bf16[4,2,1024,128]{3,2,1,0:T(8,128)(2,1)} %copy-done.4), calls=%async_computation.1 | async-start | bytes 4194304 | tf_op jit(solution)/shard_map/all_to_all | solution.py:367
  91.7 9.0 %collective-permute-start.16 = (bf16[2,128,512]{2,1,0:T(8,128)(2,1)}, bf16[2,128,512]{2,1,0:T(8,128)(2,1)S(1)}, u32[]{:S(2)}, u32[]{:S(2)}) collective-permute-start(bf16[2,128,512]{2,1,0:T(8,128)(2,1)} %copy-done.16), channel_id=1, source_target_pairs={{0,6},{1,7},{2,0},{3,1},{4,2},{5,3},{6,4},{7,5},{8,14},{9,15},{10,... | collective-permute-start | bytes 786440 | tf_op jit(solution)/shard_map/ppermute | solution.py:234
  93.5 13.6 %collective-permute-start.18 = (bf16[2,128,512]{2,1,0:T(8,128)(2,1)S(1)}, bf16[2,128,512]{2,1,0:T(8,128)(2,1)S(1)}, u32[]{:S(2)}, u32[]{:S(2)}) collective-permute-start(bf16[2,128,512]{2,1,0:T(8,128)(2,1)S(1)} %get-tuple-element.115.refs_0_), channel_id=1, source_target_pairs={{0,2},{1,3},{2,4},{3,5},{4,6},{5,7},{6,0},{7,1},{8,10},{9,11},{10,... | collective-permute-start | bytes 786440 | tf_op jit(solution)/shard_map/ppermute | solution.py:234
  93.7 13.4 %collective-permute-start.17 = (bf16[2,128,512]{2,1,0:T(8,128)(2,1)}, bf16[2,128,512]{2,1,0:T(8,128)(2,1)S(1)}, u32[]{:S(2)}, u32[]{:S(2)}) collective-permute-start(bf16[2,128,512]{2,1,0:T(8,128)(2,1)} %copy-done.23), channel_id=1, source_target_pairs={{0,1},{1,0},{2,3},{3,2},{4,5},{5,4},{6,7},{7,6},{8,9},{9,8},{10,11... | collective-permute-start | bytes 786440 | tf_op jit(solution)/shard_map/ppermute | solution.py:238
  93.8 18.2 %collective-permute-start.15 = (bf16[2,128,512]{2,1,0:T(8,128)(2,1)}, bf16[2,128,512]{2,1,0:T(8,128)(2,1)S(1)}, u32[]{:S(2)}, u32[]{:S(2)}) collective-permute-start(bf16[2,128,512]{2,1,0:T(8,128)(2,1)} %copy-done.23), channel_id=1, source_target_pairs={{0,2},{1,3},{2,4},{3,5},{4,6},{5,7},{6,0},{7,1},{8,10},{9,11},{10,... | collective-permute-start | bytes 786440 | tf_op jit(solution)/shard_map/ppermute | solution.py:234
  107.1 6.4 %copy-start.25 = (bf16[2,128,512]{2,1,0:T(8,128)(2,1)}, bf16[2,128,512]{2,1,0:T(8,128)(2,1)S(1)}, u32[]{:S(2)}) copy-start(bf16[2,128,512]{2,1,0:T(8,128)(2,1)S(1)} %collective-permute-done.18.refs_1_) | copy-start | bytes 786436
  111.9 1.5 collective-permute-start.19
  111.9 1.9 %collective-permute-start.20 = (bf16[2,128,512]{2,1,0:T(8,128)(2,1)S(1)}, bf16[2,128,512]{2,1,0:T(8,128)(2,1)S(1)}, u32[]{:S(2)}, u32[]{:S(2)}) collective-permute-start(bf16[2,128,512]{2,1,0:T(8,128)(2,1)S(1)} %collective-permute-done.16.refs_5_), channel_id=1, source_target_pairs={{0,1},{1,0},{2,3},{3,2},{4,5},{5,4},{6,7},{7,6},{8,9},{9,8},{10,11... | collective-permute-start | bytes 786440 | tf_op jit(solution)/shard_map/ppermute | solution.py:238
  113.8 1.6 copy-start.2
  123.0 30.0 %all-to-all-start.3 = ((bf16[4,2,1024,128]{3,2,1,0:T(8,128)(2,1)}), bf16[4,2,1024,128]{3,2,1,0:T(8,128)(2,1)}, u32[]{:S(2)}, u32[]{:S(2)}) async-start(bf16[4,2,1024,128]{3,2,1,0:T(8,128)(2,1)} %copy-done.5), calls=%async_computation.3 | async-start | bytes 4194304 | tf_op jit(solution)/shard_map/all_to_all | solution.py:367
  127.5 8.4 %collective-permute-start.22 = (bf16[2,128,512]{2,1,0:T(8,128)(2,1)S(1)}, bf16[2,128,512]{2,1,0:T(8,128)(2,1)S(1)}, u32[]{:S(2)}, u32[]{:S(2)}) collective-permute-start(bf16[2,128,512]{2,1,0:T(8,128)(2,1)S(1)} %get-tuple-element.115.refs_0_), channel_id=1, source_target_pairs={{0,6},{1,7},{2,0},{3,1},{4,2},{5,3},{6,4},{7,5},{8,14},{9,15},{10,... | collective-permute-start | bytes 786440 | tf_op jit(solution)/shard_map/ppermute | solution.py:234
  129.0 6.8 %collective-permute-start.23 = (bf16[2,128,512]{2,1,0:T(8,128)(2,1)}, bf16[2,128,512]{2,1,0:T(8,128)(2,1)S(1)}, u32[]{:S(2)}, u32[]{:S(2)}) collective-permute-start(bf16[2,128,512]{2,1,0:T(8,128)(2,1)} %copy-done.25), channel_id=1, source_target_pairs={{0,1},{1,0},{2,3},{3,2},{4,5},{5,4},{6,7},{7,6},{8,9},{9,8},{10,11... | collective-permute-start | bytes 786440 | tf_op jit(solution)/shard_map/ppermute | solution.py:238
  129.0 13.3 %collective-permute-start.21 = (bf16[2,128,512]{2,1,0:T(8,128)(2,1)}, bf16[2,128,512]{2,1,0:T(8,128)(2,1)S(1)}, u32[]{:S(2)}, u32[]{:S(2)}) collective-permute-start(bf16[2,128,512]{2,1,0:T(8,128)(2,1)} %copy-done.25), channel_id=1, source_target_pairs={{0,2},{1,3},{2,4},{3,5},{4,6},{5,7},{6,0},{7,1},{8,10},{9,11},{10,... | collective-permute-start | bytes 786440 | tf_op jit(solution)/shard_map/ppermute | solution.py:234
  142.4 1.5 collective-permute-start.24
  142.4 1.9 %collective-permute-start.25 = (bf16[2,128,512]{2,1,0:T(8,128)(2,1)S(1)}, bf16[2,128,512]{2,1,0:T(8,128)(2,1)S(1)}, u32[]{:S(2)}, u32[]{:S(2)}) collective-permute-start(bf16[2,128,512]{2,1,0:T(8,128)(2,1)S(1)} %collective-permute-done.22.refs_5_), channel_id=1, source_target_pairs={{0,1},{1,0},{2,3},{3,2},{4,5},{5,4},{6,7},{7,6},{8,9},{9,8},{10,11... | collective-permute-start | bytes 786440 | tf_op jit(solution)/shard_map/ppermute | solution.py:238
  144.3 1.6 copy-start.3
  151.2 1.4 copy-start.7
  153.0 28.7 %all-to-all-start.2 = ((bf16[4,2,1024,128]{3,2,1,0:T(8,128)(2,1)}), bf16[4,2,1024,128]{3,2,1,0:T(8,128)(2,1)S(1)}, u32[]{:S(2)}, u32[]{:S(2)}) async-start(bf16[4,2,1024,128]{3,2,1,0:T(8,128)(2,1)} %copy-done.7), calls=%async_computation.2 | async-start | bytes 4194304 | tf_op jit(solution)/shard_map/all_to_all | solution.py:367
  (12 other events, 13.1 us)

commit v7 on v6

--- a/solution.py
+++ b/solution.py
@@ -18,27 +18,31 @@
 vmem_bytes = 16 * 1024 * 1024
 
 
-def arrange_kernel(owners, tangent_ref, value_ref, whole_ref, *chunk_refs):
+def arrange_kernel(owners, tangent_ref, value_ref, *refs):
+    *chunk_refs, sems = refs
     columns = tangent_ref.shape[1] // owners
     part = columns // len(chunk_refs)
+    copies = []
     for chunk, chunk_ref in enumerate(chunk_refs):
-        for owner in range(owners):
-            of = slice(owner * columns + chunk * part, owner * columns + (chunk + 1) * part)
-            to = slice(owner * part, (owner + 1) * part)
-            for mat, ref in enumerate((tangent_ref, value_ref)):
-                whole_ref[chunk, mat, :, to] = ref[:, of]
-                chunk_ref[mat, :, to] = ref[:, of]
+        for mat, ref in enumerate((tangent_ref, value_ref)):
+            for owner in range(owners):
+                source = ref.at[:, pl.ds(owner * columns + chunk * part, part)]
+                target = chunk_ref.at[0, mat, :, pl.ds(owner * part, part)]
+                copies.append(pltpu.make_async_copy(source, target, sems.at[len(copies)]))
+                copies[-1].start()
+    for copy in copies:
+        copy.wait()
 
 
 def arrange(owners, tangent, value):
     rows, columns = value.shape
-    chunk = (2, rows, columns // CHUNKS)
-    shapes = [jax.ShapeDtypeStruct(shape, value.dtype) for shape in [(CHUNKS, *chunk)] + [chunk] * CHUNKS]
+    shape = jax.ShapeDtypeStruct((1, 2, rows, columns // CHUNKS), value.dtype)
     return pl.pallas_call(
         functools.partial(arrange_kernel, owners),
-        in_specs=[pl.BlockSpec(memory_space=pltpu.VMEM)] * 2,
-        out_specs=[pl.BlockSpec(memory_space=pltpu.VMEM)] * len(shapes),
-        out_shape=shapes,
+        in_specs=[pl.BlockSpec(memory_space=pltpu.HBM)] * 2,
+        out_specs=[pl.BlockSpec(memory_space=pl.ANY)] * CHUNKS,
+        out_shape=[shape] * CHUNKS,
+        scratch_shapes=[pltpu.SemaphoreType.DMA((2 * CHUNKS * owners,))],
         compiler_params=pltpu.CompilerParams(vmem_limit_bytes=vmem_bytes),
         name="arrange",
     )(tangent, value)
@@ -137,21 +141,33 @@
     )(order, queries, query_tangent, context, low)
 
 
-def project_kernel(chunk, first_ref, second_ref, whole_ref, *refs):
-    *piece_refs, send_ref, weight_ref, sems = refs
+def project_kernel(chunk, places, place_ref, first_ref, second_ref, *refs):
+    *array_refs, send_ref, keep_ref, weight_ref, sems = refs
     step, steps = pl.program_id(0), pl.num_programs(0)
-    rows = whole_ref.shape[2]
     depth = weight_ref.shape[1]
-    owners, _, _, part = send_ref.shape
-    sources = [piece_refs[0], whole_ref.at[chunk], *piece_refs[1:]]
+    owners = place_ref.shape[0]
+    part = weight_ref.shape[2] // owners
+    rows = depth // len(places)
+    columns = array_refs[0].shape[1] // owners
 
     @pl.when(step == 0)
     def _():
         copies = []
-        for place, source in enumerate(sources):
-            to = weight_ref.at[:, pl.ds(place * rows, rows), :]
-            copies.append(pltpu.make_async_copy(source, to, sems.at[place]))
-            copies[-1].start()
+        for place, (kind, which, index) in enumerate(places):
+            for mat in range(2):
+                for position in range(owners):
+                    owner = place_ref[position]
+                    if kind:
+                        start = pl.multiple_of(owner * part, part)
+                        source = array_refs[which].at[index, mat, :, pl.ds(start, part)]
+                    else:
+                        start = pl.multiple_of(owner * columns + chunk * part, part)
+                        source = array_refs[which + mat].at[:, pl.ds(start, part)]
+                    target = weight_ref.at[
+                        mat, pl.ds(place * rows, rows), pl.ds(position * part, part)
+                    ]
+                    copies.append(pltpu.make_async_copy(source, target, sems.at[len(copies)]))
+                    copies[-1].start()
         for copy in copies:
             copy.wait()
 
@@ -159,10 +175,9 @@
         dot = functools.partial(jnp.dot, preferred_element_type=jnp.float32)
         value = dot(pair_ref[:, :depth], weight_ref[1])
         tangent = dot(pair_ref[:, :depth], weight_ref[0]) + dot(pair_ref[:, depth:], weight_ref[1])
-        for owner in range(owners):
-            of = slice(owner * part, (owner + 1) * part)
-            send_ref[owner, 0] = value[:, of].astype(send_ref.dtype)
-            send_ref[owner, 1] = tangent[:, of].astype(send_ref.dtype)
+        for mat, result in enumerate((value, tangent)):
+            send_ref[mat] = result[:, : 2 * part].astype(send_ref.dtype)
+            keep_ref[mat] = result[:, 2 * part :]
 
     @pl.when(step < steps // 2)
     def _():
@@ -173,60 +188,69 @@
         run(second_ref)
 
 
-def project(owners, chunk, pairs, whole, pieces):
+def project(chunk, places, order, pairs, arrays, columns):
     tokens, width = pairs[0].shape
     tile = min(2 * TILE, tokens)
     steps = tokens // tile
-    _, rows, columns = pieces[0].shape
-    part = columns // owners
-    count = len(pieces) + 1
+    block = pl.BlockSpec((2, tile, columns // 2), lambda i: (0, i, 0))
+    out = (2, 2 * tokens, columns // 2)
     return pl.pallas_call(
-        functools.partial(project_kernel, chunk),
+        functools.partial(project_kernel, chunk, places),
         grid=(2 * steps,),
         in_specs=[
+            pl.BlockSpec(memory_space=pltpu.SMEM),
             pl.BlockSpec((tile, width), lambda i: (jnp.minimum(i, steps - 1), 0)),
             pl.BlockSpec((tile, width), lambda i: (jnp.maximum(i - steps, 0), 0)),
-            *[pl.BlockSpec(memory_space=pl.ANY)] * count,
+            *[pl.BlockSpec(memory_space=pl.ANY)] * len(arrays),
         ],
-        out_specs=pl.BlockSpec((owners, 2, tile, part), lambda i: (0, 0, i, 0)),
-        out_shape=jax.ShapeDtypeStruct((owners, 2, 2 * tokens, part), jnp.bfloat16),
+        out_specs=[block, block],
+        out_shape=[jax.ShapeDtypeStruct(out, jnp.bfloat16), jax.ShapeDtypeStruct(out, jnp.float32)],
         scratch_shapes=[
-            pltpu.VMEM((2, rows * count, columns), jnp.bfloat16),
-            pltpu.SemaphoreType.DMA((count,)),
+            pltpu.VMEM((2, width // 2, columns), jnp.bfloat16),
+            pltpu.SemaphoreType.DMA((2 * len(places) * order.shape[0],)),
         ],
         compiler_params=pltpu.CompilerParams(vmem_limit_bytes=vmem_bytes),
         cost_estimate=pl.CostEstimate(
             flops=tokens * columns, bytes_accessed=tokens, transcendentals=0
         ),
         name="project",
-    )(*pairs, whole, *pieces)
-
-
-def finish_kernel(parts_ref, *refs):
+    )(order, *pairs, *arrays)
+
+
+def finish_kernel(keep_ref, received_ref, last_ref, *refs):
     for mat, ref in enumerate(refs[-2:]):
-        total = parts_ref[0, mat].astype(jnp.float32)
-        for owner in range(1, parts_ref.shape[0]):
-            total = total + parts_ref[owner, mat]
-        ref[...] = total.astype(ref.dtype)
-
-
-def finish(chunk, outputs, parts):
-    owners, _, tokens, part = parts.shape
+        ref[...] = (keep_ref[mat] + received_ref[mat] + last_ref[mat]).astype(ref.dtype)
+
+
+def finish(chunk, outputs, keep, received, last):
+    _, tokens, part = last.shape
     shape = jax.ShapeDtypeStruct((tokens, part * CHUNKS), jnp.bfloat16)
     tile = tokens // 2
     return pl.pallas_call(
         finish_kernel,
         grid=(tokens // tile,),
         in_specs=[
-            pl.BlockSpec((owners, 2, tile, part), lambda i: (0, 0, i, 0)),
+            pl.BlockSpec((2, tile, part), lambda i: (0, i, 1)),
+            pl.BlockSpec((2, tile, part), lambda i: (0, i, 0)),
+            pl.BlockSpec((2, tile, part), lambda i: (0, i, 0)),
             *[pl.BlockSpec(memory_space=pl.ANY)] * len(outputs),
         ],
         out_specs=[pl.BlockSpec((tile, part), lambda i: (i, chunk))] * 2,
         out_shape=[shape, shape],
-        input_output_aliases={1 + i: i for i in range(len(outputs))},
+        input_output_aliases={3 + i: i for i in range(len(outputs))},
         compiler_params=pltpu.CompilerParams(vmem_limit_bytes=vmem_bytes),
         name="finish",
-    )(parts, *outputs)
+    )(keep, received, last, *outputs)
+
+
+def across(block, stage):
+    owners, places = lax.axis_size("kv"), lax.axis_size("seq")
+    route = []
+    for owner in range(owners):
+        for place in range(places):
+            flip = 1 + (place + stage) % CORES
+            route.append((owner * places + place, (owner ^ flip) * places + place))
+    return lax.ppermute(block, ("kv", "seq"), route)
 
 
 def along(block, chips):
@@ -242,45 +266,37 @@
     return lax.optimization_barrier(trees)
 
 
-class Gather:
-    def __init__(self, mine, chips):
-        self.blocks = {0: mine}
-        self.others = {}
-        self.chips = chips
-        self.forward, self.backward = chips // 2, (chips - 1) // 2
-
-    def ahead(self):
-        if self.forward:
-            self.blocks[1] = along(self.blocks[0], 1)
-
-    def behind(self):
-        if self.backward:
-            self.blocks[self.chips - 1] = along(self.blocks[0], -1)
-
-    def farther_ahead(self):
-        for step in range(2, self.forward + 1):
-            self.blocks[step] = along(self.blocks[step - 1], 1)
-
-    def farther_behind(self):
-        for step in range(2, self.backward + 1):
-            self.blocks[self.chips - step] = along(self.blocks[self.chips - step + 1], -1)
-
-    def exchange(self, *steps):
-        for step in steps or range(1, self.chips):
-            if step % self.chips in self.blocks and step % self.chips not in self.others:
-                self.others[step % self.chips] = other_core(self.blocks[step % self.chips])
-
-    def get(self):
-        return self.blocks, self.others
-
-    def put(self, state):
-        self.blocks, self.others = (dict(part) for part in state)
-
-    def pieces(self):
-        pieces = [self.blocks[0]]
-        for step in range(1, self.chips):
-            pieces += [self.blocks[step], self.others[step]]
-        return pieces
+class Pieces:
+    def __init__(self):
+        self.arrays, self.near, self.far = [], {}, {}
+
+    def add(self, table, members, array):
+        for index, member in enumerate(members):
+            table[member] = (len(self.arrays), index)
+        self.arrays.append(array)
+
+    def send(self, members, direction, chips):
+        blocks = [
+            self.arrays[which][index : index + 1]
+            for which, index in (self.near[member] for member in members)
+        ]
+        block = jnp.concatenate(blocks) if len(blocks) > 1 else blocks[0]
+        moved = [(chunk, (step + direction) % chips) for chunk, step in members]
+        self.add(self.near, moved, along(block, direction))
+
+    def exchange(self):
+        waiting = {}
+        for member, (which, index) in self.near.items():
+            if member[1] and member not in self.far:
+                waiting.setdefault(which, []).append((index, member))
+        for which, members in waiting.items():
+            members = [member for _, member in sorted(members)]
+            self.add(self.far, members, other_core(self.arrays[which]))
+
+    def taken(self, chunk, chips):
+        members = [self.near[chunk, step] for step in range(1, chips)]
+        others = [self.far[chunk, step] for step in range(1, chips)]
+        return [piece for pair in zip(members, others) for piece in pair]
 
 
 def body(
@@ -291,15 +307,21 @@
     heads = width // head_dim
     half = tokens // 2
     seq_index = lax.axis_index("seq")
+    kv_index = lax.axis_index("kv")
     seq_size = lax.axis_size("seq")
     chips = seq_size // CORES
 
     owners = lax.axis_size("kv")
-    whole, *mine = arrange(owners, weight_tangent, out_weight)
-    gathers = [Gather(block, chips) for block in mine]
-    gathers[0].behind()
-    gathers[0].ahead()
-    whole = other_core(whole)
+    core = seq_index % CORES
+    flips = jnp.stack([1 + core, 3 + 0 * core, 2 - core, 0 * core])
+    places_order = (kv_index ^ flips).astype(jnp.int32)
+    mine = arrange(owners, weight_tangent, out_weight)
+    pieces = Pieces()
+    for chunk in range(CHUNKS):
+        pieces.add(pieces.near, [(chunk, 0)], mine[chunk])
+    pieces.send([(0, 0)], -1, chips)
+    pieces.send([(0, 0)], 1, chips)
+    other_tangent, other_value = other_core(weight_tangent), other_core(out_weight)
 
     key_value, key_value_tangents, _ = lax.optimization_barrier(
         (key_value, key_value_tangents, mine[0])
@@ -322,7 +344,7 @@
     low = jnp.broadcast_to(low[:, None], (tokens, 128))
 
     step = jnp.arange(chips, dtype=jnp.int32)
-    chip, core = seq_index // CORES, seq_index % CORES
+    chip = seq_index // CORES
     owner = (chip - step + chips) % chips * CORES
     order = jnp.stack([owner + core, owner + 1 - core], axis=1).reshape(-1)
     whole_heads = order.shape[0] == heads
@@ -335,40 +357,60 @@
             pair = pair.reshape(half, 2 * width)
         return pair
 
+    forward, backward = chips // 2, (chips - 1) // 2
+    columns = out_weight.shape[1] // CHUNKS
+    part = columns // owners
+
+    def hop(chunk):
+        first = [(chunk, 1)] if chunk < CHUNKS else []
+        if chunk and first:
+            pieces.send([(chunk, 0)], -1, chips)
+        following = [(chunk + 1, 0)] if chunk + 1 < CHUNKS else []
+        if first + following:
+            pieces.send(first + following, 1, chips)
+        for step in range(2, forward if first else 0):
+            pieces.send([(chunk, step)], 1, chips)
+        for step in range(1, backward if first else 0):
+            pieces.send([(chunk, chips - step)], -1, chips)
+
+    def add_stage(keep, received):
+        return (keep[:, :, :part] + received[:, :, part:]).astype(jnp.bfloat16)
+
     pair_second = attend(1, stacked)
-    state, held, pair_second, prior = together(
-        gathers[0].get(), gathers[1].blocks, pair_second, prior
-    )
-    gathers[0].put(state)
-    gathers[1].blocks = dict(held)
-    gathers[0].farther_ahead()
-    gathers[0].farther_behind()
-    gathers[0].exchange(1, -1)
-    gathers[1].ahead()
+    pieces.arrays, pair_second, prior = together(pieces.arrays, pair_second, prior)
+    pieces.exchange()
+    hop(0)
     pair_first = attend(0, jnp.concatenate([prior, stacked[:half]], axis=0))
 
-    pairs, sent = (pair_first, pair_second), ()
-    received, outputs = [], ()
+    pairs, send, sums = (pair_first, pair_second), (), ()
+    raw = (weight_tangent, out_weight, other_tangent, other_value)
+    kept, received, last, outputs = [], [], [], ()
     for chunk in range(CHUNKS):
-        states = [gathering.get() for gathering in gathers]
-        arrived = received[chunk - 2] if chunk >= 2 else ()
-        states, pairs, whole, arrived, sent = together(states, pairs, whole, arrived, sent)
-        for gathering, state in zip(gathers, states):
-            gathering.put(state)
+        pieces.arrays, pairs, raw, send, sums = together(pieces.arrays, pairs, raw, send, sums)
+        pieces.exchange()
         if chunk + 1 < CHUNKS:
-            gathers[chunk + 1].behind()
-            gathers[chunk + 1].farther_ahead()
-            gathers[chunk + 1].farther_behind()
-            gathers[chunk + 1].exchange(1)
-        if chunk + 2 < CHUNKS:
-            gathers[chunk + 2].ahead()
-        gathers[chunk].exchange()
-        sent = project(owners, chunk, pairs, whole, gathers[chunk].pieces())
-        received.append(lax.all_to_all(sent, "kv", 0, 0, tiled=True))
+            hop(chunk + 1)
+        places = [(0, 0, 0), (0, 2, 0)] + [
+            (1, 4 + place, index)
+            for place, (_, index) in enumerate(pieces.taken(chunk, chips))
+        ]
+        arrays = [pieces.arrays[which] for which, _ in pieces.taken(chunk, chips)]
         if chunk >= 2:
-            outputs = finish(chunk - 2, outputs, arrived)
+            last[chunk - 2], pairs = together(last[chunk - 2], pairs)
+        send, keep = project(chunk, places, places_order, pairs, (*raw, *arrays), columns)
+        kept.append(keep)
+        received.append(across(send, 0))
+        if chunk:
+            received[chunk - 1], send = together(received[chunk - 1], send)
+            sums = add_stage(kept[chunk - 1], received[chunk - 1])
+            last.append(across(sums, 1))
+            if chunk >= 2:
+                outputs = finish(
+                    chunk - 2, outputs, kept[chunk - 2], received[chunk - 2], last[chunk - 2]
+                )
+    last.append(across(add_stage(kept[-1], received[-1]), 1))
     for chunk in range(max(CHUNKS - 2, 0), CHUNKS):
-        outputs = finish(chunk, outputs, received[chunk])
+        outputs = finish(chunk, outputs, kept[chunk], received[chunk], last[chunk])
     return tuple(outputs)
 
 

time: 184 us -> 157 us (0.85)
  waiting for transfers between devices: 79.1 us -> 57.8 us
  Pallas kernels: 37.1 us -> 49.6 us
  local copies, waits for them, and re-layouts: 26.2 us -> 16.1 us
  starting transfers between devices: 37.8 us -> 28.9 us
    ppermute x0 -> x8, waiting for transfers between devices: none -> 32.4 us  [across(): return lax.ppermute(block, ('kv', 'seq'), route)]
    ppermute x12 -> x9, waiting for transfers between devices: 54.9 us -> 24.7 us  [along(): lax.ppermute(block, 'seq', [(i, (i + CORES * chips) % size) for i in rang...]
    all_to_all x4 -> x0, waiting for transfers between devices: 18.4 us -> none  [body(): received.append(lax.all_to_all(sent, 'kv', 0, 0, tiled=True))]
    all_to_all x4 -> x0, starting transfers between devices: 17 us -> none  [body(): received.append(lax.all_to_all(sent, 'kv', 0, 0, tiled=True))]
    unnamed x58 -> x40, local copies, waits for them, and re-layouts: 23.8 us -> 11.6 us
    ppermute x0 -> x8, starting transfers between devices: none -> 8.82 us  [across(): return lax.ppermute(block, ('kv', 'seq'), route)]
    pallas_call x4, Pallas kernels: 18.4 us -> 26.4 us  [project(): pl.pallas_call(functools.partial(project_kernel, chunk, places), grid=(2...]
    pallas_call x1, Pallas kernels: 1.41 us -> 9.37 us  [arrange(): pl.pallas_call(functools.partial(arrange_kernel, owners), in_specs=[pl.Bl...]
  transfers between devices with their start and end apart: 30 -> 29, of which waited for: 19 -> 10; matrix products, arithmetic and copies ran while one was open for 2% -> 5% of each run, Pallas kernels for 16% -> 25%
where the time goes in v7:
time: 157 us; the launch traced here: 156 us
  waiting for transfers between devices  57.8 us (37%)
  Pallas kernels  49.6 us (32%)
  starting transfers between devices  28.9 us (18%)
  local copies, waits for them, and re-layouts  16.1 us (10%)
  other arithmetic  2.98 us (2%)
    ppermute x8, waiting for transfers between devices, across(): return lax.ppermute(block, ('kv', 'seq'), route)  32.4 us
    pallas_call x4, Pallas kernels, project(): pl.pallas_call(functools.partial(project_kernel, chunk, places), grid=(2...  26.4 us
    ppermute x9, waiting for transfers between devices, along(): lax.ppermute(block, 'seq', [(i, (i + CORES * chips) % size) for i in rang...  24.7 us
    ppermute x9, starting transfers between devices, along(): lax.ppermute(block, 'seq', [(i, (i + CORES * chips) % size) for i in rang...  14.9 us
    unnamed x40, local copies, waits for them, and re-layouts  11.6 us
    pallas_call x2, Pallas kernels, attention(): pl.pallas_call(functools.partial(attention_kernel, heads, head_dim, offse...  9.53 us
    pallas_call x1, Pallas kernels, arrange(): pl.pallas_call(functools.partial(arrange_kernel, owners), in_specs=[pl.Bl...  9.37 us
    ppermute x8, starting transfers between devices, across(): return lax.ppermute(block, ('kv', 'seq'), route)  8.82 us
  transfers between devices with their start and end apart: 29, of which 10 were waited for; matrix products, arithmetic and copies ran while one was open for 5% of the time, Pallas kernels for 25%

profile of v7, /device:TPU:0, one launch (start us, length us, event | category | flops | bytes accessed | tf_op | source)
XLA Modules:
  0.0 156.3 jit_solution(15102216241295198687)
XLA Ops:
  0.6 9.4 %arrange.1 = (bf16[1,2,128,512]{3,2,1,0:T(8,128)(2,1)}, bf16[1,2,128,512]{3,2,1,0:T(8,128)(2,1)S(1)}, bf16[1,2,128,512]{3,2,1,0:T(8,128)(2,1)S(1)}, bf16[1,2,128,512]{3,2,1,0:T(8,128)(2,1)S(1)}) custom-call(bf16[128,2048]{1,0:T(8,128)(2,1)} %refs_0_.3, bf16[128,2048]{1,0:T(8,128)(2,1)} %refs_1_.3), custom_call_target="tpu_custom_call" | custom-call | tf_op jit(solution)/shard_map/arrange/pallas_call | solution.py:40
  10.0 5.1 %collective-permute-start = (bf16[1,2,128,512]{3,2,1,0:T(8,128)(2,1)}, bf16[1,2,128,512]{3,2,1,0:T(8,128)(2,1)}, u32[]{:S(2)}, u32[]{:S(2)}) collective-permute-start(bf16[1,2,128,512]{3,2,1,0:T(8,128)(2,1)} %get-tuple-element.85), channel_id=1, source_target_pairs={{0,6},{1,7},{2,0},{3,1},{4,2},{5,3},{6,4},{7,5},{8,14},{9,15},{10,... | collective-permute-start | bytes 786440 | tf_op jit(solution)/shard_map/ppermute | solution.py:258
  15.7 1.1 copy.25
  17.1 0.7 slice.72
  17.8 1.0 copy-done.4
  18.8 2.6 %collective-permute-start.2 = (bf16[224,512]{1,0:T(8,128)(2,1)}, bf16[224,512]{1,0:T(8,128)(2,1)}, u32[]{:S(2)}, u32[]{:S(2)}) collective-permute-start(bf16[224,512]{1,0:T(8,128)(2,1)} %slice.72), channel_id=1, source_target_pairs={{0,1},{1,2},{2,3},{3,4},{4,5},{5,6},{6,7},{8,9},{9,10},{10,11},{11... | collective-permute-start | bytes 688136 | tf_op jit(solution)/shard_map/ppermute | solution.py:333
  22.2 1.6 %copy-done.2 = bf16[1024,1024]{1,0:T(8,128)(2,1)S(1)} copy-done((bf16[1024,1024]{1,0:T(8,128)(2,1)S(1)}, bf16[1024,1024]{1,0:T(8,128)(2,1)}, u32[]{:S(2)}) %copy-start.2) | copy-done | bytes 2097176
  23.8 1.6 %copy-done.3 = bf16[1024,1024]{1,0:T(8,128)(2,1)S(1)} copy-done((bf16[1024,1024]{1,0:T(8,128)(2,1)S(1)}, bf16[1024,1024]{1,0:T(8,128)(2,1)}, u32[]{:S(2)}) %copy-start.3) | copy-done | bytes 2097176
  25.4 1.2 copy-done.5
  26.7 4.8 %attention.2.second_ref = bf16[512,2048]{1,0:T(8,128)(2,1)S(1)} custom-call(s32[8]{0:T(128)S(1)} %reshape.115.order_ref, bf16[1024,1024]{1,0:T(8,128)(2,1)S(1)} %copy-done.2, bf16[1024,1024]{1,0:T(8,128)(2,1)S(1)} %copy-done.3, bf16[1024,512]{1,0:T(8,128)(2,1)S(1)} %copy-done.5, s32[1024,128]{1,0:T(8,128)S(1)} %broadcast_in_dim.13.low_ref), custom_call_target="tpu_custom_call" | custom-call | flops 1048576 | bytes 512 | tf_op jit(solution)/shard_map/attention/pallas_call | solution.py:124
  32.5 1.0 pad_maximum_fusion.1.ctx_ref
  33.5 4.8 %attention.3.first_ref = bf16[512,2048]{1,0:T(8,128)(2,1)S(1)} custom-call(s32[8]{0:T(128)S(1)} %reshape.115.order_ref, bf16[1024,1024]{1,0:T(8,128)(2,1)S(1)} %copy-done.2, bf16[1024,1024]{1,0:T(8,128)(2,1)S(1)} %copy-done.3, bf16[736,512]{1,0:T(8,128)(2,1)S(1)} %pad_maximum_fusion.1.ctx_ref, s32[1024,128]{1,0:T(8,128)S(1)} %broadcast_in_dim.13.low_ref), custom_call_target="tpu_custom_call" | custom-call | flops 1048576 | bytes 512 | tf_op jit(solution)/shard_map/attention/pallas_call | solution.py:124
  38.3 1.3 copy-done
  39.6 0.7 copy-done.6
  40.3 0.7 copy-done.8
  41.0 5.8 %collective-permute-done.5.refs_6_.refs_4_ = bf16[2,2,128,512]{3,2,1,0:T(8,128)(2,1)} collective-permute-done((bf16[2,2,128,512]{3,2,1,0:T(8,128)(2,1)S(1)}, bf16[2,2,128,512]{3,2,1,0:T(8,128)(2,1)}, u32[]{:S(2)}, u32[]{:S(2)}) %collective-permute-start.5) | collective-permute-done | bytes 524320 | tf_op jit(solution)/shard_map/ppermute | solution.py:258
  46.8 1.0 slice.57
  47.7 0.8 pad_maximum_fusion.3
  49.0 1.6 %copy-done.1 = bf16[512,2048]{1,0:T(8,128)(2,1)S(1)} copy-done((bf16[512,2048]{1,0:T(8,128)(2,1)S(1)}, bf16[512,2048]{1,0:T(8,128)(2,1)}, u32[]{:S(2)}) %copy-start.1) | copy-done | bytes 2097176
  50.6 0.9 copy-done.7
  51.6 0.9 copy-done.9
  52.5 6.8 %project.4 = (bf16[2,1024,256]{2,1,0:T(8,128)(2,1)S(1)}, f32[2,1024,256]{2,1,0:T(8,128)S(1)}) custom-call(s32[4]{0:T(128)S(1)} %add_xor_fusion.place_ref, bf16[512,2048]{1,0:T(8,128)(2,1)S(1)} %copy-done.1, bf16[512,2048]{1,0:T(8,128)(2,1)S(1)} %attention.2.second_ref, bf16[128,2048]{1,0:T(8,128)(2,1)} %refs_0_.3, bf16[128,2048]{1,0:T(8,128)(2,1)} %refs_1_.3, ...), custom_call_target="tpu_custom_call" | custom-call | flops 262144 | bytes 512 | tf_op jit(solution)/shard_map/project/pallas_call | solution.py:197
  59.3 1.6 collective-permute-start.14
  60.9 3.5 %collective-permute-start.9 = (bf16[1,2,128,512]{3,2,1,0:T(8,128)(2,1)S(1)}, bf16[1,2,128,512]{3,2,1,0:T(8,128)(2,1)S(1)}, u32[]{:S(2)}, u32[]{:S(2)}) collective-permute-start(bf16[1,2,128,512]{3,2,1,0:T(8,128)(2,1)S(1)} %copy-done.17), channel_id=1, source_target_pairs={{0,6},{1,7},{2,0},{3,1},{4,2},{5,3},{6,4},{7,5},{8,14},{9,15},{10,... | collective-permute-start | bytes 786440 | tf_op jit(solution)/shard_map/ppermute | solution.py:258
  64.4 6.2 %collective-permute-done.9.refs_8_ = bf16[1,2,128,512]{3,2,1,0:T(8,128)(2,1)S(1)} collective-permute-done((bf16[1,2,128,512]{3,2,1,0:T(8,128)(2,1)S(1)}, bf16[1,2,128,512]{3,2,1,0:T(8,128)(2,1)S(1)}, u32[]{:S(2)}, u32[]{:S(2)}) %collective-permute-start.9) | collective-permute-done | bytes 262176 | tf_op jit(solution)/shard_map/ppermute | solution.py:258
  71.1 1.0 slice.61
  72.1 0.6 collective-permute-start.17
  73.0 6.7 %project.5 = (bf16[2,1024,256]{2,1,0:T(8,128)(2,1)S(1)}, f32[2,1024,256]{2,1,0:T(8,128)S(1)}) custom-call(s32[4]{0:T(128)S(1)} %add_xor_fusion.place_ref, bf16[512,2048]{1,0:T(8,128)(2,1)S(1)} %copy-done.1, bf16[512,2048]{1,0:T(8,128)(2,1)S(1)} %attention.2.second_ref, bf16[128,2048]{1,0:T(8,128)(2,1)} %refs_0_.3, bf16[128,2048]{1,0:T(8,128)(2,1)} %refs_1_.3, ...), custom_call_target="tpu_custom_call" | custom-call | flops 262144 | bytes 512 | tf_op jit(solution)/shard_map/project/pallas_call | solution.py:197
  79.7 1.4 collective-permute-start.13
  81.1 3.8 %collective-permute-start.16 = (bf16[1,2,128,512]{3,2,1,0:T(8,128)(2,1)S(1)}, bf16[1,2,128,512]{3,2,1,0:T(8,128)(2,1)S(1)}, u32[]{:S(2)}, u32[]{:S(2)}) collective-permute-start(bf16[1,2,128,512]{3,2,1,0:T(8,128)(2,1)S(1)} %copy-done.14), channel_id=1, source_target_pairs={{0,6},{1,7},{2,0},{3,1},{4,2},{5,3},{6,4},{7,5},{8,14},{9,15},{10,... | collective-permute-start | bytes 786440 | tf_op jit(solution)/shard_map/ppermute | solution.py:258
  85.0 0.9 collective-permute-start.15
  85.9 7.8 %collective-permute-done.16.refs_8_ = bf16[1,2,128,512]{3,2,1,0:T(8,128)(2,1)S(1)} collective-permute-done((bf16[1,2,128,512]{3,2,1,0:T(8,128)(2,1)S(1)}, bf16[1,2,128,512]{3,2,1,0:T(8,128)(2,1)S(1)}, u32[]{:S(2)}, u32[]{:S(2)}) %collective-permute-start.16) | collective-permute-done | bytes 262176 | tf_op jit(solution)/shard_map/ppermute | solution.py:258
  94.8 4.5 %collective-permute-done.15.last_ref = bf16[2,1024,128]{2,1,0:T(8,128)(2,1)S(1)} collective-permute-done((bf16[2,1024,128]{2,1,0:T(8,128)(2,1)S(1)}, bf16[2,1024,128]{2,1,0:T(8,128)(2,1)S(1)}, u32[]{:S(2)}, u32[]{:S(2)}) %collective-permute-start.15) | collective-permute-done | bytes 524320 | tf_op jit(solution)/shard_map/ppermute | solution.py:253
  99.4 6.5 %project.6 = (bf16[2,1024,256]{2,1,0:T(8,128)(2,1)S(1)}, f32[2,1024,256]{2,1,0:T(8,128)S(1)}) custom-call(s32[4]{0:T(128)S(1)} %add_xor_fusion.place_ref, bf16[512,2048]{1,0:T(8,128)(2,1)S(1)} %copy-done.1, bf16[512,2048]{1,0:T(8,128)(2,1)S(1)} %attention.2.second_ref, bf16[128,2048]{1,0:T(8,128)(2,1)} %refs_0_.3, bf16[128,2048]{1,0:T(8,128)(2,1)} %refs_1_.3, ...), custom_call_target="tpu_custom_call" | custom-call | flops 262144 | bytes 512 | tf_op jit(solution)/shard_map/project/pallas_call | solution.py:197
  106.0 1.5 collective-permute-start.20
  107.5 1.0 collective-permute-start.21
  109.1 5.0 %collective-permute-done.21.refs_8_ = bf16[1,2,128,512]{3,2,1,0:T(8,128)(2,1)S(1)} collective-permute-done((bf16[1,2,128,512]{3,2,1,0:T(8,128)(2,1)S(1)}, bf16[1,2,128,512]{3,2,1,0:T(8,128)(2,1)S(1)}, u32[]{:S(2)}, u32[]{:S(2)}) %collective-permute-start.21) | collective-permute-done | bytes 262176 | tf_op jit(solution)/shard_map/ppermute | solution.py:258
  114.6 6.3 %collective-permute-done.20.last_ref = bf16[2,1024,128]{2,1,0:T(8,128)(2,1)S(1)} collective-permute-done((bf16[2,1024,128]{2,1,0:T(8,128)(2,1)S(1)}, bf16[2,1024,128]{2,1,0:T(8,128)(2,1)S(1)}, u32[]{:S(2)}, u32[]{:S(2)}) %collective-permute-start.20) | collective-permute-done | bytes 524320 | tf_op jit(solution)/shard_map/ppermute | solution.py:253
  120.9 6.4 %project.7 = (bf16[2,1024,256]{2,1,0:T(8,128)(2,1)S(1)}, f32[2,1024,256]{2,1,0:T(8,128)S(1)}) custom-call(s32[4]{0:T(128)S(1)} %add_xor_fusion.place_ref, bf16[512,2048]{1,0:T(8,128)(2,1)S(1)} %copy-done.1, bf16[512,2048]{1,0:T(8,128)(2,1)S(1)} %attention.2.second_ref, bf16[128,2048]{1,0:T(8,128)(2,1)} %refs_0_.3, bf16[128,2048]{1,0:T(8,128)(2,1)} %refs_1_.3, ...), custom_call_target="tpu_custom_call" | custom-call | flops 262144 | bytes 512 | tf_op jit(solution)/shard_map/project/pallas_call | solution.py:197
  127.3 1.4 collective-permute-start.25
  128.8 0.6 collective-permute-start.28
  129.5 16.4 %collective-permute-done.25.received_ref = bf16[2,1024,256]{2,1,0:T(8,128)(2,1)S(1)} collective-permute-done((bf16[2,1024,256]{2,1,0:T(8,128)(2,1)S(1)}, bf16[2,1024,256]{2,1,0:T(8,128)(2,1)S(1)}, u32[]{:S(2)}, u32[]{:S(2)}) %collective-permute-start.25) | collective-permute-done | bytes 1048608 | tf_op jit(solution)/shard_map/ppermute | solution.py:253
  146.0 0.9 collective-permute-start.26
  146.9 1.1 finish.4
  147.9 1.1 finish.5
  149.0 1.1 finish.6
  150.1 5.2 %collective-permute-done.26.last_ref = bf16[2,1024,128]{2,1,0:T(8,128)(2,1)S(1)} collective-permute-done((bf16[2,1024,128]{2,1,0:T(8,128)(2,1)S(1)}, bf16[2,1024,128]{2,1,0:T(8,128)(2,1)S(1)}, u32[]{:S(2)}, u32[]{:S(2)}) %collective-permute-start.26) | collective-permute-done | bytes 524320 | tf_op jit(solution)/shard_map/ppermute | solution.py:253
  155.2 1.1 finish.7
  (91 shorter events, 6.6 us)
Async XLA Ops:
  0.6 16.1 %copy-start.18 = (bf16[1024,2,128]{2,1,0:T(2,128)(2,1)S(1)}, bf16[1024,2,128]{2,1,0:T(2,128)(2,1)}, u32[]{:S(2)}) copy-start(bf16[1024,2,128]{2,1,0:T(2,128)(2,1)} %param.10) | copy-start | bytes 1572868
  10.0 6.9 %copy-start.10 = (bf16[1,2,128,512]{3,2,1,0:T(8,128)(2,1)}, bf16[1,2,128,512]{3,2,1,0:T(8,128)(2,1)S(1)}, u32[]{:S(2)}) copy-start(bf16[1,2,128,512]{3,2,1,0:T(8,128)(2,1)S(1)} %get-tuple-element.143) | copy-start | bytes 786436
  10.0 6.9 %copy-start.12 = (bf16[1,2,128,512]{3,2,1,0:T(8,128)(2,1)}, bf16[1,2,128,512]{3,2,1,0:T(8,128)(2,1)S(1)}, u32[]{:S(2)}) copy-start(bf16[1,2,128,512]{3,2,1,0:T(8,128)(2,1)S(1)} %get-tuple-element.127) | copy-start | bytes 786436
  10.0 6.9 %copy-start.15 = (bf16[1,2,128,512]{3,2,1,0:T(8,128)(2,1)}, bf16[1,2,128,512]{3,2,1,0:T(8,128)(2,1)S(1)}, u32[]{:S(2)}) copy-start(bf16[1,2,128,512]{3,2,1,0:T(8,128)(2,1)S(1)} %get-tuple-element.98) | copy-start | bytes 786436
  10.0 21.4 %collective-permute-start = (bf16[1,2,128,512]{3,2,1,0:T(8,128)(2,1)}, bf16[1,2,128,512]{3,2,1,0:T(8,128)(2,1)}, u32[]{:S(2)}, u32[]{:S(2)}) collective-permute-start(bf16[1,2,128,512]{3,2,1,0:T(8,128)(2,1)} %get-tuple-element.85), channel_id=1, source_target_pairs={{0,6},{1,7},{2,0},{3,1},{4,2},{5,3},{6,4},{7,5},{8,14},{9,15},{10,... | collective-permute-start | bytes 786440 | tf_op jit(solution)/shard_map/ppermute | solution.py:258
  15.1 16.3 %collective-permute-start.1 = (bf16[1,2,128,512]{3,2,1,0:T(8,128)(2,1)}, bf16[1,2,128,512]{3,2,1,0:T(8,128)(2,1)S(1)}, u32[]{:S(2)}, u32[]{:S(2)}) collective-permute-start(bf16[1,2,128,512]{3,2,1,0:T(8,128)(2,1)} %get-tuple-element.85), channel_id=1, source_target_pairs={{0,2},{1,3},{2,4},{3,5},{4,6},{5,7},{6,0},{7,1},{8,10},{9,11},{10,... | collective-permute-start | bytes 786440 | tf_op jit(solution)/shard_map/ppermute | solution.py:258
  15.2 25.9 %collective-permute-start.6 = (bf16[128,2048]{1,0:T(8,128)(2,1)}, bf16[128,2048]{1,0:T(8,128)(2,1)S(1)}, u32[]{:S(2)}, u32[]{:S(2)}) collective-permute-start(bf16[128,2048]{1,0:T(8,128)(2,1)} %refs_0_.3), channel_id=1, source_target_pairs={{0,1},{1,0},{2,3},{3,2},{4,5},{5,4},{6,7},{7,6},{8,9},{9,8},{10,11... | collective-permute-start | bytes 1572872 | tf_op jit(solution)/shard_map/ppermute | solution.py:262
  15.2 25.9 %collective-permute-start.7 = (bf16[128,2048]{1,0:T(8,128)(2,1)}, bf16[128,2048]{1,0:T(8,128)(2,1)S(1)}, u32[]{:S(2)}, u32[]{:S(2)}) collective-permute-start(bf16[128,2048]{1,0:T(8,128)(2,1)} %refs_1_.3), channel_id=1, source_target_pairs={{0,1},{1,0},{2,3},{3,2},{4,5},{5,4},{6,7},{7,6},{8,9},{9,8},{10,11... | collective-permute-start | bytes 1572872 | tf_op jit(solution)/shard_map/ppermute | solution.py:262
  16.9 4.5 %copy-start.19 = (s32[64]{0:T(128)S(1)}, s32[64]{0:T(128)}, u32[]{:S(2)}) copy-start(s32[64]{0:T(128)} %param.11) | copy-start | bytes 772
  17.8 1.0 copy-start.4
  18.8 12.7 %collective-permute-start.2 = (bf16[224,512]{1,0:T(8,128)(2,1)}, bf16[224,512]{1,0:T(8,128)(2,1)}, u32[]{:S(2)}, u32[]{:S(2)}) collective-permute-start(bf16[224,512]{1,0:T(8,128)(2,1)} %slice.72), channel_id=1, source_target_pairs={{0,1},{1,2},{2,3},{3,4},{4,5},{5,6},{6,7},{8,9},{9,10},{10,11},{11... | collective-permute-start | bytes 688136 | tf_op jit(solution)/shard_map/ppermute | solution.py:333
  22.2 1.6 %copy-start.2 = (bf16[1024,1024]{1,0:T(8,128)(2,1)S(1)}, bf16[1024,1024]{1,0:T(8,128)(2,1)}, u32[]{:S(2)}) copy-start(bf16[1024,1024]{1,0:T(8,128)(2,1)} %q_ref.3) | copy-start | bytes 6291460
  23.8 1.6 %copy-start.3 = (bf16[1024,1024]{1,0:T(8,128)(2,1)S(1)}, bf16[1024,1024]{1,0:T(8,128)(2,1)}, u32[]{:S(2)}) copy-start(bf16[1024,1024]{1,0:T(8,128)(2,1)} %qt_ref.3) | copy-start | bytes 6291460
  25.4 1.2 copy-start.5
  26.7 4.8 %copy-start.16 = (bf16[1,2,128,512]{3,2,1,0:T(8,128)(2,1)S(1)}, bf16[1,2,128,512]{3,2,1,0:T(8,128)(2,1)}, u32[]{:S(2)}) copy-start(bf16[1,2,128,512]{3,2,1,0:T(8,128)(2,1)} %copy-done.15) | copy-start | bytes 786436
  31.4 1.0 slice-start
  31.5 15.2 %collective-permute-start.5 = (bf16[2,2,128,512]{3,2,1,0:T(8,128)(2,1)S(1)}, bf16[2,2,128,512]{3,2,1,0:T(8,128)(2,1)}, u32[]{:S(2)}, u32[]{:S(2)}) collective-permute-start(bf16[2,2,128,512]{3,2,1,0:T(8,128)(2,1)S(1)} %pad_maximum_fusion.2), channel_id=1, source_target_pairs={{0,2},{1,3},{2,4},{3,5},{4,6},{5,7},{6,0},{7,1},{8,10},{9,11},{10,... | collective-permute-start | bytes 1572872 | tf_op jit(solution)/shard_map/ppermute | solution.py:258
  31.8 7.8 %collective-permute-start.3 = (bf16[1,2,128,512]{3,2,1,0:T(8,128)(2,1)}, bf16[1,2,128,512]{3,2,1,0:T(8,128)(2,1)S(1)}, u32[]{:S(2)}, u32[]{:S(2)}) collective-permute-start(bf16[1,2,128,512]{3,2,1,0:T(8,128)(2,1)} %collective-permute-done.refs_8_), channel_id=1, source_target_pairs={{0,1},{1,0},{2,3},{3,2},{4,5},{5,4},{6,7},{7,6},{8,9},{9,8},{10,11... | collective-permute-start | bytes 786440 | tf_op jit(solution)/shard_map/ppermute | solution.py:262
  32.3 8.0 %collective-permute-start.4 = (bf16[1,2,128,512]{3,2,1,0:T(8,128)(2,1)S(1)}, bf16[1,2,128,512]{3,2,1,0:T(8,128)(2,1)S(1)}, u32[]{:S(2)}, u32[]{:S(2)}) collective-permute-start(bf16[1,2,128,512]{3,2,1,0:T(8,128)(2,1)S(1)} %collective-permute-done.1.refs_4_), channel_id=1, source_target_pairs={{0,1},{1,0},{2,3},{3,2},{4,5},{5,4},{6,7},{7,6},{8,9},{9,8},{10,11... | collective-permute-start | bytes 786440 | tf_op jit(solution)/shard_map/ppermute | solution.py:262
  33.5 14.3 %copy-start.13 = (bf16[1,2,128,512]{3,2,1,0:T(8,128)(2,1)S(1)}, bf16[1,2,128,512]{3,2,1,0:T(8,128)(2,1)}, u32[]{:S(2)}) copy-start(bf16[1,2,128,512]{3,2,1,0:T(8,128)(2,1)} %copy-done.12) | copy-start | bytes 786436
  38.2 1.3 copy-start
  46.8 2.3 %collective-permute-start.8 = (bf16[2,2,128,512]{3,2,1,0:T(8,128)(2,1)}, bf16[2,2,128,512]{3,2,1,0:T(8,128)(2,1)}, u32[]{:S(2)}, u32[]{:S(2)}) collective-permute-start(bf16[2,2,128,512]{3,2,1,0:T(8,128)(2,1)} %collective-permute-done.5.refs_6_.refs_4_), channel_id=1, source_target_pairs={{0,1},{1,0},{2,3},{3,2},{4,5},{5,4},{6,7},{7,6},{8,9},{9,8},{10,11... | collective-permute-start | bytes 1572872 | tf_op jit(solution)/shard_map/ppermute | solution.py:262
  48.6 22.0 %collective-permute-start.10 = (bf16[2,2,128,512]{3,2,1,0:T(8,128)(2,1)}, bf16[2,2,128,512]{3,2,1,0:T(8,128)(2,1)}, u32[]{:S(2)}, u32[]{:S(2)}) collective-permute-start(bf16[2,2,128,512]{3,2,1,0:T(8,128)(2,1)} %pad_maximum_fusion.3), channel_id=1, source_target_pairs={{0,2},{1,3},{2,4},{3,5},{4,6},{5,7},{6,0},{7,1},{8,10},{9,11},{10,... | collective-permute-start | bytes 1572872 | tf_op jit(solution)/shard_map/ppermute | solution.py:258
  49.0 1.6 %copy-start.1 = (bf16[512,2048]{1,0:T(8,128)(2,1)S(1)}, bf16[512,2048]{1,0:T(8,128)(2,1)}, u32[]{:S(2)}) copy-start(bf16[512,2048]{1,0:T(8,128)(2,1)} %copy-done) | copy-start | bytes 6291460
  50.6 0.9 copy-start.7
  51.6 0.9 copy-start.9
  52.5 8.4 %copy-start.17 = (bf16[1,2,128,512]{3,2,1,0:T(8,128)(2,1)S(1)}, bf16[1,2,128,512]{3,2,1,0:T(8,128)(2,1)}, u32[]{:S(2)}) copy-start(bf16[1,2,128,512]{3,2,1,0:T(8,128)(2,1)} %copy-done.15) | copy-start | bytes 786436
  52.5 19.5 %copy-start.11 = (bf16[1,2,128,512]{3,2,1,0:T(8,128)(2,1)S(1)}, bf16[1,2,128,512]{3,2,1,0:T(8,128)(2,1)}, u32[]{:S(2)}) copy-start(bf16[1,2,128,512]{3,2,1,0:T(8,128)(2,1)} %copy-done.10) | copy-start | bytes 786436
  59.3 25.6 %collective-permute-start.14 = (bf16[2,1024,256]{2,1,0:T(8,128)(2,1)S(1)}, bf16[2,1024,256]{2,1,0:T(8,128)(2,1)S(1)}, u32[]{:S(2)}, u32[]{:S(2)}) collective-permute-start(bf16[2,1024,256]{2,1,0:T(8,128)(2,1)S(1)} %get-tuple-element.112), channel_id=1, source_target_pairs={{0,8},{1,17},{2,10},{3,19},{4,12},{5,21},{6,14},{7,23},{8,0},{9,25... | collective-permute-start | bytes 3145736 | tf_op jit(solution)/shard_map/ppermute | solution.py:253
  60.9 9.6 %collective-permute-start.9 = (bf16[1,2,128,512]{3,2,1,0:T(8,128)(2,1)S(1)}, bf16[1,2,128,512]{3,2,1,0:T(8,128)(2,1)S(1)}, u32[]{:S(2)}, u32[]{:S(2)}) collective-permute-start(bf16[1,2,128,512]{3,2,1,0:T(8,128)(2,1)S(1)} %copy-done.17), channel_id=1, source_target_pairs={{0,6},{1,7},{2,0},{3,1},{4,2},{5,3},{6,4},{7,5},{8,14},{9,15},{10,... | collective-permute-start | bytes 786440 | tf_op jit(solution)/shard_map/ppermute | solution.py:258
  70.6 2.5 %collective-permute-start.11 = (bf16[2,2,128,512]{3,2,1,0:T(8,128)(2,1)}, bf16[2,2,128,512]{3,2,1,0:T(8,128)(2,1)S(1)}, u32[]{:S(2)}, u32[]{:S(2)}) collective-permute-start(bf16[2,2,128,512]{3,2,1,0:T(8,128)(2,1)} %collective-permute-done.10.refs_6_.refs_4_), channel_id=1, source_target_pairs={{0,1},{1,0},{2,3},{3,2},{4,5},{5,4},{6,7},{7,6},{8,9},{9,8},{10,11... | collective-permute-start | bytes 1572872 | tf_op jit(solution)/shard_map/ppermute | solution.py:262
  70.6 2.2 %collective-permute-start.12 = (bf16[1,2,128,512]{3,2,1,0:T(8,128)(2,1)S(1)}, bf16[1,2,128,512]{3,2,1,0:T(8,128)(2,1)S(1)}, u32[]{:S(2)}, u32[]{:S(2)}) collective-permute-start(bf16[1,2,128,512]{3,2,1,0:T(8,128)(2,1)S(1)} %collective-permute-done.9.refs_8_), channel_id=1, source_target_pairs={{0,1},{1,0},{2,3},{3,2},{4,5},{5,4},{6,7},{7,6},{8,9},{9,8},{10,11... | collective-permute-start | bytes 786440 | tf_op jit(solution)/shard_map/ppermute | solution.py:262
  72.1 9.0 %copy-start.14 = (bf16[1,2,128,512]{3,2,1,0:T(8,128)(2,1)S(1)}, bf16[1,2,128,512]{3,2,1,0:T(8,128)(2,1)}, u32[]{:S(2)}) copy-start(bf16[1,2,128,512]{3,2,1,0:T(8,128)(2,1)} %copy-done.12) | copy-start | bytes 786436
  72.1 21.6 %collective-permute-start.17 = (bf16[2,2,128,512]{3,2,1,0:T(8,128)(2,1)S(1)}, bf16[2,2,128,512]{3,2,1,0:T(8,128)(2,1)S(1)}, u32[]{:S(2)}, u32[]{:S(2)}) collective-permute-start(bf16[2,2,128,512]{3,2,1,0:T(8,128)(2,1)S(1)} %pad_maximum_fusion.4), channel_id=1, source_target_pairs={{0,2},{1,3},{2,4},{3,5},{4,6},{5,7},{6,0},{7,1},{8,10},{9,11},{10,... | collective-permute-start | bytes 1572872 | tf_op jit(solution)/shard_map/ppermute | solution.py:258
  79.7 26.2 %collective-permute-start.13 = (bf16[2,1024,256]{2,1,0:T(8,128)(2,1)S(1)}, bf16[2,1024,256]{2,1,0:T(8,128)(2,1)S(1)}, u32[]{:S(2)}, u32[]{:S(2)}) collective-permute-start(bf16[2,1024,256]{2,1,0:T(8,128)(2,1)S(1)} %get-tuple-element.124), channel_id=1, source_target_pairs={{0,8},{1,17},{2,10},{3,19},{4,12},{5,21},{6,14},{7,23},{8,0},{9,25... | collective-permute-start | bytes 3145736 | tf_op jit(solution)/shard_map/ppermute | solution.py:253
  81.1 12.6 %collective-permute-start.16 = (bf16[1,2,128,512]{3,2,1,0:T(8,128)(2,1)S(1)}, bf16[1,2,128,512]{3,2,1,0:T(8,128)(2,1)S(1)}, u32[]{:S(2)}, u32[]{:S(2)}) collective-permute-start(bf16[1,2,128,512]{3,2,1,0:T(8,128)(2,1)S(1)} %copy-done.14), channel_id=1, source_target_pairs={{0,6},{1,7},{2,0},{3,1},{4,2},{5,3},{6,4},{7,5},{8,14},{9,15},{10,... | collective-permute-start | bytes 786440 | tf_op jit(solution)/shard_map/ppermute | solution.py:258
  85.0 14.4 %collective-permute-start.15 = (bf16[2,1024,128]{2,1,0:T(8,128)(2,1)S(1)}, bf16[2,1024,128]{2,1,0:T(8,128)(2,1)S(1)}, u32[]{:S(2)}, u32[]{:S(2)}) collective-permute-start(bf16[2,1024,128]{2,1,0:T(8,128)(2,1)S(1)} %add_convert_fusion.3), channel_id=1, source_target_pairs={{0,16},{1,9},{2,18},{3,11},{4,20},{5,13},{6,22},{7,15},{8,24},{9,1... | collective-permute-start | bytes 1572872 | tf_op jit(solution)/shard_map/ppermute | solution.py:253
  93.7 5.7 %collective-permute-start.18 = (bf16[2,2,128,512]{3,2,1,0:T(8,128)(2,1)S(1)}, bf16[2,2,128,512]{3,2,1,0:T(8,128)(2,1)S(1)}, u32[]{:S(2)}, u32[]{:S(2)}) collective-permute-start(bf16[2,2,128,512]{3,2,1,0:T(8,128)(2,1)S(1)} %collective-permute-done.17.refs_6_.refs_4_), channel_id=1, source_target_pairs={{0,1},{1,0},{2,3},{3,2},{4,5},{5,4},{6,7},{7,6},{8,9},{9,8},{10,11... | collective-permute-start | bytes 1572872 | tf_op jit(solution)/shard_map/ppermute | solution.py:262
  93.7 5.6 %collective-permute-start.19 = (bf16[1,2,128,512]{3,2,1,0:T(8,128)(2,1)S(1)}, bf16[1,2,128,512]{3,2,1,0:T(8,128)(2,1)S(1)}, u32[]{:S(2)}, u32[]{:S(2)}) collective-permute-start(bf16[1,2,128,512]{3,2,1,0:T(8,128)(2,1)S(1)} %collective-permute-done.16.refs_8_), channel_id=1, source_target_pairs={{0,1},{1,0},{2,3},{3,2},{4,5},{5,4},{6,7},{7,6},{8,9},{9,8},{10,11... | collective-permute-start | bytes 786440 | tf_op jit(solution)/shard_map/ppermute | solution.py:262
  94.2 14.8 %collective-permute-start.22 = (bf16[1,2,128,512]{3,2,1,0:T(8,128)(2,1)S(1)}, bf16[1,2,128,512]{3,2,1,0:T(8,128)(2,1)S(1)}, u32[]{:S(2)}, u32[]{:S(2)}) collective-permute-start(bf16[1,2,128,512]{3,2,1,0:T(8,128)(2,1)S(1)} %slice.63), channel_id=1, source_target_pairs={{0,2},{1,3},{2,4},{3,5},{4,6},{5,7},{6,0},{7,1},{8,10},{9,11},{10,... | collective-permute-start | bytes 786440 | tf_op jit(solution)/shard_map/ppermute | solution.py:258
  106.0 14.8 %collective-permute-start.20 = (bf16[2,1024,128]{2,1,0:T(8,128)(2,1)S(1)}, bf16[2,1024,128]{2,1,0:T(8,128)(2,1)S(1)}, u32[]{:S(2)}, u32[]{:S(2)}) collective-permute-start(bf16[2,1024,128]{2,1,0:T(8,128)(2,1)S(1)} %add_convert_fusion.2), channel_id=1, source_target_pairs={{0,16},{1,9},{2,18},{3,11},{4,20},{5,13},{6,22},{7,15},{8,24},{9,1... | collective-permute-start | bytes 1572872 | tf_op jit(solution)/shard_map/ppermute | solution.py:253
  107.5 6.5 %collective-permute-start.21 = (bf16[1,2,128,512]{3,2,1,0:T(8,128)(2,1)S(1)}, bf16[1,2,128,512]{3,2,1,0:T(8,128)(2,1)S(1)}, u32[]{:S(2)}, u32[]{:S(2)}) collective-permute-start(bf16[1,2,128,512]{3,2,1,0:T(8,128)(2,1)S(1)} %copy-done.11), channel_id=1, source_target_pairs={{0,6},{1,7},{2,0},{3,1},{4,2},{5,3},{6,4},{7,5},{8,14},{9,15},{10,... | collective-permute-start | bytes 786440 | tf_op jit(solution)/shard_map/ppermute | solution.py:258
  108.5 20.2 %collective-permute-start.27 = (bf16[2,1024,256]{2,1,0:T(8,128)(2,1)S(1)}, bf16[2,1024,256]{2,1,0:T(8,128)(2,1)S(1)}, u32[]{:S(2)}, u32[]{:S(2)}) collective-permute-start(bf16[2,1024,256]{2,1,0:T(8,128)(2,1)S(1)} %get-tuple-element.141), channel_id=1, source_target_pairs={{0,8},{1,17},{2,10},{3,19},{4,12},{5,21},{6,14},{7,23},{8,0},{9,25... | collective-permute-start | bytes 3145736 | tf_op jit(solution)/shard_map/ppermute | solution.py:253
  114.0 6.8 %collective-permute-start.23 = (bf16[1,2,128,512]{3,2,1,0:T(8,128)(2,1)S(1)}, bf16[1,2,128,512]{3,2,1,0:T(8,128)(2,1)S(1)}, u32[]{:S(2)}, u32[]{:S(2)}) collective-permute-start(bf16[1,2,128,512]{3,2,1,0:T(8,128)(2,1)S(1)} %collective-permute-done.22.refs_6_), channel_id=1, source_target_pairs={{0,1},{1,0},{2,3},{3,2},{4,5},{5,4},{6,7},{7,6},{8,9},{9,8},{10,11... | collective-permute-start | bytes 786440 | tf_op jit(solution)/shard_map/ppermute | solution.py:262
  114.0 6.8 %collective-permute-start.24 = (bf16[1,2,128,512]{3,2,1,0:T(8,128)(2,1)S(1)}, bf16[1,2,128,512]{3,2,1,0:T(8,128)(2,1)S(1)}, u32[]{:S(2)}, u32[]{:S(2)}) collective-permute-start(bf16[1,2,128,512]{3,2,1,0:T(8,128)(2,1)S(1)} %collective-permute-done.21.refs_8_), channel_id=1, source_target_pairs={{0,1},{1,0},{2,3},{3,2},{4,5},{5,4},{6,7},{7,6},{8,9},{9,8},{10,11... | collective-permute-start | bytes 786440 | tf_op jit(solution)/shard_map/ppermute | solution.py:262
  127.3 18.6 %collective-permute-start.25 = (bf16[2,1024,256]{2,1,0:T(8,128)(2,1)S(1)}, bf16[2,1024,256]{2,1,0:T(8,128)(2,1)S(1)}, u32[]{:S(2)}, u32[]{:S(2)}) collective-permute-start(bf16[2,1024,256]{2,1,0:T(8,128)(2,1)S(1)} %get-tuple-element.157), channel_id=1, source_target_pairs={{0,8},{1,17},{2,10},{3,19},{4,12},{5,21},{6,14},{7,23},{8,0},{9,25... | collective-permute-start | bytes 3145736 | tf_op jit(solution)/shard_map/ppermute | solution.py:253
  128.8 20.2 %collective-permute-start.28 = (bf16[2,1024,128]{2,1,0:T(8,128)(2,1)S(1)}, bf16[2,1024,128]{2,1,0:T(8,128)(2,1)S(1)}, u32[]{:S(2)}, u32[]{:S(2)}) collective-permute-start(bf16[2,1024,128]{2,1,0:T(8,128)(2,1)S(1)} %add_convert_fusion), channel_id=1, source_target_pairs={{0,16},{1,9},{2,18},{3,11},{4,20},{5,13},{6,22},{7,15},{8,24},{9,1... | collective-permute-start | bytes 1572872 | tf_op jit(solution)/shard_map/ppermute | solution.py:253
  146.0 9.2 %collective-permute-start.26 = (bf16[2,1024,128]{2,1,0:T(8,128)(2,1)S(1)}, bf16[2,1024,128]{2,1,0:T(8,128)(2,1)S(1)}, u32[]{:S(2)}, u32[]{:S(2)}) collective-permute-start(bf16[2,1024,128]{2,1,0:T(8,128)(2,1)S(1)} %add_convert_fusion.1), channel_id=1, source_target_pairs={{0,16},{1,9},{2,18},{3,11},{4,20},{5,13},{6,22},{7,15},{8,24},{9,1... | collective-permute-start | bytes 1572872 | tf_op jit(solution)/shard_map/ppermute | solution.py:253
  (2 other events, 1.4 us)

commit v8 on v6

--- a/solution.py
+++ b/solution.py
@@ -11,37 +11,43 @@
 STRETCH = 32
 WINDOW = 224
 CHUNKS = 4
+SCHEDULED_GFLOPS = (5, 5, 1.5, 0.01)
 TILE = 128
 CORES = 2
 
 masked_score = -1e30
-vmem_bytes = 16 * 1024 * 1024
-
-
-def arrange_kernel(owners, tangent_ref, value_ref, whole_ref, *chunk_refs):
+vmem_bytes = 12 * 1024 * 1024
+
+
+def arrange_kernel(owner_ref, tangent_ref, value_ref, whole_ref, *chunk_refs):
+    owners = owner_ref.shape[0]
     columns = tangent_ref.shape[1] // owners
     part = columns // len(chunk_refs)
     for chunk, chunk_ref in enumerate(chunk_refs):
-        for owner in range(owners):
-            of = slice(owner * columns + chunk * part, owner * columns + (chunk + 1) * part)
-            to = slice(owner * part, (owner + 1) * part)
+        for place in range(owners):
+            start = pl.multiple_of(owner_ref[place] * columns + chunk * part, part)
+            to = slice(place * part, (place + 1) * part)
             for mat, ref in enumerate((tangent_ref, value_ref)):
-                whole_ref[chunk, mat, :, to] = ref[:, of]
-                chunk_ref[mat, :, to] = ref[:, of]
+                block = ref[:, pl.ds(start, part)]
+                whole_ref[chunk, mat, :, to] = block
+                chunk_ref[0, mat, :, to] = block
 
 
 def arrange(owners, tangent, value):
     rows, columns = value.shape
-    chunk = (2, rows, columns // CHUNKS)
-    shapes = [jax.ShapeDtypeStruct(shape, value.dtype) for shape in [(CHUNKS, *chunk)] + [chunk] * CHUNKS]
+    shapes = [
+        jax.ShapeDtypeStruct((count, 2, rows, columns // CHUNKS), value.dtype)
+        for count in [CHUNKS] + [1] * CHUNKS
+    ]
     return pl.pallas_call(
-        functools.partial(arrange_kernel, owners),
-        in_specs=[pl.BlockSpec(memory_space=pltpu.VMEM)] * 2,
+        arrange_kernel,
+        in_specs=[pl.BlockSpec(memory_space=pltpu.SMEM)]
+        + [pl.BlockSpec(memory_space=pltpu.VMEM)] * 2,
         out_specs=[pl.BlockSpec(memory_space=pltpu.VMEM)] * len(shapes),
         out_shape=shapes,
         compiler_params=pltpu.CompilerParams(vmem_limit_bytes=vmem_bytes),
         name="arrange",
-    )(tangent, value)
+    )(owners, tangent, value)
 
 
 def attention_kernel(heads, head_dim, offset, order_ref, q_ref, qt_ref, ctx_ref, low_ref, out_ref):
@@ -137,32 +143,41 @@
     )(order, queries, query_tangent, context, low)
 
 
-def project_kernel(chunk, first_ref, second_ref, whole_ref, *refs):
-    *piece_refs, send_ref, weight_ref, sems = refs
+def project_kernel(indices, first_ref, second_ref, *refs):
+    *piece_refs, send_ref, keep_ref, weight_ref, sems = refs
     step, steps = pl.program_id(0), pl.num_programs(0)
-    rows = whole_ref.shape[2]
-    depth = weight_ref.shape[1]
-    owners, _, _, part = send_ref.shape
-    sources = [piece_refs[0], whole_ref.at[chunk], *piece_refs[1:]]
+    width, columns = weight_ref.shape[1:]
+    rows = width // len(indices)
+    near = width // 2
+    part = columns // 4
 
     @pl.when(step == 0)
     def _():
         copies = []
-        for place, source in enumerate(sources):
-            to = weight_ref.at[:, pl.ds(place * rows, rows), :]
-            copies.append(pltpu.make_async_copy(source, to, sems.at[place]))
+        for place, (index, ref) in enumerate(zip(indices, piece_refs)):
+            target = weight_ref.at[:, pl.ds(place * rows, rows), :]
+            copies.append(pltpu.make_async_copy(ref.at[index], target, sems.at[place]))
             copies[-1].start()
         for copy in copies:
             copy.wait()
 
     def run(pair_ref):
         dot = functools.partial(jnp.dot, preferred_element_type=jnp.float32)
-        value = dot(pair_ref[:, :depth], weight_ref[1])
-        tangent = dot(pair_ref[:, :depth], weight_ref[0]) + dot(pair_ref[:, depth:], weight_ref[1])
-        for owner in range(owners):
-            of = slice(owner * part, (owner + 1) * part)
-            send_ref[owner, 0] = value[:, of].astype(send_ref.dtype)
-            send_ref[owner, 1] = tangent[:, of].astype(send_ref.dtype)
+
+        def products(mine, of):
+            return dot(pair_ref[:, mine], weight_ref[1, of]), dot(
+                pair_ref[:, mine], weight_ref[0, of]
+            ) + dot(pair_ref[:, slice(width + mine.start, width + mine.stop)], weight_ref[1, of])
+
+        here = products(slice(0, near), slice(0, near))
+        there = products(slice(near, width), slice(near, width))
+        for mat in range(2):
+            for place, crossed in enumerate((2, 1, 0, 3)):
+                to = slice(place * part, (place + 1) * part)
+                total = here[mat][:, to] + there[mat][:, crossed * part : (crossed + 1) * part]
+                ref = send_ref if place < 2 else keep_ref
+                at = place % 2 * part
+                ref[mat, :, at : at + part] = total.astype(ref.dtype)
 
     @pl.when(step < steps // 2)
     def _():
@@ -173,60 +188,72 @@
         run(second_ref)
 
 
-def project(owners, chunk, pairs, whole, pieces):
+def project(gflops, pairs, pieces):
     tokens, width = pairs[0].shape
     tile = min(2 * TILE, tokens)
     steps = tokens // tile
-    _, rows, columns = pieces[0].shape
-    part = columns // owners
-    count = len(pieces) + 1
+    indices = [index for index, _ in pieces]
+    arrays = [array for _, array in pieces]
+    columns = arrays[0].shape[3]
+    block = pl.BlockSpec((2, tile, columns // 2), lambda i: (0, i, 0))
+    out = jax.ShapeDtypeStruct((2, 2 * tokens, columns // 2), jnp.bfloat16)
     return pl.pallas_call(
-        functools.partial(project_kernel, chunk),
+        functools.partial(project_kernel, indices),
         grid=(2 * steps,),
         in_specs=[
             pl.BlockSpec((tile, width), lambda i: (jnp.minimum(i, steps - 1), 0)),
             pl.BlockSpec((tile, width), lambda i: (jnp.maximum(i - steps, 0), 0)),
-            *[pl.BlockSpec(memory_space=pl.ANY)] * count,
+            *[pl.BlockSpec(memory_space=pl.ANY)] * len(arrays),
         ],
-        out_specs=pl.BlockSpec((owners, 2, tile, part), lambda i: (0, 0, i, 0)),
-        out_shape=jax.ShapeDtypeStruct((owners, 2, 2 * tokens, part), jnp.bfloat16),
+        out_specs=[block, block],
+        out_shape=[out, out],
         scratch_shapes=[
-            pltpu.VMEM((2, rows * count, columns), jnp.bfloat16),
-            pltpu.SemaphoreType.DMA((count,)),
+            pltpu.VMEM((2, width // 2, columns), jnp.bfloat16),
+            pltpu.SemaphoreType.DMA((len(arrays),)),
         ],
         compiler_params=pltpu.CompilerParams(vmem_limit_bytes=vmem_bytes),
         cost_estimate=pl.CostEstimate(
-            flops=tokens * columns, bytes_accessed=tokens, transcendentals=0
+            flops=int(gflops * 1e9), bytes_accessed=tokens, transcendentals=0
         ),
         name="project",
-    )(*pairs, whole, *pieces)
-
-
-def finish_kernel(parts_ref, *refs):
+    )(*pairs, *arrays)
+
+
+def finish_kernel(keep_ref, received_ref, last_ref, *refs):
     for mat, ref in enumerate(refs[-2:]):
-        total = parts_ref[0, mat].astype(jnp.float32)
-        for owner in range(1, parts_ref.shape[0]):
-            total = total + parts_ref[owner, mat]
+        total = keep_ref[mat].astype(jnp.float32) + received_ref[mat] + last_ref[mat]
         ref[...] = total.astype(ref.dtype)
 
 
-def finish(chunk, outputs, parts):
-    owners, _, tokens, part = parts.shape
+def finish(chunk, outputs, keep, received, last):
+    _, tokens, part = last.shape
     shape = jax.ShapeDtypeStruct((tokens, part * CHUNKS), jnp.bfloat16)
     tile = tokens // 2
     return pl.pallas_call(
         finish_kernel,
         grid=(tokens // tile,),
         in_specs=[
-            pl.BlockSpec((owners, 2, tile, part), lambda i: (0, 0, i, 0)),
+            pl.BlockSpec((2, tile, part), lambda i: (0, i, 1)),
+            pl.BlockSpec((2, tile, part), lambda i: (0, i, 0)),
+            pl.BlockSpec((2, tile, part), lambda i: (0, i, 0)),
             *[pl.BlockSpec(memory_space=pl.ANY)] * len(outputs),
         ],
         out_specs=[pl.BlockSpec((tile, part), lambda i: (i, chunk))] * 2,
         out_shape=[shape, shape],
-        input_output_aliases={1 + i: i for i in range(len(outputs))},
+        input_output_aliases={3 + i: i for i in range(len(outputs))},
         compiler_params=pltpu.CompilerParams(vmem_limit_bytes=vmem_bytes),
         name="finish",
-    )(parts, *outputs)
+    )(keep, received, last, *outputs)
+
+
+def across(block, stage):
+    owners, places = lax.axis_size("kv"), lax.axis_size("seq")
+    route = []
+    for owner in range(owners):
+        for place in range(places):
+            flip = 1 + (place + stage) % CORES
+            route.append((owner * places + place, (owner ^ flip) * places + place))
+    return lax.ppermute(block, ("kv", "seq"), route)
 
 
 def along(block, chips):
@@ -244,43 +271,33 @@
 
 class Gather:
     def __init__(self, mine, chips):
-        self.blocks = {0: mine}
-        self.others = {}
+        self.near, self.far = {0: mine}, {}
         self.chips = chips
         self.forward, self.backward = chips // 2, (chips - 1) // 2
 
     def ahead(self):
         if self.forward:
-            self.blocks[1] = along(self.blocks[0], 1)
+            self.near[1] = along(self.near[0], 1)
 
     def behind(self):
         if self.backward:
-            self.blocks[self.chips - 1] = along(self.blocks[0], -1)
-
-    def farther_ahead(self):
+            self.near[self.chips - 1] = along(self.near[0], -1)
+
+    def farther(self):
         for step in range(2, self.forward + 1):
-            self.blocks[step] = along(self.blocks[step - 1], 1)
-
-    def farther_behind(self):
+            self.near[step] = along(self.near[step - 1], 1)
         for step in range(2, self.backward + 1):
-            self.blocks[self.chips - step] = along(self.blocks[self.chips - step + 1], -1)
-
-    def exchange(self, *steps):
-        for step in steps or range(1, self.chips):
-            if step % self.chips in self.blocks and step % self.chips not in self.others:
-                self.others[step % self.chips] = other_core(self.blocks[step % self.chips])
-
-    def get(self):
-        return self.blocks, self.others
-
-    def put(self, state):
-        self.blocks, self.others = (dict(part) for part in state)
-
-    def pieces(self):
-        pieces = [self.blocks[0]]
-        for step in range(1, self.chips):
-            pieces += [self.blocks[step], self.others[step]]
-        return pieces
+            self.near[self.chips - step] = along(self.near[self.chips - step + 1], -1)
+
+    def exchange(self):
+        for step in sorted(self.near):
+            if step and step not in self.far:
+                self.far[step] = other_core(self.near[step])
+
+    def pieces(self, chunk, whole):
+        near = [(0, self.near[step]) for step in range(self.chips)]
+        far = [(0, self.far[step]) for step in range(1, self.chips)]
+        return near + [(chunk, whole)] + far
 
 
 def body(
@@ -291,11 +308,13 @@
     heads = width // head_dim
     half = tokens // 2
     seq_index = lax.axis_index("seq")
+    kv_index = lax.axis_index("kv")
     seq_size = lax.axis_size("seq")
     chips = seq_size // CORES
 
-    owners = lax.axis_size("kv")
-    whole, *mine = arrange(owners, weight_tangent, out_weight)
+    core = seq_index % CORES
+    flips = jnp.stack([1 + core, 3 + 0 * core, 2 - core, 0 * core])
+    whole, *mine = arrange((kv_index ^ flips).astype(jnp.int32), weight_tangent, out_weight)
     gathers = [Gather(block, chips) for block in mine]
     gathers[0].behind()
     gathers[0].ahead()
@@ -322,9 +341,9 @@
     low = jnp.broadcast_to(low[:, None], (tokens, 128))
 
     step = jnp.arange(chips, dtype=jnp.int32)
-    chip, core = seq_index // CORES, seq_index % CORES
+    chip = seq_index // CORES
     owner = (chip - step + chips) % chips * CORES
-    order = jnp.stack([owner + core, owner + 1 - core], axis=1).reshape(-1)
+    order = jnp.concatenate([owner + core, owner + 1 - core])
     whole_heads = order.shape[0] == heads
 
     def attend(part, context):
@@ -335,40 +354,55 @@
             pair = pair.reshape(half, 2 * width)
         return pair
 
+    part = out_weight.shape[1] // CHUNKS // lax.axis_size("kv")
+
+    def add_stage(keep, received):
+        total = keep[:, :, :part].astype(jnp.float32) + received[:, :, part:]
+        return total.astype(jnp.bfloat16)
+
+    def settle(*others):
+        states = [(gathering.near, gathering.far) for gathering in gathers]
+        states, *others = together(states, *others)
+        for gathering, (near, far) in zip(gathers, states):
+            gathering.near, gathering.far = dict(near), dict(far)
+        return others
+
     pair_second = attend(1, stacked)
-    state, held, pair_second, prior = together(
-        gathers[0].get(), gathers[1].blocks, pair_second, prior
-    )
-    gathers[0].put(state)
-    gathers[1].blocks = dict(held)
-    gathers[0].farther_ahead()
-    gathers[0].farther_behind()
-    gathers[0].exchange(1, -1)
+    pair_second, prior = settle(pair_second, prior)
+    gathers[0].exchange()
+    gathers[0].farther()
     gathers[1].ahead()
     pair_first = attend(0, jnp.concatenate([prior, stacked[:half]], axis=0))
 
-    pairs, sent = (pair_first, pair_second), ()
-    received, outputs = [], ()
+    pairs, send, sums = (pair_first, pair_second), (), ()
+    kept, received, last, outputs = [], [], [], ()
     for chunk in range(CHUNKS):
-        states = [gathering.get() for gathering in gathers]
-        arrived = received[chunk - 2] if chunk >= 2 else ()
-        states, pairs, whole, arrived, sent = together(states, pairs, whole, arrived, sent)
-        for gathering, state in zip(gathers, states):
-            gathering.put(state)
+        pairs, whole, send, sums = settle(pairs, whole, send, sums)
+        gathers[chunk].exchange()
         if chunk + 1 < CHUNKS:
+            gathers[chunk + 1].exchange()
             gathers[chunk + 1].behind()
-            gathers[chunk + 1].farther_ahead()
-            gathers[chunk + 1].farther_behind()
-            gathers[chunk + 1].exchange(1)
+            gathers[chunk + 1].farther()
         if chunk + 2 < CHUNKS:
             gathers[chunk + 2].ahead()
-        gathers[chunk].exchange()
-        sent = project(owners, chunk, pairs, whole, gathers[chunk].pieces())
-        received.append(lax.all_to_all(sent, "kv", 0, 0, tiled=True))
-        if chunk >= 2:
-            outputs = finish(chunk - 2, outputs, arrived)
+        if 2 <= chunk < CHUNKS - 1:
+            last[chunk - 2], pairs = together(last[chunk - 2], pairs)
+        send, keep = project(
+            SCHEDULED_GFLOPS[chunk], pairs, gathers[chunk].pieces(chunk, whole)
+        )
+        kept.append(keep)
+        received.append(across(send, 0))
+        if chunk:
+            received[chunk - 1], send = together(received[chunk - 1], send)
+            sums = add_stage(kept[chunk - 1], received[chunk - 1])
+            last.append(across(sums, 1))
+            if chunk >= 2:
+                outputs = finish(
+                    chunk - 2, outputs, kept[chunk - 2], received[chunk - 2], last[chunk - 2]
+                )
+    last.append(across(add_stage(kept[-1], received[-1]), 1))
     for chunk in range(max(CHUNKS - 2, 0), CHUNKS):
-        outputs = finish(chunk, outputs, received[chunk])
+        outputs = finish(chunk, outputs, kept[chunk], received[chunk], last[chunk])
     return tuple(outputs)
 
 

time: 184 us -> 152 us (0.83)
  local copies, waits for them, and re-layouts: 26.2 us -> 5.99 us
  waiting for transfers between devices: 79.1 us -> 68.5 us
    ppermute x0 -> x8, waiting for transfers between devices: none -> 24.7 us  [across(): return lax.ppermute(block, ('kv', 'seq'), route)]
    unnamed x58 -> x20, local copies, waits for them, and re-layouts: 23.8 us -> 3.7 us
    all_to_all x4 -> x0, waiting for transfers between devices: 18.4 us -> none  [body(): received.append(lax.all_to_all(sent, 'kv', 0, 0, tiled=True))]
    all_to_all x4 -> x0, starting transfers between devices: 17 us -> none  [body(): received.append(lax.all_to_all(sent, 'kv', 0, 0, tiled=True))]
    ppermute x12, waiting for transfers between devices: 54.9 us -> 39.9 us  [along(): lax.ppermute(block, 'seq', [(i, (i + CORES * chips) % size) for i in rang...]
    ppermute x0 -> x8, starting transfers between devices: none -> 14.1 us  [across(): return lax.ppermute(block, ('kv', 'seq'), route)]
    pallas_call x4, Pallas kernels: 8.1 us -> 4.45 us  [finish(): pl.pallas_call(finish_kernel, grid=(tokens // tile,), in_specs=[pl.BlockS...]
    pallas_call x5, Pallas kernels: 19.8 us -> 23.1 us  [the longest x4 21.2 us: project(): pl.pallas_call(functools.partial(project_kernel, indices), grid=(2 * step...]
  transfers between devices with their start and end apart: 30 -> 34, of which waited for: 19 -> 15; matrix products, arithmetic and copies ran while one was open for 2% -> 3% of each run, Pallas kernels for 16% -> 22%
where the time goes in v8:
time: 152 us
  waiting for transfers between devices  68.5 us (45%)
  starting transfers between devices  37.3 us (25%)
  Pallas kernels  36.9 us (24%)
  local copies, waits for them, and re-layouts  5.99 us (4%)
  other arithmetic  2.18 us (1%)
    ppermute x12, waiting for transfers between devices, along(): lax.ppermute(block, 'seq', [(i, (i + CORES * chips) % size) for i in rang...  39.9 us
    ppermute x8, waiting for transfers between devices, across(): return lax.ppermute(block, ('kv', 'seq'), route)  24.7 us
    pallas_call x4, Pallas kernels, project(): pl.pallas_call(functools.partial(project_kernel, indices), grid=(2 * step...  21.2 us
    ppermute x12, starting transfers between devices, along(): lax.ppermute(block, 'seq', [(i, (i + CORES * chips) % size) for i in rang...  16.4 us
    ppermute x8, starting transfers between devices, across(): return lax.ppermute(block, ('kv', 'seq'), route)  14.1 us
    pallas_call x2, Pallas kernels, attention(): pl.pallas_call(functools.partial(attention_kernel, heads, head_dim, offse...  9.4 us
    pallas_call x4, Pallas kernels, finish(): pl.pallas_call(finish_kernel, grid=(tokens // tile,), in_specs=[pl.BlockS...  4.45 us
    ppermute x13, waiting for transfers between devices, other_core(): lax.ppermute(block, 'seq', [(i, i ^ 1) for i in range(lax.axis_size('seq'...  3.83 us
  transfers between devices with their start and end apart: 34, of which 15 were waited for; matrix products, arithmetic and copies ran while one was open for 3% of the time, Pallas kernels for 22%

profile of v8, /device:TPU:0, one launch (start us, length us, event | category | flops | bytes accessed | tf_op | source)
XLA Modules:
  0.0 151.8 jit_solution(17061898304863686678)
XLA Ops:
  0.7 1.0 copy-done.2
  1.8 1.0 copy-done.3
  2.8 1.9 %arrange.1 = (bf16[4,2,128,512]{3,2,1,0:T(8,128)(2,1)}, bf16[1,2,128,512]{3,2,1,0:T(8,128)(2,1)}, bf16[1,2,128,512]{3,2,1,0:T(8,128)(2,1)S(1)}, bf16[1,2,128,512...) custom-call(s32[4]{0:T(128)S(1)} %add_xor_fusion.owner_ref, bf16[128,2048]{1,0:T(8,128)(2,1)S(1)} %copy-done.2, ...), custom_call_target="tpu_custom_call" | custom-call | tf_op jit(solution)/shard_map/arrange/pallas_call | solution.py:42
  4.7 5.0 %collective-permute-start.1 = (bf16[1,2,128,512]{3,2,1,0:T(8,128)(2,1)}, bf16[1,2,128,512]{3,2,1,0:T(8,128)(2,1)}, u32[]{:S(2)}, u32[]{:S(2)}) collective-permute-start(bf16[1,2,128,512]{3,2,1,0:T(8,128)(2,1)} %get-tuple-element.94.refs_0_), channel_id=1, source_target_pairs={{0,6},{1,7},{2,0},{3,1},{4,2},{5,3},{6,4},{7,5},{8,14},{9,15},{10,... | collective-permute-start | bytes 786440 | tf_op jit(solution)/shard_map/ppermute | solution.py:261
  9.8 1.1 copy.25
  11.2 0.7 slice.60
  11.9 3.1 %collective-permute-start.2 = (bf16[224,512]{1,0:T(8,128)(2,1)}, bf16[224,512]{1,0:T(8,128)(2,1)}, u32[]{:S(2)}, u32[]{:S(2)}) collective-permute-start(bf16[224,512]{1,0:T(8,128)(2,1)} %slice.60), channel_id=1, source_target_pairs={{0,1},{1,2},{2,3},{3,4},{4,5},{5,6},{6,7},{8,9},{9,10},{10,11},{11... | collective-permute-start | bytes 688136 | tf_op jit(solution)/shard_map/ppermute | solution.py:330
  15.8 1.6 %copy-done.1 = bf16[1024,1024]{1,0:T(8,128)(2,1)S(1)} copy-done((bf16[1024,1024]{1,0:T(8,128)(2,1)S(1)}, bf16[1024,1024]{1,0:T(8,128)(2,1)}, u32[]{:S(2)}) %copy-start.1) | copy-done | bytes 2097176
  17.4 4.6 %attention.2.second_ref = bf16[512,2048]{1,0:T(8,128)(2,1)S(1)} custom-call(s32[8]{0:T(128)S(1)} %pad_add_fusion.order_ref, bf16[1024,1024]{1,0:T(8,128)(2,1)S(1)} %copy-done, bf16[1024,1024]{1,0:T(8,128)(2,1)S(1)} %copy-done.1, bf16[1024,512]{1,0:T(8,128)(2,1)S(1)} %pad_maximum_fusion.ctx_ref, s32[1024,128]{1,0:T(8,128)S(1)} %broadcast_in_dim.13.low_ref), custom_call_target="tpu_custom_call" | custom-call | flops 1048576 | bytes 512 | tf_op jit(solution)/shard_map/attention/pallas_call | solution.py:126
  22.4 1.5 collective-permute-start.5
  23.9 2.4 %collective-permute-start.6 = (bf16[1,2,128,512]{3,2,1,0:T(8,128)(2,1)S(1)}, bf16[1,2,128,512]{3,2,1,0:T(8,128)(2,1)S(1)}, u32[]{:S(2)}, u32[]{:S(2)}) collective-permute-start(bf16[1,2,128,512]{3,2,1,0:T(8,128)(2,1)S(1)} %copy-done.7), channel_id=1, source_target_pairs={{0,2},{1,3},{2,4},{3,5},{4,6},{5,7},{6,0},{7,1},{8,10},{9,11},{10,... | collective-permute-start | bytes 786440 | tf_op jit(solution)/shard_map/ppermute | solution.py:261
  26.8 1.0 pad_maximum_fusion.1.ctx_ref
  27.8 4.8 %attention.3.first_ref = bf16[512,2048]{1,0:T(8,128)(2,1)S(1)} custom-call(s32[8]{0:T(128)S(1)} %pad_add_fusion.order_ref, bf16[1024,1024]{1,0:T(8,128)(2,1)S(1)} %copy-done, bf16[1024,1024]{1,0:T(8,128)(2,1)S(1)} %copy-done.1, bf16[736,512]{1,0:T(8,128)(2,1)S(1)} %pad_maximum_fusion.1.ctx_ref, s32[1024,128]{1,0:T(8,128)S(1)} %broadcast_in_dim.13.low_ref), custom_call_target="tpu_custom_call" | custom-call | flops 1048576 | bytes 512 | tf_op jit(solution)/shard_map/attention/pallas_call | solution.py:126
  32.6 2.2 %collective-permute-done.6.refs_1_ = bf16[1,2,128,512]{3,2,1,0:T(8,128)(2,1)S(1)} collective-permute-done((bf16[1,2,128,512]{3,2,1,0:T(8,128)(2,1)S(1)}, bf16[1,2,128,512]{3,2,1,0:T(8,128)(2,1)S(1)}, u32[]{:S(2)}, u32[]{:S(2)}) %collective-permute-start.6) | collective-permute-done | bytes 262176 | tf_op jit(solution)/shard_map/ppermute | solution.py:261
  34.8 4.7 %collective-permute-done.3.refs_2_ = bf16[1,2,128,512]{3,2,1,0:T(8,128)(2,1)S(1)} collective-permute-done((bf16[1,2,128,512]{3,2,1,0:T(8,128)(2,1)}, bf16[1,2,128,512]{3,2,1,0:T(8,128)(2,1)S(1)}, u32[]{:S(2)}, u32[]{:S(2)}) %collective-permute-start.3) | collective-permute-done | bytes 262176 | tf_op jit(solution)/shard_map/ppermute | solution.py:261
  39.6 0.5 collective-permute-start.11
  40.1 1.0 collective-permute-start.9
  41.1 2.8 %collective-permute-start.10 = (bf16[1,2,128,512]{3,2,1,0:T(8,128)(2,1)S(1)}, bf16[1,2,128,512]{3,2,1,0:T(8,128)(2,1)S(1)}, u32[]{:S(2)}, u32[]{:S(2)}) collective-permute-start(bf16[1,2,128,512]{3,2,1,0:T(8,128)(2,1)S(1)} %copy-done.7), channel_id=1, source_target_pairs={{0,6},{1,7},{2,0},{3,1},{4,2},{5,3},{6,4},{7,5},{8,14},{9,15},{10,... | collective-permute-start | bytes 786440 | tf_op jit(solution)/shard_map/ppermute | solution.py:261
  43.9 5.5 %project.4 = (bf16[2,1024,256]{2,1,0:T(8,128)(2,1)S(1)}, bf16[2,1024,256]{2,1,0:T(8,128)(2,1)S(1)}) custom-call(bf16[512,2048]{1,0:T(8,128)(2,1)S(1)} %attention.3.first_ref, bf16[512,2048]{1,0:T(8,128)(2,1)S(1)} %attention.2.second_ref, bf16[1,2,128,512]{3,2,1,0:T(8,128)(2,1)} %get-tuple-element.94.refs_0_, ...), custom_call_target="tpu_custom_call" | custom-call | flops 5000000000 | bytes 512 | tf_op jit(solution)/shard_map/project/pallas_call | solution.py:200
  49.4 1.6 %collective-permute-start.19 = (bf16[2,1024,256]{2,1,0:T(8,128)(2,1)S(1)}, bf16[2,1024,256]{2,1,0:T(8,128)(2,1)S(1)}, u32[]{:S(2)}, u32[]{:S(2)}) collective-permute-start(bf16[2,1024,256]{2,1,0:T(8,128)(2,1)S(1)} %get-tuple-element.107), channel_id=1, source_target_pairs={{0,8},{1,17},{2,10},{3,19},{4,12},{5,21},{6,14},{7,23},{8,0},{9,25... | collective-permute-start | bytes 3145736 | tf_op jit(solution)/shard_map/ppermute | solution.py:256
  51.0 3.7 %collective-permute-done.10.refs_3_ = bf16[1,2,128,512]{3,2,1,0:T(8,128)(2,1)S(1)} collective-permute-done((bf16[1,2,128,512]{3,2,1,0:T(8,128)(2,1)S(1)}, bf16[1,2,128,512]{3,2,1,0:T(8,128)(2,1)S(1)}, u32[]{:S(2)}, u32[]{:S(2)}) %collective-permute-start.10) | collective-permute-done | bytes 262176 | tf_op jit(solution)/shard_map/ppermute | solution.py:261
  54.7 6.7 %collective-permute-done.12.refs_1_ = bf16[1,2,128,512]{3,2,1,0:T(8,128)(2,1)S(1)} collective-permute-done((bf16[1,2,128,512]{3,2,1,0:T(8,128)(2,1)S(1)}, bf16[1,2,128,512]{3,2,1,0:T(8,128)(2,1)S(1)}, u32[]{:S(2)}, u32[]{:S(2)}) %collective-permute-start.12) | collective-permute-done | bytes 262176 | tf_op jit(solution)/shard_map/ppermute | solution.py:261
  61.4 0.5 collective-permute-start.14
  61.9 1.0 collective-permute-done.13.refs_6_
  63.3 5.2 %project.5 = (bf16[2,1024,256]{2,1,0:T(8,128)(2,1)S(1)}, bf16[2,1024,256]{2,1,0:T(8,128)(2,1)S(1)}) custom-call(bf16[512,2048]{1,0:T(8,128)(2,1)S(1)} %attention.3.first_ref, bf16[512,2048]{1,0:T(8,128)(2,1)S(1)} %attention.2.second_ref, bf16[1,2,128,512]{3,2,1,0:T(8,128)(2,1)S(1)} %copy-done.7, bf16[1,2,128,512]{3,2,1,0:T(8,128)(2,1)S(1)} %collective-permute-done.6.refs_1_, ...), custom_call_target="tpu_custom_call" | custom-call | flops 5000000000 | bytes 512 | tf_op jit(solution)/shard_map/project/pallas_call | solution.py:200
  68.6 1.6 %collective-permute-start.26 = (bf16[2,1024,256]{2,1,0:T(8,128)(2,1)S(1)}, bf16[2,1024,256]{2,1,0:T(8,128)(2,1)S(1)}, u32[]{:S(2)}, u32[]{:S(2)}) collective-permute-start(bf16[2,1024,256]{2,1,0:T(8,128)(2,1)S(1)} %get-tuple-element.120), channel_id=1, source_target_pairs={{0,8},{1,17},{2,10},{3,19},{4,12},{5,21},{6,14},{7,23},{8,0},{9,25... | collective-permute-start | bytes 3145736 | tf_op jit(solution)/shard_map/ppermute | solution.py:256
  70.1 2.0 %collective-permute-start.18 = (bf16[1,2,128,512]{3,2,1,0:T(8,128)(2,1)S(1)}, bf16[1,2,128,512]{3,2,1,0:T(8,128)(2,1)S(1)}, u32[]{:S(2)}, u32[]{:S(2)}) collective-permute-start(bf16[1,2,128,512]{3,2,1,0:T(8,128)(2,1)S(1)} %get-tuple-element.139.refs_0_), channel_id=1, source_target_pairs={{0,2},{1,3},{2,4},{3,5},{4,6},{5,7},{6,0},{7,1},{8,10},{9,11},{10,... | collective-permute-start | bytes 786440 | tf_op jit(solution)/shard_map/ppermute | solution.py:261
  72.3 1.6 %collective-permute-start.25 = (bf16[2,1024,128]{2,1,0:T(8,128)(2,1)S(1)}, bf16[2,1024,128]{2,1,0:T(8,128)(2,1)S(1)}, u32[]{:S(2)}, u32[]{:S(2)}) collective-permute-start(bf16[2,1024,128]{2,1,0:T(8,128)(2,1)S(1)} %add_convert_fusion.3), channel_id=1, source_target_pairs={{0,16},{1,9},{2,18},{3,11},{4,20},{5,13},{6,22},{7,15},{8,24},{9,1... | collective-permute-start | bytes 1572872 | tf_op jit(solution)/shard_map/ppermute | solution.py:256
  73.9 10.0 %collective-permute-done.16.refs_3_ = bf16[1,2,128,512]{3,2,1,0:T(8,128)(2,1)S(1)} collective-permute-done((bf16[1,2,128,512]{3,2,1,0:T(8,128)(2,1)S(1)}, bf16[1,2,128,512]{3,2,1,0:T(8,128)(2,1)S(1)}, u32[]{:S(2)}, u32[]{:S(2)}) %collective-permute-start.16) | collective-permute-done | bytes 262176 | tf_op jit(solution)/shard_map/ppermute | solution.py:261
  83.8 9.0 %collective-permute-done.15.refs_2_ = bf16[1,2,128,512]{3,2,1,0:T(8,128)(2,1)S(1)} collective-permute-done((bf16[1,2,128,512]{3,2,1,0:T(8,128)(2,1)S(1)}, bf16[1,2,128,512]{3,2,1,0:T(8,128)(2,1)S(1)}, u32[]{:S(2)}, u32[]{:S(2)}) %collective-permute-start.15) | collective-permute-done | bytes 262176 | tf_op jit(solution)/shard_map/ppermute | solution.py:261
  92.9 0.5 collective-permute-start.21
  93.4 1.0 collective-permute-done.20.refs_6_
  94.4 2.8 %collective-permute-start.23 = (bf16[1,2,128,512]{3,2,1,0:T(8,128)(2,1)S(1)}, bf16[1,2,128,512]{3,2,1,0:T(8,128)(2,1)S(1)}, u32[]{:S(2)}, u32[]{:S(2)}) collective-permute-start(bf16[1,2,128,512]{3,2,1,0:T(8,128)(2,1)S(1)} %get-tuple-element.139.refs_0_), channel_id=1, source_target_pairs={{0,6},{1,7},{2,0},{3,1},{4,2},{5,3},{6,4},{7,5},{8,14},{9,15},{10,... | collective-permute-start | bytes 786440 | tf_op jit(solution)/shard_map/ppermute | solution.py:261
  97.2 5.2 %project.6 = (bf16[2,1024,256]{2,1,0:T(8,128)(2,1)S(1)}, bf16[2,1024,256]{2,1,0:T(8,128)(2,1)S(1)}) custom-call(bf16[512,2048]{1,0:T(8,128)(2,1)S(1)} %attention.3.first_ref, bf16[512,2048]{1,0:T(8,128)(2,1)S(1)} %attention.2.second_ref, bf16[1,2,128,512]{3,2,1,0:T(8,128)(2,1)S(1)} %copy-done.5, ...), custom_call_target="tpu_custom_call" | custom-call | flops 1500000000 | bytes 512 | tf_op jit(solution)/shard_map/project/pallas_call | solution.py:200
  102.5 2.5 %collective-permute-start.31 = (bf16[2,1024,256]{2,1,0:T(8,128)(2,1)S(1)}, bf16[2,1024,256]{2,1,0:T(8,128)(2,1)S(1)}, u32[]{:S(2)}, u32[]{:S(2)}) collective-permute-start(bf16[2,1024,256]{2,1,0:T(8,128)(2,1)S(1)} %get-tuple-element.135), channel_id=1, source_target_pairs={{0,8},{1,17},{2,10},{3,19},{4,12},{5,21},{6,14},{7,23},{8,0},{9,25... | collective-permute-start | bytes 3145736 | tf_op jit(solution)/shard_map/ppermute | solution.py:256
  105.1 3.2 %collective-permute-done.23.refs_3_ = bf16[1,2,128,512]{3,2,1,0:T(8,128)(2,1)S(1)} collective-permute-done((bf16[1,2,128,512]{3,2,1,0:T(8,128)(2,1)S(1)}, bf16[1,2,128,512]{3,2,1,0:T(8,128)(2,1)S(1)}, u32[]{:S(2)}, u32[]{:S(2)}) %collective-permute-start.23) | collective-permute-done | bytes 262176 | tf_op jit(solution)/shard_map/ppermute | solution.py:261
  108.4 0.5 collective-permute-start.28
  108.9 1.0 collective-permute-done.27.refs_6_
  110.3 5.2 %project.7 = (bf16[2,1024,256]{2,1,0:T(8,128)(2,1)S(1)}, bf16[2,1024,256]{2,1,0:T(8,128)(2,1)S(1)}) custom-call(bf16[512,2048]{1,0:T(8,128)(2,1)S(1)} %attention.3.first_ref, bf16[512,2048]{1,0:T(8,128)(2,1)S(1)} %attention.2.second_ref, bf16[1,2,128,512]{3,2,1,0:T(8,128)(2,1)S(1)} %get-tuple-element.139.refs_0_, ...), custom_call_target="tpu_custom_call" | custom-call | flops 10000000 | bytes 512 | tf_op jit(solution)/shard_map/project/pallas_call | solution.py:200
  115.5 2.5 %collective-permute-start.29 = (bf16[2,1024,256]{2,1,0:T(8,128)(2,1)S(1)}, bf16[2,1024,256]{2,1,0:T(8,128)(2,1)S(1)}, u32[]{:S(2)}, u32[]{:S(2)}) collective-permute-start(bf16[2,1024,256]{2,1,0:T(8,128)(2,1)S(1)} %get-tuple-element.146), channel_id=1, source_target_pairs={{0,8},{1,17},{2,10},{3,19},{4,12},{5,21},{6,14},{7,23},{8,0},{9,25... | collective-permute-start | bytes 3145736 | tf_op jit(solution)/shard_map/ppermute | solution.py:256
  118.3 2.0 %collective-permute-start.32 = (bf16[2,1024,128]{2,1,0:T(8,128)(2,1)S(1)}, bf16[2,1024,128]{2,1,0:T(8,128)(2,1)S(1)}, u32[]{:S(2)}, u32[]{:S(2)}) collective-permute-start(bf16[2,1024,128]{2,1,0:T(8,128)(2,1)S(1)} %add_convert_fusion), channel_id=1, source_target_pairs={{0,16},{1,9},{2,18},{3,11},{4,20},{5,13},{6,22},{7,15},{8,24},{9,1... | collective-permute-start | bytes 1572872 | tf_op jit(solution)/shard_map/ppermute | solution.py:256
  120.3 20.9 %collective-permute-done.29.received_ref = bf16[2,1024,256]{2,1,0:T(8,128)(2,1)S(1)} collective-permute-done((bf16[2,1024,256]{2,1,0:T(8,128)(2,1)S(1)}, bf16[2,1024,256]{2,1,0:T(8,128)(2,1)S(1)}, u32[]{:S(2)}, u32[]{:S(2)}) %collective-permute-start.29) | collective-permute-done | bytes 1048608 | tf_op jit(solution)/shard_map/ppermute | solution.py:256
  141.3 2.2 %collective-permute-start.30 = (bf16[2,1024,128]{2,1,0:T(8,128)(2,1)S(1)}, bf16[2,1024,128]{2,1,0:T(8,128)(2,1)S(1)}, u32[]{:S(2)}, u32[]{:S(2)}) collective-permute-start(bf16[2,1024,128]{2,1,0:T(8,128)(2,1)S(1)} %add_convert_fusion.1), channel_id=1, source_target_pairs={{0,16},{1,9},{2,18},{3,11},{4,20},{5,13},{6,22},{7,15},{8,24},{9,1... | collective-permute-start | bytes 1572872 | tf_op jit(solution)/shard_map/ppermute | solution.py:256
  143.5 1.1 finish.4
  144.7 1.1 finish.5
  145.8 1.1 finish.6
  146.9 3.8 %collective-permute-done.30.last_ref = bf16[2,1024,128]{2,1,0:T(8,128)(2,1)S(1)} collective-permute-done((bf16[2,1024,128]{2,1,0:T(8,128)(2,1)S(1)}, bf16[2,1024,128]{2,1,0:T(8,128)(2,1)S(1)}, u32[]{:S(2)}, u32[]{:S(2)}) %collective-permute-start.30) | collective-permute-done | bytes 524320 | tf_op jit(solution)/shard_map/ppermute | solution.py:256
  150.7 1.1 finish.7
  (73 shorter events, 3.4 us)
Async XLA Ops:
  0.7 1.0 copy-start.2
  1.8 1.0 copy-start.3
  2.8 8.1 %copy-start.8 = (bf16[1024,2,128]{2,1,0:T(2,128)(2,1)S(1)}, bf16[1024,2,128]{2,1,0:T(2,128)(2,1)}, u32[]{:S(2)}) copy-start(bf16[1024,2,128]{2,1,0:T(2,128)(2,1)} %param.10) | copy-start | bytes 1572868
  4.7 6.4 %copy-start.4 = (bf16[1,2,128,512]{3,2,1,0:T(8,128)(2,1)}, bf16[1,2,128,512]{3,2,1,0:T(8,128)(2,1)S(1)}, u32[]{:S(2)}) copy-start(bf16[1,2,128,512]{3,2,1,0:T(8,128)(2,1)S(1)} %get-tuple-element.122.refs_0_) | copy-start | bytes 786436
  4.7 6.4 %copy-start.6 = (bf16[1,2,128,512]{3,2,1,0:T(8,128)(2,1)}, bf16[1,2,128,512]{3,2,1,0:T(8,128)(2,1)S(1)}, u32[]{:S(2)}) copy-start(bf16[1,2,128,512]{3,2,1,0:T(8,128)(2,1)S(1)} %get-tuple-element.108.refs_0_) | copy-start | bytes 786436
  4.7 17.3 %collective-permute-start.1 = (bf16[1,2,128,512]{3,2,1,0:T(8,128)(2,1)}, bf16[1,2,128,512]{3,2,1,0:T(8,128)(2,1)}, u32[]{:S(2)}, u32[]{:S(2)}) collective-permute-start(bf16[1,2,128,512]{3,2,1,0:T(8,128)(2,1)} %get-tuple-element.94.refs_0_), channel_id=1, source_target_pairs={{0,6},{1,7},{2,0},{3,1},{4,2},{5,3},{6,4},{7,5},{8,14},{9,15},{10,... | collective-permute-start | bytes 786440 | tf_op jit(solution)/shard_map/ppermute | solution.py:261
  9.8 12.6 %collective-permute-start = (bf16[1,2,128,512]{3,2,1,0:T(8,128)(2,1)}, bf16[1,2,128,512]{3,2,1,0:T(8,128)(2,1)}, u32[]{:S(2)}, u32[]{:S(2)}) collective-permute-start(bf16[1,2,128,512]{3,2,1,0:T(8,128)(2,1)} %get-tuple-element.94.refs_0_), channel_id=1, source_target_pairs={{0,2},{1,3},{2,4},{3,5},{4,6},{5,7},{6,0},{7,1},{8,10},{9,11},{10,... | collective-permute-start | bytes 786440 | tf_op jit(solution)/shard_map/ppermute | solution.py:261
  9.8 29.8 %collective-permute-start.7 = (bf16[4,2,128,512]{3,2,1,0:T(8,128)(2,1)}, bf16[4,2,128,512]{3,2,1,0:T(8,128)(2,1)}, u32[]{:S(2)}, u32[]{:S(2)}) collective-permute-start(bf16[4,2,128,512]{3,2,1,0:T(8,128)(2,1)} %get-tuple-element.93), channel_id=1, source_target_pairs={{0,1},{1,0},{2,3},{3,2},{4,5},{5,4},{6,7},{7,6},{8,9},{9,8},{10,11... | collective-permute-start | bytes 3145736 | tf_op jit(solution)/shard_map/ppermute | solution.py:265
  11.0 4.1 %copy-start.9 = (s32[64]{0:T(128)S(1)}, s32[64]{0:T(128)}, u32[]{:S(2)}) copy-start(s32[64]{0:T(128)} %param.11) | copy-start | bytes 772
  11.1 4.7 %copy-start = (bf16[1024,1024]{1,0:T(8,128)(2,1)S(1)}, bf16[1024,1024]{1,0:T(8,128)(2,1)}, u32[]{:S(2)}) copy-start(bf16[1024,1024]{1,0:T(8,128)(2,1)} %q_ref.3) | copy-start | bytes 6291460
  11.9 10.1 %collective-permute-start.2 = (bf16[224,512]{1,0:T(8,128)(2,1)}, bf16[224,512]{1,0:T(8,128)(2,1)}, u32[]{:S(2)}, u32[]{:S(2)}) collective-permute-start(bf16[224,512]{1,0:T(8,128)(2,1)} %slice.60), channel_id=1, source_target_pairs={{0,1},{1,2},{2,3},{3,4},{4,5},{5,6},{6,7},{8,9},{9,10},{10,11},{11... | collective-permute-start | bytes 688136 | tf_op jit(solution)/shard_map/ppermute | solution.py:330
  15.8 1.6 %copy-start.1 = (bf16[1024,1024]{1,0:T(8,128)(2,1)S(1)}, bf16[1024,1024]{1,0:T(8,128)(2,1)}, u32[]{:S(2)}) copy-start(bf16[1024,1024]{1,0:T(8,128)(2,1)} %qt_ref.3) | copy-start | bytes 6291460
  17.4 6.5 %copy-start.7 = (bf16[1,2,128,512]{3,2,1,0:T(8,128)(2,1)S(1)}, bf16[1,2,128,512]{3,2,1,0:T(8,128)(2,1)}, u32[]{:S(2)}) copy-start(bf16[1,2,128,512]{3,2,1,0:T(8,128)(2,1)} %copy-done.6) | copy-start | bytes 786436
  22.4 10.2 %collective-permute-start.5 = (bf16[1,2,128,512]{3,2,1,0:T(8,128)(2,1)}, bf16[1,2,128,512]{3,2,1,0:T(8,128)(2,1)S(1)}, u32[]{:S(2)}, u32[]{:S(2)}) collective-permute-start(bf16[1,2,128,512]{3,2,1,0:T(8,128)(2,1)} %collective-permute-done.1.refs_3_), channel_id=1, source_target_pairs={{0,1},{1,0},{2,3},{3,2},{4,5},{5,4},{6,7},{7,6},{8,9},{9,8},{10,11... | collective-permute-start | bytes 786440 | tf_op jit(solution)/shard_map/ppermute | solution.py:265
  23.9 11.0 %collective-permute-start.6 = (bf16[1,2,128,512]{3,2,1,0:T(8,128)(2,1)S(1)}, bf16[1,2,128,512]{3,2,1,0:T(8,128)(2,1)S(1)}, u32[]{:S(2)}, u32[]{:S(2)}) collective-permute-start(bf16[1,2,128,512]{3,2,1,0:T(8,128)(2,1)S(1)} %copy-done.7), channel_id=1, source_target_pairs={{0,2},{1,3},{2,4},{3,5},{4,6},{5,7},{6,0},{7,1},{8,10},{9,11},{10,... | collective-permute-start | bytes 786440 | tf_op jit(solution)/shard_map/ppermute | solution.py:261
  26.3 8.5 %collective-permute-start.4 = (bf16[1,2,128,512]{3,2,1,0:T(8,128)(2,1)}, bf16[1,2,128,512]{3,2,1,0:T(8,128)(2,1)S(1)}, u32[]{:S(2)}, u32[]{:S(2)}) collective-permute-start(bf16[1,2,128,512]{3,2,1,0:T(8,128)(2,1)} %collective-permute-done.refs_1_), channel_id=1, source_target_pairs={{0,1},{1,0},{2,3},{3,2},{4,5},{5,4},{6,7},{7,6},{8,9},{9,8},{10,11... | collective-permute-start | bytes 786440 | tf_op jit(solution)/shard_map/ppermute | solution.py:265
  26.5 13.1 %collective-permute-start.3 = (bf16[1,2,128,512]{3,2,1,0:T(8,128)(2,1)}, bf16[1,2,128,512]{3,2,1,0:T(8,128)(2,1)S(1)}, u32[]{:S(2)}, u32[]{:S(2)}) collective-permute-start(bf16[1,2,128,512]{3,2,1,0:T(8,128)(2,1)} %collective-permute-done.refs_1_), channel_id=1, source_target_pairs={{0,2},{1,3},{2,4},{3,5},{4,6},{5,7},{6,0},{7,1},{8,10},{9,11},{10,... | collective-permute-start | bytes 786440 | tf_op jit(solution)/shard_map/ppermute | solution.py:261
  27.8 16.1 %copy-start.5 = (bf16[1,2,128,512]{3,2,1,0:T(8,128)(2,1)S(1)}, bf16[1,2,128,512]{3,2,1,0:T(8,128)(2,1)}, u32[]{:S(2)}) copy-start(bf16[1,2,128,512]{3,2,1,0:T(8,128)(2,1)} %copy-done.4) | copy-start | bytes 786436
  39.6 4.3 %collective-permute-start.8 = (bf16[1,2,128,512]{3,2,1,0:T(8,128)(2,1)S(1)}, bf16[1,2,128,512]{3,2,1,0:T(8,128)(2,1)S(1)}, u32[]{:S(2)}, u32[]{:S(2)}) collective-permute-start(bf16[1,2,128,512]{3,2,1,0:T(8,128)(2,1)S(1)} %collective-permute-done.3.refs_2_), channel_id=1, source_target_pairs={{0,1},{1,0},{2,3},{3,2},{4,5},{5,4},{6,7},{7,6},{8,9},{9,8},{10,11... | collective-permute-start | bytes 786440 | tf_op jit(solution)/shard_map/ppermute | solution.py:265
  39.6 21.8 %collective-permute-start.11 = (bf16[1,2,128,512]{3,2,1,0:T(8,128)(2,1)S(1)}, bf16[1,2,128,512]{3,2,1,0:T(8,128)(2,1)S(1)}, u32[]{:S(2)}, u32[]{:S(2)}) collective-permute-start(bf16[1,2,128,512]{3,2,1,0:T(8,128)(2,1)S(1)} %collective-permute-done.6.refs_1_), channel_id=1, source_target_pairs={{0,1},{1,0},{2,3},{3,2},{4,5},{5,4},{6,7},{7,6},{8,9},{9,8},{10,11... | collective-permute-start | bytes 786440 | tf_op jit(solution)/shard_map/ppermute | solution.py:265
  40.1 21.3 %collective-permute-start.9 = (bf16[1,2,128,512]{3,2,1,0:T(8,128)(2,1)S(1)}, bf16[1,2,128,512]{3,2,1,0:T(8,128)(2,1)S(1)}, u32[]{:S(2)}, u32[]{:S(2)}) collective-permute-start(bf16[1,2,128,512]{3,2,1,0:T(8,128)(2,1)S(1)} %collective-permute-done.6.refs_1_), channel_id=1, source_target_pairs={{0,2},{1,3},{2,4},{3,5},{4,6},{5,7},{6,0},{7,1},{8,10},{9,11},{10,... | collective-permute-start | bytes 786440 | tf_op jit(solution)/shard_map/ppermute | solution.py:261
  41.1 13.6 %collective-permute-start.10 = (bf16[1,2,128,512]{3,2,1,0:T(8,128)(2,1)S(1)}, bf16[1,2,128,512]{3,2,1,0:T(8,128)(2,1)S(1)}, u32[]{:S(2)}, u32[]{:S(2)}) collective-permute-start(bf16[1,2,128,512]{3,2,1,0:T(8,128)(2,1)S(1)} %copy-done.7), channel_id=1, source_target_pairs={{0,6},{1,7},{2,0},{3,1},{4,2},{5,3},{6,4},{7,5},{8,14},{9,15},{10,... | collective-permute-start | bytes 786440 | tf_op jit(solution)/shard_map/ppermute | solution.py:261
  43.9 17.5 %collective-permute-start.12 = (bf16[1,2,128,512]{3,2,1,0:T(8,128)(2,1)S(1)}, bf16[1,2,128,512]{3,2,1,0:T(8,128)(2,1)S(1)}, u32[]{:S(2)}, u32[]{:S(2)}) collective-permute-start(bf16[1,2,128,512]{3,2,1,0:T(8,128)(2,1)S(1)} %copy-done.5), channel_id=1, source_target_pairs={{0,2},{1,3},{2,4},{3,5},{4,6},{5,7},{6,0},{7,1},{8,10},{9,11},{10,... | collective-permute-start | bytes 786440 | tf_op jit(solution)/shard_map/ppermute | solution.py:261
  49.4 22.7 %collective-permute-start.19 = (bf16[2,1024,256]{2,1,0:T(8,128)(2,1)S(1)}, bf16[2,1024,256]{2,1,0:T(8,128)(2,1)S(1)}, u32[]{:S(2)}, u32[]{:S(2)}) collective-permute-start(bf16[2,1024,256]{2,1,0:T(8,128)(2,1)S(1)} %get-tuple-element.107), channel_id=1, source_target_pairs={{0,8},{1,17},{2,10},{3,19},{4,12},{5,21},{6,14},{7,23},{8,0},{9,25... | collective-permute-start | bytes 3145736 | tf_op jit(solution)/shard_map/ppermute | solution.py:256
  61.4 1.5 %collective-permute-start.13 = (bf16[1,2,128,512]{3,2,1,0:T(8,128)(2,1)S(1)}, bf16[1,2,128,512]{3,2,1,0:T(8,128)(2,1)S(1)}, u32[]{:S(2)}, u32[]{:S(2)}) collective-permute-start(bf16[1,2,128,512]{3,2,1,0:T(8,128)(2,1)S(1)} %collective-permute-done.9.refs_2_), channel_id=1, source_target_pairs={{0,1},{1,0},{2,3},{3,2},{4,5},{5,4},{6,7},{7,6},{8,9},{9,8},{10,11... | collective-permute-start | bytes 786440 | tf_op jit(solution)/shard_map/ppermute | solution.py:265
  61.4 1.9 %collective-permute-start.14 = (bf16[1,2,128,512]{3,2,1,0:T(8,128)(2,1)S(1)}, bf16[1,2,128,512]{3,2,1,0:T(8,128)(2,1)S(1)}, u32[]{:S(2)}, u32[]{:S(2)}) collective-permute-start(bf16[1,2,128,512]{3,2,1,0:T(8,128)(2,1)S(1)} %collective-permute-done.10.refs_3_), channel_id=1, source_target_pairs={{0,1},{1,0},{2,3},{3,2},{4,5},{5,4},{6,7},{7,6},{8,9},{9,8},{10,11... | collective-permute-start | bytes 786440 | tf_op jit(solution)/shard_map/ppermute | solution.py:265
  68.6 36.4 %collective-permute-start.26 = (bf16[2,1024,256]{2,1,0:T(8,128)(2,1)S(1)}, bf16[2,1024,256]{2,1,0:T(8,128)(2,1)S(1)}, u32[]{:S(2)}, u32[]{:S(2)}) collective-permute-start(bf16[2,1024,256]{2,1,0:T(8,128)(2,1)S(1)} %get-tuple-element.120), channel_id=1, source_target_pairs={{0,8},{1,17},{2,10},{3,19},{4,12},{5,21},{6,14},{7,23},{8,0},{9,25... | collective-permute-start | bytes 3145736 | tf_op jit(solution)/shard_map/ppermute | solution.py:256
  70.1 13.7 %collective-permute-start.16 = (bf16[1,2,128,512]{3,2,1,0:T(8,128)(2,1)S(1)}, bf16[1,2,128,512]{3,2,1,0:T(8,128)(2,1)S(1)}, u32[]{:S(2)}, u32[]{:S(2)}) collective-permute-start(bf16[1,2,128,512]{3,2,1,0:T(8,128)(2,1)S(1)} %copy-done.5), channel_id=1, source_target_pairs={{0,6},{1,7},{2,0},{3,1},{4,2},{5,3},{6,4},{7,5},{8,14},{9,15},{10,... | collective-permute-start | bytes 786440 | tf_op jit(solution)/shard_map/ppermute | solution.py:261
  70.1 13.7 %collective-permute-start.18 = (bf16[1,2,128,512]{3,2,1,0:T(8,128)(2,1)S(1)}, bf16[1,2,128,512]{3,2,1,0:T(8,128)(2,1)S(1)}, u32[]{:S(2)}, u32[]{:S(2)}) collective-permute-start(bf16[1,2,128,512]{3,2,1,0:T(8,128)(2,1)S(1)} %get-tuple-element.139.refs_0_), channel_id=1, source_target_pairs={{0,2},{1,3},{2,4},{3,5},{4,6},{5,7},{6,0},{7,1},{8,10},{9,11},{10,... | collective-permute-start | bytes 786440 | tf_op jit(solution)/shard_map/ppermute | solution.py:261
  72.3 21.1 %collective-permute-start.25 = (bf16[2,1024,128]{2,1,0:T(8,128)(2,1)S(1)}, bf16[2,1024,128]{2,1,0:T(8,128)(2,1)S(1)}, u32[]{:S(2)}, u32[]{:S(2)}) collective-permute-start(bf16[2,1024,128]{2,1,0:T(8,128)(2,1)S(1)} %add_convert_fusion.3), channel_id=1, source_target_pairs={{0,16},{1,9},{2,18},{3,11},{4,20},{5,13},{6,22},{7,15},{8,24},{9,1... | collective-permute-start | bytes 1572872 | tf_op jit(solution)/shard_map/ppermute | solution.py:256
  73.9 10.0 %collective-permute-start.17 = (bf16[1,2,128,512]{3,2,1,0:T(8,128)(2,1)S(1)}, bf16[1,2,128,512]{3,2,1,0:T(8,128)(2,1)S(1)}, u32[]{:S(2)}, u32[]{:S(2)}) collective-permute-start(bf16[1,2,128,512]{3,2,1,0:T(8,128)(2,1)S(1)} %collective-permute-done.12.refs_1_), channel_id=1, source_target_pairs={{0,1},{1,0},{2,3},{3,2},{4,5},{5,4},{6,7},{7,6},{8,9},{9,8},{10,11... | collective-permute-start | bytes 786440 | tf_op jit(solution)/shard_map/ppermute | solution.py:265
  83.8 9.0 %collective-permute-start.15 = (bf16[1,2,128,512]{3,2,1,0:T(8,128)(2,1)S(1)}, bf16[1,2,128,512]{3,2,1,0:T(8,128)(2,1)S(1)}, u32[]{:S(2)}, u32[]{:S(2)}) collective-permute-start(bf16[1,2,128,512]{3,2,1,0:T(8,128)(2,1)S(1)} %collective-permute-done.12.refs_1_), channel_id=1, source_target_pairs={{0,2},{1,3},{2,4},{3,5},{4,6},{5,7},{6,0},{7,1},{8,10},{9,11},{10,... | collective-permute-start | bytes 786440 | tf_op jit(solution)/shard_map/ppermute | solution.py:261
  92.8 1.5 %collective-permute-start.20 = (bf16[1,2,128,512]{3,2,1,0:T(8,128)(2,1)S(1)}, bf16[1,2,128,512]{3,2,1,0:T(8,128)(2,1)S(1)}, u32[]{:S(2)}, u32[]{:S(2)}) collective-permute-start(bf16[1,2,128,512]{3,2,1,0:T(8,128)(2,1)S(1)} %collective-permute-done.15.refs_2_), channel_id=1, source_target_pairs={{0,1},{1,0},{2,3},{3,2},{4,5},{5,4},{6,7},{7,6},{8,9},{9,8},{10,11... | collective-permute-start | bytes 786440 | tf_op jit(solution)/shard_map/ppermute | solution.py:265
  92.9 4.3 %collective-permute-start.21 = (bf16[1,2,128,512]{3,2,1,0:T(8,128)(2,1)S(1)}, bf16[1,2,128,512]{3,2,1,0:T(8,128)(2,1)S(1)}, u32[]{:S(2)}, u32[]{:S(2)}) collective-permute-start(bf16[1,2,128,512]{3,2,1,0:T(8,128)(2,1)S(1)} %collective-permute-done.16.refs_3_), channel_id=1, source_target_pairs={{0,1},{1,0},{2,3},{3,2},{4,5},{5,4},{6,7},{7,6},{8,9},{9,8},{10,11... | collective-permute-start | bytes 786440 | tf_op jit(solution)/shard_map/ppermute | solution.py:265
  93.4 15.0 %collective-permute-start.24 = (bf16[1,2,128,512]{3,2,1,0:T(8,128)(2,1)S(1)}, bf16[1,2,128,512]{3,2,1,0:T(8,128)(2,1)S(1)}, u32[]{:S(2)}, u32[]{:S(2)}) collective-permute-start(bf16[1,2,128,512]{3,2,1,0:T(8,128)(2,1)S(1)} %collective-permute-done.18.refs_1_), channel_id=1, source_target_pairs={{0,1},{1,0},{2,3},{3,2},{4,5},{5,4},{6,7},{7,6},{8,9},{9,8},{10,11... | collective-permute-start | bytes 786440 | tf_op jit(solution)/shard_map/ppermute | solution.py:265
  93.4 15.0 %collective-permute-start.22 = (bf16[1,2,128,512]{3,2,1,0:T(8,128)(2,1)S(1)}, bf16[1,2,128,512]{3,2,1,0:T(8,128)(2,1)S(1)}, u32[]{:S(2)}, u32[]{:S(2)}) collective-permute-start(bf16[1,2,128,512]{3,2,1,0:T(8,128)(2,1)S(1)} %collective-permute-done.18.refs_1_), channel_id=1, source_target_pairs={{0,2},{1,3},{2,4},{3,5},{4,6},{5,7},{6,0},{7,1},{8,10},{9,11},{10,... | collective-permute-start | bytes 786440 | tf_op jit(solution)/shard_map/ppermute | solution.py:261
  94.4 14.0 %collective-permute-start.23 = (bf16[1,2,128,512]{3,2,1,0:T(8,128)(2,1)S(1)}, bf16[1,2,128,512]{3,2,1,0:T(8,128)(2,1)S(1)}, u32[]{:S(2)}, u32[]{:S(2)}) collective-permute-start(bf16[1,2,128,512]{3,2,1,0:T(8,128)(2,1)S(1)} %get-tuple-element.139.refs_0_), channel_id=1, source_target_pairs={{0,6},{1,7},{2,0},{3,1},{4,2},{5,3},{6,4},{7,5},{8,14},{9,15},{10,... | collective-permute-start | bytes 786440 | tf_op jit(solution)/shard_map/ppermute | solution.py:261
  102.5 15.7 %collective-permute-start.31 = (bf16[2,1024,256]{2,1,0:T(8,128)(2,1)S(1)}, bf16[2,1024,256]{2,1,0:T(8,128)(2,1)S(1)}, u32[]{:S(2)}, u32[]{:S(2)}) collective-permute-start(bf16[2,1024,256]{2,1,0:T(8,128)(2,1)S(1)} %get-tuple-element.135), channel_id=1, source_target_pairs={{0,8},{1,17},{2,10},{3,19},{4,12},{5,21},{6,14},{7,23},{8,0},{9,25... | collective-permute-start | bytes 3145736 | tf_op jit(solution)/shard_map/ppermute | solution.py:256
  108.4 1.5 %collective-permute-start.27 = (bf16[1,2,128,512]{3,2,1,0:T(8,128)(2,1)S(1)}, bf16[1,2,128,512]{3,2,1,0:T(8,128)(2,1)S(1)}, u32[]{:S(2)}, u32[]{:S(2)}) collective-permute-start(bf16[1,2,128,512]{3,2,1,0:T(8,128)(2,1)S(1)} %collective-permute-done.22.refs_2_), channel_id=1, source_target_pairs={{0,1},{1,0},{2,3},{3,2},{4,5},{5,4},{6,7},{7,6},{8,9},{9,8},{10,11... | collective-permute-start | bytes 786440 | tf_op jit(solution)/shard_map/ppermute | solution.py:265
  108.4 1.9 %collective-permute-start.28 = (bf16[1,2,128,512]{3,2,1,0:T(8,128)(2,1)S(1)}, bf16[1,2,128,512]{3,2,1,0:T(8,128)(2,1)S(1)}, u32[]{:S(2)}, u32[]{:S(2)}) collective-permute-start(bf16[1,2,128,512]{3,2,1,0:T(8,128)(2,1)S(1)} %collective-permute-done.23.refs_3_), channel_id=1, source_target_pairs={{0,1},{1,0},{2,3},{3,2},{4,5},{5,4},{6,7},{7,6},{8,9},{9,8},{10,11... | collective-permute-start | bytes 786440 | tf_op jit(solution)/shard_map/ppermute | solution.py:265
  115.5 25.7 %collective-permute-start.29 = (bf16[2,1024,256]{2,1,0:T(8,128)(2,1)S(1)}, bf16[2,1024,256]{2,1,0:T(8,128)(2,1)S(1)}, u32[]{:S(2)}, u32[]{:S(2)}) collective-permute-start(bf16[2,1024,256]{2,1,0:T(8,128)(2,1)S(1)} %get-tuple-element.146), channel_id=1, source_target_pairs={{0,8},{1,17},{2,10},{3,19},{4,12},{5,21},{6,14},{7,23},{8,0},{9,25... | collective-permute-start | bytes 3145736 | tf_op jit(solution)/shard_map/ppermute | solution.py:256
  118.1 26.6 %collective-permute-start.33 = (bf16[2,1024,128]{2,1,0:T(8,128)(2,1)S(1)}, bf16[2,1024,128]{2,1,0:T(8,128)(2,1)S(1)}, u32[]{:S(2)}, u32[]{:S(2)}) collective-permute-start(bf16[2,1024,128]{2,1,0:T(8,128)(2,1)S(1)} %add_convert_fusion.2), channel_id=1, source_target_pairs={{0,16},{1,9},{2,18},{3,11},{4,20},{5,13},{6,22},{7,15},{8,24},{9,1... | collective-permute-start | bytes 1572872 | tf_op jit(solution)/shard_map/ppermute | solution.py:256
  118.3 27.5 %collective-permute-start.32 = (bf16[2,1024,128]{2,1,0:T(8,128)(2,1)S(1)}, bf16[2,1024,128]{2,1,0:T(8,128)(2,1)S(1)}, u32[]{:S(2)}, u32[]{:S(2)}) collective-permute-start(bf16[2,1024,128]{2,1,0:T(8,128)(2,1)S(1)} %add_convert_fusion), channel_id=1, source_target_pairs={{0,16},{1,9},{2,18},{3,11},{4,20},{5,13},{6,22},{7,15},{8,24},{9,1... | collective-permute-start | bytes 1572872 | tf_op jit(solution)/shard_map/ppermute | solution.py:256
  141.3 9.4 %collective-permute-start.30 = (bf16[2,1024,128]{2,1,0:T(8,128)(2,1)S(1)}, bf16[2,1024,128]{2,1,0:T(8,128)(2,1)S(1)}, u32[]{:S(2)}, u32[]{:S(2)}) collective-permute-start(bf16[2,1024,128]{2,1,0:T(8,128)(2,1)S(1)} %add_convert_fusion.1), channel_id=1, source_target_pairs={{0,16},{1,9},{2,18},{3,11},{4,20},{5,13},{6,22},{7,15},{8,24},{9,1... | collective-permute-start | bytes 1572872 | tf_op jit(solution)/shard_map/ppermute | solution.py:256

commit v9 on v8

--- a/solution.py
+++ b/solution.py
@@ -11,7 +11,7 @@
 STRETCH = 32
 WINDOW = 224
 CHUNKS = 4
-SCHEDULED_GFLOPS = (5, 5, 1.5, 0.01)
+SCHEDULED_GFLOPS = (5, 4, 1.5, 0.01)
 TILE = 128
 CORES = 2
 
@@ -318,6 +318,7 @@
     gathers = [Gather(block, chips) for block in mine]
     gathers[0].behind()
     gathers[0].ahead()
+    gathers[1].ahead()
     whole = other_core(whole)
 
     key_value, key_value_tangents, _ = lax.optimization_barrier(
@@ -371,7 +372,7 @@
     pair_second, prior = settle(pair_second, prior)
     gathers[0].exchange()
     gathers[0].farther()
-    gathers[1].ahead()
+    gathers[2].ahead()
     pair_first = attend(0, jnp.concatenate([prior, stacked[:half]], axis=0))
 
     pairs, send, sums = (pair_first, pair_second), (), ()
@@ -383,14 +384,14 @@
             gathers[chunk + 1].exchange()
             gathers[chunk + 1].behind()
             gathers[chunk + 1].farther()
-        if chunk + 2 < CHUNKS:
-            gathers[chunk + 2].ahead()
-        if 2 <= chunk < CHUNKS - 1:
-            last[chunk - 2], pairs = together(last[chunk - 2], pairs)
+        if chunk + 3 < CHUNKS:
+            gathers[chunk + 3].ahead()
         send, keep = project(
             SCHEDULED_GFLOPS[chunk], pairs, gathers[chunk].pieces(chunk, whole)
         )
         kept.append(keep)
+        if chunk >= 2:
+            last[chunk - 2], send = together(last[chunk - 2], send)
         received.append(across(send, 0))
         if chunk:
             received[chunk - 1], send = together(received[chunk - 1], send)

time: 152 us -> 146 us (0.961)
  waiting for transfers between devices: 68.5 us -> 63.7 us
  starting transfers between devices: 37.3 us -> 35.6 us
    ppermute x12, waiting for transfers between devices: 39.9 us -> 34.7 us  [along(): lax.ppermute(block, 'seq', [(i, (i + CORES * chips) % size) for i in rang...]
    ppermute x8, starting transfers between devices: 14.1 us -> 10.9 us  [across(): return lax.ppermute(block, ('kv', 'seq'), route)]
    ppermute x12, starting transfers between devices: 16.4 us -> 18.9 us  [along(): lax.ppermute(block, 'seq', [(i, (i + CORES * chips) % size) for i in rang...]
    unnamed x20 -> x16, local copies, waits for them, and re-layouts: 3.7 us -> 3.69 us
  transfers between devices with their start and end apart: 34 -> 34, of which waited for: 15 -> 19; matrix products, arithmetic and copies ran while one was open for 3% -> 3% of each run, Pallas kernels for 22% -> 23%
where the time goes in v9:
time: 146 us
  waiting for transfers between devices  63.7 us (44%)
  Pallas kernels  37.1 us (25%)
  starting transfers between devices  35.6 us (24%)
  local copies, waits for them, and re-layouts  6 us (4%)
  other arithmetic  2.18 us (1%)
    ppermute x12, waiting for transfers between devices, along(): lax.ppermute(block, 'seq', [(i, (i + CORES * chips) % size) for i in rang...  34.7 us
    ppermute x8, waiting for transfers between devices, across(): return lax.ppermute(block, ('kv', 'seq'), route)  25 us
    pallas_call x4, Pallas kernels, project(): pl.pallas_call(functools.partial(project_kernel, indices), grid=(2 * step...  21.3 us
    ppermute x12, starting transfers between devices, along(): lax.ppermute(block, 'seq', [(i, (i + CORES * chips) % size) for i in rang...  18.9 us
    ppermute x8, starting transfers between devices, across(): return lax.ppermute(block, ('kv', 'seq'), route)  10.9 us
    pallas_call x2, Pallas kernels, attention(): pl.pallas_call(functools.partial(attention_kernel, heads, head_dim, offse...  9.39 us
    pallas_call x4, Pallas kernels, finish(): pl.pallas_call(finish_kernel, grid=(tokens // tile,), in_specs=[pl.BlockS...  4.45 us
    ppermute x13, waiting for transfers between devices, other_core(): lax.ppermute(block, 'seq', [(i, i ^ 1) for i in range(lax.axis_size('seq'...  4.07 us
  transfers between devices with their start and end apart: 34, of which 19 were waited for; matrix products, arithmetic and copies ran while one was open for 3% of the time, Pallas kernels for 23%

profile of v9, /device:TPU:0, one launch (start us, length us, event | category | flops | bytes accessed | tf_op | source)
XLA Modules:
  0.0 145.5 jit_solution(14660807865618997828)
XLA Ops:
  0.7 1.0 copy-done.2
  1.8 1.0 copy-done.3
  2.8 2.0 %arrange.1 = (bf16[4,2,128,512]{3,2,1,0:T(8,128)(2,1)}, bf16[1,2,128,512]{3,2,1,0:T(8,128)(2,1)}, bf16[1,2,128,512]{3,2,1,0:T(8,128)(2,1)}, bf16[1,2,128,512]{3,...) custom-call(s32[4]{0:T(128)S(1)} %add_xor_fusion.owner_ref, bf16[128,2048]{1,0:T(8,128)(2,1)S(1)} %copy-done.2, ...), custom_call_target="tpu_custom_call" | custom-call | tf_op jit(solution)/shard_map/arrange/pallas_call | solution.py:42
  4.8 3.0 %collective-permute-start = (bf16[1,2,128,512]{3,2,1,0:T(8,128)(2,1)}, bf16[1,2,128,512]{3,2,1,0:T(8,128)(2,1)}, u32[]{:S(2)}, u32[]{:S(2)}) collective-permute-start(bf16[1,2,128,512]{3,2,1,0:T(8,128)(2,1)} %get-tuple-element.99.refs_0_), channel_id=1, source_target_pairs={{0,2},{1,3},{2,4},{3,5},{4,6},{5,7},{6,0},{7,1},{8,10},{9,11},{10,... | collective-permute-start | bytes 786440 | tf_op jit(solution)/shard_map/ppermute | solution.py:261
  7.8 2.0 %collective-permute-start.1 = (bf16[1,2,128,512]{3,2,1,0:T(8,128)(2,1)}, bf16[1,2,128,512]{3,2,1,0:T(8,128)(2,1)}, u32[]{:S(2)}, u32[]{:S(2)}) collective-permute-start(bf16[1,2,128,512]{3,2,1,0:T(8,128)(2,1)} %get-tuple-element.99.refs_0_), channel_id=1, source_target_pairs={{0,6},{1,7},{2,0},{3,1},{4,2},{5,3},{6,4},{7,5},{8,14},{9,15},{10,... | collective-permute-start | bytes 786440 | tf_op jit(solution)/shard_map/ppermute | solution.py:261
  9.8 1.1 copy.26
  11.3 0.7 slice.60
  12.0 3.1 %collective-permute-start.3 = (bf16[224,512]{1,0:T(8,128)(2,1)}, bf16[224,512]{1,0:T(8,128)(2,1)}, u32[]{:S(2)}, u32[]{:S(2)}) collective-permute-start(bf16[224,512]{1,0:T(8,128)(2,1)} %slice.60), channel_id=1, source_target_pairs={{0,1},{1,2},{2,3},{3,4},{4,5},{5,6},{6,7},{8,9},{9,10},{10,11},{11... | collective-permute-start | bytes 688136 | tf_op jit(solution)/shard_map/ppermute | solution.py:331
  15.9 1.6 %copy-done.1 = bf16[1024,1024]{1,0:T(8,128)(2,1)S(1)} copy-done((bf16[1024,1024]{1,0:T(8,128)(2,1)S(1)}, bf16[1024,1024]{1,0:T(8,128)(2,1)}, u32[]{:S(2)}) %copy-start.1) | copy-done | bytes 2097176
  17.5 4.6 %attention.2.second_ref = bf16[512,2048]{1,0:T(8,128)(2,1)S(1)} custom-call(s32[8]{0:T(128)S(1)} %pad_add_fusion.order_ref, bf16[1024,1024]{1,0:T(8,128)(2,1)S(1)} %copy-done, bf16[1024,1024]{1,0:T(8,128)(2,1)S(1)} %copy-done.1, bf16[1024,512]{1,0:T(8,128)(2,1)S(1)} %pad_maximum_fusion.ctx_ref, s32[1024,128]{1,0:T(8,128)S(1)} %broadcast_in_dim.13.low_ref), custom_call_target="tpu_custom_call" | custom-call | flops 1048576 | bytes 512 | tf_op jit(solution)/shard_map/attention/pallas_call | solution.py:126
  22.2 5.6 %collective-permute-done.2.refs_1_ = bf16[1,2,128,512]{3,2,1,0:T(8,128)(2,1)} collective-permute-done((bf16[1,2,128,512]{3,2,1,0:T(8,128)(2,1)}, bf16[1,2,128,512]{3,2,1,0:T(8,128)(2,1)}, u32[]{:S(2)}, u32[]{:S(2)}) %collective-permute-start.2) | collective-permute-done | bytes 262176 | tf_op jit(solution)/shard_map/ppermute | solution.py:261
  27.7 2.2 %collective-permute-start.4 = (bf16[1,2,128,512]{3,2,1,0:T(8,128)(2,1)}, bf16[1,2,128,512]{3,2,1,0:T(8,128)(2,1)S(1)}, u32[]{:S(2)}, u32[]{:S(2)}) collective-permute-start(bf16[1,2,128,512]{3,2,1,0:T(8,128)(2,1)} %collective-permute-done.refs_1_), channel_id=1, source_target_pairs={{0,2},{1,3},{2,4},{3,5},{4,6},{5,7},{6,0},{7,1},{8,10},{9,11},{10,... | collective-permute-start | bytes 786440 | tf_op jit(solution)/shard_map/ppermute | solution.py:261
  30.5 1.5 %collective-permute-start.7 = (bf16[1,2,128,512]{3,2,1,0:T(8,128)(2,1)S(1)}, bf16[1,2,128,512]{3,2,1,0:T(8,128)(2,1)S(1)}, u32[]{:S(2)}, u32[]{:S(2)}) collective-permute-start(bf16[1,2,128,512]{3,2,1,0:T(8,128)(2,1)S(1)} %copy-done.5), channel_id=1, source_target_pairs={{0,2},{1,3},{2,4},{3,5},{4,6},{5,7},{6,0},{7,1},{8,10},{9,11},{10,... | collective-permute-start | bytes 786440 | tf_op jit(solution)/shard_map/ppermute | solution.py:261
  32.1 1.0 pad_maximum_fusion.1.ctx_ref
  33.1 4.8 %attention.3.first_ref = bf16[512,2048]{1,0:T(8,128)(2,1)S(1)} custom-call(s32[8]{0:T(128)S(1)} %pad_add_fusion.order_ref, bf16[1024,1024]{1,0:T(8,128)(2,1)S(1)} %copy-done, bf16[1024,1024]{1,0:T(8,128)(2,1)S(1)} %copy-done.1, bf16[736,512]{1,0:T(8,128)(2,1)S(1)} %pad_maximum_fusion.1.ctx_ref, s32[1024,128]{1,0:T(8,128)S(1)} %broadcast_in_dim.13.low_ref), custom_call_target="tpu_custom_call" | custom-call | flops 1048576 | bytes 512 | tf_op jit(solution)/shard_map/attention/pallas_call | solution.py:126
  37.8 1.6 %collective-permute-done.4.refs_2_ = bf16[1,2,128,512]{3,2,1,0:T(8,128)(2,1)S(1)} collective-permute-done((bf16[1,2,128,512]{3,2,1,0:T(8,128)(2,1)}, bf16[1,2,128,512]{3,2,1,0:T(8,128)(2,1)S(1)}, u32[]{:S(2)}, u32[]{:S(2)}) %collective-permute-start.4) | collective-permute-done | bytes 262176 | tf_op jit(solution)/shard_map/ppermute | solution.py:261
  39.4 4.1 %collective-permute-done.7.refs_1_ = bf16[1,2,128,512]{3,2,1,0:T(8,128)(2,1)S(1)} collective-permute-done((bf16[1,2,128,512]{3,2,1,0:T(8,128)(2,1)S(1)}, bf16[1,2,128,512]{3,2,1,0:T(8,128)(2,1)S(1)}, u32[]{:S(2)}, u32[]{:S(2)}) %collective-permute-start.7) | collective-permute-done | bytes 262176 | tf_op jit(solution)/shard_map/ppermute | solution.py:261
  44.0 3.5 %collective-permute-start.11 = (bf16[1,2,128,512]{3,2,1,0:T(8,128)(2,1)}, bf16[1,2,128,512]{3,2,1,0:T(8,128)(2,1)S(1)}, u32[]{:S(2)}, u32[]{:S(2)}) collective-permute-start(bf16[1,2,128,512]{3,2,1,0:T(8,128)(2,1)} %get-tuple-element.114.refs_0_), channel_id=1, source_target_pairs={{0,6},{1,7},{2,0},{3,1},{4,2},{5,3},{6,4},{7,5},{8,14},{9,15},{10,... | collective-permute-start | bytes 786440 | tf_op jit(solution)/shard_map/ppermute | solution.py:261
  47.5 5.4 %project.4 = (bf16[2,1024,256]{2,1,0:T(8,128)(2,1)S(1)}, bf16[2,1024,256]{2,1,0:T(8,128)(2,1)S(1)}) custom-call(bf16[512,2048]{1,0:T(8,128)(2,1)S(1)} %attention.3.first_ref, bf16[512,2048]{1,0:T(8,128)(2,1)S(1)} %attention.2.second_ref, bf16[1,2,128,512]{3,2,1,0:T(8,128)(2,1)} %get-tuple-element.99.refs_0_, ...), custom_call_target="tpu_custom_call" | custom-call | flops 5000000000 | bytes 512 | tf_op jit(solution)/shard_map/project/pallas_call | solution.py:200
  53.0 1.6 %collective-permute-start.19 = (bf16[2,1024,256]{2,1,0:T(8,128)(2,1)S(1)}, bf16[2,1024,256]{2,1,0:T(8,128)(2,1)S(1)}, u32[]{:S(2)}, u32[]{:S(2)}) collective-permute-start(bf16[2,1024,256]{2,1,0:T(8,128)(2,1)S(1)} %get-tuple-element.113), channel_id=1, source_target_pairs={{0,8},{1,17},{2,10},{3,19},{4,12},{5,21},{6,14},{7,23},{8,0},{9,25... | collective-permute-start | bytes 3145736 | tf_op jit(solution)/shard_map/ppermute | solution.py:256
  54.6 3.5 %collective-permute-done.11.refs_3_ = bf16[1,2,128,512]{3,2,1,0:T(8,128)(2,1)S(1)} collective-permute-done((bf16[1,2,128,512]{3,2,1,0:T(8,128)(2,1)}, bf16[1,2,128,512]{3,2,1,0:T(8,128)(2,1)S(1)}, u32[]{:S(2)}, u32[]{:S(2)}) %collective-permute-start.11) | collective-permute-done | bytes 262176 | tf_op jit(solution)/shard_map/ppermute | solution.py:261
  58.1 7.4 %collective-permute-done.13.refs_1_ = bf16[1,2,128,512]{3,2,1,0:T(8,128)(2,1)S(1)} collective-permute-done((bf16[1,2,128,512]{3,2,1,0:T(8,128)(2,1)S(1)}, bf16[1,2,128,512]{3,2,1,0:T(8,128)(2,1)S(1)}, u32[]{:S(2)}, u32[]{:S(2)}) %collective-permute-start.13) | collective-permute-done | bytes 262176 | tf_op jit(solution)/shard_map/ppermute | solution.py:261
  66.0 1.0 collective-permute-done.14.refs_6_
  67.4 5.4 %project.5 = (bf16[2,1024,256]{2,1,0:T(8,128)(2,1)S(1)}, bf16[2,1024,256]{2,1,0:T(8,128)(2,1)S(1)}) custom-call(bf16[512,2048]{1,0:T(8,128)(2,1)S(1)} %attention.3.first_ref, bf16[512,2048]{1,0:T(8,128)(2,1)S(1)} %attention.2.second_ref, bf16[1,2,128,512]{3,2,1,0:T(8,128)(2,1)} %get-tuple-element.114.refs_0_, ...), custom_call_target="tpu_custom_call" | custom-call | flops 4000000000 | bytes 512 | tf_op jit(solution)/shard_map/project/pallas_call | solution.py:200
  72.7 1.6 %collective-permute-start.25 = (bf16[2,1024,256]{2,1,0:T(8,128)(2,1)S(1)}, bf16[2,1024,256]{2,1,0:T(8,128)(2,1)S(1)}, u32[]{:S(2)}, u32[]{:S(2)}) collective-permute-start(bf16[2,1024,256]{2,1,0:T(8,128)(2,1)S(1)} %get-tuple-element.127), channel_id=1, source_target_pairs={{0,8},{1,17},{2,10},{3,19},{4,12},{5,21},{6,14},{7,23},{8,0},{9,25... | collective-permute-start | bytes 3145736 | tf_op jit(solution)/shard_map/ppermute | solution.py:256
  74.3 3.8 %collective-permute-start.17 = (bf16[1,2,128,512]{3,2,1,0:T(8,128)(2,1)S(1)}, bf16[1,2,128,512]{3,2,1,0:T(8,128)(2,1)S(1)}, u32[]{:S(2)}, u32[]{:S(2)}) collective-permute-start(bf16[1,2,128,512]{3,2,1,0:T(8,128)(2,1)S(1)} %copy-done.5), channel_id=1, source_target_pairs={{0,6},{1,7},{2,0},{3,1},{4,2},{5,3},{6,4},{7,5},{8,14},{9,15},{10,... | collective-permute-start | bytes 786440 | tf_op jit(solution)/shard_map/ppermute | solution.py:261
  78.3 1.6 %collective-permute-start.26 = (bf16[2,1024,128]{2,1,0:T(8,128)(2,1)S(1)}, bf16[2,1024,128]{2,1,0:T(8,128)(2,1)S(1)}, u32[]{:S(2)}, u32[]{:S(2)}) collective-permute-start(bf16[2,1024,128]{2,1,0:T(8,128)(2,1)S(1)} %add_convert_fusion.3), channel_id=1, source_target_pairs={{0,16},{1,9},{2,18},{3,11},{4,20},{5,13},{6,22},{7,15},{8,24},{9,1... | collective-permute-start | bytes 1572872 | tf_op jit(solution)/shard_map/ppermute | solution.py:256
  79.9 5.4 %collective-permute-done.16.refs_2_ = bf16[1,2,128,512]{3,2,1,0:T(8,128)(2,1)S(1)} collective-permute-done((bf16[1,2,128,512]{3,2,1,0:T(8,128)(2,1)S(1)}, bf16[1,2,128,512]{3,2,1,0:T(8,128)(2,1)S(1)}, u32[]{:S(2)}, u32[]{:S(2)}) %collective-permute-start.16) | collective-permute-done | bytes 262176 | tf_op jit(solution)/shard_map/ppermute | solution.py:261
  85.3 3.4 %collective-permute-done.17.refs_3_ = bf16[1,2,128,512]{3,2,1,0:T(8,128)(2,1)S(1)} collective-permute-done((bf16[1,2,128,512]{3,2,1,0:T(8,128)(2,1)S(1)}, bf16[1,2,128,512]{3,2,1,0:T(8,128)(2,1)S(1)}, u32[]{:S(2)}, u32[]{:S(2)}) %collective-permute-start.17) | collective-permute-done | bytes 262176 | tf_op jit(solution)/shard_map/ppermute | solution.py:261
  89.2 1.0 collective-permute-done.20.refs_6_
  90.6 2.7 %collective-permute-start.23 = (bf16[1,2,128,512]{3,2,1,0:T(8,128)(2,1)S(1)}, bf16[1,2,128,512]{3,2,1,0:T(8,128)(2,1)S(1)}, u32[]{:S(2)}, u32[]{:S(2)}) collective-permute-start(bf16[1,2,128,512]{3,2,1,0:T(8,128)(2,1)S(1)} %get-tuple-element.145.refs_0_), channel_id=1, source_target_pairs={{0,6},{1,7},{2,0},{3,1},{4,2},{5,3},{6,4},{7,5},{8,14},{9,15},{10,... | collective-permute-start | bytes 786440 | tf_op jit(solution)/shard_map/ppermute | solution.py:261
  93.2 5.2 %project.6 = (bf16[2,1024,256]{2,1,0:T(8,128)(2,1)S(1)}, bf16[2,1024,256]{2,1,0:T(8,128)(2,1)S(1)}) custom-call(bf16[512,2048]{1,0:T(8,128)(2,1)S(1)} %attention.3.first_ref, bf16[512,2048]{1,0:T(8,128)(2,1)S(1)} %attention.2.second_ref, bf16[1,2,128,512]{3,2,1,0:T(8,128)(2,1)S(1)} %copy-done.5, bf16[1,2,128,512]{3,2,1,0:T(8,128)(2,1)S(1)} %collective-permute-done.7.refs_1_, ...), custom_call_target="tpu_custom_call" | custom-call | flops 1500000000 | bytes 512 | tf_op jit(solution)/shard_map/project/pallas_call | solution.py:200
  98.6 1.6 %collective-permute-start.29 = (bf16[2,1024,128]{2,1,0:T(8,128)(2,1)S(1)}, bf16[2,1024,128]{2,1,0:T(8,128)(2,1)S(1)}, u32[]{:S(2)}, u32[]{:S(2)}) collective-permute-start(bf16[2,1024,128]{2,1,0:T(8,128)(2,1)S(1)} %add_convert_fusion.2), channel_id=1, source_target_pairs={{0,16},{1,9},{2,18},{3,11},{4,20},{5,13},{6,22},{7,15},{8,24},{9,1... | collective-permute-start | bytes 1572872 | tf_op jit(solution)/shard_map/ppermute | solution.py:256
  100.2 0.5 collective-permute-start.32
  100.8 3.8 %collective-permute-done.23.refs_3_ = bf16[1,2,128,512]{3,2,1,0:T(8,128)(2,1)S(1)} collective-permute-done((bf16[1,2,128,512]{3,2,1,0:T(8,128)(2,1)S(1)}, bf16[1,2,128,512]{3,2,1,0:T(8,128)(2,1)S(1)}, u32[]{:S(2)}, u32[]{:S(2)}) %collective-permute-start.23) | collective-permute-done | bytes 262176 | tf_op jit(solution)/shard_map/ppermute | solution.py:261
  105.0 1.0 collective-permute-done.27.refs_6_
  106.4 5.2 %project.7 = (bf16[2,1024,256]{2,1,0:T(8,128)(2,1)S(1)}, bf16[2,1024,256]{2,1,0:T(8,128)(2,1)S(1)}) custom-call(bf16[512,2048]{1,0:T(8,128)(2,1)S(1)} %attention.3.first_ref, bf16[512,2048]{1,0:T(8,128)(2,1)S(1)} %attention.2.second_ref, bf16[1,2,128,512]{3,2,1,0:T(8,128)(2,1)S(1)} %get-tuple-element.145.refs_0_, ...), custom_call_target="tpu_custom_call" | custom-call | flops 10000000 | bytes 512 | tf_op jit(solution)/shard_map/project/pallas_call | solution.py:200
  111.7 1.7 %collective-permute-done.29.last_ref = bf16[2,1024,128]{2,1,0:T(8,128)(2,1)S(1)} collective-permute-done((bf16[2,1024,128]{2,1,0:T(8,128)(2,1)S(1)}, bf16[2,1024,128]{2,1,0:T(8,128)(2,1)S(1)}, u32[]{:S(2)}, u32[]{:S(2)}) %collective-permute-start.29) | collective-permute-done | bytes 524320 | tf_op jit(solution)/shard_map/ppermute | solution.py:256
  113.4 1.0 collective-permute-start.30
  114.4 3.8 %collective-permute-done.32.received_ref = bf16[2,1024,256]{2,1,0:T(8,128)(2,1)S(1)} collective-permute-done((bf16[2,1024,256]{2,1,0:T(8,128)(2,1)S(1)}, bf16[2,1024,256]{2,1,0:T(8,128)(2,1)S(1)}, u32[]{:S(2)}, u32[]{:S(2)}) %collective-permute-start.32) | collective-permute-done | bytes 1048608 | tf_op jit(solution)/shard_map/ppermute | solution.py:256
  118.3 1.6 %collective-permute-start.33 = (bf16[2,1024,128]{2,1,0:T(8,128)(2,1)S(1)}, bf16[2,1024,128]{2,1,0:T(8,128)(2,1)S(1)}, u32[]{:S(2)}, u32[]{:S(2)}) collective-permute-start(bf16[2,1024,128]{2,1,0:T(8,128)(2,1)S(1)} %add_convert_fusion), channel_id=1, source_target_pairs={{0,16},{1,9},{2,18},{3,11},{4,20},{5,13},{6,22},{7,15},{8,24},{9,1... | collective-permute-start | bytes 1572872 | tf_op jit(solution)/shard_map/ppermute | solution.py:256
  119.9 15.1 %collective-permute-done.30.received_ref = bf16[2,1024,256]{2,1,0:T(8,128)(2,1)S(1)} collective-permute-done((bf16[2,1024,256]{2,1,0:T(8,128)(2,1)S(1)}, bf16[2,1024,256]{2,1,0:T(8,128)(2,1)S(1)}, u32[]{:S(2)}, u32[]{:S(2)}) %collective-permute-start.30) | collective-permute-done | bytes 1048608 | tf_op jit(solution)/shard_map/ppermute | solution.py:256
  135.2 1.6 %collective-permute-start.31 = (bf16[2,1024,128]{2,1,0:T(8,128)(2,1)S(1)}, bf16[2,1024,128]{2,1,0:T(8,128)(2,1)S(1)}, u32[]{:S(2)}, u32[]{:S(2)}) collective-permute-start(bf16[2,1024,128]{2,1,0:T(8,128)(2,1)S(1)} %add_convert_fusion.1), channel_id=1, source_target_pairs={{0,16},{1,9},{2,18},{3,11},{4,20},{5,13},{6,22},{7,15},{8,24},{9,1... | collective-permute-start | bytes 1572872 | tf_op jit(solution)/shard_map/ppermute | solution.py:256
  136.7 1.1 finish.4
  137.8 1.1 finish.5
  139.0 1.1 finish.6
  140.1 4.3 %collective-permute-done.31.last_ref = bf16[2,1024,128]{2,1,0:T(8,128)(2,1)S(1)} collective-permute-done((bf16[2,1024,128]{2,1,0:T(8,128)(2,1)S(1)}, bf16[2,1024,128]{2,1,0:T(8,128)(2,1)S(1)}, u32[]{:S(2)}, u32[]{:S(2)}) %collective-permute-start.31) | collective-permute-done | bytes 524320 | tf_op jit(solution)/shard_map/ppermute | solution.py:256
  144.4 1.1 finish.7
  (69 shorter events, 5.6 us)
Async XLA Ops:
  0.7 1.0 copy-start.2
  1.8 1.0 copy-start.3
  2.8 8.2 %copy-start.6 = (bf16[1024,2,128]{2,1,0:T(2,128)(2,1)S(1)}, bf16[1024,2,128]{2,1,0:T(2,128)(2,1)}, u32[]{:S(2)}) copy-start(bf16[1024,2,128]{2,1,0:T(2,128)(2,1)} %param.9) | copy-start | bytes 1572868
  4.8 6.4 %copy-start.4 = (bf16[1,2,128,512]{3,2,1,0:T(8,128)(2,1)}, bf16[1,2,128,512]{3,2,1,0:T(8,128)(2,1)S(1)}, u32[]{:S(2)}) copy-start(bf16[1,2,128,512]{3,2,1,0:T(8,128)(2,1)S(1)} %get-tuple-element.129.refs_0_) | copy-start | bytes 786436
  4.8 17.4 %collective-permute-start = (bf16[1,2,128,512]{3,2,1,0:T(8,128)(2,1)}, bf16[1,2,128,512]{3,2,1,0:T(8,128)(2,1)}, u32[]{:S(2)}, u32[]{:S(2)}) collective-permute-start(bf16[1,2,128,512]{3,2,1,0:T(8,128)(2,1)} %get-tuple-element.99.refs_0_), channel_id=1, source_target_pairs={{0,2},{1,3},{2,4},{3,5},{4,6},{5,7},{6,0},{7,1},{8,10},{9,11},{10,... | collective-permute-start | bytes 786440 | tf_op jit(solution)/shard_map/ppermute | solution.py:261
  7.8 14.3 %collective-permute-start.1 = (bf16[1,2,128,512]{3,2,1,0:T(8,128)(2,1)}, bf16[1,2,128,512]{3,2,1,0:T(8,128)(2,1)}, u32[]{:S(2)}, u32[]{:S(2)}) collective-permute-start(bf16[1,2,128,512]{3,2,1,0:T(8,128)(2,1)} %get-tuple-element.99.refs_0_), channel_id=1, source_target_pairs={{0,6},{1,7},{2,0},{3,1},{4,2},{5,3},{6,4},{7,5},{8,14},{9,15},{10,... | collective-permute-start | bytes 786440 | tf_op jit(solution)/shard_map/ppermute | solution.py:261
  9.8 17.9 %collective-permute-start.2 = (bf16[1,2,128,512]{3,2,1,0:T(8,128)(2,1)}, bf16[1,2,128,512]{3,2,1,0:T(8,128)(2,1)}, u32[]{:S(2)}, u32[]{:S(2)}) collective-permute-start(bf16[1,2,128,512]{3,2,1,0:T(8,128)(2,1)} %get-tuple-element.114.refs_0_), channel_id=1, source_target_pairs={{0,2},{1,3},{2,4},{3,5},{4,6},{5,7},{6,0},{7,1},{8,10},{9,11},{10,... | collective-permute-start | bytes 786440 | tf_op jit(solution)/shard_map/ppermute | solution.py:261
  9.8 33.6 %collective-permute-start.8 = (bf16[4,2,128,512]{3,2,1,0:T(8,128)(2,1)}, bf16[4,2,128,512]{3,2,1,0:T(8,128)(2,1)}, u32[]{:S(2)}, u32[]{:S(2)}) collective-permute-start(bf16[4,2,128,512]{3,2,1,0:T(8,128)(2,1)} %get-tuple-element.98), channel_id=1, source_target_pairs={{0,1},{1,0},{2,3},{3,2},{4,5},{5,4},{6,7},{7,6},{8,9},{9,8},{10,11... | collective-permute-start | bytes 3145736 | tf_op jit(solution)/shard_map/ppermute | solution.py:265
  11.1 4.1 %copy-start.7 = (s32[64]{0:T(128)S(1)}, s32[64]{0:T(128)}, u32[]{:S(2)}) copy-start(s32[64]{0:T(128)} %param.11) | copy-start | bytes 772
  11.2 4.7 %copy-start = (bf16[1024,1024]{1,0:T(8,128)(2,1)S(1)}, bf16[1024,1024]{1,0:T(8,128)(2,1)}, u32[]{:S(2)}) copy-start(bf16[1024,1024]{1,0:T(8,128)(2,1)} %q_ref.3) | copy-start | bytes 6291460
  12.0 10.1 %collective-permute-start.3 = (bf16[224,512]{1,0:T(8,128)(2,1)}, bf16[224,512]{1,0:T(8,128)(2,1)}, u32[]{:S(2)}, u32[]{:S(2)}) collective-permute-start(bf16[224,512]{1,0:T(8,128)(2,1)} %slice.60), channel_id=1, source_target_pairs={{0,1},{1,2},{2,3},{3,4},{4,5},{5,6},{6,7},{8,9},{9,10},{10,11},{11... | collective-permute-start | bytes 688136 | tf_op jit(solution)/shard_map/ppermute | solution.py:331
  15.9 1.6 %copy-start.1 = (bf16[1024,1024]{1,0:T(8,128)(2,1)S(1)}, bf16[1024,1024]{1,0:T(8,128)(2,1)}, u32[]{:S(2)}) copy-start(bf16[1024,1024]{1,0:T(8,128)(2,1)} %qt_ref.3) | copy-start | bytes 6291460
  17.5 13.0 %copy-start.5 = (bf16[1,2,128,512]{3,2,1,0:T(8,128)(2,1)S(1)}, bf16[1,2,128,512]{3,2,1,0:T(8,128)(2,1)}, u32[]{:S(2)}) copy-start(bf16[1,2,128,512]{3,2,1,0:T(8,128)(2,1)} %copy-done.4) | copy-start | bytes 786436
  27.7 11.7 %collective-permute-start.4 = (bf16[1,2,128,512]{3,2,1,0:T(8,128)(2,1)}, bf16[1,2,128,512]{3,2,1,0:T(8,128)(2,1)S(1)}, u32[]{:S(2)}, u32[]{:S(2)}) collective-permute-start(bf16[1,2,128,512]{3,2,1,0:T(8,128)(2,1)} %collective-permute-done.refs_1_), channel_id=1, source_target_pairs={{0,2},{1,3},{2,4},{3,5},{4,6},{5,7},{6,0},{7,1},{8,10},{9,11},{10,... | collective-permute-start | bytes 786440 | tf_op jit(solution)/shard_map/ppermute | solution.py:261
  30.0 9.4 %collective-permute-start.5 = (bf16[1,2,128,512]{3,2,1,0:T(8,128)(2,1)}, bf16[1,2,128,512]{3,2,1,0:T(8,128)(2,1)S(1)}, u32[]{:S(2)}, u32[]{:S(2)}) collective-permute-start(bf16[1,2,128,512]{3,2,1,0:T(8,128)(2,1)} %collective-permute-done.refs_1_), channel_id=1, source_target_pairs={{0,1},{1,0},{2,3},{3,2},{4,5},{5,4},{6,7},{7,6},{8,9},{9,8},{10,11... | collective-permute-start | bytes 786440 | tf_op jit(solution)/shard_map/ppermute | solution.py:265
  30.0 9.4 %collective-permute-start.6 = (bf16[1,2,128,512]{3,2,1,0:T(8,128)(2,1)}, bf16[1,2,128,512]{3,2,1,0:T(8,128)(2,1)S(1)}, u32[]{:S(2)}, u32[]{:S(2)}) collective-permute-start(bf16[1,2,128,512]{3,2,1,0:T(8,128)(2,1)} %collective-permute-done.1.refs_3_), channel_id=1, source_target_pairs={{0,1},{1,0},{2,3},{3,2},{4,5},{5,4},{6,7},{7,6},{8,9},{9,8},{10,11... | collective-permute-start | bytes 786440 | tf_op jit(solution)/shard_map/ppermute | solution.py:265
  30.5 13.0 %collective-permute-start.7 = (bf16[1,2,128,512]{3,2,1,0:T(8,128)(2,1)S(1)}, bf16[1,2,128,512]{3,2,1,0:T(8,128)(2,1)S(1)}, u32[]{:S(2)}, u32[]{:S(2)}) collective-permute-start(bf16[1,2,128,512]{3,2,1,0:T(8,128)(2,1)S(1)} %copy-done.5), channel_id=1, source_target_pairs={{0,2},{1,3},{2,4},{3,5},{4,6},{5,7},{6,0},{7,1},{8,10},{9,11},{10,... | collective-permute-start | bytes 786440 | tf_op jit(solution)/shard_map/ppermute | solution.py:261
  43.5 4.1 %collective-permute-start.9 = (bf16[1,2,128,512]{3,2,1,0:T(8,128)(2,1)S(1)}, bf16[1,2,128,512]{3,2,1,0:T(8,128)(2,1)S(1)}, u32[]{:S(2)}, u32[]{:S(2)}) collective-permute-start(bf16[1,2,128,512]{3,2,1,0:T(8,128)(2,1)S(1)} %collective-permute-done.4.refs_2_), channel_id=1, source_target_pairs={{0,1},{1,0},{2,3},{3,2},{4,5},{5,4},{6,7},{7,6},{8,9},{9,8},{10,11... | collective-permute-start | bytes 786440 | tf_op jit(solution)/shard_map/ppermute | solution.py:265
  43.5 11.2 %collective-permute-start.10 = (bf16[1,2,128,512]{3,2,1,0:T(8,128)(2,1)}, bf16[1,2,128,512]{3,2,1,0:T(8,128)(2,1)S(1)}, u32[]{:S(2)}, u32[]{:S(2)}) collective-permute-start(bf16[1,2,128,512]{3,2,1,0:T(8,128)(2,1)} %collective-permute-done.2.refs_1_), channel_id=1, source_target_pairs={{0,2},{1,3},{2,4},{3,5},{4,6},{5,7},{6,0},{7,1},{8,10},{9,11},{10,... | collective-permute-start | bytes 786440 | tf_op jit(solution)/shard_map/ppermute | solution.py:261
  43.5 14.6 %collective-permute-start.12 = (bf16[1,2,128,512]{3,2,1,0:T(8,128)(2,1)}, bf16[1,2,128,512]{3,2,1,0:T(8,128)(2,1)S(1)}, u32[]{:S(2)}, u32[]{:S(2)}) collective-permute-start(bf16[1,2,128,512]{3,2,1,0:T(8,128)(2,1)} %collective-permute-done.2.refs_1_), channel_id=1, source_target_pairs={{0,1},{1,0},{2,3},{3,2},{4,5},{5,4},{6,7},{7,6},{8,9},{9,8},{10,11... | collective-permute-start | bytes 786440 | tf_op jit(solution)/shard_map/ppermute | solution.py:265
  44.0 14.1 %collective-permute-start.11 = (bf16[1,2,128,512]{3,2,1,0:T(8,128)(2,1)}, bf16[1,2,128,512]{3,2,1,0:T(8,128)(2,1)S(1)}, u32[]{:S(2)}, u32[]{:S(2)}) collective-permute-start(bf16[1,2,128,512]{3,2,1,0:T(8,128)(2,1)} %get-tuple-element.114.refs_0_), channel_id=1, source_target_pairs={{0,6},{1,7},{2,0},{3,1},{4,2},{5,3},{6,4},{7,5},{8,14},{9,15},{10,... | collective-permute-start | bytes 786440 | tf_op jit(solution)/shard_map/ppermute | solution.py:261
  47.5 18.0 %collective-permute-start.13 = (bf16[1,2,128,512]{3,2,1,0:T(8,128)(2,1)S(1)}, bf16[1,2,128,512]{3,2,1,0:T(8,128)(2,1)S(1)}, u32[]{:S(2)}, u32[]{:S(2)}) collective-permute-start(bf16[1,2,128,512]{3,2,1,0:T(8,128)(2,1)S(1)} %get-tuple-element.145.refs_0_), channel_id=1, source_target_pairs={{0,2},{1,3},{2,4},{3,5},{4,6},{5,7},{6,0},{7,1},{8,10},{9,11},{10,... | collective-permute-start | bytes 786440 | tf_op jit(solution)/shard_map/ppermute | solution.py:261
  53.0 25.2 %collective-permute-start.19 = (bf16[2,1024,256]{2,1,0:T(8,128)(2,1)S(1)}, bf16[2,1024,256]{2,1,0:T(8,128)(2,1)S(1)}, u32[]{:S(2)}, u32[]{:S(2)}) collective-permute-start(bf16[2,1024,256]{2,1,0:T(8,128)(2,1)S(1)} %get-tuple-element.113), channel_id=1, source_target_pairs={{0,8},{1,17},{2,10},{3,19},{4,12},{5,21},{6,14},{7,23},{8,0},{9,25... | collective-permute-start | bytes 3145736 | tf_op jit(solution)/shard_map/ppermute | solution.py:256
  65.5 1.5 %collective-permute-start.14 = (bf16[1,2,128,512]{3,2,1,0:T(8,128)(2,1)S(1)}, bf16[1,2,128,512]{3,2,1,0:T(8,128)(2,1)S(1)}, u32[]{:S(2)}, u32[]{:S(2)}) collective-permute-start(bf16[1,2,128,512]{3,2,1,0:T(8,128)(2,1)S(1)} %collective-permute-done.10.refs_2_), channel_id=1, source_target_pairs={{0,1},{1,0},{2,3},{3,2},{4,5},{5,4},{6,7},{7,6},{8,9},{9,8},{10,11... | collective-permute-start | bytes 786440 | tf_op jit(solution)/shard_map/ppermute | solution.py:265
  65.5 1.9 %collective-permute-start.15 = (bf16[1,2,128,512]{3,2,1,0:T(8,128)(2,1)S(1)}, bf16[1,2,128,512]{3,2,1,0:T(8,128)(2,1)S(1)}, u32[]{:S(2)}, u32[]{:S(2)}) collective-permute-start(bf16[1,2,128,512]{3,2,1,0:T(8,128)(2,1)S(1)} %collective-permute-done.11.refs_3_), channel_id=1, source_target_pairs={{0,1},{1,0},{2,3},{3,2},{4,5},{5,4},{6,7},{7,6},{8,9},{9,8},{10,11... | collective-permute-start | bytes 786440 | tf_op jit(solution)/shard_map/ppermute | solution.py:265
  72.7 25.8 %collective-permute-start.25 = (bf16[2,1024,256]{2,1,0:T(8,128)(2,1)S(1)}, bf16[2,1024,256]{2,1,0:T(8,128)(2,1)S(1)}, u32[]{:S(2)}, u32[]{:S(2)}) collective-permute-start(bf16[2,1024,256]{2,1,0:T(8,128)(2,1)S(1)} %get-tuple-element.127), channel_id=1, source_target_pairs={{0,8},{1,17},{2,10},{3,19},{4,12},{5,21},{6,14},{7,23},{8,0},{9,25... | collective-permute-start | bytes 3145736 | tf_op jit(solution)/shard_map/ppermute | solution.py:256
  74.3 11.0 %collective-permute-start.16 = (bf16[1,2,128,512]{3,2,1,0:T(8,128)(2,1)S(1)}, bf16[1,2,128,512]{3,2,1,0:T(8,128)(2,1)S(1)}, u32[]{:S(2)}, u32[]{:S(2)}) collective-permute-start(bf16[1,2,128,512]{3,2,1,0:T(8,128)(2,1)S(1)} %collective-permute-done.7.refs_1_), channel_id=1, source_target_pairs={{0,2},{1,3},{2,4},{3,5},{4,6},{5,7},{6,0},{7,1},{8,10},{9,11},{10,... | collective-permute-start | bytes 786440 | tf_op jit(solution)/shard_map/ppermute | solution.py:261
  74.3 14.3 %collective-permute-start.18 = (bf16[1,2,128,512]{3,2,1,0:T(8,128)(2,1)S(1)}, bf16[1,2,128,512]{3,2,1,0:T(8,128)(2,1)S(1)}, u32[]{:S(2)}, u32[]{:S(2)}) collective-permute-start(bf16[1,2,128,512]{3,2,1,0:T(8,128)(2,1)S(1)} %collective-permute-done.7.refs_1_), channel_id=1, source_target_pairs={{0,1},{1,0},{2,3},{3,2},{4,5},{5,4},{6,7},{7,6},{8,9},{9,8},{10,11... | collective-permute-start | bytes 786440 | tf_op jit(solution)/shard_map/ppermute | solution.py:265
  74.3 14.3 %collective-permute-start.17 = (bf16[1,2,128,512]{3,2,1,0:T(8,128)(2,1)S(1)}, bf16[1,2,128,512]{3,2,1,0:T(8,128)(2,1)S(1)}, u32[]{:S(2)}, u32[]{:S(2)}) collective-permute-start(bf16[1,2,128,512]{3,2,1,0:T(8,128)(2,1)S(1)} %copy-done.5), channel_id=1, source_target_pairs={{0,6},{1,7},{2,0},{3,1},{4,2},{5,3},{6,4},{7,5},{8,14},{9,15},{10,... | collective-permute-start | bytes 786440 | tf_op jit(solution)/shard_map/ppermute | solution.py:261
  78.3 20.2 %collective-permute-start.26 = (bf16[2,1024,128]{2,1,0:T(8,128)(2,1)S(1)}, bf16[2,1024,128]{2,1,0:T(8,128)(2,1)S(1)}, u32[]{:S(2)}, u32[]{:S(2)}) collective-permute-start(bf16[2,1024,128]{2,1,0:T(8,128)(2,1)S(1)} %add_convert_fusion.3), channel_id=1, source_target_pairs={{0,16},{1,9},{2,18},{3,11},{4,20},{5,13},{6,22},{7,15},{8,24},{9,1... | collective-permute-start | bytes 1572872 | tf_op jit(solution)/shard_map/ppermute | solution.py:256
  88.6 1.5 %collective-permute-start.20 = (bf16[1,2,128,512]{3,2,1,0:T(8,128)(2,1)S(1)}, bf16[1,2,128,512]{3,2,1,0:T(8,128)(2,1)S(1)}, u32[]{:S(2)}, u32[]{:S(2)}) collective-permute-start(bf16[1,2,128,512]{3,2,1,0:T(8,128)(2,1)S(1)} %collective-permute-done.16.refs_2_), channel_id=1, source_target_pairs={{0,1},{1,0},{2,3},{3,2},{4,5},{5,4},{6,7},{7,6},{8,9},{9,8},{10,11... | collective-permute-start | bytes 786440 | tf_op jit(solution)/shard_map/ppermute | solution.py:265
  88.6 1.9 %collective-permute-start.21 = (bf16[1,2,128,512]{3,2,1,0:T(8,128)(2,1)S(1)}, bf16[1,2,128,512]{3,2,1,0:T(8,128)(2,1)S(1)}, u32[]{:S(2)}, u32[]{:S(2)}) collective-permute-start(bf16[1,2,128,512]{3,2,1,0:T(8,128)(2,1)S(1)} %collective-permute-done.17.refs_3_), channel_id=1, source_target_pairs={{0,1},{1,0},{2,3},{3,2},{4,5},{5,4},{6,7},{7,6},{8,9},{9,8},{10,11... | collective-permute-start | bytes 786440 | tf_op jit(solution)/shard_map/ppermute | solution.py:265
  89.2 11.6 %collective-permute-start.22 = (bf16[1,2,128,512]{3,2,1,0:T(8,128)(2,1)S(1)}, bf16[1,2,128,512]{3,2,1,0:T(8,128)(2,1)S(1)}, u32[]{:S(2)}, u32[]{:S(2)}) collective-permute-start(bf16[1,2,128,512]{3,2,1,0:T(8,128)(2,1)S(1)} %collective-permute-done.13.refs_1_), channel_id=1, source_target_pairs={{0,2},{1,3},{2,4},{3,5},{4,6},{5,7},{6,0},{7,1},{8,10},{9,11},{10,... | collective-permute-start | bytes 786440 | tf_op jit(solution)/shard_map/ppermute | solution.py:261
  90.2 14.3 %collective-permute-start.24 = (bf16[1,2,128,512]{3,2,1,0:T(8,128)(2,1)S(1)}, bf16[1,2,128,512]{3,2,1,0:T(8,128)(2,1)S(1)}, u32[]{:S(2)}, u32[]{:S(2)}) collective-permute-start(bf16[1,2,128,512]{3,2,1,0:T(8,128)(2,1)S(1)} %collective-permute-done.13.refs_1_), channel_id=1, source_target_pairs={{0,1},{1,0},{2,3},{3,2},{4,5},{5,4},{6,7},{7,6},{8,9},{9,8},{10,11... | collective-permute-start | bytes 786440 | tf_op jit(solution)/shard_map/ppermute | solution.py:265
  90.6 14.0 %collective-permute-start.23 = (bf16[1,2,128,512]{3,2,1,0:T(8,128)(2,1)S(1)}, bf16[1,2,128,512]{3,2,1,0:T(8,128)(2,1)S(1)}, u32[]{:S(2)}, u32[]{:S(2)}) collective-permute-start(bf16[1,2,128,512]{3,2,1,0:T(8,128)(2,1)S(1)} %get-tuple-element.145.refs_0_), channel_id=1, source_target_pairs={{0,6},{1,7},{2,0},{3,1},{4,2},{5,3},{6,4},{7,5},{8,14},{9,15},{10,... | collective-permute-start | bytes 786440 | tf_op jit(solution)/shard_map/ppermute | solution.py:261
  98.6 14.8 %collective-permute-start.29 = (bf16[2,1024,128]{2,1,0:T(8,128)(2,1)S(1)}, bf16[2,1024,128]{2,1,0:T(8,128)(2,1)S(1)}, u32[]{:S(2)}, u32[]{:S(2)}) collective-permute-start(bf16[2,1024,128]{2,1,0:T(8,128)(2,1)S(1)} %add_convert_fusion.2), channel_id=1, source_target_pairs={{0,16},{1,9},{2,18},{3,11},{4,20},{5,13},{6,22},{7,15},{8,24},{9,1... | collective-permute-start | bytes 1572872 | tf_op jit(solution)/shard_map/ppermute | solution.py:256
  100.2 17.9 %collective-permute-start.32 = (bf16[2,1024,256]{2,1,0:T(8,128)(2,1)S(1)}, bf16[2,1024,256]{2,1,0:T(8,128)(2,1)S(1)}, u32[]{:S(2)}, u32[]{:S(2)}) collective-permute-start(bf16[2,1024,256]{2,1,0:T(8,128)(2,1)S(1)} %get-tuple-element.141), channel_id=1, source_target_pairs={{0,8},{1,17},{2,10},{3,19},{4,12},{5,21},{6,14},{7,23},{8,0},{9,25... | collective-permute-start | bytes 3145736 | tf_op jit(solution)/shard_map/ppermute | solution.py:256
  104.5 1.5 %collective-permute-start.27 = (bf16[1,2,128,512]{3,2,1,0:T(8,128)(2,1)S(1)}, bf16[1,2,128,512]{3,2,1,0:T(8,128)(2,1)S(1)}, u32[]{:S(2)}, u32[]{:S(2)}) collective-permute-start(bf16[1,2,128,512]{3,2,1,0:T(8,128)(2,1)S(1)} %collective-permute-done.22.refs_2_), channel_id=1, source_target_pairs={{0,1},{1,0},{2,3},{3,2},{4,5},{5,4},{6,7},{7,6},{8,9},{9,8},{10,11... | collective-permute-start | bytes 786440 | tf_op jit(solution)/shard_map/ppermute | solution.py:265
  104.5 1.9 %collective-permute-start.28 = (bf16[1,2,128,512]{3,2,1,0:T(8,128)(2,1)S(1)}, bf16[1,2,128,512]{3,2,1,0:T(8,128)(2,1)S(1)}, u32[]{:S(2)}, u32[]{:S(2)}) collective-permute-start(bf16[1,2,128,512]{3,2,1,0:T(8,128)(2,1)S(1)} %collective-permute-done.23.refs_3_), channel_id=1, source_target_pairs={{0,1},{1,0},{2,3},{3,2},{4,5},{5,4},{6,7},{7,6},{8,9},{9,8},{10,11... | collective-permute-start | bytes 786440 | tf_op jit(solution)/shard_map/ppermute | solution.py:265
  113.4 21.6 %collective-permute-start.30 = (bf16[2,1024,256]{2,1,0:T(8,128)(2,1)S(1)}, bf16[2,1024,256]{2,1,0:T(8,128)(2,1)S(1)}, u32[]{:S(2)}, u32[]{:S(2)}) collective-permute-start(bf16[2,1024,256]{2,1,0:T(8,128)(2,1)S(1)} %get-tuple-element.153), channel_id=1, source_target_pairs={{0,8},{1,17},{2,10},{3,19},{4,12},{5,21},{6,14},{7,23},{8,0},{9,25... | collective-permute-start | bytes 3145736 | tf_op jit(solution)/shard_map/ppermute | solution.py:256
  118.3 20.7 %collective-permute-start.33 = (bf16[2,1024,128]{2,1,0:T(8,128)(2,1)S(1)}, bf16[2,1024,128]{2,1,0:T(8,128)(2,1)S(1)}, u32[]{:S(2)}, u32[]{:S(2)}) collective-permute-start(bf16[2,1024,128]{2,1,0:T(8,128)(2,1)S(1)} %add_convert_fusion), channel_id=1, source_target_pairs={{0,16},{1,9},{2,18},{3,11},{4,20},{5,13},{6,22},{7,15},{8,24},{9,1... | collective-permute-start | bytes 1572872 | tf_op jit(solution)/shard_map/ppermute | solution.py:256
  135.2 9.2 %collective-permute-start.31 = (bf16[2,1024,128]{2,1,0:T(8,128)(2,1)S(1)}, bf16[2,1024,128]{2,1,0:T(8,128)(2,1)S(1)}, u32[]{:S(2)}, u32[]{:S(2)}) collective-permute-start(bf16[2,1024,128]{2,1,0:T(8,128)(2,1)S(1)} %add_convert_fusion.1), channel_id=1, source_target_pairs={{0,16},{1,9},{2,18},{3,11},{4,20},{5,13},{6,22},{7,15},{8,24},{9,1... | collective-permute-start | bytes 1572872 | tf_op jit(solution)/shard_map/ppermute | solution.py:256

commit v10 on v9

--- a/solution.py
+++ b/solution.py
@@ -11,7 +11,7 @@
 STRETCH = 32
 WINDOW = 224
 CHUNKS = 4
-SCHEDULED_GFLOPS = (5, 4, 1.5, 0.01)
+SCHEDULED_GFLOPS = (3, 2, 1.5, 0.01)
 TILE = 128
 CORES = 2
 
@@ -289,15 +289,20 @@
         for step in range(2, self.backward + 1):
             self.near[self.chips - step] = along(self.near[self.chips - step + 1], -1)
 
-    def exchange(self):
-        for step in sorted(self.near):
-            if step and step not in self.far:
-                self.far[step] = other_core(self.near[step])
+    def exchange(self, joint=True):
+        steps = [step for step in sorted(self.near) if step and step not in self.far]
+        if not joint:
+            self.far.update({step: (0, other_core(self.near[step])) for step in steps})
+        elif steps:
+            blocks = [self.near[step] for step in steps]
+            joined = jnp.concatenate(blocks) if len(blocks) > 1 else blocks[0]
+            moved = other_core(joined)
+            for index, step in enumerate(steps):
+                self.far[step] = (index, moved)
 
     def pieces(self, chunk, whole):
         near = [(0, self.near[step]) for step in range(self.chips)]
-        far = [(0, self.far[step]) for step in range(1, self.chips)]
-        return near + [(chunk, whole)] + far
+        return near + [(chunk, whole)] + [self.far[step] for step in range(1, self.chips)]
 
 
 def body(
@@ -362,15 +367,20 @@
         return total.astype(jnp.bfloat16)
 
     def settle(*others):
-        states = [(gathering.near, gathering.far) for gathering in gathers]
+        states = [
+            (gathering.near, {step: far[1] for step, far in gathering.far.items()})
+            for gathering in gathers
+        ]
         states, *others = together(states, *others)
         for gathering, (near, far) in zip(gathers, states):
-            gathering.near, gathering.far = dict(near), dict(far)
+            gathering.near = dict(near)
+            gathering.far = {step: (gathering.far[step][0], far[step]) for step in far}
         return others
 
     pair_second = attend(1, stacked)
-    pair_second, prior = settle(pair_second, prior)
+    pair_second, prior, whole = settle(pair_second, prior, whole)
     gathers[0].exchange()
+    gathers[1].exchange()
     gathers[0].farther()
     gathers[2].ahead()
     pair_first = attend(0, jnp.concatenate([prior, stacked[:half]], axis=0))
@@ -379,9 +389,11 @@
     kept, received, last, outputs = [], [], [], ()
     for chunk in range(CHUNKS):
         pairs, whole, send, sums = settle(pairs, whole, send, sums)
-        gathers[chunk].exchange()
+        gathers[chunk].exchange(chunk < CHUNKS - 1)
+        first = chunk + 1 + (chunk == 0)
+        if chunk != 1 and first < CHUNKS:
+            gathers[first].exchange()
         if chunk + 1 < CHUNKS:
-            gathers[chunk + 1].exchange()
             gathers[chunk + 1].behind()
             gathers[chunk + 1].farther()
         if chunk + 3 < CHUNKS:

time: 146 us -> 144 us (0.986)
  waiting for transfers between devices: 63.7 us -> 59.5 us
  local copies, waits for them, and re-layouts: 6 us -> 8.14 us
  Pallas kernels: 37.1 us -> 35.2 us
    ppermute x12, waiting for transfers between devices: 34.7 us -> 25.3 us  [along(): lax.ppermute(block, 'seq', [(i, (i + CORES * chips) % size) for i in rang...]
    ppermute x8, waiting for transfers between devices: 25 us -> 32.6 us  [across(): return lax.ppermute(block, ('kv', 'seq'), route)]
    ppermute x13 -> x10, waiting for transfers between devices: 4.07 us -> 1.6 us  [other_core(): lax.ppermute(block, 'seq', [(i, i ^ 1) for i in range(lax.axis_size('seq'...]
    unnamed x16 -> x20, local copies, waits for them, and re-layouts: 3.69 us -> 5.89 us
    pallas_call x4, Pallas kernels: 21.3 us -> 19.4 us  [project(): pl.pallas_call(functools.partial(project_kernel, indices), grid=(2 * step...]
    ppermute x8, starting transfers between devices: 10.9 us -> 12.6 us  [across(): return lax.ppermute(block, ('kv', 'seq'), route)]
    ppermute x13 -> x10, starting transfers between devices: 2.69 us -> 1.08 us  [other_core(): lax.ppermute(block, 'seq', [(i, i ^ 1) for i in range(lax.axis_size('seq'...]
  transfers between devices with their start and end apart: 34 -> 31, of which waited for: 19 -> 17; matrix products, arithmetic and copies ran while one was open for 3% -> 3% of each run, Pallas kernels for 23% -> 22%
where the time goes in v10:
time: 144 us
  waiting for transfers between devices  59.5 us (41%)
  starting transfers between devices  36.8 us (26%)
  Pallas kernels  35.2 us (24%)
  local copies, waits for them, and re-layouts  8.14 us (6%)
  other arithmetic  3.35 us (2%)
    ppermute x8, waiting for transfers between devices, across(): return lax.ppermute(block, ('kv', 'seq'), route)  32.6 us
    ppermute x12, waiting for transfers between devices, along(): lax.ppermute(block, 'seq', [(i, (i + CORES * chips) % size) for i in rang...  25.3 us
    ppermute x12, starting transfers between devices, along(): lax.ppermute(block, 'seq', [(i, (i + CORES * chips) % size) for i in rang...  20 us
    pallas_call x4, Pallas kernels, project(): pl.pallas_call(functools.partial(project_kernel, indices), grid=(2 * step...  19.4 us
    ppermute x8, starting transfers between devices, across(): return lax.ppermute(block, ('kv', 'seq'), route)  12.6 us
    pallas_call x2, Pallas kernels, attention(): pl.pallas_call(functools.partial(attention_kernel, heads, head_dim, offse...  9.39 us
    unnamed x20, local copies, waits for them, and re-layouts  5.89 us
    pallas_call x4, Pallas kernels, finish(): pl.pallas_call(finish_kernel, grid=(tokens // tile,), in_specs=[pl.BlockS...  4.45 us
  transfers between devices with their start and end apart: 31, of which 17 were waited for; matrix products, arithmetic and copies ran while one was open for 3% of the time, Pallas kernels for 22%

profile of v10, /device:TPU:0, one launch (start us, length us, event | category | flops | bytes accessed | tf_op | source)
XLA Modules:
  0.0 144.0 jit_solution(3678927738918249011)
XLA Ops:
  0.7 1.0 copy-done.4
  1.8 1.0 copy-done.5
  2.8 2.0 %arrange.1 = (bf16[4,2,128,512]{3,2,1,0:T(8,128)(2,1)}, bf16[1,2,128,512]{3,2,1,0:T(8,128)(2,1)}, bf16[1,2,128,512]{3,2,1,0:T(8,128)(2,1)}, bf16[1,2,128,512]{3,...) custom-call(s32[4]{0:T(128)S(1)} %add_xor_fusion.owner_ref, bf16[128,2048]{1,0:T(8,128)(2,1)S(1)} %copy-done.4, ...), custom_call_target="tpu_custom_call" | custom-call | tf_op jit(solution)/shard_map/arrange/pallas_call | solution.py:42
  4.8 3.0 %collective-permute-start = (bf16[1,2,128,512]{3,2,1,0:T(8,128)(2,1)}, bf16[1,2,128,512]{3,2,1,0:T(8,128)(2,1)}, u32[]{:S(2)}, u32[]{:S(2)}) collective-permute-start(bf16[1,2,128,512]{3,2,1,0:T(8,128)(2,1)} %get-tuple-element.103.refs_0_), channel_id=1, source_target_pairs={{0,2},{1,3},{2,4},{3,5},{4,6},{5,7},{6,0},{7,1},{8,10},{9,11},{10,... | collective-permute-start | bytes 786440 | tf_op jit(solution)/shard_map/ppermute | solution.py:261
  7.8 2.0 %collective-permute-start.1 = (bf16[1,2,128,512]{3,2,1,0:T(8,128)(2,1)}, bf16[1,2,128,512]{3,2,1,0:T(8,128)(2,1)}, u32[]{:S(2)}, u32[]{:S(2)}) collective-permute-start(bf16[1,2,128,512]{3,2,1,0:T(8,128)(2,1)} %get-tuple-element.103.refs_0_), channel_id=1, source_target_pairs={{0,6},{1,7},{2,0},{3,1},{4,2},{5,3},{6,4},{7,5},{8,14},{9,15},{10,... | collective-permute-start | bytes 786440 | tf_op jit(solution)/shard_map/ppermute | solution.py:261
  9.8 1.1 copy.26
  12.0 1.0 copy-done.2
  13.0 3.1 %collective-permute-start.3 = (bf16[224,512]{1,0:T(8,128)(2,1)}, bf16[224,512]{1,0:T(8,128)(2,1)}, u32[]{:S(2)}, u32[]{:S(2)}) collective-permute-start(bf16[224,512]{1,0:T(8,128)(2,1)} %slice.60), channel_id=1, source_target_pairs={{0,1},{1,2},{2,3},{3,4},{4,5},{5,6},{6,7},{8,9},{9,10},{10,11},{11... | collective-permute-start | bytes 688136 | tf_op jit(solution)/shard_map/ppermute | solution.py:336
  16.8 1.6 %copy-done.1 = bf16[1024,1024]{1,0:T(8,128)(2,1)S(1)} copy-done((bf16[1024,1024]{1,0:T(8,128)(2,1)S(1)}, bf16[1024,1024]{1,0:T(8,128)(2,1)}, u32[]{:S(2)}) %copy-start.1) | copy-done | bytes 2097176
  18.4 1.2 copy-done.3
  19.6 4.8 %attention.2.second_ref = bf16[512,2048]{1,0:T(8,128)(2,1)S(1)} custom-call(s32[8]{0:T(128)S(1)} %pad_add_fusion.order_ref, bf16[1024,1024]{1,0:T(8,128)(2,1)S(1)} %copy-done, bf16[1024,1024]{1,0:T(8,128)(2,1)S(1)} %copy-done.1, bf16[1024,512]{1,0:T(8,128)(2,1)S(1)} %copy-done.3, s32[1024,128]{1,0:T(8,128)S(1)} %broadcast_in_dim.13.low_ref), custom_call_target="tpu_custom_call" | custom-call | flops 1048576 | bytes 512 | tf_op jit(solution)/shard_map/attention/pallas_call | solution.py:126
  24.4 3.3 %collective-permute-done.2.refs_1_ = bf16[1,2,128,512]{3,2,1,0:T(8,128)(2,1)} collective-permute-done((bf16[1,2,128,512]{3,2,1,0:T(8,128)(2,1)}, bf16[1,2,128,512]{3,2,1,0:T(8,128)(2,1)}, u32[]{:S(2)}, u32[]{:S(2)}) %collective-permute-start.2) | collective-permute-done | bytes 262176 | tf_op jit(solution)/shard_map/ppermute | solution.py:261
  27.7 1.1 pad_maximum_fusion.2
  28.9 2.3 %collective-permute-start.5 = (bf16[1,2,128,512]{3,2,1,0:T(8,128)(2,1)}, bf16[1,2,128,512]{3,2,1,0:T(8,128)(2,1)S(1)}, u32[]{:S(2)}, u32[]{:S(2)}) collective-permute-start(bf16[1,2,128,512]{3,2,1,0:T(8,128)(2,1)} %collective-permute-done.refs_1_), channel_id=1, source_target_pairs={{0,2},{1,3},{2,4},{3,5},{4,6},{5,7},{6,0},{7,1},{8,10},{9,11},{10,... | collective-permute-start | bytes 786440 | tf_op jit(solution)/shard_map/ppermute | solution.py:261
  31.3 1.5 %collective-permute-start.8 = (bf16[1,2,128,512]{3,2,1,0:T(8,128)(2,1)S(1)}, bf16[1,2,128,512]{3,2,1,0:T(8,128)(2,1)S(1)}, u32[]{:S(2)}, u32[]{:S(2)}) collective-permute-start(bf16[1,2,128,512]{3,2,1,0:T(8,128)(2,1)S(1)} %copy-done.7), channel_id=1, source_target_pairs={{0,2},{1,3},{2,4},{3,5},{4,6},{5,7},{6,0},{7,1},{8,10},{9,11},{10,... | collective-permute-start | bytes 786440 | tf_op jit(solution)/shard_map/ppermute | solution.py:261
  32.8 1.0 pad_maximum_fusion.1.ctx_ref
  33.8 4.6 %attention.3.first_ref = bf16[512,2048]{1,0:T(8,128)(2,1)S(1)} custom-call(s32[8]{0:T(128)S(1)} %pad_add_fusion.order_ref, bf16[1024,1024]{1,0:T(8,128)(2,1)S(1)} %copy-done, bf16[1024,1024]{1,0:T(8,128)(2,1)S(1)} %copy-done.1, bf16[736,512]{1,0:T(8,128)(2,1)S(1)} %pad_maximum_fusion.1.ctx_ref, s32[1024,128]{1,0:T(8,128)S(1)} %broadcast_in_dim.13.low_ref), custom_call_target="tpu_custom_call" | custom-call | flops 1048576 | bytes 512 | tf_op jit(solution)/shard_map/attention/pallas_call | solution.py:126
  38.5 2.0 %collective-permute-done.5.refs_2_ = bf16[1,2,128,512]{3,2,1,0:T(8,128)(2,1)S(1)} collective-permute-done((bf16[1,2,128,512]{3,2,1,0:T(8,128)(2,1)}, bf16[1,2,128,512]{3,2,1,0:T(8,128)(2,1)S(1)}, u32[]{:S(2)}, u32[]{:S(2)}) %collective-permute-start.5) | collective-permute-done | bytes 262176 | tf_op jit(solution)/shard_map/ppermute | solution.py:261
  40.5 5.4 %collective-permute-done.8.refs_1_ = bf16[1,2,128,512]{3,2,1,0:T(8,128)(2,1)S(1)} collective-permute-done((bf16[1,2,128,512]{3,2,1,0:T(8,128)(2,1)S(1)}, bf16[1,2,128,512]{3,2,1,0:T(8,128)(2,1)S(1)}, u32[]{:S(2)}, u32[]{:S(2)}) %collective-permute-start.8) | collective-permute-done | bytes 262176 | tf_op jit(solution)/shard_map/ppermute | solution.py:261
  45.9 3.8 %collective-permute-start.11 = (bf16[1,2,128,512]{3,2,1,0:T(8,128)(2,1)}, bf16[1,2,128,512]{3,2,1,0:T(8,128)(2,1)S(1)}, u32[]{:S(2)}, u32[]{:S(2)}) collective-permute-start(bf16[1,2,128,512]{3,2,1,0:T(8,128)(2,1)} %get-tuple-element.119.refs_0_), channel_id=1, source_target_pairs={{0,6},{1,7},{2,0},{3,1},{4,2},{5,3},{6,4},{7,5},{8,14},{9,15},{10,... | collective-permute-start | bytes 786440 | tf_op jit(solution)/shard_map/ppermute | solution.py:261
  49.7 5.4 %project.4 = (bf16[2,1024,256]{2,1,0:T(8,128)(2,1)S(1)}, bf16[2,1024,256]{2,1,0:T(8,128)(2,1)S(1)}) custom-call(bf16[512,2048]{1,0:T(8,128)(2,1)S(1)} %attention.3.first_ref, bf16[512,2048]{1,0:T(8,128)(2,1)S(1)} %attention.2.second_ref, bf16[1,2,128,512]{3,2,1,0:T(8,128)(2,1)} %get-tuple-element.103.refs_0_, ...), custom_call_target="tpu_custom_call" | custom-call | flops 3000000000 | bytes 512 | tf_op jit(solution)/shard_map/project/pallas_call | solution.py:200
  55.1 1.6 %collective-permute-start.17 = (bf16[2,1024,256]{2,1,0:T(8,128)(2,1)S(1)}, bf16[2,1024,256]{2,1,0:T(8,128)(2,1)S(1)}, u32[]{:S(2)}, u32[]{:S(2)}) collective-permute-start(bf16[2,1024,256]{2,1,0:T(8,128)(2,1)S(1)} %get-tuple-element.118), channel_id=1, source_target_pairs={{0,8},{1,17},{2,10},{3,19},{4,12},{5,21},{6,14},{7,23},{8,0},{9,25... | collective-permute-start | bytes 3145736 | tf_op jit(solution)/shard_map/ppermute | solution.py:256
  57.0 3.4 %collective-permute-done.11.refs_3_ = bf16[1,2,128,512]{3,2,1,0:T(8,128)(2,1)S(1)} collective-permute-done((bf16[1,2,128,512]{3,2,1,0:T(8,128)(2,1)}, bf16[1,2,128,512]{3,2,1,0:T(8,128)(2,1)S(1)}, u32[]{:S(2)}, u32[]{:S(2)}) %collective-permute-start.11) | collective-permute-done | bytes 262176 | tf_op jit(solution)/shard_map/ppermute | solution.py:261
  60.4 7.5 %collective-permute-done.13.refs_1_ = bf16[1,2,128,512]{3,2,1,0:T(8,128)(2,1)S(1)} collective-permute-done((bf16[1,2,128,512]{3,2,1,0:T(8,128)(2,1)S(1)}, bf16[1,2,128,512]{3,2,1,0:T(8,128)(2,1)S(1)}, u32[]{:S(2)}, u32[]{:S(2)}) %collective-permute-start.13) | collective-permute-done | bytes 262176 | tf_op jit(solution)/shard_map/ppermute | solution.py:261
  68.1 3.8 %collective-permute-start.16 = (bf16[1,2,128,512]{3,2,1,0:T(8,128)(2,1)S(1)}, bf16[1,2,128,512]{3,2,1,0:T(8,128)(2,1)S(1)}, u32[]{:S(2)}, u32[]{:S(2)}) collective-permute-start(bf16[1,2,128,512]{3,2,1,0:T(8,128)(2,1)S(1)} %copy-done.7), channel_id=1, source_target_pairs={{0,6},{1,7},{2,0},{3,1},{4,2},{5,3},{6,4},{7,5},{8,14},{9,15},{10,... | collective-permute-start | bytes 786440 | tf_op jit(solution)/shard_map/ppermute | solution.py:261
  71.9 5.3 %project.5 = (bf16[2,1024,256]{2,1,0:T(8,128)(2,1)S(1)}, bf16[2,1024,256]{2,1,0:T(8,128)(2,1)S(1)}) custom-call(bf16[512,2048]{1,0:T(8,128)(2,1)S(1)} %attention.3.first_ref, bf16[512,2048]{1,0:T(8,128)(2,1)S(1)} %attention.2.second_ref, bf16[1,2,128,512]{3,2,1,0:T(8,128)(2,1)} %get-tuple-element.119.refs_0_, ...), custom_call_target="tpu_custom_call" | custom-call | flops 2000000000 | bytes 512 | tf_op jit(solution)/shard_map/project/pallas_call | solution.py:200
  77.2 1.6 %collective-permute-start.22 = (bf16[2,1024,256]{2,1,0:T(8,128)(2,1)S(1)}, bf16[2,1024,256]{2,1,0:T(8,128)(2,1)S(1)}, u32[]{:S(2)}, u32[]{:S(2)}) collective-permute-start(bf16[2,1024,256]{2,1,0:T(8,128)(2,1)S(1)} %get-tuple-element.133), channel_id=1, source_target_pairs={{0,8},{1,17},{2,10},{3,19},{4,12},{5,21},{6,14},{7,23},{8,0},{9,25... | collective-permute-start | bytes 3145736 | tf_op jit(solution)/shard_map/ppermute | solution.py:256
  79.0 3.3 %collective-permute-done.16.refs_3_ = bf16[1,2,128,512]{3,2,1,0:T(8,128)(2,1)S(1)} collective-permute-done((bf16[1,2,128,512]{3,2,1,0:T(8,128)(2,1)S(1)}, bf16[1,2,128,512]{3,2,1,0:T(8,128)(2,1)S(1)}, u32[]{:S(2)}, u32[]{:S(2)}) %collective-permute-start.16) | collective-permute-done | bytes 262176 | tf_op jit(solution)/shard_map/ppermute | solution.py:261
  82.5 1.6 %collective-permute-start.23 = (bf16[2,1024,128]{2,1,0:T(8,128)(2,1)S(1)}, bf16[2,1024,128]{2,1,0:T(8,128)(2,1)S(1)}, u32[]{:S(2)}, u32[]{:S(2)}) collective-permute-start(bf16[2,1024,128]{2,1,0:T(8,128)(2,1)S(1)} %add_convert_fusion.3), channel_id=1, source_target_pairs={{0,16},{1,9},{2,18},{3,11},{4,20},{5,13},{6,22},{7,15},{8,24},{9,1... | collective-permute-start | bytes 1572872 | tf_op jit(solution)/shard_map/ppermute | solution.py:256
  84.4 3.5 %collective-permute-start.20 = (bf16[1,2,128,512]{3,2,1,0:T(8,128)(2,1)S(1)}, bf16[1,2,128,512]{3,2,1,0:T(8,128)(2,1)S(1)}, u32[]{:S(2)}, u32[]{:S(2)}) collective-permute-start(bf16[1,2,128,512]{3,2,1,0:T(8,128)(2,1)S(1)} %get-tuple-element.151.refs_0_), channel_id=1, source_target_pairs={{0,6},{1,7},{2,0},{3,1},{4,2},{5,3},{6,4},{7,5},{8,14},{9,15},{10,... | collective-permute-start | bytes 786440 | tf_op jit(solution)/shard_map/ppermute | solution.py:261
  87.9 4.4 %project.6 = (bf16[2,1024,256]{2,1,0:T(8,128)(2,1)S(1)}, bf16[2,1024,256]{2,1,0:T(8,128)(2,1)S(1)}) custom-call(bf16[512,2048]{1,0:T(8,128)(2,1)S(1)} %attention.3.first_ref, bf16[512,2048]{1,0:T(8,128)(2,1)S(1)} %attention.2.second_ref, bf16[1,2,128,512]{3,2,1,0:T(8,128)(2,1)S(1)} %copy-done.7, bf16[1,2,128,512]{3,2,1,0:T(8,128)(2,1)S(1)} %collective-permute-done.8.refs_1_, ...), custom_call_target="tpu_custom_call" | custom-call | flops 1500000000 | bytes 512 | tf_op jit(solution)/shard_map/project/pallas_call | solution.py:200
  92.3 4.3 %collective-permute-done.23.last_ref = bf16[2,1024,128]{2,1,0:T(8,128)(2,1)S(1)} collective-permute-done((bf16[2,1024,128]{2,1,0:T(8,128)(2,1)S(1)}, bf16[2,1024,128]{2,1,0:T(8,128)(2,1)S(1)}, u32[]{:S(2)}, u32[]{:S(2)}) %collective-permute-start.23) | collective-permute-done | bytes 524320 | tf_op jit(solution)/shard_map/ppermute | solution.py:256
  96.6 1.1 collective-permute-done.22.received_ref
  97.8 1.6 %collective-permute-start.26 = (bf16[2,1024,128]{2,1,0:T(8,128)(2,1)S(1)}, bf16[2,1024,128]{2,1,0:T(8,128)(2,1)S(1)}, u32[]{:S(2)}, u32[]{:S(2)}) collective-permute-start(bf16[2,1024,128]{2,1,0:T(8,128)(2,1)S(1)} %add_convert_fusion.2), channel_id=1, source_target_pairs={{0,16},{1,9},{2,18},{3,11},{4,20},{5,13},{6,22},{7,15},{8,24},{9,1... | collective-permute-start | bytes 1572872 | tf_op jit(solution)/shard_map/ppermute | solution.py:256
  99.4 1.5 %collective-permute-start.29 = (bf16[2,1024,256]{2,1,0:T(8,128)(2,1)S(1)}, bf16[2,1024,256]{2,1,0:T(8,128)(2,1)S(1)}, u32[]{:S(2)}, u32[]{:S(2)}) collective-permute-start(bf16[2,1024,256]{2,1,0:T(8,128)(2,1)S(1)} %get-tuple-element.147), channel_id=1, source_target_pairs={{0,8},{1,17},{2,10},{3,19},{4,12},{5,21},{6,14},{7,23},{8,0},{9,25... | collective-permute-start | bytes 3145736 | tf_op jit(solution)/shard_map/ppermute | solution.py:256
  101.5 1.0 collective-permute-done.24.refs_6_
  102.9 4.4 %project.7 = (bf16[2,1024,256]{2,1,0:T(8,128)(2,1)S(1)}, bf16[2,1024,256]{2,1,0:T(8,128)(2,1)S(1)}) custom-call(bf16[512,2048]{1,0:T(8,128)(2,1)S(1)} %attention.3.first_ref, bf16[512,2048]{1,0:T(8,128)(2,1)S(1)} %attention.2.second_ref, bf16[1,2,128,512]{3,2,1,0:T(8,128)(2,1)S(1)} %get-tuple-element.151.refs_0_, ...), custom_call_target="tpu_custom_call" | custom-call | flops 10000000 | bytes 512 | tf_op jit(solution)/shard_map/project/pallas_call | solution.py:200
  107.3 5.3 %collective-permute-done.26.last_ref = bf16[2,1024,128]{2,1,0:T(8,128)(2,1)S(1)} collective-permute-done((bf16[2,1024,128]{2,1,0:T(8,128)(2,1)S(1)}, bf16[2,1024,128]{2,1,0:T(8,128)(2,1)S(1)}, u32[]{:S(2)}, u32[]{:S(2)}) %collective-permute-start.26) | collective-permute-done | bytes 524320 | tf_op jit(solution)/shard_map/ppermute | solution.py:256
  112.6 1.6 %collective-permute-start.27 = (bf16[2,1024,256]{2,1,0:T(8,128)(2,1)S(1)}, bf16[2,1024,256]{2,1,0:T(8,128)(2,1)S(1)}, u32[]{:S(2)}, u32[]{:S(2)}) collective-permute-start(bf16[2,1024,256]{2,1,0:T(8,128)(2,1)S(1)} %get-tuple-element.159), channel_id=1, source_target_pairs={{0,8},{1,17},{2,10},{3,19},{4,12},{5,21},{6,14},{7,23},{8,0},{9,25... | collective-permute-start | bytes 3145736 | tf_op jit(solution)/shard_map/ppermute | solution.py:256
  114.2 2.4 %collective-permute-done.29.received_ref = bf16[2,1024,256]{2,1,0:T(8,128)(2,1)S(1)} collective-permute-done((bf16[2,1024,256]{2,1,0:T(8,128)(2,1)S(1)}, bf16[2,1024,256]{2,1,0:T(8,128)(2,1)S(1)}, u32[]{:S(2)}, u32[]{:S(2)}) %collective-permute-start.29) | collective-permute-done | bytes 1048608 | tf_op jit(solution)/shard_map/ppermute | solution.py:256
  116.8 1.6 %collective-permute-start.30 = (bf16[2,1024,128]{2,1,0:T(8,128)(2,1)S(1)}, bf16[2,1024,128]{2,1,0:T(8,128)(2,1)S(1)}, u32[]{:S(2)}, u32[]{:S(2)}) collective-permute-start(bf16[2,1024,128]{2,1,0:T(8,128)(2,1)S(1)} %add_convert_fusion), channel_id=1, source_target_pairs={{0,16},{1,9},{2,18},{3,11},{4,20},{5,13},{6,22},{7,15},{8,24},{9,1... | collective-permute-start | bytes 1572872 | tf_op jit(solution)/shard_map/ppermute | solution.py:256
  118.4 15.1 %collective-permute-done.27.received_ref = bf16[2,1024,256]{2,1,0:T(8,128)(2,1)S(1)} collective-permute-done((bf16[2,1024,256]{2,1,0:T(8,128)(2,1)S(1)}, bf16[2,1024,256]{2,1,0:T(8,128)(2,1)S(1)}, u32[]{:S(2)}, u32[]{:S(2)}) %collective-permute-start.27) | collective-permute-done | bytes 1048608 | tf_op jit(solution)/shard_map/ppermute | solution.py:256
  133.6 1.6 %collective-permute-start.28 = (bf16[2,1024,128]{2,1,0:T(8,128)(2,1)S(1)}, bf16[2,1024,128]{2,1,0:T(8,128)(2,1)S(1)}, u32[]{:S(2)}, u32[]{:S(2)}) collective-permute-start(bf16[2,1024,128]{2,1,0:T(8,128)(2,1)S(1)} %add_convert_fusion.1), channel_id=1, source_target_pairs={{0,16},{1,9},{2,18},{3,11},{4,20},{5,13},{6,22},{7,15},{8,24},{9,1... | collective-permute-start | bytes 1572872 | tf_op jit(solution)/shard_map/ppermute | solution.py:256
  135.2 1.1 finish.4
  136.3 1.1 finish.5
  137.4 1.1 finish.6
  138.6 4.3 %collective-permute-done.28.last_ref = bf16[2,1024,128]{2,1,0:T(8,128)(2,1)S(1)} collective-permute-done((bf16[2,1024,128]{2,1,0:T(8,128)(2,1)S(1)}, bf16[2,1024,128]{2,1,0:T(8,128)(2,1)S(1)}, u32[]{:S(2)}, u32[]{:S(2)}) %collective-permute-start.28) | collective-permute-done | bytes 524320 | tf_op jit(solution)/shard_map/ppermute | solution.py:256
  142.9 1.1 finish.7
  (71 shorter events, 4.7 us)
Async XLA Ops:
  0.7 1.0 copy-start.4
  1.8 1.0 copy-start.5
  2.8 8.1 %copy-start.8 = (bf16[1024,2,128]{2,1,0:T(2,128)(2,1)S(1)}, bf16[1024,2,128]{2,1,0:T(2,128)(2,1)}, u32[]{:S(2)}) copy-start(bf16[1024,2,128]{2,1,0:T(2,128)(2,1)} %param.9) | copy-start | bytes 1572868
  4.8 6.4 %copy-start.6 = (bf16[1,2,128,512]{3,2,1,0:T(8,128)(2,1)}, bf16[1,2,128,512]{3,2,1,0:T(8,128)(2,1)S(1)}, u32[]{:S(2)}) copy-start(bf16[1,2,128,512]{3,2,1,0:T(8,128)(2,1)S(1)} %get-tuple-element.135.refs_0_) | copy-start | bytes 786436
  4.8 19.7 %collective-permute-start = (bf16[1,2,128,512]{3,2,1,0:T(8,128)(2,1)}, bf16[1,2,128,512]{3,2,1,0:T(8,128)(2,1)}, u32[]{:S(2)}, u32[]{:S(2)}) collective-permute-start(bf16[1,2,128,512]{3,2,1,0:T(8,128)(2,1)} %get-tuple-element.103.refs_0_), channel_id=1, source_target_pairs={{0,2},{1,3},{2,4},{3,5},{4,6},{5,7},{6,0},{7,1},{8,10},{9,11},{10,... | collective-permute-start | bytes 786440 | tf_op jit(solution)/shard_map/ppermute | solution.py:261
  7.8 16.6 %collective-permute-start.1 = (bf16[1,2,128,512]{3,2,1,0:T(8,128)(2,1)}, bf16[1,2,128,512]{3,2,1,0:T(8,128)(2,1)}, u32[]{:S(2)}, u32[]{:S(2)}) collective-permute-start(bf16[1,2,128,512]{3,2,1,0:T(8,128)(2,1)} %get-tuple-element.103.refs_0_), channel_id=1, source_target_pairs={{0,6},{1,7},{2,0},{3,1},{4,2},{5,3},{6,4},{7,5},{8,14},{9,15},{10,... | collective-permute-start | bytes 786440 | tf_op jit(solution)/shard_map/ppermute | solution.py:261
  9.8 17.9 %collective-permute-start.2 = (bf16[1,2,128,512]{3,2,1,0:T(8,128)(2,1)}, bf16[1,2,128,512]{3,2,1,0:T(8,128)(2,1)}, u32[]{:S(2)}, u32[]{:S(2)}) collective-permute-start(bf16[1,2,128,512]{3,2,1,0:T(8,128)(2,1)} %get-tuple-element.119.refs_0_), channel_id=1, source_target_pairs={{0,2},{1,3},{2,4},{3,5},{4,6},{5,7},{6,0},{7,1},{8,10},{9,11},{10,... | collective-permute-start | bytes 786440 | tf_op jit(solution)/shard_map/ppermute | solution.py:261
  9.8 17.9 %collective-permute-start.4 = (bf16[4,2,128,512]{3,2,1,0:T(8,128)(2,1)}, bf16[4,2,128,512]{3,2,1,0:T(8,128)(2,1)S(1)}, u32[]{:S(2)}, u32[]{:S(2)}) collective-permute-start(bf16[4,2,128,512]{3,2,1,0:T(8,128)(2,1)} %get-tuple-element.92), channel_id=1, source_target_pairs={{0,1},{1,0},{2,3},{3,2},{4,5},{5,4},{6,7},{7,6},{8,9},{9,8},{10,11... | collective-permute-start | bytes 3145736 | tf_op jit(solution)/shard_map/ppermute | solution.py:265
  11.0 5.0 %copy-start.9 = (s32[64]{0:T(128)S(1)}, s32[64]{0:T(128)}, u32[]{:S(2)}) copy-start(s32[64]{0:T(128)} %param.11) | copy-start | bytes 772
  11.1 5.7 %copy-start = (bf16[1024,1024]{1,0:T(8,128)(2,1)S(1)}, bf16[1024,1024]{1,0:T(8,128)(2,1)}, u32[]{:S(2)}) copy-start(bf16[1024,1024]{1,0:T(8,128)(2,1)} %q_ref.3) | copy-start | bytes 6291460
  12.0 1.0 copy-start.2
  13.0 11.5 %collective-permute-start.3 = (bf16[224,512]{1,0:T(8,128)(2,1)}, bf16[224,512]{1,0:T(8,128)(2,1)}, u32[]{:S(2)}, u32[]{:S(2)}) collective-permute-start(bf16[224,512]{1,0:T(8,128)(2,1)} %slice.60), channel_id=1, source_target_pairs={{0,1},{1,2},{2,3},{3,4},{4,5},{5,6},{6,7},{8,9},{9,10},{10,11},{11... | collective-permute-start | bytes 688136 | tf_op jit(solution)/shard_map/ppermute | solution.py:336
  16.8 1.6 %copy-start.1 = (bf16[1024,1024]{1,0:T(8,128)(2,1)S(1)}, bf16[1024,1024]{1,0:T(8,128)(2,1)}, u32[]{:S(2)}) copy-start(bf16[1024,1024]{1,0:T(8,128)(2,1)} %qt_ref.3) | copy-start | bytes 6291460
  18.4 1.2 copy-start.3
  19.6 11.7 %copy-start.7 = (bf16[1,2,128,512]{3,2,1,0:T(8,128)(2,1)S(1)}, bf16[1,2,128,512]{3,2,1,0:T(8,128)(2,1)}, u32[]{:S(2)}) copy-start(bf16[1,2,128,512]{3,2,1,0:T(8,128)(2,1)} %copy-done.6) | copy-start | bytes 786436
  24.4 8.4 %slice-start = ((bf16[1024,512]{1,0:T(8,128)(2,1)}), bf16[512,512]{1,0:T(8,128)(2,1)S(1)}, s32[]{:S(2)}) async-start(bf16[1024,512]{1,0:T(8,128)(2,1)} %copy-done.2), calls=%async_computation | async-start | bytes 1048576 | tf_op jit(solution)/shard_map/slice | solution.py:386
  28.8 17.1 %collective-permute-start.6 = (bf16[2,2,128,512]{3,2,1,0:T(8,128)(2,1)S(1)}, bf16[2,2,128,512]{3,2,1,0:T(8,128)(2,1)S(1)}, u32[]{:S(2)}, u32[]{:S(2)}) collective-permute-start(bf16[2,2,128,512]{3,2,1,0:T(8,128)(2,1)S(1)} %pad_maximum_fusion.2), channel_id=1, source_target_pairs={{0,1},{1,0},{2,3},{3,2},{4,5},{5,4},{6,7},{7,6},{8,9},{9,8},{10,11... | collective-permute-start | bytes 1572872 | tf_op jit(solution)/shard_map/ppermute | solution.py:265
  28.9 11.6 %collective-permute-start.5 = (bf16[1,2,128,512]{3,2,1,0:T(8,128)(2,1)}, bf16[1,2,128,512]{3,2,1,0:T(8,128)(2,1)S(1)}, u32[]{:S(2)}, u32[]{:S(2)}) collective-permute-start(bf16[1,2,128,512]{3,2,1,0:T(8,128)(2,1)} %collective-permute-done.refs_1_), channel_id=1, source_target_pairs={{0,2},{1,3},{2,4},{3,5},{4,6},{5,7},{6,0},{7,1},{8,10},{9,11},{10,... | collective-permute-start | bytes 786440 | tf_op jit(solution)/shard_map/ppermute | solution.py:261
  31.1 9.3 %collective-permute-start.7 = (bf16[1,2,128,512]{3,2,1,0:T(8,128)(2,1)}, bf16[1,2,128,512]{3,2,1,0:T(8,128)(2,1)S(1)}, u32[]{:S(2)}, u32[]{:S(2)}) collective-permute-start(bf16[1,2,128,512]{3,2,1,0:T(8,128)(2,1)} %collective-permute-done.2.refs_1_), channel_id=1, source_target_pairs={{0,1},{1,0},{2,3},{3,2},{4,5},{5,4},{6,7},{7,6},{8,9},{9,8},{10,11... | collective-permute-start | bytes 786440 | tf_op jit(solution)/shard_map/ppermute | solution.py:265
  31.3 14.6 %collective-permute-start.8 = (bf16[1,2,128,512]{3,2,1,0:T(8,128)(2,1)S(1)}, bf16[1,2,128,512]{3,2,1,0:T(8,128)(2,1)S(1)}, u32[]{:S(2)}, u32[]{:S(2)}) collective-permute-start(bf16[1,2,128,512]{3,2,1,0:T(8,128)(2,1)S(1)} %copy-done.7), channel_id=1, source_target_pairs={{0,2},{1,3},{2,4},{3,5},{4,6},{5,7},{6,0},{7,1},{8,10},{9,11},{10,... | collective-permute-start | bytes 786440 | tf_op jit(solution)/shard_map/ppermute | solution.py:261
  45.9 3.8 %collective-permute-start.9 = (bf16[1,2,128,512]{3,2,1,0:T(8,128)(2,1)S(1)}, bf16[1,2,128,512]{3,2,1,0:T(8,128)(2,1)S(1)}, u32[]{:S(2)}, u32[]{:S(2)}) collective-permute-start(bf16[1,2,128,512]{3,2,1,0:T(8,128)(2,1)S(1)} %collective-permute-done.5.refs_2_), channel_id=1, source_target_pairs={{0,1},{1,0},{2,3},{3,2},{4,5},{5,4},{6,7},{7,6},{8,9},{9,8},{10,11... | collective-permute-start | bytes 786440 | tf_op jit(solution)/shard_map/ppermute | solution.py:265
  45.9 11.2 %collective-permute-start.10 = (bf16[1,2,128,512]{3,2,1,0:T(8,128)(2,1)}, bf16[1,2,128,512]{3,2,1,0:T(8,128)(2,1)S(1)}, u32[]{:S(2)}, u32[]{:S(2)}) collective-permute-start(bf16[1,2,128,512]{3,2,1,0:T(8,128)(2,1)} %collective-permute-done.2.refs_1_), channel_id=1, source_target_pairs={{0,2},{1,3},{2,4},{3,5},{4,6},{5,7},{6,0},{7,1},{8,10},{9,11},{10,... | collective-permute-start | bytes 786440 | tf_op jit(solution)/shard_map/ppermute | solution.py:261
  45.9 14.5 %collective-permute-start.11 = (bf16[1,2,128,512]{3,2,1,0:T(8,128)(2,1)}, bf16[1,2,128,512]{3,2,1,0:T(8,128)(2,1)S(1)}, u32[]{:S(2)}, u32[]{:S(2)}) collective-permute-start(bf16[1,2,128,512]{3,2,1,0:T(8,128)(2,1)} %get-tuple-element.119.refs_0_), channel_id=1, source_target_pairs={{0,6},{1,7},{2,0},{3,1},{4,2},{5,3},{6,4},{7,5},{8,14},{9,15},{10,... | collective-permute-start | bytes 786440 | tf_op jit(solution)/shard_map/ppermute | solution.py:261
  49.7 10.7 %collective-permute-start.12 = (bf16[1,2,128,512]{3,2,1,0:T(8,128)(2,1)S(1)}, bf16[1,2,128,512]{3,2,1,0:T(8,128)(2,1)S(1)}, u32[]{:S(2)}, u32[]{:S(2)}) collective-permute-start(bf16[1,2,128,512]{3,2,1,0:T(8,128)(2,1)S(1)} %collective-permute-done.8.refs_1_), channel_id=1, source_target_pairs={{0,1},{1,0},{2,3},{3,2},{4,5},{5,4},{6,7},{7,6},{8,9},{9,8},{10,11... | collective-permute-start | bytes 786440 | tf_op jit(solution)/shard_map/ppermute | solution.py:265
  49.7 18.2 %collective-permute-start.13 = (bf16[1,2,128,512]{3,2,1,0:T(8,128)(2,1)S(1)}, bf16[1,2,128,512]{3,2,1,0:T(8,128)(2,1)S(1)}, u32[]{:S(2)}, u32[]{:S(2)}) collective-permute-start(bf16[1,2,128,512]{3,2,1,0:T(8,128)(2,1)S(1)} %get-tuple-element.151.refs_0_), channel_id=1, source_target_pairs={{0,2},{1,3},{2,4},{3,5},{4,6},{5,7},{6,0},{7,1},{8,10},{9,11},{10,... | collective-permute-start | bytes 786440 | tf_op jit(solution)/shard_map/ppermute | solution.py:261
  55.1 23.6 %collective-permute-start.17 = (bf16[2,1024,256]{2,1,0:T(8,128)(2,1)S(1)}, bf16[2,1024,256]{2,1,0:T(8,128)(2,1)S(1)}, u32[]{:S(2)}, u32[]{:S(2)}) collective-permute-start(bf16[2,1024,256]{2,1,0:T(8,128)(2,1)S(1)} %get-tuple-element.118), channel_id=1, source_target_pairs={{0,8},{1,17},{2,10},{3,19},{4,12},{5,21},{6,14},{7,23},{8,0},{9,25... | collective-permute-start | bytes 3145736 | tf_op jit(solution)/shard_map/ppermute | solution.py:256
  67.9 4.0 %collective-permute-start.14 = (bf16[2,2,128,512]{3,2,1,0:T(8,128)(2,1)S(1)}, bf16[2,2,128,512]{3,2,1,0:T(8,128)(2,1)S(1)}, u32[]{:S(2)}, u32[]{:S(2)}) collective-permute-start(bf16[2,2,128,512]{3,2,1,0:T(8,128)(2,1)S(1)} %pad_maximum_fusion.3), channel_id=1, source_target_pairs={{0,1},{1,0},{2,3},{3,2},{4,5},{5,4},{6,7},{7,6},{8,9},{9,8},{10,11... | collective-permute-start | bytes 1572872 | tf_op jit(solution)/shard_map/ppermute | solution.py:265
  68.0 11.0 %collective-permute-start.15 = (bf16[1,2,128,512]{3,2,1,0:T(8,128)(2,1)S(1)}, bf16[1,2,128,512]{3,2,1,0:T(8,128)(2,1)S(1)}, u32[]{:S(2)}, u32[]{:S(2)}) collective-permute-start(bf16[1,2,128,512]{3,2,1,0:T(8,128)(2,1)S(1)} %collective-permute-done.8.refs_1_), channel_id=1, source_target_pairs={{0,2},{1,3},{2,4},{3,5},{4,6},{5,7},{6,0},{7,1},{8,10},{9,11},{10,... | collective-permute-start | bytes 786440 | tf_op jit(solution)/shard_map/ppermute | solution.py:261
  68.1 14.3 %collective-permute-start.16 = (bf16[1,2,128,512]{3,2,1,0:T(8,128)(2,1)S(1)}, bf16[1,2,128,512]{3,2,1,0:T(8,128)(2,1)S(1)}, u32[]{:S(2)}, u32[]{:S(2)}) collective-permute-start(bf16[1,2,128,512]{3,2,1,0:T(8,128)(2,1)S(1)} %copy-done.7), channel_id=1, source_target_pairs={{0,6},{1,7},{2,0},{3,1},{4,2},{5,3},{6,4},{7,5},{8,14},{9,15},{10,... | collective-permute-start | bytes 786440 | tf_op jit(solution)/shard_map/ppermute | solution.py:261
  77.2 20.5 %collective-permute-start.22 = (bf16[2,1024,256]{2,1,0:T(8,128)(2,1)S(1)}, bf16[2,1024,256]{2,1,0:T(8,128)(2,1)S(1)}, u32[]{:S(2)}, u32[]{:S(2)}) collective-permute-start(bf16[2,1024,256]{2,1,0:T(8,128)(2,1)S(1)} %get-tuple-element.133), channel_id=1, source_target_pairs={{0,8},{1,17},{2,10},{3,19},{4,12},{5,21},{6,14},{7,23},{8,0},{9,25... | collective-permute-start | bytes 3145736 | tf_op jit(solution)/shard_map/ppermute | solution.py:256
  82.4 2.0 %collective-permute-start.18 = (bf16[2,2,128,512]{3,2,1,0:T(8,128)(2,1)S(1)}, bf16[2,2,128,512]{3,2,1,0:T(8,128)(2,1)S(1)}, u32[]{:S(2)}, u32[]{:S(2)}) collective-permute-start(bf16[2,2,128,512]{3,2,1,0:T(8,128)(2,1)S(1)} %pad_maximum_fusion.4), channel_id=1, source_target_pairs={{0,1},{1,0},{2,3},{3,2},{4,5},{5,4},{6,7},{7,6},{8,9},{9,8},{10,11... | collective-permute-start | bytes 1572872 | tf_op jit(solution)/shard_map/ppermute | solution.py:265
  82.5 14.1 %collective-permute-start.23 = (bf16[2,1024,128]{2,1,0:T(8,128)(2,1)S(1)}, bf16[2,1024,128]{2,1,0:T(8,128)(2,1)S(1)}, u32[]{:S(2)}, u32[]{:S(2)}) collective-permute-start(bf16[2,1024,128]{2,1,0:T(8,128)(2,1)S(1)} %add_convert_fusion.3), channel_id=1, source_target_pairs={{0,16},{1,9},{2,18},{3,11},{4,20},{5,13},{6,22},{7,15},{8,24},{9,1... | collective-permute-start | bytes 1572872 | tf_op jit(solution)/shard_map/ppermute | solution.py:256
  84.1 16.8 %collective-permute-start.19 = (bf16[1,2,128,512]{3,2,1,0:T(8,128)(2,1)S(1)}, bf16[1,2,128,512]{3,2,1,0:T(8,128)(2,1)S(1)}, u32[]{:S(2)}, u32[]{:S(2)}) collective-permute-start(bf16[1,2,128,512]{3,2,1,0:T(8,128)(2,1)S(1)} %collective-permute-done.13.refs_1_), channel_id=1, source_target_pairs={{0,2},{1,3},{2,4},{3,5},{4,6},{5,7},{6,0},{7,1},{8,10},{9,11},{10,... | collective-permute-start | bytes 786440 | tf_op jit(solution)/shard_map/ppermute | solution.py:261
  84.1 16.8 %collective-permute-start.21 = (bf16[1,2,128,512]{3,2,1,0:T(8,128)(2,1)S(1)}, bf16[1,2,128,512]{3,2,1,0:T(8,128)(2,1)S(1)}, u32[]{:S(2)}, u32[]{:S(2)}) collective-permute-start(bf16[1,2,128,512]{3,2,1,0:T(8,128)(2,1)S(1)} %collective-permute-done.13.refs_1_), channel_id=1, source_target_pairs={{0,1},{1,0},{2,3},{3,2},{4,5},{5,4},{6,7},{7,6},{8,9},{9,8},{10,11... | collective-permute-start | bytes 786440 | tf_op jit(solution)/shard_map/ppermute | solution.py:265
  84.4 16.5 %collective-permute-start.20 = (bf16[1,2,128,512]{3,2,1,0:T(8,128)(2,1)S(1)}, bf16[1,2,128,512]{3,2,1,0:T(8,128)(2,1)S(1)}, u32[]{:S(2)}, u32[]{:S(2)}) collective-permute-start(bf16[1,2,128,512]{3,2,1,0:T(8,128)(2,1)S(1)} %get-tuple-element.151.refs_0_), channel_id=1, source_target_pairs={{0,6},{1,7},{2,0},{3,1},{4,2},{5,3},{6,4},{7,5},{8,14},{9,15},{10,... | collective-permute-start | bytes 786440 | tf_op jit(solution)/shard_map/ppermute | solution.py:261
  97.8 14.8 %collective-permute-start.26 = (bf16[2,1024,128]{2,1,0:T(8,128)(2,1)S(1)}, bf16[2,1024,128]{2,1,0:T(8,128)(2,1)S(1)}, u32[]{:S(2)}, u32[]{:S(2)}) collective-permute-start(bf16[2,1024,128]{2,1,0:T(8,128)(2,1)S(1)} %add_convert_fusion.2), channel_id=1, source_target_pairs={{0,16},{1,9},{2,18},{3,11},{4,20},{5,13},{6,22},{7,15},{8,24},{9,1... | collective-permute-start | bytes 1572872 | tf_op jit(solution)/shard_map/ppermute | solution.py:256
  99.4 17.2 %collective-permute-start.29 = (bf16[2,1024,256]{2,1,0:T(8,128)(2,1)S(1)}, bf16[2,1024,256]{2,1,0:T(8,128)(2,1)S(1)}, u32[]{:S(2)}, u32[]{:S(2)}) collective-permute-start(bf16[2,1024,256]{2,1,0:T(8,128)(2,1)S(1)} %get-tuple-element.147), channel_id=1, source_target_pairs={{0,8},{1,17},{2,10},{3,19},{4,12},{5,21},{6,14},{7,23},{8,0},{9,25... | collective-permute-start | bytes 3145736 | tf_op jit(solution)/shard_map/ppermute | solution.py:256
  100.9 1.6 %collective-permute-start.24 = (bf16[1,2,128,512]{3,2,1,0:T(8,128)(2,1)S(1)}, bf16[1,2,128,512]{3,2,1,0:T(8,128)(2,1)S(1)}, u32[]{:S(2)}, u32[]{:S(2)}) collective-permute-start(bf16[1,2,128,512]{3,2,1,0:T(8,128)(2,1)S(1)} %collective-permute-done.19.refs_2_), channel_id=1, source_target_pairs={{0,1},{1,0},{2,3},{3,2},{4,5},{5,4},{6,7},{7,6},{8,9},{9,8},{10,11... | collective-permute-start | bytes 786440 | tf_op jit(solution)/shard_map/ppermute | solution.py:265
  101.0 1.9 %collective-permute-start.25 = (bf16[1,2,128,512]{3,2,1,0:T(8,128)(2,1)S(1)}, bf16[1,2,128,512]{3,2,1,0:T(8,128)(2,1)S(1)}, u32[]{:S(2)}, u32[]{:S(2)}) collective-permute-start(bf16[1,2,128,512]{3,2,1,0:T(8,128)(2,1)S(1)} %collective-permute-done.20.refs_3_), channel_id=1, source_target_pairs={{0,1},{1,0},{2,3},{3,2},{4,5},{5,4},{6,7},{7,6},{8,9},{9,8},{10,11... | collective-permute-start | bytes 786440 | tf_op jit(solution)/shard_map/ppermute | solution.py:265
  112.6 20.9 %collective-permute-start.27 = (bf16[2,1024,256]{2,1,0:T(8,128)(2,1)S(1)}, bf16[2,1024,256]{2,1,0:T(8,128)(2,1)S(1)}, u32[]{:S(2)}, u32[]{:S(2)}) collective-permute-start(bf16[2,1024,256]{2,1,0:T(8,128)(2,1)S(1)} %get-tuple-element.159), channel_id=1, source_target_pairs={{0,8},{1,17},{2,10},{3,19},{4,12},{5,21},{6,14},{7,23},{8,0},{9,25... | collective-permute-start | bytes 3145736 | tf_op jit(solution)/shard_map/ppermute | solution.py:256
  116.8 20.7 %collective-permute-start.30 = (bf16[2,1024,128]{2,1,0:T(8,128)(2,1)S(1)}, bf16[2,1024,128]{2,1,0:T(8,128)(2,1)S(1)}, u32[]{:S(2)}, u32[]{:S(2)}) collective-permute-start(bf16[2,1024,128]{2,1,0:T(8,128)(2,1)S(1)} %add_convert_fusion), channel_id=1, source_target_pairs={{0,16},{1,9},{2,18},{3,11},{4,20},{5,13},{6,22},{7,15},{8,24},{9,1... | collective-permute-start | bytes 1572872 | tf_op jit(solution)/shard_map/ppermute | solution.py:256
  133.6 9.2 %collective-permute-start.28 = (bf16[2,1024,128]{2,1,0:T(8,128)(2,1)S(1)}, bf16[2,1024,128]{2,1,0:T(8,128)(2,1)S(1)}, u32[]{:S(2)}, u32[]{:S(2)}) collective-permute-start(bf16[2,1024,128]{2,1,0:T(8,128)(2,1)S(1)} %add_convert_fusion.1), channel_id=1, source_target_pairs={{0,16},{1,9},{2,18},{3,11},{4,20},{5,13},{6,22},{7,15},{8,24},{9,1... | collective-permute-start | bytes 1572872 | tf_op jit(solution)/shard_map/ppermute | solution.py:256

commit v11 on v10

--- a/solution.py
+++ b/solution.py
@@ -11,7 +11,7 @@
 STRETCH = 32
 WINDOW = 224
 CHUNKS = 4
-SCHEDULED_GFLOPS = (3, 2, 1.5, 0.01)
+SCHEDULED_GFLOPS = (3, 3, 1.5, 0.01)
 TILE = 128
 CORES = 2
 
@@ -281,13 +281,13 @@
 
     def behind(self):
         if self.backward:
-            self.near[self.chips - 1] = along(self.near[0], -1)
+            self.near[-1] = along(self.near[0], -1)
 
     def farther(self):
         for step in range(2, self.forward + 1):
             self.near[step] = along(self.near[step - 1], 1)
         for step in range(2, self.backward + 1):
-            self.near[self.chips - step] = along(self.near[self.chips - step + 1], -1)
+            self.near[-step] = along(self.near[1 - step], -1)
 
     def exchange(self, joint=True):
         steps = [step for step in sorted(self.near) if step and step not in self.far]
@@ -301,8 +301,9 @@
                 self.far[step] = (index, moved)
 
     def pieces(self, chunk, whole):
-        near = [(0, self.near[step]) for step in range(self.chips)]
-        return near + [(chunk, whole)] + [self.far[step] for step in range(1, self.chips)]
+        steps = [*range(1, self.forward + 1), *range(-self.backward, 0)]
+        near = [(0, self.near[step]) for step in [0, *steps]]
+        return near + [(chunk, whole)] + [self.far[step] for step in steps]
 
 
 def body(
@@ -379,7 +380,7 @@
 
     pair_second = attend(1, stacked)
     pair_second, prior, whole = settle(pair_second, prior, whole)
-    gathers[0].exchange()
+    gathers[0].exchange(False)
     gathers[1].exchange()
     gathers[0].farther()
     gathers[2].ahead()
@@ -396,8 +397,8 @@
         if chunk + 1 < CHUNKS:
             gathers[chunk + 1].behind()
             gathers[chunk + 1].farther()
-        if chunk + 3 < CHUNKS:
-            gathers[chunk + 3].ahead()
+        if 0 < chunk < CHUNKS - 2:
+            gathers[chunk + 2].ahead()
         send, keep = project(
             SCHEDULED_GFLOPS[chunk], pairs, gathers[chunk].pieces(chunk, whole)
         )

time: 144 us -> 139 us (0.965)
  starting transfers between devices: 36.8 us -> 32 us
  local copies, waits for them, and re-layouts: 8.14 us -> 6 us
  Pallas kernels: 35.2 us -> 37.1 us
    ppermute x12, waiting for transfers between devices: 25.3 us -> 31.9 us  [along(): lax.ppermute(block, 'seq', [(i, (i + CORES * chips) % size) for i in rang...]
    ppermute x8, waiting for transfers between devices: 32.6 us -> 26.3 us  [across(): return lax.ppermute(block, ('kv', 'seq'), route)]
    ppermute x12, starting transfers between devices: 20 us -> 17.2 us  [along(): lax.ppermute(block, 'seq', [(i, (i + CORES * chips) % size) for i in rang...]
    unnamed x20 -> x16, local copies, waits for them, and re-layouts: 5.89 us -> 3.69 us
    ppermute x8, starting transfers between devices: 12.6 us -> 10.4 us  [across(): return lax.ppermute(block, ('kv', 'seq'), route)]
    pallas_call x4, Pallas kernels: 19.4 us -> 21.3 us  [project(): pl.pallas_call(functools.partial(project_kernel, indices), grid=(2 * step...]
  transfers between devices with their start and end apart: 31 -> 32, of which waited for: 17 -> 15; matrix products, arithmetic and copies ran while one was open for 3% -> 3% of each run, Pallas kernels for 22% -> 25%
where the time goes in v11:
time: 139 us; the launch traced here: 138 us
  waiting for transfers between devices  59.8 us (43%)
  Pallas kernels  37.1 us (27%)
  starting transfers between devices  32 us (23%)
  local copies, waits for them, and re-layouts  6 us (4%)
  other arithmetic  2.28 us (2%)
    ppermute x12, waiting for transfers between devices, along(): lax.ppermute(block, 'seq', [(i, (i + CORES * chips) % size) for i in rang...  31.9 us
    ppermute x8, waiting for transfers between devices, across(): return lax.ppermute(block, ('kv', 'seq'), route)  26.3 us
    pallas_call x4, Pallas kernels, project(): pl.pallas_call(functools.partial(project_kernel, indices), grid=(2 * step...  21.3 us
    ppermute x12, starting transfers between devices, along(): lax.ppermute(block, 'seq', [(i, (i + CORES * chips) % size) for i in rang...  17.2 us
    ppermute x8, starting transfers between devices, across(): return lax.ppermute(block, ('kv', 'seq'), route)  10.4 us
    pallas_call x2, Pallas kernels, attention(): pl.pallas_call(functools.partial(attention_kernel, heads, head_dim, offse...  9.39 us
    pallas_call x4, Pallas kernels, finish(): pl.pallas_call(finish_kernel, grid=(tokens // tile,), in_specs=[pl.BlockS...  4.45 us
    unnamed x16, local copies, waits for them, and re-layouts  3.69 us
  transfers between devices with their start and end apart: 32, of which 15 were waited for; matrix products, arithmetic and copies ran while one was open for 3% of the time, Pallas kernels for 25%

profile of v11, /device:TPU:0, one launch (start us, length us, event | category | flops | bytes accessed | tf_op | source)
XLA Modules:
  0.0 138.2 jit_solution(9781985414326118481)
XLA Ops:
  0.7 1.0 copy-done.2
  1.8 1.0 copy-done.3
  2.8 2.0 %arrange.1 = (bf16[4,2,128,512]{3,2,1,0:T(8,128)(2,1)}, bf16[1,2,128,512]{3,2,1,0:T(8,128)(2,1)}, bf16[1,2,128,512]{3,2,1,0:T(8,128)(2,1)}, bf16[1,2,128,512]{3,...) custom-call(s32[4]{0:T(128)S(1)} %add_xor_fusion.owner_ref, bf16[128,2048]{1,0:T(8,128)(2,1)S(1)} %copy-done.2, ...), custom_call_target="tpu_custom_call" | custom-call | tf_op jit(solution)/shard_map/arrange/pallas_call | solution.py:42
  4.8 5.0 %collective-permute-start = (bf16[1,2,128,512]{3,2,1,0:T(8,128)(2,1)}, bf16[1,2,128,512]{3,2,1,0:T(8,128)(2,1)}, u32[]{:S(2)}, u32[]{:S(2)}) collective-permute-start(bf16[1,2,128,512]{3,2,1,0:T(8,128)(2,1)} %get-tuple-element.103.refs_0_), channel_id=1, source_target_pairs={{0,6},{1,7},{2,0},{3,1},{4,2},{5,3},{6,4},{7,5},{8,14},{9,15},{10,... | collective-permute-start | bytes 786440 | tf_op jit(solution)/shard_map/ppermute | solution.py:261
  9.8 1.1 copy.26
  11.3 0.7 slice.60
  12.0 3.1 %collective-permute-start.3 = (bf16[224,512]{1,0:T(8,128)(2,1)}, bf16[224,512]{1,0:T(8,128)(2,1)}, u32[]{:S(2)}, u32[]{:S(2)}) collective-permute-start(bf16[224,512]{1,0:T(8,128)(2,1)} %slice.60), channel_id=1, source_target_pairs={{0,1},{1,2},{2,3},{3,4},{4,5},{5,6},{6,7},{8,9},{9,10},{10,11},{11... | collective-permute-start | bytes 688136 | tf_op jit(solution)/shard_map/ppermute | solution.py:337
  15.9 1.6 %copy-done.1 = bf16[1024,1024]{1,0:T(8,128)(2,1)S(1)} copy-done((bf16[1024,1024]{1,0:T(8,128)(2,1)S(1)}, bf16[1024,1024]{1,0:T(8,128)(2,1)}, u32[]{:S(2)}) %copy-start.1) | copy-done | bytes 2097176
  17.5 4.6 %attention.2.second_ref = bf16[512,2048]{1,0:T(8,128)(2,1)S(1)} custom-call(s32[8]{0:T(128)S(1)} %pad_add_fusion.order_ref, bf16[1024,1024]{1,0:T(8,128)(2,1)S(1)} %copy-done, bf16[1024,1024]{1,0:T(8,128)(2,1)S(1)} %copy-done.1, bf16[1024,512]{1,0:T(8,128)(2,1)S(1)} %pad_maximum_fusion.ctx_ref, s32[1024,128]{1,0:T(8,128)S(1)} %broadcast_in_dim.13.low_ref), custom_call_target="tpu_custom_call" | custom-call | flops 1048576 | bytes 512 | tf_op jit(solution)/shard_map/attention/pallas_call | solution.py:126
  22.1 1.2 collective-permute-done.1.refs_1_
  23.4 4.7 %collective-permute-done.2.refs_1_ = bf16[1,2,128,512]{3,2,1,0:T(8,128)(2,1)} collective-permute-done((bf16[1,2,128,512]{3,2,1,0:T(8,128)(2,1)}, bf16[1,2,128,512]{3,2,1,0:T(8,128)(2,1)}, u32[]{:S(2)}, u32[]{:S(2)}) %collective-permute-start.2) | collective-permute-done | bytes 262176 | tf_op jit(solution)/shard_map/ppermute | solution.py:261
  28.1 3.9 %collective-permute-start.5 = (bf16[1,2,128,512]{3,2,1,0:T(8,128)(2,1)}, bf16[1,2,128,512]{3,2,1,0:T(8,128)(2,1)S(1)}, u32[]{:S(2)}, u32[]{:S(2)}) collective-permute-start(bf16[1,2,128,512]{3,2,1,0:T(8,128)(2,1)} %collective-permute-done.1.refs_1_), channel_id=1, source_target_pairs={{0,2},{1,3},{2,4},{3,5},{4,6},{5,7},{6,0},{7,1},{8,10},{9,11},{10,... | collective-permute-start | bytes 786440 | tf_op jit(solution)/shard_map/ppermute | solution.py:261
  32.0 0.5 collective-permute-start.6
  32.7 1.0 pad_maximum_fusion.1.ctx_ref
  33.7 4.8 %attention.3.first_ref = bf16[512,2048]{1,0:T(8,128)(2,1)S(1)} custom-call(s32[8]{0:T(128)S(1)} %pad_add_fusion.order_ref, bf16[1024,1024]{1,0:T(8,128)(2,1)S(1)} %copy-done, bf16[1024,1024]{1,0:T(8,128)(2,1)S(1)} %copy-done.1, bf16[736,512]{1,0:T(8,128)(2,1)S(1)} %pad_maximum_fusion.1.ctx_ref, s32[1024,128]{1,0:T(8,128)S(1)} %broadcast_in_dim.13.low_ref), custom_call_target="tpu_custom_call" | custom-call | flops 1048576 | bytes 512 | tf_op jit(solution)/shard_map/attention/pallas_call | solution.py:126
  38.5 0.7 collective-permute-done.5.refs_2_
  39.2 5.6 %collective-permute-done.9.refs_1_ = bf16[1,2,128,512]{3,2,1,0:T(8,128)(2,1)S(1)} collective-permute-done((bf16[1,2,128,512]{3,2,1,0:T(8,128)(2,1)S(1)}, bf16[1,2,128,512]{3,2,1,0:T(8,128)(2,1)S(1)}, u32[]{:S(2)}, u32[]{:S(2)}) %collective-permute-start.9) | collective-permute-done | bytes 262176 | tf_op jit(solution)/shard_map/ppermute | solution.py:261
  45.0 2.1 %collective-permute-start.12 = (bf16[1,2,128,512]{3,2,1,0:T(8,128)(2,1)}, bf16[1,2,128,512]{3,2,1,0:T(8,128)(2,1)S(1)}, u32[]{:S(2)}, u32[]{:S(2)}) collective-permute-start(bf16[1,2,128,512]{3,2,1,0:T(8,128)(2,1)} %collective-permute-done.2.refs_1_), channel_id=1, source_target_pairs={{0,2},{1,3},{2,4},{3,5},{4,6},{5,7},{6,0},{7,1},{8,10},{9,11},{10,... | collective-permute-start | bytes 786440 | tf_op jit(solution)/shard_map/ppermute | solution.py:261
  47.0 5.4 %project.4 = (bf16[2,1024,256]{2,1,0:T(8,128)(2,1)S(1)}, bf16[2,1024,256]{2,1,0:T(8,128)(2,1)S(1)}) custom-call(bf16[512,2048]{1,0:T(8,128)(2,1)S(1)} %attention.3.first_ref, bf16[512,2048]{1,0:T(8,128)(2,1)S(1)} %attention.2.second_ref, bf16[1,2,128,512]{3,2,1,0:T(8,128)(2,1)} %get-tuple-element.103.refs_0_, ...), custom_call_target="tpu_custom_call" | custom-call | flops 3000000000 | bytes 512 | tf_op jit(solution)/shard_map/project/pallas_call | solution.py:200
  52.5 1.6 %collective-permute-start.18 = (bf16[2,1024,256]{2,1,0:T(8,128)(2,1)S(1)}, bf16[2,1024,256]{2,1,0:T(8,128)(2,1)S(1)}, u32[]{:S(2)}, u32[]{:S(2)}) collective-permute-start(bf16[2,1024,256]{2,1,0:T(8,128)(2,1)S(1)} %get-tuple-element.117), channel_id=1, source_target_pairs={{0,8},{1,17},{2,10},{3,19},{4,12},{5,21},{6,14},{7,23},{8,0},{9,25... | collective-permute-start | bytes 3145736 | tf_op jit(solution)/shard_map/ppermute | solution.py:256
  54.0 5.4 %collective-permute-done.11.refs_3_ = bf16[1,2,128,512]{3,2,1,0:T(8,128)(2,1)S(1)} collective-permute-done((bf16[1,2,128,512]{3,2,1,0:T(8,128)(2,1)}, bf16[1,2,128,512]{3,2,1,0:T(8,128)(2,1)S(1)}, u32[]{:S(2)}, u32[]{:S(2)}) %collective-permute-start.11) | collective-permute-done | bytes 262176 | tf_op jit(solution)/shard_map/ppermute | solution.py:261
  59.5 0.7 collective-permute-start.15
  60.3 1.3 collective-permute-start.16
  61.9 5.4 %project.5 = (bf16[2,1024,256]{2,1,0:T(8,128)(2,1)S(1)}, bf16[2,1024,256]{2,1,0:T(8,128)(2,1)S(1)}) custom-call(bf16[512,2048]{1,0:T(8,128)(2,1)S(1)} %attention.3.first_ref, bf16[512,2048]{1,0:T(8,128)(2,1)S(1)} %attention.2.second_ref, bf16[1,2,128,512]{3,2,1,0:T(8,128)(2,1)} %get-tuple-element.119.refs_0_, ...), custom_call_target="tpu_custom_call" | custom-call | flops 3000000000 | bytes 512 | tf_op jit(solution)/shard_map/project/pallas_call | solution.py:200
  67.3 1.6 %collective-permute-start.23 = (bf16[2,1024,256]{2,1,0:T(8,128)(2,1)S(1)}, bf16[2,1024,256]{2,1,0:T(8,128)(2,1)S(1)}, u32[]{:S(2)}, u32[]{:S(2)}) collective-permute-start(bf16[2,1024,256]{2,1,0:T(8,128)(2,1)S(1)} %get-tuple-element.131), channel_id=1, source_target_pairs={{0,8},{1,17},{2,10},{3,19},{4,12},{5,21},{6,14},{7,23},{8,0},{9,25... | collective-permute-start | bytes 3145736 | tf_op jit(solution)/shard_map/ppermute | solution.py:256
  69.0 5.9 %collective-permute-done.16.refs_2_ = bf16[1,2,128,512]{3,2,1,0:T(8,128)(2,1)S(1)} collective-permute-done((bf16[1,2,128,512]{3,2,1,0:T(8,128)(2,1)S(1)}, bf16[1,2,128,512]{3,2,1,0:T(8,128)(2,1)S(1)}, u32[]{:S(2)}, u32[]{:S(2)}) %collective-permute-start.16) | collective-permute-done | bytes 262176 | tf_op jit(solution)/shard_map/ppermute | solution.py:261
  74.9 5.2 %collective-permute-done.17.refs_1_ = bf16[1,2,128,512]{3,2,1,0:T(8,128)(2,1)S(1)} collective-permute-done((bf16[1,2,128,512]{3,2,1,0:T(8,128)(2,1)S(1)}, bf16[1,2,128,512]{3,2,1,0:T(8,128)(2,1)S(1)}, u32[]{:S(2)}, u32[]{:S(2)}) %collective-permute-start.17) | collective-permute-done | bytes 262176 | tf_op jit(solution)/shard_map/ppermute | solution.py:261
  80.2 1.6 %collective-permute-start.24 = (bf16[2,1024,128]{2,1,0:T(8,128)(2,1)S(1)}, bf16[2,1024,128]{2,1,0:T(8,128)(2,1)S(1)}, u32[]{:S(2)}, u32[]{:S(2)}) collective-permute-start(bf16[2,1024,128]{2,1,0:T(8,128)(2,1)S(1)} %add_convert_fusion.3), channel_id=1, source_target_pairs={{0,16},{1,9},{2,18},{3,11},{4,20},{5,13},{6,22},{7,15},{8,24},{9,1... | collective-permute-start | bytes 1572872 | tf_op jit(solution)/shard_map/ppermute | solution.py:256
  82.1 3.5 %collective-permute-start.20 = (bf16[1,2,128,512]{3,2,1,0:T(8,128)(2,1)S(1)}, bf16[1,2,128,512]{3,2,1,0:T(8,128)(2,1)S(1)}, u32[]{:S(2)}, u32[]{:S(2)}) collective-permute-start(bf16[1,2,128,512]{3,2,1,0:T(8,128)(2,1)S(1)} %get-tuple-element.149.refs_0_), channel_id=1, source_target_pairs={{0,6},{1,7},{2,0},{3,1},{4,2},{5,3},{6,4},{7,5},{8,14},{9,15},{10,... | collective-permute-start | bytes 786440 | tf_op jit(solution)/shard_map/ppermute | solution.py:261
  85.6 5.2 %project.6 = (bf16[2,1024,256]{2,1,0:T(8,128)(2,1)S(1)}, bf16[2,1024,256]{2,1,0:T(8,128)(2,1)S(1)}) custom-call(bf16[512,2048]{1,0:T(8,128)(2,1)S(1)} %attention.3.first_ref, bf16[512,2048]{1,0:T(8,128)(2,1)S(1)} %attention.2.second_ref, bf16[1,2,128,512]{3,2,1,0:T(8,128)(2,1)S(1)} %copy-done.5, bf16[1,2,128,512]{3,2,1,0:T(8,128)(2,1)S(1)} %collective-permute-done.9.refs_1_, ...), custom_call_target="tpu_custom_call" | custom-call | flops 1500000000 | bytes 512 | tf_op jit(solution)/shard_map/project/pallas_call | solution.py:200
  91.1 1.4 %collective-permute-start.27 = (bf16[2,1024,128]{2,1,0:T(8,128)(2,1)S(1)}, bf16[2,1024,128]{2,1,0:T(8,128)(2,1)S(1)}, u32[]{:S(2)}, u32[]{:S(2)}) collective-permute-start(bf16[2,1024,128]{2,1,0:T(8,128)(2,1)S(1)} %add_convert_fusion.2), channel_id=1, source_target_pairs={{0,16},{1,9},{2,18},{3,11},{4,20},{5,13},{6,22},{7,15},{8,24},{9,1... | collective-permute-start | bytes 1572872 | tf_op jit(solution)/shard_map/ppermute | solution.py:256
  92.5 0.6 collective-permute-start.30
  93.1 3.2 %collective-permute-done.20.refs_3_ = bf16[1,2,128,512]{3,2,1,0:T(8,128)(2,1)S(1)} collective-permute-done((bf16[1,2,128,512]{3,2,1,0:T(8,128)(2,1)S(1)}, bf16[1,2,128,512]{3,2,1,0:T(8,128)(2,1)S(1)}, u32[]{:S(2)}, u32[]{:S(2)}) %collective-permute-start.20) | collective-permute-done | bytes 262176 | tf_op jit(solution)/shard_map/ppermute | solution.py:261
  96.3 0.5 collective-permute-start.26
  96.8 1.0 collective-permute-done.25.refs_6_
  97.8 0.4 collective-permute-done.26.refs_7_
  98.2 5.2 %project.7 = (bf16[2,1024,256]{2,1,0:T(8,128)(2,1)S(1)}, bf16[2,1024,256]{2,1,0:T(8,128)(2,1)S(1)}) custom-call(bf16[512,2048]{1,0:T(8,128)(2,1)S(1)} %attention.3.first_ref, bf16[512,2048]{1,0:T(8,128)(2,1)S(1)} %attention.2.second_ref, bf16[1,2,128,512]{3,2,1,0:T(8,128)(2,1)S(1)} %get-tuple-element.149.refs_0_, ...), custom_call_target="tpu_custom_call" | custom-call | flops 10000000 | bytes 512 | tf_op jit(solution)/shard_map/project/pallas_call | solution.py:200
  103.5 2.1 %collective-permute-done.27.last_ref = bf16[2,1024,128]{2,1,0:T(8,128)(2,1)S(1)} collective-permute-done((bf16[2,1024,128]{2,1,0:T(8,128)(2,1)S(1)}, bf16[2,1024,128]{2,1,0:T(8,128)(2,1)S(1)}, u32[]{:S(2)}, u32[]{:S(2)}) %collective-permute-start.27) | collective-permute-done | bytes 524320 | tf_op jit(solution)/shard_map/ppermute | solution.py:256
  105.5 1.8 %collective-permute-start.28 = (bf16[2,1024,256]{2,1,0:T(8,128)(2,1)S(1)}, bf16[2,1024,256]{2,1,0:T(8,128)(2,1)S(1)}, u32[]{:S(2)}, u32[]{:S(2)}) collective-permute-start(bf16[2,1024,256]{2,1,0:T(8,128)(2,1)S(1)} %get-tuple-element.157), channel_id=1, source_target_pairs={{0,8},{1,17},{2,10},{3,19},{4,12},{5,21},{6,14},{7,23},{8,0},{9,25... | collective-permute-start | bytes 3145736 | tf_op jit(solution)/shard_map/ppermute | solution.py:256
  107.4 3.5 %collective-permute-done.30.received_ref = bf16[2,1024,256]{2,1,0:T(8,128)(2,1)S(1)} collective-permute-done((bf16[2,1024,256]{2,1,0:T(8,128)(2,1)S(1)}, bf16[2,1024,256]{2,1,0:T(8,128)(2,1)S(1)}, u32[]{:S(2)}, u32[]{:S(2)}) %collective-permute-start.30) | collective-permute-done | bytes 1048608 | tf_op jit(solution)/shard_map/ppermute | solution.py:256
  111.0 0.9 collective-permute-start.31
  111.9 15.8 %collective-permute-done.28.received_ref = bf16[2,1024,256]{2,1,0:T(8,128)(2,1)S(1)} collective-permute-done((bf16[2,1024,256]{2,1,0:T(8,128)(2,1)S(1)}, bf16[2,1024,256]{2,1,0:T(8,128)(2,1)S(1)}, u32[]{:S(2)}, u32[]{:S(2)}) %collective-permute-start.28) | collective-permute-done | bytes 1048608 | tf_op jit(solution)/shard_map/ppermute | solution.py:256
  127.8 0.9 collective-permute-start.29
  128.7 1.1 finish.4
  129.8 1.1 finish.5
  131.0 1.1 finish.6
  132.1 5.0 %collective-permute-done.29.last_ref = bf16[2,1024,128]{2,1,0:T(8,128)(2,1)S(1)} collective-permute-done((bf16[2,1024,128]{2,1,0:T(8,128)(2,1)S(1)}, bf16[2,1024,128]{2,1,0:T(8,128)(2,1)S(1)}, u32[]{:S(2)}, u32[]{:S(2)}) %collective-permute-start.29) | collective-permute-done | bytes 524320 | tf_op jit(solution)/shard_map/ppermute | solution.py:256
  137.1 1.1 finish.7
  (67 shorter events, 2.9 us)
Async XLA Ops:
  0.7 1.0 copy-start.2
  1.8 1.0 copy-start.3
  2.8 8.2 %copy-start.6 = (bf16[1024,2,128]{2,1,0:T(2,128)(2,1)S(1)}, bf16[1024,2,128]{2,1,0:T(2,128)(2,1)}, u32[]{:S(2)}) copy-start(bf16[1024,2,128]{2,1,0:T(2,128)(2,1)} %param.9) | copy-start | bytes 1572868
  4.8 6.4 %copy-start.4 = (bf16[1,2,128,512]{3,2,1,0:T(8,128)(2,1)}, bf16[1,2,128,512]{3,2,1,0:T(8,128)(2,1)S(1)}, u32[]{:S(2)}) copy-start(bf16[1,2,128,512]{3,2,1,0:T(8,128)(2,1)S(1)} %get-tuple-element.134.refs_0_) | copy-start | bytes 786436
  4.8 17.3 %collective-permute-start = (bf16[1,2,128,512]{3,2,1,0:T(8,128)(2,1)}, bf16[1,2,128,512]{3,2,1,0:T(8,128)(2,1)}, u32[]{:S(2)}, u32[]{:S(2)}) collective-permute-start(bf16[1,2,128,512]{3,2,1,0:T(8,128)(2,1)} %get-tuple-element.103.refs_0_), channel_id=1, source_target_pairs={{0,6},{1,7},{2,0},{3,1},{4,2},{5,3},{6,4},{7,5},{8,14},{9,15},{10,... | collective-permute-start | bytes 786440 | tf_op jit(solution)/shard_map/ppermute | solution.py:261
  9.8 13.6 %collective-permute-start.1 = (bf16[1,2,128,512]{3,2,1,0:T(8,128)(2,1)}, bf16[1,2,128,512]{3,2,1,0:T(8,128)(2,1)}, u32[]{:S(2)}, u32[]{:S(2)}) collective-permute-start(bf16[1,2,128,512]{3,2,1,0:T(8,128)(2,1)} %get-tuple-element.103.refs_0_), channel_id=1, source_target_pairs={{0,2},{1,3},{2,4},{3,5},{4,6},{5,7},{6,0},{7,1},{8,10},{9,11},{10,... | collective-permute-start | bytes 786440 | tf_op jit(solution)/shard_map/ppermute | solution.py:261
  9.8 18.3 %collective-permute-start.2 = (bf16[1,2,128,512]{3,2,1,0:T(8,128)(2,1)}, bf16[1,2,128,512]{3,2,1,0:T(8,128)(2,1)}, u32[]{:S(2)}, u32[]{:S(2)}) collective-permute-start(bf16[1,2,128,512]{3,2,1,0:T(8,128)(2,1)} %get-tuple-element.119.refs_0_), channel_id=1, source_target_pairs={{0,2},{1,3},{2,4},{3,5},{4,6},{5,7},{6,0},{7,1},{8,10},{9,11},{10,... | collective-permute-start | bytes 786440 | tf_op jit(solution)/shard_map/ppermute | solution.py:261
  9.8 18.3 %collective-permute-start.4 = (bf16[4,2,128,512]{3,2,1,0:T(8,128)(2,1)}, bf16[4,2,128,512]{3,2,1,0:T(8,128)(2,1)}, u32[]{:S(2)}, u32[]{:S(2)}) collective-permute-start(bf16[4,2,128,512]{3,2,1,0:T(8,128)(2,1)} %get-tuple-element.91), channel_id=1, source_target_pairs={{0,1},{1,0},{2,3},{3,2},{4,5},{5,4},{6,7},{7,6},{8,9},{9,8},{10,11... | collective-permute-start | bytes 3145736 | tf_op jit(solution)/shard_map/ppermute | solution.py:265
  11.1 4.1 %copy-start.7 = (s32[64]{0:T(128)S(1)}, s32[64]{0:T(128)}, u32[]{:S(2)}) copy-start(s32[64]{0:T(128)} %param.11) | copy-start | bytes 772
  11.2 4.7 %copy-start = (bf16[1024,1024]{1,0:T(8,128)(2,1)S(1)}, bf16[1024,1024]{1,0:T(8,128)(2,1)}, u32[]{:S(2)}) copy-start(bf16[1024,1024]{1,0:T(8,128)(2,1)} %q_ref.3) | copy-start | bytes 6291460
  12.0 10.1 %collective-permute-start.3 = (bf16[224,512]{1,0:T(8,128)(2,1)}, bf16[224,512]{1,0:T(8,128)(2,1)}, u32[]{:S(2)}, u32[]{:S(2)}) collective-permute-start(bf16[224,512]{1,0:T(8,128)(2,1)} %slice.60), channel_id=1, source_target_pairs={{0,1},{1,2},{2,3},{3,4},{4,5},{5,6},{6,7},{8,9},{9,10},{10,11},{11... | collective-permute-start | bytes 688136 | tf_op jit(solution)/shard_map/ppermute | solution.py:337
  15.9 1.6 %copy-start.1 = (bf16[1024,1024]{1,0:T(8,128)(2,1)S(1)}, bf16[1024,1024]{1,0:T(8,128)(2,1)}, u32[]{:S(2)}) copy-start(bf16[1024,1024]{1,0:T(8,128)(2,1)} %qt_ref.3) | copy-start | bytes 6291460
  17.5 15.0 %copy-start.5 = (bf16[1,2,128,512]{3,2,1,0:T(8,128)(2,1)S(1)}, bf16[1,2,128,512]{3,2,1,0:T(8,128)(2,1)}, u32[]{:S(2)}) copy-start(bf16[1,2,128,512]{3,2,1,0:T(8,128)(2,1)} %copy-done.4) | copy-start | bytes 786436
  28.1 11.1 %collective-permute-start.5 = (bf16[1,2,128,512]{3,2,1,0:T(8,128)(2,1)}, bf16[1,2,128,512]{3,2,1,0:T(8,128)(2,1)S(1)}, u32[]{:S(2)}, u32[]{:S(2)}) collective-permute-start(bf16[1,2,128,512]{3,2,1,0:T(8,128)(2,1)} %collective-permute-done.1.refs_1_), channel_id=1, source_target_pairs={{0,2},{1,3},{2,4},{3,5},{4,6},{5,7},{6,0},{7,1},{8,10},{9,11},{10,... | collective-permute-start | bytes 786440 | tf_op jit(solution)/shard_map/ppermute | solution.py:261
  32.0 7.2 %collective-permute-start.7 = (bf16[1,2,128,512]{3,2,1,0:T(8,128)(2,1)}, bf16[1,2,128,512]{3,2,1,0:T(8,128)(2,1)S(1)}, u32[]{:S(2)}, u32[]{:S(2)}) collective-permute-start(bf16[1,2,128,512]{3,2,1,0:T(8,128)(2,1)} %collective-permute-done.1.refs_1_), channel_id=1, source_target_pairs={{0,1},{1,0},{2,3},{3,2},{4,5},{5,4},{6,7},{7,6},{8,9},{9,8},{10,11... | collective-permute-start | bytes 786440 | tf_op jit(solution)/shard_map/ppermute | solution.py:265
  32.0 7.2 %collective-permute-start.6 = (bf16[1,2,128,512]{3,2,1,0:T(8,128)(2,1)}, bf16[1,2,128,512]{3,2,1,0:T(8,128)(2,1)S(1)}, u32[]{:S(2)}, u32[]{:S(2)}) collective-permute-start(bf16[1,2,128,512]{3,2,1,0:T(8,128)(2,1)} %collective-permute-done.refs_3_), channel_id=1, source_target_pairs={{0,1},{1,0},{2,3},{3,2},{4,5},{5,4},{6,7},{7,6},{8,9},{9,8},{10,11... | collective-permute-start | bytes 786440 | tf_op jit(solution)/shard_map/ppermute | solution.py:265
  32.5 6.7 %collective-permute-start.8 = (bf16[1,2,128,512]{3,2,1,0:T(8,128)(2,1)}, bf16[1,2,128,512]{3,2,1,0:T(8,128)(2,1)S(1)}, u32[]{:S(2)}, u32[]{:S(2)}) collective-permute-start(bf16[1,2,128,512]{3,2,1,0:T(8,128)(2,1)} %collective-permute-done.2.refs_1_), channel_id=1, source_target_pairs={{0,1},{1,0},{2,3},{3,2},{4,5},{5,4},{6,7},{7,6},{8,9},{9,8},{10,11... | collective-permute-start | bytes 786440 | tf_op jit(solution)/shard_map/ppermute | solution.py:265
  32.5 12.3 %collective-permute-start.9 = (bf16[1,2,128,512]{3,2,1,0:T(8,128)(2,1)S(1)}, bf16[1,2,128,512]{3,2,1,0:T(8,128)(2,1)S(1)}, u32[]{:S(2)}, u32[]{:S(2)}) collective-permute-start(bf16[1,2,128,512]{3,2,1,0:T(8,128)(2,1)S(1)} %copy-done.5), channel_id=1, source_target_pairs={{0,2},{1,3},{2,4},{3,5},{4,6},{5,7},{6,0},{7,1},{8,10},{9,11},{10,... | collective-permute-start | bytes 786440 | tf_op jit(solution)/shard_map/ppermute | solution.py:261
  44.8 2.2 %collective-permute-start.10 = (bf16[1,2,128,512]{3,2,1,0:T(8,128)(2,1)S(1)}, bf16[1,2,128,512]{3,2,1,0:T(8,128)(2,1)S(1)}, u32[]{:S(2)}, u32[]{:S(2)}) collective-permute-start(bf16[1,2,128,512]{3,2,1,0:T(8,128)(2,1)S(1)} %collective-permute-done.5.refs_2_), channel_id=1, source_target_pairs={{0,1},{1,0},{2,3},{3,2},{4,5},{5,4},{6,7},{7,6},{8,9},{9,8},{10,11... | collective-permute-start | bytes 786440 | tf_op jit(solution)/shard_map/ppermute | solution.py:265
  45.0 14.4 %collective-permute-start.11 = (bf16[1,2,128,512]{3,2,1,0:T(8,128)(2,1)}, bf16[1,2,128,512]{3,2,1,0:T(8,128)(2,1)S(1)}, u32[]{:S(2)}, u32[]{:S(2)}) collective-permute-start(bf16[1,2,128,512]{3,2,1,0:T(8,128)(2,1)} %get-tuple-element.119.refs_0_), channel_id=1, source_target_pairs={{0,6},{1,7},{2,0},{3,1},{4,2},{5,3},{6,4},{7,5},{8,14},{9,15},{10,... | collective-permute-start | bytes 786440 | tf_op jit(solution)/shard_map/ppermute | solution.py:261
  45.0 14.4 %collective-permute-start.12 = (bf16[1,2,128,512]{3,2,1,0:T(8,128)(2,1)}, bf16[1,2,128,512]{3,2,1,0:T(8,128)(2,1)S(1)}, u32[]{:S(2)}, u32[]{:S(2)}) collective-permute-start(bf16[1,2,128,512]{3,2,1,0:T(8,128)(2,1)} %collective-permute-done.2.refs_1_), channel_id=1, source_target_pairs={{0,2},{1,3},{2,4},{3,5},{4,6},{5,7},{6,0},{7,1},{8,10},{9,11},{10,... | collective-permute-start | bytes 786440 | tf_op jit(solution)/shard_map/ppermute | solution.py:261
  47.0 12.4 %collective-permute-start.13 = (bf16[1,2,128,512]{3,2,1,0:T(8,128)(2,1)S(1)}, bf16[1,2,128,512]{3,2,1,0:T(8,128)(2,1)S(1)}, u32[]{:S(2)}, u32[]{:S(2)}) collective-permute-start(bf16[1,2,128,512]{3,2,1,0:T(8,128)(2,1)S(1)} %collective-permute-done.9.refs_1_), channel_id=1, source_target_pairs={{0,1},{1,0},{2,3},{3,2},{4,5},{5,4},{6,7},{7,6},{8,9},{9,8},{10,11... | collective-permute-start | bytes 786440 | tf_op jit(solution)/shard_map/ppermute | solution.py:265
  52.5 16.4 %collective-permute-start.18 = (bf16[2,1024,256]{2,1,0:T(8,128)(2,1)S(1)}, bf16[2,1024,256]{2,1,0:T(8,128)(2,1)S(1)}, u32[]{:S(2)}, u32[]{:S(2)}) collective-permute-start(bf16[2,1024,256]{2,1,0:T(8,128)(2,1)S(1)} %get-tuple-element.117), channel_id=1, source_target_pairs={{0,8},{1,17},{2,10},{3,19},{4,12},{5,21},{6,14},{7,23},{8,0},{9,25... | collective-permute-start | bytes 3145736 | tf_op jit(solution)/shard_map/ppermute | solution.py:256
  59.5 2.5 %collective-permute-start.14 = (bf16[2,2,128,512]{3,2,1,0:T(8,128)(2,1)S(1)}, bf16[2,2,128,512]{3,2,1,0:T(8,128)(2,1)S(1)}, u32[]{:S(2)}, u32[]{:S(2)}) collective-permute-start(bf16[2,2,128,512]{3,2,1,0:T(8,128)(2,1)S(1)} %pad_maximum_fusion.2), channel_id=1, source_target_pairs={{0,1},{1,0},{2,3},{3,2},{4,5},{5,4},{6,7},{7,6},{8,9},{9,8},{10,11... | collective-permute-start | bytes 1572872 | tf_op jit(solution)/shard_map/ppermute | solution.py:265
  59.5 9.5 %collective-permute-start.15 = (bf16[1,2,128,512]{3,2,1,0:T(8,128)(2,1)S(1)}, bf16[1,2,128,512]{3,2,1,0:T(8,128)(2,1)S(1)}, u32[]{:S(2)}, u32[]{:S(2)}) collective-permute-start(bf16[1,2,128,512]{3,2,1,0:T(8,128)(2,1)S(1)} %copy-done.5), channel_id=1, source_target_pairs={{0,6},{1,7},{2,0},{3,1},{4,2},{5,3},{6,4},{7,5},{8,14},{9,15},{10,... | collective-permute-start | bytes 786440 | tf_op jit(solution)/shard_map/ppermute | solution.py:261
  60.3 14.6 %collective-permute-start.16 = (bf16[1,2,128,512]{3,2,1,0:T(8,128)(2,1)S(1)}, bf16[1,2,128,512]{3,2,1,0:T(8,128)(2,1)S(1)}, u32[]{:S(2)}, u32[]{:S(2)}) collective-permute-start(bf16[1,2,128,512]{3,2,1,0:T(8,128)(2,1)S(1)} %collective-permute-done.9.refs_1_), channel_id=1, source_target_pairs={{0,2},{1,3},{2,4},{3,5},{4,6},{5,7},{6,0},{7,1},{8,10},{9,11},{10,... | collective-permute-start | bytes 786440 | tf_op jit(solution)/shard_map/ppermute | solution.py:261
  61.6 18.5 %collective-permute-start.17 = (bf16[1,2,128,512]{3,2,1,0:T(8,128)(2,1)S(1)}, bf16[1,2,128,512]{3,2,1,0:T(8,128)(2,1)S(1)}, u32[]{:S(2)}, u32[]{:S(2)}) collective-permute-start(bf16[1,2,128,512]{3,2,1,0:T(8,128)(2,1)S(1)} %get-tuple-element.149.refs_0_), channel_id=1, source_target_pairs={{0,2},{1,3},{2,4},{3,5},{4,6},{5,7},{6,0},{7,1},{8,10},{9,11},{10,... | collective-permute-start | bytes 786440 | tf_op jit(solution)/shard_map/ppermute | solution.py:261
  67.3 23.6 %collective-permute-start.23 = (bf16[2,1024,256]{2,1,0:T(8,128)(2,1)S(1)}, bf16[2,1024,256]{2,1,0:T(8,128)(2,1)S(1)}, u32[]{:S(2)}, u32[]{:S(2)}) collective-permute-start(bf16[2,1024,256]{2,1,0:T(8,128)(2,1)S(1)} %get-tuple-element.131), channel_id=1, source_target_pairs={{0,8},{1,17},{2,10},{3,19},{4,12},{5,21},{6,14},{7,23},{8,0},{9,25... | collective-permute-start | bytes 3145736 | tf_op jit(solution)/shard_map/ppermute | solution.py:256
  80.2 2.0 %collective-permute-start.19 = (bf16[2,2,128,512]{3,2,1,0:T(8,128)(2,1)S(1)}, bf16[2,2,128,512]{3,2,1,0:T(8,128)(2,1)S(1)}, u32[]{:S(2)}, u32[]{:S(2)}) collective-permute-start(bf16[2,2,128,512]{3,2,1,0:T(8,128)(2,1)S(1)} %pad_maximum_fusion.3), channel_id=1, source_target_pairs={{0,1},{1,0},{2,3},{3,2},{4,5},{5,4},{6,7},{7,6},{8,9},{9,8},{10,11... | collective-permute-start | bytes 1572872 | tf_op jit(solution)/shard_map/ppermute | solution.py:265
  80.2 10.7 %collective-permute-start.24 = (bf16[2,1024,128]{2,1,0:T(8,128)(2,1)S(1)}, bf16[2,1024,128]{2,1,0:T(8,128)(2,1)S(1)}, u32[]{:S(2)}, u32[]{:S(2)}) collective-permute-start(bf16[2,1024,128]{2,1,0:T(8,128)(2,1)S(1)} %add_convert_fusion.3), channel_id=1, source_target_pairs={{0,16},{1,9},{2,18},{3,11},{4,20},{5,13},{6,22},{7,15},{8,24},{9,1... | collective-permute-start | bytes 1572872 | tf_op jit(solution)/shard_map/ppermute | solution.py:256
  81.8 14.5 %collective-permute-start.21 = (bf16[1,2,128,512]{3,2,1,0:T(8,128)(2,1)S(1)}, bf16[1,2,128,512]{3,2,1,0:T(8,128)(2,1)S(1)}, u32[]{:S(2)}, u32[]{:S(2)}) collective-permute-start(bf16[1,2,128,512]{3,2,1,0:T(8,128)(2,1)S(1)} %collective-permute-done.17.refs_1_), channel_id=1, source_target_pairs={{0,2},{1,3},{2,4},{3,5},{4,6},{5,7},{6,0},{7,1},{8,10},{9,11},{10,... | collective-permute-start | bytes 786440 | tf_op jit(solution)/shard_map/ppermute | solution.py:261
  81.9 14.3 %collective-permute-start.22 = (bf16[1,2,128,512]{3,2,1,0:T(8,128)(2,1)S(1)}, bf16[1,2,128,512]{3,2,1,0:T(8,128)(2,1)S(1)}, u32[]{:S(2)}, u32[]{:S(2)}) collective-permute-start(bf16[1,2,128,512]{3,2,1,0:T(8,128)(2,1)S(1)} %collective-permute-done.17.refs_1_), channel_id=1, source_target_pairs={{0,1},{1,0},{2,3},{3,2},{4,5},{5,4},{6,7},{7,6},{8,9},{9,8},{10,11... | collective-permute-start | bytes 786440 | tf_op jit(solution)/shard_map/ppermute | solution.py:265
  82.1 14.2 %collective-permute-start.20 = (bf16[1,2,128,512]{3,2,1,0:T(8,128)(2,1)S(1)}, bf16[1,2,128,512]{3,2,1,0:T(8,128)(2,1)S(1)}, u32[]{:S(2)}, u32[]{:S(2)}) collective-permute-start(bf16[1,2,128,512]{3,2,1,0:T(8,128)(2,1)S(1)} %get-tuple-element.149.refs_0_), channel_id=1, source_target_pairs={{0,6},{1,7},{2,0},{3,1},{4,2},{5,3},{6,4},{7,5},{8,14},{9,15},{10,... | collective-permute-start | bytes 786440 | tf_op jit(solution)/shard_map/ppermute | solution.py:261
  91.1 14.5 %collective-permute-start.27 = (bf16[2,1024,128]{2,1,0:T(8,128)(2,1)S(1)}, bf16[2,1024,128]{2,1,0:T(8,128)(2,1)S(1)}, u32[]{:S(2)}, u32[]{:S(2)}) collective-permute-start(bf16[2,1024,128]{2,1,0:T(8,128)(2,1)S(1)} %add_convert_fusion.2), channel_id=1, source_target_pairs={{0,16},{1,9},{2,18},{3,11},{4,20},{5,13},{6,22},{7,15},{8,24},{9,1... | collective-permute-start | bytes 1572872 | tf_op jit(solution)/shard_map/ppermute | solution.py:256
  92.5 18.3 %collective-permute-start.30 = (bf16[2,1024,256]{2,1,0:T(8,128)(2,1)S(1)}, bf16[2,1024,256]{2,1,0:T(8,128)(2,1)S(1)}, u32[]{:S(2)}, u32[]{:S(2)}) collective-permute-start(bf16[2,1024,256]{2,1,0:T(8,128)(2,1)S(1)} %get-tuple-element.145), channel_id=1, source_target_pairs={{0,8},{1,17},{2,10},{3,19},{4,12},{5,21},{6,14},{7,23},{8,0},{9,25... | collective-permute-start | bytes 3145736 | tf_op jit(solution)/shard_map/ppermute | solution.py:256
  96.3 1.5 %collective-permute-start.25 = (bf16[1,2,128,512]{3,2,1,0:T(8,128)(2,1)S(1)}, bf16[1,2,128,512]{3,2,1,0:T(8,128)(2,1)S(1)}, u32[]{:S(2)}, u32[]{:S(2)}) collective-permute-start(bf16[1,2,128,512]{3,2,1,0:T(8,128)(2,1)S(1)} %collective-permute-done.21.refs_2_), channel_id=1, source_target_pairs={{0,1},{1,0},{2,3},{3,2},{4,5},{5,4},{6,7},{7,6},{8,9},{9,8},{10,11... | collective-permute-start | bytes 786440 | tf_op jit(solution)/shard_map/ppermute | solution.py:265
  96.3 1.9 %collective-permute-start.26 = (bf16[1,2,128,512]{3,2,1,0:T(8,128)(2,1)S(1)}, bf16[1,2,128,512]{3,2,1,0:T(8,128)(2,1)S(1)}, u32[]{:S(2)}, u32[]{:S(2)}) collective-permute-start(bf16[1,2,128,512]{3,2,1,0:T(8,128)(2,1)S(1)} %collective-permute-done.20.refs_3_), channel_id=1, source_target_pairs={{0,1},{1,0},{2,3},{3,2},{4,5},{5,4},{6,7},{7,6},{8,9},{9,8},{10,11... | collective-permute-start | bytes 786440 | tf_op jit(solution)/shard_map/ppermute | solution.py:265
  105.5 22.1 %collective-permute-start.28 = (bf16[2,1024,256]{2,1,0:T(8,128)(2,1)S(1)}, bf16[2,1024,256]{2,1,0:T(8,128)(2,1)S(1)}, u32[]{:S(2)}, u32[]{:S(2)}) collective-permute-start(bf16[2,1024,256]{2,1,0:T(8,128)(2,1)S(1)} %get-tuple-element.157), channel_id=1, source_target_pairs={{0,8},{1,17},{2,10},{3,19},{4,12},{5,21},{6,14},{7,23},{8,0},{9,25... | collective-permute-start | bytes 3145736 | tf_op jit(solution)/shard_map/ppermute | solution.py:256
  111.0 20.0 %collective-permute-start.31 = (bf16[2,1024,128]{2,1,0:T(8,128)(2,1)S(1)}, bf16[2,1024,128]{2,1,0:T(8,128)(2,1)S(1)}, u32[]{:S(2)}, u32[]{:S(2)}) collective-permute-start(bf16[2,1024,128]{2,1,0:T(8,128)(2,1)S(1)} %add_convert_fusion), channel_id=1, source_target_pairs={{0,16},{1,9},{2,18},{3,11},{4,20},{5,13},{6,22},{7,15},{8,24},{9,1... | collective-permute-start | bytes 1572872 | tf_op jit(solution)/shard_map/ppermute | solution.py:256
  127.8 9.2 %collective-permute-start.29 = (bf16[2,1024,128]{2,1,0:T(8,128)(2,1)S(1)}, bf16[2,1024,128]{2,1,0:T(8,128)(2,1)S(1)}, u32[]{:S(2)}, u32[]{:S(2)}) collective-permute-start(bf16[2,1024,128]{2,1,0:T(8,128)(2,1)S(1)} %add_convert_fusion.1), channel_id=1, source_target_pairs={{0,16},{1,9},{2,18},{3,11},{4,20},{5,13},{6,22},{7,15},{8,24},{9,1... | collective-permute-start | bytes 1572872 | tf_op jit(solution)/shard_map/ppermute | solution.py:256

commit v12 on v11

--- a/solution.py
+++ b/solution.py
@@ -19,7 +19,17 @@
 vmem_bytes = 12 * 1024 * 1024
 
 
-def arrange_kernel(owner_ref, tangent_ref, value_ref, whole_ref, *chunk_refs):
+def arrange_kernel(owner_ref, tangent_hbm, value_hbm, whole_ref, *refs):
+    *chunk_refs, tangent_ref, value_ref, sems = refs
+    sources = ((tangent_hbm, tangent_ref), (value_hbm, value_ref))
+    copies = [
+        pltpu.make_async_copy(source, target, sems.at[index])
+        for index, (source, target) in enumerate(sources)
+    ]
+    for copy in copies:
+        copy.start()
+    for copy in copies:
+        copy.wait()
     owners = owner_ref.shape[0]
     columns = tangent_ref.shape[1] // owners
     part = columns // len(chunk_refs)
@@ -42,9 +52,11 @@
     return pl.pallas_call(
         arrange_kernel,
         in_specs=[pl.BlockSpec(memory_space=pltpu.SMEM)]
-        + [pl.BlockSpec(memory_space=pltpu.VMEM)] * 2,
+        + [pl.BlockSpec(memory_space=pltpu.HBM)] * 2,
         out_specs=[pl.BlockSpec(memory_space=pltpu.VMEM)] * len(shapes),
         out_shape=shapes,
+        scratch_shapes=[pltpu.VMEM(value.shape, value.dtype)] * 2
+        + [pltpu.SemaphoreType.DMA((2,))],
         compiler_params=pltpu.CompilerParams(vmem_limit_bytes=vmem_bytes),
         name="arrange",
     )(owners, tangent, value)
@@ -283,9 +295,11 @@
         if self.backward:
             self.near[-1] = along(self.near[0], -1)
 
-    def farther(self):
+    def farther_ahead(self):
         for step in range(2, self.forward + 1):
             self.near[step] = along(self.near[step - 1], 1)
+
+    def farther_behind(self):
         for step in range(2, self.backward + 1):
             self.near[-step] = along(self.near[1 - step], -1)
 
@@ -382,7 +396,8 @@
     pair_second, prior, whole = settle(pair_second, prior, whole)
     gathers[0].exchange(False)
     gathers[1].exchange()
-    gathers[0].farther()
+    gathers[0].farther_ahead()
+    gathers[0].farther_behind()
     gathers[2].ahead()
     pair_first = attend(0, jnp.concatenate([prior, stacked[:half]], axis=0))
 
@@ -395,14 +410,21 @@
         if chunk != 1 and first < CHUNKS:
             gathers[first].exchange()
         if chunk + 1 < CHUNKS:
-            gathers[chunk + 1].behind()
-            gathers[chunk + 1].farther()
+            if chunk + 2 < CHUNKS:
+                gathers[chunk + 1].behind()
+                gathers[chunk + 1].farther_behind()
+            gathers[chunk + 1].farther_ahead()
         if 0 < chunk < CHUNKS - 2:
             gathers[chunk + 2].ahead()
         send, keep = project(
             SCHEDULED_GFLOPS[chunk], pairs, gathers[chunk].pieces(chunk, whole)
         )
         kept.append(keep)
+        if chunk == CHUNKS - 2:
+            final = gathers[chunk + 1]
+            final.near[0], send = together(final.near[0], send)
+            final.behind()
+            final.farther_behind()
         if chunk >= 2:
             last[chunk - 2], send = together(last[chunk - 2], send)
         received.append(across(send, 0))

time: 139 us -> 139 us (level)
  no operation moved by 1% of the time
where the time goes in v12:
time: 139 us
  waiting for transfers between devices  59.9 us (43%)
  Pallas kernels  37.2 us (27%)
  starting transfers between devices  32.3 us (23%)
  local copies, waits for them, and re-layouts  6 us (4%)
  other arithmetic  2.28 us (2%)
    ppermute x12, waiting for transfers between devices, along(): lax.ppermute(block, 'seq', [(i, (i + CORES * chips) % size) for i in rang...  33 us
    ppermute x8, waiting for transfers between devices, across(): return lax.ppermute(block, ('kv', 'seq'), route)  25.3 us
    pallas_call x4, Pallas kernels, project(): pl.pallas_call(functools.partial(project_kernel, indices), grid=(2 * step...  21.3 us
    ppermute x12, starting transfers between devices, along(): lax.ppermute(block, 'seq', [(i, (i + CORES * chips) % size) for i in rang...  17.5 us
    ppermute x8, starting transfers between devices, across(): return lax.ppermute(block, ('kv', 'seq'), route)  10.4 us
    pallas_call x2, Pallas kernels, attention(): pl.pallas_call(functools.partial(attention_kernel, heads, head_dim, offse...  9.39 us
    pallas_call x4, Pallas kernels, finish(): pl.pallas_call(finish_kernel, grid=(tokens // tile,), in_specs=[pl.BlockS...  4.45 us
    unnamed x16, local copies, waits for them, and re-layouts  3.69 us
  transfers between devices with their start and end apart: 32, of which 15 were waited for; matrix products, arithmetic and copies ran while one was open for 3% of the time, Pallas kernels for 25%

profile of v12, /device:TPU:0, one launch (start us, length us, event | category | flops | bytes accessed | tf_op | source)
XLA Modules:
  0.0 138.5 jit_solution(16830823755844069989)
XLA Ops:
  0.7 1.0 copy-done.2
  1.8 1.0 copy-done.3
  2.8 2.1 %arrange.1 = (bf16[4,2,128,512]{3,2,1,0:T(8,128)(2,1)}, bf16[1,2,128,512]{3,2,1,0:T(8,128)(2,1)}, bf16[1,2,128,512]{3,2,1,0:T(8,128)(2,1)}, bf16[1,2,128,512]{3,...) custom-call(s32[4]{0:T(128)S(1)} %add_xor_fusion.owner_ref, bf16[128,2048]{1,0:T(8,128)(2,1)S(1)} %copy-done.2, ...), custom_call_target="tpu_custom_call" | custom-call | tf_op jit(solution)/shard_map/arrange/pallas_call | solution.py:52
  4.9 5.1 %collective-permute-start = (bf16[1,2,128,512]{3,2,1,0:T(8,128)(2,1)}, bf16[1,2,128,512]{3,2,1,0:T(8,128)(2,1)}, u32[]{:S(2)}, u32[]{:S(2)}) collective-permute-start(bf16[1,2,128,512]{3,2,1,0:T(8,128)(2,1)} %get-tuple-element.105.refs_0_), channel_id=1, source_target_pairs={{0,6},{1,7},{2,0},{3,1},{4,2},{5,3},{6,4},{7,5},{8,14},{9,15},{10,... | collective-permute-start | bytes 786440 | tf_op jit(solution)/shard_map/ppermute | solution.py:273
  10.0 1.1 copy.26
  11.5 0.7 slice.60
  12.2 3.1 %collective-permute-start.3 = (bf16[224,512]{1,0:T(8,128)(2,1)}, bf16[224,512]{1,0:T(8,128)(2,1)}, u32[]{:S(2)}, u32[]{:S(2)}) collective-permute-start(bf16[224,512]{1,0:T(8,128)(2,1)} %slice.60), channel_id=1, source_target_pairs={{0,1},{1,2},{2,3},{3,4},{4,5},{5,6},{6,7},{8,9},{9,10},{10,11},{11... | collective-permute-start | bytes 688136 | tf_op jit(solution)/shard_map/ppermute | solution.py:351
  16.1 1.6 %copy-done.1 = bf16[1024,1024]{1,0:T(8,128)(2,1)S(1)} copy-done((bf16[1024,1024]{1,0:T(8,128)(2,1)S(1)}, bf16[1024,1024]{1,0:T(8,128)(2,1)}, u32[]{:S(2)}) %copy-start.1) | copy-done | bytes 2097176
  17.6 4.6 %attention.2.second_ref = bf16[512,2048]{1,0:T(8,128)(2,1)S(1)} custom-call(s32[8]{0:T(128)S(1)} %pad_add_fusion.order_ref, bf16[1024,1024]{1,0:T(8,128)(2,1)S(1)} %copy-done, bf16[1024,1024]{1,0:T(8,128)(2,1)S(1)} %copy-done.1, bf16[1024,512]{1,0:T(8,128)(2,1)S(1)} %pad_maximum_fusion.ctx_ref, s32[1024,128]{1,0:T(8,128)S(1)} %broadcast_in_dim.13.low_ref), custom_call_target="tpu_custom_call" | custom-call | flops 1048576 | bytes 512 | tf_op jit(solution)/shard_map/attention/pallas_call | solution.py:138
  22.3 1.2 collective-permute-done.1.refs_1_
  23.5 4.7 %collective-permute-done.2.refs_1_ = bf16[1,2,128,512]{3,2,1,0:T(8,128)(2,1)} collective-permute-done((bf16[1,2,128,512]{3,2,1,0:T(8,128)(2,1)}, bf16[1,2,128,512]{3,2,1,0:T(8,128)(2,1)}, u32[]{:S(2)}, u32[]{:S(2)}) %collective-permute-start.2) | collective-permute-done | bytes 262176 | tf_op jit(solution)/shard_map/ppermute | solution.py:273
  28.3 3.9 %collective-permute-start.5 = (bf16[1,2,128,512]{3,2,1,0:T(8,128)(2,1)}, bf16[1,2,128,512]{3,2,1,0:T(8,128)(2,1)S(1)}, u32[]{:S(2)}, u32[]{:S(2)}) collective-permute-start(bf16[1,2,128,512]{3,2,1,0:T(8,128)(2,1)} %collective-permute-done.1.refs_1_), channel_id=1, source_target_pairs={{0,2},{1,3},{2,4},{3,5},{4,6},{5,7},{6,0},{7,1},{8,10},{9,11},{10,... | collective-permute-start | bytes 786440 | tf_op jit(solution)/shard_map/ppermute | solution.py:273
  32.2 0.5 collective-permute-start.6
  32.9 1.0 pad_maximum_fusion.1.ctx_ref
  33.9 4.8 %attention.3.first_ref = bf16[512,2048]{1,0:T(8,128)(2,1)S(1)} custom-call(s32[8]{0:T(128)S(1)} %pad_add_fusion.order_ref, bf16[1024,1024]{1,0:T(8,128)(2,1)S(1)} %copy-done, bf16[1024,1024]{1,0:T(8,128)(2,1)S(1)} %copy-done.1, bf16[736,512]{1,0:T(8,128)(2,1)S(1)} %pad_maximum_fusion.1.ctx_ref, s32[1024,128]{1,0:T(8,128)S(1)} %broadcast_in_dim.13.low_ref), custom_call_target="tpu_custom_call" | custom-call | flops 1048576 | bytes 512 | tf_op jit(solution)/shard_map/attention/pallas_call | solution.py:138
  38.6 0.7 collective-permute-done.5.refs_2_
  39.4 5.6 %collective-permute-done.9.refs_1_ = bf16[1,2,128,512]{3,2,1,0:T(8,128)(2,1)S(1)} collective-permute-done((bf16[1,2,128,512]{3,2,1,0:T(8,128)(2,1)S(1)}, bf16[1,2,128,512]{3,2,1,0:T(8,128)(2,1)S(1)}, u32[]{:S(2)}, u32[]{:S(2)}) %collective-permute-start.9) | collective-permute-done | bytes 262176 | tf_op jit(solution)/shard_map/ppermute | solution.py:273
  45.1 2.1 %collective-permute-start.12 = (bf16[1,2,128,512]{3,2,1,0:T(8,128)(2,1)}, bf16[1,2,128,512]{3,2,1,0:T(8,128)(2,1)S(1)}, u32[]{:S(2)}, u32[]{:S(2)}) collective-permute-start(bf16[1,2,128,512]{3,2,1,0:T(8,128)(2,1)} %collective-permute-done.2.refs_1_), channel_id=1, source_target_pairs={{0,2},{1,3},{2,4},{3,5},{4,6},{5,7},{6,0},{7,1},{8,10},{9,11},{10,... | collective-permute-start | bytes 786440 | tf_op jit(solution)/shard_map/ppermute | solution.py:273
  47.2 5.4 %project.4 = (bf16[2,1024,256]{2,1,0:T(8,128)(2,1)S(1)}, bf16[2,1024,256]{2,1,0:T(8,128)(2,1)S(1)}) custom-call(bf16[512,2048]{1,0:T(8,128)(2,1)S(1)} %attention.3.first_ref, bf16[512,2048]{1,0:T(8,128)(2,1)S(1)} %attention.2.second_ref, bf16[1,2,128,512]{3,2,1,0:T(8,128)(2,1)} %get-tuple-element.105.refs_0_, ...), custom_call_target="tpu_custom_call" | custom-call | flops 3000000000 | bytes 512 | tf_op jit(solution)/shard_map/project/pallas_call | solution.py:212
  52.6 1.6 %collective-permute-start.18 = (bf16[2,1024,256]{2,1,0:T(8,128)(2,1)S(1)}, bf16[2,1024,256]{2,1,0:T(8,128)(2,1)S(1)}, u32[]{:S(2)}, u32[]{:S(2)}) collective-permute-start(bf16[2,1024,256]{2,1,0:T(8,128)(2,1)S(1)} %get-tuple-element.119), channel_id=1, source_target_pairs={{0,8},{1,17},{2,10},{3,19},{4,12},{5,21},{6,14},{7,23},{8,0},{9,25... | collective-permute-start | bytes 3145736 | tf_op jit(solution)/shard_map/ppermute | solution.py:268
  54.2 5.4 %collective-permute-done.11.refs_3_ = bf16[1,2,128,512]{3,2,1,0:T(8,128)(2,1)S(1)} collective-permute-done((bf16[1,2,128,512]{3,2,1,0:T(8,128)(2,1)}, bf16[1,2,128,512]{3,2,1,0:T(8,128)(2,1)S(1)}, u32[]{:S(2)}, u32[]{:S(2)}) %collective-permute-start.11) | collective-permute-done | bytes 262176 | tf_op jit(solution)/shard_map/ppermute | solution.py:273
  59.7 0.7 collective-permute-start.15
  60.5 1.3 collective-permute-start.16
  62.1 5.4 %project.5 = (bf16[2,1024,256]{2,1,0:T(8,128)(2,1)S(1)}, bf16[2,1024,256]{2,1,0:T(8,128)(2,1)S(1)}) custom-call(bf16[512,2048]{1,0:T(8,128)(2,1)S(1)} %attention.3.first_ref, bf16[512,2048]{1,0:T(8,128)(2,1)S(1)} %attention.2.second_ref, bf16[1,2,128,512]{3,2,1,0:T(8,128)(2,1)} %get-tuple-element.121.refs_0_, ...), custom_call_target="tpu_custom_call" | custom-call | flops 3000000000 | bytes 512 | tf_op jit(solution)/shard_map/project/pallas_call | solution.py:212
  67.5 1.6 %collective-permute-start.23 = (bf16[2,1024,256]{2,1,0:T(8,128)(2,1)S(1)}, bf16[2,1024,256]{2,1,0:T(8,128)(2,1)S(1)}, u32[]{:S(2)}, u32[]{:S(2)}) collective-permute-start(bf16[2,1024,256]{2,1,0:T(8,128)(2,1)S(1)} %get-tuple-element.133), channel_id=1, source_target_pairs={{0,8},{1,17},{2,10},{3,19},{4,12},{5,21},{6,14},{7,23},{8,0},{9,25... | collective-permute-start | bytes 3145736 | tf_op jit(solution)/shard_map/ppermute | solution.py:268
  69.2 5.9 %collective-permute-done.16.refs_2_ = bf16[1,2,128,512]{3,2,1,0:T(8,128)(2,1)S(1)} collective-permute-done((bf16[1,2,128,512]{3,2,1,0:T(8,128)(2,1)S(1)}, bf16[1,2,128,512]{3,2,1,0:T(8,128)(2,1)S(1)}, u32[]{:S(2)}, u32[]{:S(2)}) %collective-permute-start.16) | collective-permute-done | bytes 262176 | tf_op jit(solution)/shard_map/ppermute | solution.py:273
  75.1 5.2 %collective-permute-done.17.refs_1_ = bf16[1,2,128,512]{3,2,1,0:T(8,128)(2,1)S(1)} collective-permute-done((bf16[1,2,128,512]{3,2,1,0:T(8,128)(2,1)S(1)}, bf16[1,2,128,512]{3,2,1,0:T(8,128)(2,1)S(1)}, u32[]{:S(2)}, u32[]{:S(2)}) %collective-permute-start.17) | collective-permute-done | bytes 262176 | tf_op jit(solution)/shard_map/ppermute | solution.py:273
  80.4 1.6 %collective-permute-start.24 = (bf16[2,1024,128]{2,1,0:T(8,128)(2,1)S(1)}, bf16[2,1024,128]{2,1,0:T(8,128)(2,1)S(1)}, u32[]{:S(2)}, u32[]{:S(2)}) collective-permute-start(bf16[2,1024,128]{2,1,0:T(8,128)(2,1)S(1)} %add_convert_fusion.3), channel_id=1, source_target_pairs={{0,16},{1,9},{2,18},{3,11},{4,20},{5,13},{6,22},{7,15},{8,24},{9,1... | collective-permute-start | bytes 1572872 | tf_op jit(solution)/shard_map/ppermute | solution.py:268
  82.3 5.2 %project.6 = (bf16[2,1024,256]{2,1,0:T(8,128)(2,1)S(1)}, bf16[2,1024,256]{2,1,0:T(8,128)(2,1)S(1)}) custom-call(bf16[512,2048]{1,0:T(8,128)(2,1)S(1)} %attention.3.first_ref, bf16[512,2048]{1,0:T(8,128)(2,1)S(1)} %attention.2.second_ref, bf16[1,2,128,512]{3,2,1,0:T(8,128)(2,1)S(1)} %copy-done.5, bf16[1,2,128,512]{3,2,1,0:T(8,128)(2,1)S(1)} %collective-permute-done.9.refs_1_, ...), custom_call_target="tpu_custom_call" | custom-call | flops 1500000000 | bytes 512 | tf_op jit(solution)/shard_map/project/pallas_call | solution.py:212
  87.5 3.8 %collective-permute-start.20 = (bf16[1,2,128,512]{3,2,1,0:T(8,128)(2,1)S(1)}, bf16[1,2,128,512]{3,2,1,0:T(8,128)(2,1)S(1)}, u32[]{:S(2)}, u32[]{:S(2)}) collective-permute-start(bf16[1,2,128,512]{3,2,1,0:T(8,128)(2,1)S(1)} %get-tuple-element.153.refs_0_), channel_id=1, source_target_pairs={{0,6},{1,7},{2,0},{3,1},{4,2},{5,3},{6,4},{7,5},{8,14},{9,15},{10,... | collective-permute-start | bytes 786440 | tf_op jit(solution)/shard_map/ppermute | solution.py:273
  91.4 1.4 %collective-permute-start.27 = (bf16[2,1024,128]{2,1,0:T(8,128)(2,1)S(1)}, bf16[2,1024,128]{2,1,0:T(8,128)(2,1)S(1)}, u32[]{:S(2)}, u32[]{:S(2)}) collective-permute-start(bf16[2,1024,128]{2,1,0:T(8,128)(2,1)S(1)} %add_convert_fusion.2), channel_id=1, source_target_pairs={{0,16},{1,9},{2,18},{3,11},{4,20},{5,13},{6,22},{7,15},{8,24},{9,1... | collective-permute-start | bytes 1572872 | tf_op jit(solution)/shard_map/ppermute | solution.py:268
  92.9 0.6 collective-permute-start.30
  93.5 4.2 %collective-permute-done.20.refs_3_ = bf16[1,2,128,512]{3,2,1,0:T(8,128)(2,1)S(1)} collective-permute-done((bf16[1,2,128,512]{3,2,1,0:T(8,128)(2,1)S(1)}, bf16[1,2,128,512]{3,2,1,0:T(8,128)(2,1)S(1)}, u32[]{:S(2)}, u32[]{:S(2)}) %collective-permute-start.20) | collective-permute-done | bytes 262176 | tf_op jit(solution)/shard_map/ppermute | solution.py:273
  97.8 0.5 collective-permute-start.26
  98.2 1.0 collective-permute-done.25.refs_6_
  99.3 0.4 collective-permute-done.26.refs_7_
  99.6 5.2 %project.7 = (bf16[2,1024,256]{2,1,0:T(8,128)(2,1)S(1)}, bf16[2,1024,256]{2,1,0:T(8,128)(2,1)S(1)}) custom-call(bf16[512,2048]{1,0:T(8,128)(2,1)S(1)} %attention.3.first_ref, bf16[512,2048]{1,0:T(8,128)(2,1)S(1)} %attention.2.second_ref, bf16[1,2,128,512]{3,2,1,0:T(8,128)(2,1)S(1)} %get-tuple-element.153.refs_0_, ...), custom_call_target="tpu_custom_call" | custom-call | flops 10000000 | bytes 512 | tf_op jit(solution)/shard_map/project/pallas_call | solution.py:212
  104.9 1.0 collective-permute-done.27.last_ref
  105.9 1.8 %collective-permute-start.28 = (bf16[2,1024,256]{2,1,0:T(8,128)(2,1)S(1)}, bf16[2,1024,256]{2,1,0:T(8,128)(2,1)S(1)}, u32[]{:S(2)}, u32[]{:S(2)}) collective-permute-start(bf16[2,1024,256]{2,1,0:T(8,128)(2,1)S(1)} %get-tuple-element.161), channel_id=1, source_target_pairs={{0,8},{1,17},{2,10},{3,19},{4,12},{5,21},{6,14},{7,23},{8,0},{9,25... | collective-permute-start | bytes 3145736 | tf_op jit(solution)/shard_map/ppermute | solution.py:268
  107.7 3.5 %collective-permute-done.30.received_ref = bf16[2,1024,256]{2,1,0:T(8,128)(2,1)S(1)} collective-permute-done((bf16[2,1024,256]{2,1,0:T(8,128)(2,1)S(1)}, bf16[2,1024,256]{2,1,0:T(8,128)(2,1)S(1)}, u32[]{:S(2)}, u32[]{:S(2)}) %collective-permute-start.30) | collective-permute-done | bytes 1048608 | tf_op jit(solution)/shard_map/ppermute | solution.py:268
  111.3 0.9 collective-permute-start.31
  112.2 15.8 %collective-permute-done.28.received_ref = bf16[2,1024,256]{2,1,0:T(8,128)(2,1)S(1)} collective-permute-done((bf16[2,1024,256]{2,1,0:T(8,128)(2,1)S(1)}, bf16[2,1024,256]{2,1,0:T(8,128)(2,1)S(1)}, u32[]{:S(2)}, u32[]{:S(2)}) %collective-permute-start.28) | collective-permute-done | bytes 1048608 | tf_op jit(solution)/shard_map/ppermute | solution.py:268
  128.2 0.9 collective-permute-start.29
  129.1 1.1 finish.4
  130.2 1.1 finish.5
  131.3 1.1 finish.6
  132.4 5.0 %collective-permute-done.29.last_ref = bf16[2,1024,128]{2,1,0:T(8,128)(2,1)S(1)} collective-permute-done((bf16[2,1024,128]{2,1,0:T(8,128)(2,1)S(1)}, bf16[2,1024,128]{2,1,0:T(8,128)(2,1)S(1)}, u32[]{:S(2)}, u32[]{:S(2)}) %collective-permute-start.29) | collective-permute-done | bytes 524320 | tf_op jit(solution)/shard_map/ppermute | solution.py:268
  137.4 1.1 finish.7
  (67 shorter events, 3.0 us)
Async XLA Ops:
  0.7 1.0 copy-start.2
  1.8 1.0 copy-start.3
  2.8 8.3 %copy-start.6 = (bf16[1024,2,128]{2,1,0:T(2,128)(2,1)S(1)}, bf16[1024,2,128]{2,1,0:T(2,128)(2,1)}, u32[]{:S(2)}) copy-start(bf16[1024,2,128]{2,1,0:T(2,128)(2,1)} %param.9) | copy-start | bytes 1572868
  4.9 6.5 %copy-start.4 = (bf16[1,2,128,512]{3,2,1,0:T(8,128)(2,1)}, bf16[1,2,128,512]{3,2,1,0:T(8,128)(2,1)S(1)}, u32[]{:S(2)}) copy-start(bf16[1,2,128,512]{3,2,1,0:T(8,128)(2,1)S(1)} %get-tuple-element.136.refs_0_) | copy-start | bytes 786436
  4.9 17.4 %collective-permute-start = (bf16[1,2,128,512]{3,2,1,0:T(8,128)(2,1)}, bf16[1,2,128,512]{3,2,1,0:T(8,128)(2,1)}, u32[]{:S(2)}, u32[]{:S(2)}) collective-permute-start(bf16[1,2,128,512]{3,2,1,0:T(8,128)(2,1)} %get-tuple-element.105.refs_0_), channel_id=1, source_target_pairs={{0,6},{1,7},{2,0},{3,1},{4,2},{5,3},{6,4},{7,5},{8,14},{9,15},{10,... | collective-permute-start | bytes 786440 | tf_op jit(solution)/shard_map/ppermute | solution.py:273
  10.0 13.6 %collective-permute-start.1 = (bf16[1,2,128,512]{3,2,1,0:T(8,128)(2,1)}, bf16[1,2,128,512]{3,2,1,0:T(8,128)(2,1)}, u32[]{:S(2)}, u32[]{:S(2)}) collective-permute-start(bf16[1,2,128,512]{3,2,1,0:T(8,128)(2,1)} %get-tuple-element.105.refs_0_), channel_id=1, source_target_pairs={{0,2},{1,3},{2,4},{3,5},{4,6},{5,7},{6,0},{7,1},{8,10},{9,11},{10,... | collective-permute-start | bytes 786440 | tf_op jit(solution)/shard_map/ppermute | solution.py:273
  10.0 18.3 %collective-permute-start.2 = (bf16[1,2,128,512]{3,2,1,0:T(8,128)(2,1)}, bf16[1,2,128,512]{3,2,1,0:T(8,128)(2,1)}, u32[]{:S(2)}, u32[]{:S(2)}) collective-permute-start(bf16[1,2,128,512]{3,2,1,0:T(8,128)(2,1)} %get-tuple-element.121.refs_0_), channel_id=1, source_target_pairs={{0,2},{1,3},{2,4},{3,5},{4,6},{5,7},{6,0},{7,1},{8,10},{9,11},{10,... | collective-permute-start | bytes 786440 | tf_op jit(solution)/shard_map/ppermute | solution.py:273
  10.0 18.3 %collective-permute-start.4 = (bf16[4,2,128,512]{3,2,1,0:T(8,128)(2,1)}, bf16[4,2,128,512]{3,2,1,0:T(8,128)(2,1)}, u32[]{:S(2)}, u32[]{:S(2)}) collective-permute-start(bf16[4,2,128,512]{3,2,1,0:T(8,128)(2,1)} %get-tuple-element.93), channel_id=1, source_target_pairs={{0,1},{1,0},{2,3},{3,2},{4,5},{5,4},{6,7},{7,6},{8,9},{9,8},{10,11... | collective-permute-start | bytes 3145736 | tf_op jit(solution)/shard_map/ppermute | solution.py:277
  11.2 4.1 %copy-start.7 = (s32[64]{0:T(128)S(1)}, s32[64]{0:T(128)}, u32[]{:S(2)}) copy-start(s32[64]{0:T(128)} %param.11) | copy-start | bytes 772
  11.3 4.7 %copy-start = (bf16[1024,1024]{1,0:T(8,128)(2,1)S(1)}, bf16[1024,1024]{1,0:T(8,128)(2,1)}, u32[]{:S(2)}) copy-start(bf16[1024,1024]{1,0:T(8,128)(2,1)} %q_ref.3) | copy-start | bytes 6291460
  12.2 10.1 %collective-permute-start.3 = (bf16[224,512]{1,0:T(8,128)(2,1)}, bf16[224,512]{1,0:T(8,128)(2,1)}, u32[]{:S(2)}, u32[]{:S(2)}) collective-permute-start(bf16[224,512]{1,0:T(8,128)(2,1)} %slice.60), channel_id=1, source_target_pairs={{0,1},{1,2},{2,3},{3,4},{4,5},{5,6},{6,7},{8,9},{9,10},{10,11},{11... | collective-permute-start | bytes 688136 | tf_op jit(solution)/shard_map/ppermute | solution.py:351
  16.1 1.6 %copy-start.1 = (bf16[1024,1024]{1,0:T(8,128)(2,1)S(1)}, bf16[1024,1024]{1,0:T(8,128)(2,1)}, u32[]{:S(2)}) copy-start(bf16[1024,1024]{1,0:T(8,128)(2,1)} %qt_ref.3) | copy-start | bytes 6291460
  17.6 15.0 %copy-start.5 = (bf16[1,2,128,512]{3,2,1,0:T(8,128)(2,1)S(1)}, bf16[1,2,128,512]{3,2,1,0:T(8,128)(2,1)}, u32[]{:S(2)}) copy-start(bf16[1,2,128,512]{3,2,1,0:T(8,128)(2,1)} %copy-done.4) | copy-start | bytes 786436
  28.3 11.1 %collective-permute-start.5 = (bf16[1,2,128,512]{3,2,1,0:T(8,128)(2,1)}, bf16[1,2,128,512]{3,2,1,0:T(8,128)(2,1)S(1)}, u32[]{:S(2)}, u32[]{:S(2)}) collective-permute-start(bf16[1,2,128,512]{3,2,1,0:T(8,128)(2,1)} %collective-permute-done.1.refs_1_), channel_id=1, source_target_pairs={{0,2},{1,3},{2,4},{3,5},{4,6},{5,7},{6,0},{7,1},{8,10},{9,11},{10,... | collective-permute-start | bytes 786440 | tf_op jit(solution)/shard_map/ppermute | solution.py:273
  32.2 7.2 %collective-permute-start.7 = (bf16[1,2,128,512]{3,2,1,0:T(8,128)(2,1)}, bf16[1,2,128,512]{3,2,1,0:T(8,128)(2,1)S(1)}, u32[]{:S(2)}, u32[]{:S(2)}) collective-permute-start(bf16[1,2,128,512]{3,2,1,0:T(8,128)(2,1)} %collective-permute-done.1.refs_1_), channel_id=1, source_target_pairs={{0,1},{1,0},{2,3},{3,2},{4,5},{5,4},{6,7},{7,6},{8,9},{9,8},{10,11... | collective-permute-start | bytes 786440 | tf_op jit(solution)/shard_map/ppermute | solution.py:277
  32.2 7.2 %collective-permute-start.6 = (bf16[1,2,128,512]{3,2,1,0:T(8,128)(2,1)}, bf16[1,2,128,512]{3,2,1,0:T(8,128)(2,1)S(1)}, u32[]{:S(2)}, u32[]{:S(2)}) collective-permute-start(bf16[1,2,128,512]{3,2,1,0:T(8,128)(2,1)} %collective-permute-done.refs_3_), channel_id=1, source_target_pairs={{0,1},{1,0},{2,3},{3,2},{4,5},{5,4},{6,7},{7,6},{8,9},{9,8},{10,11... | collective-permute-start | bytes 786440 | tf_op jit(solution)/shard_map/ppermute | solution.py:277
  32.7 6.7 %collective-permute-start.8 = (bf16[1,2,128,512]{3,2,1,0:T(8,128)(2,1)}, bf16[1,2,128,512]{3,2,1,0:T(8,128)(2,1)S(1)}, u32[]{:S(2)}, u32[]{:S(2)}) collective-permute-start(bf16[1,2,128,512]{3,2,1,0:T(8,128)(2,1)} %collective-permute-done.2.refs_1_), channel_id=1, source_target_pairs={{0,1},{1,0},{2,3},{3,2},{4,5},{5,4},{6,7},{7,6},{8,9},{9,8},{10,11... | collective-permute-start | bytes 786440 | tf_op jit(solution)/shard_map/ppermute | solution.py:277
  32.7 12.3 %collective-permute-start.9 = (bf16[1,2,128,512]{3,2,1,0:T(8,128)(2,1)S(1)}, bf16[1,2,128,512]{3,2,1,0:T(8,128)(2,1)S(1)}, u32[]{:S(2)}, u32[]{:S(2)}) collective-permute-start(bf16[1,2,128,512]{3,2,1,0:T(8,128)(2,1)S(1)} %copy-done.5), channel_id=1, source_target_pairs={{0,2},{1,3},{2,4},{3,5},{4,6},{5,7},{6,0},{7,1},{8,10},{9,11},{10,... | collective-permute-start | bytes 786440 | tf_op jit(solution)/shard_map/ppermute | solution.py:273
  45.0 2.2 %collective-permute-start.10 = (bf16[1,2,128,512]{3,2,1,0:T(8,128)(2,1)S(1)}, bf16[1,2,128,512]{3,2,1,0:T(8,128)(2,1)S(1)}, u32[]{:S(2)}, u32[]{:S(2)}) collective-permute-start(bf16[1,2,128,512]{3,2,1,0:T(8,128)(2,1)S(1)} %collective-permute-done.5.refs_2_), channel_id=1, source_target_pairs={{0,1},{1,0},{2,3},{3,2},{4,5},{5,4},{6,7},{7,6},{8,9},{9,8},{10,11... | collective-permute-start | bytes 786440 | tf_op jit(solution)/shard_map/ppermute | solution.py:277
  45.1 14.4 %collective-permute-start.11 = (bf16[1,2,128,512]{3,2,1,0:T(8,128)(2,1)}, bf16[1,2,128,512]{3,2,1,0:T(8,128)(2,1)S(1)}, u32[]{:S(2)}, u32[]{:S(2)}) collective-permute-start(bf16[1,2,128,512]{3,2,1,0:T(8,128)(2,1)} %get-tuple-element.121.refs_0_), channel_id=1, source_target_pairs={{0,6},{1,7},{2,0},{3,1},{4,2},{5,3},{6,4},{7,5},{8,14},{9,15},{10,... | collective-permute-start | bytes 786440 | tf_op jit(solution)/shard_map/ppermute | solution.py:273
  45.1 14.4 %collective-permute-start.12 = (bf16[1,2,128,512]{3,2,1,0:T(8,128)(2,1)}, bf16[1,2,128,512]{3,2,1,0:T(8,128)(2,1)S(1)}, u32[]{:S(2)}, u32[]{:S(2)}) collective-permute-start(bf16[1,2,128,512]{3,2,1,0:T(8,128)(2,1)} %collective-permute-done.2.refs_1_), channel_id=1, source_target_pairs={{0,2},{1,3},{2,4},{3,5},{4,6},{5,7},{6,0},{7,1},{8,10},{9,11},{10,... | collective-permute-start | bytes 786440 | tf_op jit(solution)/shard_map/ppermute | solution.py:273
  47.2 12.4 %collective-permute-start.13 = (bf16[1,2,128,512]{3,2,1,0:T(8,128)(2,1)S(1)}, bf16[1,2,128,512]{3,2,1,0:T(8,128)(2,1)S(1)}, u32[]{:S(2)}, u32[]{:S(2)}) collective-permute-start(bf16[1,2,128,512]{3,2,1,0:T(8,128)(2,1)S(1)} %collective-permute-done.9.refs_1_), channel_id=1, source_target_pairs={{0,1},{1,0},{2,3},{3,2},{4,5},{5,4},{6,7},{7,6},{8,9},{9,8},{10,11... | collective-permute-start | bytes 786440 | tf_op jit(solution)/shard_map/ppermute | solution.py:277
  52.6 16.4 %collective-permute-start.18 = (bf16[2,1024,256]{2,1,0:T(8,128)(2,1)S(1)}, bf16[2,1024,256]{2,1,0:T(8,128)(2,1)S(1)}, u32[]{:S(2)}, u32[]{:S(2)}) collective-permute-start(bf16[2,1024,256]{2,1,0:T(8,128)(2,1)S(1)} %get-tuple-element.119), channel_id=1, source_target_pairs={{0,8},{1,17},{2,10},{3,19},{4,12},{5,21},{6,14},{7,23},{8,0},{9,25... | collective-permute-start | bytes 3145736 | tf_op jit(solution)/shard_map/ppermute | solution.py:268
  59.6 2.5 %collective-permute-start.14 = (bf16[2,2,128,512]{3,2,1,0:T(8,128)(2,1)S(1)}, bf16[2,2,128,512]{3,2,1,0:T(8,128)(2,1)S(1)}, u32[]{:S(2)}, u32[]{:S(2)}) collective-permute-start(bf16[2,2,128,512]{3,2,1,0:T(8,128)(2,1)S(1)} %pad_maximum_fusion.2), channel_id=1, source_target_pairs={{0,1},{1,0},{2,3},{3,2},{4,5},{5,4},{6,7},{7,6},{8,9},{9,8},{10,11... | collective-permute-start | bytes 1572872 | tf_op jit(solution)/shard_map/ppermute | solution.py:277
  59.7 9.5 %collective-permute-start.15 = (bf16[1,2,128,512]{3,2,1,0:T(8,128)(2,1)S(1)}, bf16[1,2,128,512]{3,2,1,0:T(8,128)(2,1)S(1)}, u32[]{:S(2)}, u32[]{:S(2)}) collective-permute-start(bf16[1,2,128,512]{3,2,1,0:T(8,128)(2,1)S(1)} %copy-done.5), channel_id=1, source_target_pairs={{0,6},{1,7},{2,0},{3,1},{4,2},{5,3},{6,4},{7,5},{8,14},{9,15},{10,... | collective-permute-start | bytes 786440 | tf_op jit(solution)/shard_map/ppermute | solution.py:273
  60.5 14.6 %collective-permute-start.16 = (bf16[1,2,128,512]{3,2,1,0:T(8,128)(2,1)S(1)}, bf16[1,2,128,512]{3,2,1,0:T(8,128)(2,1)S(1)}, u32[]{:S(2)}, u32[]{:S(2)}) collective-permute-start(bf16[1,2,128,512]{3,2,1,0:T(8,128)(2,1)S(1)} %collective-permute-done.9.refs_1_), channel_id=1, source_target_pairs={{0,2},{1,3},{2,4},{3,5},{4,6},{5,7},{6,0},{7,1},{8,10},{9,11},{10,... | collective-permute-start | bytes 786440 | tf_op jit(solution)/shard_map/ppermute | solution.py:273
  61.8 18.5 %collective-permute-start.17 = (bf16[1,2,128,512]{3,2,1,0:T(8,128)(2,1)S(1)}, bf16[1,2,128,512]{3,2,1,0:T(8,128)(2,1)S(1)}, u32[]{:S(2)}, u32[]{:S(2)}) collective-permute-start(bf16[1,2,128,512]{3,2,1,0:T(8,128)(2,1)S(1)} %get-tuple-element.153.refs_0_), channel_id=1, source_target_pairs={{0,2},{1,3},{2,4},{3,5},{4,6},{5,7},{6,0},{7,1},{8,10},{9,11},{10,... | collective-permute-start | bytes 786440 | tf_op jit(solution)/shard_map/ppermute | solution.py:273
  67.5 23.8 %collective-permute-start.23 = (bf16[2,1024,256]{2,1,0:T(8,128)(2,1)S(1)}, bf16[2,1024,256]{2,1,0:T(8,128)(2,1)S(1)}, u32[]{:S(2)}, u32[]{:S(2)}) collective-permute-start(bf16[2,1024,256]{2,1,0:T(8,128)(2,1)S(1)} %get-tuple-element.133), channel_id=1, source_target_pairs={{0,8},{1,17},{2,10},{3,19},{4,12},{5,21},{6,14},{7,23},{8,0},{9,25... | collective-permute-start | bytes 3145736 | tf_op jit(solution)/shard_map/ppermute | solution.py:268
  80.3 2.0 %collective-permute-start.19 = (bf16[2,2,128,512]{3,2,1,0:T(8,128)(2,1)S(1)}, bf16[2,2,128,512]{3,2,1,0:T(8,128)(2,1)S(1)}, u32[]{:S(2)}, u32[]{:S(2)}) collective-permute-start(bf16[2,2,128,512]{3,2,1,0:T(8,128)(2,1)S(1)} %pad_maximum_fusion.3), channel_id=1, source_target_pairs={{0,1},{1,0},{2,3},{3,2},{4,5},{5,4},{6,7},{7,6},{8,9},{9,8},{10,11... | collective-permute-start | bytes 1572872 | tf_op jit(solution)/shard_map/ppermute | solution.py:277
  80.4 10.9 %collective-permute-start.24 = (bf16[2,1024,128]{2,1,0:T(8,128)(2,1)S(1)}, bf16[2,1024,128]{2,1,0:T(8,128)(2,1)S(1)}, u32[]{:S(2)}, u32[]{:S(2)}) collective-permute-start(bf16[2,1024,128]{2,1,0:T(8,128)(2,1)S(1)} %add_convert_fusion.3), channel_id=1, source_target_pairs={{0,16},{1,9},{2,18},{3,11},{4,20},{5,13},{6,22},{7,15},{8,24},{9,1... | collective-permute-start | bytes 1572872 | tf_op jit(solution)/shard_map/ppermute | solution.py:268
  82.0 11.5 %collective-permute-start.21 = (bf16[1,2,128,512]{3,2,1,0:T(8,128)(2,1)S(1)}, bf16[1,2,128,512]{3,2,1,0:T(8,128)(2,1)S(1)}, u32[]{:S(2)}, u32[]{:S(2)}) collective-permute-start(bf16[1,2,128,512]{3,2,1,0:T(8,128)(2,1)S(1)} %collective-permute-done.17.refs_1_), channel_id=1, source_target_pairs={{0,2},{1,3},{2,4},{3,5},{4,6},{5,7},{6,0},{7,1},{8,10},{9,11},{10,... | collective-permute-start | bytes 786440 | tf_op jit(solution)/shard_map/ppermute | solution.py:273
  82.1 11.4 %collective-permute-start.22 = (bf16[1,2,128,512]{3,2,1,0:T(8,128)(2,1)S(1)}, bf16[1,2,128,512]{3,2,1,0:T(8,128)(2,1)S(1)}, u32[]{:S(2)}, u32[]{:S(2)}) collective-permute-start(bf16[1,2,128,512]{3,2,1,0:T(8,128)(2,1)S(1)} %collective-permute-done.17.refs_1_), channel_id=1, source_target_pairs={{0,1},{1,0},{2,3},{3,2},{4,5},{5,4},{6,7},{7,6},{8,9},{9,8},{10,11... | collective-permute-start | bytes 786440 | tf_op jit(solution)/shard_map/ppermute | solution.py:277
  87.5 10.2 %collective-permute-start.20 = (bf16[1,2,128,512]{3,2,1,0:T(8,128)(2,1)S(1)}, bf16[1,2,128,512]{3,2,1,0:T(8,128)(2,1)S(1)}, u32[]{:S(2)}, u32[]{:S(2)}) collective-permute-start(bf16[1,2,128,512]{3,2,1,0:T(8,128)(2,1)S(1)} %get-tuple-element.153.refs_0_), channel_id=1, source_target_pairs={{0,6},{1,7},{2,0},{3,1},{4,2},{5,3},{6,4},{7,5},{8,14},{9,15},{10,... | collective-permute-start | bytes 786440 | tf_op jit(solution)/shard_map/ppermute | solution.py:273
  91.4 14.5 %collective-permute-start.27 = (bf16[2,1024,128]{2,1,0:T(8,128)(2,1)S(1)}, bf16[2,1024,128]{2,1,0:T(8,128)(2,1)S(1)}, u32[]{:S(2)}, u32[]{:S(2)}) collective-permute-start(bf16[2,1024,128]{2,1,0:T(8,128)(2,1)S(1)} %add_convert_fusion.2), channel_id=1, source_target_pairs={{0,16},{1,9},{2,18},{3,11},{4,20},{5,13},{6,22},{7,15},{8,24},{9,1... | collective-permute-start | bytes 1572872 | tf_op jit(solution)/shard_map/ppermute | solution.py:268
  92.9 18.3 %collective-permute-start.30 = (bf16[2,1024,256]{2,1,0:T(8,128)(2,1)S(1)}, bf16[2,1024,256]{2,1,0:T(8,128)(2,1)S(1)}, u32[]{:S(2)}, u32[]{:S(2)}) collective-permute-start(bf16[2,1024,256]{2,1,0:T(8,128)(2,1)S(1)} %get-tuple-element.149), channel_id=1, source_target_pairs={{0,8},{1,17},{2,10},{3,19},{4,12},{5,21},{6,14},{7,23},{8,0},{9,25... | collective-permute-start | bytes 3145736 | tf_op jit(solution)/shard_map/ppermute | solution.py:268
  97.7 1.5 %collective-permute-start.25 = (bf16[1,2,128,512]{3,2,1,0:T(8,128)(2,1)S(1)}, bf16[1,2,128,512]{3,2,1,0:T(8,128)(2,1)S(1)}, u32[]{:S(2)}, u32[]{:S(2)}) collective-permute-start(bf16[1,2,128,512]{3,2,1,0:T(8,128)(2,1)S(1)} %collective-permute-done.21.refs_2_), channel_id=1, source_target_pairs={{0,1},{1,0},{2,3},{3,2},{4,5},{5,4},{6,7},{7,6},{8,9},{9,8},{10,11... | collective-permute-start | bytes 786440 | tf_op jit(solution)/shard_map/ppermute | solution.py:277
  97.8 1.9 %collective-permute-start.26 = (bf16[1,2,128,512]{3,2,1,0:T(8,128)(2,1)S(1)}, bf16[1,2,128,512]{3,2,1,0:T(8,128)(2,1)S(1)}, u32[]{:S(2)}, u32[]{:S(2)}) collective-permute-start(bf16[1,2,128,512]{3,2,1,0:T(8,128)(2,1)S(1)} %collective-permute-done.20.refs_3_), channel_id=1, source_target_pairs={{0,1},{1,0},{2,3},{3,2},{4,5},{5,4},{6,7},{7,6},{8,9},{9,8},{10,11... | collective-permute-start | bytes 786440 | tf_op jit(solution)/shard_map/ppermute | solution.py:277
  105.9 22.1 %collective-permute-start.28 = (bf16[2,1024,256]{2,1,0:T(8,128)(2,1)S(1)}, bf16[2,1024,256]{2,1,0:T(8,128)(2,1)S(1)}, u32[]{:S(2)}, u32[]{:S(2)}) collective-permute-start(bf16[2,1024,256]{2,1,0:T(8,128)(2,1)S(1)} %get-tuple-element.161), channel_id=1, source_target_pairs={{0,8},{1,17},{2,10},{3,19},{4,12},{5,21},{6,14},{7,23},{8,0},{9,25... | collective-permute-start | bytes 3145736 | tf_op jit(solution)/shard_map/ppermute | solution.py:268
  111.3 20.0 %collective-permute-start.31 = (bf16[2,1024,128]{2,1,0:T(8,128)(2,1)S(1)}, bf16[2,1024,128]{2,1,0:T(8,128)(2,1)S(1)}, u32[]{:S(2)}, u32[]{:S(2)}) collective-permute-start(bf16[2,1024,128]{2,1,0:T(8,128)(2,1)S(1)} %add_convert_fusion), channel_id=1, source_target_pairs={{0,16},{1,9},{2,18},{3,11},{4,20},{5,13},{6,22},{7,15},{8,24},{9,1... | collective-permute-start | bytes 1572872 | tf_op jit(solution)/shard_map/ppermute | solution.py:268
  128.2 9.2 %collective-permute-start.29 = (bf16[2,1024,128]{2,1,0:T(8,128)(2,1)S(1)}, bf16[2,1024,128]{2,1,0:T(8,128)(2,1)S(1)}, u32[]{:S(2)}, u32[]{:S(2)}) collective-permute-start(bf16[2,1024,128]{2,1,0:T(8,128)(2,1)S(1)} %add_convert_fusion.1), channel_id=1, source_target_pairs={{0,16},{1,9},{2,18},{3,11},{4,20},{5,13},{6,22},{7,15},{8,24},{9,1... | collective-permute-start | bytes 1572872 | tf_op jit(solution)/shard_map/ppermute | solution.py:268

commit v13 on v12

--- a/solution.py
+++ b/solution.py
@@ -57,7 +57,7 @@
         out_shape=shapes,
         scratch_shapes=[pltpu.VMEM(value.shape, value.dtype)] * 2
         + [pltpu.SemaphoreType.DMA((2,))],
-        compiler_params=pltpu.CompilerParams(vmem_limit_bytes=vmem_bytes),
+        compiler_params=pltpu.CompilerParams(vmem_limit_bytes=5 * vmem_bytes),
         name="arrange",
     )(owners, tangent, value)
 

time: 139 us -> 139 us (level)
  local copies, waits for them, and re-layouts: 6 us -> 3.9 us
    unnamed x16, local copies, waits for them, and re-layouts: 3.69 us -> 1.62 us
    pallas_call x1, Pallas kernels: 2.06 us -> 3.48 us  [arrange(): pl.pallas_call(arrange_kernel, in_specs=[pl.BlockSpec(memory_space=pltpu....]
  transfers between devices with their start and end apart: 32 -> 32, of which waited for: 15 -> 15; matrix products, arithmetic and copies ran while one was open for 3% -> 3% of each run, Pallas kernels for 25% -> 24%
where the time goes in v13:
time: 139 us; the launch traced here: 138 us
  waiting for transfers between devices  59.8 us (43%)
  Pallas kernels  38.4 us (28%)
  starting transfers between devices  32.3 us (23%)
  local copies, waits for them, and re-layouts  3.9 us (3%)
  other arithmetic  2.82 us (2%)
    ppermute x12, waiting for transfers between devices, along(): lax.ppermute(block, 'seq', [(i, (i + CORES * chips) % size) for i in rang...  32.9 us
    ppermute x8, waiting for transfers between devices, across(): return lax.ppermute(block, ('kv', 'seq'), route)  25.3 us
    pallas_call x4, Pallas kernels, project(): pl.pallas_call(functools.partial(project_kernel, indices), grid=(2 * step...  21.1 us
    ppermute x12, starting transfers between devices, along(): lax.ppermute(block, 'seq', [(i, (i + CORES * chips) % size) for i in rang...  17.5 us
    ppermute x8, starting transfers between devices, across(): return lax.ppermute(block, ('kv', 'seq'), route)  10.4 us
    pallas_call x2, Pallas kernels, attention(): pl.pallas_call(functools.partial(attention_kernel, heads, head_dim, offse...  9.39 us
    pallas_call x4, Pallas kernels, finish(): pl.pallas_call(finish_kernel, grid=(tokens // tile,), in_specs=[pl.BlockS...  4.45 us
    pallas_call x1, Pallas kernels, arrange(): pl.pallas_call(arrange_kernel, in_specs=[pl.BlockSpec(memory_space=pltpu....  3.48 us
  transfers between devices with their start and end apart: 32, of which 15 were waited for; matrix products, arithmetic and copies ran while one was open for 3% of the time, Pallas kernels for 24%

profile of v13, /device:TPU:0, one launch (start us, length us, event | category | flops | bytes accessed | tf_op | source)
XLA Modules:
  0.0 138.2 jit_solution(18271169734779783013)
XLA Ops:
  0.7 0.6 add_xor_fusion.owner_ref
  1.3 3.5 %arrange.1 = (bf16[4,2,128,512]{3,2,1,0:T(8,128)(2,1)}, bf16[1,2,128,512]{3,2,1,0:T(8,128)(2,1)}, bf16[1,2,128,512]{3,2,1,0:T(8,128)(2,1)}, bf16[1,2,128,512]{3,2,1,0:T(8,128)(2,1)}, bf16[1,2,128,512]{3,2,1,0:T(8,128)(2,1)}) custom-call(s32[4]{0:T(128)} %add_xor_fusion.owner_ref, bf16[128,2048]{1,0:T(8,128)(2,1)} %tangent_hbm.1, bf16[128,2048]{1,0:T(8,128)(2,1)} %value_hbm.1), custom_call_target="tpu_custom_call" | custom-call | tf_op jit(solution)/shard_map/arrange/pallas_call | solution.py:52
  4.8 5.1 %collective-permute-start = (bf16[1,2,128,512]{3,2,1,0:T(8,128)(2,1)}, bf16[1,2,128,512]{3,2,1,0:T(8,128)(2,1)}, u32[]{:S(2)}, u32[]{:S(2)}) collective-permute-start(bf16[1,2,128,512]{3,2,1,0:T(8,128)(2,1)} %get-tuple-element.105.refs_0_), channel_id=1, source_target_pairs={{0,6},{1,7},{2,0},{3,1},{4,2},{5,3},{6,4},{7,5},{8,14},{9,15},{10,... | collective-permute-start | bytes 786440 | tf_op jit(solution)/shard_map/ppermute | solution.py:273
  9.9 1.1 copy.26
  11.3 0.7 slice.60
  12.0 3.1 %collective-permute-start.3 = (bf16[224,512]{1,0:T(8,128)(2,1)}, bf16[224,512]{1,0:T(8,128)(2,1)}, u32[]{:S(2)}, u32[]{:S(2)}) collective-permute-start(bf16[224,512]{1,0:T(8,128)(2,1)} %slice.60), channel_id=1, source_target_pairs={{0,1},{1,2},{2,3},{3,4},{4,5},{5,6},{6,7},{8,9},{9,10},{10,11},{11... | collective-permute-start | bytes 688136 | tf_op jit(solution)/shard_map/ppermute | solution.py:351
  15.9 1.6 %copy-done.1 = bf16[1024,1024]{1,0:T(8,128)(2,1)S(1)} copy-done((bf16[1024,1024]{1,0:T(8,128)(2,1)S(1)}, bf16[1024,1024]{1,0:T(8,128)(2,1)}, u32[]{:S(2)}) %copy-start.1) | copy-done | bytes 2097176
  17.5 4.6 %attention.2.second_ref = bf16[512,2048]{1,0:T(8,128)(2,1)S(1)} custom-call(s32[8]{0:T(128)S(1)} %pad_add_fusion.order_ref, bf16[1024,1024]{1,0:T(8,128)(2,1)S(1)} %copy-done, bf16[1024,1024]{1,0:T(8,128)(2,1)S(1)} %copy-done.1, bf16[1024,512]{1,0:T(8,128)(2,1)S(1)} %pad_maximum_fusion.ctx_ref, s32[1024,128]{1,0:T(8,128)S(1)} %broadcast_in_dim.13.low_ref), custom_call_target="tpu_custom_call" | custom-call | flops 1048576 | bytes 512 | tf_op jit(solution)/shard_map/attention/pallas_call | solution.py:138
  22.1 1.3 collective-permute-done.1.refs_1_
  23.4 4.7 %collective-permute-done.2.refs_1_ = bf16[1,2,128,512]{3,2,1,0:T(8,128)(2,1)S(1)} collective-permute-done((bf16[1,2,128,512]{3,2,1,0:T(8,128)(2,1)}, bf16[1,2,128,512]{3,2,1,0:T(8,128)(2,1)S(1)}, u32[]{:S(2)}, u32[]{:S(2)}) %collective-permute-start.2) | collective-permute-done | bytes 262176 | tf_op jit(solution)/shard_map/ppermute | solution.py:273
  28.1 3.9 %collective-permute-start.5 = (bf16[1,2,128,512]{3,2,1,0:T(8,128)(2,1)}, bf16[1,2,128,512]{3,2,1,0:T(8,128)(2,1)S(1)}, u32[]{:S(2)}, u32[]{:S(2)}) collective-permute-start(bf16[1,2,128,512]{3,2,1,0:T(8,128)(2,1)} %collective-permute-done.1.refs_1_), channel_id=1, source_target_pairs={{0,2},{1,3},{2,4},{3,5},{4,6},{5,7},{6,0},{7,1},{8,10},{9,11},{10,... | collective-permute-start | bytes 786440 | tf_op jit(solution)/shard_map/ppermute | solution.py:273
  32.0 0.5 collective-permute-start.6
  32.7 1.0 pad_maximum_fusion.1.ctx_ref
  33.8 4.8 %attention.3.first_ref = bf16[512,2048]{1,0:T(8,128)(2,1)S(1)} custom-call(s32[8]{0:T(128)S(1)} %pad_add_fusion.order_ref, bf16[1024,1024]{1,0:T(8,128)(2,1)S(1)} %copy-done, bf16[1024,1024]{1,0:T(8,128)(2,1)S(1)} %copy-done.1, bf16[736,512]{1,0:T(8,128)(2,1)S(1)} %pad_maximum_fusion.1.ctx_ref, s32[1024,128]{1,0:T(8,128)S(1)} %broadcast_in_dim.13.low_ref), custom_call_target="tpu_custom_call" | custom-call | flops 1048576 | bytes 512 | tf_op jit(solution)/shard_map/attention/pallas_call | solution.py:138
  38.5 0.7 collective-permute-done.5.refs_2_
  39.3 5.6 %collective-permute-done.9.refs_1_ = bf16[1,2,128,512]{3,2,1,0:T(8,128)(2,1)S(1)} collective-permute-done((bf16[1,2,128,512]{3,2,1,0:T(8,128)(2,1)S(1)}, bf16[1,2,128,512]{3,2,1,0:T(8,128)(2,1)S(1)}, u32[]{:S(2)}, u32[]{:S(2)}) %collective-permute-start.9) | collective-permute-done | bytes 262176 | tf_op jit(solution)/shard_map/ppermute | solution.py:273
  45.0 2.1 %collective-permute-start.12 = (bf16[1,2,128,512]{3,2,1,0:T(8,128)(2,1)S(1)}, bf16[1,2,128,512]{3,2,1,0:T(8,128)(2,1)S(1)}, u32[]{:S(2)}, u32[]{:S(2)}) collective-permute-start(bf16[1,2,128,512]{3,2,1,0:T(8,128)(2,1)S(1)} %collective-permute-done.2.refs_1_), channel_id=1, source_target_pairs={{0,2},{1,3},{2,4},{3,5},{4,6},{5,7},{6,0},{7,1},{8,10},{9,11},{10,... | collective-permute-start | bytes 786440 | tf_op jit(solution)/shard_map/ppermute | solution.py:273
  47.1 5.4 %project.4 = (bf16[2,1024,256]{2,1,0:T(8,128)(2,1)S(1)}, bf16[2,1024,256]{2,1,0:T(8,128)(2,1)S(1)}) custom-call(bf16[512,2048]{1,0:T(8,128)(2,1)S(1)} %attention.3.first_ref, bf16[512,2048]{1,0:T(8,128)(2,1)S(1)} %attention.2.second_ref, bf16[1,2,128,512]{3,2,1,0:T(8,128)(2,1)S(1)} %copy-done.5, bf16[1,2,128,512]{3,2,1,0:T(8,128)(2,1)} %collective-permute-done.1.refs_1_, ...), custom_call_target="tpu_custom_call" | custom-call | flops 3000000000 | bytes 512 | tf_op jit(solution)/shard_map/project/pallas_call | solution.py:212
  52.5 1.6 %collective-permute-start.18 = (bf16[2,1024,256]{2,1,0:T(8,128)(2,1)S(1)}, bf16[2,1024,256]{2,1,0:T(8,128)(2,1)S(1)}, u32[]{:S(2)}, u32[]{:S(2)}) collective-permute-start(bf16[2,1024,256]{2,1,0:T(8,128)(2,1)S(1)} %get-tuple-element.119), channel_id=1, source_target_pairs={{0,8},{1,17},{2,10},{3,19},{4,12},{5,21},{6,14},{7,23},{8,0},{9,25... | collective-permute-start | bytes 3145736 | tf_op jit(solution)/shard_map/ppermute | solution.py:268
  54.0 5.2 %collective-permute-done.11.refs_3_ = bf16[1,2,128,512]{3,2,1,0:T(8,128)(2,1)S(1)} collective-permute-done((bf16[1,2,128,512]{3,2,1,0:T(8,128)(2,1)S(1)}, bf16[1,2,128,512]{3,2,1,0:T(8,128)(2,1)S(1)}, u32[]{:S(2)}, u32[]{:S(2)}) %collective-permute-start.11) | collective-permute-done | bytes 262176 | tf_op jit(solution)/shard_map/ppermute | solution.py:273
  59.4 0.7 collective-permute-start.15
  60.1 1.3 collective-permute-start.16
  61.4 0.3 collective-permute-start.17
  61.8 5.2 %project.5 = (bf16[2,1024,256]{2,1,0:T(8,128)(2,1)S(1)}, bf16[2,1024,256]{2,1,0:T(8,128)(2,1)S(1)}) custom-call(bf16[512,2048]{1,0:T(8,128)(2,1)S(1)} %attention.3.first_ref, bf16[512,2048]{1,0:T(8,128)(2,1)S(1)} %attention.2.second_ref, bf16[1,2,128,512]{3,2,1,0:T(8,128)(2,1)S(1)} %copy-done.4, bf16[1,2,128,512]{3,2,1,0:T(8,128)(2,1)S(1)} %collective-permute-done.2.refs_1_, ...), custom_call_target="tpu_custom_call" | custom-call | flops 3000000000 | bytes 512 | tf_op jit(solution)/shard_map/project/pallas_call | solution.py:212
  67.0 1.6 %collective-permute-start.23 = (bf16[2,1024,256]{2,1,0:T(8,128)(2,1)S(1)}, bf16[2,1024,256]{2,1,0:T(8,128)(2,1)S(1)}, u32[]{:S(2)}, u32[]{:S(2)}) collective-permute-start(bf16[2,1024,256]{2,1,0:T(8,128)(2,1)S(1)} %get-tuple-element.133), channel_id=1, source_target_pairs={{0,8},{1,17},{2,10},{3,19},{4,12},{5,21},{6,14},{7,23},{8,0},{9,25... | collective-permute-start | bytes 3145736 | tf_op jit(solution)/shard_map/ppermute | solution.py:268
  68.7 6.0 %collective-permute-done.16.refs_2_ = bf16[1,2,128,512]{3,2,1,0:T(8,128)(2,1)S(1)} collective-permute-done((bf16[1,2,128,512]{3,2,1,0:T(8,128)(2,1)S(1)}, bf16[1,2,128,512]{3,2,1,0:T(8,128)(2,1)S(1)}, u32[]{:S(2)}, u32[]{:S(2)}) %collective-permute-start.16) | collective-permute-done | bytes 262176 | tf_op jit(solution)/shard_map/ppermute | solution.py:273
  74.8 5.2 %collective-permute-done.17.refs_1_ = bf16[1,2,128,512]{3,2,1,0:T(8,128)(2,1)S(1)} collective-permute-done((bf16[1,2,128,512]{3,2,1,0:T(8,128)(2,1)S(1)}, bf16[1,2,128,512]{3,2,1,0:T(8,128)(2,1)S(1)}, u32[]{:S(2)}, u32[]{:S(2)}) %collective-permute-start.17) | collective-permute-done | bytes 262176 | tf_op jit(solution)/shard_map/ppermute | solution.py:273
  80.1 1.6 %collective-permute-start.24 = (bf16[2,1024,128]{2,1,0:T(8,128)(2,1)S(1)}, bf16[2,1024,128]{2,1,0:T(8,128)(2,1)S(1)}, u32[]{:S(2)}, u32[]{:S(2)}) collective-permute-start(bf16[2,1024,128]{2,1,0:T(8,128)(2,1)S(1)} %add_convert_fusion.3), channel_id=1, source_target_pairs={{0,16},{1,9},{2,18},{3,11},{4,20},{5,13},{6,22},{7,15},{8,24},{9,1... | collective-permute-start | bytes 1572872 | tf_op jit(solution)/shard_map/ppermute | solution.py:268
  81.9 5.2 %project.6 = (bf16[2,1024,256]{2,1,0:T(8,128)(2,1)S(1)}, bf16[2,1024,256]{2,1,0:T(8,128)(2,1)S(1)}) custom-call(bf16[512,2048]{1,0:T(8,128)(2,1)S(1)} %attention.3.first_ref, bf16[512,2048]{1,0:T(8,128)(2,1)S(1)} %attention.2.second_ref, bf16[1,2,128,512]{3,2,1,0:T(8,128)(2,1)S(1)} %copy-done.3, bf16[1,2,128,512]{3,2,1,0:T(8,128)(2,1)S(1)} %collective-permute-done.9.refs_1_, ...), custom_call_target="tpu_custom_call" | custom-call | flops 1500000000 | bytes 512 | tf_op jit(solution)/shard_map/project/pallas_call | solution.py:212
  87.2 3.8 %collective-permute-start.20 = (bf16[1,2,128,512]{3,2,1,0:T(8,128)(2,1)S(1)}, bf16[1,2,128,512]{3,2,1,0:T(8,128)(2,1)S(1)}, u32[]{:S(2)}, u32[]{:S(2)}) collective-permute-start(bf16[1,2,128,512]{3,2,1,0:T(8,128)(2,1)S(1)} %copy-done.2), channel_id=1, source_target_pairs={{0,6},{1,7},{2,0},{3,1},{4,2},{5,3},{6,4},{7,5},{8,14},{9,15},{10,... | collective-permute-start | bytes 786440 | tf_op jit(solution)/shard_map/ppermute | solution.py:273
  91.1 1.4 %collective-permute-start.27 = (bf16[2,1024,128]{2,1,0:T(8,128)(2,1)S(1)}, bf16[2,1024,128]{2,1,0:T(8,128)(2,1)S(1)}, u32[]{:S(2)}, u32[]{:S(2)}) collective-permute-start(bf16[2,1024,128]{2,1,0:T(8,128)(2,1)S(1)} %add_convert_fusion.2), channel_id=1, source_target_pairs={{0,16},{1,9},{2,18},{3,11},{4,20},{5,13},{6,22},{7,15},{8,24},{9,1... | collective-permute-start | bytes 1572872 | tf_op jit(solution)/shard_map/ppermute | solution.py:268
  92.5 0.6 collective-permute-start.30
  93.2 4.2 %collective-permute-done.20.refs_3_ = bf16[1,2,128,512]{3,2,1,0:T(8,128)(2,1)S(1)} collective-permute-done((bf16[1,2,128,512]{3,2,1,0:T(8,128)(2,1)S(1)}, bf16[1,2,128,512]{3,2,1,0:T(8,128)(2,1)S(1)}, u32[]{:S(2)}, u32[]{:S(2)}) %collective-permute-start.20) | collective-permute-done | bytes 262176 | tf_op jit(solution)/shard_map/ppermute | solution.py:273
  97.4 0.5 collective-permute-start.26
  97.9 1.0 collective-permute-done.25.refs_6_
  98.9 0.4 collective-permute-done.26.refs_7_
  99.3 5.2 %project.7 = (bf16[2,1024,256]{2,1,0:T(8,128)(2,1)S(1)}, bf16[2,1024,256]{2,1,0:T(8,128)(2,1)S(1)}) custom-call(bf16[512,2048]{1,0:T(8,128)(2,1)S(1)} %attention.3.first_ref, bf16[512,2048]{1,0:T(8,128)(2,1)S(1)} %attention.2.second_ref, bf16[1,2,128,512]{3,2,1,0:T(8,128)(2,1)S(1)} %copy-done.2, ...), custom_call_target="tpu_custom_call" | custom-call | flops 10000000 | bytes 512 | tf_op jit(solution)/shard_map/project/pallas_call | solution.py:212
  104.6 1.0 collective-permute-done.27.last_ref
  105.6 1.8 %collective-permute-start.28 = (bf16[2,1024,256]{2,1,0:T(8,128)(2,1)S(1)}, bf16[2,1024,256]{2,1,0:T(8,128)(2,1)S(1)}, u32[]{:S(2)}, u32[]{:S(2)}) collective-permute-start(bf16[2,1024,256]{2,1,0:T(8,128)(2,1)S(1)} %get-tuple-element.161), channel_id=1, source_target_pairs={{0,8},{1,17},{2,10},{3,19},{4,12},{5,21},{6,14},{7,23},{8,0},{9,25... | collective-permute-start | bytes 3145736 | tf_op jit(solution)/shard_map/ppermute | solution.py:268
  107.4 3.5 %collective-permute-done.30.received_ref = bf16[2,1024,256]{2,1,0:T(8,128)(2,1)S(1)} collective-permute-done((bf16[2,1024,256]{2,1,0:T(8,128)(2,1)S(1)}, bf16[2,1024,256]{2,1,0:T(8,128)(2,1)S(1)}, u32[]{:S(2)}, u32[]{:S(2)}) %collective-permute-start.30) | collective-permute-done | bytes 1048608 | tf_op jit(solution)/shard_map/ppermute | solution.py:268
  111.0 0.9 collective-permute-start.31
  111.9 15.8 %collective-permute-done.28.received_ref = bf16[2,1024,256]{2,1,0:T(8,128)(2,1)S(1)} collective-permute-done((bf16[2,1024,256]{2,1,0:T(8,128)(2,1)S(1)}, bf16[2,1024,256]{2,1,0:T(8,128)(2,1)S(1)}, u32[]{:S(2)}, u32[]{:S(2)}) %collective-permute-start.28) | collective-permute-done | bytes 1048608 | tf_op jit(solution)/shard_map/ppermute | solution.py:268
  127.8 0.9 collective-permute-start.29
  128.8 1.1 finish.4
  129.9 1.1 finish.5
  131.0 1.1 finish.6
  132.1 5.0 %collective-permute-done.29.last_ref = bf16[2,1024,128]{2,1,0:T(8,128)(2,1)S(1)} collective-permute-done((bf16[2,1024,128]{2,1,0:T(8,128)(2,1)S(1)}, bf16[2,1024,128]{2,1,0:T(8,128)(2,1)S(1)}, u32[]{:S(2)}, u32[]{:S(2)}) %collective-permute-start.29) | collective-permute-done | bytes 524320 | tf_op jit(solution)/shard_map/ppermute | solution.py:268
  137.1 1.1 finish.7
  (67 shorter events, 2.5 us)
Async XLA Ops:
  0.6 10.4 %copy-start.6 = (bf16[1024,2,128]{2,1,0:T(2,128)(2,1)S(1)}, bf16[1024,2,128]{2,1,0:T(2,128)(2,1)}, u32[]{:S(2)}) copy-start(bf16[1024,2,128]{2,1,0:T(2,128)(2,1)} %param.9) | copy-start | bytes 1572868
  4.8 17.4 %collective-permute-start = (bf16[1,2,128,512]{3,2,1,0:T(8,128)(2,1)}, bf16[1,2,128,512]{3,2,1,0:T(8,128)(2,1)}, u32[]{:S(2)}, u32[]{:S(2)}) collective-permute-start(bf16[1,2,128,512]{3,2,1,0:T(8,128)(2,1)} %get-tuple-element.105.refs_0_), channel_id=1, source_target_pairs={{0,6},{1,7},{2,0},{3,1},{4,2},{5,3},{6,4},{7,5},{8,14},{9,15},{10,... | collective-permute-start | bytes 786440 | tf_op jit(solution)/shard_map/ppermute | solution.py:273
  9.9 13.6 %collective-permute-start.1 = (bf16[1,2,128,512]{3,2,1,0:T(8,128)(2,1)}, bf16[1,2,128,512]{3,2,1,0:T(8,128)(2,1)}, u32[]{:S(2)}, u32[]{:S(2)}) collective-permute-start(bf16[1,2,128,512]{3,2,1,0:T(8,128)(2,1)} %get-tuple-element.105.refs_0_), channel_id=1, source_target_pairs={{0,2},{1,3},{2,4},{3,5},{4,6},{5,7},{6,0},{7,1},{8,10},{9,11},{10,... | collective-permute-start | bytes 786440 | tf_op jit(solution)/shard_map/ppermute | solution.py:273
  9.9 18.3 %collective-permute-start.2 = (bf16[1,2,128,512]{3,2,1,0:T(8,128)(2,1)}, bf16[1,2,128,512]{3,2,1,0:T(8,128)(2,1)S(1)}, u32[]{:S(2)}, u32[]{:S(2)}) collective-permute-start(bf16[1,2,128,512]{3,2,1,0:T(8,128)(2,1)} %get-tuple-element.121.refs_0_), channel_id=1, source_target_pairs={{0,2},{1,3},{2,4},{3,5},{4,6},{5,7},{6,0},{7,1},{8,10},{9,11},{10,... | collective-permute-start | bytes 786440 | tf_op jit(solution)/shard_map/ppermute | solution.py:273
  9.9 18.3 %collective-permute-start.4 = (bf16[4,2,128,512]{3,2,1,0:T(8,128)(2,1)}, bf16[4,2,128,512]{3,2,1,0:T(8,128)(2,1)}, u32[]{:S(2)}, u32[]{:S(2)}) collective-permute-start(bf16[4,2,128,512]{3,2,1,0:T(8,128)(2,1)} %get-tuple-element.93), channel_id=1, source_target_pairs={{0,1},{1,0},{2,3},{3,2},{4,5},{5,4},{6,7},{7,6},{8,9},{9,8},{10,11... | collective-permute-start | bytes 3145736 | tf_op jit(solution)/shard_map/ppermute | solution.py:277
  11.1 4.0 %copy-start.7 = (s32[64]{0:T(128)S(1)}, s32[64]{0:T(128)}, u32[]{:S(2)}) copy-start(s32[64]{0:T(128)} %param.11) | copy-start | bytes 772
  11.2 4.7 %copy-start = (bf16[1024,1024]{1,0:T(8,128)(2,1)S(1)}, bf16[1024,1024]{1,0:T(8,128)(2,1)}, u32[]{:S(2)}) copy-start(bf16[1024,1024]{1,0:T(8,128)(2,1)} %q_ref.3) | copy-start | bytes 6291460
  12.0 10.1 %collective-permute-start.3 = (bf16[224,512]{1,0:T(8,128)(2,1)}, bf16[224,512]{1,0:T(8,128)(2,1)}, u32[]{:S(2)}, u32[]{:S(2)}) collective-permute-start(bf16[224,512]{1,0:T(8,128)(2,1)} %slice.60), channel_id=1, source_target_pairs={{0,1},{1,2},{2,3},{3,4},{4,5},{5,6},{6,7},{8,9},{9,10},{10,11},{11... | collective-permute-start | bytes 688136 | tf_op jit(solution)/shard_map/ppermute | solution.py:351
  15.9 1.6 %copy-start.1 = (bf16[1024,1024]{1,0:T(8,128)(2,1)S(1)}, bf16[1024,1024]{1,0:T(8,128)(2,1)}, u32[]{:S(2)}) copy-start(bf16[1024,1024]{1,0:T(8,128)(2,1)} %qt_ref.3) | copy-start | bytes 6291460
  17.5 15.1 %copy-start.3 = (bf16[1,2,128,512]{3,2,1,0:T(8,128)(2,1)S(1)}, bf16[1,2,128,512]{3,2,1,0:T(8,128)(2,1)}, u32[]{:S(2)}) copy-start(bf16[1,2,128,512]{3,2,1,0:T(8,128)(2,1)} %get-tuple-element.136.refs_0_) | copy-start | bytes 786436
  28.1 11.1 %collective-permute-start.5 = (bf16[1,2,128,512]{3,2,1,0:T(8,128)(2,1)}, bf16[1,2,128,512]{3,2,1,0:T(8,128)(2,1)S(1)}, u32[]{:S(2)}, u32[]{:S(2)}) collective-permute-start(bf16[1,2,128,512]{3,2,1,0:T(8,128)(2,1)} %collective-permute-done.1.refs_1_), channel_id=1, source_target_pairs={{0,2},{1,3},{2,4},{3,5},{4,6},{5,7},{6,0},{7,1},{8,10},{9,11},{10,... | collective-permute-start | bytes 786440 | tf_op jit(solution)/shard_map/ppermute | solution.py:273
  32.0 7.2 %collective-permute-start.7 = (bf16[1,2,128,512]{3,2,1,0:T(8,128)(2,1)}, bf16[1,2,128,512]{3,2,1,0:T(8,128)(2,1)S(1)}, u32[]{:S(2)}, u32[]{:S(2)}) collective-permute-start(bf16[1,2,128,512]{3,2,1,0:T(8,128)(2,1)} %collective-permute-done.1.refs_1_), channel_id=1, source_target_pairs={{0,1},{1,0},{2,3},{3,2},{4,5},{5,4},{6,7},{7,6},{8,9},{9,8},{10,11... | collective-permute-start | bytes 786440 | tf_op jit(solution)/shard_map/ppermute | solution.py:277
  32.0 7.2 %collective-permute-start.6 = (bf16[1,2,128,512]{3,2,1,0:T(8,128)(2,1)}, bf16[1,2,128,512]{3,2,1,0:T(8,128)(2,1)S(1)}, u32[]{:S(2)}, u32[]{:S(2)}) collective-permute-start(bf16[1,2,128,512]{3,2,1,0:T(8,128)(2,1)} %collective-permute-done.refs_3_), channel_id=1, source_target_pairs={{0,1},{1,0},{2,3},{3,2},{4,5},{5,4},{6,7},{7,6},{8,9},{9,8},{10,11... | collective-permute-start | bytes 786440 | tf_op jit(solution)/shard_map/ppermute | solution.py:277
  32.5 6.7 %collective-permute-start.8 = (bf16[1,2,128,512]{3,2,1,0:T(8,128)(2,1)S(1)}, bf16[1,2,128,512]{3,2,1,0:T(8,128)(2,1)S(1)}, u32[]{:S(2)}, u32[]{:S(2)}) collective-permute-start(bf16[1,2,128,512]{3,2,1,0:T(8,128)(2,1)S(1)} %collective-permute-done.2.refs_1_), channel_id=1, source_target_pairs={{0,1},{1,0},{2,3},{3,2},{4,5},{5,4},{6,7},{7,6},{8,9},{9,8},{10,11... | collective-permute-start | bytes 786440 | tf_op jit(solution)/shard_map/ppermute | solution.py:277
  32.6 12.3 %collective-permute-start.9 = (bf16[1,2,128,512]{3,2,1,0:T(8,128)(2,1)S(1)}, bf16[1,2,128,512]{3,2,1,0:T(8,128)(2,1)S(1)}, u32[]{:S(2)}, u32[]{:S(2)}) collective-permute-start(bf16[1,2,128,512]{3,2,1,0:T(8,128)(2,1)S(1)} %copy-done.3), channel_id=1, source_target_pairs={{0,2},{1,3},{2,4},{3,5},{4,6},{5,7},{6,0},{7,1},{8,10},{9,11},{10,... | collective-permute-start | bytes 786440 | tf_op jit(solution)/shard_map/ppermute | solution.py:273
  33.7 11.3 %copy-start.4 = (bf16[1,2,128,512]{3,2,1,0:T(8,128)(2,1)S(1)}, bf16[1,2,128,512]{3,2,1,0:T(8,128)(2,1)}, u32[]{:S(2)}) copy-start(bf16[1,2,128,512]{3,2,1,0:T(8,128)(2,1)} %get-tuple-element.121.refs_0_) | copy-start | bytes 786436
  33.7 13.3 %copy-start.5 = (bf16[1,2,128,512]{3,2,1,0:T(8,128)(2,1)S(1)}, bf16[1,2,128,512]{3,2,1,0:T(8,128)(2,1)}, u32[]{:S(2)}) copy-start(bf16[1,2,128,512]{3,2,1,0:T(8,128)(2,1)} %get-tuple-element.105.refs_0_) | copy-start | bytes 786436
  38.5 22.9 %copy-start.2 = (bf16[1,2,128,512]{3,2,1,0:T(8,128)(2,1)S(1)}, bf16[1,2,128,512]{3,2,1,0:T(8,128)(2,1)}, u32[]{:S(2)}) copy-start(bf16[1,2,128,512]{3,2,1,0:T(8,128)(2,1)} %get-tuple-element.153.refs_0_) | copy-start | bytes 786436
  44.9 2.2 %collective-permute-start.10 = (bf16[1,2,128,512]{3,2,1,0:T(8,128)(2,1)S(1)}, bf16[1,2,128,512]{3,2,1,0:T(8,128)(2,1)S(1)}, u32[]{:S(2)}, u32[]{:S(2)}) collective-permute-start(bf16[1,2,128,512]{3,2,1,0:T(8,128)(2,1)S(1)} %collective-permute-done.5.refs_2_), channel_id=1, source_target_pairs={{0,1},{1,0},{2,3},{3,2},{4,5},{5,4},{6,7},{7,6},{8,9},{9,8},{10,11... | collective-permute-start | bytes 786440 | tf_op jit(solution)/shard_map/ppermute | solution.py:277
  45.0 14.2 %collective-permute-start.11 = (bf16[1,2,128,512]{3,2,1,0:T(8,128)(2,1)S(1)}, bf16[1,2,128,512]{3,2,1,0:T(8,128)(2,1)S(1)}, u32[]{:S(2)}, u32[]{:S(2)}) collective-permute-start(bf16[1,2,128,512]{3,2,1,0:T(8,128)(2,1)S(1)} %copy-done.4), channel_id=1, source_target_pairs={{0,6},{1,7},{2,0},{3,1},{4,2},{5,3},{6,4},{7,5},{8,14},{9,15},{10,... | collective-permute-start | bytes 786440 | tf_op jit(solution)/shard_map/ppermute | solution.py:273
  45.0 14.2 %collective-permute-start.12 = (bf16[1,2,128,512]{3,2,1,0:T(8,128)(2,1)S(1)}, bf16[1,2,128,512]{3,2,1,0:T(8,128)(2,1)S(1)}, u32[]{:S(2)}, u32[]{:S(2)}) collective-permute-start(bf16[1,2,128,512]{3,2,1,0:T(8,128)(2,1)S(1)} %collective-permute-done.2.refs_1_), channel_id=1, source_target_pairs={{0,2},{1,3},{2,4},{3,5},{4,6},{5,7},{6,0},{7,1},{8,10},{9,11},{10,... | collective-permute-start | bytes 786440 | tf_op jit(solution)/shard_map/ppermute | solution.py:273
  47.1 12.2 %collective-permute-start.13 = (bf16[1,2,128,512]{3,2,1,0:T(8,128)(2,1)S(1)}, bf16[1,2,128,512]{3,2,1,0:T(8,128)(2,1)S(1)}, u32[]{:S(2)}, u32[]{:S(2)}) collective-permute-start(bf16[1,2,128,512]{3,2,1,0:T(8,128)(2,1)S(1)} %collective-permute-done.9.refs_1_), channel_id=1, source_target_pairs={{0,1},{1,0},{2,3},{3,2},{4,5},{5,4},{6,7},{7,6},{8,9},{9,8},{10,11... | collective-permute-start | bytes 786440 | tf_op jit(solution)/shard_map/ppermute | solution.py:277
  52.5 16.1 %collective-permute-start.18 = (bf16[2,1024,256]{2,1,0:T(8,128)(2,1)S(1)}, bf16[2,1024,256]{2,1,0:T(8,128)(2,1)S(1)}, u32[]{:S(2)}, u32[]{:S(2)}) collective-permute-start(bf16[2,1024,256]{2,1,0:T(8,128)(2,1)S(1)} %get-tuple-element.119), channel_id=1, source_target_pairs={{0,8},{1,17},{2,10},{3,19},{4,12},{5,21},{6,14},{7,23},{8,0},{9,25... | collective-permute-start | bytes 3145736 | tf_op jit(solution)/shard_map/ppermute | solution.py:268
  59.3 2.5 %collective-permute-start.14 = (bf16[2,2,128,512]{3,2,1,0:T(8,128)(2,1)S(1)}, bf16[2,2,128,512]{3,2,1,0:T(8,128)(2,1)S(1)}, u32[]{:S(2)}, u32[]{:S(2)}) collective-permute-start(bf16[2,2,128,512]{3,2,1,0:T(8,128)(2,1)S(1)} %pad_maximum_fusion.2), channel_id=1, source_target_pairs={{0,1},{1,0},{2,3},{3,2},{4,5},{5,4},{6,7},{7,6},{8,9},{9,8},{10,11... | collective-permute-start | bytes 1572872 | tf_op jit(solution)/shard_map/ppermute | solution.py:277
  59.4 9.4 %collective-permute-start.15 = (bf16[1,2,128,512]{3,2,1,0:T(8,128)(2,1)S(1)}, bf16[1,2,128,512]{3,2,1,0:T(8,128)(2,1)S(1)}, u32[]{:S(2)}, u32[]{:S(2)}) collective-permute-start(bf16[1,2,128,512]{3,2,1,0:T(8,128)(2,1)S(1)} %copy-done.3), channel_id=1, source_target_pairs={{0,6},{1,7},{2,0},{3,1},{4,2},{5,3},{6,4},{7,5},{8,14},{9,15},{10,... | collective-permute-start | bytes 786440 | tf_op jit(solution)/shard_map/ppermute | solution.py:273
  60.1 14.6 %collective-permute-start.16 = (bf16[1,2,128,512]{3,2,1,0:T(8,128)(2,1)S(1)}, bf16[1,2,128,512]{3,2,1,0:T(8,128)(2,1)S(1)}, u32[]{:S(2)}, u32[]{:S(2)}) collective-permute-start(bf16[1,2,128,512]{3,2,1,0:T(8,128)(2,1)S(1)} %collective-permute-done.9.refs_1_), channel_id=1, source_target_pairs={{0,2},{1,3},{2,4},{3,5},{4,6},{5,7},{6,0},{7,1},{8,10},{9,11},{10,... | collective-permute-start | bytes 786440 | tf_op jit(solution)/shard_map/ppermute | solution.py:273
  61.4 18.5 %collective-permute-start.17 = (bf16[1,2,128,512]{3,2,1,0:T(8,128)(2,1)S(1)}, bf16[1,2,128,512]{3,2,1,0:T(8,128)(2,1)S(1)}, u32[]{:S(2)}, u32[]{:S(2)}) collective-permute-start(bf16[1,2,128,512]{3,2,1,0:T(8,128)(2,1)S(1)} %copy-done.2), channel_id=1, source_target_pairs={{0,2},{1,3},{2,4},{3,5},{4,6},{5,7},{6,0},{7,1},{8,10},{9,11},{10,... | collective-permute-start | bytes 786440 | tf_op jit(solution)/shard_map/ppermute | solution.py:273
  67.0 23.9 %collective-permute-start.23 = (bf16[2,1024,256]{2,1,0:T(8,128)(2,1)S(1)}, bf16[2,1024,256]{2,1,0:T(8,128)(2,1)S(1)}, u32[]{:S(2)}, u32[]{:S(2)}) collective-permute-start(bf16[2,1024,256]{2,1,0:T(8,128)(2,1)S(1)} %get-tuple-element.133), channel_id=1, source_target_pairs={{0,8},{1,17},{2,10},{3,19},{4,12},{5,21},{6,14},{7,23},{8,0},{9,25... | collective-permute-start | bytes 3145736 | tf_op jit(solution)/shard_map/ppermute | solution.py:268
  80.0 2.0 %collective-permute-start.19 = (bf16[2,2,128,512]{3,2,1,0:T(8,128)(2,1)S(1)}, bf16[2,2,128,512]{3,2,1,0:T(8,128)(2,1)S(1)}, u32[]{:S(2)}, u32[]{:S(2)}) collective-permute-start(bf16[2,2,128,512]{3,2,1,0:T(8,128)(2,1)S(1)} %pad_maximum_fusion.3), channel_id=1, source_target_pairs={{0,1},{1,0},{2,3},{3,2},{4,5},{5,4},{6,7},{7,6},{8,9},{9,8},{10,11... | collective-permute-start | bytes 1572872 | tf_op jit(solution)/shard_map/ppermute | solution.py:277
  80.1 10.9 %collective-permute-start.24 = (bf16[2,1024,128]{2,1,0:T(8,128)(2,1)S(1)}, bf16[2,1024,128]{2,1,0:T(8,128)(2,1)S(1)}, u32[]{:S(2)}, u32[]{:S(2)}) collective-permute-start(bf16[2,1024,128]{2,1,0:T(8,128)(2,1)S(1)} %add_convert_fusion.3), channel_id=1, source_target_pairs={{0,16},{1,9},{2,18},{3,11},{4,20},{5,13},{6,22},{7,15},{8,24},{9,1... | collective-permute-start | bytes 1572872 | tf_op jit(solution)/shard_map/ppermute | solution.py:268
  81.6 11.5 %collective-permute-start.21 = (bf16[1,2,128,512]{3,2,1,0:T(8,128)(2,1)S(1)}, bf16[1,2,128,512]{3,2,1,0:T(8,128)(2,1)S(1)}, u32[]{:S(2)}, u32[]{:S(2)}) collective-permute-start(bf16[1,2,128,512]{3,2,1,0:T(8,128)(2,1)S(1)} %collective-permute-done.17.refs_1_), channel_id=1, source_target_pairs={{0,2},{1,3},{2,4},{3,5},{4,6},{5,7},{6,0},{7,1},{8,10},{9,11},{10,... | collective-permute-start | bytes 786440 | tf_op jit(solution)/shard_map/ppermute | solution.py:273
  81.8 11.4 %collective-permute-start.22 = (bf16[1,2,128,512]{3,2,1,0:T(8,128)(2,1)S(1)}, bf16[1,2,128,512]{3,2,1,0:T(8,128)(2,1)S(1)}, u32[]{:S(2)}, u32[]{:S(2)}) collective-permute-start(bf16[1,2,128,512]{3,2,1,0:T(8,128)(2,1)S(1)} %collective-permute-done.17.refs_1_), channel_id=1, source_target_pairs={{0,1},{1,0},{2,3},{3,2},{4,5},{5,4},{6,7},{7,6},{8,9},{9,8},{10,11... | collective-permute-start | bytes 786440 | tf_op jit(solution)/shard_map/ppermute | solution.py:277
  87.2 10.2 %collective-permute-start.20 = (bf16[1,2,128,512]{3,2,1,0:T(8,128)(2,1)S(1)}, bf16[1,2,128,512]{3,2,1,0:T(8,128)(2,1)S(1)}, u32[]{:S(2)}, u32[]{:S(2)}) collective-permute-start(bf16[1,2,128,512]{3,2,1,0:T(8,128)(2,1)S(1)} %copy-done.2), channel_id=1, source_target_pairs={{0,6},{1,7},{2,0},{3,1},{4,2},{5,3},{6,4},{7,5},{8,14},{9,15},{10,... | collective-permute-start | bytes 786440 | tf_op jit(solution)/shard_map/ppermute | solution.py:273
  91.1 14.5 %collective-permute-start.27 = (bf16[2,1024,128]{2,1,0:T(8,128)(2,1)S(1)}, bf16[2,1024,128]{2,1,0:T(8,128)(2,1)S(1)}, u32[]{:S(2)}, u32[]{:S(2)}) collective-permute-start(bf16[2,1024,128]{2,1,0:T(8,128)(2,1)S(1)} %add_convert_fusion.2), channel_id=1, source_target_pairs={{0,16},{1,9},{2,18},{3,11},{4,20},{5,13},{6,22},{7,15},{8,24},{9,1... | collective-permute-start | bytes 1572872 | tf_op jit(solution)/shard_map/ppermute | solution.py:268
  92.5 18.3 %collective-permute-start.30 = (bf16[2,1024,256]{2,1,0:T(8,128)(2,1)S(1)}, bf16[2,1024,256]{2,1,0:T(8,128)(2,1)S(1)}, u32[]{:S(2)}, u32[]{:S(2)}) collective-permute-start(bf16[2,1024,256]{2,1,0:T(8,128)(2,1)S(1)} %get-tuple-element.149), channel_id=1, source_target_pairs={{0,8},{1,17},{2,10},{3,19},{4,12},{5,21},{6,14},{7,23},{8,0},{9,25... | collective-permute-start | bytes 3145736 | tf_op jit(solution)/shard_map/ppermute | solution.py:268
  97.4 1.5 %collective-permute-start.25 = (bf16[1,2,128,512]{3,2,1,0:T(8,128)(2,1)S(1)}, bf16[1,2,128,512]{3,2,1,0:T(8,128)(2,1)S(1)}, u32[]{:S(2)}, u32[]{:S(2)}) collective-permute-start(bf16[1,2,128,512]{3,2,1,0:T(8,128)(2,1)S(1)} %collective-permute-done.21.refs_2_), channel_id=1, source_target_pairs={{0,1},{1,0},{2,3},{3,2},{4,5},{5,4},{6,7},{7,6},{8,9},{9,8},{10,11... | collective-permute-start | bytes 786440 | tf_op jit(solution)/shard_map/ppermute | solution.py:277
  97.4 1.9 %collective-permute-start.26 = (bf16[1,2,128,512]{3,2,1,0:T(8,128)(2,1)S(1)}, bf16[1,2,128,512]{3,2,1,0:T(8,128)(2,1)S(1)}, u32[]{:S(2)}, u32[]{:S(2)}) collective-permute-start(bf16[1,2,128,512]{3,2,1,0:T(8,128)(2,1)S(1)} %collective-permute-done.20.refs_3_), channel_id=1, source_target_pairs={{0,1},{1,0},{2,3},{3,2},{4,5},{5,4},{6,7},{7,6},{8,9},{9,8},{10,11... | collective-permute-start | bytes 786440 | tf_op jit(solution)/shard_map/ppermute | solution.py:277
  105.6 22.1 %collective-permute-start.28 = (bf16[2,1024,256]{2,1,0:T(8,128)(2,1)S(1)}, bf16[2,1024,256]{2,1,0:T(8,128)(2,1)S(1)}, u32[]{:S(2)}, u32[]{:S(2)}) collective-permute-start(bf16[2,1024,256]{2,1,0:T(8,128)(2,1)S(1)} %get-tuple-element.161), channel_id=1, source_target_pairs={{0,8},{1,17},{2,10},{3,19},{4,12},{5,21},{6,14},{7,23},{8,0},{9,25... | collective-permute-start | bytes 3145736 | tf_op jit(solution)/shard_map/ppermute | solution.py:268
  111.0 20.0 %collective-permute-start.31 = (bf16[2,1024,128]{2,1,0:T(8,128)(2,1)S(1)}, bf16[2,1024,128]{2,1,0:T(8,128)(2,1)S(1)}, u32[]{:S(2)}, u32[]{:S(2)}) collective-permute-start(bf16[2,1024,128]{2,1,0:T(8,128)(2,1)S(1)} %add_convert_fusion), channel_id=1, source_target_pairs={{0,16},{1,9},{2,18},{3,11},{4,20},{5,13},{6,22},{7,15},{8,24},{9,1... | collective-permute-start | bytes 1572872 | tf_op jit(solution)/shard_map/ppermute | solution.py:268
  127.8 9.2 %collective-permute-start.29 = (bf16[2,1024,128]{2,1,0:T(8,128)(2,1)S(1)}, bf16[2,1024,128]{2,1,0:T(8,128)(2,1)S(1)}, u32[]{:S(2)}, u32[]{:S(2)}) collective-permute-start(bf16[2,1024,128]{2,1,0:T(8,128)(2,1)S(1)} %add_convert_fusion.1), channel_id=1, source_target_pairs={{0,16},{1,9},{2,18},{3,11},{4,20},{5,13},{6,22},{7,15},{8,24},{9,1... | collective-permute-start | bytes 1572872 | tf_op jit(solution)/shard_map/ppermute | solution.py:268

commit v14 on v11

--- a/solution.py
+++ b/solution.py
@@ -391,9 +391,8 @@
     for chunk in range(CHUNKS):
         pairs, whole, send, sums = settle(pairs, whole, send, sums)
         gathers[chunk].exchange(chunk < CHUNKS - 1)
-        first = chunk + 1 + (chunk == 0)
-        if chunk != 1 and first < CHUNKS:
-            gathers[first].exchange()
+        if chunk == 0 and CHUNKS > 2:
+            gathers[2].exchange()
         if chunk + 1 < CHUNKS:
             gathers[chunk + 1].behind()
             gathers[chunk + 1].farther()

time: 139 us -> 137 us (0.986)
  waiting for transfers between devices: 59.8 us -> 57.4 us
    ppermute x8, waiting for transfers between devices: 26.3 us -> 23.4 us  [across(): return lax.ppermute(block, ('kv', 'seq'), route)]
    ppermute x8, starting transfers between devices: 10.4 us -> 12.4 us  [across(): return lax.ppermute(block, ('kv', 'seq'), route)]
    ppermute x12, starting transfers between devices: 17.2 us -> 15.6 us  [along(): lax.ppermute(block, 'seq', [(i, (i + CORES * chips) % size) for i in rang...]
  transfers between devices with their start and end apart: 32 -> 32, of which waited for: 15 -> 16; matrix products, arithmetic and copies ran while one was open for 3% -> 3% of each run, Pallas kernels for 25% -> 25%
where the time goes in v14:
time: 137 us; the launch traced here: 136 us
  waiting for transfers between devices  57.4 us (42%)
  Pallas kernels  37.1 us (27%)
  starting transfers between devices  32.4 us (24%)
  local copies, waits for them, and re-layouts  6 us (4%)
  other arithmetic  2.28 us (2%)
    ppermute x12, waiting for transfers between devices, along(): lax.ppermute(block, 'seq', [(i, (i + CORES * chips) % size) for i in rang...  32.2 us
    ppermute x8, waiting for transfers between devices, across(): return lax.ppermute(block, ('kv', 'seq'), route)  23.4 us
    pallas_call x4, Pallas kernels, project(): pl.pallas_call(functools.partial(project_kernel, indices), grid=(2 * step...  21.3 us
    ppermute x12, starting transfers between devices, along(): lax.ppermute(block, 'seq', [(i, (i + CORES * chips) % size) for i in rang...  15.6 us
    ppermute x8, starting transfers between devices, across(): return lax.ppermute(block, ('kv', 'seq'), route)  12.4 us
    pallas_call x2, Pallas kernels, attention(): pl.pallas_call(functools.partial(attention_kernel, heads, head_dim, offse...  9.39 us
    pallas_call x4, Pallas kernels, finish(): pl.pallas_call(finish_kernel, grid=(tokens // tile,), in_specs=[pl.BlockS...  4.45 us
    unnamed x16, local copies, waits for them, and re-layouts  3.69 us
  transfers between devices with their start and end apart: 32, of which 16 were waited for; matrix products, arithmetic and copies ran while one was open for 3% of the time, Pallas kernels for 25%

profile of v14, /device:TPU:0, one launch (start us, length us, event | category | flops | bytes accessed | tf_op | source)
XLA Modules:
  0.0 136.1 jit_solution(3453908261483402555)
XLA Ops:
  0.7 1.0 copy-done.2
  1.8 1.0 copy-done.3
  2.8 2.0 %arrange.1 = (bf16[4,2,128,512]{3,2,1,0:T(8,128)(2,1)}, bf16[1,2,128,512]{3,2,1,0:T(8,128)(2,1)}, bf16[1,2,128,512]{3,2,1,0:T(8,128)(2,1)}, bf16[1,2,128,512]{3,...) custom-call(s32[4]{0:T(128)S(1)} %add_xor_fusion.owner_ref, bf16[128,2048]{1,0:T(8,128)(2,1)S(1)} %copy-done.2, ...), custom_call_target="tpu_custom_call" | custom-call | tf_op jit(solution)/shard_map/arrange/pallas_call | solution.py:42
  4.8 5.0 %collective-permute-start = (bf16[1,2,128,512]{3,2,1,0:T(8,128)(2,1)}, bf16[1,2,128,512]{3,2,1,0:T(8,128)(2,1)}, u32[]{:S(2)}, u32[]{:S(2)}) collective-permute-start(bf16[1,2,128,512]{3,2,1,0:T(8,128)(2,1)} %get-tuple-element.102.refs_0_), channel_id=1, source_target_pairs={{0,6},{1,7},{2,0},{3,1},{4,2},{5,3},{6,4},{7,5},{8,14},{9,15},{10,... | collective-permute-start | bytes 786440 | tf_op jit(solution)/shard_map/ppermute | solution.py:261
  9.8 1.1 copy.26
  11.3 0.7 slice.60
  12.0 3.1 %collective-permute-start.3 = (bf16[224,512]{1,0:T(8,128)(2,1)}, bf16[224,512]{1,0:T(8,128)(2,1)}, u32[]{:S(2)}, u32[]{:S(2)}) collective-permute-start(bf16[224,512]{1,0:T(8,128)(2,1)} %slice.60), channel_id=1, source_target_pairs={{0,1},{1,2},{2,3},{3,4},{4,5},{5,6},{6,7},{8,9},{9,10},{10,11},{11... | collective-permute-start | bytes 688136 | tf_op jit(solution)/shard_map/ppermute | solution.py:337
  15.9 1.6 %copy-done.1 = bf16[1024,1024]{1,0:T(8,128)(2,1)S(1)} copy-done((bf16[1024,1024]{1,0:T(8,128)(2,1)S(1)}, bf16[1024,1024]{1,0:T(8,128)(2,1)}, u32[]{:S(2)}) %copy-start.1) | copy-done | bytes 2097176
  17.5 4.6 %attention.2.second_ref = bf16[512,2048]{1,0:T(8,128)(2,1)S(1)} custom-call(s32[8]{0:T(128)S(1)} %pad_add_fusion.order_ref, bf16[1024,1024]{1,0:T(8,128)(2,1)S(1)} %copy-done, bf16[1024,1024]{1,0:T(8,128)(2,1)S(1)} %copy-done.1, bf16[1024,512]{1,0:T(8,128)(2,1)S(1)} %pad_maximum_fusion.ctx_ref, s32[1024,128]{1,0:T(8,128)S(1)} %broadcast_in_dim.13.low_ref), custom_call_target="tpu_custom_call" | custom-call | flops 1048576 | bytes 512 | tf_op jit(solution)/shard_map/attention/pallas_call | solution.py:126
  22.1 1.2 collective-permute-done.1.refs_1_
  23.4 4.7 %collective-permute-done.2.refs_1_ = bf16[1,2,128,512]{3,2,1,0:T(8,128)(2,1)} collective-permute-done((bf16[1,2,128,512]{3,2,1,0:T(8,128)(2,1)}, bf16[1,2,128,512]{3,2,1,0:T(8,128)(2,1)}, u32[]{:S(2)}, u32[]{:S(2)}) %collective-permute-start.2) | collective-permute-done | bytes 262176 | tf_op jit(solution)/shard_map/ppermute | solution.py:261
  28.1 3.9 %collective-permute-start.5 = (bf16[1,2,128,512]{3,2,1,0:T(8,128)(2,1)}, bf16[1,2,128,512]{3,2,1,0:T(8,128)(2,1)S(1)}, u32[]{:S(2)}, u32[]{:S(2)}) collective-permute-start(bf16[1,2,128,512]{3,2,1,0:T(8,128)(2,1)} %collective-permute-done.1.refs_1_), channel_id=1, source_target_pairs={{0,2},{1,3},{2,4},{3,5},{4,6},{5,7},{6,0},{7,1},{8,10},{9,11},{10,... | collective-permute-start | bytes 786440 | tf_op jit(solution)/shard_map/ppermute | solution.py:261
  32.0 0.5 collective-permute-start.6
  32.7 1.0 pad_maximum_fusion.1.ctx_ref
  33.7 4.8 %attention.3.first_ref = bf16[512,2048]{1,0:T(8,128)(2,1)S(1)} custom-call(s32[8]{0:T(128)S(1)} %pad_add_fusion.order_ref, bf16[1024,1024]{1,0:T(8,128)(2,1)S(1)} %copy-done, bf16[1024,1024]{1,0:T(8,128)(2,1)S(1)} %copy-done.1, bf16[736,512]{1,0:T(8,128)(2,1)S(1)} %pad_maximum_fusion.1.ctx_ref, s32[1024,128]{1,0:T(8,128)S(1)} %broadcast_in_dim.13.low_ref), custom_call_target="tpu_custom_call" | custom-call | flops 1048576 | bytes 512 | tf_op jit(solution)/shard_map/attention/pallas_call | solution.py:126
  38.5 0.7 collective-permute-done.5.refs_2_
  39.2 5.6 %collective-permute-done.9.refs_1_ = bf16[1,2,128,512]{3,2,1,0:T(8,128)(2,1)S(1)} collective-permute-done((bf16[1,2,128,512]{3,2,1,0:T(8,128)(2,1)S(1)}, bf16[1,2,128,512]{3,2,1,0:T(8,128)(2,1)S(1)}, u32[]{:S(2)}, u32[]{:S(2)}) %collective-permute-start.9) | collective-permute-done | bytes 262176 | tf_op jit(solution)/shard_map/ppermute | solution.py:261
  45.0 2.1 %collective-permute-start.12 = (bf16[1,2,128,512]{3,2,1,0:T(8,128)(2,1)}, bf16[1,2,128,512]{3,2,1,0:T(8,128)(2,1)S(1)}, u32[]{:S(2)}, u32[]{:S(2)}) collective-permute-start(bf16[1,2,128,512]{3,2,1,0:T(8,128)(2,1)} %collective-permute-done.2.refs_1_), channel_id=1, source_target_pairs={{0,2},{1,3},{2,4},{3,5},{4,6},{5,7},{6,0},{7,1},{8,10},{9,11},{10,... | collective-permute-start | bytes 786440 | tf_op jit(solution)/shard_map/ppermute | solution.py:261
  47.0 5.4 %project.4 = (bf16[2,1024,256]{2,1,0:T(8,128)(2,1)S(1)}, bf16[2,1024,256]{2,1,0:T(8,128)(2,1)S(1)}) custom-call(bf16[512,2048]{1,0:T(8,128)(2,1)S(1)} %attention.3.first_ref, bf16[512,2048]{1,0:T(8,128)(2,1)S(1)} %attention.2.second_ref, bf16[1,2,128,512]{3,2,1,0:T(8,128)(2,1)} %get-tuple-element.102.refs_0_, ...), custom_call_target="tpu_custom_call" | custom-call | flops 3000000000 | bytes 512 | tf_op jit(solution)/shard_map/project/pallas_call | solution.py:200
  52.5 1.6 %collective-permute-start.18 = (bf16[2,1024,256]{2,1,0:T(8,128)(2,1)S(1)}, bf16[2,1024,256]{2,1,0:T(8,128)(2,1)S(1)}, u32[]{:S(2)}, u32[]{:S(2)}) collective-permute-start(bf16[2,1024,256]{2,1,0:T(8,128)(2,1)S(1)} %get-tuple-element.116), channel_id=1, source_target_pairs={{0,8},{1,17},{2,10},{3,19},{4,12},{5,21},{6,14},{7,23},{8,0},{9,25... | collective-permute-start | bytes 3145736 | tf_op jit(solution)/shard_map/ppermute | solution.py:256
  54.0 5.4 %collective-permute-done.11.refs_3_ = bf16[1,2,128,512]{3,2,1,0:T(8,128)(2,1)S(1)} collective-permute-done((bf16[1,2,128,512]{3,2,1,0:T(8,128)(2,1)}, bf16[1,2,128,512]{3,2,1,0:T(8,128)(2,1)S(1)}, u32[]{:S(2)}, u32[]{:S(2)}) %collective-permute-start.11) | collective-permute-done | bytes 262176 | tf_op jit(solution)/shard_map/ppermute | solution.py:261
  59.5 0.7 collective-permute-start.15
  60.3 1.3 collective-permute-start.16
  61.9 5.4 %project.5 = (bf16[2,1024,256]{2,1,0:T(8,128)(2,1)S(1)}, bf16[2,1024,256]{2,1,0:T(8,128)(2,1)S(1)}) custom-call(bf16[512,2048]{1,0:T(8,128)(2,1)S(1)} %attention.3.first_ref, bf16[512,2048]{1,0:T(8,128)(2,1)S(1)} %attention.2.second_ref, bf16[1,2,128,512]{3,2,1,0:T(8,128)(2,1)} %get-tuple-element.118.refs_0_, ...), custom_call_target="tpu_custom_call" | custom-call | flops 3000000000 | bytes 512 | tf_op jit(solution)/shard_map/project/pallas_call | solution.py:200
  67.3 1.6 %collective-permute-start.22 = (bf16[2,1024,256]{2,1,0:T(8,128)(2,1)S(1)}, bf16[2,1024,256]{2,1,0:T(8,128)(2,1)S(1)}, u32[]{:S(2)}, u32[]{:S(2)}) collective-permute-start(bf16[2,1024,256]{2,1,0:T(8,128)(2,1)S(1)} %get-tuple-element.130), channel_id=1, source_target_pairs={{0,8},{1,17},{2,10},{3,19},{4,12},{5,21},{6,14},{7,23},{8,0},{9,25... | collective-permute-start | bytes 3145736 | tf_op jit(solution)/shard_map/ppermute | solution.py:256
  69.0 5.9 %collective-permute-done.16.refs_2_ = bf16[1,2,128,512]{3,2,1,0:T(8,128)(2,1)S(1)} collective-permute-done((bf16[1,2,128,512]{3,2,1,0:T(8,128)(2,1)S(1)}, bf16[1,2,128,512]{3,2,1,0:T(8,128)(2,1)S(1)}, u32[]{:S(2)}, u32[]{:S(2)}) %collective-permute-start.16) | collective-permute-done | bytes 262176 | tf_op jit(solution)/shard_map/ppermute | solution.py:261
  74.9 5.2 %collective-permute-done.17.refs_1_ = bf16[1,2,128,512]{3,2,1,0:T(8,128)(2,1)S(1)} collective-permute-done((bf16[1,2,128,512]{3,2,1,0:T(8,128)(2,1)S(1)}, bf16[1,2,128,512]{3,2,1,0:T(8,128)(2,1)S(1)}, u32[]{:S(2)}, u32[]{:S(2)}) %collective-permute-start.17) | collective-permute-done | bytes 262176 | tf_op jit(solution)/shard_map/ppermute | solution.py:261
  80.2 1.6 %collective-permute-start.23 = (bf16[2,1024,128]{2,1,0:T(8,128)(2,1)S(1)}, bf16[2,1024,128]{2,1,0:T(8,128)(2,1)S(1)}, u32[]{:S(2)}, u32[]{:S(2)}) collective-permute-start(bf16[2,1024,128]{2,1,0:T(8,128)(2,1)S(1)} %add_convert_fusion.3), channel_id=1, source_target_pairs={{0,16},{1,9},{2,18},{3,11},{4,20},{5,13},{6,22},{7,15},{8,24},{9,1... | collective-permute-start | bytes 1572872 | tf_op jit(solution)/shard_map/ppermute | solution.py:256
  81.8 1.7 %collective-permute-start.20 = (bf16[1,2,128,512]{3,2,1,0:T(8,128)(2,1)S(1)}, bf16[1,2,128,512]{3,2,1,0:T(8,128)(2,1)S(1)}, u32[]{:S(2)}, u32[]{:S(2)}) collective-permute-start(bf16[1,2,128,512]{3,2,1,0:T(8,128)(2,1)S(1)} %get-tuple-element.148.refs_0_), channel_id=1, source_target_pairs={{0,6},{1,7},{2,0},{3,1},{4,2},{5,3},{6,4},{7,5},{8,14},{9,15},{10,... | collective-permute-start | bytes 786440 | tf_op jit(solution)/shard_map/ppermute | solution.py:261
  83.8 5.2 %project.6 = (bf16[2,1024,256]{2,1,0:T(8,128)(2,1)S(1)}, bf16[2,1024,256]{2,1,0:T(8,128)(2,1)S(1)}) custom-call(bf16[512,2048]{1,0:T(8,128)(2,1)S(1)} %attention.3.first_ref, bf16[512,2048]{1,0:T(8,128)(2,1)S(1)} %attention.2.second_ref, bf16[1,2,128,512]{3,2,1,0:T(8,128)(2,1)S(1)} %copy-done.5, bf16[1,2,128,512]{3,2,1,0:T(8,128)(2,1)S(1)} %collective-permute-done.9.refs_1_, ...), custom_call_target="tpu_custom_call" | custom-call | flops 1500000000 | bytes 512 | tf_op jit(solution)/shard_map/project/pallas_call | solution.py:200
  89.1 0.4 collective-permute-done.23.last_ref
  89.6 1.6 %collective-permute-start.27 = (bf16[2,1024,128]{2,1,0:T(8,128)(2,1)S(1)}, bf16[2,1024,128]{2,1,0:T(8,128)(2,1)S(1)}, u32[]{:S(2)}, u32[]{:S(2)}) collective-permute-start(bf16[2,1024,128]{2,1,0:T(8,128)(2,1)S(1)} %add_convert_fusion.2), channel_id=1, source_target_pairs={{0,16},{1,9},{2,18},{3,11},{4,20},{5,13},{6,22},{7,15},{8,24},{9,1... | collective-permute-start | bytes 1572872 | tf_op jit(solution)/shard_map/ppermute | solution.py:256
  91.2 1.5 %collective-permute-start.30 = (bf16[2,1024,256]{2,1,0:T(8,128)(2,1)S(1)}, bf16[2,1024,256]{2,1,0:T(8,128)(2,1)S(1)}, u32[]{:S(2)}, u32[]{:S(2)}) collective-permute-start(bf16[2,1024,256]{2,1,0:T(8,128)(2,1)S(1)} %get-tuple-element.144), channel_id=1, source_target_pairs={{0,8},{1,17},{2,10},{3,19},{4,12},{5,21},{6,14},{7,23},{8,0},{9,25... | collective-permute-start | bytes 3145736 | tf_op jit(solution)/shard_map/ppermute | solution.py:256
  92.7 3.4 %collective-permute-done.21.refs_2_ = bf16[1,2,128,512]{3,2,1,0:T(8,128)(2,1)S(1)} collective-permute-done((bf16[1,2,128,512]{3,2,1,0:T(8,128)(2,1)S(1)}, bf16[1,2,128,512]{3,2,1,0:T(8,128)(2,1)S(1)}, u32[]{:S(2)}, u32[]{:S(2)}) %collective-permute-start.21) | collective-permute-done | bytes 262176 | tf_op jit(solution)/shard_map/ppermute | solution.py:261
  96.1 0.5 collective-permute-start.25
  96.6 1.0 collective-permute-done.24.refs_5_
  98.4 5.2 %project.7 = (bf16[2,1024,256]{2,1,0:T(8,128)(2,1)S(1)}, bf16[2,1024,256]{2,1,0:T(8,128)(2,1)S(1)}) custom-call(bf16[512,2048]{1,0:T(8,128)(2,1)S(1)} %attention.3.first_ref, bf16[512,2048]{1,0:T(8,128)(2,1)S(1)} %attention.2.second_ref, bf16[1,2,128,512]{3,2,1,0:T(8,128)(2,1)S(1)} %get-tuple-element.148.refs_0_, ...), custom_call_target="tpu_custom_call" | custom-call | flops 10000000 | bytes 512 | tf_op jit(solution)/shard_map/project/pallas_call | solution.py:200
  103.6 0.9 collective-permute-done.27.last_ref
  104.5 1.5 %collective-permute-start.28 = (bf16[2,1024,256]{2,1,0:T(8,128)(2,1)S(1)}, bf16[2,1024,256]{2,1,0:T(8,128)(2,1)S(1)}, u32[]{:S(2)}, u32[]{:S(2)}) collective-permute-start(bf16[2,1024,256]{2,1,0:T(8,128)(2,1)S(1)} %get-tuple-element.155), channel_id=1, source_target_pairs={{0,8},{1,17},{2,10},{3,19},{4,12},{5,21},{6,14},{7,23},{8,0},{9,25... | collective-permute-start | bytes 3145736 | tf_op jit(solution)/shard_map/ppermute | solution.py:256
  106.0 2.7 %collective-permute-done.30.received_ref = bf16[2,1024,256]{2,1,0:T(8,128)(2,1)S(1)} collective-permute-done((bf16[2,1024,256]{2,1,0:T(8,128)(2,1)S(1)}, bf16[2,1024,256]{2,1,0:T(8,128)(2,1)S(1)}, u32[]{:S(2)}, u32[]{:S(2)}) %collective-permute-start.30) | collective-permute-done | bytes 1048608 | tf_op jit(solution)/shard_map/ppermute | solution.py:256
  108.9 1.6 %collective-permute-start.31 = (bf16[2,1024,128]{2,1,0:T(8,128)(2,1)S(1)}, bf16[2,1024,128]{2,1,0:T(8,128)(2,1)S(1)}, u32[]{:S(2)}, u32[]{:S(2)}) collective-permute-start(bf16[2,1024,128]{2,1,0:T(8,128)(2,1)S(1)} %add_convert_fusion), channel_id=1, source_target_pairs={{0,16},{1,9},{2,18},{3,11},{4,20},{5,13},{6,22},{7,15},{8,24},{9,1... | collective-permute-start | bytes 1572872 | tf_op jit(solution)/shard_map/ppermute | solution.py:256
  110.4 15.1 %collective-permute-done.28.received_ref = bf16[2,1024,256]{2,1,0:T(8,128)(2,1)S(1)} collective-permute-done((bf16[2,1024,256]{2,1,0:T(8,128)(2,1)S(1)}, bf16[2,1024,256]{2,1,0:T(8,128)(2,1)S(1)}, u32[]{:S(2)}, u32[]{:S(2)}) %collective-permute-start.28) | collective-permute-done | bytes 1048608 | tf_op jit(solution)/shard_map/ppermute | solution.py:256
  125.7 1.6 %collective-permute-start.29 = (bf16[2,1024,128]{2,1,0:T(8,128)(2,1)S(1)}, bf16[2,1024,128]{2,1,0:T(8,128)(2,1)S(1)}, u32[]{:S(2)}, u32[]{:S(2)}) collective-permute-start(bf16[2,1024,128]{2,1,0:T(8,128)(2,1)S(1)} %add_convert_fusion.1), channel_id=1, source_target_pairs={{0,16},{1,9},{2,18},{3,11},{4,20},{5,13},{6,22},{7,15},{8,24},{9,1... | collective-permute-start | bytes 1572872 | tf_op jit(solution)/shard_map/ppermute | solution.py:256
  127.3 1.1 finish.4
  128.4 1.1 finish.5
  129.5 1.1 finish.6
  130.6 4.3 %collective-permute-done.29.last_ref = bf16[2,1024,128]{2,1,0:T(8,128)(2,1)S(1)} collective-permute-done((bf16[2,1024,128]{2,1,0:T(8,128)(2,1)S(1)}, bf16[2,1024,128]{2,1,0:T(8,128)(2,1)S(1)}, u32[]{:S(2)}, u32[]{:S(2)}) %collective-permute-start.29) | collective-permute-done | bytes 524320 | tf_op jit(solution)/shard_map/ppermute | solution.py:256
  135.0 1.1 finish.7
  (67 shorter events, 3.6 us)
Async XLA Ops:
  0.7 1.0 copy-start.2
  1.8 1.0 copy-start.3
  2.8 8.2 %copy-start.6 = (bf16[1024,2,128]{2,1,0:T(2,128)(2,1)S(1)}, bf16[1024,2,128]{2,1,0:T(2,128)(2,1)}, u32[]{:S(2)}) copy-start(bf16[1024,2,128]{2,1,0:T(2,128)(2,1)} %param.9) | copy-start | bytes 1572868
  4.8 6.4 %copy-start.4 = (bf16[1,2,128,512]{3,2,1,0:T(8,128)(2,1)}, bf16[1,2,128,512]{3,2,1,0:T(8,128)(2,1)S(1)}, u32[]{:S(2)}) copy-start(bf16[1,2,128,512]{3,2,1,0:T(8,128)(2,1)S(1)} %get-tuple-element.133.refs_0_) | copy-start | bytes 786436
  4.8 17.3 %collective-permute-start = (bf16[1,2,128,512]{3,2,1,0:T(8,128)(2,1)}, bf16[1,2,128,512]{3,2,1,0:T(8,128)(2,1)}, u32[]{:S(2)}, u32[]{:S(2)}) collective-permute-start(bf16[1,2,128,512]{3,2,1,0:T(8,128)(2,1)} %get-tuple-element.102.refs_0_), channel_id=1, source_target_pairs={{0,6},{1,7},{2,0},{3,1},{4,2},{5,3},{6,4},{7,5},{8,14},{9,15},{10,... | collective-permute-start | bytes 786440 | tf_op jit(solution)/shard_map/ppermute | solution.py:261
  9.8 13.6 %collective-permute-start.1 = (bf16[1,2,128,512]{3,2,1,0:T(8,128)(2,1)}, bf16[1,2,128,512]{3,2,1,0:T(8,128)(2,1)}, u32[]{:S(2)}, u32[]{:S(2)}) collective-permute-start(bf16[1,2,128,512]{3,2,1,0:T(8,128)(2,1)} %get-tuple-element.102.refs_0_), channel_id=1, source_target_pairs={{0,2},{1,3},{2,4},{3,5},{4,6},{5,7},{6,0},{7,1},{8,10},{9,11},{10,... | collective-permute-start | bytes 786440 | tf_op jit(solution)/shard_map/ppermute | solution.py:261
  9.8 18.3 %collective-permute-start.2 = (bf16[1,2,128,512]{3,2,1,0:T(8,128)(2,1)}, bf16[1,2,128,512]{3,2,1,0:T(8,128)(2,1)}, u32[]{:S(2)}, u32[]{:S(2)}) collective-permute-start(bf16[1,2,128,512]{3,2,1,0:T(8,128)(2,1)} %get-tuple-element.118.refs_0_), channel_id=1, source_target_pairs={{0,2},{1,3},{2,4},{3,5},{4,6},{5,7},{6,0},{7,1},{8,10},{9,11},{10,... | collective-permute-start | bytes 786440 | tf_op jit(solution)/shard_map/ppermute | solution.py:261
  9.8 18.3 %collective-permute-start.4 = (bf16[4,2,128,512]{3,2,1,0:T(8,128)(2,1)}, bf16[4,2,128,512]{3,2,1,0:T(8,128)(2,1)}, u32[]{:S(2)}, u32[]{:S(2)}) collective-permute-start(bf16[4,2,128,512]{3,2,1,0:T(8,128)(2,1)} %get-tuple-element.90), channel_id=1, source_target_pairs={{0,1},{1,0},{2,3},{3,2},{4,5},{5,4},{6,7},{7,6},{8,9},{9,8},{10,11... | collective-permute-start | bytes 3145736 | tf_op jit(solution)/shard_map/ppermute | solution.py:265
  11.1 4.1 %copy-start.7 = (s32[64]{0:T(128)S(1)}, s32[64]{0:T(128)}, u32[]{:S(2)}) copy-start(s32[64]{0:T(128)} %param.11) | copy-start | bytes 772
  11.2 4.7 %copy-start = (bf16[1024,1024]{1,0:T(8,128)(2,1)S(1)}, bf16[1024,1024]{1,0:T(8,128)(2,1)}, u32[]{:S(2)}) copy-start(bf16[1024,1024]{1,0:T(8,128)(2,1)} %q_ref.3) | copy-start | bytes 6291460
  12.0 10.1 %collective-permute-start.3 = (bf16[224,512]{1,0:T(8,128)(2,1)}, bf16[224,512]{1,0:T(8,128)(2,1)}, u32[]{:S(2)}, u32[]{:S(2)}) collective-permute-start(bf16[224,512]{1,0:T(8,128)(2,1)} %slice.60), channel_id=1, source_target_pairs={{0,1},{1,2},{2,3},{3,4},{4,5},{5,6},{6,7},{8,9},{9,10},{10,11},{11... | collective-permute-start | bytes 688136 | tf_op jit(solution)/shard_map/ppermute | solution.py:337
  15.9 1.6 %copy-start.1 = (bf16[1024,1024]{1,0:T(8,128)(2,1)S(1)}, bf16[1024,1024]{1,0:T(8,128)(2,1)}, u32[]{:S(2)}) copy-start(bf16[1024,1024]{1,0:T(8,128)(2,1)} %qt_ref.3) | copy-start | bytes 6291460
  17.5 15.0 %copy-start.5 = (bf16[1,2,128,512]{3,2,1,0:T(8,128)(2,1)S(1)}, bf16[1,2,128,512]{3,2,1,0:T(8,128)(2,1)}, u32[]{:S(2)}) copy-start(bf16[1,2,128,512]{3,2,1,0:T(8,128)(2,1)} %copy-done.4) | copy-start | bytes 786436
  28.1 11.1 %collective-permute-start.5 = (bf16[1,2,128,512]{3,2,1,0:T(8,128)(2,1)}, bf16[1,2,128,512]{3,2,1,0:T(8,128)(2,1)S(1)}, u32[]{:S(2)}, u32[]{:S(2)}) collective-permute-start(bf16[1,2,128,512]{3,2,1,0:T(8,128)(2,1)} %collective-permute-done.1.refs_1_), channel_id=1, source_target_pairs={{0,2},{1,3},{2,4},{3,5},{4,6},{5,7},{6,0},{7,1},{8,10},{9,11},{10,... | collective-permute-start | bytes 786440 | tf_op jit(solution)/shard_map/ppermute | solution.py:261
  32.0 7.2 %collective-permute-start.7 = (bf16[1,2,128,512]{3,2,1,0:T(8,128)(2,1)}, bf16[1,2,128,512]{3,2,1,0:T(8,128)(2,1)S(1)}, u32[]{:S(2)}, u32[]{:S(2)}) collective-permute-start(bf16[1,2,128,512]{3,2,1,0:T(8,128)(2,1)} %collective-permute-done.1.refs_1_), channel_id=1, source_target_pairs={{0,1},{1,0},{2,3},{3,2},{4,5},{5,4},{6,7},{7,6},{8,9},{9,8},{10,11... | collective-permute-start | bytes 786440 | tf_op jit(solution)/shard_map/ppermute | solution.py:265
  32.0 7.2 %collective-permute-start.6 = (bf16[1,2,128,512]{3,2,1,0:T(8,128)(2,1)}, bf16[1,2,128,512]{3,2,1,0:T(8,128)(2,1)S(1)}, u32[]{:S(2)}, u32[]{:S(2)}) collective-permute-start(bf16[1,2,128,512]{3,2,1,0:T(8,128)(2,1)} %collective-permute-done.refs_3_), channel_id=1, source_target_pairs={{0,1},{1,0},{2,3},{3,2},{4,5},{5,4},{6,7},{7,6},{8,9},{9,8},{10,11... | collective-permute-start | bytes 786440 | tf_op jit(solution)/shard_map/ppermute | solution.py:265
  32.5 6.7 %collective-permute-start.8 = (bf16[1,2,128,512]{3,2,1,0:T(8,128)(2,1)}, bf16[1,2,128,512]{3,2,1,0:T(8,128)(2,1)S(1)}, u32[]{:S(2)}, u32[]{:S(2)}) collective-permute-start(bf16[1,2,128,512]{3,2,1,0:T(8,128)(2,1)} %collective-permute-done.2.refs_1_), channel_id=1, source_target_pairs={{0,1},{1,0},{2,3},{3,2},{4,5},{5,4},{6,7},{7,6},{8,9},{9,8},{10,11... | collective-permute-start | bytes 786440 | tf_op jit(solution)/shard_map/ppermute | solution.py:265
  32.5 12.3 %collective-permute-start.9 = (bf16[1,2,128,512]{3,2,1,0:T(8,128)(2,1)S(1)}, bf16[1,2,128,512]{3,2,1,0:T(8,128)(2,1)S(1)}, u32[]{:S(2)}, u32[]{:S(2)}) collective-permute-start(bf16[1,2,128,512]{3,2,1,0:T(8,128)(2,1)S(1)} %copy-done.5), channel_id=1, source_target_pairs={{0,2},{1,3},{2,4},{3,5},{4,6},{5,7},{6,0},{7,1},{8,10},{9,11},{10,... | collective-permute-start | bytes 786440 | tf_op jit(solution)/shard_map/ppermute | solution.py:261
  44.8 2.2 %collective-permute-start.10 = (bf16[1,2,128,512]{3,2,1,0:T(8,128)(2,1)S(1)}, bf16[1,2,128,512]{3,2,1,0:T(8,128)(2,1)S(1)}, u32[]{:S(2)}, u32[]{:S(2)}) collective-permute-start(bf16[1,2,128,512]{3,2,1,0:T(8,128)(2,1)S(1)} %collective-permute-done.5.refs_2_), channel_id=1, source_target_pairs={{0,1},{1,0},{2,3},{3,2},{4,5},{5,4},{6,7},{7,6},{8,9},{9,8},{10,11... | collective-permute-start | bytes 786440 | tf_op jit(solution)/shard_map/ppermute | solution.py:265
  45.0 14.4 %collective-permute-start.11 = (bf16[1,2,128,512]{3,2,1,0:T(8,128)(2,1)}, bf16[1,2,128,512]{3,2,1,0:T(8,128)(2,1)S(1)}, u32[]{:S(2)}, u32[]{:S(2)}) collective-permute-start(bf16[1,2,128,512]{3,2,1,0:T(8,128)(2,1)} %get-tuple-element.118.refs_0_), channel_id=1, source_target_pairs={{0,6},{1,7},{2,0},{3,1},{4,2},{5,3},{6,4},{7,5},{8,14},{9,15},{10,... | collective-permute-start | bytes 786440 | tf_op jit(solution)/shard_map/ppermute | solution.py:261
  45.0 14.4 %collective-permute-start.12 = (bf16[1,2,128,512]{3,2,1,0:T(8,128)(2,1)}, bf16[1,2,128,512]{3,2,1,0:T(8,128)(2,1)S(1)}, u32[]{:S(2)}, u32[]{:S(2)}) collective-permute-start(bf16[1,2,128,512]{3,2,1,0:T(8,128)(2,1)} %collective-permute-done.2.refs_1_), channel_id=1, source_target_pairs={{0,2},{1,3},{2,4},{3,5},{4,6},{5,7},{6,0},{7,1},{8,10},{9,11},{10,... | collective-permute-start | bytes 786440 | tf_op jit(solution)/shard_map/ppermute | solution.py:261
  47.0 12.4 %collective-permute-start.13 = (bf16[1,2,128,512]{3,2,1,0:T(8,128)(2,1)S(1)}, bf16[1,2,128,512]{3,2,1,0:T(8,128)(2,1)S(1)}, u32[]{:S(2)}, u32[]{:S(2)}) collective-permute-start(bf16[1,2,128,512]{3,2,1,0:T(8,128)(2,1)S(1)} %collective-permute-done.9.refs_1_), channel_id=1, source_target_pairs={{0,1},{1,0},{2,3},{3,2},{4,5},{5,4},{6,7},{7,6},{8,9},{9,8},{10,11... | collective-permute-start | bytes 786440 | tf_op jit(solution)/shard_map/ppermute | solution.py:265
  52.5 16.4 %collective-permute-start.18 = (bf16[2,1024,256]{2,1,0:T(8,128)(2,1)S(1)}, bf16[2,1024,256]{2,1,0:T(8,128)(2,1)S(1)}, u32[]{:S(2)}, u32[]{:S(2)}) collective-permute-start(bf16[2,1024,256]{2,1,0:T(8,128)(2,1)S(1)} %get-tuple-element.116), channel_id=1, source_target_pairs={{0,8},{1,17},{2,10},{3,19},{4,12},{5,21},{6,14},{7,23},{8,0},{9,25... | collective-permute-start | bytes 3145736 | tf_op jit(solution)/shard_map/ppermute | solution.py:256
  59.5 2.5 %collective-permute-start.14 = (bf16[2,2,128,512]{3,2,1,0:T(8,128)(2,1)S(1)}, bf16[2,2,128,512]{3,2,1,0:T(8,128)(2,1)S(1)}, u32[]{:S(2)}, u32[]{:S(2)}) collective-permute-start(bf16[2,2,128,512]{3,2,1,0:T(8,128)(2,1)S(1)} %pad_maximum_fusion.2), channel_id=1, source_target_pairs={{0,1},{1,0},{2,3},{3,2},{4,5},{5,4},{6,7},{7,6},{8,9},{9,8},{10,11... | collective-permute-start | bytes 1572872 | tf_op jit(solution)/shard_map/ppermute | solution.py:265
  59.5 9.5 %collective-permute-start.15 = (bf16[1,2,128,512]{3,2,1,0:T(8,128)(2,1)S(1)}, bf16[1,2,128,512]{3,2,1,0:T(8,128)(2,1)S(1)}, u32[]{:S(2)}, u32[]{:S(2)}) collective-permute-start(bf16[1,2,128,512]{3,2,1,0:T(8,128)(2,1)S(1)} %copy-done.5), channel_id=1, source_target_pairs={{0,6},{1,7},{2,0},{3,1},{4,2},{5,3},{6,4},{7,5},{8,14},{9,15},{10,... | collective-permute-start | bytes 786440 | tf_op jit(solution)/shard_map/ppermute | solution.py:261
  60.3 14.6 %collective-permute-start.16 = (bf16[1,2,128,512]{3,2,1,0:T(8,128)(2,1)S(1)}, bf16[1,2,128,512]{3,2,1,0:T(8,128)(2,1)S(1)}, u32[]{:S(2)}, u32[]{:S(2)}) collective-permute-start(bf16[1,2,128,512]{3,2,1,0:T(8,128)(2,1)S(1)} %collective-permute-done.9.refs_1_), channel_id=1, source_target_pairs={{0,2},{1,3},{2,4},{3,5},{4,6},{5,7},{6,0},{7,1},{8,10},{9,11},{10,... | collective-permute-start | bytes 786440 | tf_op jit(solution)/shard_map/ppermute | solution.py:261
  61.6 18.5 %collective-permute-start.17 = (bf16[1,2,128,512]{3,2,1,0:T(8,128)(2,1)S(1)}, bf16[1,2,128,512]{3,2,1,0:T(8,128)(2,1)S(1)}, u32[]{:S(2)}, u32[]{:S(2)}) collective-permute-start(bf16[1,2,128,512]{3,2,1,0:T(8,128)(2,1)S(1)} %get-tuple-element.148.refs_0_), channel_id=1, source_target_pairs={{0,2},{1,3},{2,4},{3,5},{4,6},{5,7},{6,0},{7,1},{8,10},{9,11},{10,... | collective-permute-start | bytes 786440 | tf_op jit(solution)/shard_map/ppermute | solution.py:261
  67.3 22.2 %collective-permute-start.22 = (bf16[2,1024,256]{2,1,0:T(8,128)(2,1)S(1)}, bf16[2,1024,256]{2,1,0:T(8,128)(2,1)S(1)}, u32[]{:S(2)}, u32[]{:S(2)}) collective-permute-start(bf16[2,1024,256]{2,1,0:T(8,128)(2,1)S(1)} %get-tuple-element.130), channel_id=1, source_target_pairs={{0,8},{1,17},{2,10},{3,19},{4,12},{5,21},{6,14},{7,23},{8,0},{9,25... | collective-permute-start | bytes 3145736 | tf_op jit(solution)/shard_map/ppermute | solution.py:256
  80.2 3.7 %collective-permute-start.19 = (bf16[2,2,128,512]{3,2,1,0:T(8,128)(2,1)S(1)}, bf16[2,2,128,512]{3,2,1,0:T(8,128)(2,1)S(1)}, u32[]{:S(2)}, u32[]{:S(2)}) collective-permute-start(bf16[2,2,128,512]{3,2,1,0:T(8,128)(2,1)S(1)} %pad_maximum_fusion.3), channel_id=1, source_target_pairs={{0,1},{1,0},{2,3},{3,2},{4,5},{5,4},{6,7},{7,6},{8,9},{9,8},{10,11... | collective-permute-start | bytes 1572872 | tf_op jit(solution)/shard_map/ppermute | solution.py:265
  80.2 9.2 %collective-permute-start.23 = (bf16[2,1024,128]{2,1,0:T(8,128)(2,1)S(1)}, bf16[2,1024,128]{2,1,0:T(8,128)(2,1)S(1)}, u32[]{:S(2)}, u32[]{:S(2)}) collective-permute-start(bf16[2,1024,128]{2,1,0:T(8,128)(2,1)S(1)} %add_convert_fusion.3), channel_id=1, source_target_pairs={{0,16},{1,9},{2,18},{3,11},{4,20},{5,13},{6,22},{7,15},{8,24},{9,1... | collective-permute-start | bytes 1572872 | tf_op jit(solution)/shard_map/ppermute | solution.py:256
  81.8 10.9 %collective-permute-start.20 = (bf16[1,2,128,512]{3,2,1,0:T(8,128)(2,1)S(1)}, bf16[1,2,128,512]{3,2,1,0:T(8,128)(2,1)S(1)}, u32[]{:S(2)}, u32[]{:S(2)}) collective-permute-start(bf16[1,2,128,512]{3,2,1,0:T(8,128)(2,1)S(1)} %get-tuple-element.148.refs_0_), channel_id=1, source_target_pairs={{0,6},{1,7},{2,0},{3,1},{4,2},{5,3},{6,4},{7,5},{8,14},{9,15},{10,... | collective-permute-start | bytes 786440 | tf_op jit(solution)/shard_map/ppermute | solution.py:261
  83.6 12.5 %collective-permute-start.21 = (bf16[1,2,128,512]{3,2,1,0:T(8,128)(2,1)S(1)}, bf16[1,2,128,512]{3,2,1,0:T(8,128)(2,1)S(1)}, u32[]{:S(2)}, u32[]{:S(2)}) collective-permute-start(bf16[1,2,128,512]{3,2,1,0:T(8,128)(2,1)S(1)} %collective-permute-done.17.refs_1_), channel_id=1, source_target_pairs={{0,2},{1,3},{2,4},{3,5},{4,6},{5,7},{6,0},{7,1},{8,10},{9,11},{10,... | collective-permute-start | bytes 786440 | tf_op jit(solution)/shard_map/ppermute | solution.py:261
  89.6 14.9 %collective-permute-start.27 = (bf16[2,1024,128]{2,1,0:T(8,128)(2,1)S(1)}, bf16[2,1024,128]{2,1,0:T(8,128)(2,1)S(1)}, u32[]{:S(2)}, u32[]{:S(2)}) collective-permute-start(bf16[2,1024,128]{2,1,0:T(8,128)(2,1)S(1)} %add_convert_fusion.2), channel_id=1, source_target_pairs={{0,16},{1,9},{2,18},{3,11},{4,20},{5,13},{6,22},{7,15},{8,24},{9,1... | collective-permute-start | bytes 1572872 | tf_op jit(solution)/shard_map/ppermute | solution.py:256
  91.2 17.5 %collective-permute-start.30 = (bf16[2,1024,256]{2,1,0:T(8,128)(2,1)S(1)}, bf16[2,1024,256]{2,1,0:T(8,128)(2,1)S(1)}, u32[]{:S(2)}, u32[]{:S(2)}) collective-permute-start(bf16[2,1024,256]{2,1,0:T(8,128)(2,1)S(1)} %get-tuple-element.144), channel_id=1, source_target_pairs={{0,8},{1,17},{2,10},{3,19},{4,12},{5,21},{6,14},{7,23},{8,0},{9,25... | collective-permute-start | bytes 3145736 | tf_op jit(solution)/shard_map/ppermute | solution.py:256
  96.1 1.5 %collective-permute-start.24 = (bf16[1,2,128,512]{3,2,1,0:T(8,128)(2,1)S(1)}, bf16[1,2,128,512]{3,2,1,0:T(8,128)(2,1)S(1)}, u32[]{:S(2)}, u32[]{:S(2)}) collective-permute-start(bf16[1,2,128,512]{3,2,1,0:T(8,128)(2,1)S(1)} %collective-permute-done.17.refs_1_), channel_id=1, source_target_pairs={{0,1},{1,0},{2,3},{3,2},{4,5},{5,4},{6,7},{7,6},{8,9},{9,8},{10,11... | collective-permute-start | bytes 786440 | tf_op jit(solution)/shard_map/ppermute | solution.py:265
  96.1 1.9 %collective-permute-start.25 = (bf16[1,2,128,512]{3,2,1,0:T(8,128)(2,1)S(1)}, bf16[1,2,128,512]{3,2,1,0:T(8,128)(2,1)S(1)}, u32[]{:S(2)}, u32[]{:S(2)}) collective-permute-start(bf16[1,2,128,512]{3,2,1,0:T(8,128)(2,1)S(1)} %collective-permute-done.21.refs_2_), channel_id=1, source_target_pairs={{0,1},{1,0},{2,3},{3,2},{4,5},{5,4},{6,7},{7,6},{8,9},{9,8},{10,11... | collective-permute-start | bytes 786440 | tf_op jit(solution)/shard_map/ppermute | solution.py:265
  96.6 1.8 %collective-permute-start.26 = (bf16[1,2,128,512]{3,2,1,0:T(8,128)(2,1)S(1)}, bf16[1,2,128,512]{3,2,1,0:T(8,128)(2,1)S(1)}, u32[]{:S(2)}, u32[]{:S(2)}) collective-permute-start(bf16[1,2,128,512]{3,2,1,0:T(8,128)(2,1)S(1)} %collective-permute-done.20.refs_3_), channel_id=1, source_target_pairs={{0,1},{1,0},{2,3},{3,2},{4,5},{5,4},{6,7},{7,6},{8,9},{9,8},{10,11... | collective-permute-start | bytes 786440 | tf_op jit(solution)/shard_map/ppermute | solution.py:265
  104.5 21.1 %collective-permute-start.28 = (bf16[2,1024,256]{2,1,0:T(8,128)(2,1)S(1)}, bf16[2,1024,256]{2,1,0:T(8,128)(2,1)S(1)}, u32[]{:S(2)}, u32[]{:S(2)}) collective-permute-start(bf16[2,1024,256]{2,1,0:T(8,128)(2,1)S(1)} %get-tuple-element.155), channel_id=1, source_target_pairs={{0,8},{1,17},{2,10},{3,19},{4,12},{5,21},{6,14},{7,23},{8,0},{9,25... | collective-permute-start | bytes 3145736 | tf_op jit(solution)/shard_map/ppermute | solution.py:256
  108.9 20.7 %collective-permute-start.31 = (bf16[2,1024,128]{2,1,0:T(8,128)(2,1)S(1)}, bf16[2,1024,128]{2,1,0:T(8,128)(2,1)S(1)}, u32[]{:S(2)}, u32[]{:S(2)}) collective-permute-start(bf16[2,1024,128]{2,1,0:T(8,128)(2,1)S(1)} %add_convert_fusion), channel_id=1, source_target_pairs={{0,16},{1,9},{2,18},{3,11},{4,20},{5,13},{6,22},{7,15},{8,24},{9,1... | collective-permute-start | bytes 1572872 | tf_op jit(solution)/shard_map/ppermute | solution.py:256
  125.7 9.2 %collective-permute-start.29 = (bf16[2,1024,128]{2,1,0:T(8,128)(2,1)S(1)}, bf16[2,1024,128]{2,1,0:T(8,128)(2,1)S(1)}, u32[]{:S(2)}, u32[]{:S(2)}) collective-permute-start(bf16[2,1024,128]{2,1,0:T(8,128)(2,1)S(1)} %add_convert_fusion.1), channel_id=1, source_target_pairs={{0,16},{1,9},{2,18},{3,11},{4,20},{5,13},{6,22},{7,15},{8,24},{9,1... | collective-permute-start | bytes 1572872 | tf_op jit(solution)/shard_map/ppermute | solution.py:256

commit v15 on v14

--- a/solution.py
+++ b/solution.py
@@ -190,7 +190,7 @@
 
 def project(gflops, pairs, pieces):
     tokens, width = pairs[0].shape
-    tile = min(2 * TILE, tokens)
+    tile = min(4 * TILE, tokens)
     steps = tokens // tile
     indices = [index for index, _ in pieces]
     arrays = [array for _, array in pieces]
@@ -211,7 +211,7 @@
             pltpu.VMEM((2, width // 2, columns), jnp.bfloat16),
             pltpu.SemaphoreType.DMA((len(arrays),)),
         ],
-        compiler_params=pltpu.CompilerParams(vmem_limit_bytes=vmem_bytes),
+        compiler_params=pltpu.CompilerParams(vmem_limit_bytes=2 * vmem_bytes),
         cost_estimate=pl.CostEstimate(
             flops=int(gflops * 1e9), bytes_accessed=tokens, transcendentals=0
         ),

time: 137 us -> 137 us (level)
  Pallas kernels: 37.1 us -> 35.5 us
  waiting for transfers between devices: 57.4 us -> 58.9 us
    pallas_call x4, Pallas kernels: 21.3 us -> 19.8 us  [project(): pl.pallas_call(functools.partial(project_kernel, indices), grid=(2 * step...]
    unnamed x16 -> x18, local copies, waits for them, and re-layouts: 3.69 us -> 3.7 us
  transfers between devices with their start and end apart: 32 -> 32, of which waited for: 16 -> 16; matrix products, arithmetic and copies ran while one was open for 3% -> 3% of each run, Pallas kernels for 25% -> 24%
where the time goes in v15:
time: 137 us; the launch traced here: 136 us
  waiting for transfers between devices  58.9 us (43%)
  Pallas kernels  35.5 us (26%)
  starting transfers between devices  32.4 us (24%)
  local copies, waits for them, and re-layouts  6.01 us (4%)
  other arithmetic  2.28 us (2%)
    ppermute x12, waiting for transfers between devices, along(): lax.ppermute(block, 'seq', [(i, (i + CORES * chips) % size) for i in rang...  33 us
    ppermute x8, waiting for transfers between devices, across(): return lax.ppermute(block, ('kv', 'seq'), route)  24.1 us
    pallas_call x4, Pallas kernels, project(): pl.pallas_call(functools.partial(project_kernel, indices), grid=(2 * step...  19.8 us
    ppermute x12, starting transfers between devices, along(): lax.ppermute(block, 'seq', [(i, (i + CORES * chips) % size) for i in rang...  15.6 us
    ppermute x8, starting transfers between devices, across(): return lax.ppermute(block, ('kv', 'seq'), route)  12.4 us
    pallas_call x2, Pallas kernels, attention(): pl.pallas_call(functools.partial(attention_kernel, heads, head_dim, offse...  9.29 us
    pallas_call x4, Pallas kernels, finish(): pl.pallas_call(finish_kernel, grid=(tokens // tile,), in_specs=[pl.BlockS...  4.45 us
    unnamed x18, local copies, waits for them, and re-layouts  3.7 us
  transfers between devices with their start and end apart: 32, of which 16 were waited for; matrix products, arithmetic and copies ran while one was open for 3% of the time, Pallas kernels for 24%

profile of v15, /device:TPU:0, one launch (start us, length us, event | category | flops | bytes accessed | tf_op | source)
XLA Modules:
  0.0 136.1 jit_solution(8744251755009624332)
XLA Ops:
  0.7 1.0 copy-done.3
  1.8 1.0 copy-done.4
  2.8 2.0 %arrange.1 = (bf16[4,2,128,512]{3,2,1,0:T(8,128)(2,1)}, bf16[1,2,128,512]{3,2,1,0:T(8,128)(2,1)}, bf16[1,2,128,512]{3,2,1,0:T(8,128)(2,1)}, bf16[1,2,128,512]{3,...) custom-call(s32[4]{0:T(128)S(1)} %add_xor_fusion.owner_ref, bf16[128,2048]{1,0:T(8,128)(2,1)S(1)} %copy-done.3, ...), custom_call_target="tpu_custom_call" | custom-call | tf_op jit(solution)/shard_map/arrange/pallas_call | solution.py:42
  4.8 5.0 %collective-permute-start = (bf16[1,2,128,512]{3,2,1,0:T(8,128)(2,1)}, bf16[1,2,128,512]{3,2,1,0:T(8,128)(2,1)}, u32[]{:S(2)}, u32[]{:S(2)}) collective-permute-start(bf16[1,2,128,512]{3,2,1,0:T(8,128)(2,1)} %get-tuple-element.102.refs_0_), channel_id=1, source_target_pairs={{0,6},{1,7},{2,0},{3,1},{4,2},{5,3},{6,4},{7,5},{8,14},{9,15},{10,... | collective-permute-start | bytes 786440 | tf_op jit(solution)/shard_map/ppermute | solution.py:261
  9.9 1.1 copy.26
  11.3 0.7 slice.60
  12.0 3.1 %collective-permute-start.3 = (bf16[224,512]{1,0:T(8,128)(2,1)}, bf16[224,512]{1,0:T(8,128)(2,1)}, u32[]{:S(2)}, u32[]{:S(2)}) collective-permute-start(bf16[224,512]{1,0:T(8,128)(2,1)} %slice.60), channel_id=1, source_target_pairs={{0,1},{1,2},{2,3},{3,4},{4,5},{5,6},{6,7},{8,9},{9,10},{10,11},{11... | collective-permute-start | bytes 688136 | tf_op jit(solution)/shard_map/ppermute | solution.py:337
  15.9 1.6 %copy-done.1 = bf16[1024,1024]{1,0:T(8,128)(2,1)S(1)} copy-done((bf16[1024,1024]{1,0:T(8,128)(2,1)S(1)}, bf16[1024,1024]{1,0:T(8,128)(2,1)}, u32[]{:S(2)}) %copy-start.1) | copy-done | bytes 2097176
  17.5 4.6 %attention.2.second_ref = bf16[512,2048]{1,0:T(8,128)(2,1)S(1)} custom-call(s32[8]{0:T(128)S(1)} %pad_add_fusion.order_ref, bf16[1024,1024]{1,0:T(8,128)(2,1)S(1)} %copy-done, bf16[1024,1024]{1,0:T(8,128)(2,1)S(1)} %copy-done.1, bf16[1024,512]{1,0:T(8,128)(2,1)S(1)} %pad_maximum_fusion.ctx_ref, s32[1024,128]{1,0:T(8,128)S(1)} %broadcast_in_dim.13.low_ref), custom_call_target="tpu_custom_call" | custom-call | flops 1048576 | bytes 512 | tf_op jit(solution)/shard_map/attention/pallas_call | solution.py:126
  22.2 1.2 collective-permute-done.1.refs_1_
  23.4 4.7 %collective-permute-done.2.refs_1_ = bf16[1,2,128,512]{3,2,1,0:T(8,128)(2,1)} collective-permute-done((bf16[1,2,128,512]{3,2,1,0:T(8,128)(2,1)}, bf16[1,2,128,512]{3,2,1,0:T(8,128)(2,1)}, u32[]{:S(2)}, u32[]{:S(2)}) %collective-permute-start.2) | collective-permute-done | bytes 262176 | tf_op jit(solution)/shard_map/ppermute | solution.py:261
  28.1 3.9 %collective-permute-start.5 = (bf16[1,2,128,512]{3,2,1,0:T(8,128)(2,1)}, bf16[1,2,128,512]{3,2,1,0:T(8,128)(2,1)S(1)}, u32[]{:S(2)}, u32[]{:S(2)}) collective-permute-start(bf16[1,2,128,512]{3,2,1,0:T(8,128)(2,1)} %collective-permute-done.1.refs_1_), channel_id=1, source_target_pairs={{0,2},{1,3},{2,4},{3,5},{4,6},{5,7},{6,0},{7,1},{8,10},{9,11},{10,... | collective-permute-start | bytes 786440 | tf_op jit(solution)/shard_map/ppermute | solution.py:261
  32.0 0.5 collective-permute-start.6
  32.7 1.0 pad_maximum_fusion.1.ctx_ref
  33.7 4.7 %attention.3.first_ref = bf16[512,2048]{1,0:T(8,128)(2,1)S(1)} custom-call(s32[8]{0:T(128)S(1)} %pad_add_fusion.order_ref, bf16[1024,1024]{1,0:T(8,128)(2,1)S(1)} %copy-done, bf16[1024,1024]{1,0:T(8,128)(2,1)S(1)} %copy-done.2, bf16[736,512]{1,0:T(8,128)(2,1)S(1)} %pad_maximum_fusion.1.ctx_ref, s32[1024,128]{1,0:T(8,128)S(1)} %broadcast_in_dim.13.low_ref), custom_call_target="tpu_custom_call" | custom-call | flops 1048576 | bytes 512 | tf_op jit(solution)/shard_map/attention/pallas_call | solution.py:126
  38.4 0.8 collective-permute-done.5.refs_2_
  39.3 5.6 %collective-permute-done.9.refs_1_ = bf16[1,2,128,512]{3,2,1,0:T(8,128)(2,1)S(1)} collective-permute-done((bf16[1,2,128,512]{3,2,1,0:T(8,128)(2,1)S(1)}, bf16[1,2,128,512]{3,2,1,0:T(8,128)(2,1)S(1)}, u32[]{:S(2)}, u32[]{:S(2)}) %collective-permute-start.9) | collective-permute-done | bytes 262176 | tf_op jit(solution)/shard_map/ppermute | solution.py:261
  45.0 2.1 %collective-permute-start.12 = (bf16[1,2,128,512]{3,2,1,0:T(8,128)(2,1)}, bf16[1,2,128,512]{3,2,1,0:T(8,128)(2,1)S(1)}, u32[]{:S(2)}, u32[]{:S(2)}) collective-permute-start(bf16[1,2,128,512]{3,2,1,0:T(8,128)(2,1)} %collective-permute-done.2.refs_1_), channel_id=1, source_target_pairs={{0,2},{1,3},{2,4},{3,5},{4,6},{5,7},{6,0},{7,1},{8,10},{9,11},{10,... | collective-permute-start | bytes 786440 | tf_op jit(solution)/shard_map/ppermute | solution.py:261
  47.0 5.0 %project.4 = (bf16[2,1024,256]{2,1,0:T(8,128)(2,1)S(1)}, bf16[2,1024,256]{2,1,0:T(8,128)(2,1)S(1)}) custom-call(bf16[512,2048]{1,0:T(8,128)(2,1)S(1)} %attention.3.first_ref, bf16[512,2048]{1,0:T(8,128)(2,1)S(1)} %attention.2.second_ref, bf16[1,2,128,512]{3,2,1,0:T(8,128)(2,1)} %get-tuple-element.102.refs_0_, ...), custom_call_target="tpu_custom_call" | custom-call | flops 3000000000 | bytes 512 | tf_op jit(solution)/shard_map/project/pallas_call | solution.py:200
  52.1 1.6 %collective-permute-start.18 = (bf16[2,1024,256]{2,1,0:T(8,128)(2,1)S(1)}, bf16[2,1024,256]{2,1,0:T(8,128)(2,1)S(1)}, u32[]{:S(2)}, u32[]{:S(2)}) collective-permute-start(bf16[2,1024,256]{2,1,0:T(8,128)(2,1)S(1)} %get-tuple-element.116), channel_id=1, source_target_pairs={{0,8},{1,17},{2,10},{3,19},{4,12},{5,21},{6,14},{7,23},{8,0},{9,25... | collective-permute-start | bytes 3145736 | tf_op jit(solution)/shard_map/ppermute | solution.py:256
  53.7 5.8 %collective-permute-done.11.refs_3_ = bf16[1,2,128,512]{3,2,1,0:T(8,128)(2,1)S(1)} collective-permute-done((bf16[1,2,128,512]{3,2,1,0:T(8,128)(2,1)}, bf16[1,2,128,512]{3,2,1,0:T(8,128)(2,1)S(1)}, u32[]{:S(2)}, u32[]{:S(2)}) %collective-permute-start.11) | collective-permute-done | bytes 262176 | tf_op jit(solution)/shard_map/ppermute | solution.py:261
  59.6 0.7 collective-permute-start.15
  60.3 1.3 collective-permute-start.16
  62.0 5.0 %project.5 = (bf16[2,1024,256]{2,1,0:T(8,128)(2,1)S(1)}, bf16[2,1024,256]{2,1,0:T(8,128)(2,1)S(1)}) custom-call(bf16[512,2048]{1,0:T(8,128)(2,1)S(1)} %attention.3.first_ref, bf16[512,2048]{1,0:T(8,128)(2,1)S(1)} %attention.2.second_ref, bf16[1,2,128,512]{3,2,1,0:T(8,128)(2,1)} %get-tuple-element.118.refs_0_, ...), custom_call_target="tpu_custom_call" | custom-call | flops 3000000000 | bytes 512 | tf_op jit(solution)/shard_map/project/pallas_call | solution.py:200
  66.9 1.6 %collective-permute-start.22 = (bf16[2,1024,256]{2,1,0:T(8,128)(2,1)S(1)}, bf16[2,1024,256]{2,1,0:T(8,128)(2,1)S(1)}, u32[]{:S(2)}, u32[]{:S(2)}) collective-permute-start(bf16[2,1024,256]{2,1,0:T(8,128)(2,1)S(1)} %get-tuple-element.130), channel_id=1, source_target_pairs={{0,8},{1,17},{2,10},{3,19},{4,12},{5,21},{6,14},{7,23},{8,0},{9,25... | collective-permute-start | bytes 3145736 | tf_op jit(solution)/shard_map/ppermute | solution.py:256
  68.7 6.3 %collective-permute-done.16.refs_2_ = bf16[1,2,128,512]{3,2,1,0:T(8,128)(2,1)S(1)} collective-permute-done((bf16[1,2,128,512]{3,2,1,0:T(8,128)(2,1)S(1)}, bf16[1,2,128,512]{3,2,1,0:T(8,128)(2,1)S(1)}, u32[]{:S(2)}, u32[]{:S(2)}) %collective-permute-start.16) | collective-permute-done | bytes 262176 | tf_op jit(solution)/shard_map/ppermute | solution.py:261
  74.9 5.2 %collective-permute-done.17.refs_1_ = bf16[1,2,128,512]{3,2,1,0:T(8,128)(2,1)S(1)} collective-permute-done((bf16[1,2,128,512]{3,2,1,0:T(8,128)(2,1)S(1)}, bf16[1,2,128,512]{3,2,1,0:T(8,128)(2,1)S(1)}, u32[]{:S(2)}, u32[]{:S(2)}) %collective-permute-start.17) | collective-permute-done | bytes 262176 | tf_op jit(solution)/shard_map/ppermute | solution.py:261
  80.2 1.6 %collective-permute-start.23 = (bf16[2,1024,128]{2,1,0:T(8,128)(2,1)S(1)}, bf16[2,1024,128]{2,1,0:T(8,128)(2,1)S(1)}, u32[]{:S(2)}, u32[]{:S(2)}) collective-permute-start(bf16[2,1024,128]{2,1,0:T(8,128)(2,1)S(1)} %add_convert_fusion.3), channel_id=1, source_target_pairs={{0,16},{1,9},{2,18},{3,11},{4,20},{5,13},{6,22},{7,15},{8,24},{9,1... | collective-permute-start | bytes 1572872 | tf_op jit(solution)/shard_map/ppermute | solution.py:256
  81.8 1.7 %collective-permute-start.20 = (bf16[1,2,128,512]{3,2,1,0:T(8,128)(2,1)S(1)}, bf16[1,2,128,512]{3,2,1,0:T(8,128)(2,1)S(1)}, u32[]{:S(2)}, u32[]{:S(2)}) collective-permute-start(bf16[1,2,128,512]{3,2,1,0:T(8,128)(2,1)S(1)} %get-tuple-element.148.refs_0_), channel_id=1, source_target_pairs={{0,6},{1,7},{2,0},{3,1},{4,2},{5,3},{6,4},{7,5},{8,14},{9,15},{10,... | collective-permute-start | bytes 786440 | tf_op jit(solution)/shard_map/ppermute | solution.py:261
  83.9 4.9 %project.6 = (bf16[2,1024,256]{2,1,0:T(8,128)(2,1)S(1)}, bf16[2,1024,256]{2,1,0:T(8,128)(2,1)S(1)}) custom-call(bf16[512,2048]{1,0:T(8,128)(2,1)S(1)} %attention.3.first_ref, bf16[512,2048]{1,0:T(8,128)(2,1)S(1)} %attention.2.second_ref, bf16[1,2,128,512]{3,2,1,0:T(8,128)(2,1)S(1)} %copy-done.6, bf16[1,2,128,512]{3,2,1,0:T(8,128)(2,1)S(1)} %collective-permute-done.9.refs_1_, ...), custom_call_target="tpu_custom_call" | custom-call | flops 1500000000 | bytes 512 | tf_op jit(solution)/shard_map/project/pallas_call | solution.py:200
  88.7 0.7 collective-permute-done.23.last_ref
  89.6 1.6 %collective-permute-start.27 = (bf16[2,1024,128]{2,1,0:T(8,128)(2,1)S(1)}, bf16[2,1024,128]{2,1,0:T(8,128)(2,1)S(1)}, u32[]{:S(2)}, u32[]{:S(2)}) collective-permute-start(bf16[2,1024,128]{2,1,0:T(8,128)(2,1)S(1)} %add_convert_fusion.2), channel_id=1, source_target_pairs={{0,16},{1,9},{2,18},{3,11},{4,20},{5,13},{6,22},{7,15},{8,24},{9,1... | collective-permute-start | bytes 1572872 | tf_op jit(solution)/shard_map/ppermute | solution.py:256
  91.2 1.5 %collective-permute-start.30 = (bf16[2,1024,256]{2,1,0:T(8,128)(2,1)S(1)}, bf16[2,1024,256]{2,1,0:T(8,128)(2,1)S(1)}, u32[]{:S(2)}, u32[]{:S(2)}) collective-permute-start(bf16[2,1024,256]{2,1,0:T(8,128)(2,1)S(1)} %get-tuple-element.144), channel_id=1, source_target_pairs={{0,8},{1,17},{2,10},{3,19},{4,12},{5,21},{6,14},{7,23},{8,0},{9,25... | collective-permute-start | bytes 3145736 | tf_op jit(solution)/shard_map/ppermute | solution.py:256
  92.7 3.4 %collective-permute-done.21.refs_2_ = bf16[1,2,128,512]{3,2,1,0:T(8,128)(2,1)S(1)} collective-permute-done((bf16[1,2,128,512]{3,2,1,0:T(8,128)(2,1)S(1)}, bf16[1,2,128,512]{3,2,1,0:T(8,128)(2,1)S(1)}, u32[]{:S(2)}, u32[]{:S(2)}) %collective-permute-start.21) | collective-permute-done | bytes 262176 | tf_op jit(solution)/shard_map/ppermute | solution.py:261
  96.1 0.5 collective-permute-start.25
  96.6 1.0 collective-permute-done.24.refs_5_
  98.4 4.9 %project.7 = (bf16[2,1024,256]{2,1,0:T(8,128)(2,1)S(1)}, bf16[2,1024,256]{2,1,0:T(8,128)(2,1)S(1)}) custom-call(bf16[512,2048]{1,0:T(8,128)(2,1)S(1)} %attention.3.first_ref, bf16[512,2048]{1,0:T(8,128)(2,1)S(1)} %attention.2.second_ref, bf16[1,2,128,512]{3,2,1,0:T(8,128)(2,1)S(1)} %get-tuple-element.148.refs_0_, ...), custom_call_target="tpu_custom_call" | custom-call | flops 10000000 | bytes 512 | tf_op jit(solution)/shard_map/project/pallas_call | solution.py:200
  103.3 1.2 collective-permute-done.27.last_ref
  104.5 1.5 %collective-permute-start.28 = (bf16[2,1024,256]{2,1,0:T(8,128)(2,1)S(1)}, bf16[2,1024,256]{2,1,0:T(8,128)(2,1)S(1)}, u32[]{:S(2)}, u32[]{:S(2)}) collective-permute-start(bf16[2,1024,256]{2,1,0:T(8,128)(2,1)S(1)} %get-tuple-element.155), channel_id=1, source_target_pairs={{0,8},{1,17},{2,10},{3,19},{4,12},{5,21},{6,14},{7,23},{8,0},{9,25... | collective-permute-start | bytes 3145736 | tf_op jit(solution)/shard_map/ppermute | solution.py:256
  106.0 2.7 %collective-permute-done.30.received_ref = bf16[2,1024,256]{2,1,0:T(8,128)(2,1)S(1)} collective-permute-done((bf16[2,1024,256]{2,1,0:T(8,128)(2,1)S(1)}, bf16[2,1024,256]{2,1,0:T(8,128)(2,1)S(1)}, u32[]{:S(2)}, u32[]{:S(2)}) %collective-permute-start.30) | collective-permute-done | bytes 1048608 | tf_op jit(solution)/shard_map/ppermute | solution.py:256
  108.9 1.6 %collective-permute-start.31 = (bf16[2,1024,128]{2,1,0:T(8,128)(2,1)S(1)}, bf16[2,1024,128]{2,1,0:T(8,128)(2,1)S(1)}, u32[]{:S(2)}, u32[]{:S(2)}) collective-permute-start(bf16[2,1024,128]{2,1,0:T(8,128)(2,1)S(1)} %add_convert_fusion), channel_id=1, source_target_pairs={{0,16},{1,9},{2,18},{3,11},{4,20},{5,13},{6,22},{7,15},{8,24},{9,1... | collective-permute-start | bytes 1572872 | tf_op jit(solution)/shard_map/ppermute | solution.py:256
  110.5 15.1 %collective-permute-done.28.received_ref = bf16[2,1024,256]{2,1,0:T(8,128)(2,1)S(1)} collective-permute-done((bf16[2,1024,256]{2,1,0:T(8,128)(2,1)S(1)}, bf16[2,1024,256]{2,1,0:T(8,128)(2,1)S(1)}, u32[]{:S(2)}, u32[]{:S(2)}) %collective-permute-start.28) | collective-permute-done | bytes 1048608 | tf_op jit(solution)/shard_map/ppermute | solution.py:256
  125.7 1.6 %collective-permute-start.29 = (bf16[2,1024,128]{2,1,0:T(8,128)(2,1)S(1)}, bf16[2,1024,128]{2,1,0:T(8,128)(2,1)S(1)}, u32[]{:S(2)}, u32[]{:S(2)}) collective-permute-start(bf16[2,1024,128]{2,1,0:T(8,128)(2,1)S(1)} %add_convert_fusion.1), channel_id=1, source_target_pairs={{0,16},{1,9},{2,18},{3,11},{4,20},{5,13},{6,22},{7,15},{8,24},{9,1... | collective-permute-start | bytes 1572872 | tf_op jit(solution)/shard_map/ppermute | solution.py:256
  127.3 1.1 finish.4
  128.4 1.1 finish.5
  129.5 1.1 finish.6
  130.6 4.3 %collective-permute-done.29.last_ref = bf16[2,1024,128]{2,1,0:T(8,128)(2,1)S(1)} collective-permute-done((bf16[2,1024,128]{2,1,0:T(8,128)(2,1)S(1)}, bf16[2,1024,128]{2,1,0:T(8,128)(2,1)S(1)}, u32[]{:S(2)}, u32[]{:S(2)}) %collective-permute-start.29) | collective-permute-done | bytes 524320 | tf_op jit(solution)/shard_map/ppermute | solution.py:256
  135.0 1.1 finish.7
  (69 shorter events, 3.6 us)
Async XLA Ops:
  0.7 1.0 copy-start.3
  1.8 1.0 copy-start.4
  2.8 8.2 %copy-start.7 = (bf16[1024,2,128]{2,1,0:T(2,128)(2,1)S(1)}, bf16[1024,2,128]{2,1,0:T(2,128)(2,1)}, u32[]{:S(2)}) copy-start(bf16[1024,2,128]{2,1,0:T(2,128)(2,1)} %param.9) | copy-start | bytes 1572868
  4.8 6.4 %copy-start.5 = (bf16[1,2,128,512]{3,2,1,0:T(8,128)(2,1)}, bf16[1,2,128,512]{3,2,1,0:T(8,128)(2,1)S(1)}, u32[]{:S(2)}) copy-start(bf16[1,2,128,512]{3,2,1,0:T(8,128)(2,1)S(1)} %get-tuple-element.133.refs_0_) | copy-start | bytes 786436
  4.8 17.4 %collective-permute-start = (bf16[1,2,128,512]{3,2,1,0:T(8,128)(2,1)}, bf16[1,2,128,512]{3,2,1,0:T(8,128)(2,1)}, u32[]{:S(2)}, u32[]{:S(2)}) collective-permute-start(bf16[1,2,128,512]{3,2,1,0:T(8,128)(2,1)} %get-tuple-element.102.refs_0_), channel_id=1, source_target_pairs={{0,6},{1,7},{2,0},{3,1},{4,2},{5,3},{6,4},{7,5},{8,14},{9,15},{10,... | collective-permute-start | bytes 786440 | tf_op jit(solution)/shard_map/ppermute | solution.py:261
  9.8 13.6 %collective-permute-start.1 = (bf16[1,2,128,512]{3,2,1,0:T(8,128)(2,1)}, bf16[1,2,128,512]{3,2,1,0:T(8,128)(2,1)}, u32[]{:S(2)}, u32[]{:S(2)}) collective-permute-start(bf16[1,2,128,512]{3,2,1,0:T(8,128)(2,1)} %get-tuple-element.102.refs_0_), channel_id=1, source_target_pairs={{0,2},{1,3},{2,4},{3,5},{4,6},{5,7},{6,0},{7,1},{8,10},{9,11},{10,... | collective-permute-start | bytes 786440 | tf_op jit(solution)/shard_map/ppermute | solution.py:261
  9.8 18.3 %collective-permute-start.2 = (bf16[1,2,128,512]{3,2,1,0:T(8,128)(2,1)}, bf16[1,2,128,512]{3,2,1,0:T(8,128)(2,1)}, u32[]{:S(2)}, u32[]{:S(2)}) collective-permute-start(bf16[1,2,128,512]{3,2,1,0:T(8,128)(2,1)} %get-tuple-element.118.refs_0_), channel_id=1, source_target_pairs={{0,2},{1,3},{2,4},{3,5},{4,6},{5,7},{6,0},{7,1},{8,10},{9,11},{10,... | collective-permute-start | bytes 786440 | tf_op jit(solution)/shard_map/ppermute | solution.py:261
  9.8 18.3 %collective-permute-start.4 = (bf16[4,2,128,512]{3,2,1,0:T(8,128)(2,1)}, bf16[4,2,128,512]{3,2,1,0:T(8,128)(2,1)}, u32[]{:S(2)}, u32[]{:S(2)}) collective-permute-start(bf16[4,2,128,512]{3,2,1,0:T(8,128)(2,1)} %get-tuple-element.90), channel_id=1, source_target_pairs={{0,1},{1,0},{2,3},{3,2},{4,5},{5,4},{6,7},{7,6},{8,9},{9,8},{10,11... | collective-permute-start | bytes 3145736 | tf_op jit(solution)/shard_map/ppermute | solution.py:265
  11.1 4.1 %copy-start.8 = (s32[64]{0:T(128)S(1)}, s32[64]{0:T(128)}, u32[]{:S(2)}) copy-start(s32[64]{0:T(128)} %param.11) | copy-start | bytes 772
  11.2 4.7 %copy-start = (bf16[1024,1024]{1,0:T(8,128)(2,1)S(1)}, bf16[1024,1024]{1,0:T(8,128)(2,1)}, u32[]{:S(2)}) copy-start(bf16[1024,1024]{1,0:T(8,128)(2,1)} %q_ref.3) | copy-start | bytes 6291460
  12.0 10.1 %collective-permute-start.3 = (bf16[224,512]{1,0:T(8,128)(2,1)}, bf16[224,512]{1,0:T(8,128)(2,1)}, u32[]{:S(2)}, u32[]{:S(2)}) collective-permute-start(bf16[224,512]{1,0:T(8,128)(2,1)} %slice.60), channel_id=1, source_target_pairs={{0,1},{1,2},{2,3},{3,4},{4,5},{5,6},{6,7},{8,9},{9,10},{10,11},{11... | collective-permute-start | bytes 688136 | tf_op jit(solution)/shard_map/ppermute | solution.py:337
  15.9 1.6 %copy-start.1 = (bf16[1024,1024]{1,0:T(8,128)(2,1)S(1)}, bf16[1024,1024]{1,0:T(8,128)(2,1)}, u32[]{:S(2)}) copy-start(bf16[1024,1024]{1,0:T(8,128)(2,1)} %qt_ref.3) | copy-start | bytes 6291460
  17.5 15.0 %copy-start.6 = (bf16[1,2,128,512]{3,2,1,0:T(8,128)(2,1)S(1)}, bf16[1,2,128,512]{3,2,1,0:T(8,128)(2,1)}, u32[]{:S(2)}) copy-start(bf16[1,2,128,512]{3,2,1,0:T(8,128)(2,1)} %copy-done.5) | copy-start | bytes 786436
  22.1 11.6 %copy-start.2 = (bf16[1024,1024]{1,0:T(8,128)(2,1)S(1)}, bf16[1024,1024]{1,0:T(8,128)(2,1)}, u32[]{:S(2)}) copy-start(bf16[1024,1024]{1,0:T(8,128)(2,1)} %qt_ref.3) | copy-start | bytes 6291460
  28.1 11.1 %collective-permute-start.5 = (bf16[1,2,128,512]{3,2,1,0:T(8,128)(2,1)}, bf16[1,2,128,512]{3,2,1,0:T(8,128)(2,1)S(1)}, u32[]{:S(2)}, u32[]{:S(2)}) collective-permute-start(bf16[1,2,128,512]{3,2,1,0:T(8,128)(2,1)} %collective-permute-done.1.refs_1_), channel_id=1, source_target_pairs={{0,2},{1,3},{2,4},{3,5},{4,6},{5,7},{6,0},{7,1},{8,10},{9,11},{10,... | collective-permute-start | bytes 786440 | tf_op jit(solution)/shard_map/ppermute | solution.py:261
  32.0 7.2 %collective-permute-start.7 = (bf16[1,2,128,512]{3,2,1,0:T(8,128)(2,1)}, bf16[1,2,128,512]{3,2,1,0:T(8,128)(2,1)S(1)}, u32[]{:S(2)}, u32[]{:S(2)}) collective-permute-start(bf16[1,2,128,512]{3,2,1,0:T(8,128)(2,1)} %collective-permute-done.1.refs_1_), channel_id=1, source_target_pairs={{0,1},{1,0},{2,3},{3,2},{4,5},{5,4},{6,7},{7,6},{8,9},{9,8},{10,11... | collective-permute-start | bytes 786440 | tf_op jit(solution)/shard_map/ppermute | solution.py:265
  32.0 7.2 %collective-permute-start.6 = (bf16[1,2,128,512]{3,2,1,0:T(8,128)(2,1)}, bf16[1,2,128,512]{3,2,1,0:T(8,128)(2,1)S(1)}, u32[]{:S(2)}, u32[]{:S(2)}) collective-permute-start(bf16[1,2,128,512]{3,2,1,0:T(8,128)(2,1)} %collective-permute-done.refs_3_), channel_id=1, source_target_pairs={{0,1},{1,0},{2,3},{3,2},{4,5},{5,4},{6,7},{7,6},{8,9},{9,8},{10,11... | collective-permute-start | bytes 786440 | tf_op jit(solution)/shard_map/ppermute | solution.py:265
  32.5 6.7 %collective-permute-start.8 = (bf16[1,2,128,512]{3,2,1,0:T(8,128)(2,1)}, bf16[1,2,128,512]{3,2,1,0:T(8,128)(2,1)S(1)}, u32[]{:S(2)}, u32[]{:S(2)}) collective-permute-start(bf16[1,2,128,512]{3,2,1,0:T(8,128)(2,1)} %collective-permute-done.2.refs_1_), channel_id=1, source_target_pairs={{0,1},{1,0},{2,3},{3,2},{4,5},{5,4},{6,7},{7,6},{8,9},{9,8},{10,11... | collective-permute-start | bytes 786440 | tf_op jit(solution)/shard_map/ppermute | solution.py:265
  32.5 12.3 %collective-permute-start.9 = (bf16[1,2,128,512]{3,2,1,0:T(8,128)(2,1)S(1)}, bf16[1,2,128,512]{3,2,1,0:T(8,128)(2,1)S(1)}, u32[]{:S(2)}, u32[]{:S(2)}) collective-permute-start(bf16[1,2,128,512]{3,2,1,0:T(8,128)(2,1)S(1)} %copy-done.6), channel_id=1, source_target_pairs={{0,2},{1,3},{2,4},{3,5},{4,6},{5,7},{6,0},{7,1},{8,10},{9,11},{10,... | collective-permute-start | bytes 786440 | tf_op jit(solution)/shard_map/ppermute | solution.py:261
  44.9 2.2 %collective-permute-start.10 = (bf16[1,2,128,512]{3,2,1,0:T(8,128)(2,1)S(1)}, bf16[1,2,128,512]{3,2,1,0:T(8,128)(2,1)S(1)}, u32[]{:S(2)}, u32[]{:S(2)}) collective-permute-start(bf16[1,2,128,512]{3,2,1,0:T(8,128)(2,1)S(1)} %collective-permute-done.5.refs_2_), channel_id=1, source_target_pairs={{0,1},{1,0},{2,3},{3,2},{4,5},{5,4},{6,7},{7,6},{8,9},{9,8},{10,11... | collective-permute-start | bytes 786440 | tf_op jit(solution)/shard_map/ppermute | solution.py:265
  45.0 14.4 %collective-permute-start.11 = (bf16[1,2,128,512]{3,2,1,0:T(8,128)(2,1)}, bf16[1,2,128,512]{3,2,1,0:T(8,128)(2,1)S(1)}, u32[]{:S(2)}, u32[]{:S(2)}) collective-permute-start(bf16[1,2,128,512]{3,2,1,0:T(8,128)(2,1)} %get-tuple-element.118.refs_0_), channel_id=1, source_target_pairs={{0,6},{1,7},{2,0},{3,1},{4,2},{5,3},{6,4},{7,5},{8,14},{9,15},{10,... | collective-permute-start | bytes 786440 | tf_op jit(solution)/shard_map/ppermute | solution.py:261
  45.0 14.4 %collective-permute-start.12 = (bf16[1,2,128,512]{3,2,1,0:T(8,128)(2,1)}, bf16[1,2,128,512]{3,2,1,0:T(8,128)(2,1)S(1)}, u32[]{:S(2)}, u32[]{:S(2)}) collective-permute-start(bf16[1,2,128,512]{3,2,1,0:T(8,128)(2,1)} %collective-permute-done.2.refs_1_), channel_id=1, source_target_pairs={{0,2},{1,3},{2,4},{3,5},{4,6},{5,7},{6,0},{7,1},{8,10},{9,11},{10,... | collective-permute-start | bytes 786440 | tf_op jit(solution)/shard_map/ppermute | solution.py:261
  47.0 12.4 %collective-permute-start.13 = (bf16[1,2,128,512]{3,2,1,0:T(8,128)(2,1)S(1)}, bf16[1,2,128,512]{3,2,1,0:T(8,128)(2,1)S(1)}, u32[]{:S(2)}, u32[]{:S(2)}) collective-permute-start(bf16[1,2,128,512]{3,2,1,0:T(8,128)(2,1)S(1)} %collective-permute-done.9.refs_1_), channel_id=1, source_target_pairs={{0,1},{1,0},{2,3},{3,2},{4,5},{5,4},{6,7},{7,6},{8,9},{9,8},{10,11... | collective-permute-start | bytes 786440 | tf_op jit(solution)/shard_map/ppermute | solution.py:265
  52.1 16.4 %collective-permute-start.18 = (bf16[2,1024,256]{2,1,0:T(8,128)(2,1)S(1)}, bf16[2,1024,256]{2,1,0:T(8,128)(2,1)S(1)}, u32[]{:S(2)}, u32[]{:S(2)}) collective-permute-start(bf16[2,1024,256]{2,1,0:T(8,128)(2,1)S(1)} %get-tuple-element.116), channel_id=1, source_target_pairs={{0,8},{1,17},{2,10},{3,19},{4,12},{5,21},{6,14},{7,23},{8,0},{9,25... | collective-permute-start | bytes 3145736 | tf_op jit(solution)/shard_map/ppermute | solution.py:256
  59.5 2.5 %collective-permute-start.14 = (bf16[2,2,128,512]{3,2,1,0:T(8,128)(2,1)S(1)}, bf16[2,2,128,512]{3,2,1,0:T(8,128)(2,1)S(1)}, u32[]{:S(2)}, u32[]{:S(2)}) collective-permute-start(bf16[2,2,128,512]{3,2,1,0:T(8,128)(2,1)S(1)} %pad_maximum_fusion.2), channel_id=1, source_target_pairs={{0,1},{1,0},{2,3},{3,2},{4,5},{5,4},{6,7},{7,6},{8,9},{9,8},{10,11... | collective-permute-start | bytes 1572872 | tf_op jit(solution)/shard_map/ppermute | solution.py:265
  59.6 9.1 %collective-permute-start.15 = (bf16[1,2,128,512]{3,2,1,0:T(8,128)(2,1)S(1)}, bf16[1,2,128,512]{3,2,1,0:T(8,128)(2,1)S(1)}, u32[]{:S(2)}, u32[]{:S(2)}) collective-permute-start(bf16[1,2,128,512]{3,2,1,0:T(8,128)(2,1)S(1)} %copy-done.6), channel_id=1, source_target_pairs={{0,6},{1,7},{2,0},{3,1},{4,2},{5,3},{6,4},{7,5},{8,14},{9,15},{10,... | collective-permute-start | bytes 786440 | tf_op jit(solution)/shard_map/ppermute | solution.py:261
  60.3 14.6 %collective-permute-start.16 = (bf16[1,2,128,512]{3,2,1,0:T(8,128)(2,1)S(1)}, bf16[1,2,128,512]{3,2,1,0:T(8,128)(2,1)S(1)}, u32[]{:S(2)}, u32[]{:S(2)}) collective-permute-start(bf16[1,2,128,512]{3,2,1,0:T(8,128)(2,1)S(1)} %collective-permute-done.9.refs_1_), channel_id=1, source_target_pairs={{0,2},{1,3},{2,4},{3,5},{4,6},{5,7},{6,0},{7,1},{8,10},{9,11},{10,... | collective-permute-start | bytes 786440 | tf_op jit(solution)/shard_map/ppermute | solution.py:261
  61.6 18.5 %collective-permute-start.17 = (bf16[1,2,128,512]{3,2,1,0:T(8,128)(2,1)S(1)}, bf16[1,2,128,512]{3,2,1,0:T(8,128)(2,1)S(1)}, u32[]{:S(2)}, u32[]{:S(2)}) collective-permute-start(bf16[1,2,128,512]{3,2,1,0:T(8,128)(2,1)S(1)} %get-tuple-element.148.refs_0_), channel_id=1, source_target_pairs={{0,2},{1,3},{2,4},{3,5},{4,6},{5,7},{6,0},{7,1},{8,10},{9,11},{10,... | collective-permute-start | bytes 786440 | tf_op jit(solution)/shard_map/ppermute | solution.py:261
  66.9 22.6 %collective-permute-start.22 = (bf16[2,1024,256]{2,1,0:T(8,128)(2,1)S(1)}, bf16[2,1024,256]{2,1,0:T(8,128)(2,1)S(1)}, u32[]{:S(2)}, u32[]{:S(2)}) collective-permute-start(bf16[2,1024,256]{2,1,0:T(8,128)(2,1)S(1)} %get-tuple-element.130), channel_id=1, source_target_pairs={{0,8},{1,17},{2,10},{3,19},{4,12},{5,21},{6,14},{7,23},{8,0},{9,25... | collective-permute-start | bytes 3145736 | tf_op jit(solution)/shard_map/ppermute | solution.py:256
  80.2 3.7 %collective-permute-start.19 = (bf16[2,2,128,512]{3,2,1,0:T(8,128)(2,1)S(1)}, bf16[2,2,128,512]{3,2,1,0:T(8,128)(2,1)S(1)}, u32[]{:S(2)}, u32[]{:S(2)}) collective-permute-start(bf16[2,2,128,512]{3,2,1,0:T(8,128)(2,1)S(1)} %pad_maximum_fusion.3), channel_id=1, source_target_pairs={{0,1},{1,0},{2,3},{3,2},{4,5},{5,4},{6,7},{7,6},{8,9},{9,8},{10,11... | collective-permute-start | bytes 1572872 | tf_op jit(solution)/shard_map/ppermute | solution.py:265
  80.2 9.2 %collective-permute-start.23 = (bf16[2,1024,128]{2,1,0:T(8,128)(2,1)S(1)}, bf16[2,1024,128]{2,1,0:T(8,128)(2,1)S(1)}, u32[]{:S(2)}, u32[]{:S(2)}) collective-permute-start(bf16[2,1024,128]{2,1,0:T(8,128)(2,1)S(1)} %add_convert_fusion.3), channel_id=1, source_target_pairs={{0,16},{1,9},{2,18},{3,11},{4,20},{5,13},{6,22},{7,15},{8,24},{9,1... | collective-permute-start | bytes 1572872 | tf_op jit(solution)/shard_map/ppermute | solution.py:256
  81.8 10.9 %collective-permute-start.20 = (bf16[1,2,128,512]{3,2,1,0:T(8,128)(2,1)S(1)}, bf16[1,2,128,512]{3,2,1,0:T(8,128)(2,1)S(1)}, u32[]{:S(2)}, u32[]{:S(2)}) collective-permute-start(bf16[1,2,128,512]{3,2,1,0:T(8,128)(2,1)S(1)} %get-tuple-element.148.refs_0_), channel_id=1, source_target_pairs={{0,6},{1,7},{2,0},{3,1},{4,2},{5,3},{6,4},{7,5},{8,14},{9,15},{10,... | collective-permute-start | bytes 786440 | tf_op jit(solution)/shard_map/ppermute | solution.py:261
  83.6 12.5 %collective-permute-start.21 = (bf16[1,2,128,512]{3,2,1,0:T(8,128)(2,1)S(1)}, bf16[1,2,128,512]{3,2,1,0:T(8,128)(2,1)S(1)}, u32[]{:S(2)}, u32[]{:S(2)}) collective-permute-start(bf16[1,2,128,512]{3,2,1,0:T(8,128)(2,1)S(1)} %collective-permute-done.17.refs_1_), channel_id=1, source_target_pairs={{0,2},{1,3},{2,4},{3,5},{4,6},{5,7},{6,0},{7,1},{8,10},{9,11},{10,... | collective-permute-start | bytes 786440 | tf_op jit(solution)/shard_map/ppermute | solution.py:261
  89.6 14.9 %collective-permute-start.27 = (bf16[2,1024,128]{2,1,0:T(8,128)(2,1)S(1)}, bf16[2,1024,128]{2,1,0:T(8,128)(2,1)S(1)}, u32[]{:S(2)}, u32[]{:S(2)}) collective-permute-start(bf16[2,1024,128]{2,1,0:T(8,128)(2,1)S(1)} %add_convert_fusion.2), channel_id=1, source_target_pairs={{0,16},{1,9},{2,18},{3,11},{4,20},{5,13},{6,22},{7,15},{8,24},{9,1... | collective-permute-start | bytes 1572872 | tf_op jit(solution)/shard_map/ppermute | solution.py:256
  91.2 17.5 %collective-permute-start.30 = (bf16[2,1024,256]{2,1,0:T(8,128)(2,1)S(1)}, bf16[2,1024,256]{2,1,0:T(8,128)(2,1)S(1)}, u32[]{:S(2)}, u32[]{:S(2)}) collective-permute-start(bf16[2,1024,256]{2,1,0:T(8,128)(2,1)S(1)} %get-tuple-element.144), channel_id=1, source_target_pairs={{0,8},{1,17},{2,10},{3,19},{4,12},{5,21},{6,14},{7,23},{8,0},{9,25... | collective-permute-start | bytes 3145736 | tf_op jit(solution)/shard_map/ppermute | solution.py:256
  96.1 1.5 %collective-permute-start.24 = (bf16[1,2,128,512]{3,2,1,0:T(8,128)(2,1)S(1)}, bf16[1,2,128,512]{3,2,1,0:T(8,128)(2,1)S(1)}, u32[]{:S(2)}, u32[]{:S(2)}) collective-permute-start(bf16[1,2,128,512]{3,2,1,0:T(8,128)(2,1)S(1)} %collective-permute-done.17.refs_1_), channel_id=1, source_target_pairs={{0,1},{1,0},{2,3},{3,2},{4,5},{5,4},{6,7},{7,6},{8,9},{9,8},{10,11... | collective-permute-start | bytes 786440 | tf_op jit(solution)/shard_map/ppermute | solution.py:265
  96.1 1.9 %collective-permute-start.25 = (bf16[1,2,128,512]{3,2,1,0:T(8,128)(2,1)S(1)}, bf16[1,2,128,512]{3,2,1,0:T(8,128)(2,1)S(1)}, u32[]{:S(2)}, u32[]{:S(2)}) collective-permute-start(bf16[1,2,128,512]{3,2,1,0:T(8,128)(2,1)S(1)} %collective-permute-done.21.refs_2_), channel_id=1, source_target_pairs={{0,1},{1,0},{2,3},{3,2},{4,5},{5,4},{6,7},{7,6},{8,9},{9,8},{10,11... | collective-permute-start | bytes 786440 | tf_op jit(solution)/shard_map/ppermute | solution.py:265
  96.6 1.8 %collective-permute-start.26 = (bf16[1,2,128,512]{3,2,1,0:T(8,128)(2,1)S(1)}, bf16[1,2,128,512]{3,2,1,0:T(8,128)(2,1)S(1)}, u32[]{:S(2)}, u32[]{:S(2)}) collective-permute-start(bf16[1,2,128,512]{3,2,1,0:T(8,128)(2,1)S(1)} %collective-permute-done.20.refs_3_), channel_id=1, source_target_pairs={{0,1},{1,0},{2,3},{3,2},{4,5},{5,4},{6,7},{7,6},{8,9},{9,8},{10,11... | collective-permute-start | bytes 786440 | tf_op jit(solution)/shard_map/ppermute | solution.py:265
  104.5 21.1 %collective-permute-start.28 = (bf16[2,1024,256]{2,1,0:T(8,128)(2,1)S(1)}, bf16[2,1024,256]{2,1,0:T(8,128)(2,1)S(1)}, u32[]{:S(2)}, u32[]{:S(2)}) collective-permute-start(bf16[2,1024,256]{2,1,0:T(8,128)(2,1)S(1)} %get-tuple-element.155), channel_id=1, source_target_pairs={{0,8},{1,17},{2,10},{3,19},{4,12},{5,21},{6,14},{7,23},{8,0},{9,25... | collective-permute-start | bytes 3145736 | tf_op jit(solution)/shard_map/ppermute | solution.py:256
  108.9 20.7 %collective-permute-start.31 = (bf16[2,1024,128]{2,1,0:T(8,128)(2,1)S(1)}, bf16[2,1024,128]{2,1,0:T(8,128)(2,1)S(1)}, u32[]{:S(2)}, u32[]{:S(2)}) collective-permute-start(bf16[2,1024,128]{2,1,0:T(8,128)(2,1)S(1)} %add_convert_fusion), channel_id=1, source_target_pairs={{0,16},{1,9},{2,18},{3,11},{4,20},{5,13},{6,22},{7,15},{8,24},{9,1... | collective-permute-start | bytes 1572872 | tf_op jit(solution)/shard_map/ppermute | solution.py:256
  125.7 9.2 %collective-permute-start.29 = (bf16[2,1024,128]{2,1,0:T(8,128)(2,1)S(1)}, bf16[2,1024,128]{2,1,0:T(8,128)(2,1)S(1)}, u32[]{:S(2)}, u32[]{:S(2)}) collective-permute-start(bf16[2,1024,128]{2,1,0:T(8,128)(2,1)S(1)} %add_convert_fusion.1), channel_id=1, source_target_pairs={{0,16},{1,9},{2,18},{3,11},{4,20},{5,13},{6,22},{7,15},{8,24},{9,1... | collective-permute-start | bytes 1572872 | tf_op jit(solution)/shard_map/ppermute | solution.py:256
